TPU v7x, 32 devices: a whole 2x2x4 slice. The times are simulated.
32 devices in a mesh: groups: 2 (over x), gx: 8 (over z, y), gy: 2 (over core).
Axes of the slice: x: 2, y: 2, z: 4, core: 2. Of those that a mesh axis runs over, the one named last changes fastest.
Arguments:
- tokens: bfloat16 [512, 16384], P('groups', 'gx'), parts along dimension 0, may hold values from -4000 to 4000
- norm_gain: float32 [16384], P('gx'), may hold values from 0.1 to 1.9
- w_query: bfloat16 [16384, 8192], P('gx', 'gy'), may hold values from -0.046875 to 0.046875
- w_key: bfloat16 [16384, 512], P('gx', 'gy'), may hold values from -0.09375 to 0.09375
- w_value: bfloat16 [16384, 512], P('gx', 'gy'), may hold values from -0.046875 to 0.046875
- w_out: bfloat16 [8192, 16384], P('gy', 'gx'), may hold values from -0.1875 to 0.1875
- cache_keys: bfloat16 [128, 1024, 512], P(('groups', 'gx'), None, 'gy'), parts along dimension 0, may hold values from -400 to 400
- cache_values: bfloat16 [128, 1024, 512], P(('groups', 'gx'), None, 'gy'), parts along dimension 0, may hold values from -4 to 4
- cache_lengths: int32 [128], P(('groups', 'gx')), parts along dimension 0, may hold values from 128 to 1024, as said below
Outputs:
- attended: bfloat16 [512, 16384], P(('groups', 'gy'), 'gx'), parts along dimension 0
There are 2 independent parts, one for each index of `groups`. A program takes and returns all parts, laid end to end along the dimension named above; an argument that names none is the same for every part. Nothing has to cross between parts.
Inputs may be any that keep to these rules, and one draw needn't show every extreme that they name: `cache_lengths`: one sequence has exactly 1024 live slots.
All inputs are finite; a program needn't handle non-finite values.
Results may differ from a plain program's by a relative error of at most 0.012.
The roundings to bfloat16 on the way count: a program that leaves them out, or rounds other values in their place, can miss the bound.
Values may be sent and summed in bfloat16 or wider, within the bound.
No kernel may reach another device: no remote copies, remote signals or barrier semaphores. Data moves between devices by JAX's collectives and lax.ppermute only.
A program may use at most 128 MiB of HBM per device.

v0:
```python
import functools

import jax
import jax.numpy as jnp
from jax import lax
from jax.experimental import pallas as pl
from jax.experimental.pallas import tpu as pltpu
from jax.sharding import PartitionSpec as P

D = 16384
HD = 128
NEW = 4
EPS = 1e-05
THETA = 500000.0

CHUNKS = 2
TILE = 256
AHEAD = 4
MIB = 1 << 20


def bit_orders(n):
    levels = n.bit_length() - 1
    first = list(range(levels))
    second = list(first)
    if levels > 1:
        second[0], second[1] = second[1], second[0]
    return first, second


def slot_shift(slot, order):
    levels = len(order)
    shift = 0
    for stage in range(levels):
        shift |= ((slot >> (levels - 1 - stage)) & 1) << order[stage]
    return shift


def slot_owner(n, slot, gx, gy):
    first, second = (slot_shift(slot, order) for order in bit_orders(n))
    return gx ^ jnp.where(gy == 0, first, second)


def exchange(value, n, cores, stage):
    orders = bit_orders(n)
    pairs = []
    for gx in range(n):
        for gy in range(cores):
            other = gx ^ (1 << orders[gy % 2][stage])
            pairs.append((gx * cores + gy, other * cores + gy))
    return lax.ppermute(value, ("gx", "gy"), pairs)


def project_kernel(n, tile, chunk, *refs):
    first = chunk == 0
    if first:
        tokens_ref, gain_ref, wq_ref, wk_ref, wv_ref, send_ref, keep_ref, x_ref = refs[:8]
    else:
        x_ref, wq_ref, wk_ref, wv_ref, send_ref, keep_ref = refs[:6]
    wq_buf, wk_buf, wv_buf, sems = refs[-4:]
    rows, half = 2 * send_ref.shape[0], send_ref.shape[0]
    depth = wq_ref.shape[0]
    tiles = wq_buf.shape[0]
    kv = wk_buf.shape[1]
    cols = tiles * tile

    def q_copy(i):
        return pltpu.make_async_copy(
            wq_ref.at[:, pl.ds(pl.multiple_of(chunk * cols + i * tile, tile), tile)],
            wq_buf.at[i],
            sems.at[i],
        )

    k_copy = pltpu.make_async_copy(
        wk_ref.at[:, pl.ds(chunk * kv, kv)], wk_buf, sems.at[tiles]
    )
    v_copy = pltpu.make_async_copy(
        wv_ref.at[:, pl.ds(chunk * kv, kv)], wv_buf, sems.at[tiles + 1]
    )
    for i in range(min(AHEAD, tiles)):
        q_copy(i).start()

    extra = cols + 2 * kv
    if first:
        block = rows // n
        me = lax.axis_index("gx")
        gy = lax.axis_index("gy")
        lanes = lax.broadcasted_iota(jnp.int32, (block, 128), 1)
        for slot in range(n):
            start = pl.multiple_of(slot_owner(n, slot, me, gy) * block, block)
            wide = tokens_ref[pl.ds(start, block), :].astype(jnp.float32)
            x_ref[slot * block : (slot + 1) * block, :] = (wide * gain_ref[...]).astype(jnp.bfloat16)
            square = jnp.sum(wide * wide, axis=1, keepdims=True)
            high = square.astype(jnp.bfloat16).astype(jnp.float32)
            rest = square - high
            middle = rest.astype(jnp.bfloat16).astype(jnp.float32)
            low = rest - middle
            packed = jnp.where(
                lanes == 3 * me,
                high,
                jnp.where(lanes == 3 * me + 1, middle, jnp.where(lanes == 3 * me + 2, low, 0.0)),
            )
            if slot < n // 2:
                keep_ref[slot * block : (slot + 1) * block, extra : extra + 128] = packed
            else:
                at = (slot - n // 2) * block
                send_ref[at : at + block, extra : extra + 128] = packed.astype(jnp.bfloat16)

    def emit(weights, start, width):
        product = jnp.dot(x_ref[...], weights, preferred_element_type=jnp.float32)
        keep_ref[:, pl.ds(start, width)] = product[:half]
        send_ref[:, pl.ds(start, width)] = product[half:].astype(jnp.bfloat16)

    @pl.loop(0, tiles)
    def _(i):
        q_copy(i).wait()

        @pl.when(i + AHEAD < tiles)
        def _():
            q_copy(i + AHEAD).start()

        @pl.when(i + AHEAD == tiles)
        def _():
            k_copy.start()
            v_copy.start()

        emit(wq_buf[i], pl.multiple_of(i * tile, tile), tile)

    k_copy.wait()
    emit(wk_buf[...], cols, kv)
    v_copy.wait()
    emit(wv_buf[...], cols + kv, kv)


def project(n, chunk, x, gain, w_query, w_key, w_value):
    rows, depth = x.shape
    cols = w_query.shape[1] // CHUNKS
    kv = w_key.shape[1] // CHUNKS
    tile = min(TILE, cols)
    tiles = cols // tile
    assert tiles >= AHEAD
    first = chunk == 0
    width = cols + 2 * kv + (128 if first else 0)
    hbm = pl.BlockSpec(memory_space=pltpu.HBM)
    vmem = pl.BlockSpec(memory_space=pltpu.VMEM)
    out_shape = [
        jax.ShapeDtypeStruct((rows // 2, width), jnp.bfloat16),
        jax.ShapeDtypeStruct((rows // 2, width), jnp.float32),
    ]
    args = [x]
    in_specs = [vmem]
    if first:
        out_shape.append(jax.ShapeDtypeStruct((rows, depth), jnp.bfloat16))
        args.append(gain)
        in_specs.append(vmem)
    return pl.pallas_call(
        functools.partial(project_kernel, n, tile, chunk),
        out_shape=out_shape,
        in_specs=in_specs + [hbm] * 3,
        out_specs=[vmem] * len(out_shape),
        scratch_shapes=[
            pltpu.VMEM((tiles, depth, tile), jnp.bfloat16),
            pltpu.VMEM((depth, kv), jnp.bfloat16),
            pltpu.VMEM((depth, kv), jnp.bfloat16),
            pltpu.SemaphoreType.DMA((tiles + 2,)),
        ],
        compiler_params=pltpu.CompilerParams(vmem_limit_bytes=48 * MIB),
        cost_estimate=pl.CostEstimate(
            flops=2 * rows * depth * (cols + 2 * kv),
            bytes_accessed=2 * depth * (cols + 2 * kv) + 8 * rows * depth,
            transcendentals=0,
        ),
        name="project",
    )(*args, w_query, w_key, w_value)


def attend_kernel(chunk, stages, groups, heads, seqs, length_ref, *refs):
    sums, squares = refs[: stages + 1], refs[stages + 1 : 2 * stages + 2]
    cos_ref, sin_ref, k_ref, v_ref, out_ref, k_buf, v_buf, q_scr, o_scr, sems = refs[
        2 * stages + 2 :
    ]
    rows = seqs * NEW
    cols = groups * heads * HD
    kv = groups * HD
    seq_count = k_ref.shape[0]

    def copies(b):
        at = pl.ds(chunk * kv, kv)
        return (
            pltpu.make_async_copy(k_ref.at[b, :, at], k_buf.at[b], sems.at[0, b]),
            pltpu.make_async_copy(v_ref.at[b, :, at], v_buf.at[b], sems.at[1, b]),
        )

    for b in range(seq_count):
        for copy in copies(b):
            copy.start()

    scale = HD**-0.5
    slots = k_ref.shape[1]
    many = heads * NEW
    slot_ids = lax.broadcasted_iota(jnp.int32, (many, slots), 1)
    new_cols = lax.broadcasted_iota(jnp.int32, (many, rows), 1)
    new_rows = lax.broadcasted_iota(jnp.int32, (many, rows), 0) % NEW

    @pl.loop(0, seq_count // seqs)
    def _(step):
        mine = pl.ds(pl.multiple_of(step * rows, rows), rows)
        total_squares = squares[0][mine, :]
        for part in squares[1:]:
            total_squares = total_squares + part[mine, :].astype(jnp.float32)
        mean = jnp.sum(total_squares, axis=1, keepdims=True) / D
        row_scale = lax.rsqrt(mean + EPS)
        cosine, sine = cos_ref[mine, :], sin_ref[mine, :]

        def raw(start):
            value = sums[0][mine, start : start + HD]
            for part in sums[1:]:
                value = value + part[mine, start : start + HD].astype(jnp.float32)
            return value * row_scale

        def rotary(value):
            return value * cosine + pltpu.roll(value, HD // 2, 1) * sine

        for g in range(groups):
            for h in range(heads):
                turned = rotary(raw((g * heads + h) * HD))
                for s in range(seqs):
                    q_scr[s, h * NEW : (h + 1) * NEW, :] = turned[s * NEW : (s + 1) * NEW]
            new_keys = rotary(raw(cols + g * HD)).astype(jnp.bfloat16)
            new_values = raw(cols + (groups + g) * HD).astype(jnp.bfloat16)
            for s in range(seqs):
                b = step * seqs + s
                if g == 0:
                    for copy in copies(b):
                        copy.wait()
                length = length_ref[b]
                query = q_scr[s].astype(jnp.bfloat16)
                keys = k_buf[b, :, g * HD : (g + 1) * HD]
                values = v_buf[b, :, g * HD : (g + 1) * HD]
                old = lax.dot_general(
                    query, keys, (((1,), (1,)), ((), ())), preferred_element_type=jnp.float32
                )
                new = lax.dot_general(
                    query, new_keys, (((1,), (1,)), ((), ())), preferred_element_type=jnp.float32
                )
                old = jnp.where(slot_ids < length, old * scale, -1e30)
                seen = (new_cols >= s * NEW) & (new_cols <= s * NEW + new_rows)
                new = jnp.where(seen, new * scale, -1e30)
                top = jnp.maximum(
                    jnp.max(old, axis=1, keepdims=True), jnp.max(new, axis=1, keepdims=True)
                )
                old = jnp.exp(old - top)
                new = jnp.exp(new - top)
                total = jnp.sum(old, axis=1, keepdims=True) + jnp.sum(new, axis=1, keepdims=True)
                inverse = 1.0 / total
                mixed = jnp.dot(
                    (old * inverse).astype(jnp.bfloat16),
                    values,
                    preferred_element_type=jnp.float32,
                ) + jnp.dot(
                    (new * inverse).astype(jnp.bfloat16),
                    new_values,
                    preferred_element_type=jnp.float32,
                )
                for h in range(heads):
                    at = (g * heads + h) * HD
                    o_scr[s * NEW : (s + 1) * NEW, at : at + HD] = mixed[h * NEW : (h + 1) * NEW]
        out_ref[mine, :] = o_scr[...].astype(jnp.bfloat16)


def attend(chunk, sums, squares, cosine, sine, cache_keys, cache_values, lengths, square_col):
    seq_count, slots, kv_all = cache_keys.shape
    kv = kv_all // CHUNKS
    groups = kv // HD
    width = sums[0].shape[1]
    cols = width - 2 * kv - (128 if chunk == 0 else 0)
    heads = cols // kv
    seqs = min(4, seq_count)
    rows = seq_count * NEW
    stages = len(sums) - 1
    wide = pl.BlockSpec((rows, width), lambda i, _: (0, 0))
    square = pl.BlockSpec((rows, 128), lambda i, _: (0, square_col))
    turn = pl.BlockSpec((rows, HD), lambda i, _: (0, 0))
    cache = pl.BlockSpec(memory_space=pltpu.HBM)
    flops = 4 * seq_count * groups * heads * NEW * slots * HD
    return pl.pallas_call(
        functools.partial(attend_kernel, chunk, stages, groups, heads, seqs),
        out_shape=jax.ShapeDtypeStruct((rows, cols), jnp.bfloat16),
        grid_spec=pltpu.PrefetchScalarGridSpec(
            num_scalar_prefetch=1,
            grid=(1,),
            in_specs=[wide] * (stages + 1) + [square] * (stages + 1) + [turn] * 2 + [cache] * 2,
            out_specs=pl.BlockSpec((rows, cols), lambda i, _: (0, 0)),
            scratch_shapes=[
                pltpu.VMEM((seq_count, slots, kv), jnp.bfloat16),
                pltpu.VMEM((seq_count, slots, kv), jnp.bfloat16),
                pltpu.VMEM((seqs, heads * NEW, HD), jnp.float32),
                pltpu.VMEM((seqs * NEW, cols), jnp.float32),
                pltpu.SemaphoreType.DMA((2, seq_count)),
            ],
        ),
        compiler_params=pltpu.CompilerParams(vmem_limit_bytes=48 * MIB),
        cost_estimate=pl.CostEstimate(
            flops=flops,
            bytes_accessed=4 * seq_count * slots * kv,
            transcendentals=seq_count * groups * heads * NEW * slots,
        ),
        name="attend",
    )(lengths, *sums, *squares, cosine, sine, cache_keys, cache_values)


def combine_kernel(n, block, tile, chunk, *refs):
    pieces, refs = refs[:n], refs[n:]
    gx, gy = lax.axis_index("gx"), lax.axis_index("gy")
    moved = jnp.where(gy == 0, n // 2, 0)
    if chunk:
        before_ref, refs = refs[0], refs[1:]
    w_ref, outs, (x_buf, w_buf, w_sems, x_sems) = refs[0], refs[1:-4], refs[-4:]
    depth, tiles = x_buf.shape[1], w_buf.shape[0]
    half = x_buf.shape[0] // 2

    def w_copy(i):
        return pltpu.make_async_copy(
            w_ref.at[pl.ds(chunk * depth, depth), pl.ds(pl.multiple_of(i * tile, tile), tile)],
            w_buf.at[i],
            w_sems.at[i],
        )

    x_copies = []
    for slot, piece in enumerate(pieces):
        ref, at = piece
        start = pl.multiple_of((slot_owner(n, slot, gx, gy) ^ moved) * block, block)
        x_copies.append(
            pltpu.make_async_copy(
                ref.at[pl.ds(at, block), :], x_buf.at[pl.ds(start, block), :], x_sems.at[slot]
            )
        )
    for copy in x_copies:
        copy.start()
    for i in range(min(AHEAD, tiles)):
        w_copy(i).start()
    for copy in x_copies:
        copy.wait()

    @pl.loop(0, tiles)
    def _(i):
        w_copy(i).wait()

        @pl.when(i + AHEAD < tiles)
        def _():
            w_copy(i + AHEAD).start()

        at = pl.ds(pl.multiple_of(i * tile, tile), tile)
        product = jnp.dot(x_buf[...], w_buf[i], preferred_element_type=jnp.float32)
        if chunk:
            product = product + before_ref[:, at]
        if len(outs) == 1:
            outs[0][:, at] = product
        else:
            outs[0][:, at] = product[:half].astype(jnp.bfloat16)
            outs[1][:, at] = product[half:]


def combine(chunk, pieces, before, w_out):
    block = pieces[0].shape[0]
    n = sum(piece.shape[0] for piece in pieces) // block
    rows, depth = n * block, pieces[0].shape[1]
    cols = w_out.shape[1]
    tile = min(TILE, cols)
    tiles = cols // tile
    last = chunk == CHUNKS - 1
    hbm = pl.BlockSpec(memory_space=pltpu.HBM)
    vmem = pl.BlockSpec(memory_space=pltpu.VMEM)
    spans = [(p, at) for p, piece in enumerate(pieces) for at in range(0, piece.shape[0], block)]

    def body(*refs):
        arrays, rest = refs[: len(pieces)], refs[len(pieces) :]
        slots = [(arrays[p], at) for p, at in spans]
        combine_kernel(n, block, tile, chunk, *slots, *rest)

    if last:
        out_shape = [
            jax.ShapeDtypeStruct((rows // 2, cols), jnp.bfloat16),
            jax.ShapeDtypeStruct((rows // 2, cols), jnp.float32),
        ]
    else:
        out_shape = [jax.ShapeDtypeStruct((rows, cols), jnp.float32)]
    earlier = [] if chunk == 0 else [before]
    return pl.pallas_call(
        body,
        out_shape=out_shape,
        in_specs=[pl.BlockSpec(memory_space=pl.ANY)] * len(pieces)
        + [vmem] * len(earlier)
        + [hbm],
        out_specs=[vmem] * len(out_shape),
        scratch_shapes=[
            pltpu.VMEM((rows, depth), jnp.bfloat16),
            pltpu.VMEM((tiles, depth, tile), jnp.bfloat16),
            pltpu.SemaphoreType.DMA((tiles,)),
            pltpu.SemaphoreType.DMA((n,)),
        ],
        compiler_params=pltpu.CompilerParams(vmem_limit_bytes=48 * MIB),
        cost_estimate=pl.CostEstimate(
            flops=2 * rows * depth * cols,
            bytes_accessed=2 * depth * cols + 2 * rows * depth + 4 * rows * cols,
            transcendentals=0,
        ),
        name="combine",
    )(*pieces, *earlier, w_out)


def shards(
    tokens, norm_gain, w_query, w_key, w_value, w_out, cache_keys, cache_values, cache_lengths
):
    n = lax.axis_size("gx")
    cores = lax.axis_size("gy")
    levels = n.bit_length() - 1
    position = (cache_lengths[:, None] + jnp.arange(NEW, dtype=jnp.int32)[None, :]).reshape(-1)
    inverse = THETA ** (-2.0 * jnp.arange(HD // 2, dtype=jnp.float32) / HD)
    angles = position.astype(jnp.float32)[:, None] * inverse[None, :]
    cosine, sine = jnp.cos(angles), jnp.sin(angles)
    cosine = jnp.concatenate([cosine, cosine], axis=1)
    sine = jnp.concatenate([-sine, sine], axis=1)

    x, gain = tokens, norm_gain[None, :]
    gathered = []
    squares = None
    for chunk in range(CHUNKS):
        out = project(n, chunk, x, gain, w_query, w_key, w_value)
        send, keep = out[:2]
        if chunk == 0:
            x = out[2]
        sums = [keep]
        rows = keep.shape[0]
        for stage in range(levels):
            sums.append(exchange(send, n, cores, stage))
            if stage < levels - 1:
                low = rows // 2
                value = sums[0][low:rows]
                for part in sums[1:]:
                    value = value + part[low:rows].astype(jnp.float32)
                send = value.astype(jnp.bfloat16)
                rows = low
        if chunk == 0:
            squares = sums
            square_col = keep.shape[1] // 128 - 1
        attention = attend(
            chunk, sums, squares, cosine, sine, cache_keys, cache_values, cache_lengths, square_col
        )
        pieces = [attention]
        for stage in reversed(range(levels)):
            send = pieces[0] if len(pieces) == 1 else jnp.concatenate(pieces, axis=0)
            pieces.append(exchange(send, n, cores, stage))
        gathered.append(pieces)
    result = None
    for chunk in range(CHUNKS):
        result = combine(chunk, gathered[chunk], result and result[0], w_out)
    send, keep = result
    other = lax.ppermute(send, "gy", [(0, 1), (1, 0)])
    return (keep + other.astype(jnp.float32)).astype(jnp.bfloat16)


def solution(mesh):
    return jax.shard_map(
        shards,
        mesh=mesh,
        in_specs=(
            P("groups", "gx"),
            P("gx"),
            P("gx", "gy"),
            P("gx", "gy"),
            P("gx", "gy"),
            P("gy", "gx"),
            P(("groups", "gx"), None, "gy"),
            P(("groups", "gx"), None, "gy"),
            P(("groups", "gx")),
        ),
        out_specs=P(("groups", "gy"), "gx"),
        check_vma=False,
    )
```

profile of v0, /device:TPU:0, one launch (start us, length us, event | category | flops | bytes accessed | tf_op | source)
XLA Modules:
  0.0 101.3 jit_solution(1117857158647722756)
XLA Ops:
  0.0 0.0 copy-start
  0.0 1.2 %copy-done = bf16[2048,256]{1,0:T(8,128)(2,1)S(1)} copy-done((bf16[2048,256]{1,0:T(8,128)(2,1)S(1)}, bf16[2048,256]{1,0:T(8,128)(2,1)}, u32[]{:S(2)}) %copy-start) | copy-done | bytes 1048600
  1.2 0.0 copy-start.2
  1.2 1.2 %copy-done.2 = bf16[2048,256]{1,0:T(8,128)(2,1)S(1)} copy-done((bf16[2048,256]{1,0:T(8,128)(2,1)S(1)}, bf16[2048,256]{1,0:T(8,128)(2,1)}, u32[]{:S(2)}) %copy-start.2) | copy-done | bytes 1048600
  2.5 0.0 copy-start.4
  2.5 1.2 %copy-done.4 = bf16[256,2048]{1,0:T(8,128)(2,1)S(1)} copy-done((bf16[256,2048]{1,0:T(8,128)(2,1)S(1)}, bf16[256,2048]{1,0:T(8,128)(2,1)}, u32[]{:S(2)}) %copy-start.4) | copy-done | bytes 1048600
  3.7 0.0 copy-start.5
  3.7 0.7 copy-done.5
  4.4 0.0 copy-start.1
  4.4 0.0 copy-start.3
  4.4 7.3 %project.2 = (bf16[128,2432]{1,0:T(8,128)(2,1)}, f32[128,2432]{1,0:T(8,128)S(1)}, bf16[256,2048]{1,0:T(8,128)(2,1)S(1)}) custom-call(bf16[256,2048]{1,0:T(8,128)(2,1)S(1)} %copy-done.4, f32[1,2048]{1,0:T(1,128)S(1)} %bitcast.1, bf16[2048,4096]{1,0:T(8,128)(2,1)} %refs_1_.1, bf16[2048,256]{1,0:T(8,128)(2,1)S(1)} %copy-done, bf16[2048,256]{1,0:T(8,128)(2,1)S(1)} %copy-done.2), custom_call_target="tpu_custom_call" | custom-call | flops 2415919104 | bytes 13631488 | tf_op jit(solution)/shard_map/project/pallas_call | solution.py:156
  11.7 3.0 %collective-permute-start.3 = (bf16[128,2432]{1,0:T(8,128)(2,1)}, bf16[128,2432]{1,0:T(8,128)(2,1)S(1)}, u32[]{:S(2)}, u32[]{:S(2)}) collective-permute-start(bf16[128,2432]{1,0:T(8,128)(2,1)} %get-tuple-element.16), channel_id=1, source_target_pairs={{0,2},{1,5},{2,0},{3,7},{4,6},{5,1},{6,4},{7,3},{8,10},{9,13},{10,... | collective-permute-start | bytes 1867784 | tf_op jit(solution)/shard_map/ppermute | solution.py:51
  14.7 0.0 copy-done.1
  14.7 0.0 copy-done.3
  14.7 0.0 copy-start.6
  14.7 6.9 %project.3 = (bf16[128,2304]{1,0:T(8,128)(2,1)}, f32[128,2304]{1,0:T(8,128)S(1)}) custom-call(bf16[256,2048]{1,0:T(8,128)(2,1)S(1)} %get-tuple-element.12.refs_0_, bf16[2048,4096]{1,0:T(8,128)(2,1)} %refs_1_.1, bf16[2048,256]{1,0:T(8,128)(2,1)S(1)} %copy-done.1, bf16[2048,256]{1,0:T(8,128)(2,1)S(1)} %copy-done.3), custom_call_target="tpu_custom_call" | custom-call | flops 2415919104 | bytes 13631488 | tf_op jit(solution)/shard_map/project/pallas_call | solution.py:156
  21.6 0.1 collective-permute-start
  21.7 0.0 copy-done.6
  21.7 0.1 add_convert_fusion.5
  21.8 0.1 convert_element_type.57
  21.9 0.1 fusion
  22.1 1.1 %collective-permute-done.3.refs_5_.refs_1_ = bf16[128,2432]{1,0:T(8,128)(2,1)S(1)} collective-permute-done((bf16[128,2432]{1,0:T(8,128)(2,1)}, bf16[128,2432]{1,0:T(8,128)(2,1)S(1)}, u32[]{:S(2)}, u32[]{:S(2)}) %collective-permute-start.3) | collective-permute-done | bytes 622624 | tf_op jit(solution)/shard_map/ppermute | solution.py:51
  23.2 0.1 add_convert_fusion.1
  23.2 2.1 %collective-permute-start.4 = (bf16[64,2432]{1,0:T(8,128)(2,1)S(1)}, bf16[64,2432]{1,0:T(8,128)(2,1)S(1)}, u32[]{:S(2)}, u32[]{:S(2)}) collective-permute-start(bf16[64,2432]{1,0:T(8,128)(2,1)S(1)} %add_convert_fusion.1), channel_id=1, source_target_pairs={{0,4},{1,3},{2,6},{3,1},{4,0},{5,7},{6,2},{7,5},{8,12},{9,11},{10,... | collective-permute-start | bytes 933896 | tf_op jit(solution)/shard_map/ppermute | solution.py:51
  25.4 9.6 %collective-permute-done.refs_1_ = bf16[128,2304]{1,0:T(8,128)(2,1)} collective-permute-done((bf16[128,2304]{1,0:T(8,128)(2,1)}, bf16[128,2304]{1,0:T(8,128)(2,1)}, u32[]{:S(2)}, u32[]{:S(2)}) %collective-permute-start) | collective-permute-done | bytes 589856 | tf_op jit(solution)/shard_map/ppermute | solution.py:51
  34.9 1.0 add_convert_fusion.2
  36.0 1.8 %collective-permute-start.1 = (bf16[64,2304]{1,0:T(8,128)(2,1)S(1)}, bf16[64,2304]{1,0:T(8,128)(2,1)S(1)}, u32[]{:S(2)}, u32[]{:S(2)}) collective-permute-start(bf16[64,2304]{1,0:T(8,128)(2,1)S(1)} %add_convert_fusion.2), channel_id=1, source_target_pairs={{0,4},{1,3},{2,6},{3,1},{4,0},{5,7},{6,2},{7,5},{8,12},{9,11},{10,... | collective-permute-start | bytes 884744 | tf_op jit(solution)/shard_map/ppermute | solution.py:51
  37.8 0.0 collective-permute-done.4.refs_6_.refs_2_
  37.8 0.1 add_convert_fusion.3
  37.8 2.7 %collective-permute-start.5 = (bf16[32,2432]{1,0:T(8,128)(2,1)S(1)}, bf16[32,2432]{1,0:T(8,128)(2,1)S(1)}, u32[]{:S(2)}, u32[]{:S(2)}) collective-permute-start(bf16[32,2432]{1,0:T(8,128)(2,1)S(1)} %add_convert_fusion.3), channel_id=1, source_target_pairs={{0,8},{1,9},{2,10},{3,11},{4,12},{5,13},{6,14},{7,15},{8,0},{9,1},... | collective-permute-start | bytes 466952 | tf_op jit(solution)/shard_map/ppermute | solution.py:51
  40.5 5.8 %collective-permute-done.1.refs_2_ = bf16[64,2304]{1,0:T(8,128)(2,1)S(1)} collective-permute-done((bf16[64,2304]{1,0:T(8,128)(2,1)S(1)}, bf16[64,2304]{1,0:T(8,128)(2,1)S(1)}, u32[]{:S(2)}, u32[]{:S(2)}) %collective-permute-start.1) | collective-permute-done | bytes 294944 | tf_op jit(solution)/shard_map/ppermute | solution.py:51
  46.3 1.0 add_convert_fusion.4
  47.3 0.7 collective-permute-start.2
  48.0 0.1 pad_maximum_fusion.4
  48.1 0.0 collective-permute-done.5.refs_7_.refs_3_
  48.1 6.7 %attend.3.refs_0_ = bf16[32,2048]{1,0:T(8,128)(2,1)S(1)} custom-call(s32[8]{0:T(128)S(1)} %copy-done.6, f32[128,2432]{1,0:T(8,128)S(1)} %get-tuple-element.15.refs_4_.refs_0_, bf16[128,2432]{1,0:T(8,128)(2,1)S(1)} %collective-permute-done.3.refs_5_.refs_1_, bf16[64,2432]{1,0:T(8,128)(2,1)S(1)} %collective-permute-done.4.refs_6_.refs_2_, ...), custom_call_target="tpu_custom_call" | custom-call | flops 268435456 | bytes 4194304 | tf_op jit(solution)/shard_map/attend/pallas_call | solution.py:286
  54.8 2.3 %collective-permute-start.9 = (bf16[32,2048]{1,0:T(8,128)(2,1)S(1)}, bf16[32,2048]{1,0:T(8,128)(2,1)S(1)}, u32[]{:S(2)}, u32[]{:S(2)}) collective-permute-start(bf16[32,2048]{1,0:T(8,128)(2,1)S(1)} %attend.3.refs_0_), channel_id=1, source_target_pairs={{0,8},{1,9},{2,10},{3,11},{4,12},{5,13},{6,14},{7,15},{8,0},{9,1},... | collective-permute-start | bytes 393224 | tf_op jit(solution)/shard_map/ppermute | solution.py:51
  57.1 0.3 collective-permute-done.2.refs_3_
  57.4 7.6 %attend.2.refs_0_ = bf16[32,2048]{1,0:T(8,128)(2,1)S(1)} custom-call(s32[8]{0:T(128)S(1)} %copy-done.6, f32[128,2304]{1,0:T(8,128)S(1)} %get-tuple-element.13.refs_0_, bf16[128,2304]{1,0:T(8,128)(2,1)} %collective-permute-done.refs_1_, bf16[64,2304]{1,0:T(8,128)(2,1)S(1)} %collective-permute-done.1.refs_2_, ...), custom_call_target="tpu_custom_call" | custom-call | flops 268435456 | bytes 4194304 | tf_op jit(solution)/shard_map/attend/pallas_call | solution.py:286
  65.0 0.4 collective-permute-start.6
  65.4 0.0 collective-permute-done.9.refs_1_
  65.4 2.5 %collective-permute-start.10 = (bf16[64,2048]{1,0:T(8,128)(2,1)S(1)}, bf16[64,2048]{1,0:T(8,128)(2,1)S(1)}, u32[]{:S(2)}, u32[]{:S(2)}) collective-permute-start(bf16[64,2048]{1,0:T(8,128)(2,1)S(1)} %pad_maximum_fusion.3), channel_id=1, source_target_pairs={{0,4},{1,3},{2,6},{3,1},{4,0},{5,7},{6,2},{7,5},{8,12},{9,11},{10,... | collective-permute-start | bytes 786440 | tf_op jit(solution)/shard_map/ppermute | solution.py:51
  68.0 3.7 %collective-permute-done.6.refs_1_ = bf16[32,2048]{1,0:T(8,128)(2,1)S(1)} collective-permute-done((bf16[32,2048]{1,0:T(8,128)(2,1)S(1)}, bf16[32,2048]{1,0:T(8,128)(2,1)S(1)}, u32[]{:S(2)}, u32[]{:S(2)}) %collective-permute-start.6) | collective-permute-done | bytes 131104 | tf_op jit(solution)/shard_map/ppermute | solution.py:51
  71.7 2.0 %collective-permute-start.7 = (bf16[64,2048]{1,0:T(8,128)(2,1)S(1)}, bf16[64,2048]{1,0:T(8,128)(2,1)S(1)}, u32[]{:S(2)}, u32[]{:S(2)}) collective-permute-start(bf16[64,2048]{1,0:T(8,128)(2,1)S(1)} %pad_maximum_fusion.2), channel_id=1, source_target_pairs={{0,4},{1,3},{2,6},{3,1},{4,0},{5,7},{6,2},{7,5},{8,12},{9,11},{10,... | collective-permute-start | bytes 786440 | tf_op jit(solution)/shard_map/ppermute | solution.py:51
  73.7 2.8 %collective-permute-done.10.refs_2_ = bf16[64,2048]{1,0:T(8,128)(2,1)S(1)} collective-permute-done((bf16[64,2048]{1,0:T(8,128)(2,1)S(1)}, bf16[64,2048]{1,0:T(8,128)(2,1)S(1)}, u32[]{:S(2)}, u32[]{:S(2)}) %collective-permute-start.10) | collective-permute-done | bytes 262176 | tf_op jit(solution)/shard_map/ppermute | solution.py:51
  76.6 0.2 collective-permute-start.11
  76.7 5.4 %collective-permute-done.7.refs_2_ = bf16[64,2048]{1,0:T(8,128)(2,1)S(1)} collective-permute-done((bf16[64,2048]{1,0:T(8,128)(2,1)S(1)}, bf16[64,2048]{1,0:T(8,128)(2,1)S(1)}, u32[]{:S(2)}, u32[]{:S(2)}) %collective-permute-start.7) | collective-permute-done | bytes 262176 | tf_op jit(solution)/shard_map/ppermute | solution.py:51
  82.2 0.2 collective-permute-start.8
  82.3 3.5 %collective-permute-done.11.refs_3_ = bf16[128,2048]{1,0:T(8,128)(2,1)S(1)} collective-permute-done((bf16[128,2048]{1,0:T(8,128)(2,1)S(1)}, bf16[128,2048]{1,0:T(8,128)(2,1)S(1)}, u32[]{:S(2)}, u32[]{:S(2)}) %collective-permute-start.11) | collective-permute-done | bytes 524320 | tf_op jit(solution)/shard_map/ppermute | solution.py:51
  85.8 6.2 %combine.2.refs_4_ = f32[256,2048]{1,0:T(8,128)S(1)} custom-call(bf16[32,2048]{1,0:T(8,128)(2,1)S(1)} %attend.3.refs_0_, bf16[32,2048]{1,0:T(8,128)(2,1)S(1)} %collective-permute-done.9.refs_1_, bf16[64,2048]{1,0:T(8,128)(2,1)S(1)} %collective-permute-done.10.refs_2_, bf16[128,2048]{1,0:T(8,128)(2,1)S(1)} %collective-permute-done.11.refs_3_, ...), custom_call_target="tpu_custom_call" | custom-call | flops 2147483648 | bytes 11534336 | tf_op jit(solution)/shard_map/combine/pallas_call | solution.py:389
  92.1 0.0 collective-permute-done.8.refs_3_
  92.1 6.3 %combine.3 = (bf16[128,2048]{1,0:T(8,128)(2,1)S(1)}, f32[128,2048]{1,0:T(8,128)S(1)}) custom-call(bf16[32,2048]{1,0:T(8,128)(2,1)S(1)} %attend.2.refs_0_, bf16[32,2048]{1,0:T(8,128)(2,1)S(1)} %collective-permute-done.6.refs_1_, bf16[64,2048]{1,0:T(8,128)(2,1)S(1)} %collective-permute-done.7.refs_2_, bf16[128,2048]{1,0:T(8,128)(2,1)S(1)} %collective-permute-done.8.refs_3_, ...), custom_call_target="tpu_custom_call" | custom-call | flops 2147483648 | bytes 11534336 | tf_op jit(solution)/shard_map/combine/pallas_call | solution.py:389
  98.4 0.1 collective-permute-start.12
  98.5 1.9 %collective-permute-done.12 = bf16[128,2048]{1,0:T(8,128)(2,1)S(1)} collective-permute-done((bf16[128,2048]{1,0:T(8,128)(2,1)S(1)}, bf16[128,2048]{1,0:T(8,128)(2,1)S(1)}, u32[]{:S(2)}, u32[]{:S(2)}) %collective-permute-start.12) | collective-permute-done | bytes 524320 | tf_op jit(solution)/shard_map/ppermute | solution.py:459
  100.4 0.9 add_convert_fusion
  (5 shorter events, 0.1 us)
Async XLA Ops:
  0.0 1.2 %copy-start = (bf16[2048,256]{1,0:T(8,128)(2,1)S(1)}, bf16[2048,256]{1,0:T(8,128)(2,1)}, u32[]{:S(2)}) copy-start(bf16[2048,256]{1,0:T(8,128)(2,1)} %refs_2_.3) | copy-start | bytes 3145732
  1.2 1.2 %copy-start.2 = (bf16[2048,256]{1,0:T(8,128)(2,1)S(1)}, bf16[2048,256]{1,0:T(8,128)(2,1)}, u32[]{:S(2)}) copy-start(bf16[2048,256]{1,0:T(8,128)(2,1)} %refs_3_.3) | copy-start | bytes 3145732
  2.5 1.2 %copy-start.4 = (bf16[256,2048]{1,0:T(8,128)(2,1)S(1)}, bf16[256,2048]{1,0:T(8,128)(2,1)}, u32[]{:S(2)}) copy-start(bf16[256,2048]{1,0:T(8,128)(2,1)} %refs_0_.1) | copy-start | bytes 3145732
  3.7 0.7 copy-start.5
  4.4 10.4 %copy-start.1 = (bf16[2048,256]{1,0:T(8,128)(2,1)S(1)}, bf16[2048,256]{1,0:T(8,128)(2,1)}, u32[]{:S(2)}) copy-start(bf16[2048,256]{1,0:T(8,128)(2,1)} %refs_2_.3) | copy-start | bytes 3145732
  4.4 10.4 %copy-start.3 = (bf16[2048,256]{1,0:T(8,128)(2,1)S(1)}, bf16[2048,256]{1,0:T(8,128)(2,1)}, u32[]{:S(2)}) copy-start(bf16[2048,256]{1,0:T(8,128)(2,1)} %refs_3_.3) | copy-start | bytes 3145732
  11.7 11.5 %collective-permute-start.3 = (bf16[128,2432]{1,0:T(8,128)(2,1)}, bf16[128,2432]{1,0:T(8,128)(2,1)S(1)}, u32[]{:S(2)}, u32[]{:S(2)}) collective-permute-start(bf16[128,2432]{1,0:T(8,128)(2,1)} %get-tuple-element.16), channel_id=1, source_target_pairs={{0,2},{1,5},{2,0},{3,7},{4,6},{5,1},{6,4},{7,3},{8,10},{9,13},{10,... | collective-permute-start | bytes 1867784 | tf_op jit(solution)/shard_map/ppermute | solution.py:51
  14.7 7.0 %copy-start.6 = (s32[8]{0:T(128)S(1)}, s32[8]{0:T(128)}, u32[]{:S(2)}) copy-start(s32[8]{0:T(128)} %length_ref.3) | copy-start | bytes 100
  21.6 13.3 %collective-permute-start = (bf16[128,2304]{1,0:T(8,128)(2,1)}, bf16[128,2304]{1,0:T(8,128)(2,1)}, u32[]{:S(2)}, u32[]{:S(2)}) collective-permute-start(bf16[128,2304]{1,0:T(8,128)(2,1)} %get-tuple-element.14), channel_id=1, source_target_pairs={{0,2},{1,5},{2,0},{3,7},{4,6},{5,1},{6,4},{7,3},{8,10},{9,13},{10,... | collective-permute-start | bytes 1769480 | tf_op jit(solution)/shard_map/ppermute | solution.py:51
  23.2 14.6 %collective-permute-start.4 = (bf16[64,2432]{1,0:T(8,128)(2,1)S(1)}, bf16[64,2432]{1,0:T(8,128)(2,1)S(1)}, u32[]{:S(2)}, u32[]{:S(2)}) collective-permute-start(bf16[64,2432]{1,0:T(8,128)(2,1)S(1)} %add_convert_fusion.1), channel_id=1, source_target_pairs={{0,4},{1,3},{2,6},{3,1},{4,0},{5,7},{6,2},{7,5},{8,12},{9,11},{10,... | collective-permute-start | bytes 933896 | tf_op jit(solution)/shard_map/ppermute | solution.py:51
  36.0 10.3 %collective-permute-start.1 = (bf16[64,2304]{1,0:T(8,128)(2,1)S(1)}, bf16[64,2304]{1,0:T(8,128)(2,1)S(1)}, u32[]{:S(2)}, u32[]{:S(2)}) collective-permute-start(bf16[64,2304]{1,0:T(8,128)(2,1)S(1)} %add_convert_fusion.2), channel_id=1, source_target_pairs={{0,4},{1,3},{2,6},{3,1},{4,0},{5,7},{6,2},{7,5},{8,12},{9,11},{10,... | collective-permute-start | bytes 884744 | tf_op jit(solution)/shard_map/ppermute | solution.py:51
  37.8 10.2 %collective-permute-start.5 = (bf16[32,2432]{1,0:T(8,128)(2,1)S(1)}, bf16[32,2432]{1,0:T(8,128)(2,1)S(1)}, u32[]{:S(2)}, u32[]{:S(2)}) collective-permute-start(bf16[32,2432]{1,0:T(8,128)(2,1)S(1)} %add_convert_fusion.3), channel_id=1, source_target_pairs={{0,8},{1,9},{2,10},{3,11},{4,12},{5,13},{6,14},{7,15},{8,0},{9,1},... | collective-permute-start | bytes 466952 | tf_op jit(solution)/shard_map/ppermute | solution.py:51
  47.3 10.2 %collective-permute-start.2 = (bf16[32,2304]{1,0:T(8,128)(2,1)S(1)}, bf16[32,2304]{1,0:T(8,128)(2,1)S(1)}, u32[]{:S(2)}, u32[]{:S(2)}) collective-permute-start(bf16[32,2304]{1,0:T(8,128)(2,1)S(1)} %add_convert_fusion.4), channel_id=1, source_target_pairs={{0,8},{1,9},{2,10},{3,11},{4,12},{5,13},{6,14},{7,15},{8,0},{9,1},... | collective-permute-start | bytes 442376 | tf_op jit(solution)/shard_map/ppermute | solution.py:51
  54.8 10.7 %collective-permute-start.9 = (bf16[32,2048]{1,0:T(8,128)(2,1)S(1)}, bf16[32,2048]{1,0:T(8,128)(2,1)S(1)}, u32[]{:S(2)}, u32[]{:S(2)}) collective-permute-start(bf16[32,2048]{1,0:T(8,128)(2,1)S(1)} %attend.3.refs_0_), channel_id=1, source_target_pairs={{0,8},{1,9},{2,10},{3,11},{4,12},{5,13},{6,14},{7,15},{8,0},{9,1},... | collective-permute-start | bytes 393224 | tf_op jit(solution)/shard_map/ppermute | solution.py:51
  65.0 6.6 %collective-permute-start.6 = (bf16[32,2048]{1,0:T(8,128)(2,1)S(1)}, bf16[32,2048]{1,0:T(8,128)(2,1)S(1)}, u32[]{:S(2)}, u32[]{:S(2)}) collective-permute-start(bf16[32,2048]{1,0:T(8,128)(2,1)S(1)} %attend.2.refs_0_), channel_id=1, source_target_pairs={{0,8},{1,9},{2,10},{3,11},{4,12},{5,13},{6,14},{7,15},{8,0},{9,1},... | collective-permute-start | bytes 393224 | tf_op jit(solution)/shard_map/ppermute | solution.py:51
  65.4 11.1 %collective-permute-start.10 = (bf16[64,2048]{1,0:T(8,128)(2,1)S(1)}, bf16[64,2048]{1,0:T(8,128)(2,1)S(1)}, u32[]{:S(2)}, u32[]{:S(2)}) collective-permute-start(bf16[64,2048]{1,0:T(8,128)(2,1)S(1)} %pad_maximum_fusion.3), channel_id=1, source_target_pairs={{0,4},{1,3},{2,6},{3,1},{4,0},{5,7},{6,2},{7,5},{8,12},{9,11},{10,... | collective-permute-start | bytes 786440 | tf_op jit(solution)/shard_map/ppermute | solution.py:51
  71.7 10.4 %collective-permute-start.7 = (bf16[64,2048]{1,0:T(8,128)(2,1)S(1)}, bf16[64,2048]{1,0:T(8,128)(2,1)S(1)}, u32[]{:S(2)}, u32[]{:S(2)}) collective-permute-start(bf16[64,2048]{1,0:T(8,128)(2,1)S(1)} %pad_maximum_fusion.2), channel_id=1, source_target_pairs={{0,4},{1,3},{2,6},{3,1},{4,0},{5,7},{6,2},{7,5},{8,12},{9,11},{10,... | collective-permute-start | bytes 786440 | tf_op jit(solution)/shard_map/ppermute | solution.py:51
  76.6 9.2 %collective-permute-start.11 = (bf16[128,2048]{1,0:T(8,128)(2,1)S(1)}, bf16[128,2048]{1,0:T(8,128)(2,1)S(1)}, u32[]{:S(2)}, u32[]{:S(2)}) collective-permute-start(bf16[128,2048]{1,0:T(8,128)(2,1)S(1)} %pad_maximum_fusion.1), channel_id=1, source_target_pairs={{0,2},{1,5},{2,0},{3,7},{4,6},{5,1},{6,4},{7,3},{8,10},{9,13},{10,... | collective-permute-start | bytes 1572872 | tf_op jit(solution)/shard_map/ppermute | solution.py:51
  82.2 9.9 %collective-permute-start.8 = (bf16[128,2048]{1,0:T(8,128)(2,1)S(1)}, bf16[128,2048]{1,0:T(8,128)(2,1)S(1)}, u32[]{:S(2)}, u32[]{:S(2)}) collective-permute-start(bf16[128,2048]{1,0:T(8,128)(2,1)S(1)} %pad_maximum_fusion), channel_id=1, source_target_pairs={{0,2},{1,5},{2,0},{3,7},{4,6},{5,1},{6,4},{7,3},{8,10},{9,13},{10,... | collective-permute-start | bytes 1572872 | tf_op jit(solution)/shard_map/ppermute | solution.py:51
  98.4 2.0 %collective-permute-start.12 = (bf16[128,2048]{1,0:T(8,128)(2,1)S(1)}, bf16[128,2048]{1,0:T(8,128)(2,1)S(1)}, u32[]{:S(2)}, u32[]{:S(2)}) collective-permute-start(bf16[128,2048]{1,0:T(8,128)(2,1)S(1)} %get-tuple-element.18), channel_id=1, source_target_pairs={{0,1},{1,0},{2,3},{3,2},{4,5},{5,4},{6,7},{7,6},{8,9},{9,8},{10,11... | collective-permute-start | bytes 1572872 | tf_op jit(solution)/shard_map/ppermute | solution.py:459
where the time goes:
time: 102 us; the launch traced here: 101 us
  Pallas kernels  41 us (40%)
  waiting for transfers between devices  34.1 us (33%)
  starting transfers between devices  18.2 us (18%)
  local copies, waits for them, and re-layouts  4.46 us (4%)
  other arithmetic  3.41 us (3%)
    ppermute x12, waiting for transfers between devices, exchange(): return lax.ppermute(value, ('gx', 'gy'), pairs)  32.2 us
    ppermute x12, starting transfers between devices, exchange(): return lax.ppermute(value, ('gx', 'gy'), pairs)  18.1 us
    pallas_call x2, Pallas kernels, attend(): pl.pallas_call(functools.partial(attend_kernel, chunk, stages, groups, he...  14.3 us
    pallas_call x2, Pallas kernels, project(): pl.pallas_call(functools.partial(project_kernel, n, tile, chunk), out_sha...  14.2 us
    pallas_call x2, Pallas kernels, combine(): pl.pallas_call(body, out_shape=out_shape, in_specs=[pl.BlockSpec(memory_s...  12.6 us
    unnamed x14, local copies, waits for them, and re-layouts  4.38 us
    convert_element_type x4, other arithmetic, shards(): send = value.astype(jnp.bfloat16)  2.09 us
  transfers between devices with their start and end apart: 13, of which 9 were waited for; matrix products, arithmetic and copies ran while one was open for 3% of the time, Pallas kernels for 27%

commit v1 on v0

--- a/solution.py
+++ b/solution.py
@@ -1,4 +1,5 @@
 import functools
+import math
 
 import jax
 import jax.numpy as jnp
@@ -14,8 +15,7 @@
 THETA = 500000.0
 
 CHUNKS = 2
-TILE = 256
-AHEAD = 4
+PARTS = 2
 MIB = 1 << 20
 
 
@@ -51,44 +51,57 @@
     return lax.ppermute(value, ("gx", "gy"), pairs)
 
 
-def project_kernel(n, tile, chunk, *refs):
+def project_kernel(n, parts, chunk, *refs):
     first = chunk == 0
     if first:
         tokens_ref, gain_ref, wq_ref, wk_ref, wv_ref, send_ref, keep_ref, x_ref = refs[:8]
+        t_buf, t_sems = refs[8:10]
     else:
         x_ref, wq_ref, wk_ref, wv_ref, send_ref, keep_ref = refs[:6]
-    wq_buf, wk_buf, wv_buf, sems = refs[-4:]
-    rows, half = 2 * send_ref.shape[0], send_ref.shape[0]
-    depth = wq_ref.shape[0]
-    tiles = wq_buf.shape[0]
-    kv = wk_buf.shape[1]
-    cols = tiles * tile
-
-    def q_copy(i):
+    w_buf, sems = refs[-2:]
+    half = send_ref.shape[0]
+    rows = 2 * half
+    kv = wk_ref.shape[1] // CHUNKS
+    cols = wq_ref.shape[1] // CHUNKS
+    part = cols // parts
+    tile = part // 2
+
+    def w_copy(ref, start, width, at, sem):
         return pltpu.make_async_copy(
-            wq_ref.at[:, pl.ds(pl.multiple_of(chunk * cols + i * tile, tile), tile)],
-            wq_buf.at[i],
-            sems.at[i],
+            ref.at[:, start : start + width], w_buf.at[:, at : at + width], sems.at[sem]
         )
 
-    k_copy = pltpu.make_async_copy(
-        wk_ref.at[:, pl.ds(chunk * kv, kv)], wk_buf, sems.at[tiles]
-    )
-    v_copy = pltpu.make_async_copy(
-        wv_ref.at[:, pl.ds(chunk * kv, kv)], wv_buf, sems.at[tiles + 1]
-    )
-    for i in range(min(AHEAD, tiles)):
-        q_copy(i).start()
-
-    extra = cols + 2 * kv
+    copies = [
+        [
+            w_copy(wq_ref, chunk * cols + at, tile, at, at // tile)
+            for at in range(p * part, (p + 1) * part, tile)
+        ]
+        for p in range(parts)
+    ]
+    copies[-1].append(w_copy(wk_ref, chunk * kv, kv, cols, 2 * parts))
+    copies[-1].append(w_copy(wv_ref, chunk * kv, kv, cols + kv, 2 * parts + 1))
+
     if first:
         block = rows // n
-        me = lax.axis_index("gx")
-        gy = lax.axis_index("gy")
+        me, gy = lax.axis_index("gx"), lax.axis_index("gy")
+        t_copies = []
+        for slot in range(n):
+            start = pl.multiple_of(slot_owner(n, slot, me, gy) * block, block)
+            t_copies.append(
+                pltpu.make_async_copy(
+                    tokens_ref.at[pl.ds(start, block), :], t_buf.at[slot], t_sems.at[slot]
+                )
+            )
+            t_copies[-1].start()
+    for group in copies:
+        for copy in group:
+            copy.start()
+    if first:
+        extra = cols + 2 * kv
         lanes = lax.broadcasted_iota(jnp.int32, (block, 128), 1)
         for slot in range(n):
-            start = pl.multiple_of(slot_owner(n, slot, me, gy) * block, block)
-            wide = tokens_ref[pl.ds(start, block), :].astype(jnp.float32)
+            t_copies[slot].wait()
+            wide = t_buf[slot].astype(jnp.float32)
             x_ref[slot * block : (slot + 1) * block, :] = (wide * gain_ref[...]).astype(jnp.bfloat16)
             square = jnp.sum(wide * wide, axis=1, keepdims=True)
             high = square.astype(jnp.bfloat16).astype(jnp.float32)
@@ -106,39 +119,23 @@
                 at = (slot - n // 2) * block
                 send_ref[at : at + block, extra : extra + 128] = packed.astype(jnp.bfloat16)
 
-    def emit(weights, start, width):
-        product = jnp.dot(x_ref[...], weights, preferred_element_type=jnp.float32)
-        keep_ref[:, pl.ds(start, width)] = product[:half]
-        send_ref[:, pl.ds(start, width)] = product[half:].astype(jnp.bfloat16)
-
-    @pl.loop(0, tiles)
-    def _(i):
-        q_copy(i).wait()
-
-        @pl.when(i + AHEAD < tiles)
-        def _():
-            q_copy(i + AHEAD).start()
-
-        @pl.when(i + AHEAD == tiles)
-        def _():
-            k_copy.start()
-            v_copy.start()
-
-        emit(wq_buf[i], pl.multiple_of(i * tile, tile), tile)
-
-    k_copy.wait()
-    emit(wk_buf[...], cols, kv)
-    v_copy.wait()
-    emit(wv_buf[...], cols + kv, kv)
+    for p in range(parts):
+        for copy in copies[p]:
+            copy.wait()
+        start, end = p * part, (p + 1) * part if p < parts - 1 else cols + 2 * kv
+        product = jnp.dot(x_ref[...], w_buf[:, start:end], preferred_element_type=jnp.float32)
+        keep_ref[:, start:end] = product[:half]
+        send_ref[:, start:end] = product[half:].astype(jnp.bfloat16)
+
+
+def in_hbm(value):
+    return pltpu.with_memory_space_constraint(value, pltpu.HBM)
 
 
 def project(n, chunk, x, gain, w_query, w_key, w_value):
     rows, depth = x.shape
     cols = w_query.shape[1] // CHUNKS
     kv = w_key.shape[1] // CHUNKS
-    tile = min(TILE, cols)
-    tiles = cols // tile
-    assert tiles >= AHEAD
     first = chunk == 0
     width = cols + 2 * kv + (128 if first else 0)
     hbm = pl.BlockSpec(memory_space=pltpu.HBM)
@@ -147,31 +144,34 @@
         jax.ShapeDtypeStruct((rows // 2, width), jnp.bfloat16),
         jax.ShapeDtypeStruct((rows // 2, width), jnp.float32),
     ]
-    args = [x]
-    in_specs = [vmem]
+    scratch = [
+        pltpu.VMEM((depth, cols + 2 * kv), jnp.bfloat16),
+        pltpu.SemaphoreType.DMA((2 * PARTS + 2,)),
+    ]
     if first:
         out_shape.append(jax.ShapeDtypeStruct((rows, depth), jnp.bfloat16))
-        args.append(gain)
-        in_specs.append(vmem)
+        args = [in_hbm(x), in_hbm(gain)]
+        in_specs = [hbm, vmem]
+        scratch = [
+            pltpu.VMEM((n, rows // n, depth), jnp.bfloat16),
+            pltpu.SemaphoreType.DMA((n,)),
+        ] + scratch
+    else:
+        args, in_specs = [x], [vmem]
     return pl.pallas_call(
-        functools.partial(project_kernel, n, tile, chunk),
+        functools.partial(project_kernel, n, PARTS, chunk),
         out_shape=out_shape,
         in_specs=in_specs + [hbm] * 3,
         out_specs=[vmem] * len(out_shape),
-        scratch_shapes=[
-            pltpu.VMEM((tiles, depth, tile), jnp.bfloat16),
-            pltpu.VMEM((depth, kv), jnp.bfloat16),
-            pltpu.VMEM((depth, kv), jnp.bfloat16),
-            pltpu.SemaphoreType.DMA((tiles + 2,)),
-        ],
-        compiler_params=pltpu.CompilerParams(vmem_limit_bytes=48 * MIB),
+        scratch_shapes=scratch,
+        compiler_params=pltpu.CompilerParams(vmem_limit_bytes=28 * MIB),
         cost_estimate=pl.CostEstimate(
             flops=2 * rows * depth * (cols + 2 * kv),
             bytes_accessed=2 * depth * (cols + 2 * kv) + 8 * rows * depth,
             transcendentals=0,
         ),
         name="project",
-    )(*args, w_query, w_key, w_value)
+    )(*args, in_hbm(w_query), in_hbm(w_key), in_hbm(w_value))
 
 
 def attend_kernel(chunk, stages, groups, heads, seqs, length_ref, *refs):
@@ -184,21 +184,21 @@
     kv = groups * HD
     seq_count = k_ref.shape[0]
 
-    def copies(b):
-        at = pl.ds(chunk * kv, kv)
-        return (
-            pltpu.make_async_copy(k_ref.at[b, :, at], k_buf.at[b], sems.at[0, b]),
-            pltpu.make_async_copy(v_ref.at[b, :, at], v_buf.at[b], sems.at[1, b]),
+    def cache_copy(kind, b):
+        source, target = ((k_ref, k_buf), (v_ref, v_buf))[kind]
+        return pltpu.make_async_copy(
+            source.at[b, :, pl.ds(chunk * kv, kv)], target.at[b], sems.at[kind, b]
         )
 
-    for b in range(seq_count):
-        for copy in copies(b):
-            copy.start()
-
-    scale = HD**-0.5
+    for start in range(0, seq_count, seqs):
+        for kind in range(2):
+            for b in range(start, start + seqs):
+                cache_copy(kind, b).start()
+
+    scale = HD**-0.5 * math.log2(math.e)
     slots = k_ref.shape[1]
     many = heads * NEW
-    slot_ids = lax.broadcasted_iota(jnp.int32, (many, slots), 1)
+    slot_ids = lax.broadcasted_iota(jnp.int32, (1, slots), 1)
     new_cols = lax.broadcasted_iota(jnp.int32, (many, rows), 1)
     new_rows = lax.broadcasted_iota(jnp.int32, (many, rows), 0) % NEW
 
@@ -221,50 +221,57 @@
         def rotary(value):
             return value * cosine + pltpu.roll(value, HD // 2, 1) * sine
 
+        for h in range(heads * groups):
+            turned = rotary(raw(h * HD))
+            for s in range(seqs):
+                q_scr[s, h * NEW : (h + 1) * NEW, :] = turned[s * NEW : (s + 1) * NEW]
+        for s in range(seqs):
+            cache_copy(0, step * seqs + s).wait()
+            cache_copy(1, step * seqs + s).wait()
         for g in range(groups):
-            for h in range(heads):
-                turned = rotary(raw((g * heads + h) * HD))
-                for s in range(seqs):
-                    q_scr[s, h * NEW : (h + 1) * NEW, :] = turned[s * NEW : (s + 1) * NEW]
             new_keys = rotary(raw(cols + g * HD)).astype(jnp.bfloat16)
             new_values = raw(cols + (groups + g) * HD).astype(jnp.bfloat16)
+            lanes = slice(g * HD, (g + 1) * HD)
+            olds, news, mixes = [], [], []
             for s in range(seqs):
-                b = step * seqs + s
-                if g == 0:
-                    for copy in copies(b):
-                        copy.wait()
-                length = length_ref[b]
-                query = q_scr[s].astype(jnp.bfloat16)
-                keys = k_buf[b, :, g * HD : (g + 1) * HD]
-                values = v_buf[b, :, g * HD : (g + 1) * HD]
-                old = lax.dot_general(
-                    query, keys, (((1,), (1,)), ((), ())), preferred_element_type=jnp.float32
+                query = q_scr[s, g * many : (g + 1) * many, :].astype(jnp.bfloat16)
+                keys = k_buf[step * seqs + s, :, lanes]
+                olds.append(
+                    lax.dot_general(
+                        query, keys, (((1,), (1,)), ((), ())), preferred_element_type=jnp.float32
+                    )
                 )
-                new = lax.dot_general(
-                    query, new_keys, (((1,), (1,)), ((), ())), preferred_element_type=jnp.float32
+                news.append(
+                    lax.dot_general(
+                        query, new_keys, (((1,), (1,)), ((), ())), preferred_element_type=jnp.float32
+                    )
                 )
-                old = jnp.where(slot_ids < length, old * scale, -1e30)
+            for s in range(seqs):
+                live = slot_ids < length_ref[step * seqs + s]
                 seen = (new_cols >= s * NEW) & (new_cols <= s * NEW + new_rows)
-                new = jnp.where(seen, new * scale, -1e30)
+                old = jnp.where(live, olds[s] * scale, -1e30)
+                new = jnp.where(seen, news[s] * scale, -1e30)
                 top = jnp.maximum(
                     jnp.max(old, axis=1, keepdims=True), jnp.max(new, axis=1, keepdims=True)
                 )
-                old = jnp.exp(old - top)
-                new = jnp.exp(new - top)
+                old = jnp.exp2(old - top)
+                new = jnp.exp2(new - top)
                 total = jnp.sum(old, axis=1, keepdims=True) + jnp.sum(new, axis=1, keepdims=True)
                 inverse = 1.0 / total
-                mixed = jnp.dot(
-                    (old * inverse).astype(jnp.bfloat16),
-                    values,
-                    preferred_element_type=jnp.float32,
-                ) + jnp.dot(
-                    (new * inverse).astype(jnp.bfloat16),
-                    new_values,
-                    preferred_element_type=jnp.float32,
+                olds[s] = (old * inverse).astype(jnp.bfloat16)
+                news[s] = (new * inverse).astype(jnp.bfloat16)
+            for s in range(seqs):
+                values = v_buf[step * seqs + s, :, lanes]
+                mixes.append(
+                    jnp.dot(olds[s], values, preferred_element_type=jnp.float32)
+                    + jnp.dot(news[s], new_values, preferred_element_type=jnp.float32)
                 )
+            for s in range(seqs):
                 for h in range(heads):
                     at = (g * heads + h) * HD
-                    o_scr[s * NEW : (s + 1) * NEW, at : at + HD] = mixed[h * NEW : (h + 1) * NEW]
+                    o_scr[s * NEW : (s + 1) * NEW, at : at + HD] = mixes[s][
+                        h * NEW : (h + 1) * NEW
+                    ]
         out_ref[mine, :] = o_scr[...].astype(jnp.bfloat16)
 
 
@@ -294,36 +301,38 @@
             scratch_shapes=[
                 pltpu.VMEM((seq_count, slots, kv), jnp.bfloat16),
                 pltpu.VMEM((seq_count, slots, kv), jnp.bfloat16),
-                pltpu.VMEM((seqs, heads * NEW, HD), jnp.float32),
+                pltpu.VMEM((seqs, groups * heads * NEW, HD), jnp.float32),
                 pltpu.VMEM((seqs * NEW, cols), jnp.float32),
                 pltpu.SemaphoreType.DMA((2, seq_count)),
             ],
         ),
-        compiler_params=pltpu.CompilerParams(vmem_limit_bytes=48 * MIB),
+        compiler_params=pltpu.CompilerParams(vmem_limit_bytes=24 * MIB),
         cost_estimate=pl.CostEstimate(
             flops=flops,
             bytes_accessed=4 * seq_count * slots * kv,
             transcendentals=seq_count * groups * heads * NEW * slots,
         ),
         name="attend",
-    )(lengths, *sums, *squares, cosine, sine, cache_keys, cache_values)
-
-
-def combine_kernel(n, block, tile, chunk, *refs):
+    )(lengths, *sums, *squares, cosine, sine, in_hbm(cache_keys), in_hbm(cache_values))
+
+
+def combine_kernel(n, block, chunk, *refs):
     pieces, refs = refs[:n], refs[n:]
     gx, gy = lax.axis_index("gx"), lax.axis_index("gy")
     moved = jnp.where(gy == 0, n // 2, 0)
     if chunk:
         before_ref, refs = refs[0], refs[1:]
     w_ref, outs, (x_buf, w_buf, w_sems, x_sems) = refs[0], refs[1:-4], refs[-4:]
-    depth, tiles = x_buf.shape[1], w_buf.shape[0]
+    depth, cols = w_buf.shape
     half = x_buf.shape[0] // 2
-
-    def w_copy(i):
+    part = cols // PARTS
+    tile = part // 2
+
+    def w_copy(at):
         return pltpu.make_async_copy(
-            w_ref.at[pl.ds(chunk * depth, depth), pl.ds(pl.multiple_of(i * tile, tile), tile)],
-            w_buf.at[i],
-            w_sems.at[i],
+            w_ref.at[chunk * depth : (chunk + 1) * depth, at : at + tile],
+            w_buf.at[:, at : at + tile],
+            w_sems.at[at // tile],
         )
 
     x_copies = []
@@ -337,21 +346,16 @@
         )
     for copy in x_copies:
         copy.start()
-    for i in range(min(AHEAD, tiles)):
-        w_copy(i).start()
+    for at in range(0, cols, tile):
+        w_copy(at).start()
     for copy in x_copies:
         copy.wait()
 
-    @pl.loop(0, tiles)
-    def _(i):
-        w_copy(i).wait()
-
-        @pl.when(i + AHEAD < tiles)
-        def _():
-            w_copy(i + AHEAD).start()
-
-        at = pl.ds(pl.multiple_of(i * tile, tile), tile)
-        product = jnp.dot(x_buf[...], w_buf[i], preferred_element_type=jnp.float32)
+    for start in range(0, cols, part):
+        for at in range(start, start + part, tile):
+            w_copy(at).wait()
+        at = slice(start, start + part)
+        product = jnp.dot(x_buf[...], w_buf[:, at], preferred_element_type=jnp.float32)
         if chunk:
             product = product + before_ref[:, at]
         if len(outs) == 1:
@@ -366,8 +370,6 @@
     n = sum(piece.shape[0] for piece in pieces) // block
     rows, depth = n * block, pieces[0].shape[1]
     cols = w_out.shape[1]
-    tile = min(TILE, cols)
-    tiles = cols // tile
     last = chunk == CHUNKS - 1
     hbm = pl.BlockSpec(memory_space=pltpu.HBM)
     vmem = pl.BlockSpec(memory_space=pltpu.VMEM)
@@ -376,7 +378,7 @@
     def body(*refs):
         arrays, rest = refs[: len(pieces)], refs[len(pieces) :]
         slots = [(arrays[p], at) for p, at in spans]
-        combine_kernel(n, block, tile, chunk, *slots, *rest)
+        combine_kernel(n, block, chunk, *slots, *rest)
 
     if last:
         out_shape = [
@@ -395,18 +397,18 @@
         out_specs=[vmem] * len(out_shape),
         scratch_shapes=[
             pltpu.VMEM((rows, depth), jnp.bfloat16),
-            pltpu.VMEM((tiles, depth, tile), jnp.bfloat16),
-            pltpu.SemaphoreType.DMA((tiles,)),
+            pltpu.VMEM((depth, cols), jnp.bfloat16),
+            pltpu.SemaphoreType.DMA((2 * PARTS,)),
             pltpu.SemaphoreType.DMA((n,)),
         ],
-        compiler_params=pltpu.CompilerParams(vmem_limit_bytes=48 * MIB),
+        compiler_params=pltpu.CompilerParams(vmem_limit_bytes=24 * MIB),
         cost_estimate=pl.CostEstimate(
             flops=2 * rows * depth * cols,
             bytes_accessed=2 * depth * cols + 2 * rows * depth + 4 * rows * cols,
             transcendentals=0,
         ),
         name="combine",
-    )(*pieces, *earlier, w_out)
+    )(*pieces, *earlier, in_hbm(w_out))
 
 
 def shards(

time: 102 us -> 94.5 us (0.926)
  local copies, waits for them, and re-layouts: 4.46 us -> 0.09 us
  waiting for transfers between devices: 34.1 us -> 38.3 us
  Pallas kernels: 41 us -> 37.3 us
  starting transfers between devices: 18.2 us -> 15 us
    pallas_call x2, Pallas kernels: 14.3 us -> 9.36 us  [attend(): pl.pallas_call(functools.partial(attend_kernel, chunk, stages, groups, he...]
    unnamed x14 -> x2, local copies, waits for them, and re-layouts: 4.38 us -> 0.01 us
    ppermute x12, waiting for transfers between devices: 32.2 us -> 36.4 us  [exchange(): return lax.ppermute(value, ('gx', 'gy'), pairs)]
    ppermute x12, starting transfers between devices: 18.1 us -> 15 us  [exchange(): return lax.ppermute(value, ('gx', 'gy'), pairs)]
    pallas_call x2, Pallas kernels: 14.2 us -> 15.5 us  [project(): pl.pallas_call(functools.partial(project_kernel, n, PARTS, chunk), out_sh...]
  transfers between devices with their start and end apart: 13 -> 13, of which waited for: 9 -> 10; matrix products, arithmetic and copies ran while one was open for 3% -> 3% of each run, Pallas kernels for 27% -> 23%
where the time goes in v1:
time: 94.5 us; the launch traced here: 94.3 us
  waiting for transfers between devices  38.3 us (41%)
  Pallas kernels  37.3 us (39%)
  starting transfers between devices  15 us (16%)
  other arithmetic  3.41 us (4%)
    ppermute x12, waiting for transfers between devices, exchange(): return lax.ppermute(value, ('gx', 'gy'), pairs)  36.4 us
    pallas_call x2, Pallas kernels, project(): pl.pallas_call(functools.partial(project_kernel, n, PARTS, chunk), out_sh...  15.5 us
    ppermute x12, starting transfers between devices, exchange(): return lax.ppermute(value, ('gx', 'gy'), pairs)  15 us
    pallas_call x2, Pallas kernels, combine(): pl.pallas_call(body, out_shape=out_shape, in_specs=[pl.BlockSpec(memory_s...  12.4 us
    pallas_call x2, Pallas kernels, attend(): pl.pallas_call(functools.partial(attend_kernel, chunk, stages, groups, he...  9.36 us
    convert_element_type x4, other arithmetic, shards(): send = value.astype(jnp.bfloat16)  2.09 us
    ppermute x1, waiting for transfers between devices, shards(): other = lax.ppermute(send, 'gy', [(0, 1), (1, 0)])  1.9 us
  transfers between devices with their start and end apart: 13, of which 10 were waited for; matrix products, arithmetic and copies ran while one was open for 3% of the time, Pallas kernels for 23%

profile of v1, /device:TPU:0, one launch (start us, length us, event | category | flops | bytes accessed | tf_op | source)
XLA Modules:
  0.0 94.3 jit_solution(4589775824324862188)
XLA Ops:
  0.0 9.0 %project.2 = (bf16[128,2432]{1,0:T(8,128)(2,1)}, f32[128,2432]{1,0:T(8,128)S(1)}, bf16[256,2048]{1,0:T(8,128)(2,1)S(1)}) custom-call(bf16[256,2048]{1,0:T(8,128)(2,1)} %refs_0_.1, f32[1,2048]{1,0:T(1,128)} %bitcast.1, bf16[2048,4096]{1,0:T(8,128)(2,1)} %refs_1_.1, bf16[2048,256]{1,0:T(8,128)(2,1)} %refs_2_.3, bf16[2048,256]{1,0:T(8,128)(2,1)} %refs_3_.3), custom_call_target="tpu_custom_call" | custom-call | flops 2415919104 | bytes 13631488 | tf_op jit(solution)/shard_map/project/pallas_call | solution.py:161
  9.0 3.0 %collective-permute-start.3 = (bf16[128,2432]{1,0:T(8,128)(2,1)}, bf16[128,2432]{1,0:T(8,128)(2,1)S(1)}, u32[]{:S(2)}, u32[]{:S(2)}) collective-permute-start(bf16[128,2432]{1,0:T(8,128)(2,1)} %get-tuple-element.16), channel_id=1, source_target_pairs={{0,2},{1,5},{2,0},{3,7},{4,6},{5,1},{6,4},{7,3},{8,10},{9,13},{10,... | collective-permute-start | bytes 1867784 | tf_op jit(solution)/shard_map/ppermute | solution.py:51
  12.1 0.0 copy-start
  12.1 6.5 %project.3 = (bf16[128,2304]{1,0:T(8,128)(2,1)}, f32[128,2304]{1,0:T(8,128)S(1)}) custom-call(bf16[256,2048]{1,0:T(8,128)(2,1)S(1)} %get-tuple-element.12.refs_0_, bf16[2048,4096]{1,0:T(8,128)(2,1)} %refs_1_.1, bf16[2048,256]{1,0:T(8,128)(2,1)} %refs_2_.3, bf16[2048,256]{1,0:T(8,128)(2,1)} %refs_3_.3), custom_call_target="tpu_custom_call" | custom-call | flops 2415919104 | bytes 13631488 | tf_op jit(solution)/shard_map/project/pallas_call | solution.py:161
  18.5 0.1 collective-permute-start
  18.6 0.0 copy-done
  18.6 0.1 add_convert_fusion.5
  18.7 0.1 convert_element_type.57
  18.8 0.1 fusion
  19.0 1.5 %collective-permute-done.3.refs_5_.refs_1_ = bf16[128,2432]{1,0:T(8,128)(2,1)S(1)} collective-permute-done((bf16[128,2432]{1,0:T(8,128)(2,1)}, bf16[128,2432]{1,0:T(8,128)(2,1)S(1)}, u32[]{:S(2)}, u32[]{:S(2)}) %collective-permute-start.3) | collective-permute-done | bytes 622624 | tf_op jit(solution)/shard_map/ppermute | solution.py:51
  20.5 0.1 add_convert_fusion.1
  20.6 2.1 %collective-permute-start.4 = (bf16[64,2432]{1,0:T(8,128)(2,1)S(1)}, bf16[64,2432]{1,0:T(8,128)(2,1)S(1)}, u32[]{:S(2)}, u32[]{:S(2)}) collective-permute-start(bf16[64,2432]{1,0:T(8,128)(2,1)S(1)} %add_convert_fusion.1), channel_id=1, source_target_pairs={{0,4},{1,3},{2,6},{3,1},{4,0},{5,7},{6,2},{7,5},{8,12},{9,11},{10,... | collective-permute-start | bytes 933896 | tf_op jit(solution)/shard_map/ppermute | solution.py:51
  22.7 9.4 %collective-permute-done.refs_1_ = bf16[128,2304]{1,0:T(8,128)(2,1)} collective-permute-done((bf16[128,2304]{1,0:T(8,128)(2,1)}, bf16[128,2304]{1,0:T(8,128)(2,1)}, u32[]{:S(2)}, u32[]{:S(2)}) %collective-permute-start) | collective-permute-done | bytes 589856 | tf_op jit(solution)/shard_map/ppermute | solution.py:51
  32.1 1.0 %add_convert_fusion.2 = bf16[64,2304]{1,0:T(8,128)(2,1)S(1)} fusion(f32[128,2304]{1,0:T(8,128)S(1)} %get-tuple-element.13.refs_0_, bf16[128,2304]{1,0:T(8,128)(2,1)} %collective-permute-done.refs_1_), kind=kLoop, calls=%fused_computation.2 | loop fusion | flops 442368 | bytes 1179648 | tf_op jit(solution)/shard_map/convert_element_type | solution.py:444
  33.2 1.6 %collective-permute-start.1 = (bf16[64,2304]{1,0:T(8,128)(2,1)S(1)}, bf16[64,2304]{1,0:T(8,128)(2,1)S(1)}, u32[]{:S(2)}, u32[]{:S(2)}) collective-permute-start(bf16[64,2304]{1,0:T(8,128)(2,1)S(1)} %add_convert_fusion.2), channel_id=1, source_target_pairs={{0,4},{1,3},{2,6},{3,1},{4,0},{5,7},{6,2},{7,5},{8,12},{9,11},{10,... | collective-permute-start | bytes 884744 | tf_op jit(solution)/shard_map/ppermute | solution.py:51
  34.8 0.0 collective-permute-done.4.refs_6_.refs_2_
  34.8 0.1 add_convert_fusion.3
  34.9 2.8 %collective-permute-start.5 = (bf16[32,2432]{1,0:T(8,128)(2,1)S(1)}, bf16[32,2432]{1,0:T(8,128)(2,1)S(1)}, u32[]{:S(2)}, u32[]{:S(2)}) collective-permute-start(bf16[32,2432]{1,0:T(8,128)(2,1)S(1)} %add_convert_fusion.3), channel_id=1, source_target_pairs={{0,8},{1,9},{2,10},{3,11},{4,12},{5,13},{6,14},{7,15},{8,0},{9,1},... | collective-permute-start | bytes 466952 | tf_op jit(solution)/shard_map/ppermute | solution.py:51
  37.7 6.2 %collective-permute-done.1.refs_2_ = bf16[64,2304]{1,0:T(8,128)(2,1)S(1)} collective-permute-done((bf16[64,2304]{1,0:T(8,128)(2,1)S(1)}, bf16[64,2304]{1,0:T(8,128)(2,1)S(1)}, u32[]{:S(2)}, u32[]{:S(2)}) %collective-permute-start.1) | collective-permute-done | bytes 294944 | tf_op jit(solution)/shard_map/ppermute | solution.py:51
  43.8 1.0 %add_convert_fusion.4 = bf16[32,2304]{1,0:T(8,128)(2,1)S(1)} fusion(f32[128,2304]{1,0:T(8,128)S(1)} %get-tuple-element.13.refs_0_, bf16[64,2304]{1,0:T(8,128)(2,1)S(1)} %collective-permute-done.1.refs_2_, bf16[128,2304]{1,0:T(8,128)(2,1)} %collective-permute-done.refs_1_), kind=kLoop, calls=%fused_computation.6 | loop fusion | flops 368640 | bytes 737280 | tf_op jit(solution)/shard_map/convert_element_type | solution.py:444
  44.8 0.4 collective-permute-start.2
  45.2 0.1 pad_maximum_fusion.4
  45.2 0.0 collective-permute-done.5.refs_7_.refs_3_
  45.2 4.2 %attend.3.refs_0_ = bf16[32,2048]{1,0:T(8,128)(2,1)S(1)} custom-call(s32[8]{0:T(128)S(1)} %copy-done, f32[128,2432]{1,0:T(8,128)S(1)} %get-tuple-element.15.refs_4_.refs_0_, bf16[128,2432]{1,0:T(8,128)(2,1)S(1)} %collective-permute-done.3.refs_5_.refs_1_, bf16[64,2432]{1,0:T(8,128)(2,1)S(1)} %collective-permute-done.4.refs_6_.refs_2_, ...), custom_call_target="tpu_custom_call" | custom-call | flops 268435456 | bytes 4194304 | tf_op jit(solution)/shard_map/attend/pallas_call | solution.py:293
  49.5 2.7 %collective-permute-start.9 = (bf16[32,2048]{1,0:T(8,128)(2,1)S(1)}, bf16[32,2048]{1,0:T(8,128)(2,1)S(1)}, u32[]{:S(2)}, u32[]{:S(2)}) collective-permute-start(bf16[32,2048]{1,0:T(8,128)(2,1)S(1)} %attend.3.refs_0_), channel_id=1, source_target_pairs={{0,8},{1,9},{2,10},{3,11},{4,12},{5,13},{6,14},{7,15},{8,0},{9,1},... | collective-permute-start | bytes 393224 | tf_op jit(solution)/shard_map/ppermute | solution.py:51
  52.2 1.0 %collective-permute-done.2.refs_3_ = bf16[32,2304]{1,0:T(8,128)(2,1)S(1)} collective-permute-done((bf16[32,2304]{1,0:T(8,128)(2,1)S(1)}, bf16[32,2304]{1,0:T(8,128)(2,1)S(1)}, u32[]{:S(2)}, u32[]{:S(2)}) %collective-permute-start.2) | collective-permute-done | bytes 147488 | tf_op jit(solution)/shard_map/ppermute | solution.py:51
  53.2 5.1 %attend.2.refs_0_ = bf16[32,2048]{1,0:T(8,128)(2,1)S(1)} custom-call(s32[8]{0:T(128)S(1)} %copy-done, f32[128,2304]{1,0:T(8,128)S(1)} %get-tuple-element.13.refs_0_, bf16[128,2304]{1,0:T(8,128)(2,1)} %collective-permute-done.refs_1_, bf16[64,2304]{1,0:T(8,128)(2,1)S(1)} %collective-permute-done.1.refs_2_, ...), custom_call_target="tpu_custom_call" | custom-call | flops 268435456 | bytes 4194304 | tf_op jit(solution)/shard_map/attend/pallas_call | solution.py:293
  58.4 0.1 collective-permute-start.6
  58.4 0.5 collective-permute-done.9.refs_1_
  59.0 1.5 %collective-permute-start.10 = (bf16[64,2048]{1,0:T(8,128)(2,1)S(1)}, bf16[64,2048]{1,0:T(8,128)(2,1)S(1)}, u32[]{:S(2)}, u32[]{:S(2)}) collective-permute-start(bf16[64,2048]{1,0:T(8,128)(2,1)S(1)} %pad_maximum_fusion.3), channel_id=1, source_target_pairs={{0,4},{1,3},{2,6},{3,1},{4,0},{5,7},{6,2},{7,5},{8,12},{9,11},{10,... | collective-permute-start | bytes 786440 | tf_op jit(solution)/shard_map/ppermute | solution.py:51
  60.5 4.0 %collective-permute-done.6.refs_1_ = bf16[32,2048]{1,0:T(8,128)(2,1)S(1)} collective-permute-done((bf16[32,2048]{1,0:T(8,128)(2,1)S(1)}, bf16[32,2048]{1,0:T(8,128)(2,1)S(1)}, u32[]{:S(2)}, u32[]{:S(2)}) %collective-permute-start.6) | collective-permute-done | bytes 131104 | tf_op jit(solution)/shard_map/ppermute | solution.py:51
  64.5 0.1 collective-permute-start.7
  64.6 5.0 %collective-permute-done.10.refs_2_ = bf16[64,2048]{1,0:T(8,128)(2,1)S(1)} collective-permute-done((bf16[64,2048]{1,0:T(8,128)(2,1)S(1)}, bf16[64,2048]{1,0:T(8,128)(2,1)S(1)}, u32[]{:S(2)}, u32[]{:S(2)}) %collective-permute-start.10) | collective-permute-done | bytes 262176 | tf_op jit(solution)/shard_map/ppermute | solution.py:51
  69.7 0.3 collective-permute-start.11
  70.0 5.3 %collective-permute-done.7.refs_2_ = bf16[64,2048]{1,0:T(8,128)(2,1)S(1)} collective-permute-done((bf16[64,2048]{1,0:T(8,128)(2,1)S(1)}, bf16[64,2048]{1,0:T(8,128)(2,1)S(1)}, u32[]{:S(2)}, u32[]{:S(2)}) %collective-permute-start.7) | collective-permute-done | bytes 262176 | tf_op jit(solution)/shard_map/ppermute | solution.py:51
  75.3 0.3 collective-permute-start.8
  75.6 3.4 %collective-permute-done.11.refs_3_ = bf16[128,2048]{1,0:T(8,128)(2,1)S(1)} collective-permute-done((bf16[128,2048]{1,0:T(8,128)(2,1)S(1)}, bf16[128,2048]{1,0:T(8,128)(2,1)S(1)}, u32[]{:S(2)}, u32[]{:S(2)}) %collective-permute-start.11) | collective-permute-done | bytes 524320 | tf_op jit(solution)/shard_map/ppermute | solution.py:51
  79.0 6.2 %combine.2.refs_4_ = f32[256,2048]{1,0:T(8,128)S(1)} custom-call(bf16[32,2048]{1,0:T(8,128)(2,1)S(1)} %attend.3.refs_0_, bf16[32,2048]{1,0:T(8,128)(2,1)S(1)} %collective-permute-done.9.refs_1_, bf16[64,2048]{1,0:T(8,128)(2,1)S(1)} %collective-permute-done.10.refs_2_, bf16[128,2048]{1,0:T(8,128)(2,1)S(1)} %collective-permute-done.11.refs_3_, ...), custom_call_target="tpu_custom_call" | custom-call | flops 2147483648 | bytes 11534336 | tf_op jit(solution)/shard_map/combine/pallas_call | solution.py:391
  85.2 0.0 collective-permute-done.8.refs_3_
  85.2 6.2 %combine.3 = (bf16[128,2048]{1,0:T(8,128)(2,1)S(1)}, f32[128,2048]{1,0:T(8,128)S(1)}) custom-call(bf16[32,2048]{1,0:T(8,128)(2,1)S(1)} %attend.2.refs_0_, bf16[32,2048]{1,0:T(8,128)(2,1)S(1)} %collective-permute-done.6.refs_1_, bf16[64,2048]{1,0:T(8,128)(2,1)S(1)} %collective-permute-done.7.refs_2_, bf16[128,2048]{1,0:T(8,128)(2,1)S(1)} %collective-permute-done.8.refs_3_, ...), custom_call_target="tpu_custom_call" | custom-call | flops 2147483648 | bytes 11534336 | tf_op jit(solution)/shard_map/combine/pallas_call | solution.py:391
  91.4 0.1 collective-permute-start.12
  91.5 1.9 %collective-permute-done.12 = bf16[128,2048]{1,0:T(8,128)(2,1)S(1)} collective-permute-done((bf16[128,2048]{1,0:T(8,128)(2,1)S(1)}, bf16[128,2048]{1,0:T(8,128)(2,1)S(1)}, u32[]{:S(2)}, u32[]{:S(2)}) %collective-permute-start.12) | collective-permute-done | bytes 524320 | tf_op jit(solution)/shard_map/ppermute | solution.py:461
  93.4 0.9 add_convert_fusion
  (5 shorter events, 0.1 us)
Async XLA Ops:
  9.0 11.5 %collective-permute-start.3 = (bf16[128,2432]{1,0:T(8,128)(2,1)}, bf16[128,2432]{1,0:T(8,128)(2,1)S(1)}, u32[]{:S(2)}, u32[]{:S(2)}) collective-permute-start(bf16[128,2432]{1,0:T(8,128)(2,1)} %get-tuple-element.16), channel_id=1, source_target_pairs={{0,2},{1,5},{2,0},{3,7},{4,6},{5,1},{6,4},{7,3},{8,10},{9,13},{10,... | collective-permute-start | bytes 1867784 | tf_op jit(solution)/shard_map/ppermute | solution.py:51
  12.1 6.6 %copy-start = (s32[8]{0:T(128)S(1)}, s32[8]{0:T(128)}, u32[]{:S(2)}) copy-start(s32[8]{0:T(128)} %length_ref.3) | copy-start | bytes 100
  18.5 13.6 %collective-permute-start = (bf16[128,2304]{1,0:T(8,128)(2,1)}, bf16[128,2304]{1,0:T(8,128)(2,1)}, u32[]{:S(2)}, u32[]{:S(2)}) collective-permute-start(bf16[128,2304]{1,0:T(8,128)(2,1)} %get-tuple-element.14), channel_id=1, source_target_pairs={{0,2},{1,5},{2,0},{3,7},{4,6},{5,1},{6,4},{7,3},{8,10},{9,13},{10,... | collective-permute-start | bytes 1769480 | tf_op jit(solution)/shard_map/ppermute | solution.py:51
  20.6 14.3 %collective-permute-start.4 = (bf16[64,2432]{1,0:T(8,128)(2,1)S(1)}, bf16[64,2432]{1,0:T(8,128)(2,1)S(1)}, u32[]{:S(2)}, u32[]{:S(2)}) collective-permute-start(bf16[64,2432]{1,0:T(8,128)(2,1)S(1)} %add_convert_fusion.1), channel_id=1, source_target_pairs={{0,4},{1,3},{2,6},{3,1},{4,0},{5,7},{6,2},{7,5},{8,12},{9,11},{10,... | collective-permute-start | bytes 933896 | tf_op jit(solution)/shard_map/ppermute | solution.py:51
  33.2 10.7 %collective-permute-start.1 = (bf16[64,2304]{1,0:T(8,128)(2,1)S(1)}, bf16[64,2304]{1,0:T(8,128)(2,1)S(1)}, u32[]{:S(2)}, u32[]{:S(2)}) collective-permute-start(bf16[64,2304]{1,0:T(8,128)(2,1)S(1)} %add_convert_fusion.2), channel_id=1, source_target_pairs={{0,4},{1,3},{2,6},{3,1},{4,0},{5,7},{6,2},{7,5},{8,12},{9,11},{10,... | collective-permute-start | bytes 884744 | tf_op jit(solution)/shard_map/ppermute | solution.py:51
  34.9 10.4 %collective-permute-start.5 = (bf16[32,2432]{1,0:T(8,128)(2,1)S(1)}, bf16[32,2432]{1,0:T(8,128)(2,1)S(1)}, u32[]{:S(2)}, u32[]{:S(2)}) collective-permute-start(bf16[32,2432]{1,0:T(8,128)(2,1)S(1)} %add_convert_fusion.3), channel_id=1, source_target_pairs={{0,8},{1,9},{2,10},{3,11},{4,12},{5,13},{6,14},{7,15},{8,0},{9,1},... | collective-permute-start | bytes 466952 | tf_op jit(solution)/shard_map/ppermute | solution.py:51
  44.8 8.4 %collective-permute-start.2 = (bf16[32,2304]{1,0:T(8,128)(2,1)S(1)}, bf16[32,2304]{1,0:T(8,128)(2,1)S(1)}, u32[]{:S(2)}, u32[]{:S(2)}) collective-permute-start(bf16[32,2304]{1,0:T(8,128)(2,1)S(1)} %add_convert_fusion.4), channel_id=1, source_target_pairs={{0,8},{1,9},{2,10},{3,11},{4,12},{5,13},{6,14},{7,15},{8,0},{9,1},... | collective-permute-start | bytes 442376 | tf_op jit(solution)/shard_map/ppermute | solution.py:51
  49.5 9.5 %collective-permute-start.9 = (bf16[32,2048]{1,0:T(8,128)(2,1)S(1)}, bf16[32,2048]{1,0:T(8,128)(2,1)S(1)}, u32[]{:S(2)}, u32[]{:S(2)}) collective-permute-start(bf16[32,2048]{1,0:T(8,128)(2,1)S(1)} %attend.3.refs_0_), channel_id=1, source_target_pairs={{0,8},{1,9},{2,10},{3,11},{4,12},{5,13},{6,14},{7,15},{8,0},{9,1},... | collective-permute-start | bytes 393224 | tf_op jit(solution)/shard_map/ppermute | solution.py:51
  58.4 6.2 %collective-permute-start.6 = (bf16[32,2048]{1,0:T(8,128)(2,1)S(1)}, bf16[32,2048]{1,0:T(8,128)(2,1)S(1)}, u32[]{:S(2)}, u32[]{:S(2)}) collective-permute-start(bf16[32,2048]{1,0:T(8,128)(2,1)S(1)} %attend.2.refs_0_), channel_id=1, source_target_pairs={{0,8},{1,9},{2,10},{3,11},{4,12},{5,13},{6,14},{7,15},{8,0},{9,1},... | collective-permute-start | bytes 393224 | tf_op jit(solution)/shard_map/ppermute | solution.py:51
  59.0 10.6 %collective-permute-start.10 = (bf16[64,2048]{1,0:T(8,128)(2,1)S(1)}, bf16[64,2048]{1,0:T(8,128)(2,1)S(1)}, u32[]{:S(2)}, u32[]{:S(2)}) collective-permute-start(bf16[64,2048]{1,0:T(8,128)(2,1)S(1)} %pad_maximum_fusion.3), channel_id=1, source_target_pairs={{0,4},{1,3},{2,6},{3,1},{4,0},{5,7},{6,2},{7,5},{8,12},{9,11},{10,... | collective-permute-start | bytes 786440 | tf_op jit(solution)/shard_map/ppermute | solution.py:51
  64.5 10.7 %collective-permute-start.7 = (bf16[64,2048]{1,0:T(8,128)(2,1)S(1)}, bf16[64,2048]{1,0:T(8,128)(2,1)S(1)}, u32[]{:S(2)}, u32[]{:S(2)}) collective-permute-start(bf16[64,2048]{1,0:T(8,128)(2,1)S(1)} %pad_maximum_fusion.2), channel_id=1, source_target_pairs={{0,4},{1,3},{2,6},{3,1},{4,0},{5,7},{6,2},{7,5},{8,12},{9,11},{10,... | collective-permute-start | bytes 786440 | tf_op jit(solution)/shard_map/ppermute | solution.py:51
  69.7 9.2 %collective-permute-start.11 = (bf16[128,2048]{1,0:T(8,128)(2,1)S(1)}, bf16[128,2048]{1,0:T(8,128)(2,1)S(1)}, u32[]{:S(2)}, u32[]{:S(2)}) collective-permute-start(bf16[128,2048]{1,0:T(8,128)(2,1)S(1)} %pad_maximum_fusion.1), channel_id=1, source_target_pairs={{0,2},{1,5},{2,0},{3,7},{4,6},{5,1},{6,4},{7,3},{8,10},{9,13},{10,... | collective-permute-start | bytes 1572872 | tf_op jit(solution)/shard_map/ppermute | solution.py:51
  75.3 9.8 %collective-permute-start.8 = (bf16[128,2048]{1,0:T(8,128)(2,1)S(1)}, bf16[128,2048]{1,0:T(8,128)(2,1)S(1)}, u32[]{:S(2)}, u32[]{:S(2)}) collective-permute-start(bf16[128,2048]{1,0:T(8,128)(2,1)S(1)} %pad_maximum_fusion), channel_id=1, source_target_pairs={{0,2},{1,5},{2,0},{3,7},{4,6},{5,1},{6,4},{7,3},{8,10},{9,13},{10,... | collective-permute-start | bytes 1572872 | tf_op jit(solution)/shard_map/ppermute | solution.py:51
  91.4 2.0 %collective-permute-start.12 = (bf16[128,2048]{1,0:T(8,128)(2,1)S(1)}, bf16[128,2048]{1,0:T(8,128)(2,1)S(1)}, u32[]{:S(2)}, u32[]{:S(2)}) collective-permute-start(bf16[128,2048]{1,0:T(8,128)(2,1)S(1)} %get-tuple-element.18), channel_id=1, source_target_pairs={{0,1},{1,0},{2,3},{3,2},{4,5},{5,4},{6,7},{7,6},{8,9},{9,8},{10,11... | collective-permute-start | bytes 1572872 | tf_op jit(solution)/shard_map/ppermute | solution.py:461

commit v2 on v1

--- a/solution.py
+++ b/solution.py
@@ -51,8 +51,7 @@
     return lax.ppermute(value, ("gx", "gy"), pairs)
 
 
-def project_kernel(n, parts, chunk, *refs):
-    first = chunk == 0
+def project_kernel(n, q_start, kv_start, first, *refs):
     if first:
         tokens_ref, gain_ref, wq_ref, wk_ref, wv_ref, send_ref, keep_ref, x_ref = refs[:8]
         t_buf, t_sems = refs[8:10]
@@ -61,25 +60,21 @@
     w_buf, sems = refs[-2:]
     half = send_ref.shape[0]
     rows = 2 * half
-    kv = wk_ref.shape[1] // CHUNKS
-    cols = wq_ref.shape[1] // CHUNKS
-    part = cols // parts
-    tile = part // 2
-
-    def w_copy(ref, start, width, at, sem):
+    with_kv = kv_start is not None
+    kv = wk_ref.shape[1] // CHUNKS if with_kv else 0
+    width = w_buf.shape[1]
+    cols = width - 2 * kv
+    tile = cols // 2
+
+    def w_copy(ref, start, size, at, sem):
         return pltpu.make_async_copy(
-            ref.at[:, start : start + width], w_buf.at[:, at : at + width], sems.at[sem]
+            ref.at[:, start : start + size], w_buf.at[:, at : at + size], sems.at[sem]
         )
 
-    copies = [
-        [
-            w_copy(wq_ref, chunk * cols + at, tile, at, at // tile)
-            for at in range(p * part, (p + 1) * part, tile)
-        ]
-        for p in range(parts)
-    ]
-    copies[-1].append(w_copy(wk_ref, chunk * kv, kv, cols, 2 * parts))
-    copies[-1].append(w_copy(wv_ref, chunk * kv, kv, cols + kv, 2 * parts + 1))
+    copies = [[w_copy(wq_ref, q_start + at, tile, at, at // tile)] for at in (0, tile)]
+    if with_kv:
+        copies[1].append(w_copy(wk_ref, kv_start, kv, cols, 2))
+        copies[1].append(w_copy(wv_ref, kv_start, kv, cols + kv, 3))
 
     if first:
         block = rows // n
@@ -97,7 +92,6 @@
         for copy in group:
             copy.start()
     if first:
-        extra = cols + 2 * kv
         lanes = lax.broadcasted_iota(jnp.int32, (block, 128), 1)
         for slot in range(n):
             t_copies[slot].wait()
@@ -114,15 +108,14 @@
                 jnp.where(lanes == 3 * me + 1, middle, jnp.where(lanes == 3 * me + 2, low, 0.0)),
             )
             if slot < n // 2:
-                keep_ref[slot * block : (slot + 1) * block, extra : extra + 128] = packed
+                keep_ref[slot * block : (slot + 1) * block, width : width + 128] = packed
             else:
                 at = (slot - n // 2) * block
-                send_ref[at : at + block, extra : extra + 128] = packed.astype(jnp.bfloat16)
-
-    for p in range(parts):
+                send_ref[at : at + block, width : width + 128] = packed.astype(jnp.bfloat16)
+
+    for p, (start, end) in enumerate(((0, tile), (tile, width))):
         for copy in copies[p]:
             copy.wait()
-        start, end = p * part, (p + 1) * part if p < parts - 1 else cols + 2 * kv
         product = jnp.dot(x_ref[...], w_buf[:, start:end], preferred_element_type=jnp.float32)
         keep_ref[:, start:end] = product[:half]
         send_ref[:, start:end] = product[half:].astype(jnp.bfloat16)
@@ -132,25 +125,21 @@
     return pltpu.with_memory_space_constraint(value, pltpu.HBM)
 
 
-def project(n, chunk, x, gain, w_query, w_key, w_value):
+def project(n, q_start, q_cols, kv_start, first, x, gain, w_query, w_key, w_value):
     rows, depth = x.shape
-    cols = w_query.shape[1] // CHUNKS
-    kv = w_key.shape[1] // CHUNKS
-    first = chunk == 0
-    width = cols + 2 * kv + (128 if first else 0)
+    kv = w_key.shape[1] // CHUNKS if kv_start is not None else 0
+    width = q_cols + 2 * kv
+    full = width + (128 if first else 0)
     hbm = pl.BlockSpec(memory_space=pltpu.HBM)
     vmem = pl.BlockSpec(memory_space=pltpu.VMEM)
     out_shape = [
-        jax.ShapeDtypeStruct((rows // 2, width), jnp.bfloat16),
-        jax.ShapeDtypeStruct((rows // 2, width), jnp.float32),
+        pltpu.VMEM((rows // 2, full), jnp.bfloat16),
+        pltpu.VMEM((rows // 2, full), jnp.float32),
     ]
-    scratch = [
-        pltpu.VMEM((depth, cols + 2 * kv), jnp.bfloat16),
-        pltpu.SemaphoreType.DMA((2 * PARTS + 2,)),
-    ]
+    scratch = [pltpu.VMEM((depth, width), jnp.bfloat16), pltpu.SemaphoreType.DMA((4,))]
     if first:
-        out_shape.append(jax.ShapeDtypeStruct((rows, depth), jnp.bfloat16))
-        args = [in_hbm(x), in_hbm(gain)]
+        out_shape.append(pltpu.VMEM((rows, depth), jnp.bfloat16))
+        args = [in_hbm(x), gain]
         in_specs = [hbm, vmem]
         scratch = [
             pltpu.VMEM((n, rows // n, depth), jnp.bfloat16),
@@ -159,30 +148,29 @@
     else:
         args, in_specs = [x], [vmem]
     return pl.pallas_call(
-        functools.partial(project_kernel, n, PARTS, chunk),
+        functools.partial(project_kernel, n, q_start, kv_start, first),
         out_shape=out_shape,
         in_specs=in_specs + [hbm] * 3,
         out_specs=[vmem] * len(out_shape),
         scratch_shapes=scratch,
-        compiler_params=pltpu.CompilerParams(vmem_limit_bytes=28 * MIB),
+        compiler_params=pltpu.CompilerParams(vmem_limit_bytes=16 * MIB),
         cost_estimate=pl.CostEstimate(
-            flops=2 * rows * depth * (cols + 2 * kv),
-            bytes_accessed=2 * depth * (cols + 2 * kv) + 8 * rows * depth,
+            flops=2 * rows * depth * width,
+            bytes_accessed=2 * depth * width + 4 * rows * depth,
             transcendentals=0,
         ),
         name="project",
     )(*args, in_hbm(w_query), in_hbm(w_key), in_hbm(w_value))
 
 
-def attend_kernel(chunk, stages, groups, heads, seqs, length_ref, *refs):
-    sums, squares = refs[: stages + 1], refs[stages + 1 : 2 * stages + 2]
-    cos_ref, sin_ref, k_ref, v_ref, out_ref, k_buf, v_buf, q_scr, o_scr, sems = refs[
-        2 * stages + 2 :
-    ]
+def attend_kernel(chunk, parts, groups, heads, seqs, length_ref, *refs):
+    sums, square_ref = refs[:parts], refs[parts]
+    cos_ref, sin_ref, k_ref, v_ref, out_ref, k_buf, v_buf, q_scr, o_scr, sems = refs[parts + 1 :]
     rows = seqs * NEW
     cols = groups * heads * HD
     kv = groups * HD
     seq_count = k_ref.shape[0]
+    share = cols // parts
 
     def cache_copy(kind, b):
         source, target = ((k_ref, k_buf), (v_ref, v_buf))[kind]
@@ -205,32 +193,26 @@
     @pl.loop(0, seq_count // seqs)
     def _(step):
         mine = pl.ds(pl.multiple_of(step * rows, rows), rows)
-        total_squares = squares[0][mine, :]
-        for part in squares[1:]:
-            total_squares = total_squares + part[mine, :].astype(jnp.float32)
-        mean = jnp.sum(total_squares, axis=1, keepdims=True) / D
+        mean = jnp.sum(square_ref[mine, :], axis=1, keepdims=True) / D
         row_scale = lax.rsqrt(mean + EPS)
         cosine, sine = cos_ref[mine, :], sin_ref[mine, :]
 
-        def raw(start):
-            value = sums[0][mine, start : start + HD]
-            for part in sums[1:]:
-                value = value + part[mine, start : start + HD].astype(jnp.float32)
-            return value * row_scale
+        def raw(part, start):
+            return sums[part][mine, start : start + HD] * row_scale
 
         def rotary(value):
             return value * cosine + pltpu.roll(value, HD // 2, 1) * sine
 
         for h in range(heads * groups):
-            turned = rotary(raw(h * HD))
+            turned = rotary(raw(h * HD // share, h * HD % share))
             for s in range(seqs):
                 q_scr[s, h * NEW : (h + 1) * NEW, :] = turned[s * NEW : (s + 1) * NEW]
         for s in range(seqs):
             cache_copy(0, step * seqs + s).wait()
             cache_copy(1, step * seqs + s).wait()
         for g in range(groups):
-            new_keys = rotary(raw(cols + g * HD)).astype(jnp.bfloat16)
-            new_values = raw(cols + (groups + g) * HD).astype(jnp.bfloat16)
+            new_keys = rotary(raw(parts - 1, share + g * HD)).astype(jnp.bfloat16)
+            new_values = raw(parts - 1, share + (groups + g) * HD).astype(jnp.bfloat16)
             lanes = slice(g * HD, (g + 1) * HD)
             olds, news, mixes = [], [], []
             for s in range(seqs):
@@ -275,45 +257,38 @@
         out_ref[mine, :] = o_scr[...].astype(jnp.bfloat16)
 
 
-def attend(chunk, sums, squares, cosine, sine, cache_keys, cache_values, lengths, square_col):
+def attend(chunk, sums, squares, cosine, sine, cache_keys, cache_values, lengths):
     seq_count, slots, kv_all = cache_keys.shape
     kv = kv_all // CHUNKS
     groups = kv // HD
-    width = sums[0].shape[1]
-    cols = width - 2 * kv - (128 if chunk == 0 else 0)
+    parts = len(sums)
+    cols = parts * (sums[-1].shape[1] - 2 * kv)
     heads = cols // kv
     seqs = min(4, seq_count)
     rows = seq_count * NEW
-    stages = len(sums) - 1
-    wide = pl.BlockSpec((rows, width), lambda i, _: (0, 0))
-    square = pl.BlockSpec((rows, 128), lambda i, _: (0, square_col))
-    turn = pl.BlockSpec((rows, HD), lambda i, _: (0, 0))
-    cache = pl.BlockSpec(memory_space=pltpu.HBM)
+    vmem = pl.BlockSpec(memory_space=pltpu.VMEM)
+    hbm = pl.BlockSpec(memory_space=pltpu.HBM)
     flops = 4 * seq_count * groups * heads * NEW * slots * HD
     return pl.pallas_call(
-        functools.partial(attend_kernel, chunk, stages, groups, heads, seqs),
-        out_shape=jax.ShapeDtypeStruct((rows, cols), jnp.bfloat16),
-        grid_spec=pltpu.PrefetchScalarGridSpec(
-            num_scalar_prefetch=1,
-            grid=(1,),
-            in_specs=[wide] * (stages + 1) + [square] * (stages + 1) + [turn] * 2 + [cache] * 2,
-            out_specs=pl.BlockSpec((rows, cols), lambda i, _: (0, 0)),
-            scratch_shapes=[
-                pltpu.VMEM((seq_count, slots, kv), jnp.bfloat16),
-                pltpu.VMEM((seq_count, slots, kv), jnp.bfloat16),
-                pltpu.VMEM((seqs, groups * heads * NEW, HD), jnp.float32),
-                pltpu.VMEM((seqs * NEW, cols), jnp.float32),
-                pltpu.SemaphoreType.DMA((2, seq_count)),
-            ],
-        ),
-        compiler_params=pltpu.CompilerParams(vmem_limit_bytes=24 * MIB),
+        functools.partial(attend_kernel, chunk, parts, groups, heads, seqs),
+        out_shape=pltpu.VMEM((rows, cols), jnp.bfloat16),
+        in_specs=[pl.BlockSpec(memory_space=pltpu.SMEM)] + [vmem] * (parts + 3) + [hbm] * 2,
+        out_specs=vmem,
+        scratch_shapes=[
+            pltpu.VMEM((seq_count, slots, kv), jnp.bfloat16),
+            pltpu.VMEM((seq_count, slots, kv), jnp.bfloat16),
+            pltpu.VMEM((seqs, groups * heads * NEW, HD), jnp.float32),
+            pltpu.VMEM((seqs * NEW, cols), jnp.float32),
+            pltpu.SemaphoreType.DMA((2, seq_count)),
+        ],
+        compiler_params=pltpu.CompilerParams(vmem_limit_bytes=16 * MIB),
         cost_estimate=pl.CostEstimate(
             flops=flops,
             bytes_accessed=4 * seq_count * slots * kv,
             transcendentals=seq_count * groups * heads * NEW * slots,
         ),
         name="attend",
-    )(lengths, *sums, *squares, cosine, sine, in_hbm(cache_keys), in_hbm(cache_values))
+    )(lengths, *sums, squares, cosine, sine, in_hbm(cache_keys), in_hbm(cache_values))
 
 
 def combine_kernel(n, block, chunk, *refs):
@@ -337,12 +312,9 @@
 
     x_copies = []
     for slot, piece in enumerate(pieces):
-        ref, at = piece
         start = pl.multiple_of((slot_owner(n, slot, gx, gy) ^ moved) * block, block)
         x_copies.append(
-            pltpu.make_async_copy(
-                ref.at[pl.ds(at, block), :], x_buf.at[pl.ds(start, block), :], x_sems.at[slot]
-            )
+            pltpu.make_async_copy(piece, x_buf.at[pl.ds(start, block), :], x_sems.at[slot])
         )
     for copy in x_copies:
         copy.start()
@@ -366,30 +338,22 @@
 
 
 def combine(chunk, pieces, before, w_out):
-    block = pieces[0].shape[0]
-    n = sum(piece.shape[0] for piece in pieces) // block
-    rows, depth = n * block, pieces[0].shape[1]
+    n, (block, depth) = len(pieces), pieces[0].shape
+    rows = n * block
     cols = w_out.shape[1]
     last = chunk == CHUNKS - 1
     hbm = pl.BlockSpec(memory_space=pltpu.HBM)
     vmem = pl.BlockSpec(memory_space=pltpu.VMEM)
-    spans = [(p, at) for p, piece in enumerate(pieces) for at in range(0, piece.shape[0], block)]
-
-    def body(*refs):
-        arrays, rest = refs[: len(pieces)], refs[len(pieces) :]
-        slots = [(arrays[p], at) for p, at in spans]
-        combine_kernel(n, block, chunk, *slots, *rest)
-
     if last:
         out_shape = [
-            jax.ShapeDtypeStruct((rows // 2, cols), jnp.bfloat16),
-            jax.ShapeDtypeStruct((rows // 2, cols), jnp.float32),
+            pltpu.VMEM((rows // 2, cols), jnp.bfloat16),
+            pltpu.VMEM((rows // 2, cols), jnp.float32),
         ]
     else:
-        out_shape = [jax.ShapeDtypeStruct((rows, cols), jnp.float32)]
+        out_shape = [pltpu.VMEM((rows, cols), jnp.float32)]
     earlier = [] if chunk == 0 else [before]
     return pl.pallas_call(
-        body,
+        functools.partial(combine_kernel, n, block, chunk),
         out_shape=out_shape,
         in_specs=[pl.BlockSpec(memory_space=pl.ANY)] * len(pieces)
         + [vmem] * len(earlier)
@@ -401,7 +365,7 @@
             pltpu.SemaphoreType.DMA((2 * PARTS,)),
             pltpu.SemaphoreType.DMA((n,)),
         ],
-        compiler_params=pltpu.CompilerParams(vmem_limit_bytes=24 * MIB),
+        compiler_params=pltpu.CompilerParams(vmem_limit_bytes=16 * MIB),
         cost_estimate=pl.CostEstimate(
             flops=2 * rows * depth * cols,
             bytes_accessed=2 * depth * cols + 2 * rows * depth + 4 * rows * cols,
@@ -409,6 +373,33 @@
         ),
         name="combine",
     )(*pieces, *earlier, in_hbm(w_out))
+
+
+class Flow:
+    def __init__(self, n, cores, levels, send, keep):
+        self.n, self.cores, self.levels = n, cores, levels
+        self.send, self.keep = send, keep
+        self.rows = keep.shape[0]
+        self.received = []
+        self.value = None
+        self.sends = []
+
+    def start_exchange(self):
+        stage = len(self.received)
+        if stage < self.levels:
+            self.sends.append(self.send)
+            self.received.append(exchange(self.send, self.n, self.cores, stage))
+
+    def add_received(self):
+        if self.value is not None and len(self.received) == self.levels and self.rows == 0:
+            return
+        low = self.rows // 2 if len(self.received) < self.levels else 0
+        value = self.keep[low : self.rows]
+        for other in self.received:
+            value = value + other[low : self.rows].astype(jnp.float32)
+        self.value = value
+        self.send = value.astype(jnp.bfloat16)
+        self.rows = low
 
 
 def shards(
@@ -425,35 +416,52 @@
     sine = jnp.concatenate([-sine, sine], axis=1)
 
     x, gain = tokens, norm_gain[None, :]
+    kv = w_key.shape[1] // CHUNKS
+    q_cols = w_query.shape[1] // (CHUNKS * PARTS)
+    count = CHUNKS * PARTS
+    flows = []
+    for part in range(count + levels):
+        if part < count:
+            kv_start = part // PARTS * kv if part % PARTS == PARTS - 1 else None
+            out = project(
+                n, part * q_cols, q_cols, kv_start, part == 0, x, gain, w_query, w_key, w_value
+            )
+            if part == 0:
+                x = out[2]
+            flows.append(Flow(n, cores, levels, out[0], out[1]))
+        for flow in flows[max(0, part - levels) : part]:
+            flow.add_received()
+        if part + 1 < count:
+            waiting = flows[max(0, part - levels) : part + 1]
+            tied = lax.optimization_barrier((x, [flow.send for flow in waiting]))
+            x = tied[0]
+            for flow, send in zip(waiting, tied[1]):
+                flow.send = send
+        for flow in flows[max(0, part - levels) : part + 1]:
+            flow.start_exchange()
+    sums = [flow.value for flow in flows]
+    squares = sums[0][:, q_cols:]
+
     gathered = []
-    squares = None
     for chunk in range(CHUNKS):
-        out = project(n, chunk, x, gain, w_query, w_key, w_value)
-        send, keep = out[:2]
-        if chunk == 0:
-            x = out[2]
-        sums = [keep]
-        rows = keep.shape[0]
-        for stage in range(levels):
-            sums.append(exchange(send, n, cores, stage))
-            if stage < levels - 1:
-                low = rows // 2
-                value = sums[0][low:rows]
-                for part in sums[1:]:
-                    value = value + part[low:rows].astype(jnp.float32)
-                send = value.astype(jnp.bfloat16)
-                rows = low
-        if chunk == 0:
-            squares = sums
-            square_col = keep.shape[1] // 128 - 1
+        mine = sums[chunk * PARTS : (chunk + 1) * PARTS]
+        if chunk < CHUNKS - 1 and levels > 1:
+            mine, _ = lax.optimization_barrier((mine, flows[(chunk + 1) * PARTS].sends[1]))
         attention = attend(
-            chunk, sums, squares, cosine, sine, cache_keys, cache_values, cache_lengths, square_col
+            chunk,
+            mine,
+            squares,
+            cosine,
+            sine,
+            cache_keys,
+            cache_values,
+            cache_lengths,
         )
-        pieces = [attention]
-        for stage in reversed(range(levels)):
-            send = pieces[0] if len(pieces) == 1 else jnp.concatenate(pieces, axis=0)
-            pieces.append(exchange(send, n, cores, stage))
-        gathered.append(pieces)
+        slots = [attention]
+        for slot in range(1, n):
+            top = slot.bit_length() - 1
+            slots.append(exchange(slots[slot - (1 << top)], n, cores, levels - 1 - top))
+        gathered.append(slots)
     result = None
     for chunk in range(CHUNKS):
         result = combine(chunk, gathered[chunk], result and result[0], w_out)

time: 94.5 us -> 95.6 us (1.012)
  starting transfers between devices: 15 us -> 28.6 us
  waiting for transfers between devices: 38.3 us -> 28.8 us
  Pallas kernels: 37.3 us -> 35.4 us
  other arithmetic: 3.41 us -> 1.58 us
    ppermute x12 -> x26, starting transfers between devices: 15 us -> 28.6 us  [exchange(): return lax.ppermute(value, ('gx', 'gy'), pairs)]
    ppermute x12 -> x26, waiting for transfers between devices: 36.4 us -> 26.9 us  [exchange(): return lax.ppermute(value, ('gx', 'gy'), pairs)]
    pallas_call x6 -> x8, Pallas kernels: 37.3 us -> 35.4 us  [the longest x4 14.4 us: project(): pl.pallas_call(functools.partial(project_kernel, n, q_start, kv_start, fi...]
    convert_element_type x4 -> x8, other arithmetic: 2.09 us -> 0.24 us  [add_received(): self.send = value.astype(jnp.bfloat16)]
  transfers between devices with their start and end apart: 13 -> 27, of which waited for: 10 -> 12; matrix products, arithmetic and copies ran while one was open for 3% -> 1% of each run, Pallas kernels for 23% -> 27%
where the time goes in v2:
time: 95.6 us; the launch traced here: 95.4 us
  Pallas kernels  35.4 us (37%)
  waiting for transfers between devices  28.8 us (30%)
  starting transfers between devices  28.6 us (30%)
  other arithmetic  1.58 us (2%)
    ppermute x26, starting transfers between devices, exchange(): return lax.ppermute(value, ('gx', 'gy'), pairs)  28.6 us
    ppermute x26, waiting for transfers between devices, exchange(): return lax.ppermute(value, ('gx', 'gy'), pairs)  26.9 us
    pallas_call x4, Pallas kernels, project(): pl.pallas_call(functools.partial(project_kernel, n, q_start, kv_start, fi...  14.4 us
    pallas_call x2, Pallas kernels, combine(): pl.pallas_call(functools.partial(combine_kernel, n, block, chunk), out_sh...  12.6 us
    pallas_call x2, Pallas kernels, attend(): pl.pallas_call(functools.partial(attend_kernel, chunk, parts, groups, hea...  8.43 us
  transfers between devices with their start and end apart: 27, of which 12 were waited for; matrix products, arithmetic and copies ran while one was open for 1% of the time, Pallas kernels for 27%

profile of v2, /device:TPU:0, one launch (start us, length us, event | category | flops | bytes accessed | tf_op | source)
XLA Modules:
  0.0 95.4 jit_solution(6922998127511029415)
XLA Ops:
  0.0 0.7 copy-done
  0.7 3.6 %project.4 = (bf16[128,1152]{1,0:T(8,128)(2,1)S(1)}, f32[128,1152]{1,0:T(8,128)S(1)}, bf16[256,2048]{1,0:T(8,128)(2,1)S(1)}) custom-call(bf16[256,2048]{1,0:T(8,128)(2,1)} %refs_0_.1, f32[1,2048]{1,0:T(1,128)S(1)} %bitcast.1, bf16[2048,4096]{1,0:T(8,128)(2,1)} %refs_1_.5, bf16[2048,256]{1,0:T(8,128)(2,1)} %refs_2_.7, bf16[2048,256]{1,0:T(8,128)(2,1)} %refs_3_.7), custom_call_target="tpu_custom_call" | custom-call | flops 1073741824 | bytes 6291456 | tf_op jit(solution)/shard_map/project/pallas_call | solution.py:150
  4.3 3.0 %collective-permute-start = (bf16[128,1152]{1,0:T(8,128)(2,1)S(1)}, bf16[128,1152]{1,0:T(8,128)(2,1)S(1)}, u32[]{:S(2)}, u32[]{:S(2)}) collective-permute-start(bf16[128,1152]{1,0:T(8,128)(2,1)S(1)} %get-tuple-element.31), channel_id=1, source_target_pairs={{0,2},{1,5},{2,0},{3,7},{4,6},{5,1},{6,4},{7,3},{8,10},{9,13},{10,... | collective-permute-start | bytes 884744 | tf_op jit(solution)/shard_map/ppermute | solution.py:51
  7.3 0.1 add_convert_fusion.9
  7.4 0.1 convert_element_type.139
  7.5 3.9 %project.5 = (bf16[128,1280]{1,0:T(8,128)(2,1)S(1)}, f32[128,1280]{1,0:T(8,128)S(1)}) custom-call(bf16[256,2048]{1,0:T(8,128)(2,1)S(1)} %get-tuple-element.40.refs_0_, bf16[2048,4096]{1,0:T(8,128)(2,1)} %refs_1_.5, bf16[2048,256]{1,0:T(8,128)(2,1)} %refs_2_.7, bf16[2048,256]{1,0:T(8,128)(2,1)} %refs_3_.7), custom_call_target="tpu_custom_call" | custom-call | flops 1342177280 | bytes 7340032 | tf_op jit(solution)/shard_map/project/pallas_call | solution.py:150
  11.4 0.7 collective-permute-done
  12.1 2.1 %collective-permute-start.1 = (bf16[64,1152]{1,0:T(8,128)(2,1)S(1)}, bf16[64,1152]{1,0:T(8,128)(2,1)S(1)}, u32[]{:S(2)}, u32[]{:S(2)}) collective-permute-start(bf16[64,1152]{1,0:T(8,128)(2,1)S(1)} %add_convert_fusion.3), channel_id=1, source_target_pairs={{0,4},{1,3},{2,6},{3,1},{4,0},{5,7},{6,2},{7,5},{8,12},{9,11},{10,... | collective-permute-start | bytes 442376 | tf_op jit(solution)/shard_map/ppermute | solution.py:51
  14.2 0.1 fusion
  14.4 1.6 %collective-permute-start.2 = (bf16[128,1280]{1,0:T(8,128)(2,1)S(1)}, bf16[128,1280]{1,0:T(8,128)(2,1)S(1)}, u32[]{:S(2)}, u32[]{:S(2)}) collective-permute-start(bf16[128,1280]{1,0:T(8,128)(2,1)S(1)} %get-tuple-element.37), channel_id=1, source_target_pairs={{0,2},{1,5},{2,0},{3,7},{4,6},{5,1},{6,4},{7,3},{8,10},{9,13},{10,... | collective-permute-start | bytes 983048 | tf_op jit(solution)/shard_map/ppermute | solution.py:51
  15.9 3.0 %project.6 = (bf16[128,1024]{1,0:T(8,128)(2,1)S(1)}, f32[128,1024]{1,0:T(8,128)S(1)}) custom-call(bf16[256,2048]{1,0:T(8,128)(2,1)S(1)} %get-tuple-element.40.refs_0_, bf16[2048,4096]{1,0:T(8,128)(2,1)} %refs_1_.5, bf16[2048,256]{1,0:T(8,128)(2,1)} %refs_2_.7, bf16[2048,256]{1,0:T(8,128)(2,1)} %refs_3_.7), custom_call_target="tpu_custom_call" | custom-call | flops 1073741824 | bytes 6291456 | tf_op jit(solution)/shard_map/project/pallas_call | solution.py:150
  19.0 0.0 collective-permute-done.1
  19.0 2.5 %collective-permute-done.2 = bf16[128,1280]{1,0:T(8,128)(2,1)S(1)} collective-permute-done((bf16[128,1280]{1,0:T(8,128)(2,1)S(1)}, bf16[128,1280]{1,0:T(8,128)(2,1)S(1)}, u32[]{:S(2)}, u32[]{:S(2)}) %collective-permute-start.2) | collective-permute-done | bytes 327712 | tf_op jit(solution)/shard_map/ppermute | solution.py:51
  21.5 0.1 collective-permute-start.17
  21.6 0.1 pad_maximum_fusion
  21.7 3.0 %collective-permute-start.9 = (bf16[32,1152]{1,0:T(8,128)(2,1)S(1)}, bf16[32,1152]{1,0:T(8,128)(2,1)S(1)}, u32[]{:S(2)}, u32[]{:S(2)}) collective-permute-start(bf16[32,1152]{1,0:T(8,128)(2,1)S(1)} %add_convert_fusion.7), channel_id=1, source_target_pairs={{0,8},{1,9},{2,10},{3,11},{4,12},{5,13},{6,14},{7,15},{8,0},{9,1},... | collective-permute-start | bytes 221192 | tf_op jit(solution)/shard_map/ppermute | solution.py:51
  24.7 1.5 %collective-permute-start.3 = (bf16[128,1024]{1,0:T(8,128)(2,1)S(1)}, bf16[128,1024]{1,0:T(8,128)(2,1)S(1)}, u32[]{:S(2)}, u32[]{:S(2)}) collective-permute-start(bf16[128,1024]{1,0:T(8,128)(2,1)S(1)} %get-tuple-element.39), channel_id=1, source_target_pairs={{0,2},{1,5},{2,0},{3,7},{4,6},{5,1},{6,4},{7,3},{8,10},{9,13},{10,... | collective-permute-start | bytes 786440 | tf_op jit(solution)/shard_map/ppermute | solution.py:51
  26.2 3.9 %project.7 = (bf16[128,1280]{1,0:T(8,128)(2,1)S(1)}, f32[128,1280]{1,0:T(8,128)S(1)}) custom-call(bf16[256,2048]{1,0:T(8,128)(2,1)S(1)} %get-tuple-element.40.refs_0_, bf16[2048,4096]{1,0:T(8,128)(2,1)} %refs_1_.5, bf16[2048,256]{1,0:T(8,128)(2,1)} %refs_2_.7, bf16[2048,256]{1,0:T(8,128)(2,1)} %refs_3_.7), custom_call_target="tpu_custom_call" | custom-call | flops 1342177280 | bytes 7340032 | tf_op jit(solution)/shard_map/project/pallas_call | solution.py:150
  30.1 0.6 collective-permute-start.6
  30.7 0.0 collective-permute-done.17
  30.7 0.7 collective-permute-start.18
  31.4 0.0 collective-permute-done.9
  31.5 6.4 %collective-permute-done.18 = bf16[32,1280]{1,0:T(8,128)(2,1)S(1)} collective-permute-done((bf16[32,1280]{1,0:T(8,128)(2,1)S(1)}, bf16[32,1280]{1,0:T(8,128)(2,1)S(1)}, u32[]{:S(2)}, u32[]{:S(2)}) %collective-permute-start.18) | collective-permute-done | bytes 81952 | tf_op jit(solution)/shard_map/ppermute | solution.py:51
  37.9 0.0 collective-permute-done.3
  38.0 4.2 %attend.3.refs_0_ = bf16[32,2048]{1,0:T(8,128)(2,1)S(1)} custom-call(s32[8]{0:T(128)S(1)} %copy-done.1, f32[32,1152]{1,0:T(8,128)S(1)} %convert_add_fusion.2.refs_0_, f32[32,1280]{1,0:T(8,128)S(1)} %convert_add_fusion.refs_1_, f32[32,128]{1,0:T(8,128)S(1)} %slice.148.refs_2_, f32[32,128]{1,0:T(8,128)S(1)} %get-tuple-element.52.refs_3_, ...), custom_call_target="tpu_custom_call" | custom-call | flops 268435456 | bytes 4194304 | tf_op jit(solution)/shard_map/attend/pallas_call | solution.py:272
  42.2 1.5 %collective-permute-start.22 = (bf16[32,2048]{1,0:T(8,128)(2,1)S(1)}, bf16[32,2048]{1,0:T(8,128)(2,1)S(1)}, u32[]{:S(2)}, u32[]{:S(2)}) collective-permute-start(bf16[32,2048]{1,0:T(8,128)(2,1)S(1)} %attend.3.refs_0_), channel_id=1, source_target_pairs={{0,2},{1,5},{2,0},{3,7},{4,6},{5,1},{6,4},{7,3},{8,10},{9,13},{10,... | collective-permute-start | bytes 393224 | tf_op jit(solution)/shard_map/ppermute | solution.py:51
  43.7 0.0 collective-permute-start.20
  43.7 2.4 %collective-permute-start.19 = (bf16[32,2048]{1,0:T(8,128)(2,1)S(1)}, bf16[32,2048]{1,0:T(8,128)(2,1)S(1)}, u32[]{:S(2)}, u32[]{:S(2)}) collective-permute-start(bf16[32,2048]{1,0:T(8,128)(2,1)S(1)} %attend.3.refs_0_), channel_id=1, source_target_pairs={{0,8},{1,9},{2,10},{3,11},{4,12},{5,13},{6,14},{7,15},{8,0},{9,1},... | collective-permute-start | bytes 393224 | tf_op jit(solution)/shard_map/ppermute | solution.py:51
  46.1 0.0 collective-permute-start.4
  46.1 0.0 collective-permute-done.6
  46.2 2.1 %collective-permute-start.7 = (bf16[64,1280]{1,0:T(8,128)(2,1)S(1)}, bf16[64,1280]{1,0:T(8,128)(2,1)S(1)}, u32[]{:S(2)}, u32[]{:S(2)}) collective-permute-start(bf16[64,1280]{1,0:T(8,128)(2,1)S(1)} %add_convert_fusion.1), channel_id=1, source_target_pairs={{0,4},{1,3},{2,6},{3,1},{4,0},{5,7},{6,2},{7,5},{8,12},{9,11},{10,... | collective-permute-start | bytes 491528 | tf_op jit(solution)/shard_map/ppermute | solution.py:51
  48.3 4.1 %collective-permute-done.4 = bf16[64,1024]{1,0:T(8,128)(2,1)S(1)} collective-permute-done((bf16[64,1024]{1,0:T(8,128)(2,1)S(1)}, bf16[64,1024]{1,0:T(8,128)(2,1)S(1)}, u32[]{:S(2)}, u32[]{:S(2)}) %collective-permute-start.4) | collective-permute-done | bytes 131104 | tf_op jit(solution)/shard_map/ppermute | solution.py:51
  52.4 1.2 %collective-permute-start.5 = (bf16[32,1024]{1,0:T(8,128)(2,1)S(1)}, bf16[32,1024]{1,0:T(8,128)(2,1)S(1)}, u32[]{:S(2)}, u32[]{:S(2)}) collective-permute-start(bf16[32,1024]{1,0:T(8,128)(2,1)S(1)} %add_convert_fusion.8), channel_id=1, source_target_pairs={{0,8},{1,9},{2,10},{3,11},{4,12},{5,13},{6,14},{7,15},{8,0},{9,1},... | collective-permute-start | bytes 196616 | tf_op jit(solution)/shard_map/ppermute | solution.py:51
  53.6 2.0 %collective-permute-done.7 = bf16[64,1280]{1,0:T(8,128)(2,1)S(1)} collective-permute-done((bf16[64,1280]{1,0:T(8,128)(2,1)S(1)}, bf16[64,1280]{1,0:T(8,128)(2,1)S(1)}, u32[]{:S(2)}, u32[]{:S(2)}) %collective-permute-start.7) | collective-permute-done | bytes 163872 | tf_op jit(solution)/shard_map/ppermute | solution.py:51
  55.6 0.9 collective-permute-start.8
  56.4 1.9 %collective-permute-done.5 = bf16[32,1024]{1,0:T(8,128)(2,1)S(1)} collective-permute-done((bf16[32,1024]{1,0:T(8,128)(2,1)S(1)}, bf16[32,1024]{1,0:T(8,128)(2,1)S(1)}, u32[]{:S(2)}, u32[]{:S(2)}) %collective-permute-start.5) | collective-permute-done | bytes 65568 | tf_op jit(solution)/shard_map/ppermute | solution.py:51
  58.4 3.4 %collective-permute-done.8 = bf16[32,1280]{1,0:T(8,128)(2,1)S(1)} collective-permute-done((bf16[32,1280]{1,0:T(8,128)(2,1)S(1)}, bf16[32,1280]{1,0:T(8,128)(2,1)S(1)}, u32[]{:S(2)}, u32[]{:S(2)}) %collective-permute-start.8) | collective-permute-done | bytes 81952 | tf_op jit(solution)/shard_map/ppermute | solution.py:51
  61.8 4.2 %attend.2.refs_0_ = bf16[32,2048]{1,0:T(8,128)(2,1)S(1)} custom-call(s32[8]{0:T(128)S(1)} %copy-done.1, f32[32,1024]{1,0:T(8,128)S(1)} %convert_add_fusion.3.refs_0_, f32[32,1280]{1,0:T(8,128)S(1)} %convert_add_fusion.1.refs_1_, f32[32,128]{1,0:T(8,128)S(1)} %slice.148.refs_2_, f32[32,128]{1,0:T(8,128)S(1)} %get-tuple-element.52.refs_3_, ...), custom_call_target="tpu_custom_call" | custom-call | flops 268435456 | bytes 4194304 | tf_op jit(solution)/shard_map/attend/pallas_call | solution.py:272
  66.0 0.1 collective-permute-start.10
  66.1 0.0 collective-permute-done.19.refs_1_
  66.1 2.3 %collective-permute-start.21 = (bf16[32,2048]{1,0:T(8,128)(2,1)S(1)}, bf16[32,2048]{1,0:T(8,128)(2,1)S(1)}, u32[]{:S(2)}, u32[]{:S(2)}) collective-permute-start(bf16[32,2048]{1,0:T(8,128)(2,1)S(1)} %collective-permute-done.19.refs_1_), channel_id=1, source_target_pairs={{0,4},{1,3},{2,6},{3,1},{4,0},{5,7},{6,2},{7,5},{8,12},{9,11},{10,... | collective-permute-start | bytes 393224 | tf_op jit(solution)/shard_map/ppermute | solution.py:51
  68.4 0.0 collective-permute-done.20.refs_2_
  68.4 0.0 collective-permute-start.24
  68.4 2.0 %collective-permute-start.23 = (bf16[32,2048]{1,0:T(8,128)(2,1)S(1)}, bf16[32,2048]{1,0:T(8,128)(2,1)S(1)}, u32[]{:S(2)}, u32[]{:S(2)}) collective-permute-start(bf16[32,2048]{1,0:T(8,128)(2,1)S(1)} %collective-permute-done.19.refs_1_), channel_id=1, source_target_pairs={{0,2},{1,5},{2,0},{3,7},{4,6},{5,1},{6,4},{7,3},{8,10},{9,13},{10,... | collective-permute-start | bytes 393224 | tf_op jit(solution)/shard_map/ppermute | solution.py:51
  70.5 0.0 collective-permute-done.22.refs_4_
  70.5 0.1 collective-permute-start.11
  70.5 2.5 %collective-permute-done.10.refs_1_ = bf16[32,2048]{1,0:T(8,128)(2,1)S(1)} collective-permute-done((bf16[32,2048]{1,0:T(8,128)(2,1)S(1)}, bf16[32,2048]{1,0:T(8,128)(2,1)S(1)}, u32[]{:S(2)}, u32[]{:S(2)}) %collective-permute-start.10) | collective-permute-done | bytes 131104 | tf_op jit(solution)/shard_map/ppermute | solution.py:51
  73.1 0.0 collective-permute-start.12
  73.1 1.1 %collective-permute-done.21.refs_3_ = bf16[32,2048]{1,0:T(8,128)(2,1)S(1)} collective-permute-done((bf16[32,2048]{1,0:T(8,128)(2,1)S(1)}, bf16[32,2048]{1,0:T(8,128)(2,1)S(1)}, u32[]{:S(2)}, u32[]{:S(2)}) %collective-permute-start.21) | collective-permute-done | bytes 131104 | tf_op jit(solution)/shard_map/ppermute | solution.py:51
  74.2 0.0 collective-permute-start.25
  74.2 0.0 collective-permute-done.24.refs_6_
  74.2 2.0 %collective-permute-start.13 = (bf16[32,2048]{1,0:T(8,128)(2,1)S(1)}, bf16[32,2048]{1,0:T(8,128)(2,1)S(1)}, u32[]{:S(2)}, u32[]{:S(2)}) collective-permute-start(bf16[32,2048]{1,0:T(8,128)(2,1)S(1)} %attend.2.refs_0_), channel_id=1, source_target_pairs={{0,2},{1,5},{2,0},{3,7},{4,6},{5,1},{6,4},{7,3},{8,10},{9,13},{10,... | collective-permute-start | bytes 393224 | tf_op jit(solution)/shard_map/ppermute | solution.py:51
  76.3 0.0 collective-permute-done.23.refs_5_
  76.3 0.1 collective-permute-start.14
  76.3 0.7 collective-permute-done.11.refs_2_
  77.0 1.3 %collective-permute-start.15 = (bf16[32,2048]{1,0:T(8,128)(2,1)S(1)}, bf16[32,2048]{1,0:T(8,128)(2,1)S(1)}, u32[]{:S(2)}, u32[]{:S(2)}) collective-permute-start(bf16[32,2048]{1,0:T(8,128)(2,1)S(1)} %collective-permute-done.11.refs_2_), channel_id=1, source_target_pairs={{0,2},{1,5},{2,0},{3,7},{4,6},{5,1},{6,4},{7,3},{8,10},{9,13},{10,... | collective-permute-start | bytes 393224 | tf_op jit(solution)/shard_map/ppermute | solution.py:51
  78.3 1.6 %collective-permute-done.12.refs_3_ = bf16[32,2048]{1,0:T(8,128)(2,1)S(1)} collective-permute-done((bf16[32,2048]{1,0:T(8,128)(2,1)S(1)}, bf16[32,2048]{1,0:T(8,128)(2,1)S(1)}, u32[]{:S(2)}, u32[]{:S(2)}) %collective-permute-start.12) | collective-permute-done | bytes 131104 | tf_op jit(solution)/shard_map/ppermute | solution.py:51
  79.8 6.3 %combine.2.refs_8_ = f32[256,2048]{1,0:T(8,128)S(1)} custom-call(bf16[32,2048]{1,0:T(8,128)(2,1)S(1)} %attend.3.refs_0_, bf16[32,2048]{1,0:T(8,128)(2,1)S(1)} %collective-permute-done.19.refs_1_, bf16[32,2048]{1,0:T(8,128)(2,1)S(1)} %collective-permute-done.20.refs_2_, bf16[32,2048]{1,0:T(8,128)(2,1)S(1)} %collective-permute-done.21.refs_3_, ...), custom_call_target="tpu_custom_call" | custom-call | flops 2147483648 | bytes 11534336 | tf_op jit(solution)/shard_map/combine/pallas_call | solution.py:355
  86.2 0.0 collective-permute-done.15.refs_6_
  86.2 0.0 collective-permute-done.14.refs_5_
  86.2 6.3 %combine.3 = (bf16[128,2048]{1,0:T(8,128)(2,1)S(1)}, f32[128,2048]{1,0:T(8,128)S(1)}) custom-call(bf16[32,2048]{1,0:T(8,128)(2,1)S(1)} %attend.2.refs_0_, bf16[32,2048]{1,0:T(8,128)(2,1)S(1)} %collective-permute-done.10.refs_1_, bf16[32,2048]{1,0:T(8,128)(2,1)S(1)} %collective-permute-done.11.refs_2_, bf16[32,2048]{1,0:T(8,128)(2,1)S(1)} %collective-permute-done.12.refs_3_, ...), custom_call_target="tpu_custom_call" | custom-call | flops 2147483648 | bytes 11534336 | tf_op jit(solution)/shard_map/combine/pallas_call | solution.py:355
  92.5 0.1 collective-permute-start.26
  92.6 1.9 %collective-permute-done.26 = bf16[128,2048]{1,0:T(8,128)(2,1)S(1)} collective-permute-done((bf16[128,2048]{1,0:T(8,128)(2,1)S(1)}, bf16[128,2048]{1,0:T(8,128)(2,1)S(1)}, u32[]{:S(2)}, u32[]{:S(2)}) %collective-permute-start.26) | collective-permute-done | bytes 524320 | tf_op jit(solution)/shard_map/ppermute | solution.py:469
  94.5 0.9 add_convert_fusion
  (21 shorter events, 0.4 us)
Async XLA Ops:
  0.0 0.7 copy-start
  0.7 6.6 %copy-start.1 = (s32[8]{0:T(128)S(1)}, s32[8]{0:T(128)}, u32[]{:S(2)}) copy-start(s32[8]{0:T(128)} %length_ref.3) | copy-start | bytes 100
  4.3 7.7 %collective-permute-start = (bf16[128,1152]{1,0:T(8,128)(2,1)S(1)}, bf16[128,1152]{1,0:T(8,128)(2,1)S(1)}, u32[]{:S(2)}, u32[]{:S(2)}) collective-permute-start(bf16[128,1152]{1,0:T(8,128)(2,1)S(1)} %get-tuple-element.31), channel_id=1, source_target_pairs={{0,2},{1,5},{2,0},{3,7},{4,6},{5,1},{6,4},{7,3},{8,10},{9,13},{10,... | collective-permute-start | bytes 884744 | tf_op jit(solution)/shard_map/ppermute | solution.py:51
  12.1 6.9 %collective-permute-start.1 = (bf16[64,1152]{1,0:T(8,128)(2,1)S(1)}, bf16[64,1152]{1,0:T(8,128)(2,1)S(1)}, u32[]{:S(2)}, u32[]{:S(2)}) collective-permute-start(bf16[64,1152]{1,0:T(8,128)(2,1)S(1)} %add_convert_fusion.3), channel_id=1, source_target_pairs={{0,4},{1,3},{2,6},{3,1},{4,0},{5,7},{6,2},{7,5},{8,12},{9,11},{10,... | collective-permute-start | bytes 442376 | tf_op jit(solution)/shard_map/ppermute | solution.py:51
  14.4 7.1 %collective-permute-start.2 = (bf16[128,1280]{1,0:T(8,128)(2,1)S(1)}, bf16[128,1280]{1,0:T(8,128)(2,1)S(1)}, u32[]{:S(2)}, u32[]{:S(2)}) collective-permute-start(bf16[128,1280]{1,0:T(8,128)(2,1)S(1)} %get-tuple-element.37), channel_id=1, source_target_pairs={{0,2},{1,5},{2,0},{3,7},{4,6},{5,1},{6,4},{7,3},{8,10},{9,13},{10,... | collective-permute-start | bytes 983048 | tf_op jit(solution)/shard_map/ppermute | solution.py:51
  21.5 9.1 %collective-permute-start.17 = (bf16[64,1280]{1,0:T(8,128)(2,1)S(1)}, bf16[64,1280]{1,0:T(8,128)(2,1)S(1)}, u32[]{:S(2)}, u32[]{:S(2)}) collective-permute-start(bf16[64,1280]{1,0:T(8,128)(2,1)S(1)} %add_convert_fusion.2), channel_id=1, source_target_pairs={{0,4},{1,3},{2,6},{3,1},{4,0},{5,7},{6,2},{7,5},{8,12},{9,11},{10,... | collective-permute-start | bytes 491528 | tf_op jit(solution)/shard_map/ppermute | solution.py:51
  21.7 9.7 %collective-permute-start.9 = (bf16[32,1152]{1,0:T(8,128)(2,1)S(1)}, bf16[32,1152]{1,0:T(8,128)(2,1)S(1)}, u32[]{:S(2)}, u32[]{:S(2)}) collective-permute-start(bf16[32,1152]{1,0:T(8,128)(2,1)S(1)} %add_convert_fusion.7), channel_id=1, source_target_pairs={{0,8},{1,9},{2,10},{3,11},{4,12},{5,13},{6,14},{7,15},{8,0},{9,1},... | collective-permute-start | bytes 221192 | tf_op jit(solution)/shard_map/ppermute | solution.py:51
  24.7 13.2 %collective-permute-start.3 = (bf16[128,1024]{1,0:T(8,128)(2,1)S(1)}, bf16[128,1024]{1,0:T(8,128)(2,1)S(1)}, u32[]{:S(2)}, u32[]{:S(2)}) collective-permute-start(bf16[128,1024]{1,0:T(8,128)(2,1)S(1)} %get-tuple-element.39), channel_id=1, source_target_pairs={{0,2},{1,5},{2,0},{3,7},{4,6},{5,1},{6,4},{7,3},{8,10},{9,13},{10,... | collective-permute-start | bytes 786440 | tf_op jit(solution)/shard_map/ppermute | solution.py:51
  30.1 16.0 %collective-permute-start.6 = (bf16[128,1280]{1,0:T(8,128)(2,1)S(1)}, bf16[128,1280]{1,0:T(8,128)(2,1)S(1)}, u32[]{:S(2)}, u32[]{:S(2)}) collective-permute-start(bf16[128,1280]{1,0:T(8,128)(2,1)S(1)} %get-tuple-element.42), channel_id=1, source_target_pairs={{0,2},{1,5},{2,0},{3,7},{4,6},{5,1},{6,4},{7,3},{8,10},{9,13},{10,... | collective-permute-start | bytes 983048 | tf_op jit(solution)/shard_map/ppermute | solution.py:51
  30.7 7.2 %collective-permute-start.18 = (bf16[32,1280]{1,0:T(8,128)(2,1)S(1)}, bf16[32,1280]{1,0:T(8,128)(2,1)S(1)}, u32[]{:S(2)}, u32[]{:S(2)}) collective-permute-start(bf16[32,1280]{1,0:T(8,128)(2,1)S(1)} %add_convert_fusion.5), channel_id=1, source_target_pairs={{0,8},{1,9},{2,10},{3,11},{4,12},{5,13},{6,14},{7,15},{8,0},{9,1},... | collective-permute-start | bytes 245768 | tf_op jit(solution)/shard_map/ppermute | solution.py:51
  42.2 28.3 %collective-permute-start.22 = (bf16[32,2048]{1,0:T(8,128)(2,1)S(1)}, bf16[32,2048]{1,0:T(8,128)(2,1)S(1)}, u32[]{:S(2)}, u32[]{:S(2)}) collective-permute-start(bf16[32,2048]{1,0:T(8,128)(2,1)S(1)} %attend.3.refs_0_), channel_id=1, source_target_pairs={{0,2},{1,5},{2,0},{3,7},{4,6},{5,1},{6,4},{7,3},{8,10},{9,13},{10,... | collective-permute-start | bytes 393224 | tf_op jit(solution)/shard_map/ppermute | solution.py:51
  43.7 24.7 %collective-permute-start.20 = (bf16[32,2048]{1,0:T(8,128)(2,1)S(1)}, bf16[32,2048]{1,0:T(8,128)(2,1)S(1)}, u32[]{:S(2)}, u32[]{:S(2)}) collective-permute-start(bf16[32,2048]{1,0:T(8,128)(2,1)S(1)} %attend.3.refs_0_), channel_id=1, source_target_pairs={{0,4},{1,3},{2,6},{3,1},{4,0},{5,7},{6,2},{7,5},{8,12},{9,11},{10,... | collective-permute-start | bytes 393224 | tf_op jit(solution)/shard_map/ppermute | solution.py:51
  43.7 22.4 %collective-permute-start.19 = (bf16[32,2048]{1,0:T(8,128)(2,1)S(1)}, bf16[32,2048]{1,0:T(8,128)(2,1)S(1)}, u32[]{:S(2)}, u32[]{:S(2)}) collective-permute-start(bf16[32,2048]{1,0:T(8,128)(2,1)S(1)} %attend.3.refs_0_), channel_id=1, source_target_pairs={{0,8},{1,9},{2,10},{3,11},{4,12},{5,13},{6,14},{7,15},{8,0},{9,1},... | collective-permute-start | bytes 393224 | tf_op jit(solution)/shard_map/ppermute | solution.py:51
  46.1 6.2 %collective-permute-start.4 = (bf16[64,1024]{1,0:T(8,128)(2,1)S(1)}, bf16[64,1024]{1,0:T(8,128)(2,1)S(1)}, u32[]{:S(2)}, u32[]{:S(2)}) collective-permute-start(bf16[64,1024]{1,0:T(8,128)(2,1)S(1)} %add_convert_fusion.4), channel_id=1, source_target_pairs={{0,4},{1,3},{2,6},{3,1},{4,0},{5,7},{6,2},{7,5},{8,12},{9,11},{10,... | collective-permute-start | bytes 393224 | tf_op jit(solution)/shard_map/ppermute | solution.py:51
  46.2 9.4 %collective-permute-start.7 = (bf16[64,1280]{1,0:T(8,128)(2,1)S(1)}, bf16[64,1280]{1,0:T(8,128)(2,1)S(1)}, u32[]{:S(2)}, u32[]{:S(2)}) collective-permute-start(bf16[64,1280]{1,0:T(8,128)(2,1)S(1)} %add_convert_fusion.1), channel_id=1, source_target_pairs={{0,4},{1,3},{2,6},{3,1},{4,0},{5,7},{6,2},{7,5},{8,12},{9,11},{10,... | collective-permute-start | bytes 491528 | tf_op jit(solution)/shard_map/ppermute | solution.py:51
  52.4 5.9 %collective-permute-start.5 = (bf16[32,1024]{1,0:T(8,128)(2,1)S(1)}, bf16[32,1024]{1,0:T(8,128)(2,1)S(1)}, u32[]{:S(2)}, u32[]{:S(2)}) collective-permute-start(bf16[32,1024]{1,0:T(8,128)(2,1)S(1)} %add_convert_fusion.8), channel_id=1, source_target_pairs={{0,8},{1,9},{2,10},{3,11},{4,12},{5,13},{6,14},{7,15},{8,0},{9,1},... | collective-permute-start | bytes 196616 | tf_op jit(solution)/shard_map/ppermute | solution.py:51
  55.6 6.2 %collective-permute-start.8 = (bf16[32,1280]{1,0:T(8,128)(2,1)S(1)}, bf16[32,1280]{1,0:T(8,128)(2,1)S(1)}, u32[]{:S(2)}, u32[]{:S(2)}) collective-permute-start(bf16[32,1280]{1,0:T(8,128)(2,1)S(1)} %add_convert_fusion.6), channel_id=1, source_target_pairs={{0,8},{1,9},{2,10},{3,11},{4,12},{5,13},{6,14},{7,15},{8,0},{9,1},... | collective-permute-start | bytes 245768 | tf_op jit(solution)/shard_map/ppermute | solution.py:51
  66.0 7.0 %collective-permute-start.10 = (bf16[32,2048]{1,0:T(8,128)(2,1)S(1)}, bf16[32,2048]{1,0:T(8,128)(2,1)S(1)}, u32[]{:S(2)}, u32[]{:S(2)}) collective-permute-start(bf16[32,2048]{1,0:T(8,128)(2,1)S(1)} %attend.2.refs_0_), channel_id=1, source_target_pairs={{0,8},{1,9},{2,10},{3,11},{4,12},{5,13},{6,14},{7,15},{8,0},{9,1},... | collective-permute-start | bytes 393224 | tf_op jit(solution)/shard_map/ppermute | solution.py:51
  66.1 8.1 %collective-permute-start.21 = (bf16[32,2048]{1,0:T(8,128)(2,1)S(1)}, bf16[32,2048]{1,0:T(8,128)(2,1)S(1)}, u32[]{:S(2)}, u32[]{:S(2)}) collective-permute-start(bf16[32,2048]{1,0:T(8,128)(2,1)S(1)} %collective-permute-done.19.refs_1_), channel_id=1, source_target_pairs={{0,4},{1,3},{2,6},{3,1},{4,0},{5,7},{6,2},{7,5},{8,12},{9,11},{10,... | collective-permute-start | bytes 393224 | tf_op jit(solution)/shard_map/ppermute | solution.py:51
  68.4 5.8 %collective-permute-start.24 = (bf16[32,2048]{1,0:T(8,128)(2,1)S(1)}, bf16[32,2048]{1,0:T(8,128)(2,1)S(1)}, u32[]{:S(2)}, u32[]{:S(2)}) collective-permute-start(bf16[32,2048]{1,0:T(8,128)(2,1)S(1)} %collective-permute-done.20.refs_2_), channel_id=1, source_target_pairs={{0,2},{1,5},{2,0},{3,7},{4,6},{5,1},{6,4},{7,3},{8,10},{9,13},{10,... | collective-permute-start | bytes 393224 | tf_op jit(solution)/shard_map/ppermute | solution.py:51
  68.4 7.8 %collective-permute-start.23 = (bf16[32,2048]{1,0:T(8,128)(2,1)S(1)}, bf16[32,2048]{1,0:T(8,128)(2,1)S(1)}, u32[]{:S(2)}, u32[]{:S(2)}) collective-permute-start(bf16[32,2048]{1,0:T(8,128)(2,1)S(1)} %collective-permute-done.19.refs_1_), channel_id=1, source_target_pairs={{0,2},{1,5},{2,0},{3,7},{4,6},{5,1},{6,4},{7,3},{8,10},{9,13},{10,... | collective-permute-start | bytes 393224 | tf_op jit(solution)/shard_map/ppermute | solution.py:51
  70.5 6.6 %collective-permute-start.11 = (bf16[32,2048]{1,0:T(8,128)(2,1)S(1)}, bf16[32,2048]{1,0:T(8,128)(2,1)S(1)}, u32[]{:S(2)}, u32[]{:S(2)}) collective-permute-start(bf16[32,2048]{1,0:T(8,128)(2,1)S(1)} %attend.2.refs_0_), channel_id=1, source_target_pairs={{0,4},{1,3},{2,6},{3,1},{4,0},{5,7},{6,2},{7,5},{8,12},{9,11},{10,... | collective-permute-start | bytes 393224 | tf_op jit(solution)/shard_map/ppermute | solution.py:51
  73.1 6.8 %collective-permute-start.12 = (bf16[32,2048]{1,0:T(8,128)(2,1)S(1)}, bf16[32,2048]{1,0:T(8,128)(2,1)S(1)}, u32[]{:S(2)}, u32[]{:S(2)}) collective-permute-start(bf16[32,2048]{1,0:T(8,128)(2,1)S(1)} %collective-permute-done.10.refs_1_), channel_id=1, source_target_pairs={{0,4},{1,3},{2,6},{3,1},{4,0},{5,7},{6,2},{7,5},{8,12},{9,11},{10,... | collective-permute-start | bytes 393224 | tf_op jit(solution)/shard_map/ppermute | solution.py:51
  74.2 5.6 %collective-permute-start.25 = (bf16[32,2048]{1,0:T(8,128)(2,1)S(1)}, bf16[32,2048]{1,0:T(8,128)(2,1)S(1)}, u32[]{:S(2)}, u32[]{:S(2)}) collective-permute-start(bf16[32,2048]{1,0:T(8,128)(2,1)S(1)} %collective-permute-done.21.refs_3_), channel_id=1, source_target_pairs={{0,2},{1,5},{2,0},{3,7},{4,6},{5,1},{6,4},{7,3},{8,10},{9,13},{10,... | collective-permute-start | bytes 393224 | tf_op jit(solution)/shard_map/ppermute | solution.py:51
  74.2 11.9 %collective-permute-start.13 = (bf16[32,2048]{1,0:T(8,128)(2,1)S(1)}, bf16[32,2048]{1,0:T(8,128)(2,1)S(1)}, u32[]{:S(2)}, u32[]{:S(2)}) collective-permute-start(bf16[32,2048]{1,0:T(8,128)(2,1)S(1)} %attend.2.refs_0_), channel_id=1, source_target_pairs={{0,2},{1,5},{2,0},{3,7},{4,6},{5,1},{6,4},{7,3},{8,10},{9,13},{10,... | collective-permute-start | bytes 393224 | tf_op jit(solution)/shard_map/ppermute | solution.py:51
  76.3 9.9 %collective-permute-start.14 = (bf16[32,2048]{1,0:T(8,128)(2,1)S(1)}, bf16[32,2048]{1,0:T(8,128)(2,1)S(1)}, u32[]{:S(2)}, u32[]{:S(2)}) collective-permute-start(bf16[32,2048]{1,0:T(8,128)(2,1)S(1)} %collective-permute-done.10.refs_1_), channel_id=1, source_target_pairs={{0,2},{1,5},{2,0},{3,7},{4,6},{5,1},{6,4},{7,3},{8,10},{9,13},{10,... | collective-permute-start | bytes 393224 | tf_op jit(solution)/shard_map/ppermute | solution.py:51
  77.0 9.1 %collective-permute-start.15 = (bf16[32,2048]{1,0:T(8,128)(2,1)S(1)}, bf16[32,2048]{1,0:T(8,128)(2,1)S(1)}, u32[]{:S(2)}, u32[]{:S(2)}) collective-permute-start(bf16[32,2048]{1,0:T(8,128)(2,1)S(1)} %collective-permute-done.11.refs_2_), channel_id=1, source_target_pairs={{0,2},{1,5},{2,0},{3,7},{4,6},{5,1},{6,4},{7,3},{8,10},{9,13},{10,... | collective-permute-start | bytes 393224 | tf_op jit(solution)/shard_map/ppermute | solution.py:51
  79.8 6.3 %collective-permute-start.16 = (bf16[32,2048]{1,0:T(8,128)(2,1)S(1)}, bf16[32,2048]{1,0:T(8,128)(2,1)S(1)}, u32[]{:S(2)}, u32[]{:S(2)}) collective-permute-start(bf16[32,2048]{1,0:T(8,128)(2,1)S(1)} %collective-permute-done.12.refs_3_), channel_id=1, source_target_pairs={{0,2},{1,5},{2,0},{3,7},{4,6},{5,1},{6,4},{7,3},{8,10},{9,13},{10,... | collective-permute-start | bytes 393224 | tf_op jit(solution)/shard_map/ppermute | solution.py:51
  92.5 2.0 %collective-permute-start.26 = (bf16[128,2048]{1,0:T(8,128)(2,1)S(1)}, bf16[128,2048]{1,0:T(8,128)(2,1)S(1)}, u32[]{:S(2)}, u32[]{:S(2)}) collective-permute-start(bf16[128,2048]{1,0:T(8,128)(2,1)S(1)} %get-tuple-element.48), channel_id=1, source_target_pairs={{0,1},{1,0},{2,3},{3,2},{4,5},{5,4},{6,7},{7,6},{8,9},{9,8},{10,11... | collective-permute-start | bytes 1572872 | tf_op jit(solution)/shard_map/ppermute | solution.py:469

commit v3 on v2

--- a/solution.py
+++ b/solution.py
@@ -15,7 +15,7 @@
 THETA = 500000.0
 
 CHUNKS = 2
-PARTS = 2
+TILES = 4
 MIB = 1 << 20
 
 
@@ -54,7 +54,7 @@
 def project_kernel(n, q_start, kv_start, first, *refs):
     if first:
         tokens_ref, gain_ref, wq_ref, wk_ref, wv_ref, send_ref, keep_ref, x_ref = refs[:8]
-        t_buf, t_sems = refs[8:10]
+        t_buf, t_sems, g_buf, g_sem = refs[8:12]
     else:
         x_ref, wq_ref, wk_ref, wv_ref, send_ref, keep_ref = refs[:6]
     w_buf, sems = refs[-2:]
@@ -88,15 +88,18 @@
                 )
             )
             t_copies[-1].start()
+        g_copy = pltpu.make_async_copy(gain_ref, g_buf, g_sem)
+        g_copy.start()
     for group in copies:
         for copy in group:
             copy.start()
     if first:
         lanes = lax.broadcasted_iota(jnp.int32, (block, 128), 1)
+        g_copy.wait()
         for slot in range(n):
             t_copies[slot].wait()
             wide = t_buf[slot].astype(jnp.float32)
-            x_ref[slot * block : (slot + 1) * block, :] = (wide * gain_ref[...]).astype(jnp.bfloat16)
+            x_ref[slot * block : (slot + 1) * block, :] = (wide * g_buf[...]).astype(jnp.bfloat16)
             square = jnp.sum(wide * wide, axis=1, keepdims=True)
             high = square.astype(jnp.bfloat16).astype(jnp.float32)
             rest = square - high
@@ -121,6 +124,10 @@
         send_ref[:, start:end] = product[half:].astype(jnp.bfloat16)
 
 
+def in_vmem(value):
+    return pltpu.with_memory_space_constraint(value, pltpu.VMEM)
+
+
 def in_hbm(value):
     return pltpu.with_memory_space_constraint(value, pltpu.HBM)
 
@@ -139,11 +146,13 @@
     scratch = [pltpu.VMEM((depth, width), jnp.bfloat16), pltpu.SemaphoreType.DMA((4,))]
     if first:
         out_shape.append(pltpu.VMEM((rows, depth), jnp.bfloat16))
-        args = [in_hbm(x), gain]
-        in_specs = [hbm, vmem]
+        args = [in_hbm(x), in_hbm(gain)]
+        in_specs = [hbm, hbm]
         scratch = [
             pltpu.VMEM((n, rows // n, depth), jnp.bfloat16),
             pltpu.SemaphoreType.DMA((n,)),
+            pltpu.VMEM((1, depth), jnp.float32),
+            pltpu.SemaphoreType.DMA,
         ] + scratch
     else:
         args, in_specs = [x], [vmem]
@@ -163,25 +172,13 @@
     )(*args, in_hbm(w_query), in_hbm(w_key), in_hbm(w_value))
 
 
-def attend_kernel(chunk, parts, groups, heads, seqs, length_ref, *refs):
-    sums, square_ref = refs[:parts], refs[parts]
-    cos_ref, sin_ref, k_ref, v_ref, out_ref, k_buf, v_buf, q_scr, o_scr, sems = refs[parts + 1 :]
+def attend_kernel(chunk, offsets, kv_offset, groups, heads, seqs, length_ref, *refs):
+    sum_ref, square_ref = refs[:2]
+    cos_ref, sin_ref, k_ref, v_ref, out_ref, q_scr, o_scr = refs[2:]
     rows = seqs * NEW
     cols = groups * heads * HD
     kv = groups * HD
     seq_count = k_ref.shape[0]
-    share = cols // parts
-
-    def cache_copy(kind, b):
-        source, target = ((k_ref, k_buf), (v_ref, v_buf))[kind]
-        return pltpu.make_async_copy(
-            source.at[b, :, pl.ds(chunk * kv, kv)], target.at[b], sems.at[kind, b]
-        )
-
-    for start in range(0, seq_count, seqs):
-        for kind in range(2):
-            for b in range(start, start + seqs):
-                cache_copy(kind, b).start()
 
     scale = HD**-0.5 * math.log2(math.e)
     slots = k_ref.shape[1]
@@ -197,27 +194,24 @@
         row_scale = lax.rsqrt(mean + EPS)
         cosine, sine = cos_ref[mine, :], sin_ref[mine, :]
 
-        def raw(part, start):
-            return sums[part][mine, start : start + HD] * row_scale
+        def raw(start):
+            return sum_ref[mine, start : start + HD] * row_scale
 
         def rotary(value):
             return value * cosine + pltpu.roll(value, HD // 2, 1) * sine
 
         for h in range(heads * groups):
-            turned = rotary(raw(h * HD // share, h * HD % share))
+            turned = rotary(raw(offsets[h]))
             for s in range(seqs):
                 q_scr[s, h * NEW : (h + 1) * NEW, :] = turned[s * NEW : (s + 1) * NEW]
-        for s in range(seqs):
-            cache_copy(0, step * seqs + s).wait()
-            cache_copy(1, step * seqs + s).wait()
         for g in range(groups):
-            new_keys = rotary(raw(parts - 1, share + g * HD)).astype(jnp.bfloat16)
-            new_values = raw(parts - 1, share + (groups + g) * HD).astype(jnp.bfloat16)
-            lanes = slice(g * HD, (g + 1) * HD)
+            new_keys = rotary(raw(kv_offset + g * HD)).astype(jnp.bfloat16)
+            new_values = raw(kv_offset + (groups + g) * HD).astype(jnp.bfloat16)
+            lanes = slice(chunk * kv + g * HD, chunk * kv + (g + 1) * HD)
             olds, news, mixes = [], [], []
             for s in range(seqs):
                 query = q_scr[s, g * many : (g + 1) * many, :].astype(jnp.bfloat16)
-                keys = k_buf[step * seqs + s, :, lanes]
+                keys = k_ref[step * seqs + s, :, lanes]
                 olds.append(
                     lax.dot_general(
                         query, keys, (((1,), (1,)), ((), ())), preferred_element_type=jnp.float32
@@ -243,7 +237,7 @@
                 olds[s] = (old * inverse).astype(jnp.bfloat16)
                 news[s] = (new * inverse).astype(jnp.bfloat16)
             for s in range(seqs):
-                values = v_buf[step * seqs + s, :, lanes]
+                values = v_ref[step * seqs + s, :, lanes]
                 mixes.append(
                     jnp.dot(olds[s], values, preferred_element_type=jnp.float32)
                     + jnp.dot(news[s], new_values, preferred_element_type=jnp.float32)
@@ -257,29 +251,25 @@
         out_ref[mine, :] = o_scr[...].astype(jnp.bfloat16)
 
 
-def attend(chunk, sums, squares, cosine, sine, cache_keys, cache_values, lengths):
+def attend(chunk, offsets, kv_offset, sums, squares, cosine, sine, cache_keys, cache_values, lengths):
     seq_count, slots, kv_all = cache_keys.shape
     kv = kv_all // CHUNKS
     groups = kv // HD
-    parts = len(sums)
-    cols = parts * (sums[-1].shape[1] - 2 * kv)
-    heads = cols // kv
+    heads = len(offsets) // groups
+    cols = len(offsets) * HD
     seqs = min(4, seq_count)
     rows = seq_count * NEW
     vmem = pl.BlockSpec(memory_space=pltpu.VMEM)
     hbm = pl.BlockSpec(memory_space=pltpu.HBM)
     flops = 4 * seq_count * groups * heads * NEW * slots * HD
     return pl.pallas_call(
-        functools.partial(attend_kernel, chunk, parts, groups, heads, seqs),
+        functools.partial(attend_kernel, chunk, offsets, kv_offset, groups, heads, seqs),
         out_shape=pltpu.VMEM((rows, cols), jnp.bfloat16),
-        in_specs=[pl.BlockSpec(memory_space=pltpu.SMEM)] + [vmem] * (parts + 3) + [hbm] * 2,
+        in_specs=[pl.BlockSpec(memory_space=pltpu.SMEM)] + [vmem] * 6,
         out_specs=vmem,
         scratch_shapes=[
-            pltpu.VMEM((seq_count, slots, kv), jnp.bfloat16),
-            pltpu.VMEM((seq_count, slots, kv), jnp.bfloat16),
             pltpu.VMEM((seqs, groups * heads * NEW, HD), jnp.float32),
             pltpu.VMEM((seqs * NEW, cols), jnp.float32),
-            pltpu.SemaphoreType.DMA((2, seq_count)),
         ],
         compiler_params=pltpu.CompilerParams(vmem_limit_bytes=16 * MIB),
         cost_estimate=pl.CostEstimate(
@@ -288,7 +278,7 @@
             transcendentals=seq_count * groups * heads * NEW * slots,
         ),
         name="attend",
-    )(lengths, *sums, squares, cosine, sine, in_hbm(cache_keys), in_hbm(cache_values))
+    )(lengths, sums, squares, cosine, sine, in_vmem(cache_keys), in_vmem(cache_values))
 
 
 def combine_kernel(n, block, chunk, *refs):
@@ -297,19 +287,9 @@
     moved = jnp.where(gy == 0, n // 2, 0)
     if chunk:
         before_ref, refs = refs[0], refs[1:]
-    w_ref, outs, (x_buf, w_buf, w_sems, x_sems) = refs[0], refs[1:-4], refs[-4:]
-    depth, cols = w_buf.shape
+    w_ref, outs, (x_buf, x_sems) = refs[0], refs[1:-2], refs[-2:]
+    depth, cols = x_buf.shape[1], w_ref.shape[1]
     half = x_buf.shape[0] // 2
-    part = cols // PARTS
-    tile = part // 2
-
-    def w_copy(at):
-        return pltpu.make_async_copy(
-            w_ref.at[chunk * depth : (chunk + 1) * depth, at : at + tile],
-            w_buf.at[:, at : at + tile],
-            w_sems.at[at // tile],
-        )
-
     x_copies = []
     for slot, piece in enumerate(pieces):
         start = pl.multiple_of((slot_owner(n, slot, gx, gy) ^ moved) * block, block)
@@ -318,16 +298,14 @@
         )
     for copy in x_copies:
         copy.start()
-    for at in range(0, cols, tile):
-        w_copy(at).start()
     for copy in x_copies:
         copy.wait()
 
-    for start in range(0, cols, part):
-        for at in range(start, start + part, tile):
-            w_copy(at).wait()
-        at = slice(start, start + part)
-        product = jnp.dot(x_buf[...], w_buf[:, at], preferred_element_type=jnp.float32)
+    rows = slice(chunk * depth, (chunk + 1) * depth)
+    tile = cols // TILES
+    for start in range(0, cols, tile):
+        at = slice(start, start + tile)
+        product = jnp.dot(x_buf[...], w_ref[rows, at], preferred_element_type=jnp.float32)
         if chunk:
             product = product + before_ref[:, at]
         if len(outs) == 1:
@@ -357,12 +335,10 @@
         out_shape=out_shape,
         in_specs=[pl.BlockSpec(memory_space=pl.ANY)] * len(pieces)
         + [vmem] * len(earlier)
-        + [hbm],
+        + [vmem],
         out_specs=[vmem] * len(out_shape),
         scratch_shapes=[
             pltpu.VMEM((rows, depth), jnp.bfloat16),
-            pltpu.VMEM((depth, cols), jnp.bfloat16),
-            pltpu.SemaphoreType.DMA((2 * PARTS,)),
             pltpu.SemaphoreType.DMA((n,)),
         ],
         compiler_params=pltpu.CompilerParams(vmem_limit_bytes=16 * MIB),
@@ -372,34 +348,7 @@
             transcendentals=0,
         ),
         name="combine",
-    )(*pieces, *earlier, in_hbm(w_out))
-
-
-class Flow:
-    def __init__(self, n, cores, levels, send, keep):
-        self.n, self.cores, self.levels = n, cores, levels
-        self.send, self.keep = send, keep
-        self.rows = keep.shape[0]
-        self.received = []
-        self.value = None
-        self.sends = []
-
-    def start_exchange(self):
-        stage = len(self.received)
-        if stage < self.levels:
-            self.sends.append(self.send)
-            self.received.append(exchange(self.send, self.n, self.cores, stage))
-
-    def add_received(self):
-        if self.value is not None and len(self.received) == self.levels and self.rows == 0:
-            return
-        low = self.rows // 2 if len(self.received) < self.levels else 0
-        value = self.keep[low : self.rows]
-        for other in self.received:
-            value = value + other[low : self.rows].astype(jnp.float32)
-        self.value = value
-        self.send = value.astype(jnp.bfloat16)
-        self.rows = low
+    )(*pieces, *earlier, in_vmem(w_out))
 
 
 def shards(
@@ -417,39 +366,63 @@
 
     x, gain = tokens, norm_gain[None, :]
     kv = w_key.shape[1] // CHUNKS
-    q_cols = w_query.shape[1] // (CHUNKS * PARTS)
-    count = CHUNKS * PARTS
-    flows = []
-    for part in range(count + levels):
-        if part < count:
-            kv_start = part // PARTS * kv if part % PARTS == PARTS - 1 else None
-            out = project(
-                n, part * q_cols, q_cols, kv_start, part == 0, x, gain, w_query, w_key, w_value
-            )
-            if part == 0:
-                x = out[2]
-            flows.append(Flow(n, cores, levels, out[0], out[1]))
-        for flow in flows[max(0, part - levels) : part]:
-            flow.add_received()
-        if part + 1 < count:
-            waiting = flows[max(0, part - levels) : part + 1]
-            tied = lax.optimization_barrier((x, [flow.send for flow in waiting]))
-            x = tied[0]
-            for flow, send in zip(waiting, tied[1]):
-                flow.send = send
-        for flow in flows[max(0, part - levels) : part + 1]:
-            flow.start_exchange()
-    sums = [flow.value for flow in flows]
-    squares = sums[0][:, q_cols:]
+    q_cols = w_query.shape[1] // CHUNKS
+
+    def column_part(start, size, kv_start):
+        return project(
+            n, start, size, kv_start, start == 0, x, gain, w_query, w_key, w_value
+        )
+
+    def after(value, *earlier):
+        return lax.optimization_barrier((value, earlier))[0]
+
+    share = q_cols // 2
+    send_a, keep_a, x = column_part(0, share, None)
+    x = after(x, send_a)
+    other_a = exchange(send_a, n, cores, 0)
+    send_b, keep_b = column_part(share, share, 0)
+    x = after(x, send_b)
+    other_b = exchange(send_b, n, cores, 0)
+    sum_a = keep_a + other_a.astype(jnp.float32)
+    x = after(x, sum_a)
+    later = []
+    for chunk in range(1, CHUNKS):
+        later.append(column_part(chunk * q_cols, q_cols, chunk * kv))
+    other_b = after(other_b, *(send_c for send_c, _ in later))
+    first = jnp.concatenate([sum_a, keep_b + other_b.astype(jnp.float32)], axis=1)
+    half = first.shape[0] // 2
+    send = first[half:].astype(jnp.bfloat16)
+    flows = [[1, first[:half], send]]
+    for send_c, keep_c in later:
+        flows.append([0, keep_c, after(send_c, flows[-1][2])])
+
+    def step(flow, *earlier):
+        stage, keep, send = flow
+        other = exchange(send, n, cores, stage)
+        if earlier:
+            other = after(other, *earlier)
+        value = keep + other.astype(jnp.float32)
+        low = value.shape[0] // 2 if stage < levels - 1 else 0
+        flow[:] = stage + 1, value[:low] if low else value, value[low:].astype(jnp.bfloat16)
+
+    lead, follow = flows
+    while follow[0] < levels:
+        if lead[0] < levels:
+            step(lead)
+        step(follow, *([lead[2]] if lead[0] < levels else []))
+    sums = [flow[1] for flow in flows]
+    squares = sums[0][:, share : share + 128]
+    plain = [h * HD for h in range(q_cols // HD)]
+    offsets = [[at if at < share else at + 128 for at in plain], plain]
+    kv_offsets = [q_cols + 128, q_cols]
 
     gathered = []
     for chunk in range(CHUNKS):
-        mine = sums[chunk * PARTS : (chunk + 1) * PARTS]
-        if chunk < CHUNKS - 1 and levels > 1:
-            mine, _ = lax.optimization_barrier((mine, flows[(chunk + 1) * PARTS].sends[1]))
         attention = attend(
             chunk,
-            mine,
+            offsets[chunk],
+            kv_offsets[chunk],
+            sums[chunk],
             squares,
             cosine,
             sine,

time: 95.6 us -> 97.6 us (1.021)
  local copies, waits for them, and re-layouts: 0.78 us -> 11.7 us
  Pallas kernels: 35.4 us -> 27.1 us
  waiting for transfers between devices: 28.8 us -> 22.2 us
  starting transfers between devices: 28.6 us -> 33.4 us
  other arithmetic: 1.58 us -> 2.78 us
    unnamed x4 -> x10, local copies, waits for them, and re-layouts: 0.7 us -> 11.5 us
    ppermute x26 -> x21, waiting for transfers between devices: 26.9 us -> 20.3 us  [exchange(): return lax.ppermute(value, ('gx', 'gy'), pairs)]
    pallas_call x2, Pallas kernels: 12.6 us -> 7.61 us  [combine(): pl.pallas_call(functools.partial(combine_kernel, n, block, chunk), out_sh...]
    ppermute x26 -> x21, starting transfers between devices: 28.6 us -> 33.3 us  [exchange(): return lax.ppermute(value, ('gx', 'gy'), pairs)]
    pallas_call x2, Pallas kernels: 8.43 us -> 5.78 us  [attend(): pl.pallas_call(functools.partial(attend_kernel, chunk, offsets, kv_offset...]
    add x4 -> x7, other arithmetic: 0.14 us -> 1.54 us  [the longest x5 1.43 us: step(): value = keep + other.astype(jnp.float32)]
    pallas_call x4 -> x3, Pallas kernels: 14.4 us -> 13.8 us  [project(): pl.pallas_call(functools.partial(project_kernel, n, q_start, kv_start, fi...]
  transfers between devices with their start and end apart: 27 -> 22, of which waited for: 12 -> 10; matrix products, arithmetic and copies ran while one was open for 1% -> 2% of each run, Pallas kernels for 27% -> 19%
where the time goes in v3:
time: 97.6 us; the launch traced here: 97.5 us
  starting transfers between devices  33.4 us (34%)
  Pallas kernels  27.1 us (28%)
  waiting for transfers between devices  22.2 us (23%)
  local copies, waits for them, and re-layouts  11.7 us (12%)
  other arithmetic  2.78 us (3%)
    ppermute x21, starting transfers between devices, exchange(): return lax.ppermute(value, ('gx', 'gy'), pairs)  33.3 us
    ppermute x21, waiting for transfers between devices, exchange(): return lax.ppermute(value, ('gx', 'gy'), pairs)  20.3 us
    pallas_call x3, Pallas kernels, project(): pl.pallas_call(functools.partial(project_kernel, n, q_start, kv_start, fi...  13.8 us
    unnamed x10, local copies, waits for them, and re-layouts  11.5 us
    pallas_call x2, Pallas kernels, combine(): pl.pallas_call(functools.partial(combine_kernel, n, block, chunk), out_sh...  7.61 us
    pallas_call x2, Pallas kernels, attend(): pl.pallas_call(functools.partial(attend_kernel, chunk, offsets, kv_offset...  5.78 us
  transfers between devices with their start and end apart: 22, of which 10 were waited for; matrix products, arithmetic and copies ran while one was open for 2% of the time, Pallas kernels for 19%

profile of v3, /device:TPU:0, one launch (start us, length us, event | category | flops | bytes accessed | tf_op | source)
XLA Modules:
  0.0 97.5 jit_solution(14238997117651511909)
XLA Ops:
  0.0 4.4 %project.3 = (bf16[128,1152]{1,0:T(8,128)(2,1)S(1)}, f32[128,1152]{1,0:T(8,128)S(1)}, bf16[256,2048]{1,0:T(8,128)(2,1)S(1)}) custom-call(bf16[256,2048]{1,0:T(8,128)(2,1)} %refs_0_.1, f32[1,2048]{1,0:T(1,128)} %bitcast.1, bf16[2048,4096]{1,0:T(8,128)(2,1)} %refs_1_.3, bf16[2048,256]{1,0:T(8,128)(2,1)} %refs_2_.5, bf16[2048,256]{1,0:T(8,128)(2,1)} %refs_3_.5), custom_call_target="tpu_custom_call" | custom-call | flops 1073741824 | bytes 6291456 | tf_op jit(solution)/shard_map/project/pallas_call | solution.py:159
  4.4 3.0 %collective-permute-start = (bf16[128,1152]{1,0:T(8,128)(2,1)S(1)}, bf16[128,1152]{1,0:T(8,128)(2,1)S(1)}, u32[]{:S(2)}, u32[]{:S(2)}) collective-permute-start(bf16[128,1152]{1,0:T(8,128)(2,1)S(1)} %get-tuple-element.21), channel_id=1, source_target_pairs={{0,2},{1,5},{2,0},{3,7},{4,6},{5,1},{6,4},{7,3},{8,10},{9,13},{10,... | collective-permute-start | bytes 884744 | tf_op jit(solution)/shard_map/ppermute | solution.py:51
  7.4 3.9 %project.4 = (bf16[128,1280]{1,0:T(8,128)(2,1)S(1)}, f32[128,1280]{1,0:T(8,128)S(1)}) custom-call(bf16[256,2048]{1,0:T(8,128)(2,1)S(1)} %get-tuple-element.26.refs_0_, bf16[2048,4096]{1,0:T(8,128)(2,1)} %refs_1_.3, bf16[2048,256]{1,0:T(8,128)(2,1)} %refs_2_.5, bf16[2048,256]{1,0:T(8,128)(2,1)} %refs_3_.5), custom_call_target="tpu_custom_call" | custom-call | flops 1342177280 | bytes 7340032 | tf_op jit(solution)/shard_map/project/pallas_call | solution.py:159
  11.3 0.1 collective-permute-start.1
  11.4 0.8 collective-permute-done
  12.1 0.1 convert_add_fusion.2
  12.2 5.5 %project.5 = (bf16[128,2304]{1,0:T(8,128)(2,1)S(1)}, f32[128,2304]{1,0:T(8,128)S(1)}) custom-call(bf16[256,2048]{1,0:T(8,128)(2,1)S(1)} %get-tuple-element.26.refs_0_, bf16[2048,4096]{1,0:T(8,128)(2,1)} %refs_1_.3, bf16[2048,256]{1,0:T(8,128)(2,1)} %refs_2_.5, bf16[2048,256]{1,0:T(8,128)(2,1)} %refs_3_.5), custom_call_target="tpu_custom_call" | custom-call | flops 2415919104 | bytes 11534336 | tf_op jit(solution)/shard_map/project/pallas_call | solution.py:159
  17.7 0.7 collective-permute-done.1
  18.4 0.1 convert_add_fusion.1
  18.5 0.0 copy-start.4
  18.5 1.6 %collective-permute-start.3 = (bf16[64,2432]{1,0:T(8,128)(2,1)S(1)}, bf16[64,2432]{1,0:T(8,128)(2,1)}, u32[]{:S(2)}, u32[]{:S(2)}) collective-permute-start(bf16[64,2432]{1,0:T(8,128)(2,1)S(1)} %fusion.1), channel_id=1, source_target_pairs={{0,4},{1,3},{2,6},{3,1},{4,0},{5,7},{6,2},{7,5},{8,12},{9,11},{10,... | collective-permute-start | bytes 933896 | tf_op jit(solution)/shard_map/ppermute | solution.py:51
  20.2 0.1 add_convert_fusion.1
  20.2 0.1 convert_element_type.49
  20.3 1.4 %collective-permute-start.2 = (bf16[128,2304]{1,0:T(8,128)(2,1)S(1)}, bf16[128,2304]{1,0:T(8,128)(2,1)S(1)}, u32[]{:S(2)}, u32[]{:S(2)}) collective-permute-start(bf16[128,2304]{1,0:T(8,128)(2,1)S(1)} %get-tuple-element.31), channel_id=1, source_target_pairs={{0,2},{1,5},{2,0},{3,7},{4,6},{5,1},{6,4},{7,3},{8,10},{9,13},{10,... | collective-permute-start | bytes 1769480 | tf_op jit(solution)/shard_map/ppermute | solution.py:51
  21.7 7.1 %collective-permute-done.3 = bf16[64,2432]{1,0:T(8,128)(2,1)} collective-permute-done((bf16[64,2432]{1,0:T(8,128)(2,1)S(1)}, bf16[64,2432]{1,0:T(8,128)(2,1)}, u32[]{:S(2)}, u32[]{:S(2)}) %collective-permute-start.3) | collective-permute-done | bytes 311328 | tf_op jit(solution)/shard_map/ppermute | solution.py:51
  28.9 1.2 %fusion.2 = f32[64,2432]{1,0:T(8,128)S(1)} fusion(f32[128,1280]{1,0:T(8,128)S(1)} %convert_add_fusion.1, f32[128,1152]{1,0:T(8,128)S(1)} %convert_add_fusion.2, bf16[64,2432]{1,0:T(8,128)(2,1)} %collective-permute-done.3), kind=kLoop, calls=%fused_computation.8 | loop fusion | flops 466944 | bytes 2179072 | tf_op jit(solution)/shard_map/add | solution.py:404
  30.1 0.2 collective-permute-done.2
  30.3 0.1 convert_add_fusion
  30.4 1.5 %collective-permute-start.4 = (bf16[64,2304]{1,0:T(8,128)(2,1)S(1)}, bf16[64,2304]{1,0:T(8,128)(2,1)S(1)}, u32[]{:S(2)}, u32[]{:S(2)}) collective-permute-start(bf16[64,2304]{1,0:T(8,128)(2,1)S(1)} %slice.63), channel_id=1, source_target_pairs={{0,4},{1,3},{2,6},{3,1},{4,0},{5,7},{6,2},{7,5},{8,12},{9,11},{10,... | collective-permute-start | bytes 884744 | tf_op jit(solution)/shard_map/ppermute | solution.py:51
  31.9 0.1 fusion.3
  32.1 0.1 pad_maximum_fusion.1
  32.2 2.6 %collective-permute-start.6 = (bf16[32,2432]{1,0:T(8,128)(2,1)S(1)}, bf16[32,2432]{1,0:T(8,128)(2,1)S(1)}, u32[]{:S(2)}, u32[]{:S(2)}) collective-permute-start(bf16[32,2432]{1,0:T(8,128)(2,1)S(1)} %slice.64), channel_id=1, source_target_pairs={{0,8},{1,9},{2,10},{3,11},{4,12},{5,13},{6,14},{7,15},{8,0},{9,1},... | collective-permute-start | bytes 466952 | tf_op jit(solution)/shard_map/ppermute | solution.py:51
  34.8 5.8 %collective-permute-done.4 = bf16[64,2304]{1,0:T(8,128)(2,1)S(1)} collective-permute-done((bf16[64,2304]{1,0:T(8,128)(2,1)S(1)}, bf16[64,2304]{1,0:T(8,128)(2,1)S(1)}, u32[]{:S(2)}, u32[]{:S(2)}) %collective-permute-start.4) | collective-permute-done | bytes 294944 | tf_op jit(solution)/shard_map/ppermute | solution.py:51
  40.6 0.1 slice_add_fusion
  40.7 1.0 %collective-permute-start.5 = (bf16[32,2304]{1,0:T(8,128)(2,1)S(1)}, bf16[32,2304]{1,0:T(8,128)(2,1)S(1)}, u32[]{:S(2)}, u32[]{:S(2)}) collective-permute-start(bf16[32,2304]{1,0:T(8,128)(2,1)S(1)} %slice.65), channel_id=1, source_target_pairs={{0,8},{1,9},{2,10},{3,11},{4,12},{5,13},{6,14},{7,15},{8,0},{9,1},... | collective-permute-start | bytes 442376 | tf_op jit(solution)/shard_map/ppermute | solution.py:51
  41.6 0.0 collective-permute-done.6
  41.7 3.0 %attend.3.refs_0_ = bf16[32,2048]{1,0:T(8,128)(2,1)S(1)} custom-call(s32[8]{0:T(128)S(1)} %copy-done.4, f32[32,2432]{1,0:T(8,128)S(1)} %slice_add_fusion.1.refs_0_, f32[32,128]{1,0:T(8,128)S(1)} %slice.48.refs_1_, f32[32,128]{1,0:T(8,128)S(1)} %get-tuple-element.38.refs_2_, f32[32,128]{1,0:T(8,128)S(1)} %get-tuple-element.39.refs_3_, ...), custom_call_target="tpu_custom_call" | custom-call | flops 268435456 | bytes 4194304 | tf_op jit(solution)/shard_map/attend/pallas_call | solution.py:265
  44.7 1.4 %collective-permute-start.17 = (bf16[32,2048]{1,0:T(8,128)(2,1)S(1)}, bf16[32,2048]{1,0:T(8,128)(2,1)S(1)}, u32[]{:S(2)}, u32[]{:S(2)}) collective-permute-start(bf16[32,2048]{1,0:T(8,128)(2,1)S(1)} %attend.3.refs_0_), channel_id=1, source_target_pairs={{0,2},{1,5},{2,0},{3,7},{4,6},{5,1},{6,4},{7,3},{8,10},{9,13},{10,... | collective-permute-start | bytes 393224 | tf_op jit(solution)/shard_map/ppermute | solution.py:51
  46.1 3.0 %collective-permute-start.15 = (bf16[32,2048]{1,0:T(8,128)(2,1)S(1)}, bf16[32,2048]{1,0:T(8,128)(2,1)S(1)}, u32[]{:S(2)}, u32[]{:S(2)}) collective-permute-start(bf16[32,2048]{1,0:T(8,128)(2,1)S(1)} %attend.3.refs_0_), channel_id=1, source_target_pairs={{0,4},{1,3},{2,6},{3,1},{4,0},{5,7},{6,2},{7,5},{8,12},{9,11},{10,... | collective-permute-start | bytes 393224 | tf_op jit(solution)/shard_map/ppermute | solution.py:51
  49.1 4.8 %collective-permute-start.14 = (bf16[32,2048]{1,0:T(8,128)(2,1)S(1)}, bf16[32,2048]{1,0:T(8,128)(2,1)S(1)}, u32[]{:S(2)}, u32[]{:S(2)}) collective-permute-start(bf16[32,2048]{1,0:T(8,128)(2,1)S(1)} %attend.3.refs_0_), channel_id=1, source_target_pairs={{0,8},{1,9},{2,10},{3,11},{4,12},{5,13},{6,14},{7,15},{8,0},{9,1},... | collective-permute-start | bytes 393224 | tf_op jit(solution)/shard_map/ppermute | solution.py:51
  53.9 0.0 collective-permute-done.5
  53.9 2.8 %attend.2.refs_0_ = bf16[32,2048]{1,0:T(8,128)(2,1)S(1)} custom-call(s32[8]{0:T(128)S(1)} %copy-done.4, f32[32,2304]{1,0:T(8,128)S(1)} %slice_add_fusion.2.refs_0_, f32[32,128]{1,0:T(8,128)S(1)} %slice.48.refs_1_, f32[32,128]{1,0:T(8,128)S(1)} %get-tuple-element.38.refs_2_, f32[32,128]{1,0:T(8,128)S(1)} %get-tuple-element.39.refs_3_, ...), custom_call_target="tpu_custom_call" | custom-call | flops 268435456 | bytes 4194304 | tf_op jit(solution)/shard_map/attend/pallas_call | solution.py:265
  56.7 0.1 collective-permute-start.7
  56.8 3.4 %collective-permute-done.14.refs_1_ = bf16[32,2048]{1,0:T(8,128)(2,1)S(1)} collective-permute-done((bf16[32,2048]{1,0:T(8,128)(2,1)S(1)}, bf16[32,2048]{1,0:T(8,128)(2,1)S(1)}, u32[]{:S(2)}, u32[]{:S(2)}) %collective-permute-start.14) | collective-permute-done | bytes 131104 | tf_op jit(solution)/shard_map/ppermute | solution.py:51
  60.2 2.2 %collective-permute-start.16 = (bf16[32,2048]{1,0:T(8,128)(2,1)S(1)}, bf16[32,2048]{1,0:T(8,128)(2,1)S(1)}, u32[]{:S(2)}, u32[]{:S(2)}) collective-permute-start(bf16[32,2048]{1,0:T(8,128)(2,1)S(1)} %collective-permute-done.14.refs_1_), channel_id=1, source_target_pairs={{0,4},{1,3},{2,6},{3,1},{4,0},{5,7},{6,2},{7,5},{8,12},{9,11},{10,... | collective-permute-start | bytes 393224 | tf_op jit(solution)/shard_map/ppermute | solution.py:51
  62.4 0.0 collective-permute-done.15.refs_2_
  62.4 1.7 %collective-permute-start.19 = (bf16[32,2048]{1,0:T(8,128)(2,1)S(1)}, bf16[32,2048]{1,0:T(8,128)(2,1)S(1)}, u32[]{:S(2)}, u32[]{:S(2)}) collective-permute-start(bf16[32,2048]{1,0:T(8,128)(2,1)S(1)} %collective-permute-done.15.refs_2_), channel_id=1, source_target_pairs={{0,2},{1,5},{2,0},{3,7},{4,6},{5,1},{6,4},{7,3},{8,10},{9,13},{10,... | collective-permute-start | bytes 393224 | tf_op jit(solution)/shard_map/ppermute | solution.py:51
  64.1 0.4 collective-permute-start.18
  64.5 0.0 collective-permute-done.17.refs_4_
  64.5 0.9 collective-permute-start.8
  65.4 0.0 collective-permute-done.7.refs_1_
  65.4 1.1 %collective-permute-start.9 = (bf16[32,2048]{1,0:T(8,128)(2,1)S(1)}, bf16[32,2048]{1,0:T(8,128)(2,1)S(1)}, u32[]{:S(2)}, u32[]{:S(2)}) collective-permute-start(bf16[32,2048]{1,0:T(8,128)(2,1)S(1)} %collective-permute-done.7.refs_1_), channel_id=1, source_target_pairs={{0,4},{1,3},{2,6},{3,1},{4,0},{5,7},{6,2},{7,5},{8,12},{9,11},{10,... | collective-permute-start | bytes 393224 | tf_op jit(solution)/shard_map/ppermute | solution.py:51
  66.5 0.7 collective-permute-done.16.refs_3_
  67.2 2.5 %collective-permute-start.20 = (bf16[32,2048]{1,0:T(8,128)(2,1)S(1)}, bf16[32,2048]{1,0:T(8,128)(2,1)S(1)}, u32[]{:S(2)}, u32[]{:S(2)}) collective-permute-start(bf16[32,2048]{1,0:T(8,128)(2,1)S(1)} %collective-permute-done.16.refs_3_), channel_id=1, source_target_pairs={{0,2},{1,5},{2,0},{3,7},{4,6},{5,1},{6,4},{7,3},{8,10},{9,13},{10,... | collective-permute-start | bytes 393224 | tf_op jit(solution)/shard_map/ppermute | solution.py:51
  69.8 0.0 collective-permute-done.19.refs_6_
  69.8 0.0 collective-permute-start.10
  69.8 0.4 collective-permute-done.18.refs_5_
  70.2 1.7 %collective-permute-start.11 = (bf16[32,2048]{1,0:T(8,128)(2,1)S(1)}, bf16[32,2048]{1,0:T(8,128)(2,1)S(1)}, u32[]{:S(2)}, u32[]{:S(2)}) collective-permute-start(bf16[32,2048]{1,0:T(8,128)(2,1)S(1)} %collective-permute-done.7.refs_1_), channel_id=1, source_target_pairs={{0,2},{1,5},{2,0},{3,7},{4,6},{5,1},{6,4},{7,3},{8,10},{9,13},{10,... | collective-permute-start | bytes 393224 | tf_op jit(solution)/shard_map/ppermute | solution.py:51
  71.9 0.0 collective-permute-done.8.refs_2_
  71.9 0.7 collective-permute-start.12
  72.6 1.1 %collective-permute-done.9.refs_3_ = bf16[32,2048]{1,0:T(8,128)(2,1)S(1)} collective-permute-done((bf16[32,2048]{1,0:T(8,128)(2,1)S(1)}, bf16[32,2048]{1,0:T(8,128)(2,1)S(1)}, u32[]{:S(2)}, u32[]{:S(2)}) %collective-permute-start.9) | collective-permute-done | bytes 131104 | tf_op jit(solution)/shard_map/ppermute | solution.py:51
  73.7 1.7 %collective-permute-start.13 = (bf16[32,2048]{1,0:T(8,128)(2,1)S(1)}, bf16[32,2048]{1,0:T(8,128)(2,1)S(1)}, u32[]{:S(2)}, u32[]{:S(2)}) collective-permute-start(bf16[32,2048]{1,0:T(8,128)(2,1)S(1)} %collective-permute-done.9.refs_3_), channel_id=1, source_target_pairs={{0,2},{1,5},{2,0},{3,7},{4,6},{5,1},{6,4},{7,3},{8,10},{9,13},{10,... | collective-permute-start | bytes 393224 | tf_op jit(solution)/shard_map/ppermute | solution.py:51
  75.4 0.0 collective-permute-done.20.refs_7_
  75.4 5.8 %copy-done = bf16[4096,2048]{1,0:T(8,128)(2,1)S(1)} copy-done((bf16[4096,2048]{1,0:T(8,128)(2,1)S(1)}, bf16[4096,2048]{1,0:T(8,128)(2,1)}, u32[]{:S(2)}) %copy-start) | copy-done | bytes 16777240
  81.2 3.8 %combine.2.refs_8_ = f32[256,2048]{1,0:T(8,128)S(1)} custom-call(bf16[32,2048]{1,0:T(8,128)(2,1)S(1)} %attend.3.refs_0_, bf16[32,2048]{1,0:T(8,128)(2,1)S(1)} %collective-permute-done.14.refs_1_, bf16[32,2048]{1,0:T(8,128)(2,1)S(1)} %collective-permute-done.15.refs_2_, bf16[32,2048]{1,0:T(8,128)(2,1)S(1)} %collective-permute-done.16.refs_3_, ...), custom_call_target="tpu_custom_call" | custom-call | flops 2147483648 | bytes 11534336 | tf_op jit(solution)/shard_map/combine/pallas_call | solution.py:333
  85.0 0.0 collective-permute-done.10.refs_4_
  85.0 0.0 collective-permute-done.11.refs_5_
  85.0 0.0 collective-permute-done.13.refs_7_
  85.0 0.0 copy-start.1
  85.0 5.8 %copy-done.1 = bf16[4096,2048]{1,0:T(8,128)(2,1)S(1)} copy-done((bf16[4096,2048]{1,0:T(8,128)(2,1)S(1)}, bf16[4096,2048]{1,0:T(8,128)(2,1)}, u32[]{:S(2)}) %copy-start.1) | copy-done | bytes 16777240
  90.8 3.8 %combine.3 = (bf16[128,2048]{1,0:T(8,128)(2,1)S(1)}, f32[128,2048]{1,0:T(8,128)S(1)}) custom-call(bf16[32,2048]{1,0:T(8,128)(2,1)S(1)} %attend.2.refs_0_, bf16[32,2048]{1,0:T(8,128)(2,1)S(1)} %collective-permute-done.7.refs_1_, bf16[32,2048]{1,0:T(8,128)(2,1)S(1)} %collective-permute-done.8.refs_2_, bf16[32,2048]{1,0:T(8,128)(2,1)S(1)} %collective-permute-done.9.refs_3_, ...), custom_call_target="tpu_custom_call" | custom-call | flops 2147483648 | bytes 11534336 | tf_op jit(solution)/shard_map/combine/pallas_call | solution.py:333
  94.6 0.1 collective-permute-start.21
  94.7 1.9 %collective-permute-done.21 = bf16[128,2048]{1,0:T(8,128)(2,1)S(1)} collective-permute-done((bf16[128,2048]{1,0:T(8,128)(2,1)S(1)}, bf16[128,2048]{1,0:T(8,128)(2,1)S(1)}, u32[]{:S(2)}, u32[]{:S(2)}) %collective-permute-start.21) | collective-permute-done | bytes 524320 | tf_op jit(solution)/shard_map/ppermute | solution.py:442
  96.6 0.9 add_convert_fusion
  (15 shorter events, 0.2 us)
Async XLA Ops:
  4.4 7.7 %collective-permute-start = (bf16[128,1152]{1,0:T(8,128)(2,1)S(1)}, bf16[128,1152]{1,0:T(8,128)(2,1)S(1)}, u32[]{:S(2)}, u32[]{:S(2)}) collective-permute-start(bf16[128,1152]{1,0:T(8,128)(2,1)S(1)} %get-tuple-element.21), channel_id=1, source_target_pairs={{0,2},{1,5},{2,0},{3,7},{4,6},{5,1},{6,4},{7,3},{8,10},{9,13},{10,... | collective-permute-start | bytes 884744 | tf_op jit(solution)/shard_map/ppermute | solution.py:51
  11.3 7.1 %collective-permute-start.1 = (bf16[128,1280]{1,0:T(8,128)(2,1)S(1)}, bf16[128,1280]{1,0:T(8,128)(2,1)S(1)}, u32[]{:S(2)}, u32[]{:S(2)}) collective-permute-start(bf16[128,1280]{1,0:T(8,128)(2,1)S(1)} %get-tuple-element.23), channel_id=1, source_target_pairs={{0,2},{1,5},{2,0},{3,7},{4,6},{5,1},{6,4},{7,3},{8,10},{9,13},{10,... | collective-permute-start | bytes 983048 | tf_op jit(solution)/shard_map/ppermute | solution.py:51
  18.5 1.7 %copy-start.4 = (s32[8]{0:T(128)S(1)}, s32[8]{0:T(128)}, u32[]{:S(2)}) copy-start(s32[8]{0:T(128)} %length_ref.3) | copy-start | bytes 100
  18.5 10.4 %collective-permute-start.3 = (bf16[64,2432]{1,0:T(8,128)(2,1)S(1)}, bf16[64,2432]{1,0:T(8,128)(2,1)}, u32[]{:S(2)}, u32[]{:S(2)}) collective-permute-start(bf16[64,2432]{1,0:T(8,128)(2,1)S(1)} %fusion.1), channel_id=1, source_target_pairs={{0,4},{1,3},{2,6},{3,1},{4,0},{5,7},{6,2},{7,5},{8,12},{9,11},{10,... | collective-permute-start | bytes 933896 | tf_op jit(solution)/shard_map/ppermute | solution.py:51
  20.3 9.9 %collective-permute-start.2 = (bf16[128,2304]{1,0:T(8,128)(2,1)S(1)}, bf16[128,2304]{1,0:T(8,128)(2,1)S(1)}, u32[]{:S(2)}, u32[]{:S(2)}) collective-permute-start(bf16[128,2304]{1,0:T(8,128)(2,1)S(1)} %get-tuple-element.31), channel_id=1, source_target_pairs={{0,2},{1,5},{2,0},{3,7},{4,6},{5,1},{6,4},{7,3},{8,10},{9,13},{10,... | collective-permute-start | bytes 1769480 | tf_op jit(solution)/shard_map/ppermute | solution.py:51
  28.9 12.8 %copy-start.3 = (bf16[8,1024,256]{2,1,0:T(8,128)(2,1)S(1)}, bf16[8,1024,256]{2,1,0:T(8,128)(2,1)}, u32[]{:S(2)}) copy-start(bf16[8,1024,256]{2,1,0:T(8,128)(2,1)} %refs_5_.3) | copy-start | bytes 12582916
  30.3 11.4 %copy-start.2 = (bf16[8,1024,256]{2,1,0:T(8,128)(2,1)S(1)}, bf16[8,1024,256]{2,1,0:T(8,128)(2,1)}, u32[]{:S(2)}) copy-start(bf16[8,1024,256]{2,1,0:T(8,128)(2,1)} %refs_4_.5) | copy-start | bytes 12582916
  30.4 10.1 %collective-permute-start.4 = (bf16[64,2304]{1,0:T(8,128)(2,1)S(1)}, bf16[64,2304]{1,0:T(8,128)(2,1)S(1)}, u32[]{:S(2)}, u32[]{:S(2)}) collective-permute-start(bf16[64,2304]{1,0:T(8,128)(2,1)S(1)} %slice.63), channel_id=1, source_target_pairs={{0,4},{1,3},{2,6},{3,1},{4,0},{5,7},{6,2},{7,5},{8,12},{9,11},{10,... | collective-permute-start | bytes 884744 | tf_op jit(solution)/shard_map/ppermute | solution.py:51
  32.2 9.5 %collective-permute-start.6 = (bf16[32,2432]{1,0:T(8,128)(2,1)S(1)}, bf16[32,2432]{1,0:T(8,128)(2,1)S(1)}, u32[]{:S(2)}, u32[]{:S(2)}) collective-permute-start(bf16[32,2432]{1,0:T(8,128)(2,1)S(1)} %slice.64), channel_id=1, source_target_pairs={{0,8},{1,9},{2,10},{3,11},{4,12},{5,13},{6,14},{7,15},{8,0},{9,1},... | collective-permute-start | bytes 466952 | tf_op jit(solution)/shard_map/ppermute | solution.py:51
  40.7 13.2 %collective-permute-start.5 = (bf16[32,2304]{1,0:T(8,128)(2,1)S(1)}, bf16[32,2304]{1,0:T(8,128)(2,1)S(1)}, u32[]{:S(2)}, u32[]{:S(2)}) collective-permute-start(bf16[32,2304]{1,0:T(8,128)(2,1)S(1)} %slice.65), channel_id=1, source_target_pairs={{0,8},{1,9},{2,10},{3,11},{4,12},{5,13},{6,14},{7,15},{8,0},{9,1},... | collective-permute-start | bytes 442376 | tf_op jit(solution)/shard_map/ppermute | solution.py:51
  44.7 19.8 %collective-permute-start.17 = (bf16[32,2048]{1,0:T(8,128)(2,1)S(1)}, bf16[32,2048]{1,0:T(8,128)(2,1)S(1)}, u32[]{:S(2)}, u32[]{:S(2)}) collective-permute-start(bf16[32,2048]{1,0:T(8,128)(2,1)S(1)} %attend.3.refs_0_), channel_id=1, source_target_pairs={{0,2},{1,5},{2,0},{3,7},{4,6},{5,1},{6,4},{7,3},{8,10},{9,13},{10,... | collective-permute-start | bytes 393224 | tf_op jit(solution)/shard_map/ppermute | solution.py:51
  46.1 16.3 %collective-permute-start.15 = (bf16[32,2048]{1,0:T(8,128)(2,1)S(1)}, bf16[32,2048]{1,0:T(8,128)(2,1)S(1)}, u32[]{:S(2)}, u32[]{:S(2)}) collective-permute-start(bf16[32,2048]{1,0:T(8,128)(2,1)S(1)} %attend.3.refs_0_), channel_id=1, source_target_pairs={{0,4},{1,3},{2,6},{3,1},{4,0},{5,7},{6,2},{7,5},{8,12},{9,11},{10,... | collective-permute-start | bytes 393224 | tf_op jit(solution)/shard_map/ppermute | solution.py:51
  49.1 11.1 %collective-permute-start.14 = (bf16[32,2048]{1,0:T(8,128)(2,1)S(1)}, bf16[32,2048]{1,0:T(8,128)(2,1)S(1)}, u32[]{:S(2)}, u32[]{:S(2)}) collective-permute-start(bf16[32,2048]{1,0:T(8,128)(2,1)S(1)} %attend.3.refs_0_), channel_id=1, source_target_pairs={{0,8},{1,9},{2,10},{3,11},{4,12},{5,13},{6,14},{7,15},{8,0},{9,1},... | collective-permute-start | bytes 393224 | tf_op jit(solution)/shard_map/ppermute | solution.py:51
  56.7 8.7 %collective-permute-start.7 = (bf16[32,2048]{1,0:T(8,128)(2,1)S(1)}, bf16[32,2048]{1,0:T(8,128)(2,1)S(1)}, u32[]{:S(2)}, u32[]{:S(2)}) collective-permute-start(bf16[32,2048]{1,0:T(8,128)(2,1)S(1)} %attend.2.refs_0_), channel_id=1, source_target_pairs={{0,8},{1,9},{2,10},{3,11},{4,12},{5,13},{6,14},{7,15},{8,0},{9,1},... | collective-permute-start | bytes 393224 | tf_op jit(solution)/shard_map/ppermute | solution.py:51
  60.2 7.0 %collective-permute-start.16 = (bf16[32,2048]{1,0:T(8,128)(2,1)S(1)}, bf16[32,2048]{1,0:T(8,128)(2,1)S(1)}, u32[]{:S(2)}, u32[]{:S(2)}) collective-permute-start(bf16[32,2048]{1,0:T(8,128)(2,1)S(1)} %collective-permute-done.14.refs_1_), channel_id=1, source_target_pairs={{0,4},{1,3},{2,6},{3,1},{4,0},{5,7},{6,2},{7,5},{8,12},{9,11},{10,... | collective-permute-start | bytes 393224 | tf_op jit(solution)/shard_map/ppermute | solution.py:51
  62.4 7.3 %collective-permute-start.19 = (bf16[32,2048]{1,0:T(8,128)(2,1)S(1)}, bf16[32,2048]{1,0:T(8,128)(2,1)S(1)}, u32[]{:S(2)}, u32[]{:S(2)}) collective-permute-start(bf16[32,2048]{1,0:T(8,128)(2,1)S(1)} %collective-permute-done.15.refs_2_), channel_id=1, source_target_pairs={{0,2},{1,5},{2,0},{3,7},{4,6},{5,1},{6,4},{7,3},{8,10},{9,13},{10,... | collective-permute-start | bytes 393224 | tf_op jit(solution)/shard_map/ppermute | solution.py:51
  64.1 6.1 %collective-permute-start.18 = (bf16[32,2048]{1,0:T(8,128)(2,1)S(1)}, bf16[32,2048]{1,0:T(8,128)(2,1)S(1)}, u32[]{:S(2)}, u32[]{:S(2)}) collective-permute-start(bf16[32,2048]{1,0:T(8,128)(2,1)S(1)} %collective-permute-done.14.refs_1_), channel_id=1, source_target_pairs={{0,2},{1,5},{2,0},{3,7},{4,6},{5,1},{6,4},{7,3},{8,10},{9,13},{10,... | collective-permute-start | bytes 393224 | tf_op jit(solution)/shard_map/ppermute | solution.py:51
  64.5 7.4 %collective-permute-start.8 = (bf16[32,2048]{1,0:T(8,128)(2,1)S(1)}, bf16[32,2048]{1,0:T(8,128)(2,1)S(1)}, u32[]{:S(2)}, u32[]{:S(2)}) collective-permute-start(bf16[32,2048]{1,0:T(8,128)(2,1)S(1)} %attend.2.refs_0_), channel_id=1, source_target_pairs={{0,4},{1,3},{2,6},{3,1},{4,0},{5,7},{6,2},{7,5},{8,12},{9,11},{10,... | collective-permute-start | bytes 393224 | tf_op jit(solution)/shard_map/ppermute | solution.py:51
  65.4 8.3 %collective-permute-start.9 = (bf16[32,2048]{1,0:T(8,128)(2,1)S(1)}, bf16[32,2048]{1,0:T(8,128)(2,1)S(1)}, u32[]{:S(2)}, u32[]{:S(2)}) collective-permute-start(bf16[32,2048]{1,0:T(8,128)(2,1)S(1)} %collective-permute-done.7.refs_1_), channel_id=1, source_target_pairs={{0,4},{1,3},{2,6},{3,1},{4,0},{5,7},{6,2},{7,5},{8,12},{9,11},{10,... | collective-permute-start | bytes 393224 | tf_op jit(solution)/shard_map/ppermute | solution.py:51
  67.2 8.2 %collective-permute-start.20 = (bf16[32,2048]{1,0:T(8,128)(2,1)S(1)}, bf16[32,2048]{1,0:T(8,128)(2,1)S(1)}, u32[]{:S(2)}, u32[]{:S(2)}) collective-permute-start(bf16[32,2048]{1,0:T(8,128)(2,1)S(1)} %collective-permute-done.16.refs_3_), channel_id=1, source_target_pairs={{0,2},{1,5},{2,0},{3,7},{4,6},{5,1},{6,4},{7,3},{8,10},{9,13},{10,... | collective-permute-start | bytes 393224 | tf_op jit(solution)/shard_map/ppermute | solution.py:51
  69.8 15.2 %collective-permute-start.10 = (bf16[32,2048]{1,0:T(8,128)(2,1)S(1)}, bf16[32,2048]{1,0:T(8,128)(2,1)S(1)}, u32[]{:S(2)}, u32[]{:S(2)}) collective-permute-start(bf16[32,2048]{1,0:T(8,128)(2,1)S(1)} %attend.2.refs_0_), channel_id=1, source_target_pairs={{0,2},{1,5},{2,0},{3,7},{4,6},{5,1},{6,4},{7,3},{8,10},{9,13},{10,... | collective-permute-start | bytes 393224 | tf_op jit(solution)/shard_map/ppermute | solution.py:51
  70.2 14.8 %collective-permute-start.11 = (bf16[32,2048]{1,0:T(8,128)(2,1)S(1)}, bf16[32,2048]{1,0:T(8,128)(2,1)S(1)}, u32[]{:S(2)}, u32[]{:S(2)}) collective-permute-start(bf16[32,2048]{1,0:T(8,128)(2,1)S(1)} %collective-permute-done.7.refs_1_), channel_id=1, source_target_pairs={{0,2},{1,5},{2,0},{3,7},{4,6},{5,1},{6,4},{7,3},{8,10},{9,13},{10,... | collective-permute-start | bytes 393224 | tf_op jit(solution)/shard_map/ppermute | solution.py:51
  71.9 13.1 %collective-permute-start.12 = (bf16[32,2048]{1,0:T(8,128)(2,1)S(1)}, bf16[32,2048]{1,0:T(8,128)(2,1)S(1)}, u32[]{:S(2)}, u32[]{:S(2)}) collective-permute-start(bf16[32,2048]{1,0:T(8,128)(2,1)S(1)} %collective-permute-done.8.refs_2_), channel_id=1, source_target_pairs={{0,2},{1,5},{2,0},{3,7},{4,6},{5,1},{6,4},{7,3},{8,10},{9,13},{10,... | collective-permute-start | bytes 393224 | tf_op jit(solution)/shard_map/ppermute | solution.py:51
  73.7 11.3 %collective-permute-start.13 = (bf16[32,2048]{1,0:T(8,128)(2,1)S(1)}, bf16[32,2048]{1,0:T(8,128)(2,1)S(1)}, u32[]{:S(2)}, u32[]{:S(2)}) collective-permute-start(bf16[32,2048]{1,0:T(8,128)(2,1)S(1)} %collective-permute-done.9.refs_3_), channel_id=1, source_target_pairs={{0,2},{1,5},{2,0},{3,7},{4,6},{5,1},{6,4},{7,3},{8,10},{9,13},{10,... | collective-permute-start | bytes 393224 | tf_op jit(solution)/shard_map/ppermute | solution.py:51
  75.4 5.8 %copy-start = (bf16[4096,2048]{1,0:T(8,128)(2,1)S(1)}, bf16[4096,2048]{1,0:T(8,128)(2,1)}, u32[]{:S(2)}) copy-start(bf16[4096,2048]{1,0:T(8,128)(2,1)} %refs_9_.1) | copy-start | bytes 50331652
  85.0 5.8 %copy-start.1 = (bf16[4096,2048]{1,0:T(8,128)(2,1)S(1)}, bf16[4096,2048]{1,0:T(8,128)(2,1)}, u32[]{:S(2)}) copy-start(bf16[4096,2048]{1,0:T(8,128)(2,1)} %refs_9_.1) | copy-start | bytes 50331652
  94.6 2.0 %collective-permute-start.21 = (bf16[128,2048]{1,0:T(8,128)(2,1)S(1)}, bf16[128,2048]{1,0:T(8,128)(2,1)S(1)}, u32[]{:S(2)}, u32[]{:S(2)}) collective-permute-start(bf16[128,2048]{1,0:T(8,128)(2,1)S(1)} %get-tuple-element.34), channel_id=1, source_target_pairs={{0,1},{1,0},{2,3},{3,2},{4,5},{5,4},{6,7},{7,6},{8,9},{9,8},{10,11... | collective-permute-start | bytes 1572872 | tf_op jit(solution)/shard_map/ppermute | solution.py:442

commit v4 on v3

--- a/solution.py
+++ b/solution.py
@@ -28,6 +28,11 @@
     return first, second
 
 
+def gather_orders(n, chunk):
+    first, second = bit_orders(n)
+    return (first, first) if chunk else (first, second)
+
+
 def slot_shift(slot, order):
     levels = len(order)
     shift = 0
@@ -36,13 +41,12 @@
     return shift
 
 
-def slot_owner(n, slot, gx, gy):
-    first, second = (slot_shift(slot, order) for order in bit_orders(n))
+def slot_owner(n, slot, gx, gy, orders):
+    first, second = (slot_shift(slot, order) for order in orders)
     return gx ^ jnp.where(gy == 0, first, second)
 
 
-def exchange(value, n, cores, stage):
-    orders = bit_orders(n)
+def exchange(value, n, cores, stage, orders):
     pairs = []
     for gx in range(n):
         for gy in range(cores):
@@ -81,7 +85,7 @@
         me, gy = lax.axis_index("gx"), lax.axis_index("gy")
         t_copies = []
         for slot in range(n):
-            start = pl.multiple_of(slot_owner(n, slot, me, gy) * block, block)
+            start = pl.multiple_of(slot_owner(n, slot, me, gy, bit_orders(n)) * block, block)
             t_copies.append(
                 pltpu.make_async_copy(
                     tokens_ref.at[pl.ds(start, block), :], t_buf.at[slot], t_sems.at[slot]
@@ -124,10 +128,6 @@
         send_ref[:, start:end] = product[half:].astype(jnp.bfloat16)
 
 
-def in_vmem(value):
-    return pltpu.with_memory_space_constraint(value, pltpu.VMEM)
-
-
 def in_hbm(value):
     return pltpu.with_memory_space_constraint(value, pltpu.HBM)
 
@@ -163,11 +163,6 @@
         out_specs=[vmem] * len(out_shape),
         scratch_shapes=scratch,
         compiler_params=pltpu.CompilerParams(vmem_limit_bytes=16 * MIB),
-        cost_estimate=pl.CostEstimate(
-            flops=2 * rows * depth * width,
-            bytes_accessed=2 * depth * width + 4 * rows * depth,
-            transcendentals=0,
-        ),
         name="project",
     )(*args, in_hbm(w_query), in_hbm(w_key), in_hbm(w_value))
 
@@ -261,7 +256,6 @@
     rows = seq_count * NEW
     vmem = pl.BlockSpec(memory_space=pltpu.VMEM)
     hbm = pl.BlockSpec(memory_space=pltpu.HBM)
-    flops = 4 * seq_count * groups * heads * NEW * slots * HD
     return pl.pallas_call(
         functools.partial(attend_kernel, chunk, offsets, kv_offset, groups, heads, seqs),
         out_shape=pltpu.VMEM((rows, cols), jnp.bfloat16),
@@ -272,13 +266,66 @@
             pltpu.VMEM((seqs * NEW, cols), jnp.float32),
         ],
         compiler_params=pltpu.CompilerParams(vmem_limit_bytes=16 * MIB),
-        cost_estimate=pl.CostEstimate(
-            flops=flops,
-            bytes_accessed=4 * seq_count * slots * kv,
-            transcendentals=seq_count * groups * heads * NEW * slots,
-        ),
         name="attend",
-    )(lengths, sums, squares, cosine, sine, in_vmem(cache_keys), in_vmem(cache_values))
+    )(lengths, sums, squares, cosine, sine, cache_keys, cache_values)
+
+
+def fetch_kernel(count, pieces, *refs):
+    sources, targets, sems = refs[:count], refs[count : 2 * count], refs[2 * count]
+    copies = []
+    for i, (source, target) in enumerate(zip(sources, targets)):
+        size = target.shape[0] // pieces
+        for p in range(pieces):
+            at = slice(p * size, (p + 1) * size)
+            copies.append(
+                pltpu.make_async_copy(source.at[at], target.at[at], sems.at[i * pieces + p])
+            )
+    for copy in copies:
+        copy.start()
+    for copy in copies:
+        copy.wait()
+
+
+def fetch(*arrays):
+    pieces = 4
+    return pl.pallas_call(
+        functools.partial(fetch_kernel, len(arrays), pieces),
+        out_shape=[pltpu.VMEM(array.shape, array.dtype) for array in arrays],
+        in_specs=[pl.BlockSpec(memory_space=pltpu.HBM)] * len(arrays),
+        out_specs=[pl.BlockSpec(memory_space=pltpu.VMEM)] * len(arrays),
+        scratch_shapes=[pltpu.SemaphoreType.DMA((pieces * len(arrays),))],
+        compiler_params=pltpu.CompilerParams(vmem_limit_bytes=4 * MIB),
+        name="fetch",
+    )(*[in_hbm(array) for array in arrays])
+
+
+def fetch_rows_kernel(start, pieces, source, target, sems):
+    size = target.shape[0] // pieces
+    copies = [
+        pltpu.make_async_copy(
+            source.at[start + p * size : start + (p + 1) * size],
+            target.at[p * size : (p + 1) * size],
+            sems.at[p],
+        )
+        for p in range(pieces)
+    ]
+    for copy in copies:
+        copy.start()
+    for copy in copies:
+        copy.wait()
+
+
+def fetch_rows(array, start, rows):
+    pieces = 4
+    return pl.pallas_call(
+        functools.partial(fetch_rows_kernel, start, pieces),
+        out_shape=pltpu.VMEM((rows, array.shape[1]), array.dtype),
+        in_specs=[pl.BlockSpec(memory_space=pltpu.HBM)],
+        out_specs=pl.BlockSpec(memory_space=pltpu.VMEM),
+        scratch_shapes=[pltpu.SemaphoreType.DMA((pieces,))],
+        compiler_params=pltpu.CompilerParams(vmem_limit_bytes=4 * MIB),
+        name="fetch_rows",
+    )(in_hbm(array))
 
 
 def combine_kernel(n, block, chunk, *refs):
@@ -292,7 +339,7 @@
     half = x_buf.shape[0] // 2
     x_copies = []
     for slot, piece in enumerate(pieces):
-        start = pl.multiple_of((slot_owner(n, slot, gx, gy) ^ moved) * block, block)
+        start = pl.multiple_of((slot_owner(n, slot, gx, gy, gather_orders(n, chunk)) ^ moved) * block, block)
         x_copies.append(
             pltpu.make_async_copy(piece, x_buf.at[pl.ds(start, block), :], x_sems.at[slot])
         )
@@ -301,11 +348,10 @@
     for copy in x_copies:
         copy.wait()
 
-    rows = slice(chunk * depth, (chunk + 1) * depth)
     tile = cols // TILES
     for start in range(0, cols, tile):
         at = slice(start, start + tile)
-        product = jnp.dot(x_buf[...], w_ref[rows, at], preferred_element_type=jnp.float32)
+        product = jnp.dot(x_buf[...], w_ref[:, at], preferred_element_type=jnp.float32)
         if chunk:
             product = product + before_ref[:, at]
         if len(outs) == 1:
@@ -342,13 +388,8 @@
             pltpu.SemaphoreType.DMA((n,)),
         ],
         compiler_params=pltpu.CompilerParams(vmem_limit_bytes=16 * MIB),
-        cost_estimate=pl.CostEstimate(
-            flops=2 * rows * depth * cols,
-            bytes_accessed=2 * depth * cols + 2 * rows * depth + 4 * rows * cols,
-            transcendentals=0,
-        ),
         name="combine",
-    )(*pieces, *earlier, in_vmem(w_out))
+    )(*pieces, *earlier, w_out)
 
 
 def shards(
@@ -377,12 +418,13 @@
         return lax.optimization_barrier((value, earlier))[0]
 
     share = q_cols // 2
+    orders = bit_orders(n)
     send_a, keep_a, x = column_part(0, share, None)
     x = after(x, send_a)
-    other_a = exchange(send_a, n, cores, 0)
+    other_a = exchange(send_a, n, cores, 0, orders)
     send_b, keep_b = column_part(share, share, 0)
     x = after(x, send_b)
-    other_b = exchange(send_b, n, cores, 0)
+    other_b = exchange(send_b, n, cores, 0, orders)
     sum_a = keep_a + other_a.astype(jnp.float32)
     x = after(x, sum_a)
     later = []
@@ -396,9 +438,11 @@
     for send_c, keep_c in later:
         flows.append([0, keep_c, after(send_c, flows[-1][2])])
 
-    def step(flow, *earlier):
-        stage, keep, send = flow
-        other = exchange(send, n, cores, stage)
+    def start(flow):
+        return exchange(flow[2], n, cores, flow[0], orders)
+
+    def finish(flow, other, *earlier):
+        stage, keep, _ = flow
         if earlier:
             other = after(other, *earlier)
         value = keep + other.astype(jnp.float32)
@@ -406,10 +450,25 @@
         flow[:] = stage + 1, value[:low] if low else value, value[low:].astype(jnp.bfloat16)
 
     lead, follow = flows
+    w_rows = w_out.shape[0] // CHUNKS
+    source = after(w_out, lead[2], follow[2])
+    weights = [fetch_rows(source, chunk * w_rows, w_rows) for chunk in range(CHUNKS)]
+    stage = 0
     while follow[0] < levels:
-        if lead[0] < levels:
-            step(lead)
-        step(follow, *([lead[2]] if lead[0] < levels else []))
+        pending = [start(flow) for flow in flows if flow[0] < levels]
+        if lead[0] == levels:
+            finish(follow, pending[0])
+        elif lead[0] == levels - 1:
+            finish(lead, pending[0])
+            finish(follow, pending[1], lead[1])
+        else:
+            finish(lead, pending[0], *weights)
+            between = [lead[2]]
+            if stage == 0:
+                cache_keys, cache_values = fetch(*after((cache_keys, cache_values), lead[2]))
+                between += [cache_keys, cache_values]
+            finish(follow, pending[1], *between)
+        stage += 1
     sums = [flow[1] for flow in flows]
     squares = sums[0][:, share : share + 128]
     plain = [h * HD for h in range(q_cols // HD)]
@@ -433,11 +492,17 @@
         slots = [attention]
         for slot in range(1, n):
             top = slot.bit_length() - 1
-            slots.append(exchange(slots[slot - (1 << top)], n, cores, levels - 1 - top))
+            slots.append(exchange(
+                    slots[slot - (1 << top)],
+                    n,
+                    cores,
+                    levels - 1 - top,
+                    gather_orders(n, chunk),
+                ))
         gathered.append(slots)
     result = None
     for chunk in range(CHUNKS):
-        result = combine(chunk, gathered[chunk], result and result[0], w_out)
+        result = combine(chunk, gathered[chunk], result and result[0], weights[chunk])
     send, keep = result
     other = lax.ppermute(send, "gy", [(0, 1), (1, 0)])
     return (keep + other.astype(jnp.float32)).astype(jnp.bfloat16)

time: 97.6 us -> 84.8 us (0.87)
  local copies, waits for them, and re-layouts: 11.7 us -> 0.16 us
  Pallas kernels: 27.1 us -> 37.4 us
  starting transfers between devices: 33.4 us -> 26.2 us
  waiting for transfers between devices: 22.2 us -> 18.1 us
    unnamed x10 -> x2, local copies, waits for them, and re-layouts: 11.5 us -> 0.01 us
    pallas_call x0 -> x3, Pallas kernels: none -> 10.5 us  [the longest x2 7.01 us: fetch_rows(): pl.pallas_call(functools.partial(fetch_rows_kernel, start, pieces), out_s...]
    ppermute x21, starting transfers between devices: 33.3 us -> 26.1 us  [exchange(): return lax.ppermute(value, ('gx', 'gy'), pairs)]
    ppermute x21, waiting for transfers between devices: 20.3 us -> 16.2 us  [exchange(): return lax.ppermute(value, ('gx', 'gy'), pairs)]
  transfers between devices with their start and end apart: 22 -> 22, of which waited for: 10 -> 13; matrix products, arithmetic and copies ran while one was open for 2% -> 2% of each run, Pallas kernels for 19% -> 35%
where the time goes in v4:
time: 84.8 us; the launch traced here: 84.7 us
  Pallas kernels  37.4 us (44%)
  starting transfers between devices  26.2 us (31%)
  waiting for transfers between devices  18.1 us (21%)
  other arithmetic  2.58 us (3%)
    ppermute x21, starting transfers between devices, exchange(): return lax.ppermute(value, ('gx', 'gy'), pairs)  26.1 us
    ppermute x21, waiting for transfers between devices, exchange(): return lax.ppermute(value, ('gx', 'gy'), pairs)  16.2 us
    pallas_call x3, Pallas kernels, project(): pl.pallas_call(functools.partial(project_kernel, n, q_start, kv_start, fi...  13.8 us
    pallas_call x2, Pallas kernels, combine(): pl.pallas_call(functools.partial(combine_kernel, n, block, chunk), out_sh...  7.55 us
    pallas_call x2, Pallas kernels, fetch_rows(): pl.pallas_call(functools.partial(fetch_rows_kernel, start, pieces), out_s...  7.01 us
    pallas_call x2, Pallas kernels, attend(): pl.pallas_call(functools.partial(attend_kernel, chunk, offsets, kv_offset...  5.64 us
    pallas_call x1, Pallas kernels, fetch(): pl.pallas_call(functools.partial(fetch_kernel, len(arrays), pieces), out_...  3.47 us
    ppermute x1, waiting for transfers between devices, shards(): other = lax.ppermute(send, 'gy', [(0, 1), (1, 0)])  1.9 us
  transfers between devices with their start and end apart: 22, of which 13 were waited for; matrix products, arithmetic and copies ran while one was open for 2% of the time, Pallas kernels for 35%

profile of v4, /device:TPU:0, one launch (start us, length us, event | category | flops | bytes accessed | tf_op | source)
XLA Modules:
  0.0 84.7 jit_solution(12922003949787859301)
XLA Ops:
  0.0 4.4 %project.3 = (bf16[128,1152]{1,0:T(8,128)(2,1)S(1)}, f32[128,1152]{1,0:T(8,128)S(1)}, bf16[256,2048]{1,0:T(8,128)(2,1)S(1)}) custom-call(bf16[256,2048]{1,0:T(8,128)(2,1)} %refs_0_.1, f32[1,2048]{1,0:T(1,128)} %bitcast.1, bf16[2048,4096]{1,0:T(8,128)(2,1)} %refs_1_.3, bf16[2048,256]{1,0:T(8,128)(2,1)} %refs_2_.5, bf16[2048,256]{1,0:T(8,128)(2,1)} %refs_3_.5), custom_call_target="tpu_custom_call" | custom-call | tf_op jit(solution)/shard_map/project/pallas_call | solution.py:159
  4.4 3.0 %collective-permute-start = (bf16[128,1152]{1,0:T(8,128)(2,1)S(1)}, bf16[128,1152]{1,0:T(8,128)(2,1)S(1)}, u32[]{:S(2)}, u32[]{:S(2)}) collective-permute-start(bf16[128,1152]{1,0:T(8,128)(2,1)S(1)} %get-tuple-element.28), channel_id=1, source_target_pairs={{0,2},{1,5},{2,0},{3,7},{4,6},{5,1},{6,4},{7,3},{8,10},{9,13},{10,... | collective-permute-start | bytes 884744 | tf_op jit(solution)/shard_map/ppermute | solution.py:55
  7.4 3.9 %project.4 = (bf16[128,1280]{1,0:T(8,128)(2,1)S(1)}, f32[128,1280]{1,0:T(8,128)S(1)}) custom-call(bf16[256,2048]{1,0:T(8,128)(2,1)S(1)} %get-tuple-element.33.refs_0_, bf16[2048,4096]{1,0:T(8,128)(2,1)} %refs_1_.3, bf16[2048,256]{1,0:T(8,128)(2,1)} %refs_2_.5, bf16[2048,256]{1,0:T(8,128)(2,1)} %refs_3_.5), custom_call_target="tpu_custom_call" | custom-call | tf_op jit(solution)/shard_map/project/pallas_call | solution.py:159
  11.3 0.1 collective-permute-start.1
  11.4 0.8 collective-permute-done
  12.1 0.1 convert_add_fusion.2
  12.2 0.0 copy-start
  12.2 5.5 %project.5 = (bf16[128,2304]{1,0:T(8,128)(2,1)S(1)}, f32[128,2304]{1,0:T(8,128)S(1)}) custom-call(bf16[256,2048]{1,0:T(8,128)(2,1)S(1)} %get-tuple-element.33.refs_0_, bf16[2048,4096]{1,0:T(8,128)(2,1)} %refs_1_.3, bf16[2048,256]{1,0:T(8,128)(2,1)} %refs_2_.5, bf16[2048,256]{1,0:T(8,128)(2,1)} %refs_3_.5), custom_call_target="tpu_custom_call" | custom-call | tf_op jit(solution)/shard_map/project/pallas_call | solution.py:159
  17.7 0.7 collective-permute-done.1
  18.4 0.1 convert_add_fusion.1
  18.5 1.6 %collective-permute-start.3 = (bf16[64,2432]{1,0:T(8,128)(2,1)S(1)}, bf16[64,2432]{1,0:T(8,128)(2,1)}, u32[]{:S(2)}, u32[]{:S(2)}) collective-permute-start(bf16[64,2432]{1,0:T(8,128)(2,1)S(1)} %fusion.1), channel_id=1, source_target_pairs={{0,4},{1,3},{2,6},{3,1},{4,0},{5,7},{6,2},{7,5},{8,12},{9,11},{10,... | collective-permute-start | bytes 933896 | tf_op jit(solution)/shard_map/ppermute | solution.py:55
  20.2 0.1 add_convert_fusion.1
  20.2 0.1 convert_element_type.49
  20.3 1.4 %collective-permute-start.2 = (bf16[128,2304]{1,0:T(8,128)(2,1)S(1)}, bf16[128,2304]{1,0:T(8,128)(2,1)S(1)}, u32[]{:S(2)}, u32[]{:S(2)}) collective-permute-start(bf16[128,2304]{1,0:T(8,128)(2,1)S(1)} %get-tuple-element.38), channel_id=1, source_target_pairs={{0,2},{1,5},{2,0},{3,7},{4,6},{5,1},{6,4},{7,3},{8,10},{9,13},{10,... | collective-permute-start | bytes 1769480 | tf_op jit(solution)/shard_map/ppermute | solution.py:55
  21.7 3.5 %fetch_rows.2.refs_8_ = bf16[2048,2048]{1,0:T(8,128)(2,1)S(1)} custom-call(bf16[4096,2048]{1,0:T(8,128)(2,1)} %source.1), custom_call_target="tpu_custom_call" | custom-call | tf_op jit(solution)/shard_map/fetch_rows/pallas_call | solution.py:320
  25.2 3.5 %fetch_rows.3.refs_9_ = bf16[2048,2048]{1,0:T(8,128)(2,1)S(1)} custom-call(bf16[4096,2048]{1,0:T(8,128)(2,1)} %source.1), custom_call_target="tpu_custom_call" | custom-call | tf_op jit(solution)/shard_map/fetch_rows/pallas_call | solution.py:320
  28.8 0.1 collective-permute-done.3
  28.9 1.0 %fusion.2 = f32[64,2432]{1,0:T(8,128)S(1)} fusion(f32[128,1280]{1,0:T(8,128)S(1)} %convert_add_fusion.1, f32[128,1152]{1,0:T(8,128)S(1)} %convert_add_fusion.2, bf16[64,2432]{1,0:T(8,128)(2,1)} %collective-permute-done.3), kind=kLoop, calls=%fused_computation.8 | loop fusion | flops 466944 | bytes 2179072 | tf_op jit(solution)/shard_map/add | solution.py:448
  29.9 2.7 %collective-permute-start.5 = (bf16[32,2432]{1,0:T(8,128)(2,1)S(1)}, bf16[32,2432]{1,0:T(8,128)(2,1)S(1)}, u32[]{:S(2)}, u32[]{:S(2)}) collective-permute-start(bf16[32,2432]{1,0:T(8,128)(2,1)S(1)} %slice.64), channel_id=1, source_target_pairs={{0,8},{1,9},{2,10},{3,11},{4,12},{5,13},{6,14},{7,15},{8,0},{9,1},... | collective-permute-start | bytes 466952 | tf_op jit(solution)/shard_map/ppermute | solution.py:55
  32.6 3.5 %fetch.1 = (bf16[8,1024,256]{2,1,0:T(8,128)(2,1)S(1)}, bf16[8,1024,256]{2,1,0:T(8,128)(2,1)S(1)}) custom-call(bf16[8,1024,256]{2,1,0:T(8,128)(2,1)} %refs_0_.2, bf16[8,1024,256]{2,1,0:T(8,128)(2,1)} %refs_1_.4), custom_call_target="tpu_custom_call" | custom-call | tf_op jit(solution)/shard_map/fetch/pallas_call | solution.py:291
  36.1 0.0 collective-permute-done.2
  36.1 0.1 convert_add_fusion
  36.2 1.6 %collective-permute-start.4 = (bf16[64,2304]{1,0:T(8,128)(2,1)S(1)}, bf16[64,2304]{1,0:T(8,128)(2,1)S(1)}, u32[]{:S(2)}, u32[]{:S(2)}) collective-permute-start(bf16[64,2304]{1,0:T(8,128)(2,1)S(1)} %slice.63), channel_id=1, source_target_pairs={{0,4},{1,3},{2,6},{3,1},{4,0},{5,7},{6,2},{7,5},{8,12},{9,11},{10,... | collective-permute-start | bytes 884744 | tf_op jit(solution)/shard_map/ppermute | solution.py:55
  37.9 0.6 collective-permute-done.5
  38.5 4.8 %collective-permute-done.4 = bf16[64,2304]{1,0:T(8,128)(2,1)S(1)} collective-permute-done((bf16[64,2304]{1,0:T(8,128)(2,1)S(1)}, bf16[64,2304]{1,0:T(8,128)(2,1)S(1)}, u32[]{:S(2)}, u32[]{:S(2)}) %collective-permute-start.4) | collective-permute-done | bytes 294944 | tf_op jit(solution)/shard_map/ppermute | solution.py:55
  43.4 0.1 slice_add_fusion
  43.4 0.1 collective-permute-start.6
  43.5 0.1 fusion.3
  43.7 0.1 pad_maximum_fusion.1
  43.7 2.9 %attend.3.refs_0_ = bf16[32,2048]{1,0:T(8,128)(2,1)S(1)} custom-call(s32[8]{0:T(128)S(1)} %copy-done, f32[32,2432]{1,0:T(8,128)S(1)} %slice_add_fusion.1.refs_0_, f32[32,128]{1,0:T(8,128)S(1)} %slice.48.refs_1_, f32[32,128]{1,0:T(8,128)S(1)} %get-tuple-element.52.refs_2_, f32[32,128]{1,0:T(8,128)S(1)} %get-tuple-element.53.refs_3_, ...), custom_call_target="tpu_custom_call" | custom-call | tf_op jit(solution)/shard_map/attend/pallas_call | solution.py:259
  46.7 3.0 %collective-permute-start.14 = (bf16[32,2048]{1,0:T(8,128)(2,1)S(1)}, bf16[32,2048]{1,0:T(8,128)(2,1)S(1)}, u32[]{:S(2)}, u32[]{:S(2)}) collective-permute-start(bf16[32,2048]{1,0:T(8,128)(2,1)S(1)} %attend.3.refs_0_), channel_id=1, source_target_pairs={{0,8},{1,9},{2,10},{3,11},{4,12},{5,13},{6,14},{7,15},{8,0},{9,1},... | collective-permute-start | bytes 393224 | tf_op jit(solution)/shard_map/ppermute | solution.py:55
  49.6 2.5 %collective-permute-start.15 = (bf16[32,2048]{1,0:T(8,128)(2,1)S(1)}, bf16[32,2048]{1,0:T(8,128)(2,1)S(1)}, u32[]{:S(2)}, u32[]{:S(2)}) collective-permute-start(bf16[32,2048]{1,0:T(8,128)(2,1)S(1)} %attend.3.refs_0_), channel_id=1, source_target_pairs={{0,4},{1,3},{2,6},{3,1},{4,0},{5,7},{6,2},{7,5},{8,12},{9,11},{10,... | collective-permute-start | bytes 393224 | tf_op jit(solution)/shard_map/ppermute | solution.py:55
  52.1 1.8 %collective-permute-start.17 = (bf16[32,2048]{1,0:T(8,128)(2,1)S(1)}, bf16[32,2048]{1,0:T(8,128)(2,1)S(1)}, u32[]{:S(2)}, u32[]{:S(2)}) collective-permute-start(bf16[32,2048]{1,0:T(8,128)(2,1)S(1)} %attend.3.refs_0_), channel_id=1, source_target_pairs={{0,2},{1,5},{2,0},{3,7},{4,6},{5,1},{6,4},{7,3},{8,10},{9,13},{10,... | collective-permute-start | bytes 393224 | tf_op jit(solution)/shard_map/ppermute | solution.py:55
  53.9 2.2 %collective-permute-done.6 = bf16[32,2304]{1,0:T(8,128)(2,1)S(1)} collective-permute-done((bf16[32,2304]{1,0:T(8,128)(2,1)S(1)}, bf16[32,2304]{1,0:T(8,128)(2,1)S(1)}, u32[]{:S(2)}, u32[]{:S(2)}) %collective-permute-start.6) | collective-permute-done | bytes 147488 | tf_op jit(solution)/shard_map/ppermute | solution.py:55
  56.1 2.7 %attend.2.refs_0_ = bf16[32,2048]{1,0:T(8,128)(2,1)S(1)} custom-call(s32[8]{0:T(128)S(1)} %copy-done, f32[32,2304]{1,0:T(8,128)S(1)} %slice_add_fusion.2.refs_0_, f32[32,128]{1,0:T(8,128)S(1)} %slice.48.refs_1_, f32[32,128]{1,0:T(8,128)S(1)} %get-tuple-element.52.refs_2_, f32[32,128]{1,0:T(8,128)S(1)} %get-tuple-element.53.refs_3_, ...), custom_call_target="tpu_custom_call" | custom-call | tf_op jit(solution)/shard_map/attend/pallas_call | solution.py:259
  58.8 0.1 collective-permute-start.7
  58.9 0.0 collective-permute-done.14.refs_1_
  58.9 0.1 collective-permute-start.16
  59.0 0.3 collective-permute-start.18
  59.3 0.0 collective-permute-done.15.refs_2_
  59.3 1.8 %collective-permute-start.19 = (bf16[32,2048]{1,0:T(8,128)(2,1)S(1)}, bf16[32,2048]{1,0:T(8,128)(2,1)S(1)}, u32[]{:S(2)}, u32[]{:S(2)}) collective-permute-start(bf16[32,2048]{1,0:T(8,128)(2,1)S(1)} %collective-permute-done.15.refs_2_), channel_id=1, source_target_pairs={{0,2},{1,5},{2,0},{3,7},{4,6},{5,1},{6,4},{7,3},{8,10},{9,13},{10,... | collective-permute-start | bytes 393224 | tf_op jit(solution)/shard_map/ppermute | solution.py:55
  61.1 0.0 collective-permute-done.17.refs_4_
  61.1 1.9 %collective-permute-start.8 = (bf16[32,2048]{1,0:T(8,128)(2,1)S(1)}, bf16[32,2048]{1,0:T(8,128)(2,1)S(1)}, u32[]{:S(2)}, u32[]{:S(2)}) collective-permute-start(bf16[32,2048]{1,0:T(8,128)(2,1)S(1)} %attend.2.refs_0_), channel_id=1, source_target_pairs={{0,4},{1,5},{2,6},{3,7},{4,0},{5,1},{6,2},{7,3},{8,12},{9,13},{10,... | collective-permute-start | bytes 393224 | tf_op jit(solution)/shard_map/ppermute | solution.py:55
  63.0 1.9 %collective-permute-done.7.refs_1_ = bf16[32,2048]{1,0:T(8,128)(2,1)S(1)} collective-permute-done((bf16[32,2048]{1,0:T(8,128)(2,1)S(1)}, bf16[32,2048]{1,0:T(8,128)(2,1)S(1)}, u32[]{:S(2)}, u32[]{:S(2)}) %collective-permute-start.7) | collective-permute-done | bytes 131104 | tf_op jit(solution)/shard_map/ppermute | solution.py:55
  65.0 0.0 collective-permute-start.9
  65.0 1.9 %collective-permute-done.16.refs_3_ = bf16[32,2048]{1,0:T(8,128)(2,1)S(1)} collective-permute-done((bf16[32,2048]{1,0:T(8,128)(2,1)S(1)}, bf16[32,2048]{1,0:T(8,128)(2,1)S(1)}, u32[]{:S(2)}, u32[]{:S(2)}) %collective-permute-start.16) | collective-permute-done | bytes 131104 | tf_op jit(solution)/shard_map/ppermute | solution.py:55
  66.8 0.0 collective-permute-start.20
  66.8 0.0 collective-permute-done.18.refs_5_
  66.8 2.0 %collective-permute-start.10 = (bf16[32,2048]{1,0:T(8,128)(2,1)S(1)}, bf16[32,2048]{1,0:T(8,128)(2,1)S(1)}, u32[]{:S(2)}, u32[]{:S(2)}) collective-permute-start(bf16[32,2048]{1,0:T(8,128)(2,1)S(1)} %attend.2.refs_0_), channel_id=1, source_target_pairs={{0,2},{1,3},{2,0},{3,1},{4,6},{5,7},{6,4},{7,5},{8,10},{9,11},{10,... | collective-permute-start | bytes 393224 | tf_op jit(solution)/shard_map/ppermute | solution.py:55
  68.9 0.0 collective-permute-done.19.refs_6_
  68.9 0.1 collective-permute-start.11
  68.9 0.1 collective-permute-done.8.refs_2_
  69.1 1.8 %collective-permute-start.12 = (bf16[32,2048]{1,0:T(8,128)(2,1)S(1)}, bf16[32,2048]{1,0:T(8,128)(2,1)S(1)}, u32[]{:S(2)}, u32[]{:S(2)}) collective-permute-start(bf16[32,2048]{1,0:T(8,128)(2,1)S(1)} %collective-permute-done.8.refs_2_), channel_id=1, source_target_pairs={{0,2},{1,3},{2,0},{3,1},{4,6},{5,7},{6,4},{7,5},{8,10},{9,11},{10,... | collective-permute-start | bytes 393224 | tf_op jit(solution)/shard_map/ppermute | solution.py:55
  70.9 0.2 collective-permute-start.13
  71.1 1.4 %collective-permute-done.20.refs_7_ = bf16[32,2048]{1,0:T(8,128)(2,1)S(1)} collective-permute-done((bf16[32,2048]{1,0:T(8,128)(2,1)S(1)}, bf16[32,2048]{1,0:T(8,128)(2,1)S(1)}, u32[]{:S(2)}, u32[]{:S(2)}) %collective-permute-start.20) | collective-permute-done | bytes 131104 | tf_op jit(solution)/shard_map/ppermute | solution.py:55
  72.5 3.8 %combine.2.refs_8_ = f32[256,2048]{1,0:T(8,128)S(1)} custom-call(bf16[32,2048]{1,0:T(8,128)(2,1)S(1)} %attend.3.refs_0_, bf16[32,2048]{1,0:T(8,128)(2,1)S(1)} %collective-permute-done.14.refs_1_, bf16[32,2048]{1,0:T(8,128)(2,1)S(1)} %collective-permute-done.15.refs_2_, bf16[32,2048]{1,0:T(8,128)(2,1)S(1)} %collective-permute-done.16.refs_3_, ...), custom_call_target="tpu_custom_call" | custom-call | tf_op jit(solution)/shard_map/combine/pallas_call | solution.py:379
  76.3 0.0 collective-permute-done.10.refs_4_
  76.3 0.0 collective-permute-done.11.refs_5_
  76.3 0.4 collective-permute-done.12.refs_6_
  76.7 1.4 %collective-permute-done.13.refs_7_ = bf16[32,2048]{1,0:T(8,128)(2,1)S(1)} collective-permute-done((bf16[32,2048]{1,0:T(8,128)(2,1)S(1)}, bf16[32,2048]{1,0:T(8,128)(2,1)S(1)}, u32[]{:S(2)}, u32[]{:S(2)}) %collective-permute-start.13) | collective-permute-done | bytes 131104 | tf_op jit(solution)/shard_map/ppermute | solution.py:55
  78.1 3.7 %combine.3 = (bf16[128,2048]{1,0:T(8,128)(2,1)S(1)}, f32[128,2048]{1,0:T(8,128)S(1)}) custom-call(bf16[32,2048]{1,0:T(8,128)(2,1)S(1)} %attend.2.refs_0_, bf16[32,2048]{1,0:T(8,128)(2,1)S(1)} %collective-permute-done.7.refs_1_, bf16[32,2048]{1,0:T(8,128)(2,1)S(1)} %collective-permute-done.8.refs_2_, bf16[32,2048]{1,0:T(8,128)(2,1)S(1)} %collective-permute-done.9.refs_3_, ...), custom_call_target="tpu_custom_call" | custom-call | tf_op jit(solution)/shard_map/combine/pallas_call | solution.py:379
  81.8 0.1 collective-permute-start.21
  81.9 1.9 %collective-permute-done.21 = bf16[128,2048]{1,0:T(8,128)(2,1)S(1)} collective-permute-done((bf16[128,2048]{1,0:T(8,128)(2,1)S(1)}, bf16[128,2048]{1,0:T(8,128)(2,1)S(1)}, u32[]{:S(2)}, u32[]{:S(2)}) %collective-permute-start.21) | collective-permute-done | bytes 524320 | tf_op jit(solution)/shard_map/ppermute | solution.py:507
  83.8 0.9 %add_convert_fusion = bf16[128,2048]{1,0:T(8,128)(2,1)} fusion(f32[128,2048]{1,0:T(8,128)S(1)} %get-tuple-element.47, bf16[128,2048]{1,0:T(8,128)(2,1)S(1)} %collective-permute-done.21), kind=kLoop, calls=%fused_computation.3 | loop fusion | flops 786432 | bytes 2097152 | tf_op jit(solution)/shard_map/convert_element_type | solution.py:508
  (10 shorter events, 0.2 us)
Async XLA Ops:
  4.4 7.7 %collective-permute-start = (bf16[128,1152]{1,0:T(8,128)(2,1)S(1)}, bf16[128,1152]{1,0:T(8,128)(2,1)S(1)}, u32[]{:S(2)}, u32[]{:S(2)}) collective-permute-start(bf16[128,1152]{1,0:T(8,128)(2,1)S(1)} %get-tuple-element.28), channel_id=1, source_target_pairs={{0,2},{1,5},{2,0},{3,7},{4,6},{5,1},{6,4},{7,3},{8,10},{9,13},{10,... | collective-permute-start | bytes 884744 | tf_op jit(solution)/shard_map/ppermute | solution.py:55
  11.3 7.1 %collective-permute-start.1 = (bf16[128,1280]{1,0:T(8,128)(2,1)S(1)}, bf16[128,1280]{1,0:T(8,128)(2,1)S(1)}, u32[]{:S(2)}, u32[]{:S(2)}) collective-permute-start(bf16[128,1280]{1,0:T(8,128)(2,1)S(1)} %get-tuple-element.30), channel_id=1, source_target_pairs={{0,2},{1,5},{2,0},{3,7},{4,6},{5,1},{6,4},{7,3},{8,10},{9,13},{10,... | collective-permute-start | bytes 983048 | tf_op jit(solution)/shard_map/ppermute | solution.py:55
  12.2 8.0 %copy-start = (s32[8]{0:T(128)S(1)}, s32[8]{0:T(128)}, u32[]{:S(2)}) copy-start(s32[8]{0:T(128)} %length_ref.3) | copy-start | bytes 100
  18.5 10.4 %collective-permute-start.3 = (bf16[64,2432]{1,0:T(8,128)(2,1)S(1)}, bf16[64,2432]{1,0:T(8,128)(2,1)}, u32[]{:S(2)}, u32[]{:S(2)}) collective-permute-start(bf16[64,2432]{1,0:T(8,128)(2,1)S(1)} %fusion.1), channel_id=1, source_target_pairs={{0,4},{1,3},{2,6},{3,1},{4,0},{5,7},{6,2},{7,5},{8,12},{9,11},{10,... | collective-permute-start | bytes 933896 | tf_op jit(solution)/shard_map/ppermute | solution.py:55
  20.3 15.7 %collective-permute-start.2 = (bf16[128,2304]{1,0:T(8,128)(2,1)S(1)}, bf16[128,2304]{1,0:T(8,128)(2,1)S(1)}, u32[]{:S(2)}, u32[]{:S(2)}) collective-permute-start(bf16[128,2304]{1,0:T(8,128)(2,1)S(1)} %get-tuple-element.38), channel_id=1, source_target_pairs={{0,2},{1,5},{2,0},{3,7},{4,6},{5,1},{6,4},{7,3},{8,10},{9,13},{10,... | collective-permute-start | bytes 1769480 | tf_op jit(solution)/shard_map/ppermute | solution.py:55
  29.9 8.5 %collective-permute-start.5 = (bf16[32,2432]{1,0:T(8,128)(2,1)S(1)}, bf16[32,2432]{1,0:T(8,128)(2,1)S(1)}, u32[]{:S(2)}, u32[]{:S(2)}) collective-permute-start(bf16[32,2432]{1,0:T(8,128)(2,1)S(1)} %slice.64), channel_id=1, source_target_pairs={{0,8},{1,9},{2,10},{3,11},{4,12},{5,13},{6,14},{7,15},{8,0},{9,1},... | collective-permute-start | bytes 466952 | tf_op jit(solution)/shard_map/ppermute | solution.py:55
  36.2 7.1 %collective-permute-start.4 = (bf16[64,2304]{1,0:T(8,128)(2,1)S(1)}, bf16[64,2304]{1,0:T(8,128)(2,1)S(1)}, u32[]{:S(2)}, u32[]{:S(2)}) collective-permute-start(bf16[64,2304]{1,0:T(8,128)(2,1)S(1)} %slice.63), channel_id=1, source_target_pairs={{0,4},{1,3},{2,6},{3,1},{4,0},{5,7},{6,2},{7,5},{8,12},{9,11},{10,... | collective-permute-start | bytes 884744 | tf_op jit(solution)/shard_map/ppermute | solution.py:55
  43.4 12.6 %collective-permute-start.6 = (bf16[32,2304]{1,0:T(8,128)(2,1)S(1)}, bf16[32,2304]{1,0:T(8,128)(2,1)S(1)}, u32[]{:S(2)}, u32[]{:S(2)}) collective-permute-start(bf16[32,2304]{1,0:T(8,128)(2,1)S(1)} %slice.65), channel_id=1, source_target_pairs={{0,8},{1,9},{2,10},{3,11},{4,12},{5,13},{6,14},{7,15},{8,0},{9,1},... | collective-permute-start | bytes 442376 | tf_op jit(solution)/shard_map/ppermute | solution.py:55
  46.7 12.2 %collective-permute-start.14 = (bf16[32,2048]{1,0:T(8,128)(2,1)S(1)}, bf16[32,2048]{1,0:T(8,128)(2,1)S(1)}, u32[]{:S(2)}, u32[]{:S(2)}) collective-permute-start(bf16[32,2048]{1,0:T(8,128)(2,1)S(1)} %attend.3.refs_0_), channel_id=1, source_target_pairs={{0,8},{1,9},{2,10},{3,11},{4,12},{5,13},{6,14},{7,15},{8,0},{9,1},... | collective-permute-start | bytes 393224 | tf_op jit(solution)/shard_map/ppermute | solution.py:55
  49.6 9.7 %collective-permute-start.15 = (bf16[32,2048]{1,0:T(8,128)(2,1)S(1)}, bf16[32,2048]{1,0:T(8,128)(2,1)S(1)}, u32[]{:S(2)}, u32[]{:S(2)}) collective-permute-start(bf16[32,2048]{1,0:T(8,128)(2,1)S(1)} %attend.3.refs_0_), channel_id=1, source_target_pairs={{0,4},{1,3},{2,6},{3,1},{4,0},{5,7},{6,2},{7,5},{8,12},{9,11},{10,... | collective-permute-start | bytes 393224 | tf_op jit(solution)/shard_map/ppermute | solution.py:55
  52.1 9.0 %collective-permute-start.17 = (bf16[32,2048]{1,0:T(8,128)(2,1)S(1)}, bf16[32,2048]{1,0:T(8,128)(2,1)S(1)}, u32[]{:S(2)}, u32[]{:S(2)}) collective-permute-start(bf16[32,2048]{1,0:T(8,128)(2,1)S(1)} %attend.3.refs_0_), channel_id=1, source_target_pairs={{0,2},{1,5},{2,0},{3,7},{4,6},{5,1},{6,4},{7,3},{8,10},{9,13},{10,... | collective-permute-start | bytes 393224 | tf_op jit(solution)/shard_map/ppermute | solution.py:55
  58.8 6.1 %collective-permute-start.7 = (bf16[32,2048]{1,0:T(8,128)(2,1)S(1)}, bf16[32,2048]{1,0:T(8,128)(2,1)S(1)}, u32[]{:S(2)}, u32[]{:S(2)}) collective-permute-start(bf16[32,2048]{1,0:T(8,128)(2,1)S(1)} %attend.2.refs_0_), channel_id=1, source_target_pairs={{0,8},{1,9},{2,10},{3,11},{4,12},{5,13},{6,14},{7,15},{8,0},{9,1},... | collective-permute-start | bytes 393224 | tf_op jit(solution)/shard_map/ppermute | solution.py:55
  58.9 7.9 %collective-permute-start.16 = (bf16[32,2048]{1,0:T(8,128)(2,1)S(1)}, bf16[32,2048]{1,0:T(8,128)(2,1)S(1)}, u32[]{:S(2)}, u32[]{:S(2)}) collective-permute-start(bf16[32,2048]{1,0:T(8,128)(2,1)S(1)} %collective-permute-done.14.refs_1_), channel_id=1, source_target_pairs={{0,4},{1,3},{2,6},{3,1},{4,0},{5,7},{6,2},{7,5},{8,12},{9,11},{10,... | collective-permute-start | bytes 393224 | tf_op jit(solution)/shard_map/ppermute | solution.py:55
  59.0 7.8 %collective-permute-start.18 = (bf16[32,2048]{1,0:T(8,128)(2,1)S(1)}, bf16[32,2048]{1,0:T(8,128)(2,1)S(1)}, u32[]{:S(2)}, u32[]{:S(2)}) collective-permute-start(bf16[32,2048]{1,0:T(8,128)(2,1)S(1)} %collective-permute-done.14.refs_1_), channel_id=1, source_target_pairs={{0,2},{1,5},{2,0},{3,7},{4,6},{5,1},{6,4},{7,3},{8,10},{9,13},{10,... | collective-permute-start | bytes 393224 | tf_op jit(solution)/shard_map/ppermute | solution.py:55
  59.3 9.5 %collective-permute-start.19 = (bf16[32,2048]{1,0:T(8,128)(2,1)S(1)}, bf16[32,2048]{1,0:T(8,128)(2,1)S(1)}, u32[]{:S(2)}, u32[]{:S(2)}) collective-permute-start(bf16[32,2048]{1,0:T(8,128)(2,1)S(1)} %collective-permute-done.15.refs_2_), channel_id=1, source_target_pairs={{0,2},{1,5},{2,0},{3,7},{4,6},{5,1},{6,4},{7,3},{8,10},{9,13},{10,... | collective-permute-start | bytes 393224 | tf_op jit(solution)/shard_map/ppermute | solution.py:55
  61.1 8.0 %collective-permute-start.8 = (bf16[32,2048]{1,0:T(8,128)(2,1)S(1)}, bf16[32,2048]{1,0:T(8,128)(2,1)S(1)}, u32[]{:S(2)}, u32[]{:S(2)}) collective-permute-start(bf16[32,2048]{1,0:T(8,128)(2,1)S(1)} %attend.2.refs_0_), channel_id=1, source_target_pairs={{0,4},{1,5},{2,6},{3,7},{4,0},{5,1},{6,2},{7,3},{8,12},{9,13},{10,... | collective-permute-start | bytes 393224 | tf_op jit(solution)/shard_map/ppermute | solution.py:55
  65.0 5.9 %collective-permute-start.9 = (bf16[32,2048]{1,0:T(8,128)(2,1)S(1)}, bf16[32,2048]{1,0:T(8,128)(2,1)S(1)}, u32[]{:S(2)}, u32[]{:S(2)}) collective-permute-start(bf16[32,2048]{1,0:T(8,128)(2,1)S(1)} %collective-permute-done.7.refs_1_), channel_id=1, source_target_pairs={{0,4},{1,5},{2,6},{3,7},{4,0},{5,1},{6,2},{7,3},{8,12},{9,13},{10,... | collective-permute-start | bytes 393224 | tf_op jit(solution)/shard_map/ppermute | solution.py:55
  66.8 5.6 %collective-permute-start.20 = (bf16[32,2048]{1,0:T(8,128)(2,1)S(1)}, bf16[32,2048]{1,0:T(8,128)(2,1)S(1)}, u32[]{:S(2)}, u32[]{:S(2)}) collective-permute-start(bf16[32,2048]{1,0:T(8,128)(2,1)S(1)} %collective-permute-done.16.refs_3_), channel_id=1, source_target_pairs={{0,2},{1,5},{2,0},{3,7},{4,6},{5,1},{6,4},{7,3},{8,10},{9,13},{10,... | collective-permute-start | bytes 393224 | tf_op jit(solution)/shard_map/ppermute | solution.py:55
  66.8 9.4 %collective-permute-start.10 = (bf16[32,2048]{1,0:T(8,128)(2,1)S(1)}, bf16[32,2048]{1,0:T(8,128)(2,1)S(1)}, u32[]{:S(2)}, u32[]{:S(2)}) collective-permute-start(bf16[32,2048]{1,0:T(8,128)(2,1)S(1)} %attend.2.refs_0_), channel_id=1, source_target_pairs={{0,2},{1,3},{2,0},{3,1},{4,6},{5,7},{6,4},{7,5},{8,10},{9,11},{10,... | collective-permute-start | bytes 393224 | tf_op jit(solution)/shard_map/ppermute | solution.py:55
  68.9 7.4 %collective-permute-start.11 = (bf16[32,2048]{1,0:T(8,128)(2,1)S(1)}, bf16[32,2048]{1,0:T(8,128)(2,1)S(1)}, u32[]{:S(2)}, u32[]{:S(2)}) collective-permute-start(bf16[32,2048]{1,0:T(8,128)(2,1)S(1)} %collective-permute-done.7.refs_1_), channel_id=1, source_target_pairs={{0,2},{1,3},{2,0},{3,1},{4,6},{5,7},{6,4},{7,5},{8,10},{9,11},{10,... | collective-permute-start | bytes 393224 | tf_op jit(solution)/shard_map/ppermute | solution.py:55
  69.1 7.6 %collective-permute-start.12 = (bf16[32,2048]{1,0:T(8,128)(2,1)S(1)}, bf16[32,2048]{1,0:T(8,128)(2,1)S(1)}, u32[]{:S(2)}, u32[]{:S(2)}) collective-permute-start(bf16[32,2048]{1,0:T(8,128)(2,1)S(1)} %collective-permute-done.8.refs_2_), channel_id=1, source_target_pairs={{0,2},{1,3},{2,0},{3,1},{4,6},{5,7},{6,4},{7,5},{8,10},{9,11},{10,... | collective-permute-start | bytes 393224 | tf_op jit(solution)/shard_map/ppermute | solution.py:55
  70.9 7.2 %collective-permute-start.13 = (bf16[32,2048]{1,0:T(8,128)(2,1)S(1)}, bf16[32,2048]{1,0:T(8,128)(2,1)S(1)}, u32[]{:S(2)}, u32[]{:S(2)}) collective-permute-start(bf16[32,2048]{1,0:T(8,128)(2,1)S(1)} %collective-permute-done.9.refs_3_), channel_id=1, source_target_pairs={{0,2},{1,3},{2,0},{3,1},{4,6},{5,7},{6,4},{7,5},{8,10},{9,11},{10,... | collective-permute-start | bytes 393224 | tf_op jit(solution)/shard_map/ppermute | solution.py:55
  81.8 2.0 %collective-permute-start.21 = (bf16[128,2048]{1,0:T(8,128)(2,1)S(1)}, bf16[128,2048]{1,0:T(8,128)(2,1)S(1)}, u32[]{:S(2)}, u32[]{:S(2)}) collective-permute-start(bf16[128,2048]{1,0:T(8,128)(2,1)S(1)} %get-tuple-element.48), channel_id=1, source_target_pairs={{0,1},{1,0},{2,3},{3,2},{4,5},{5,4},{6,7},{7,6},{8,9},{9,8},{10,11... | collective-permute-start | bytes 1572872 | tf_op jit(solution)/shard_map/ppermute | solution.py:507

commit v5 on v4

--- a/solution.py
+++ b/solution.py
@@ -28,9 +28,14 @@
     return first, second
 
 
+def sum_orders(n, chunk):
+    first, second = bit_orders(n)
+    return (second, first) if chunk else (first, second)
+
+
 def gather_orders(n, chunk):
     first, second = bit_orders(n)
-    return (first, first) if chunk else (first, second)
+    return (first, second) if chunk else (first, first)
 
 
 def slot_shift(slot, order):
@@ -39,6 +44,11 @@
     for stage in range(levels):
         shift |= ((slot >> (levels - 1 - stage)) & 1) << order[stage]
     return shift
+
+
+def changed_slot(n, slot):
+    first, second = bit_orders(n)
+    return [slot_shift(other, first) for other in range(n)].index(slot_shift(slot, second))
 
 
 def slot_owner(n, slot, gx, gy, orders):
@@ -55,7 +65,7 @@
     return lax.ppermute(value, ("gx", "gy"), pairs)
 
 
-def project_kernel(n, q_start, kv_start, first, *refs):
+def project_kernel(n, q_start, kv_start, first, chunk, *refs):
     if first:
         tokens_ref, gain_ref, wq_ref, wk_ref, wv_ref, send_ref, keep_ref, x_ref = refs[:8]
         t_buf, t_sems, g_buf, g_sem = refs[8:12]
@@ -85,7 +95,7 @@
         me, gy = lax.axis_index("gx"), lax.axis_index("gy")
         t_copies = []
         for slot in range(n):
-            start = pl.multiple_of(slot_owner(n, slot, me, gy, bit_orders(n)) * block, block)
+            start = pl.multiple_of(slot_owner(n, slot, me, gy, sum_orders(n, 0)) * block, block)
             t_copies.append(
                 pltpu.make_async_copy(
                     tokens_ref.at[pl.ds(start, block), :], t_buf.at[slot], t_sems.at[slot]
@@ -103,7 +113,7 @@
         for slot in range(n):
             t_copies[slot].wait()
             wide = t_buf[slot].astype(jnp.float32)
-            x_ref[slot * block : (slot + 1) * block, :] = (wide * g_buf[...]).astype(jnp.bfloat16)
+            x_ref[0, slot * block : (slot + 1) * block, :] = (wide * g_buf[...]).astype(jnp.bfloat16)
             square = jnp.sum(wide * wide, axis=1, keepdims=True)
             high = square.astype(jnp.bfloat16).astype(jnp.float32)
             rest = square - high
@@ -120,10 +130,15 @@
                 at = (slot - n // 2) * block
                 send_ref[at : at + block, width : width + 128] = packed.astype(jnp.bfloat16)
 
+        for slot in range(n):
+            x_ref[1, slot * block : (slot + 1) * block, :] = x_ref[
+                0, changed_slot(n, slot) * block : (changed_slot(n, slot) + 1) * block, :
+            ]
+
     for p, (start, end) in enumerate(((0, tile), (tile, width))):
         for copy in copies[p]:
             copy.wait()
-        product = jnp.dot(x_ref[...], w_buf[:, start:end], preferred_element_type=jnp.float32)
+        product = jnp.dot(x_ref[chunk], w_buf[:, start:end], preferred_element_type=jnp.float32)
         keep_ref[:, start:end] = product[:half]
         send_ref[:, start:end] = product[half:].astype(jnp.bfloat16)
 
@@ -133,7 +148,8 @@
 
 
 def project(n, q_start, q_cols, kv_start, first, x, gain, w_query, w_key, w_value):
-    rows, depth = x.shape
+    rows, depth = x.shape[-2:]
+    chunk = q_start // (w_query.shape[1] // CHUNKS)
     kv = w_key.shape[1] // CHUNKS if kv_start is not None else 0
     width = q_cols + 2 * kv
     full = width + (128 if first else 0)
@@ -145,7 +161,7 @@
     ]
     scratch = [pltpu.VMEM((depth, width), jnp.bfloat16), pltpu.SemaphoreType.DMA((4,))]
     if first:
-        out_shape.append(pltpu.VMEM((rows, depth), jnp.bfloat16))
+        out_shape.append(pltpu.VMEM((CHUNKS, rows, depth), jnp.bfloat16))
         args = [in_hbm(x), in_hbm(gain)]
         in_specs = [hbm, hbm]
         scratch = [
@@ -157,7 +173,7 @@
     else:
         args, in_specs = [x], [vmem]
     return pl.pallas_call(
-        functools.partial(project_kernel, n, q_start, kv_start, first),
+        functools.partial(project_kernel, n, q_start, kv_start, first, chunk),
         out_shape=out_shape,
         in_specs=in_specs + [hbm] * 3,
         out_specs=[vmem] * len(out_shape),
@@ -328,8 +344,9 @@
     )(in_hbm(array))
 
 
-def combine_kernel(n, block, chunk, *refs):
-    pieces, refs = refs[:n], refs[n:]
+def combine_kernel(n, block, chunk, slots, *refs):
+    count = 1 + max(piece for piece, _ in slots)
+    pieces, refs = refs[:count], refs[count:]
     gx, gy = lax.axis_index("gx"), lax.axis_index("gy")
     moved = jnp.where(gy == 0, n // 2, 0)
     if chunk:
@@ -338,10 +355,14 @@
     depth, cols = x_buf.shape[1], w_ref.shape[1]
     half = x_buf.shape[0] // 2
     x_copies = []
-    for slot, piece in enumerate(pieces):
+    for slot, (piece, at) in enumerate(slots):
         start = pl.multiple_of((slot_owner(n, slot, gx, gy, gather_orders(n, chunk)) ^ moved) * block, block)
         x_copies.append(
-            pltpu.make_async_copy(piece, x_buf.at[pl.ds(start, block), :], x_sems.at[slot])
+            pltpu.make_async_copy(
+                pieces[piece].at[at : at + block, :],
+                x_buf.at[pl.ds(start, block), :],
+                x_sems.at[slot],
+            )
         )
     for copy in x_copies:
         copy.start()
@@ -361,8 +382,8 @@
             outs[1][:, at] = product[half:]
 
 
-def combine(chunk, pieces, before, w_out):
-    n, (block, depth) = len(pieces), pieces[0].shape
+def combine(chunk, pieces, slots, before, w_out):
+    n, (block, depth) = len(slots), pieces[0].shape
     rows = n * block
     cols = w_out.shape[1]
     last = chunk == CHUNKS - 1
@@ -377,7 +398,7 @@
         out_shape = [pltpu.VMEM((rows, cols), jnp.float32)]
     earlier = [] if chunk == 0 else [before]
     return pl.pallas_call(
-        functools.partial(combine_kernel, n, block, chunk),
+        functools.partial(combine_kernel, n, block, chunk, slots),
         out_shape=out_shape,
         in_specs=[pl.BlockSpec(memory_space=pl.ANY)] * len(pieces)
         + [vmem] * len(earlier)
@@ -418,13 +439,12 @@
         return lax.optimization_barrier((value, earlier))[0]
 
     share = q_cols // 2
-    orders = bit_orders(n)
     send_a, keep_a, x = column_part(0, share, None)
     x = after(x, send_a)
-    other_a = exchange(send_a, n, cores, 0, orders)
+    other_a = exchange(send_a, n, cores, 0, sum_orders(n, 0))
     send_b, keep_b = column_part(share, share, 0)
     x = after(x, send_b)
-    other_b = exchange(send_b, n, cores, 0, orders)
+    other_b = exchange(send_b, n, cores, 0, sum_orders(n, 0))
     sum_a = keep_a + other_a.astype(jnp.float32)
     x = after(x, sum_a)
     later = []
@@ -439,7 +459,7 @@
         flows.append([0, keep_c, after(send_c, flows[-1][2])])
 
     def start(flow):
-        return exchange(flow[2], n, cores, flow[0], orders)
+        return exchange(flow[2], n, cores, flow[0], sum_orders(n, 0 if flow is flows[0] else 1))
 
     def finish(flow, other, *earlier):
         stage, keep, _ = flow
@@ -451,37 +471,35 @@
 
     lead, follow = flows
     w_rows = w_out.shape[0] // CHUNKS
-    source = after(w_out, lead[2], follow[2])
-    weights = [fetch_rows(source, chunk * w_rows, w_rows) for chunk in range(CHUNKS)]
-    stage = 0
+    weights = [fetch_rows(after(w_out, lead[2], follow[2]), 0, w_rows)]
     while follow[0] < levels:
         pending = [start(flow) for flow in flows if flow[0] < levels]
         if lead[0] == levels:
             finish(follow, pending[0])
         elif lead[0] == levels - 1:
-            finish(lead, pending[0])
-            finish(follow, pending[1], lead[1])
+            cache_keys, cache_values = fetch(*after((cache_keys, cache_values), follow[2]))
+            finish(lead, pending[0], cache_keys, cache_values)
+            weights.append(fetch_rows(after(w_out, cache_keys), w_rows, w_rows))
+            finish(follow, pending[1], lead[1], weights[1])
         else:
             finish(lead, pending[0], *weights)
-            between = [lead[2]]
-            if stage == 0:
-                cache_keys, cache_values = fetch(*after((cache_keys, cache_values), lead[2]))
-                between += [cache_keys, cache_values]
-            finish(follow, pending[1], *between)
-        stage += 1
+            finish(follow, pending[1], lead[2])
     sums = [flow[1] for flow in flows]
     squares = sums[0][:, share : share + 128]
     plain = [h * HD for h in range(q_cols // HD)]
     offsets = [[at if at < share else at + 128 for at in plain], plain]
     kv_offsets = [q_cols + 128, q_cols]
 
-    gathered = []
+    attentions, own = [], []
     for chunk in range(CHUNKS):
+        mine = sums[chunk]
+        if chunk:
+            mine = after(mine, *own[-1][:-1])
         attention = attend(
             chunk,
             offsets[chunk],
             kv_offsets[chunk],
-            sums[chunk],
+            mine,
             squares,
             cosine,
             sine,
@@ -489,20 +507,36 @@
             cache_values,
             cache_lengths,
         )
-        slots = [attention]
-        for slot in range(1, n):
-            top = slot.bit_length() - 1
-            slots.append(exchange(
-                    slots[slot - (1 << top)],
-                    n,
-                    cores,
-                    levels - 1 - top,
-                    gather_orders(n, chunk),
-                ))
-        gathered.append(slots)
+        attentions.append(attention)
+        own.append(
+            [
+                exchange(attention, n, cores, stage, gather_orders(n, chunk))
+                for stage in range(levels)
+            ]
+        )
+    gathered = []
+    for chunk in range(CHUNKS):
+        block = attentions[chunk].shape[0]
+        pieces, slots = [attentions[chunk]], [(0, 0)]
+        for top in range(levels):
+            stage = levels - 1 - top
+            received = [own[chunk][stage]]
+            if top:
+                others = pieces[1:]
+                forward = jnp.concatenate(others, axis=0) if top > 1 else others[0]
+                if top == 1:
+                    forward = after(forward, *own[chunk][:-1], attentions[-1])
+                if stage == 0:
+                    forward = after(forward, *own[-1][:-1])
+                received.append(exchange(forward, n, cores, stage, gather_orders(n, chunk)))
+            for value in received:
+                for at in range(0, value.shape[0], block):
+                    slots.append((len(pieces), at))
+                pieces.append(value)
+        gathered.append((pieces, slots))
     result = None
     for chunk in range(CHUNKS):
-        result = combine(chunk, gathered[chunk], result and result[0], weights[chunk])
+        result = combine(chunk, *gathered[chunk], result and result[0], weights[chunk])
     send, keep = result
     other = lax.ppermute(send, "gy", [(0, 1), (1, 0)])
     return (keep + other.astype(jnp.float32)).astype(jnp.bfloat16)

time: 84.8 us -> 92.4 us (1.090)
  waiting for transfers between devices: 18.1 us -> 33.2 us
  starting transfers between devices: 26.2 us -> 18.8 us
    ppermute x21 -> x17, waiting for transfers between devices: 16.2 us -> 31.3 us  [exchange(): return lax.ppermute(value, ('gx', 'gy'), pairs)]
    ppermute x21 -> x17, starting transfers between devices: 26.1 us -> 18.7 us  [exchange(): return lax.ppermute(value, ('gx', 'gy'), pairs)]
  transfers between devices with their start and end apart: 22 -> 18, of which waited for: 13 -> 14; matrix products, arithmetic and copies ran while one was open for 2% -> 2% of each run, Pallas kernels for 35% -> 32%
where the time goes in v5:
time: 92.4 us; the launch traced here: 92.3 us
  Pallas kernels  37.3 us (40%)
  waiting for transfers between devices  33.2 us (36%)
  starting transfers between devices  18.8 us (20%)
  other arithmetic  2.67 us (3%)
    ppermute x17, waiting for transfers between devices, exchange(): return lax.ppermute(value, ('gx', 'gy'), pairs)  31.3 us
    ppermute x17, starting transfers between devices, exchange(): return lax.ppermute(value, ('gx', 'gy'), pairs)  18.7 us
    pallas_call x3, Pallas kernels, project(): pl.pallas_call(functools.partial(project_kernel, n, q_start, kv_start, fi...  13.7 us
    pallas_call x2, Pallas kernels, combine(): pl.pallas_call(functools.partial(combine_kernel, n, block, chunk, slots),...  7.48 us
    pallas_call x2, Pallas kernels, fetch_rows(): pl.pallas_call(functools.partial(fetch_rows_kernel, start, pieces), out_s...  7.01 us
    pallas_call x2, Pallas kernels, attend(): pl.pallas_call(functools.partial(attend_kernel, chunk, offsets, kv_offset...  5.62 us
    pallas_call x1, Pallas kernels, fetch(): pl.pallas_call(functools.partial(fetch_kernel, len(arrays), pieces), out_...  3.47 us
    ppermute x1, waiting for transfers between devices, shards(): other = lax.ppermute(send, 'gy', [(0, 1), (1, 0)])  1.9 us
  transfers between devices with their start and end apart: 18, of which 14 were waited for; matrix products, arithmetic and copies ran while one was open for 2% of the time, Pallas kernels for 32%

profile of v5, /device:TPU:0, one launch (start us, length us, event | category | flops | bytes accessed | tf_op | source)
XLA Modules:
  0.0 92.3 jit_solution(5581903297493155715)
XLA Ops:
  0.0 4.3 %project.3 = (bf16[128,1152]{1,0:T(8,128)(2,1)S(1)}, f32[128,1152]{1,0:T(8,128)S(1)}, bf16[2,256,2048]{2,1,0:T(8,128)(2,1)S(1)}) custom-call(bf16[256,2048]{1,0:T(8,128)(2,1)} %refs_0_.1, f32[1,2048]{1,0:T(1,128)} %bitcast.1, bf16[2048,4096]{1,0:T(8,128)(2,1)} %refs_1_.3, bf16[2048,256]{1,0:T(8,128)(2,1)} %refs_2_.5, bf16[2048,256]{1,0:T(8,128)(2,1)} %refs_3_.5), custom_call_target="tpu_custom_call" | custom-call | tf_op jit(solution)/shard_map/project/pallas_call | solution.py:175
  4.4 3.0 %collective-permute-start = (bf16[128,1152]{1,0:T(8,128)(2,1)S(1)}, bf16[128,1152]{1,0:T(8,128)(2,1)S(1)}, u32[]{:S(2)}, u32[]{:S(2)}) collective-permute-start(bf16[128,1152]{1,0:T(8,128)(2,1)S(1)} %get-tuple-element.35), channel_id=1, source_target_pairs={{0,2},{1,5},{2,0},{3,7},{4,6},{5,1},{6,4},{7,3},{8,10},{9,13},{10,... | collective-permute-start | bytes 884744 | tf_op jit(solution)/shard_map/ppermute | solution.py:65
  7.4 3.9 %project.4 = (bf16[128,1280]{1,0:T(8,128)(2,1)S(1)}, f32[128,1280]{1,0:T(8,128)S(1)}) custom-call(bf16[2,256,2048]{2,1,0:T(8,128)(2,1)S(1)} %get-tuple-element.40.refs_0_, bf16[2048,4096]{1,0:T(8,128)(2,1)} %refs_1_.3, bf16[2048,256]{1,0:T(8,128)(2,1)} %refs_2_.5, bf16[2048,256]{1,0:T(8,128)(2,1)} %refs_3_.5), custom_call_target="tpu_custom_call" | custom-call | tf_op jit(solution)/shard_map/project/pallas_call | solution.py:175
  11.2 0.1 collective-permute-start.1
  11.3 0.8 collective-permute-done
  12.1 0.1 convert_add_fusion.2
  12.1 0.0 copy-start
  12.2 5.5 %project.5 = (bf16[128,2304]{1,0:T(8,128)(2,1)S(1)}, f32[128,2304]{1,0:T(8,128)S(1)}) custom-call(bf16[2,256,2048]{2,1,0:T(8,128)(2,1)S(1)} %get-tuple-element.40.refs_0_, bf16[2048,4096]{1,0:T(8,128)(2,1)} %refs_1_.3, bf16[2048,256]{1,0:T(8,128)(2,1)} %refs_2_.5, bf16[2048,256]{1,0:T(8,128)(2,1)} %refs_3_.5), custom_call_target="tpu_custom_call" | custom-call | tf_op jit(solution)/shard_map/project/pallas_call | solution.py:175
  17.7 0.7 collective-permute-done.1
  18.4 0.1 convert_add_fusion.1
  18.5 1.6 %collective-permute-start.3 = (bf16[64,2432]{1,0:T(8,128)(2,1)S(1)}, bf16[64,2432]{1,0:T(8,128)(2,1)}, u32[]{:S(2)}, u32[]{:S(2)}) collective-permute-start(bf16[64,2432]{1,0:T(8,128)(2,1)S(1)} %fusion.1), channel_id=1, source_target_pairs={{0,4},{1,3},{2,6},{3,1},{4,0},{5,7},{6,2},{7,5},{8,12},{9,11},{10,... | collective-permute-start | bytes 933896 | tf_op jit(solution)/shard_map/ppermute | solution.py:65
  20.1 0.0 copy-done
  20.1 0.1 add_convert_fusion.1
  20.2 0.1 convert_element_type.49
  20.3 0.5 collective-permute-start.2
  20.8 3.5 %fetch_rows.2.refs_6_ = bf16[2048,2048]{1,0:T(8,128)(2,1)S(1)} custom-call(bf16[4096,2048]{1,0:T(8,128)(2,1)} %source.1), custom_call_target="tpu_custom_call" | custom-call | tf_op jit(solution)/shard_map/fetch_rows/pallas_call | solution.py:336
  24.3 1.2 %collective-permute-done.3 = bf16[64,2432]{1,0:T(8,128)(2,1)} collective-permute-done((bf16[64,2432]{1,0:T(8,128)(2,1)S(1)}, bf16[64,2432]{1,0:T(8,128)(2,1)}, u32[]{:S(2)}, u32[]{:S(2)}) %collective-permute-start.3) | collective-permute-done | bytes 311328 | tf_op jit(solution)/shard_map/ppermute | solution.py:65
  25.6 1.0 %fusion.2 = f32[64,2432]{1,0:T(8,128)S(1)} fusion(f32[128,1280]{1,0:T(8,128)S(1)} %convert_add_fusion.1, f32[128,1152]{1,0:T(8,128)S(1)} %convert_add_fusion.2, bf16[64,2432]{1,0:T(8,128)(2,1)} %collective-permute-done.3), kind=kLoop, calls=%fused_computation.8 | loop fusion | flops 466944 | bytes 2179072 | tf_op jit(solution)/shard_map/add | solution.py:468
  26.6 2.7 %collective-permute-start.5 = (bf16[32,2432]{1,0:T(8,128)(2,1)S(1)}, bf16[32,2432]{1,0:T(8,128)(2,1)S(1)}, u32[]{:S(2)}, u32[]{:S(2)}) collective-permute-start(bf16[32,2432]{1,0:T(8,128)(2,1)S(1)} %slice.64), channel_id=1, source_target_pairs={{0,8},{1,9},{2,10},{3,11},{4,12},{5,13},{6,14},{7,15},{8,0},{9,1},... | collective-permute-start | bytes 466952 | tf_op jit(solution)/shard_map/ppermute | solution.py:65
  29.3 7.4 %collective-permute-done.2 = bf16[128,2304]{1,0:T(8,128)(2,1)S(1)} collective-permute-done((bf16[128,2304]{1,0:T(8,128)(2,1)S(1)}, bf16[128,2304]{1,0:T(8,128)(2,1)S(1)}, u32[]{:S(2)}, u32[]{:S(2)}) %collective-permute-start.2) | collective-permute-done | bytes 589856 | tf_op jit(solution)/shard_map/ppermute | solution.py:65
  36.7 0.1 convert_add_fusion
  36.8 1.3 %collective-permute-start.4 = (bf16[64,2304]{1,0:T(8,128)(2,1)S(1)}, bf16[64,2304]{1,0:T(8,128)(2,1)S(1)}, u32[]{:S(2)}, u32[]{:S(2)}) collective-permute-start(bf16[64,2304]{1,0:T(8,128)(2,1)S(1)} %slice.63), channel_id=1, source_target_pairs={{0,2},{1,5},{2,0},{3,7},{4,6},{5,1},{6,4},{7,3},{8,10},{9,13},{10,... | collective-permute-start | bytes 884744 | tf_op jit(solution)/shard_map/ppermute | solution.py:65
  38.1 3.5 %fetch.1 = (bf16[8,1024,256]{2,1,0:T(8,128)(2,1)S(1)}, bf16[8,1024,256]{2,1,0:T(8,128)(2,1)S(1)}) custom-call(bf16[8,1024,256]{2,1,0:T(8,128)(2,1)} %refs_0_.2, bf16[8,1024,256]{2,1,0:T(8,128)(2,1)} %refs_1_.4), custom_call_target="tpu_custom_call" | custom-call | tf_op jit(solution)/shard_map/fetch/pallas_call | solution.py:307
  41.6 0.0 collective-permute-done.5
  41.7 3.5 %fetch_rows.3.refs_7_ = bf16[2048,2048]{1,0:T(8,128)(2,1)S(1)} custom-call(bf16[4096,2048]{1,0:T(8,128)(2,1)} %source.1), custom_call_target="tpu_custom_call" | custom-call | tf_op jit(solution)/shard_map/fetch_rows/pallas_call | solution.py:336
  45.2 0.0 collective-permute-done.4
  45.2 0.1 slice_add_fusion
  45.3 2.0 %collective-permute-start.6 = (bf16[32,2304]{1,0:T(8,128)(2,1)S(1)}, bf16[32,2304]{1,0:T(8,128)(2,1)S(1)}, u32[]{:S(2)}, u32[]{:S(2)}) collective-permute-start(bf16[32,2304]{1,0:T(8,128)(2,1)S(1)} %slice.65), channel_id=1, source_target_pairs={{0,8},{1,9},{2,10},{3,11},{4,12},{5,13},{6,14},{7,15},{8,0},{9,1},... | collective-permute-start | bytes 442376 | tf_op jit(solution)/shard_map/ppermute | solution.py:65
  47.2 0.1 fusion.3
  47.4 0.1 pad_maximum_fusion.3
  47.5 2.9 %attend.2.refs_0_ = bf16[32,2048]{1,0:T(8,128)(2,1)S(1)} custom-call(s32[8]{0:T(128)S(1)} %copy-done, f32[32,2432]{1,0:T(8,128)S(1)} %slice_add_fusion.1.refs_0_, f32[32,128]{1,0:T(8,128)S(1)} %slice.48.refs_1_, f32[32,128]{1,0:T(8,128)S(1)} %get-tuple-element.66.refs_2_, f32[32,128]{1,0:T(8,128)S(1)} %get-tuple-element.67.refs_3_, ...), custom_call_target="tpu_custom_call" | custom-call | tf_op jit(solution)/shard_map/attend/pallas_call | solution.py:275
  50.4 0.9 collective-permute-start.7
  51.3 2.5 %collective-permute-start.8 = (bf16[32,2048]{1,0:T(8,128)(2,1)S(1)}, bf16[32,2048]{1,0:T(8,128)(2,1)S(1)}, u32[]{:S(2)}, u32[]{:S(2)}) collective-permute-start(bf16[32,2048]{1,0:T(8,128)(2,1)S(1)} %attend.2.refs_0_), channel_id=1, source_target_pairs={{0,4},{1,5},{2,6},{3,7},{4,0},{5,1},{6,2},{7,3},{8,12},{9,13},{10,... | collective-permute-start | bytes 393224 | tf_op jit(solution)/shard_map/ppermute | solution.py:65
  53.8 0.0 collective-permute-start.14
  53.8 2.0 %collective-permute-done.6 = bf16[32,2304]{1,0:T(8,128)(2,1)S(1)} collective-permute-done((bf16[32,2304]{1,0:T(8,128)(2,1)S(1)}, bf16[32,2304]{1,0:T(8,128)(2,1)S(1)}, u32[]{:S(2)}, u32[]{:S(2)}) %collective-permute-start.6) | collective-permute-done | bytes 147488 | tf_op jit(solution)/shard_map/ppermute | solution.py:65
  55.9 0.5 collective-permute-done.7.refs_4_
  56.4 4.0 %collective-permute-done.8.refs_2_ = bf16[32,2048]{1,0:T(8,128)(2,1)S(1)} collective-permute-done((bf16[32,2048]{1,0:T(8,128)(2,1)S(1)}, bf16[32,2048]{1,0:T(8,128)(2,1)S(1)}, u32[]{:S(2)}, u32[]{:S(2)}) %collective-permute-start.8) | collective-permute-done | bytes 131104 | tf_op jit(solution)/shard_map/ppermute | solution.py:65
  60.4 2.7 %attend.3.refs_0_ = bf16[32,2048]{1,0:T(8,128)(2,1)S(1)} custom-call(s32[8]{0:T(128)S(1)} %copy-done, f32[32,2304]{1,0:T(8,128)S(1)} %slice_add_fusion.2.refs_0_, f32[32,128]{1,0:T(8,128)S(1)} %slice.48.refs_1_, f32[32,128]{1,0:T(8,128)S(1)} %get-tuple-element.66.refs_2_, f32[32,128]{1,0:T(8,128)S(1)} %get-tuple-element.67.refs_3_, ...), custom_call_target="tpu_custom_call" | custom-call | tf_op jit(solution)/shard_map/attend/pallas_call | solution.py:275
  63.1 0.1 collective-permute-start.9
  63.2 1.4 %collective-permute-start.10 = (bf16[32,2048]{1,0:T(8,128)(2,1)S(1)}, bf16[32,2048]{1,0:T(8,128)(2,1)S(1)}, u32[]{:S(2)}, u32[]{:S(2)}) collective-permute-start(bf16[32,2048]{1,0:T(8,128)(2,1)S(1)} %attend.3.refs_0_), channel_id=1, source_target_pairs={{0,4},{1,3},{2,6},{3,1},{4,0},{5,7},{6,2},{7,5},{8,12},{9,11},{10,... | collective-permute-start | bytes 393224 | tf_op jit(solution)/shard_map/ppermute | solution.py:65
  64.5 0.0 collective-permute-start.11
  64.5 0.0 collective-permute-done.14.refs_1_
  64.5 1.2 %collective-permute-start.15 = (bf16[32,2048]{1,0:T(8,128)(2,1)S(1)}, bf16[32,2048]{1,0:T(8,128)(2,1)S(1)}, u32[]{:S(2)}, u32[]{:S(2)}) collective-permute-start(bf16[32,2048]{1,0:T(8,128)(2,1)S(1)} %collective-permute-done.14.refs_1_), channel_id=1, source_target_pairs={{0,4},{1,5},{2,6},{3,7},{4,0},{5,1},{6,2},{7,3},{8,12},{9,13},{10,... | collective-permute-start | bytes 393224 | tf_op jit(solution)/shard_map/ppermute | solution.py:65
  65.7 3.6 %collective-permute-done.9.refs_1_ = bf16[32,2048]{1,0:T(8,128)(2,1)S(1)} collective-permute-done((bf16[32,2048]{1,0:T(8,128)(2,1)S(1)}, bf16[32,2048]{1,0:T(8,128)(2,1)S(1)}, u32[]{:S(2)}, u32[]{:S(2)}) %collective-permute-start.9) | collective-permute-done | bytes 131104 | tf_op jit(solution)/shard_map/ppermute | solution.py:65
  69.3 1.4 %collective-permute-done.10.refs_2_ = bf16[32,2048]{1,0:T(8,128)(2,1)S(1)} collective-permute-done((bf16[32,2048]{1,0:T(8,128)(2,1)S(1)}, bf16[32,2048]{1,0:T(8,128)(2,1)S(1)}, u32[]{:S(2)}, u32[]{:S(2)}) %collective-permute-start.10) | collective-permute-done | bytes 131104 | tf_op jit(solution)/shard_map/ppermute | solution.py:65
  70.8 0.0 collective-permute-done.11.refs_4_
  70.8 0.9 %collective-permute-start.12 = (bf16[32,2048]{1,0:T(8,128)(2,1)S(1)}, bf16[32,2048]{1,0:T(8,128)(2,1)S(1)}, u32[]{:S(2)}, u32[]{:S(2)}) collective-permute-start(bf16[32,2048]{1,0:T(8,128)(2,1)S(1)} %collective-permute-done.9.refs_1_), channel_id=1, source_target_pairs={{0,4},{1,3},{2,6},{3,1},{4,0},{5,7},{6,2},{7,5},{8,12},{9,11},{10,... | collective-permute-start | bytes 393224 | tf_op jit(solution)/shard_map/ppermute | solution.py:65
  71.7 1.9 %collective-permute-done.15.refs_3_ = bf16[32,2048]{1,0:T(8,128)(2,1)S(1)} collective-permute-done((bf16[32,2048]{1,0:T(8,128)(2,1)S(1)}, bf16[32,2048]{1,0:T(8,128)(2,1)S(1)}, u32[]{:S(2)}, u32[]{:S(2)}) %collective-permute-start.15) | collective-permute-done | bytes 131104 | tf_op jit(solution)/shard_map/ppermute | solution.py:65
  73.6 0.1 collective-permute-start.16
  73.7 3.0 %collective-permute-done.12.refs_3_ = bf16[32,2048]{1,0:T(8,128)(2,1)S(1)} collective-permute-done((bf16[32,2048]{1,0:T(8,128)(2,1)S(1)}, bf16[32,2048]{1,0:T(8,128)(2,1)S(1)}, u32[]{:S(2)}, u32[]{:S(2)}) %collective-permute-start.12) | collective-permute-done | bytes 131104 | tf_op jit(solution)/shard_map/ppermute | solution.py:65
  76.7 0.5 collective-permute-start.13
  77.2 4.3 %collective-permute-done.16.refs_5_ = bf16[96,2048]{1,0:T(8,128)(2,1)S(1)} collective-permute-done((bf16[96,2048]{1,0:T(8,128)(2,1)S(1)}, bf16[96,2048]{1,0:T(8,128)(2,1)S(1)}, u32[]{:S(2)}, u32[]{:S(2)}) %collective-permute-start.16) | collective-permute-done | bytes 393248 | tf_op jit(solution)/shard_map/ppermute | solution.py:65
  81.5 3.7 %combine.2.refs_6_ = f32[256,2048]{1,0:T(8,128)S(1)} custom-call(bf16[32,2048]{1,0:T(8,128)(2,1)S(1)} %attend.2.refs_0_, bf16[32,2048]{1,0:T(8,128)(2,1)S(1)} %collective-permute-done.14.refs_1_, bf16[32,2048]{1,0:T(8,128)(2,1)S(1)} %collective-permute-done.8.refs_2_, bf16[32,2048]{1,0:T(8,128)(2,1)S(1)} %collective-permute-done.15.refs_3_, ...), custom_call_target="tpu_custom_call" | custom-call | tf_op jit(solution)/shard_map/combine/pallas_call | solution.py:400
  85.2 0.5 collective-permute-done.13.refs_5_
  85.7 3.7 %combine.3 = (bf16[128,2048]{1,0:T(8,128)(2,1)S(1)}, f32[128,2048]{1,0:T(8,128)S(1)}) custom-call(bf16[32,2048]{1,0:T(8,128)(2,1)S(1)} %attend.3.refs_0_, bf16[32,2048]{1,0:T(8,128)(2,1)S(1)} %collective-permute-done.9.refs_1_, bf16[32,2048]{1,0:T(8,128)(2,1)S(1)} %collective-permute-done.10.refs_2_, bf16[32,2048]{1,0:T(8,128)(2,1)S(1)} %collective-permute-done.12.refs_3_, ...), custom_call_target="tpu_custom_call" | custom-call | tf_op jit(solution)/shard_map/combine/pallas_call | solution.py:400
  89.4 0.1 collective-permute-start.17
  89.5 1.9 %collective-permute-done.17 = bf16[128,2048]{1,0:T(8,128)(2,1)S(1)} collective-permute-done((bf16[128,2048]{1,0:T(8,128)(2,1)S(1)}, bf16[128,2048]{1,0:T(8,128)(2,1)S(1)}, u32[]{:S(2)}, u32[]{:S(2)}) %collective-permute-start.17) | collective-permute-done | bytes 524320 | tf_op jit(solution)/shard_map/ppermute | solution.py:541
  91.4 0.9 add_convert_fusion
  (10 shorter events, 0.2 us)
Async XLA Ops:
  4.4 7.7 %collective-permute-start = (bf16[128,1152]{1,0:T(8,128)(2,1)S(1)}, bf16[128,1152]{1,0:T(8,128)(2,1)S(1)}, u32[]{:S(2)}, u32[]{:S(2)}) collective-permute-start(bf16[128,1152]{1,0:T(8,128)(2,1)S(1)} %get-tuple-element.35), channel_id=1, source_target_pairs={{0,2},{1,5},{2,0},{3,7},{4,6},{5,1},{6,4},{7,3},{8,10},{9,13},{10,... | collective-permute-start | bytes 884744 | tf_op jit(solution)/shard_map/ppermute | solution.py:65
  11.2 7.1 %collective-permute-start.1 = (bf16[128,1280]{1,0:T(8,128)(2,1)S(1)}, bf16[128,1280]{1,0:T(8,128)(2,1)S(1)}, u32[]{:S(2)}, u32[]{:S(2)}) collective-permute-start(bf16[128,1280]{1,0:T(8,128)(2,1)S(1)} %get-tuple-element.37), channel_id=1, source_target_pairs={{0,2},{1,5},{2,0},{3,7},{4,6},{5,1},{6,4},{7,3},{8,10},{9,13},{10,... | collective-permute-start | bytes 983048 | tf_op jit(solution)/shard_map/ppermute | solution.py:65
  12.1 8.0 %copy-start = (s32[8]{0:T(128)S(1)}, s32[8]{0:T(128)}, u32[]{:S(2)}) copy-start(s32[8]{0:T(128)} %length_ref.3) | copy-start | bytes 100
  18.5 7.1 %collective-permute-start.3 = (bf16[64,2432]{1,0:T(8,128)(2,1)S(1)}, bf16[64,2432]{1,0:T(8,128)(2,1)}, u32[]{:S(2)}, u32[]{:S(2)}) collective-permute-start(bf16[64,2432]{1,0:T(8,128)(2,1)S(1)} %fusion.1), channel_id=1, source_target_pairs={{0,4},{1,3},{2,6},{3,1},{4,0},{5,7},{6,2},{7,5},{8,12},{9,11},{10,... | collective-permute-start | bytes 933896 | tf_op jit(solution)/shard_map/ppermute | solution.py:65
  20.3 16.4 %collective-permute-start.2 = (bf16[128,2304]{1,0:T(8,128)(2,1)S(1)}, bf16[128,2304]{1,0:T(8,128)(2,1)S(1)}, u32[]{:S(2)}, u32[]{:S(2)}) collective-permute-start(bf16[128,2304]{1,0:T(8,128)(2,1)S(1)} %get-tuple-element.45), channel_id=1, source_target_pairs={{0,4},{1,3},{2,6},{3,1},{4,0},{5,7},{6,2},{7,5},{8,12},{9,11},{10,... | collective-permute-start | bytes 1769480 | tf_op jit(solution)/shard_map/ppermute | solution.py:65
  26.6 15.0 %collective-permute-start.5 = (bf16[32,2432]{1,0:T(8,128)(2,1)S(1)}, bf16[32,2432]{1,0:T(8,128)(2,1)S(1)}, u32[]{:S(2)}, u32[]{:S(2)}) collective-permute-start(bf16[32,2432]{1,0:T(8,128)(2,1)S(1)} %slice.64), channel_id=1, source_target_pairs={{0,8},{1,9},{2,10},{3,11},{4,12},{5,13},{6,14},{7,15},{8,0},{9,1},... | collective-permute-start | bytes 466952 | tf_op jit(solution)/shard_map/ppermute | solution.py:65
  36.8 8.3 %collective-permute-start.4 = (bf16[64,2304]{1,0:T(8,128)(2,1)S(1)}, bf16[64,2304]{1,0:T(8,128)(2,1)S(1)}, u32[]{:S(2)}, u32[]{:S(2)}) collective-permute-start(bf16[64,2304]{1,0:T(8,128)(2,1)S(1)} %slice.63), channel_id=1, source_target_pairs={{0,2},{1,5},{2,0},{3,7},{4,6},{5,1},{6,4},{7,3},{8,10},{9,13},{10,... | collective-permute-start | bytes 884744 | tf_op jit(solution)/shard_map/ppermute | solution.py:65
  45.3 10.6 %collective-permute-start.6 = (bf16[32,2304]{1,0:T(8,128)(2,1)S(1)}, bf16[32,2304]{1,0:T(8,128)(2,1)S(1)}, u32[]{:S(2)}, u32[]{:S(2)}) collective-permute-start(bf16[32,2304]{1,0:T(8,128)(2,1)S(1)} %slice.65), channel_id=1, source_target_pairs={{0,8},{1,9},{2,10},{3,11},{4,12},{5,13},{6,14},{7,15},{8,0},{9,1},... | collective-permute-start | bytes 442376 | tf_op jit(solution)/shard_map/ppermute | solution.py:65
  50.4 6.0 %collective-permute-start.7 = (bf16[32,2048]{1,0:T(8,128)(2,1)S(1)}, bf16[32,2048]{1,0:T(8,128)(2,1)S(1)}, u32[]{:S(2)}, u32[]{:S(2)}) collective-permute-start(bf16[32,2048]{1,0:T(8,128)(2,1)S(1)} %attend.2.refs_0_), channel_id=1, source_target_pairs={{0,2},{1,3},{2,0},{3,1},{4,6},{5,7},{6,4},{7,5},{8,10},{9,11},{10,... | collective-permute-start | bytes 393224 | tf_op jit(solution)/shard_map/ppermute | solution.py:65
  51.3 9.1 %collective-permute-start.8 = (bf16[32,2048]{1,0:T(8,128)(2,1)S(1)}, bf16[32,2048]{1,0:T(8,128)(2,1)S(1)}, u32[]{:S(2)}, u32[]{:S(2)}) collective-permute-start(bf16[32,2048]{1,0:T(8,128)(2,1)S(1)} %attend.2.refs_0_), channel_id=1, source_target_pairs={{0,4},{1,5},{2,6},{3,7},{4,0},{5,1},{6,2},{7,3},{8,12},{9,13},{10,... | collective-permute-start | bytes 393224 | tf_op jit(solution)/shard_map/ppermute | solution.py:65
  53.8 10.8 %collective-permute-start.14 = (bf16[32,2048]{1,0:T(8,128)(2,1)S(1)}, bf16[32,2048]{1,0:T(8,128)(2,1)S(1)}, u32[]{:S(2)}, u32[]{:S(2)}) collective-permute-start(bf16[32,2048]{1,0:T(8,128)(2,1)S(1)} %attend.2.refs_0_), channel_id=1, source_target_pairs={{0,8},{1,9},{2,10},{3,11},{4,12},{5,13},{6,14},{7,15},{8,0},{9,1},... | collective-permute-start | bytes 393224 | tf_op jit(solution)/shard_map/ppermute | solution.py:65
  63.1 6.2 %collective-permute-start.9 = (bf16[32,2048]{1,0:T(8,128)(2,1)S(1)}, bf16[32,2048]{1,0:T(8,128)(2,1)S(1)}, u32[]{:S(2)}, u32[]{:S(2)}) collective-permute-start(bf16[32,2048]{1,0:T(8,128)(2,1)S(1)} %attend.3.refs_0_), channel_id=1, source_target_pairs={{0,8},{1,9},{2,10},{3,11},{4,12},{5,13},{6,14},{7,15},{8,0},{9,1},... | collective-permute-start | bytes 393224 | tf_op jit(solution)/shard_map/ppermute | solution.py:65
  63.2 7.6 %collective-permute-start.10 = (bf16[32,2048]{1,0:T(8,128)(2,1)S(1)}, bf16[32,2048]{1,0:T(8,128)(2,1)S(1)}, u32[]{:S(2)}, u32[]{:S(2)}) collective-permute-start(bf16[32,2048]{1,0:T(8,128)(2,1)S(1)} %attend.3.refs_0_), channel_id=1, source_target_pairs={{0,4},{1,3},{2,6},{3,1},{4,0},{5,7},{6,2},{7,5},{8,12},{9,11},{10,... | collective-permute-start | bytes 393224 | tf_op jit(solution)/shard_map/ppermute | solution.py:65
  64.5 6.2 %collective-permute-start.11 = (bf16[32,2048]{1,0:T(8,128)(2,1)S(1)}, bf16[32,2048]{1,0:T(8,128)(2,1)S(1)}, u32[]{:S(2)}, u32[]{:S(2)}) collective-permute-start(bf16[32,2048]{1,0:T(8,128)(2,1)S(1)} %attend.3.refs_0_), channel_id=1, source_target_pairs={{0,2},{1,5},{2,0},{3,7},{4,6},{5,1},{6,4},{7,3},{8,10},{9,13},{10,... | collective-permute-start | bytes 393224 | tf_op jit(solution)/shard_map/ppermute | solution.py:65
  64.5 9.0 %collective-permute-start.15 = (bf16[32,2048]{1,0:T(8,128)(2,1)S(1)}, bf16[32,2048]{1,0:T(8,128)(2,1)S(1)}, u32[]{:S(2)}, u32[]{:S(2)}) collective-permute-start(bf16[32,2048]{1,0:T(8,128)(2,1)S(1)} %collective-permute-done.14.refs_1_), channel_id=1, source_target_pairs={{0,4},{1,5},{2,6},{3,7},{4,0},{5,1},{6,2},{7,3},{8,12},{9,13},{10,... | collective-permute-start | bytes 393224 | tf_op jit(solution)/shard_map/ppermute | solution.py:65
  70.8 5.9 %collective-permute-start.12 = (bf16[32,2048]{1,0:T(8,128)(2,1)S(1)}, bf16[32,2048]{1,0:T(8,128)(2,1)S(1)}, u32[]{:S(2)}, u32[]{:S(2)}) collective-permute-start(bf16[32,2048]{1,0:T(8,128)(2,1)S(1)} %collective-permute-done.9.refs_1_), channel_id=1, source_target_pairs={{0,4},{1,3},{2,6},{3,1},{4,0},{5,7},{6,2},{7,5},{8,12},{9,11},{10,... | collective-permute-start | bytes 393224 | tf_op jit(solution)/shard_map/ppermute | solution.py:65
  73.6 7.8 %collective-permute-start.16 = (bf16[96,2048]{1,0:T(8,128)(2,1)S(1)}, bf16[96,2048]{1,0:T(8,128)(2,1)S(1)}, u32[]{:S(2)}, u32[]{:S(2)}) collective-permute-start(bf16[96,2048]{1,0:T(8,128)(2,1)S(1)} %pad_maximum_fusion.2), channel_id=1, source_target_pairs={{0,2},{1,3},{2,0},{3,1},{4,6},{5,7},{6,4},{7,5},{8,10},{9,11},{10,... | collective-permute-start | bytes 1179656 | tf_op jit(solution)/shard_map/ppermute | solution.py:65
  76.7 9.0 %collective-permute-start.13 = (bf16[96,2048]{1,0:T(8,128)(2,1)S(1)}, bf16[96,2048]{1,0:T(8,128)(2,1)S(1)}, u32[]{:S(2)}, u32[]{:S(2)}) collective-permute-start(bf16[96,2048]{1,0:T(8,128)(2,1)S(1)} %pad_maximum_fusion.1), channel_id=1, source_target_pairs={{0,2},{1,5},{2,0},{3,7},{4,6},{5,1},{6,4},{7,3},{8,10},{9,13},{10,... | collective-permute-start | bytes 1179656 | tf_op jit(solution)/shard_map/ppermute | solution.py:65
  89.4 2.0 %collective-permute-start.17 = (bf16[128,2048]{1,0:T(8,128)(2,1)S(1)}, bf16[128,2048]{1,0:T(8,128)(2,1)S(1)}, u32[]{:S(2)}, u32[]{:S(2)}) collective-permute-start(bf16[128,2048]{1,0:T(8,128)(2,1)S(1)} %get-tuple-element.62), channel_id=1, source_target_pairs={{0,1},{1,0},{2,3},{3,2},{4,5},{5,4},{6,7},{7,6},{8,9},{9,8},{10,11... | collective-permute-start | bytes 1572872 | tf_op jit(solution)/shard_map/ppermute | solution.py:541

commit v6 on v4

--- a/solution.py
+++ b/solution.py
@@ -30,7 +30,7 @@
 
 def gather_orders(n, chunk):
     first, second = bit_orders(n)
-    return (first, first) if chunk else (first, second)
+    return (first, second) if chunk else (first, first)
 
 
 def slot_shift(slot, order):
@@ -451,54 +451,54 @@
 
     lead, follow = flows
     w_rows = w_out.shape[0] // CHUNKS
-    source = after(w_out, lead[2], follow[2])
-    weights = [fetch_rows(source, chunk * w_rows, w_rows) for chunk in range(CHUNKS)]
-    stage = 0
+    weights = [fetch_rows(after(w_out, lead[2], follow[2]), 0, w_rows)]
     while follow[0] < levels:
         pending = [start(flow) for flow in flows if flow[0] < levels]
         if lead[0] == levels:
             finish(follow, pending[0])
         elif lead[0] == levels - 1:
-            finish(lead, pending[0])
+            cache_keys, cache_values = fetch(*after((cache_keys, cache_values), follow[2]))
+            finish(lead, pending[0], cache_keys, cache_values)
             finish(follow, pending[1], lead[1])
         else:
             finish(lead, pending[0], *weights)
-            between = [lead[2]]
-            if stage == 0:
-                cache_keys, cache_values = fetch(*after((cache_keys, cache_values), lead[2]))
-                between += [cache_keys, cache_values]
-            finish(follow, pending[1], *between)
-        stage += 1
+            finish(follow, pending[1], lead[2])
     sums = [flow[1] for flow in flows]
     squares = sums[0][:, share : share + 128]
     plain = [h * HD for h in range(q_cols // HD)]
     offsets = [[at if at < share else at + 128 for at in plain], plain]
     kv_offsets = [q_cols + 128, q_cols]
 
+    attentions = []
+    for chunk in range(CHUNKS):
+        attentions.append(
+            attend(
+                chunk,
+                offsets[chunk],
+                kv_offsets[chunk],
+                sums[chunk],
+                squares,
+                cosine,
+                sine,
+                cache_keys,
+                cache_values,
+                cache_lengths,
+            )
+        )
+    weights.append(fetch_rows(after(w_out, attentions[1]), w_rows, w_rows))
     gathered = []
     for chunk in range(CHUNKS):
-        attention = attend(
-            chunk,
-            offsets[chunk],
-            kv_offsets[chunk],
-            sums[chunk],
-            squares,
-            cosine,
-            sine,
-            cache_keys,
-            cache_values,
-            cache_lengths,
-        )
-        slots = [attention]
+        slots = [attentions[chunk]]
         for slot in range(1, n):
             top = slot.bit_length() - 1
-            slots.append(exchange(
-                    slots[slot - (1 << top)],
-                    n,
-                    cores,
-                    levels - 1 - top,
-                    gather_orders(n, chunk),
-                ))
+            source = slots[slot - (1 << top)]
+            if slot == 1 and chunk == 0:
+                source = after(source, sums[1])
+            if slot == 3 and chunk == 1:
+                source = after(source, weights[1])
+            slots.append(
+                exchange(source, n, cores, levels - 1 - top, gather_orders(n, chunk))
+            )
         gathered.append(slots)
     result = None
     for chunk in range(CHUNKS):

time: 84.8 us -> 83.1 us (0.980)
  waiting for transfers between devices: 18.1 us -> 14.8 us
  starting transfers between devices: 26.2 us -> 27.8 us
    ppermute x21, waiting for transfers between devices: 16.2 us -> 12.9 us  [exchange(): return lax.ppermute(value, ('gx', 'gy'), pairs)]
    ppermute x21, starting transfers between devices: 26.1 us -> 27.7 us  [exchange(): return lax.ppermute(value, ('gx', 'gy'), pairs)]
  transfers between devices with their start and end apart: 22 -> 22, of which waited for: 13 -> 10; matrix products, arithmetic and copies ran while one was open for 2% -> 2% of each run, Pallas kernels for 35% -> 35%
where the time goes in v6:
time: 83.1 us; the launch traced here: 82.9 us
  Pallas kernels  37.4 us (45%)
  starting transfers between devices  27.8 us (33%)
  waiting for transfers between devices  14.8 us (18%)
  other arithmetic  2.61 us (3%)
    ppermute x21, starting transfers between devices, exchange(): return lax.ppermute(value, ('gx', 'gy'), pairs)  27.7 us
    pallas_call x3, Pallas kernels, project(): pl.pallas_call(functools.partial(project_kernel, n, q_start, kv_start, fi...  13.8 us
    ppermute x21, waiting for transfers between devices, exchange(): return lax.ppermute(value, ('gx', 'gy'), pairs)  12.9 us
    pallas_call x2, Pallas kernels, combine(): pl.pallas_call(functools.partial(combine_kernel, n, block, chunk), out_sh...  7.55 us
    pallas_call x2, Pallas kernels, fetch_rows(): pl.pallas_call(functools.partial(fetch_rows_kernel, start, pieces), out_s...  7 us
    pallas_call x2, Pallas kernels, attend(): pl.pallas_call(functools.partial(attend_kernel, chunk, offsets, kv_offset...  5.62 us
    pallas_call x1, Pallas kernels, fetch(): pl.pallas_call(functools.partial(fetch_kernel, len(arrays), pieces), out_...  3.47 us
    ppermute x1, waiting for transfers between devices, shards(): other = lax.ppermute(send, 'gy', [(0, 1), (1, 0)])  1.9 us
  transfers between devices with their start and end apart: 22, of which 10 were waited for; matrix products, arithmetic and copies ran while one was open for 2% of the time, Pallas kernels for 35%

profile of v6, /device:TPU:0, one launch (start us, length us, event | category | flops | bytes accessed | tf_op | source)
XLA Modules:
  0.0 82.9 jit_solution(2657549579790752419)
XLA Ops:
  0.0 4.4 %project.3 = (bf16[128,1152]{1,0:T(8,128)(2,1)S(1)}, f32[128,1152]{1,0:T(8,128)S(1)}, bf16[256,2048]{1,0:T(8,128)(2,1)S(1)}) custom-call(bf16[256,2048]{1,0:T(8,128)(2,1)} %refs_0_.1, f32[1,2048]{1,0:T(1,128)} %bitcast.1, bf16[2048,4096]{1,0:T(8,128)(2,1)} %refs_1_.3, bf16[2048,256]{1,0:T(8,128)(2,1)} %refs_2_.5, bf16[2048,256]{1,0:T(8,128)(2,1)} %refs_3_.5), custom_call_target="tpu_custom_call" | custom-call | tf_op jit(solution)/shard_map/project/pallas_call | solution.py:159
  4.4 3.0 %collective-permute-start = (bf16[128,1152]{1,0:T(8,128)(2,1)S(1)}, bf16[128,1152]{1,0:T(8,128)(2,1)S(1)}, u32[]{:S(2)}, u32[]{:S(2)}) collective-permute-start(bf16[128,1152]{1,0:T(8,128)(2,1)S(1)} %get-tuple-element.32), channel_id=1, source_target_pairs={{0,2},{1,5},{2,0},{3,7},{4,6},{5,1},{6,4},{7,3},{8,10},{9,13},{10,... | collective-permute-start | bytes 884744 | tf_op jit(solution)/shard_map/ppermute | solution.py:55
  7.4 3.9 %project.4 = (bf16[128,1280]{1,0:T(8,128)(2,1)S(1)}, f32[128,1280]{1,0:T(8,128)S(1)}) custom-call(bf16[256,2048]{1,0:T(8,128)(2,1)S(1)} %get-tuple-element.37.refs_0_, bf16[2048,4096]{1,0:T(8,128)(2,1)} %refs_1_.3, bf16[2048,256]{1,0:T(8,128)(2,1)} %refs_2_.5, bf16[2048,256]{1,0:T(8,128)(2,1)} %refs_3_.5), custom_call_target="tpu_custom_call" | custom-call | tf_op jit(solution)/shard_map/project/pallas_call | solution.py:159
  11.3 0.1 collective-permute-start.1
  11.4 0.8 collective-permute-done
  12.1 0.1 convert_add_fusion.2
  12.2 0.0 copy-start
  12.2 5.5 %project.5 = (bf16[128,2304]{1,0:T(8,128)(2,1)S(1)}, f32[128,2304]{1,0:T(8,128)S(1)}) custom-call(bf16[256,2048]{1,0:T(8,128)(2,1)S(1)} %get-tuple-element.37.refs_0_, bf16[2048,4096]{1,0:T(8,128)(2,1)} %refs_1_.3, bf16[2048,256]{1,0:T(8,128)(2,1)} %refs_2_.5, bf16[2048,256]{1,0:T(8,128)(2,1)} %refs_3_.5), custom_call_target="tpu_custom_call" | custom-call | tf_op jit(solution)/shard_map/project/pallas_call | solution.py:159
  17.7 0.7 collective-permute-done.1
  18.4 0.1 convert_add_fusion.1
  18.5 1.6 %collective-permute-start.3 = (bf16[64,2432]{1,0:T(8,128)(2,1)S(1)}, bf16[64,2432]{1,0:T(8,128)(2,1)}, u32[]{:S(2)}, u32[]{:S(2)}) collective-permute-start(bf16[64,2432]{1,0:T(8,128)(2,1)S(1)} %fusion.1), channel_id=1, source_target_pairs={{0,4},{1,3},{2,6},{3,1},{4,0},{5,7},{6,2},{7,5},{8,12},{9,11},{10,... | collective-permute-start | bytes 933896 | tf_op jit(solution)/shard_map/ppermute | solution.py:55
  20.2 0.1 add_convert_fusion.1
  20.2 0.1 convert_element_type.49
  20.3 1.4 %collective-permute-start.2 = (bf16[128,2304]{1,0:T(8,128)(2,1)S(1)}, bf16[128,2304]{1,0:T(8,128)(2,1)S(1)}, u32[]{:S(2)}, u32[]{:S(2)}) collective-permute-start(bf16[128,2304]{1,0:T(8,128)(2,1)S(1)} %get-tuple-element.42), channel_id=1, source_target_pairs={{0,2},{1,5},{2,0},{3,7},{4,6},{5,1},{6,4},{7,3},{8,10},{9,13},{10,... | collective-permute-start | bytes 1769480 | tf_op jit(solution)/shard_map/ppermute | solution.py:55
  21.7 3.5 %fetch_rows.2.refs_8_ = bf16[2048,2048]{1,0:T(8,128)(2,1)S(1)} custom-call(bf16[4096,2048]{1,0:T(8,128)(2,1)} %source.1), custom_call_target="tpu_custom_call" | custom-call | tf_op jit(solution)/shard_map/fetch_rows/pallas_call | solution.py:320
  25.2 5.3 %collective-permute-done.3 = bf16[64,2432]{1,0:T(8,128)(2,1)} collective-permute-done((bf16[64,2432]{1,0:T(8,128)(2,1)S(1)}, bf16[64,2432]{1,0:T(8,128)(2,1)}, u32[]{:S(2)}, u32[]{:S(2)}) %collective-permute-start.3) | collective-permute-done | bytes 311328 | tf_op jit(solution)/shard_map/ppermute | solution.py:55
  30.5 1.0 %fusion.2 = f32[64,2432]{1,0:T(8,128)S(1)} fusion(f32[128,1280]{1,0:T(8,128)S(1)} %convert_add_fusion.1, f32[128,1152]{1,0:T(8,128)S(1)} %convert_add_fusion.2, bf16[64,2432]{1,0:T(8,128)(2,1)} %collective-permute-done.3), kind=kLoop, calls=%fused_computation.8 | loop fusion | flops 466944 | bytes 2179072 | tf_op jit(solution)/shard_map/add | solution.py:448
  31.6 1.0 %collective-permute-start.5 = (bf16[32,2432]{1,0:T(8,128)(2,1)S(1)}, bf16[32,2432]{1,0:T(8,128)(2,1)S(1)}, u32[]{:S(2)}, u32[]{:S(2)}) collective-permute-start(bf16[32,2432]{1,0:T(8,128)(2,1)S(1)} %slice.64), channel_id=1, source_target_pairs={{0,8},{1,9},{2,10},{3,11},{4,12},{5,13},{6,14},{7,15},{8,0},{9,1},... | collective-permute-start | bytes 466952 | tf_op jit(solution)/shard_map/ppermute | solution.py:55
  32.6 0.0 collective-permute-done.2
  32.6 0.1 convert_add_fusion
  32.8 3.3 %collective-permute-start.4 = (bf16[64,2304]{1,0:T(8,128)(2,1)S(1)}, bf16[64,2304]{1,0:T(8,128)(2,1)S(1)}, u32[]{:S(2)}, u32[]{:S(2)}) collective-permute-start(bf16[64,2304]{1,0:T(8,128)(2,1)S(1)} %slice.63), channel_id=1, source_target_pairs={{0,4},{1,3},{2,6},{3,1},{4,0},{5,7},{6,2},{7,5},{8,12},{9,11},{10,... | collective-permute-start | bytes 884744 | tf_op jit(solution)/shard_map/ppermute | solution.py:55
  36.1 3.5 %fetch.1 = (bf16[8,1024,256]{2,1,0:T(8,128)(2,1)S(1)}, bf16[8,1024,256]{2,1,0:T(8,128)(2,1)S(1)}) custom-call(bf16[8,1024,256]{2,1,0:T(8,128)(2,1)} %refs_0_.2, bf16[8,1024,256]{2,1,0:T(8,128)(2,1)} %refs_1_.4), custom_call_target="tpu_custom_call" | custom-call | tf_op jit(solution)/shard_map/fetch/pallas_call | solution.py:291
  39.5 0.0 collective-permute-done.5
  39.6 2.0 %collective-permute-done.4 = bf16[64,2304]{1,0:T(8,128)(2,1)S(1)} collective-permute-done((bf16[64,2304]{1,0:T(8,128)(2,1)S(1)}, bf16[64,2304]{1,0:T(8,128)(2,1)S(1)}, u32[]{:S(2)}, u32[]{:S(2)}) %collective-permute-start.4) | collective-permute-done | bytes 294944 | tf_op jit(solution)/shard_map/ppermute | solution.py:55
  41.7 0.1 slice_add_fusion
  41.7 0.7 collective-permute-start.6
  42.4 0.1 fusion.3
  42.5 0.1 pad_maximum_fusion.1
  42.6 2.9 %attend.3.refs_0_ = bf16[32,2048]{1,0:T(8,128)(2,1)S(1)} custom-call(s32[8]{0:T(128)S(1)} %copy-done, f32[32,2432]{1,0:T(8,128)S(1)} %slice_add_fusion.1.refs_0_, f32[32,128]{1,0:T(8,128)S(1)} %slice.48.refs_1_, f32[32,128]{1,0:T(8,128)S(1)} %get-tuple-element.60.refs_2_, f32[32,128]{1,0:T(8,128)S(1)} %get-tuple-element.61.refs_3_, ...), custom_call_target="tpu_custom_call" | custom-call | tf_op jit(solution)/shard_map/attend/pallas_call | solution.py:259
  45.5 2.3 %collective-permute-start.15 = (bf16[32,2048]{1,0:T(8,128)(2,1)S(1)}, bf16[32,2048]{1,0:T(8,128)(2,1)S(1)}, u32[]{:S(2)}, u32[]{:S(2)}) collective-permute-start(bf16[32,2048]{1,0:T(8,128)(2,1)S(1)} %attend.3.refs_0_), channel_id=1, source_target_pairs={{0,4},{1,5},{2,6},{3,7},{4,0},{5,1},{6,2},{7,3},{8,12},{9,13},{10,... | collective-permute-start | bytes 393224 | tf_op jit(solution)/shard_map/ppermute | solution.py:55
  47.8 1.0 %collective-permute-done.6 = bf16[32,2304]{1,0:T(8,128)(2,1)S(1)} collective-permute-done((bf16[32,2304]{1,0:T(8,128)(2,1)S(1)}, bf16[32,2304]{1,0:T(8,128)(2,1)S(1)}, u32[]{:S(2)}, u32[]{:S(2)}) %collective-permute-start.6) | collective-permute-done | bytes 147488 | tf_op jit(solution)/shard_map/ppermute | solution.py:55
  48.9 0.3 collective-permute-start.14
  49.2 2.7 %attend.2.refs_0_ = bf16[32,2048]{1,0:T(8,128)(2,1)S(1)} custom-call(s32[8]{0:T(128)S(1)} %copy-done, f32[32,2304]{1,0:T(8,128)S(1)} %slice_add_fusion.2.refs_0_, f32[32,128]{1,0:T(8,128)S(1)} %slice.48.refs_1_, f32[32,128]{1,0:T(8,128)S(1)} %get-tuple-element.60.refs_2_, f32[32,128]{1,0:T(8,128)S(1)} %get-tuple-element.61.refs_3_, ...), custom_call_target="tpu_custom_call" | custom-call | tf_op jit(solution)/shard_map/attend/pallas_call | solution.py:259
  51.9 2.8 %collective-permute-start.7 = (bf16[32,2048]{1,0:T(8,128)(2,1)S(1)}, bf16[32,2048]{1,0:T(8,128)(2,1)S(1)}, u32[]{:S(2)}, u32[]{:S(2)}) collective-permute-start(bf16[32,2048]{1,0:T(8,128)(2,1)S(1)} %attend.2.refs_0_), channel_id=1, source_target_pairs={{0,8},{1,9},{2,10},{3,11},{4,12},{5,13},{6,14},{7,15},{8,0},{9,1},... | collective-permute-start | bytes 393224 | tf_op jit(solution)/shard_map/ppermute | solution.py:55
  54.7 1.4 %collective-permute-start.17 = (bf16[32,2048]{1,0:T(8,128)(2,1)S(1)}, bf16[32,2048]{1,0:T(8,128)(2,1)S(1)}, u32[]{:S(2)}, u32[]{:S(2)}) collective-permute-start(bf16[32,2048]{1,0:T(8,128)(2,1)S(1)} %attend.3.refs_0_), channel_id=1, source_target_pairs={{0,2},{1,3},{2,0},{3,1},{4,6},{5,7},{6,4},{7,5},{8,10},{9,11},{10,... | collective-permute-start | bytes 393224 | tf_op jit(solution)/shard_map/ppermute | solution.py:55
  56.1 0.0 collective-permute-done.15.refs_2_
  56.1 0.6 collective-permute-start.19
  56.7 1.5 %collective-permute-start.8 = (bf16[32,2048]{1,0:T(8,128)(2,1)S(1)}, bf16[32,2048]{1,0:T(8,128)(2,1)S(1)}, u32[]{:S(2)}, u32[]{:S(2)}) collective-permute-start(bf16[32,2048]{1,0:T(8,128)(2,1)S(1)} %attend.2.refs_0_), channel_id=1, source_target_pairs={{0,4},{1,3},{2,6},{3,1},{4,0},{5,7},{6,2},{7,5},{8,12},{9,11},{10,... | collective-permute-start | bytes 393224 | tf_op jit(solution)/shard_map/ppermute | solution.py:55
  58.2 3.5 %fetch_rows.3.refs_9_ = bf16[2048,2048]{1,0:T(8,128)(2,1)S(1)} custom-call(bf16[4096,2048]{1,0:T(8,128)(2,1)} %source.1), custom_call_target="tpu_custom_call" | custom-call | tf_op jit(solution)/shard_map/fetch_rows/pallas_call | solution.py:320
  61.7 0.0 collective-permute-done.14.refs_1_
  61.7 0.6 collective-permute-start.16
  62.3 0.0 collective-permute-done.7.refs_1_
  62.3 1.4 %collective-permute-start.18 = (bf16[32,2048]{1,0:T(8,128)(2,1)S(1)}, bf16[32,2048]{1,0:T(8,128)(2,1)S(1)}, u32[]{:S(2)}, u32[]{:S(2)}) collective-permute-start(bf16[32,2048]{1,0:T(8,128)(2,1)S(1)} %collective-permute-done.14.refs_1_), channel_id=1, source_target_pairs={{0,2},{1,3},{2,0},{3,1},{4,6},{5,7},{6,4},{7,5},{8,10},{9,11},{10,... | collective-permute-start | bytes 393224 | tf_op jit(solution)/shard_map/ppermute | solution.py:55
  63.7 0.0 collective-permute-done.17.refs_4_
  63.7 0.2 collective-permute-start.9
  63.9 0.0 collective-permute-done.19.refs_6_
  63.9 2.0 %collective-permute-start.10 = (bf16[32,2048]{1,0:T(8,128)(2,1)S(1)}, bf16[32,2048]{1,0:T(8,128)(2,1)S(1)}, u32[]{:S(2)}, u32[]{:S(2)}) collective-permute-start(bf16[32,2048]{1,0:T(8,128)(2,1)S(1)} %attend.2.refs_0_), channel_id=1, source_target_pairs={{0,2},{1,5},{2,0},{3,7},{4,6},{5,1},{6,4},{7,3},{8,10},{9,13},{10,... | collective-permute-start | bytes 393224 | tf_op jit(solution)/shard_map/ppermute | solution.py:55
  65.8 1.2 %collective-permute-done.16.refs_3_ = bf16[32,2048]{1,0:T(8,128)(2,1)S(1)} collective-permute-done((bf16[32,2048]{1,0:T(8,128)(2,1)S(1)}, bf16[32,2048]{1,0:T(8,128)(2,1)S(1)}, u32[]{:S(2)}, u32[]{:S(2)}) %collective-permute-start.16) | collective-permute-done | bytes 131104 | tf_op jit(solution)/shard_map/ppermute | solution.py:55
  67.0 0.1 collective-permute-start.20
  67.2 0.0 collective-permute-done.8.refs_2_
  67.2 1.9 %collective-permute-start.11 = (bf16[32,2048]{1,0:T(8,128)(2,1)S(1)}, bf16[32,2048]{1,0:T(8,128)(2,1)S(1)}, u32[]{:S(2)}, u32[]{:S(2)}) collective-permute-start(bf16[32,2048]{1,0:T(8,128)(2,1)S(1)} %collective-permute-done.7.refs_1_), channel_id=1, source_target_pairs={{0,2},{1,5},{2,0},{3,7},{4,6},{5,1},{6,4},{7,3},{8,10},{9,13},{10,... | collective-permute-start | bytes 393224 | tf_op jit(solution)/shard_map/ppermute | solution.py:55
  69.1 0.0 collective-permute-done.18.refs_5_
  69.1 0.4 collective-permute-start.12
  69.5 0.5 collective-permute-done.9.refs_3_
  70.0 1.1 %collective-permute-start.13 = (bf16[32,2048]{1,0:T(8,128)(2,1)S(1)}, bf16[32,2048]{1,0:T(8,128)(2,1)S(1)}, u32[]{:S(2)}, u32[]{:S(2)}) collective-permute-start(bf16[32,2048]{1,0:T(8,128)(2,1)S(1)} %collective-permute-done.9.refs_3_), channel_id=1, source_target_pairs={{0,2},{1,5},{2,0},{3,7},{4,6},{5,1},{6,4},{7,3},{8,10},{9,13},{10,... | collective-permute-start | bytes 393224 | tf_op jit(solution)/shard_map/ppermute | solution.py:55
  71.1 0.9 %collective-permute-done.20.refs_7_ = bf16[32,2048]{1,0:T(8,128)(2,1)S(1)} collective-permute-done((bf16[32,2048]{1,0:T(8,128)(2,1)S(1)}, bf16[32,2048]{1,0:T(8,128)(2,1)S(1)}, u32[]{:S(2)}, u32[]{:S(2)}) %collective-permute-start.20) | collective-permute-done | bytes 131104 | tf_op jit(solution)/shard_map/ppermute | solution.py:55
  72.0 3.7 %combine.2.refs_8_ = f32[256,2048]{1,0:T(8,128)S(1)} custom-call(bf16[32,2048]{1,0:T(8,128)(2,1)S(1)} %attend.3.refs_0_, bf16[32,2048]{1,0:T(8,128)(2,1)S(1)} %collective-permute-done.14.refs_1_, bf16[32,2048]{1,0:T(8,128)(2,1)S(1)} %collective-permute-done.15.refs_2_, bf16[32,2048]{1,0:T(8,128)(2,1)S(1)} %collective-permute-done.16.refs_3_, ...), custom_call_target="tpu_custom_call" | custom-call | tf_op jit(solution)/shard_map/combine/pallas_call | solution.py:379
  75.8 0.0 collective-permute-done.10.refs_4_
  75.8 0.0 collective-permute-done.12.refs_6_
  75.8 0.4 collective-permute-done.13.refs_7_
  76.2 3.8 %combine.3 = (bf16[128,2048]{1,0:T(8,128)(2,1)S(1)}, f32[128,2048]{1,0:T(8,128)S(1)}) custom-call(bf16[32,2048]{1,0:T(8,128)(2,1)S(1)} %attend.2.refs_0_, bf16[32,2048]{1,0:T(8,128)(2,1)S(1)} %collective-permute-done.7.refs_1_, bf16[32,2048]{1,0:T(8,128)(2,1)S(1)} %collective-permute-done.8.refs_2_, bf16[32,2048]{1,0:T(8,128)(2,1)S(1)} %collective-permute-done.9.refs_3_, ...), custom_call_target="tpu_custom_call" | custom-call | tf_op jit(solution)/shard_map/combine/pallas_call | solution.py:379
  80.0 0.1 collective-permute-start.21
  80.1 1.9 %collective-permute-done.21 = bf16[128,2048]{1,0:T(8,128)(2,1)S(1)} collective-permute-done((bf16[128,2048]{1,0:T(8,128)(2,1)S(1)}, bf16[128,2048]{1,0:T(8,128)(2,1)S(1)}, u32[]{:S(2)}, u32[]{:S(2)}) %collective-permute-start.21) | collective-permute-done | bytes 524320 | tf_op jit(solution)/shard_map/ppermute | solution.py:507
  82.0 0.9 %add_convert_fusion = bf16[128,2048]{1,0:T(8,128)(2,1)} fusion(f32[128,2048]{1,0:T(8,128)S(1)} %get-tuple-element.55, bf16[128,2048]{1,0:T(8,128)(2,1)S(1)} %collective-permute-done.21), kind=kLoop, calls=%fused_computation.3 | loop fusion | flops 786432 | bytes 2097152 | tf_op jit(solution)/shard_map/convert_element_type | solution.py:508
  (10 shorter events, 0.2 us)
Async XLA Ops:
  4.4 7.7 %collective-permute-start = (bf16[128,1152]{1,0:T(8,128)(2,1)S(1)}, bf16[128,1152]{1,0:T(8,128)(2,1)S(1)}, u32[]{:S(2)}, u32[]{:S(2)}) collective-permute-start(bf16[128,1152]{1,0:T(8,128)(2,1)S(1)} %get-tuple-element.32), channel_id=1, source_target_pairs={{0,2},{1,5},{2,0},{3,7},{4,6},{5,1},{6,4},{7,3},{8,10},{9,13},{10,... | collective-permute-start | bytes 884744 | tf_op jit(solution)/shard_map/ppermute | solution.py:55
  11.3 7.1 %collective-permute-start.1 = (bf16[128,1280]{1,0:T(8,128)(2,1)S(1)}, bf16[128,1280]{1,0:T(8,128)(2,1)S(1)}, u32[]{:S(2)}, u32[]{:S(2)}) collective-permute-start(bf16[128,1280]{1,0:T(8,128)(2,1)S(1)} %get-tuple-element.34), channel_id=1, source_target_pairs={{0,2},{1,5},{2,0},{3,7},{4,6},{5,1},{6,4},{7,3},{8,10},{9,13},{10,... | collective-permute-start | bytes 983048 | tf_op jit(solution)/shard_map/ppermute | solution.py:55
  12.2 8.0 %copy-start = (s32[8]{0:T(128)S(1)}, s32[8]{0:T(128)}, u32[]{:S(2)}) copy-start(s32[8]{0:T(128)} %length_ref.3) | copy-start | bytes 100
  18.5 12.0 %collective-permute-start.3 = (bf16[64,2432]{1,0:T(8,128)(2,1)S(1)}, bf16[64,2432]{1,0:T(8,128)(2,1)}, u32[]{:S(2)}, u32[]{:S(2)}) collective-permute-start(bf16[64,2432]{1,0:T(8,128)(2,1)S(1)} %fusion.1), channel_id=1, source_target_pairs={{0,4},{1,3},{2,6},{3,1},{4,0},{5,7},{6,2},{7,5},{8,12},{9,11},{10,... | collective-permute-start | bytes 933896 | tf_op jit(solution)/shard_map/ppermute | solution.py:55
  20.3 12.3 %collective-permute-start.2 = (bf16[128,2304]{1,0:T(8,128)(2,1)S(1)}, bf16[128,2304]{1,0:T(8,128)(2,1)S(1)}, u32[]{:S(2)}, u32[]{:S(2)}) collective-permute-start(bf16[128,2304]{1,0:T(8,128)(2,1)S(1)} %get-tuple-element.42), channel_id=1, source_target_pairs={{0,2},{1,5},{2,0},{3,7},{4,6},{5,1},{6,4},{7,3},{8,10},{9,13},{10,... | collective-permute-start | bytes 1769480 | tf_op jit(solution)/shard_map/ppermute | solution.py:55
  31.6 8.0 %collective-permute-start.5 = (bf16[32,2432]{1,0:T(8,128)(2,1)S(1)}, bf16[32,2432]{1,0:T(8,128)(2,1)S(1)}, u32[]{:S(2)}, u32[]{:S(2)}) collective-permute-start(bf16[32,2432]{1,0:T(8,128)(2,1)S(1)} %slice.64), channel_id=1, source_target_pairs={{0,8},{1,9},{2,10},{3,11},{4,12},{5,13},{6,14},{7,15},{8,0},{9,1},... | collective-permute-start | bytes 466952 | tf_op jit(solution)/shard_map/ppermute | solution.py:55
  32.8 8.9 %collective-permute-start.4 = (bf16[64,2304]{1,0:T(8,128)(2,1)S(1)}, bf16[64,2304]{1,0:T(8,128)(2,1)S(1)}, u32[]{:S(2)}, u32[]{:S(2)}) collective-permute-start(bf16[64,2304]{1,0:T(8,128)(2,1)S(1)} %slice.63), channel_id=1, source_target_pairs={{0,4},{1,3},{2,6},{3,1},{4,0},{5,7},{6,2},{7,5},{8,12},{9,11},{10,... | collective-permute-start | bytes 884744 | tf_op jit(solution)/shard_map/ppermute | solution.py:55
  41.7 7.1 %collective-permute-start.6 = (bf16[32,2304]{1,0:T(8,128)(2,1)S(1)}, bf16[32,2304]{1,0:T(8,128)(2,1)S(1)}, u32[]{:S(2)}, u32[]{:S(2)}) collective-permute-start(bf16[32,2304]{1,0:T(8,128)(2,1)S(1)} %slice.65), channel_id=1, source_target_pairs={{0,8},{1,9},{2,10},{3,11},{4,12},{5,13},{6,14},{7,15},{8,0},{9,1},... | collective-permute-start | bytes 442376 | tf_op jit(solution)/shard_map/ppermute | solution.py:55
  45.5 10.5 %collective-permute-start.15 = (bf16[32,2048]{1,0:T(8,128)(2,1)S(1)}, bf16[32,2048]{1,0:T(8,128)(2,1)S(1)}, u32[]{:S(2)}, u32[]{:S(2)}) collective-permute-start(bf16[32,2048]{1,0:T(8,128)(2,1)S(1)} %attend.3.refs_0_), channel_id=1, source_target_pairs={{0,4},{1,5},{2,6},{3,7},{4,0},{5,1},{6,2},{7,3},{8,12},{9,13},{10,... | collective-permute-start | bytes 393224 | tf_op jit(solution)/shard_map/ppermute | solution.py:55
  48.9 12.8 %collective-permute-start.14 = (bf16[32,2048]{1,0:T(8,128)(2,1)S(1)}, bf16[32,2048]{1,0:T(8,128)(2,1)S(1)}, u32[]{:S(2)}, u32[]{:S(2)}) collective-permute-start(bf16[32,2048]{1,0:T(8,128)(2,1)S(1)} %attend.3.refs_0_), channel_id=1, source_target_pairs={{0,8},{1,9},{2,10},{3,11},{4,12},{5,13},{6,14},{7,15},{8,0},{9,1},... | collective-permute-start | bytes 393224 | tf_op jit(solution)/shard_map/ppermute | solution.py:55
  51.9 10.4 %collective-permute-start.7 = (bf16[32,2048]{1,0:T(8,128)(2,1)S(1)}, bf16[32,2048]{1,0:T(8,128)(2,1)S(1)}, u32[]{:S(2)}, u32[]{:S(2)}) collective-permute-start(bf16[32,2048]{1,0:T(8,128)(2,1)S(1)} %attend.2.refs_0_), channel_id=1, source_target_pairs={{0,8},{1,9},{2,10},{3,11},{4,12},{5,13},{6,14},{7,15},{8,0},{9,1},... | collective-permute-start | bytes 393224 | tf_op jit(solution)/shard_map/ppermute | solution.py:55
  54.7 9.0 %collective-permute-start.17 = (bf16[32,2048]{1,0:T(8,128)(2,1)S(1)}, bf16[32,2048]{1,0:T(8,128)(2,1)S(1)}, u32[]{:S(2)}, u32[]{:S(2)}) collective-permute-start(bf16[32,2048]{1,0:T(8,128)(2,1)S(1)} %attend.3.refs_0_), channel_id=1, source_target_pairs={{0,2},{1,3},{2,0},{3,1},{4,6},{5,7},{6,4},{7,5},{8,10},{9,11},{10,... | collective-permute-start | bytes 393224 | tf_op jit(solution)/shard_map/ppermute | solution.py:55
  56.1 7.8 %collective-permute-start.19 = (bf16[32,2048]{1,0:T(8,128)(2,1)S(1)}, bf16[32,2048]{1,0:T(8,128)(2,1)S(1)}, u32[]{:S(2)}, u32[]{:S(2)}) collective-permute-start(bf16[32,2048]{1,0:T(8,128)(2,1)S(1)} %collective-permute-done.15.refs_2_), channel_id=1, source_target_pairs={{0,2},{1,3},{2,0},{3,1},{4,6},{5,7},{6,4},{7,5},{8,10},{9,11},{10,... | collective-permute-start | bytes 393224 | tf_op jit(solution)/shard_map/ppermute | solution.py:55
  56.7 10.5 %collective-permute-start.8 = (bf16[32,2048]{1,0:T(8,128)(2,1)S(1)}, bf16[32,2048]{1,0:T(8,128)(2,1)S(1)}, u32[]{:S(2)}, u32[]{:S(2)}) collective-permute-start(bf16[32,2048]{1,0:T(8,128)(2,1)S(1)} %attend.2.refs_0_), channel_id=1, source_target_pairs={{0,4},{1,3},{2,6},{3,1},{4,0},{5,7},{6,2},{7,5},{8,12},{9,11},{10,... | collective-permute-start | bytes 393224 | tf_op jit(solution)/shard_map/ppermute | solution.py:55
  61.7 5.3 %collective-permute-start.16 = (bf16[32,2048]{1,0:T(8,128)(2,1)S(1)}, bf16[32,2048]{1,0:T(8,128)(2,1)S(1)}, u32[]{:S(2)}, u32[]{:S(2)}) collective-permute-start(bf16[32,2048]{1,0:T(8,128)(2,1)S(1)} %collective-permute-done.14.refs_1_), channel_id=1, source_target_pairs={{0,4},{1,5},{2,6},{3,7},{4,0},{5,1},{6,2},{7,3},{8,12},{9,13},{10,... | collective-permute-start | bytes 393224 | tf_op jit(solution)/shard_map/ppermute | solution.py:55
  62.3 6.8 %collective-permute-start.18 = (bf16[32,2048]{1,0:T(8,128)(2,1)S(1)}, bf16[32,2048]{1,0:T(8,128)(2,1)S(1)}, u32[]{:S(2)}, u32[]{:S(2)}) collective-permute-start(bf16[32,2048]{1,0:T(8,128)(2,1)S(1)} %collective-permute-done.14.refs_1_), channel_id=1, source_target_pairs={{0,2},{1,3},{2,0},{3,1},{4,6},{5,7},{6,4},{7,5},{8,10},{9,11},{10,... | collective-permute-start | bytes 393224 | tf_op jit(solution)/shard_map/ppermute | solution.py:55
  63.7 6.3 %collective-permute-start.9 = (bf16[32,2048]{1,0:T(8,128)(2,1)S(1)}, bf16[32,2048]{1,0:T(8,128)(2,1)S(1)}, u32[]{:S(2)}, u32[]{:S(2)}) collective-permute-start(bf16[32,2048]{1,0:T(8,128)(2,1)S(1)} %collective-permute-done.7.refs_1_), channel_id=1, source_target_pairs={{0,4},{1,3},{2,6},{3,1},{4,0},{5,7},{6,2},{7,5},{8,12},{9,11},{10,... | collective-permute-start | bytes 393224 | tf_op jit(solution)/shard_map/ppermute | solution.py:55
  63.9 11.9 %collective-permute-start.10 = (bf16[32,2048]{1,0:T(8,128)(2,1)S(1)}, bf16[32,2048]{1,0:T(8,128)(2,1)S(1)}, u32[]{:S(2)}, u32[]{:S(2)}) collective-permute-start(bf16[32,2048]{1,0:T(8,128)(2,1)S(1)} %attend.2.refs_0_), channel_id=1, source_target_pairs={{0,2},{1,5},{2,0},{3,7},{4,6},{5,1},{6,4},{7,3},{8,10},{9,13},{10,... | collective-permute-start | bytes 393224 | tf_op jit(solution)/shard_map/ppermute | solution.py:55
  67.0 5.0 %collective-permute-start.20 = (bf16[32,2048]{1,0:T(8,128)(2,1)S(1)}, bf16[32,2048]{1,0:T(8,128)(2,1)S(1)}, u32[]{:S(2)}, u32[]{:S(2)}) collective-permute-start(bf16[32,2048]{1,0:T(8,128)(2,1)S(1)} %collective-permute-done.16.refs_3_), channel_id=1, source_target_pairs={{0,2},{1,3},{2,0},{3,1},{4,6},{5,7},{6,4},{7,5},{8,10},{9,11},{10,... | collective-permute-start | bytes 393224 | tf_op jit(solution)/shard_map/ppermute | solution.py:55
  67.2 8.6 %collective-permute-start.11 = (bf16[32,2048]{1,0:T(8,128)(2,1)S(1)}, bf16[32,2048]{1,0:T(8,128)(2,1)S(1)}, u32[]{:S(2)}, u32[]{:S(2)}) collective-permute-start(bf16[32,2048]{1,0:T(8,128)(2,1)S(1)} %collective-permute-done.7.refs_1_), channel_id=1, source_target_pairs={{0,2},{1,5},{2,0},{3,7},{4,6},{5,1},{6,4},{7,3},{8,10},{9,13},{10,... | collective-permute-start | bytes 393224 | tf_op jit(solution)/shard_map/ppermute | solution.py:55
  69.1 6.7 %collective-permute-start.12 = (bf16[32,2048]{1,0:T(8,128)(2,1)S(1)}, bf16[32,2048]{1,0:T(8,128)(2,1)S(1)}, u32[]{:S(2)}, u32[]{:S(2)}) collective-permute-start(bf16[32,2048]{1,0:T(8,128)(2,1)S(1)} %collective-permute-done.8.refs_2_), channel_id=1, source_target_pairs={{0,2},{1,5},{2,0},{3,7},{4,6},{5,1},{6,4},{7,3},{8,10},{9,13},{10,... | collective-permute-start | bytes 393224 | tf_op jit(solution)/shard_map/ppermute | solution.py:55
  70.0 6.2 %collective-permute-start.13 = (bf16[32,2048]{1,0:T(8,128)(2,1)S(1)}, bf16[32,2048]{1,0:T(8,128)(2,1)S(1)}, u32[]{:S(2)}, u32[]{:S(2)}) collective-permute-start(bf16[32,2048]{1,0:T(8,128)(2,1)S(1)} %collective-permute-done.9.refs_3_), channel_id=1, source_target_pairs={{0,2},{1,5},{2,0},{3,7},{4,6},{5,1},{6,4},{7,3},{8,10},{9,13},{10,... | collective-permute-start | bytes 393224 | tf_op jit(solution)/shard_map/ppermute | solution.py:55
  80.0 2.0 %collective-permute-start.21 = (bf16[128,2048]{1,0:T(8,128)(2,1)S(1)}, bf16[128,2048]{1,0:T(8,128)(2,1)S(1)}, u32[]{:S(2)}, u32[]{:S(2)}) collective-permute-start(bf16[128,2048]{1,0:T(8,128)(2,1)S(1)} %get-tuple-element.56), channel_id=1, source_target_pairs={{0,1},{1,0},{2,3},{3,2},{4,5},{5,4},{6,7},{7,6},{8,9},{9,8},{10,11... | collective-permute-start | bytes 1572872 | tf_op jit(solution)/shard_map/ppermute | solution.py:507

commit v7 on v6

--- a/solution.py
+++ b/solution.py
@@ -334,7 +334,21 @@
     moved = jnp.where(gy == 0, n // 2, 0)
     if chunk:
         before_ref, refs = refs[0], refs[1:]
-    w_ref, outs, (x_buf, x_sems) = refs[0], refs[1:-2], refs[-2:]
+    x_buf, x_sems, w_sems = refs[-3:]
+    w_ref, outs = refs[0], refs[1:-3]
+    w_copies = []
+    if chunk == 0:
+        more_ref, sums_ref, next_ref = outs
+        outs = [sums_ref]
+        size = next_ref.shape[0] // 4
+        for p in range(4):
+            w_copies.append(
+                pltpu.make_async_copy(
+                    more_ref.at[next_ref.shape[0] + p * size : next_ref.shape[0] + (p + 1) * size],
+                    next_ref.at[p * size : (p + 1) * size],
+                    w_sems.at[p],
+                )
+            )
     depth, cols = x_buf.shape[1], w_ref.shape[1]
     half = x_buf.shape[0] // 2
     x_copies = []
@@ -343,7 +357,7 @@
         x_copies.append(
             pltpu.make_async_copy(piece, x_buf.at[pl.ds(start, block), :], x_sems.at[slot])
         )
-    for copy in x_copies:
+    for copy in x_copies + w_copies:
         copy.start()
     for copy in x_copies:
         copy.wait()
@@ -359,12 +373,14 @@
         else:
             outs[0][:, at] = product[:half].astype(jnp.bfloat16)
             outs[1][:, at] = product[half:]
-
-
-def combine(chunk, pieces, before, w_out):
+    for copy in w_copies:
+        copy.wait()
+
+
+def combine(chunk, pieces, before, w_rows, w_out):
     n, (block, depth) = len(pieces), pieces[0].shape
     rows = n * block
-    cols = w_out.shape[1]
+    cols = w_rows.shape[1]
     last = chunk == CHUNKS - 1
     hbm = pl.BlockSpec(memory_space=pltpu.HBM)
     vmem = pl.BlockSpec(memory_space=pltpu.VMEM)
@@ -374,22 +390,25 @@
             pltpu.VMEM((rows // 2, cols), jnp.float32),
         ]
     else:
-        out_shape = [pltpu.VMEM((rows, cols), jnp.float32)]
+        out_shape = [pltpu.VMEM((rows, cols), jnp.float32), pltpu.VMEM(w_rows.shape, w_rows.dtype)]
     earlier = [] if chunk == 0 else [before]
+    later = [in_hbm(w_out)] if chunk == 0 else []
     return pl.pallas_call(
         functools.partial(combine_kernel, n, block, chunk),
         out_shape=out_shape,
         in_specs=[pl.BlockSpec(memory_space=pl.ANY)] * len(pieces)
         + [vmem] * len(earlier)
-        + [vmem],
+        + [vmem]
+        + [pl.BlockSpec(memory_space=pltpu.HBM)] * len(later),
         out_specs=[vmem] * len(out_shape),
         scratch_shapes=[
             pltpu.VMEM((rows, depth), jnp.bfloat16),
             pltpu.SemaphoreType.DMA((n,)),
+            pltpu.SemaphoreType.DMA((4,)),
         ],
         compiler_params=pltpu.CompilerParams(vmem_limit_bytes=16 * MIB),
         name="combine",
-    )(*pieces, *earlier, w_out)
+    )(*pieces, *earlier, w_rows, *later)
 
 
 def shards(
@@ -419,24 +438,31 @@
 
     share = q_cols // 2
     orders = bit_orders(n)
+
+    def first_exchange(send):
+        return exchange(send, n, cores, 0, orders)
+
     send_a, keep_a, x = column_part(0, share, None)
     x = after(x, send_a)
-    other_a = exchange(send_a, n, cores, 0, orders)
+    other_a = first_exchange(send_a)
     send_b, keep_b = column_part(share, share, 0)
     x = after(x, send_b)
-    other_b = exchange(send_b, n, cores, 0, orders)
+    other_b = first_exchange(send_b)
     sum_a = keep_a + other_a.astype(jnp.float32)
     x = after(x, sum_a)
-    later = []
-    for chunk in range(1, CHUNKS):
-        later.append(column_part(chunk * q_cols, q_cols, chunk * kv))
-    other_b = after(other_b, *(send_c for send_c, _ in later))
-    first = jnp.concatenate([sum_a, keep_b + other_b.astype(jnp.float32)], axis=1)
-    half = first.shape[0] // 2
-    send = first[half:].astype(jnp.bfloat16)
-    flows = [[1, first[:half], send]]
-    for send_c, keep_c in later:
-        flows.append([0, keep_c, after(send_c, flows[-1][2])])
+    send_c, keep_c = column_part(q_cols, share, None)
+    other_c = first_exchange(send_c)
+    other_b = after(other_b, send_c)
+
+    def joined(left, keep, other):
+        value = jnp.concatenate([left, keep + other.astype(jnp.float32)], axis=1)
+        half = value.shape[0] // 2
+        return [1, value[:half], value[half:].astype(jnp.bfloat16)]
+
+    lead = joined(sum_a, keep_b, other_b)
+    x = after(x, lead[2], send_c)
+    send_d, keep_d = column_part(q_cols + share, share, kv)
+    other_d = first_exchange(send_d)
 
     def start(flow):
         return exchange(flow[2], n, cores, flow[0], orders)
@@ -449,20 +475,24 @@
         low = value.shape[0] // 2 if stage < levels - 1 else 0
         flow[:] = stage + 1, value[:low] if low else value, value[low:].astype(jnp.bfloat16)
 
-    lead, follow = flows
     w_rows = w_out.shape[0] // CHUNKS
-    weights = [fetch_rows(after(w_out, lead[2], follow[2]), 0, w_rows)]
+    w_first = fetch_rows(after(w_out, lead[2], send_d), 0, w_rows)
+    finish(lead, start(lead), w_first)
+    other_c, other_d = after((other_c, other_d), lead[2])
+    follow = joined(keep_c + other_c.astype(jnp.float32), keep_d, other_d)
+    flows = [lead, follow]
+    cached = False
     while follow[0] < levels:
         pending = [start(flow) for flow in flows if flow[0] < levels]
-        if lead[0] == levels:
+        if not cached:
+            cache_keys, cache_values = fetch(*after((cache_keys, cache_values), follow[2]))
+            pending[0] = after(pending[0], cache_keys, cache_values)
+            cached = True
+        if lead[0] < levels:
+            finish(lead, pending[0])
+            finish(follow, pending[1], lead[1], lead[2])
+        else:
             finish(follow, pending[0])
-        elif lead[0] == levels - 1:
-            cache_keys, cache_values = fetch(*after((cache_keys, cache_values), follow[2]))
-            finish(lead, pending[0], cache_keys, cache_values)
-            finish(follow, pending[1], lead[1])
-        else:
-            finish(lead, pending[0], *weights)
-            finish(follow, pending[1], lead[2])
     sums = [flow[1] for flow in flows]
     squares = sums[0][:, share : share + 128]
     plain = [h * HD for h in range(q_cols // HD)]
@@ -485,7 +515,6 @@
                 cache_lengths,
             )
         )
-    weights.append(fetch_rows(after(w_out, attentions[1]), w_rows, w_rows))
     gathered = []
     for chunk in range(CHUNKS):
         slots = [attentions[chunk]]
@@ -494,16 +523,14 @@
             source = slots[slot - (1 << top)]
             if slot == 1 and chunk == 0:
                 source = after(source, sums[1])
-            if slot == 3 and chunk == 1:
-                source = after(source, weights[1])
+            if slot == 3 << (levels - 2):
+                source = after(source, slots[1 << (levels - 1)])
             slots.append(
                 exchange(source, n, cores, levels - 1 - top, gather_orders(n, chunk))
             )
         gathered.append(slots)
-    result = None
-    for chunk in range(CHUNKS):
-        result = combine(chunk, gathered[chunk], result and result[0], weights[chunk])
-    send, keep = result
+    before, w_second = combine(0, gathered[0], None, w_first, w_out)
+    send, keep = combine(1, gathered[1], before, w_second, None)
     other = lax.ppermute(send, "gy", [(0, 1), (1, 0)])
     return (keep + other.astype(jnp.float32)).astype(jnp.bfloat16)
 

time: 83.1 us -> 85 us (1.023)
  waiting for transfers between devices: 14.8 us -> 21 us
  starting transfers between devices: 27.8 us -> 24.1 us
  Pallas kernels: 37.4 us -> 36.5 us
    ppermute x21 -> x22, waiting for transfers between devices: 12.9 us -> 19.1 us  [exchange(): return lax.ppermute(value, ('gx', 'gy'), pairs)]
    ppermute x21 -> x22, starting transfers between devices: 27.7 us -> 24.1 us  [exchange(): return lax.ppermute(value, ('gx', 'gy'), pairs)]
    pallas_call x2 -> x1, Pallas kernels: 7 us -> 3.5 us  [fetch_rows(): pl.pallas_call(functools.partial(fetch_rows_kernel, start, pieces), out_s...]
    pallas_call x3 -> x4, Pallas kernels: 13.8 us -> 15.1 us  [project(): pl.pallas_call(functools.partial(project_kernel, n, q_start, kv_start, fi...]
    pallas_call x2, Pallas kernels: 7.55 us -> 8.8 us  [combine(): pl.pallas_call(functools.partial(combine_kernel, n, block, chunk), out_sh...]
  transfers between devices with their start and end apart: 22 -> 23, of which waited for: 10 -> 13; matrix products, arithmetic and copies ran while one was open for 2% -> 2% of each run, Pallas kernels for 35% -> 33%
where the time goes in v7:
time: 85 us; the launch traced here: 84.7 us
  Pallas kernels  36.5 us (43%)
  starting transfers between devices  24.1 us (28%)
  waiting for transfers between devices  21 us (25%)
  other arithmetic  2.63 us (3%)
    ppermute x22, starting transfers between devices, exchange(): return lax.ppermute(value, ('gx', 'gy'), pairs)  24.1 us
    ppermute x22, waiting for transfers between devices, exchange(): return lax.ppermute(value, ('gx', 'gy'), pairs)  19.1 us
    pallas_call x4, Pallas kernels, project(): pl.pallas_call(functools.partial(project_kernel, n, q_start, kv_start, fi...  15.1 us
    pallas_call x2, Pallas kernels, combine(): pl.pallas_call(functools.partial(combine_kernel, n, block, chunk), out_sh...  8.8 us
    pallas_call x2, Pallas kernels, attend(): pl.pallas_call(functools.partial(attend_kernel, chunk, offsets, kv_offset...  5.64 us
    pallas_call x1, Pallas kernels, fetch_rows(): pl.pallas_call(functools.partial(fetch_rows_kernel, start, pieces), out_s...  3.5 us
    pallas_call x1, Pallas kernels, fetch(): pl.pallas_call(functools.partial(fetch_kernel, len(arrays), pieces), out_...  3.47 us
    ppermute x1, waiting for transfers between devices, shards(): other = lax.ppermute(send, 'gy', [(0, 1), (1, 0)])  1.9 us
  transfers between devices with their start and end apart: 23, of which 13 were waited for; matrix products, arithmetic and copies ran while one was open for 2% of the time, Pallas kernels for 33%

profile of v7, /device:TPU:0, one launch (start us, length us, event | category | flops | bytes accessed | tf_op | source)
XLA Modules:
  0.0 84.7 jit_solution(9004201965028123590)
XLA Ops:
  0.0 4.4 %project.4 = (bf16[128,1152]{1,0:T(8,128)(2,1)S(1)}, f32[128,1152]{1,0:T(8,128)S(1)}, bf16[256,2048]{1,0:T(8,128)(2,1)S(1)}) custom-call(bf16[256,2048]{1,0:T(8,128)(2,1)} %refs_0_.1, f32[1,2048]{1,0:T(1,128)} %bitcast.1, bf16[2048,4096]{1,0:T(8,128)(2,1)} %refs_1_.5, bf16[2048,256]{1,0:T(8,128)(2,1)} %refs_2_.7, bf16[2048,256]{1,0:T(8,128)(2,1)} %refs_3_.7), custom_call_target="tpu_custom_call" | custom-call | tf_op jit(solution)/shard_map/project/pallas_call | solution.py:159
  4.4 3.0 %collective-permute-start = (bf16[128,1152]{1,0:T(8,128)(2,1)S(1)}, bf16[128,1152]{1,0:T(8,128)(2,1)S(1)}, u32[]{:S(2)}, u32[]{:S(2)}) collective-permute-start(bf16[128,1152]{1,0:T(8,128)(2,1)S(1)} %get-tuple-element.37), channel_id=1, source_target_pairs={{0,2},{1,5},{2,0},{3,7},{4,6},{5,1},{6,4},{7,3},{8,10},{9,13},{10,... | collective-permute-start | bytes 884744 | tf_op jit(solution)/shard_map/ppermute | solution.py:55
  7.4 3.9 %project.5 = (bf16[128,1280]{1,0:T(8,128)(2,1)S(1)}, f32[128,1280]{1,0:T(8,128)S(1)}) custom-call(bf16[256,2048]{1,0:T(8,128)(2,1)S(1)} %get-tuple-element.47.refs_0_, bf16[2048,4096]{1,0:T(8,128)(2,1)} %refs_1_.5, bf16[2048,256]{1,0:T(8,128)(2,1)} %refs_2_.7, bf16[2048,256]{1,0:T(8,128)(2,1)} %refs_3_.7), custom_call_target="tpu_custom_call" | custom-call | tf_op jit(solution)/shard_map/project/pallas_call | solution.py:159
  11.3 0.1 collective-permute-start.2
  11.4 0.8 collective-permute-done
  12.1 0.1 convert_add_fusion.2
  12.2 0.0 copy-start
  12.2 3.1 %project.6 = (bf16[128,1024]{1,0:T(8,128)(2,1)S(1)}, f32[128,1024]{1,0:T(8,128)S(1)}) custom-call(bf16[256,2048]{1,0:T(8,128)(2,1)S(1)} %get-tuple-element.47.refs_0_, bf16[2048,4096]{1,0:T(8,128)(2,1)} %refs_1_.5, bf16[2048,256]{1,0:T(8,128)(2,1)} %refs_2_.7, bf16[2048,256]{1,0:T(8,128)(2,1)} %refs_3_.7), custom_call_target="tpu_custom_call" | custom-call | tf_op jit(solution)/shard_map/project/pallas_call | solution.py:159
  15.2 3.2 %collective-permute-done.2 = bf16[128,1280]{1,0:T(8,128)(2,1)S(1)} collective-permute-done((bf16[128,1280]{1,0:T(8,128)(2,1)S(1)}, bf16[128,1280]{1,0:T(8,128)(2,1)S(1)}, u32[]{:S(2)}, u32[]{:S(2)}) %collective-permute-start.2) | collective-permute-done | bytes 327712 | tf_op jit(solution)/shard_map/ppermute | solution.py:55
  18.4 0.1 convert_add_fusion.1
  18.5 1.6 %collective-permute-start.4 = (bf16[64,2432]{1,0:T(8,128)(2,1)S(1)}, bf16[64,2432]{1,0:T(8,128)(2,1)}, u32[]{:S(2)}, u32[]{:S(2)}) collective-permute-start(bf16[64,2432]{1,0:T(8,128)(2,1)S(1)} %fusion.1), channel_id=1, source_target_pairs={{0,4},{1,3},{2,6},{3,1},{4,0},{5,7},{6,2},{7,5},{8,12},{9,11},{10,... | collective-permute-start | bytes 933896 | tf_op jit(solution)/shard_map/ppermute | solution.py:55
  20.2 0.1 add_convert_fusion.1
  20.2 0.1 convert_element_type.54
  20.3 0.6 collective-permute-start.1
  20.9 3.9 %project.7 = (bf16[128,1280]{1,0:T(8,128)(2,1)S(1)}, f32[128,1280]{1,0:T(8,128)S(1)}) custom-call(bf16[256,2048]{1,0:T(8,128)(2,1)S(1)} %get-tuple-element.47.refs_0_, bf16[2048,4096]{1,0:T(8,128)(2,1)} %refs_1_.5, bf16[2048,256]{1,0:T(8,128)(2,1)} %refs_2_.7, bf16[2048,256]{1,0:T(8,128)(2,1)} %refs_3_.7), custom_call_target="tpu_custom_call" | custom-call | tf_op jit(solution)/shard_map/project/pallas_call | solution.py:159
  24.8 1.6 %collective-permute-start.3 = (bf16[128,1280]{1,0:T(8,128)(2,1)S(1)}, bf16[128,1280]{1,0:T(8,128)(2,1)S(1)}, u32[]{:S(2)}, u32[]{:S(2)}) collective-permute-start(bf16[128,1280]{1,0:T(8,128)(2,1)S(1)} %get-tuple-element.48), channel_id=1, source_target_pairs={{0,2},{1,5},{2,0},{3,7},{4,6},{5,1},{6,4},{7,3},{8,10},{9,13},{10,... | collective-permute-start | bytes 983048 | tf_op jit(solution)/shard_map/ppermute | solution.py:55
  26.3 3.5 %fetch_rows.1.refs_8_ = bf16[2048,2048]{1,0:T(8,128)(2,1)S(1)} custom-call(bf16[4096,2048]{1,0:T(8,128)(2,1)} %refs_9_.1), custom_call_target="tpu_custom_call" | custom-call | tf_op jit(solution)/shard_map/fetch_rows/pallas_call | solution.py:320
  29.8 0.0 collective-permute-done.4
  29.9 1.0 %fusion.2 = f32[64,2432]{1,0:T(8,128)S(1)} fusion(f32[128,1280]{1,0:T(8,128)S(1)} %convert_add_fusion.1, f32[128,1152]{1,0:T(8,128)S(1)} %convert_add_fusion.2, bf16[64,2432]{1,0:T(8,128)(2,1)} %collective-permute-done.4), kind=kLoop, calls=%fused_computation.10 | loop fusion | flops 466944 | bytes 2179072 | tf_op jit(solution)/shard_map/add | solution.py:474
  30.9 2.7 %collective-permute-start.6 = (bf16[32,2432]{1,0:T(8,128)(2,1)S(1)}, bf16[32,2432]{1,0:T(8,128)(2,1)S(1)}, u32[]{:S(2)}, u32[]{:S(2)}) collective-permute-start(bf16[32,2432]{1,0:T(8,128)(2,1)S(1)} %slice.69), channel_id=1, source_target_pairs={{0,8},{1,9},{2,10},{3,11},{4,12},{5,13},{6,14},{7,15},{8,0},{9,1},... | collective-permute-start | bytes 466952 | tf_op jit(solution)/shard_map/ppermute | solution.py:55
  33.6 0.0 collective-permute-done.1
  33.6 0.0 collective-permute-done.3
  33.6 0.1 convert_add_fusion.3
  33.6 0.1 convert_add_fusion
  33.8 0.5 collective-permute-start.5
  34.3 3.5 %fetch.1 = (bf16[8,1024,256]{2,1,0:T(8,128)(2,1)S(1)}, bf16[8,1024,256]{2,1,0:T(8,128)(2,1)S(1)}) custom-call(bf16[8,1024,256]{2,1,0:T(8,128)(2,1)} %refs_0_.2, bf16[8,1024,256]{2,1,0:T(8,128)(2,1)} %refs_1_.6), custom_call_target="tpu_custom_call" | custom-call | tf_op jit(solution)/shard_map/fetch/pallas_call | solution.py:291
  37.7 1.3 %collective-permute-done.6 = bf16[32,2432]{1,0:T(8,128)(2,1)S(1)} collective-permute-done((bf16[32,2432]{1,0:T(8,128)(2,1)S(1)}, bf16[32,2432]{1,0:T(8,128)(2,1)S(1)}, u32[]{:S(2)}, u32[]{:S(2)}) %collective-permute-start.6) | collective-permute-done | bytes 155680 | tf_op jit(solution)/shard_map/ppermute | solution.py:55
  39.1 3.1 %collective-permute-done.5 = bf16[64,2304]{1,0:T(8,128)(2,1)S(1)} collective-permute-done((bf16[64,2304]{1,0:T(8,128)(2,1)S(1)}, bf16[64,2304]{1,0:T(8,128)(2,1)S(1)}, u32[]{:S(2)}, u32[]{:S(2)}) %collective-permute-start.5) | collective-permute-done | bytes 294944 | tf_op jit(solution)/shard_map/ppermute | solution.py:55
  42.2 0.1 fusion.4
  42.3 0.1 collective-permute-start.7
  42.4 0.1 fusion.6
  42.5 0.1 pad_maximum_fusion.2
  42.6 2.9 %attend.3.refs_0_ = bf16[32,2048]{1,0:T(8,128)(2,1)S(1)} custom-call(s32[8]{0:T(128)S(1)} %copy-done, f32[32,2432]{1,0:T(8,128)S(1)} %slice_add_fusion.refs_0_, f32[32,128]{1,0:T(8,128)S(1)} %slice.48.refs_1_, f32[32,128]{1,0:T(8,128)S(1)} %get-tuple-element.70.refs_2_, f32[32,128]{1,0:T(8,128)S(1)} %get-tuple-element.71.refs_3_, ...), custom_call_target="tpu_custom_call" | custom-call | tf_op jit(solution)/shard_map/attend/pallas_call | solution.py:259
  45.5 1.9 %collective-permute-start.18 = (bf16[32,2048]{1,0:T(8,128)(2,1)S(1)}, bf16[32,2048]{1,0:T(8,128)(2,1)S(1)}, u32[]{:S(2)}, u32[]{:S(2)}) collective-permute-start(bf16[32,2048]{1,0:T(8,128)(2,1)S(1)} %attend.3.refs_0_), channel_id=1, source_target_pairs={{0,2},{1,3},{2,0},{3,1},{4,6},{5,7},{6,4},{7,5},{8,10},{9,11},{10,... | collective-permute-start | bytes 393224 | tf_op jit(solution)/shard_map/ppermute | solution.py:55
  47.4 0.1 collective-permute-start.16
  47.5 4.7 %collective-permute-done.7 = bf16[32,2304]{1,0:T(8,128)(2,1)S(1)} collective-permute-done((bf16[32,2304]{1,0:T(8,128)(2,1)S(1)}, bf16[32,2304]{1,0:T(8,128)(2,1)S(1)}, u32[]{:S(2)}, u32[]{:S(2)}) %collective-permute-start.7) | collective-permute-done | bytes 147488 | tf_op jit(solution)/shard_map/ppermute | solution.py:55
  52.2 0.1 collective-permute-start.15
  52.3 2.7 %attend.2.refs_0_ = bf16[32,2048]{1,0:T(8,128)(2,1)S(1)} custom-call(s32[8]{0:T(128)S(1)} %copy-done, f32[32,2304]{1,0:T(8,128)S(1)} %slice_add_fusion.1.refs_0_, f32[32,128]{1,0:T(8,128)S(1)} %slice.48.refs_1_, f32[32,128]{1,0:T(8,128)S(1)} %get-tuple-element.70.refs_2_, f32[32,128]{1,0:T(8,128)S(1)} %get-tuple-element.71.refs_3_, ...), custom_call_target="tpu_custom_call" | custom-call | tf_op jit(solution)/shard_map/attend/pallas_call | solution.py:259
  55.1 3.0 %collective-permute-start.8 = (bf16[32,2048]{1,0:T(8,128)(2,1)S(1)}, bf16[32,2048]{1,0:T(8,128)(2,1)S(1)}, u32[]{:S(2)}, u32[]{:S(2)}) collective-permute-start(bf16[32,2048]{1,0:T(8,128)(2,1)S(1)} %attend.2.refs_0_), channel_id=1, source_target_pairs={{0,8},{1,9},{2,10},{3,11},{4,12},{5,13},{6,14},{7,15},{8,0},{9,1},... | collective-permute-start | bytes 393224 | tf_op jit(solution)/shard_map/ppermute | solution.py:55
  58.0 0.5 collective-permute-start.11
  58.5 0.0 collective-permute-done.18.refs_4_
  58.5 0.4 collective-permute-done.15.refs_1_
  58.9 1.7 %collective-permute-start.17 = (bf16[32,2048]{1,0:T(8,128)(2,1)S(1)}, bf16[32,2048]{1,0:T(8,128)(2,1)S(1)}, u32[]{:S(2)}, u32[]{:S(2)}) collective-permute-start(bf16[32,2048]{1,0:T(8,128)(2,1)S(1)} %collective-permute-done.15.refs_1_), channel_id=1, source_target_pairs={{0,4},{1,5},{2,6},{3,7},{4,0},{5,1},{6,2},{7,3},{8,12},{9,13},{10,... | collective-permute-start | bytes 393224 | tf_op jit(solution)/shard_map/ppermute | solution.py:55
  60.5 1.6 %collective-permute-start.20 = (bf16[32,2048]{1,0:T(8,128)(2,1)S(1)}, bf16[32,2048]{1,0:T(8,128)(2,1)S(1)}, u32[]{:S(2)}, u32[]{:S(2)}) collective-permute-start(bf16[32,2048]{1,0:T(8,128)(2,1)S(1)} %collective-permute-done.16.refs_2_), channel_id=1, source_target_pairs={{0,2},{1,3},{2,0},{3,1},{4,6},{5,7},{6,4},{7,5},{8,10},{9,11},{10,... | collective-permute-start | bytes 393224 | tf_op jit(solution)/shard_map/ppermute | solution.py:55
  62.1 0.3 collective-permute-done.8.refs_1_
  62.4 0.1 collective-permute-start.10
  62.5 1.8 %collective-permute-done.11.refs_4_ = bf16[32,2048]{1,0:T(8,128)(2,1)S(1)} collective-permute-done((bf16[32,2048]{1,0:T(8,128)(2,1)S(1)}, bf16[32,2048]{1,0:T(8,128)(2,1)S(1)}, u32[]{:S(2)}, u32[]{:S(2)}) %collective-permute-start.11) | collective-permute-done | bytes 131104 | tf_op jit(solution)/shard_map/ppermute | solution.py:55
  64.3 0.9 %collective-permute-done.9.refs_2_ = bf16[32,2048]{1,0:T(8,128)(2,1)S(1)} collective-permute-done((bf16[32,2048]{1,0:T(8,128)(2,1)S(1)}, bf16[32,2048]{1,0:T(8,128)(2,1)S(1)}, u32[]{:S(2)}, u32[]{:S(2)}) %collective-permute-start.9) | collective-permute-done | bytes 131104 | tf_op jit(solution)/shard_map/ppermute | solution.py:55
  65.2 1.2 %collective-permute-start.13 = (bf16[32,2048]{1,0:T(8,128)(2,1)S(1)}, bf16[32,2048]{1,0:T(8,128)(2,1)S(1)}, u32[]{:S(2)}, u32[]{:S(2)}) collective-permute-start(bf16[32,2048]{1,0:T(8,128)(2,1)S(1)} %collective-permute-done.9.refs_2_), channel_id=1, source_target_pairs={{0,2},{1,5},{2,0},{3,7},{4,6},{5,1},{6,4},{7,3},{8,10},{9,13},{10,... | collective-permute-start | bytes 393224 | tf_op jit(solution)/shard_map/ppermute | solution.py:55
  66.4 0.8 collective-permute-start.19
  67.2 0.8 collective-permute-done.17.refs_3_
  68.0 1.1 %collective-permute-start.21 = (bf16[32,2048]{1,0:T(8,128)(2,1)S(1)}, bf16[32,2048]{1,0:T(8,128)(2,1)S(1)}, u32[]{:S(2)}, u32[]{:S(2)}) collective-permute-start(bf16[32,2048]{1,0:T(8,128)(2,1)S(1)} %collective-permute-done.17.refs_3_), channel_id=1, source_target_pairs={{0,2},{1,3},{2,0},{3,1},{4,6},{5,7},{6,4},{7,5},{8,10},{9,11},{10,... | collective-permute-start | bytes 393224 | tf_op jit(solution)/shard_map/ppermute | solution.py:55
  69.1 1.0 %collective-permute-start.12 = (bf16[32,2048]{1,0:T(8,128)(2,1)S(1)}, bf16[32,2048]{1,0:T(8,128)(2,1)S(1)}, u32[]{:S(2)}, u32[]{:S(2)}) collective-permute-start(bf16[32,2048]{1,0:T(8,128)(2,1)S(1)} %collective-permute-done.8.refs_1_), channel_id=1, source_target_pairs={{0,2},{1,5},{2,0},{3,7},{4,6},{5,1},{6,4},{7,3},{8,10},{9,13},{10,... | collective-permute-start | bytes 393224 | tf_op jit(solution)/shard_map/ppermute | solution.py:55
  70.0 0.0 collective-permute-done.10.refs_3_
  70.0 1.1 %collective-permute-start.14 = (bf16[32,2048]{1,0:T(8,128)(2,1)S(1)}, bf16[32,2048]{1,0:T(8,128)(2,1)S(1)}, u32[]{:S(2)}, u32[]{:S(2)}) collective-permute-start(bf16[32,2048]{1,0:T(8,128)(2,1)S(1)} %collective-permute-done.10.refs_3_), channel_id=1, source_target_pairs={{0,2},{1,5},{2,0},{3,7},{4,6},{5,1},{6,4},{7,3},{8,10},{9,13},{10,... | collective-permute-start | bytes 393224 | tf_op jit(solution)/shard_map/ppermute | solution.py:55
  71.1 0.5 collective-permute-done.19.refs_5_
  71.6 1.4 %collective-permute-done.21.refs_7_ = bf16[32,2048]{1,0:T(8,128)(2,1)S(1)} collective-permute-done((bf16[32,2048]{1,0:T(8,128)(2,1)S(1)}, bf16[32,2048]{1,0:T(8,128)(2,1)S(1)}, u32[]{:S(2)}, u32[]{:S(2)}) %collective-permute-start.21) | collective-permute-done | bytes 131104 | tf_op jit(solution)/shard_map/ppermute | solution.py:55
  73.0 4.9 %combine.2 = (f32[256,2048]{1,0:T(8,128)S(1)}, bf16[2048,2048]{1,0:T(8,128)(2,1)S(1)}) custom-call(bf16[32,2048]{1,0:T(8,128)(2,1)S(1)} %attend.3.refs_0_, bf16[32,2048]{1,0:T(8,128)(2,1)S(1)} %collective-permute-done.15.refs_1_, bf16[32,2048]{1,0:T(8,128)(2,1)S(1)} %collective-permute-done.16.refs_2_, bf16[32,2048]{1,0:T(8,128)(2,1)S(1)} %collective-permute-done.17.refs_3_, ...), custom_call_target="tpu_custom_call" | custom-call | tf_op jit(solution)/shard_map/combine/pallas_call | solution.py:396
  77.9 0.0 collective-permute-done.13.refs_6_
  77.9 0.0 collective-permute-done.14.refs_7_
  77.9 3.9 %combine.3 = (bf16[128,2048]{1,0:T(8,128)(2,1)S(1)}, f32[128,2048]{1,0:T(8,128)S(1)}) custom-call(bf16[32,2048]{1,0:T(8,128)(2,1)S(1)} %attend.2.refs_0_, bf16[32,2048]{1,0:T(8,128)(2,1)S(1)} %collective-permute-done.8.refs_1_, bf16[32,2048]{1,0:T(8,128)(2,1)S(1)} %collective-permute-done.9.refs_2_, bf16[32,2048]{1,0:T(8,128)(2,1)S(1)} %collective-permute-done.10.refs_3_, ...), custom_call_target="tpu_custom_call" | custom-call | tf_op jit(solution)/shard_map/combine/pallas_call | solution.py:396
  81.8 0.1 collective-permute-start.22
  81.9 1.9 %collective-permute-done.22 = bf16[128,2048]{1,0:T(8,128)(2,1)S(1)} collective-permute-done((bf16[128,2048]{1,0:T(8,128)(2,1)S(1)}, bf16[128,2048]{1,0:T(8,128)(2,1)S(1)}, u32[]{:S(2)}, u32[]{:S(2)}) %collective-permute-start.22) | collective-permute-done | bytes 524320 | tf_op jit(solution)/shard_map/ppermute | solution.py:534
  83.8 0.9 %add_convert_fusion = bf16[128,2048]{1,0:T(8,128)(2,1)} fusion(f32[128,2048]{1,0:T(8,128)S(1)} %get-tuple-element.65, bf16[128,2048]{1,0:T(8,128)(2,1)S(1)} %collective-permute-done.22), kind=kLoop, calls=%fused_computation.4 | loop fusion | flops 786432 | bytes 2097152 | tf_op jit(solution)/shard_map/convert_element_type | solution.py:535
  (13 shorter events, 0.2 us)
Async XLA Ops:
  4.4 7.7 %collective-permute-start = (bf16[128,1152]{1,0:T(8,128)(2,1)S(1)}, bf16[128,1152]{1,0:T(8,128)(2,1)S(1)}, u32[]{:S(2)}, u32[]{:S(2)}) collective-permute-start(bf16[128,1152]{1,0:T(8,128)(2,1)S(1)} %get-tuple-element.37), channel_id=1, source_target_pairs={{0,2},{1,5},{2,0},{3,7},{4,6},{5,1},{6,4},{7,3},{8,10},{9,13},{10,... | collective-permute-start | bytes 884744 | tf_op jit(solution)/shard_map/ppermute | solution.py:55
  11.3 7.1 %collective-permute-start.2 = (bf16[128,1280]{1,0:T(8,128)(2,1)S(1)}, bf16[128,1280]{1,0:T(8,128)(2,1)S(1)}, u32[]{:S(2)}, u32[]{:S(2)}) collective-permute-start(bf16[128,1280]{1,0:T(8,128)(2,1)S(1)} %get-tuple-element.39), channel_id=1, source_target_pairs={{0,2},{1,5},{2,0},{3,7},{4,6},{5,1},{6,4},{7,3},{8,10},{9,13},{10,... | collective-permute-start | bytes 983048 | tf_op jit(solution)/shard_map/ppermute | solution.py:55
  12.2 8.0 %copy-start = (s32[8]{0:T(128)S(1)}, s32[8]{0:T(128)}, u32[]{:S(2)}) copy-start(s32[8]{0:T(128)} %length_ref.3) | copy-start | bytes 100
  18.5 11.3 %collective-permute-start.4 = (bf16[64,2432]{1,0:T(8,128)(2,1)S(1)}, bf16[64,2432]{1,0:T(8,128)(2,1)}, u32[]{:S(2)}, u32[]{:S(2)}) collective-permute-start(bf16[64,2432]{1,0:T(8,128)(2,1)S(1)} %fusion.1), channel_id=1, source_target_pairs={{0,4},{1,3},{2,6},{3,1},{4,0},{5,7},{6,2},{7,5},{8,12},{9,11},{10,... | collective-permute-start | bytes 933896 | tf_op jit(solution)/shard_map/ppermute | solution.py:55
  20.3 13.3 %collective-permute-start.1 = (bf16[128,1024]{1,0:T(8,128)(2,1)S(1)}, bf16[128,1024]{1,0:T(8,128)(2,1)S(1)}, u32[]{:S(2)}, u32[]{:S(2)}) collective-permute-start(bf16[128,1024]{1,0:T(8,128)(2,1)S(1)} %get-tuple-element.44), channel_id=1, source_target_pairs={{0,2},{1,5},{2,0},{3,7},{4,6},{5,1},{6,4},{7,3},{8,10},{9,13},{10,... | collective-permute-start | bytes 786440 | tf_op jit(solution)/shard_map/ppermute | solution.py:55
  24.8 8.8 %collective-permute-start.3 = (bf16[128,1280]{1,0:T(8,128)(2,1)S(1)}, bf16[128,1280]{1,0:T(8,128)(2,1)S(1)}, u32[]{:S(2)}, u32[]{:S(2)}) collective-permute-start(bf16[128,1280]{1,0:T(8,128)(2,1)S(1)} %get-tuple-element.48), channel_id=1, source_target_pairs={{0,2},{1,5},{2,0},{3,7},{4,6},{5,1},{6,4},{7,3},{8,10},{9,13},{10,... | collective-permute-start | bytes 983048 | tf_op jit(solution)/shard_map/ppermute | solution.py:55
  30.9 8.1 %collective-permute-start.6 = (bf16[32,2432]{1,0:T(8,128)(2,1)S(1)}, bf16[32,2432]{1,0:T(8,128)(2,1)S(1)}, u32[]{:S(2)}, u32[]{:S(2)}) collective-permute-start(bf16[32,2432]{1,0:T(8,128)(2,1)S(1)} %slice.69), channel_id=1, source_target_pairs={{0,8},{1,9},{2,10},{3,11},{4,12},{5,13},{6,14},{7,15},{8,0},{9,1},... | collective-permute-start | bytes 466952 | tf_op jit(solution)/shard_map/ppermute | solution.py:55
  33.8 8.5 %collective-permute-start.5 = (bf16[64,2304]{1,0:T(8,128)(2,1)S(1)}, bf16[64,2304]{1,0:T(8,128)(2,1)S(1)}, u32[]{:S(2)}, u32[]{:S(2)}) collective-permute-start(bf16[64,2304]{1,0:T(8,128)(2,1)S(1)} %fusion.5), channel_id=1, source_target_pairs={{0,4},{1,3},{2,6},{3,1},{4,0},{5,7},{6,2},{7,5},{8,12},{9,11},{10,... | collective-permute-start | bytes 884744 | tf_op jit(solution)/shard_map/ppermute | solution.py:55
  42.3 9.9 %collective-permute-start.7 = (bf16[32,2304]{1,0:T(8,128)(2,1)S(1)}, bf16[32,2304]{1,0:T(8,128)(2,1)S(1)}, u32[]{:S(2)}, u32[]{:S(2)}) collective-permute-start(bf16[32,2304]{1,0:T(8,128)(2,1)S(1)} %slice.70), channel_id=1, source_target_pairs={{0,8},{1,9},{2,10},{3,11},{4,12},{5,13},{6,14},{7,15},{8,0},{9,1},... | collective-permute-start | bytes 442376 | tf_op jit(solution)/shard_map/ppermute | solution.py:55
  45.5 13.0 %collective-permute-start.18 = (bf16[32,2048]{1,0:T(8,128)(2,1)S(1)}, bf16[32,2048]{1,0:T(8,128)(2,1)S(1)}, u32[]{:S(2)}, u32[]{:S(2)}) collective-permute-start(bf16[32,2048]{1,0:T(8,128)(2,1)S(1)} %attend.3.refs_0_), channel_id=1, source_target_pairs={{0,2},{1,3},{2,0},{3,1},{4,6},{5,7},{6,4},{7,5},{8,10},{9,11},{10,... | collective-permute-start | bytes 393224 | tf_op jit(solution)/shard_map/ppermute | solution.py:55
  47.4 11.1 %collective-permute-start.16 = (bf16[32,2048]{1,0:T(8,128)(2,1)S(1)}, bf16[32,2048]{1,0:T(8,128)(2,1)S(1)}, u32[]{:S(2)}, u32[]{:S(2)}) collective-permute-start(bf16[32,2048]{1,0:T(8,128)(2,1)S(1)} %attend.3.refs_0_), channel_id=1, source_target_pairs={{0,4},{1,5},{2,6},{3,7},{4,0},{5,1},{6,2},{7,3},{8,12},{9,13},{10,... | collective-permute-start | bytes 393224 | tf_op jit(solution)/shard_map/ppermute | solution.py:55
  52.2 6.6 %collective-permute-start.15 = (bf16[32,2048]{1,0:T(8,128)(2,1)S(1)}, bf16[32,2048]{1,0:T(8,128)(2,1)S(1)}, u32[]{:S(2)}, u32[]{:S(2)}) collective-permute-start(bf16[32,2048]{1,0:T(8,128)(2,1)S(1)} %attend.3.refs_0_), channel_id=1, source_target_pairs={{0,8},{1,9},{2,10},{3,11},{4,12},{5,13},{6,14},{7,15},{8,0},{9,1},... | collective-permute-start | bytes 393224 | tf_op jit(solution)/shard_map/ppermute | solution.py:55
  55.1 7.4 %collective-permute-start.8 = (bf16[32,2048]{1,0:T(8,128)(2,1)S(1)}, bf16[32,2048]{1,0:T(8,128)(2,1)S(1)}, u32[]{:S(2)}, u32[]{:S(2)}) collective-permute-start(bf16[32,2048]{1,0:T(8,128)(2,1)S(1)} %attend.2.refs_0_), channel_id=1, source_target_pairs={{0,8},{1,9},{2,10},{3,11},{4,12},{5,13},{6,14},{7,15},{8,0},{9,1},... | collective-permute-start | bytes 393224 | tf_op jit(solution)/shard_map/ppermute | solution.py:55
  58.0 6.3 %collective-permute-start.11 = (bf16[32,2048]{1,0:T(8,128)(2,1)S(1)}, bf16[32,2048]{1,0:T(8,128)(2,1)S(1)}, u32[]{:S(2)}, u32[]{:S(2)}) collective-permute-start(bf16[32,2048]{1,0:T(8,128)(2,1)S(1)} %attend.2.refs_0_), channel_id=1, source_target_pairs={{0,2},{1,5},{2,0},{3,7},{4,6},{5,1},{6,4},{7,3},{8,10},{9,13},{10,... | collective-permute-start | bytes 393224 | tf_op jit(solution)/shard_map/ppermute | solution.py:55
  58.5 6.7 %collective-permute-start.9 = (bf16[32,2048]{1,0:T(8,128)(2,1)S(1)}, bf16[32,2048]{1,0:T(8,128)(2,1)S(1)}, u32[]{:S(2)}, u32[]{:S(2)}) collective-permute-start(bf16[32,2048]{1,0:T(8,128)(2,1)S(1)} %attend.2.refs_0_), channel_id=1, source_target_pairs={{0,4},{1,3},{2,6},{3,1},{4,0},{5,7},{6,2},{7,5},{8,12},{9,11},{10,... | collective-permute-start | bytes 393224 | tf_op jit(solution)/shard_map/ppermute | solution.py:55
  58.9 9.2 %collective-permute-start.17 = (bf16[32,2048]{1,0:T(8,128)(2,1)S(1)}, bf16[32,2048]{1,0:T(8,128)(2,1)S(1)}, u32[]{:S(2)}, u32[]{:S(2)}) collective-permute-start(bf16[32,2048]{1,0:T(8,128)(2,1)S(1)} %collective-permute-done.15.refs_1_), channel_id=1, source_target_pairs={{0,4},{1,5},{2,6},{3,7},{4,0},{5,1},{6,2},{7,3},{8,12},{9,13},{10,... | collective-permute-start | bytes 393224 | tf_op jit(solution)/shard_map/ppermute | solution.py:55
  60.5 8.5 %collective-permute-start.20 = (bf16[32,2048]{1,0:T(8,128)(2,1)S(1)}, bf16[32,2048]{1,0:T(8,128)(2,1)S(1)}, u32[]{:S(2)}, u32[]{:S(2)}) collective-permute-start(bf16[32,2048]{1,0:T(8,128)(2,1)S(1)} %collective-permute-done.16.refs_2_), channel_id=1, source_target_pairs={{0,2},{1,3},{2,0},{3,1},{4,6},{5,7},{6,4},{7,5},{8,10},{9,11},{10,... | collective-permute-start | bytes 393224 | tf_op jit(solution)/shard_map/ppermute | solution.py:55
  62.4 7.6 %collective-permute-start.10 = (bf16[32,2048]{1,0:T(8,128)(2,1)S(1)}, bf16[32,2048]{1,0:T(8,128)(2,1)S(1)}, u32[]{:S(2)}, u32[]{:S(2)}) collective-permute-start(bf16[32,2048]{1,0:T(8,128)(2,1)S(1)} %collective-permute-done.8.refs_1_), channel_id=1, source_target_pairs={{0,4},{1,3},{2,6},{3,1},{4,0},{5,7},{6,2},{7,5},{8,12},{9,11},{10,... | collective-permute-start | bytes 393224 | tf_op jit(solution)/shard_map/ppermute | solution.py:55
  65.2 12.7 %collective-permute-start.13 = (bf16[32,2048]{1,0:T(8,128)(2,1)S(1)}, bf16[32,2048]{1,0:T(8,128)(2,1)S(1)}, u32[]{:S(2)}, u32[]{:S(2)}) collective-permute-start(bf16[32,2048]{1,0:T(8,128)(2,1)S(1)} %collective-permute-done.9.refs_2_), channel_id=1, source_target_pairs={{0,2},{1,5},{2,0},{3,7},{4,6},{5,1},{6,4},{7,3},{8,10},{9,13},{10,... | collective-permute-start | bytes 393224 | tf_op jit(solution)/shard_map/ppermute | solution.py:55
  66.4 5.1 %collective-permute-start.19 = (bf16[32,2048]{1,0:T(8,128)(2,1)S(1)}, bf16[32,2048]{1,0:T(8,128)(2,1)S(1)}, u32[]{:S(2)}, u32[]{:S(2)}) collective-permute-start(bf16[32,2048]{1,0:T(8,128)(2,1)S(1)} %collective-permute-done.15.refs_1_), channel_id=1, source_target_pairs={{0,2},{1,3},{2,0},{3,1},{4,6},{5,7},{6,4},{7,5},{8,10},{9,11},{10,... | collective-permute-start | bytes 393224 | tf_op jit(solution)/shard_map/ppermute | solution.py:55
  68.0 5.0 %collective-permute-start.21 = (bf16[32,2048]{1,0:T(8,128)(2,1)S(1)}, bf16[32,2048]{1,0:T(8,128)(2,1)S(1)}, u32[]{:S(2)}, u32[]{:S(2)}) collective-permute-start(bf16[32,2048]{1,0:T(8,128)(2,1)S(1)} %collective-permute-done.17.refs_3_), channel_id=1, source_target_pairs={{0,2},{1,3},{2,0},{3,1},{4,6},{5,7},{6,4},{7,5},{8,10},{9,11},{10,... | collective-permute-start | bytes 393224 | tf_op jit(solution)/shard_map/ppermute | solution.py:55
  69.1 8.8 %collective-permute-start.12 = (bf16[32,2048]{1,0:T(8,128)(2,1)S(1)}, bf16[32,2048]{1,0:T(8,128)(2,1)S(1)}, u32[]{:S(2)}, u32[]{:S(2)}) collective-permute-start(bf16[32,2048]{1,0:T(8,128)(2,1)S(1)} %collective-permute-done.8.refs_1_), channel_id=1, source_target_pairs={{0,2},{1,5},{2,0},{3,7},{4,6},{5,1},{6,4},{7,3},{8,10},{9,13},{10,... | collective-permute-start | bytes 393224 | tf_op jit(solution)/shard_map/ppermute | solution.py:55
  70.0 7.9 %collective-permute-start.14 = (bf16[32,2048]{1,0:T(8,128)(2,1)S(1)}, bf16[32,2048]{1,0:T(8,128)(2,1)S(1)}, u32[]{:S(2)}, u32[]{:S(2)}) collective-permute-start(bf16[32,2048]{1,0:T(8,128)(2,1)S(1)} %collective-permute-done.10.refs_3_), channel_id=1, source_target_pairs={{0,2},{1,5},{2,0},{3,7},{4,6},{5,1},{6,4},{7,3},{8,10},{9,13},{10,... | collective-permute-start | bytes 393224 | tf_op jit(solution)/shard_map/ppermute | solution.py:55
  81.8 2.0 %collective-permute-start.22 = (bf16[128,2048]{1,0:T(8,128)(2,1)S(1)}, bf16[128,2048]{1,0:T(8,128)(2,1)S(1)}, u32[]{:S(2)}, u32[]{:S(2)}) collective-permute-start(bf16[128,2048]{1,0:T(8,128)(2,1)S(1)} %get-tuple-element.66), channel_id=1, source_target_pairs={{0,1},{1,0},{2,3},{3,2},{4,5},{5,4},{6,7},{7,6},{8,9},{9,8},{10,11... | collective-permute-start | bytes 1572872 | tf_op jit(solution)/shard_map/ppermute | solution.py:534

commit v8 on v6

--- a/solution.py
+++ b/solution.py
@@ -20,16 +20,18 @@
 
 
 def bit_orders(n):
-    levels = n.bit_length() - 1
-    first = list(range(levels))
+    first = list(range(n.bit_length() - 1))
     second = list(first)
-    if levels > 1:
+    if len(first) > 1:
         second[0], second[1] = second[1], second[0]
+    if len(first) > 2:
+        first[1], first[2] = first[2], first[1]
     return first, second
 
 
 def gather_orders(n, chunk):
-    first, second = bit_orders(n)
+    second = bit_orders(n)[1]
+    first = sorted(second)
     return (first, second) if chunk else (first, first)
 
 
@@ -169,7 +171,20 @@
 
 def attend_kernel(chunk, offsets, kv_offset, groups, heads, seqs, length_ref, *refs):
     sum_ref, square_ref = refs[:2]
-    cos_ref, sin_ref, k_ref, v_ref, out_ref, q_scr, o_scr = refs[2:]
+    w_copies = []
+    if chunk == 0:
+        cos_ref, sin_ref, k_ref, v_ref, w_ref, out_ref, next_ref, q_scr, o_scr, w_sems = refs[2:]
+        total = next_ref.shape[0]
+        for p in range(4):
+            at = slice(p * total // 4, (p + 1) * total // 4)
+            w_copies.append(
+                pltpu.make_async_copy(
+                    w_ref.at[total + at.start : total + at.stop], next_ref.at[at], w_sems.at[p]
+                )
+            )
+            w_copies[-1].start()
+    else:
+        cos_ref, sin_ref, k_ref, v_ref, out_ref, q_scr, o_scr = refs[2:]
     rows = seqs * NEW
     cols = groups * heads * HD
     kv = groups * HD
@@ -245,8 +260,11 @@
                     ]
         out_ref[mine, :] = o_scr[...].astype(jnp.bfloat16)
 
-
-def attend(chunk, offsets, kv_offset, sums, squares, cosine, sine, cache_keys, cache_values, lengths):
+    for copy in w_copies:
+        copy.wait()
+
+
+def attend(chunk, offsets, kv_offset, sums, squares, cosine, sine, cache_keys, cache_values, lengths, w_out):
     seq_count, slots, kv_all = cache_keys.shape
     kv = kv_all // CHUNKS
     groups = kv // HD
@@ -254,20 +272,25 @@
     cols = len(offsets) * HD
     seqs = min(4, seq_count)
     rows = seq_count * NEW
+    source, copied = [], []
+    if chunk == 0:
+        source.append(in_hbm(w_out))
+        copied.append(pltpu.VMEM((w_out.shape[0] // CHUNKS, w_out.shape[1]), w_out.dtype))
     vmem = pl.BlockSpec(memory_space=pltpu.VMEM)
     hbm = pl.BlockSpec(memory_space=pltpu.HBM)
     return pl.pallas_call(
         functools.partial(attend_kernel, chunk, offsets, kv_offset, groups, heads, seqs),
-        out_shape=pltpu.VMEM((rows, cols), jnp.bfloat16),
-        in_specs=[pl.BlockSpec(memory_space=pltpu.SMEM)] + [vmem] * 6,
-        out_specs=vmem,
+        out_shape=[pltpu.VMEM((rows, cols), jnp.bfloat16)] + copied,
+        in_specs=[pl.BlockSpec(memory_space=pltpu.SMEM)] + [vmem] * 6 + [hbm] * len(source),
+        out_specs=[vmem] * (1 + len(copied)),
         scratch_shapes=[
             pltpu.VMEM((seqs, groups * heads * NEW, HD), jnp.float32),
             pltpu.VMEM((seqs * NEW, cols), jnp.float32),
-        ],
+        ]
+        + [pltpu.SemaphoreType.DMA((4,))] * len(copied),
         compiler_params=pltpu.CompilerParams(vmem_limit_bytes=16 * MIB),
         name="attend",
-    )(lengths, sums, squares, cosine, sine, cache_keys, cache_values)
+    )(lengths, sums, squares, cosine, sine, cache_keys, cache_values, *source)
 
 
 def fetch_kernel(count, pieces, *refs):
@@ -471,21 +494,21 @@
 
     attentions = []
     for chunk in range(CHUNKS):
-        attentions.append(
-            attend(
-                chunk,
-                offsets[chunk],
-                kv_offsets[chunk],
-                sums[chunk],
-                squares,
-                cosine,
-                sine,
-                cache_keys,
-                cache_values,
-                cache_lengths,
-            )
+        out = attend(
+            chunk,
+            offsets[chunk],
+            kv_offsets[chunk],
+            sums[chunk],
+            squares,
+            cosine,
+            sine,
+            cache_keys,
+            cache_values,
+            cache_lengths,
+            w_out,
         )
-    weights.append(fetch_rows(after(w_out, attentions[1]), w_rows, w_rows))
+        attentions.append(out[0])
+        weights += out[1:]
     gathered = []
     for chunk in range(CHUNKS):
         slots = [attentions[chunk]]
@@ -494,8 +517,8 @@
             source = slots[slot - (1 << top)]
             if slot == 1 and chunk == 0:
                 source = after(source, sums[1])
-            if slot == 3 and chunk == 1:
-                source = after(source, weights[1])
+            if chunk == 1 and slot == 3 << (levels - 2):
+                source = after(source, slots[1 << (levels - 1)])
             slots.append(
                 exchange(source, n, cores, levels - 1 - top, gather_orders(n, chunk))
             )

time: 83.1 us -> 89.1 us (1.072)
  starting transfers between devices: 27.8 us -> 33.6 us
  waiting for transfers between devices: 14.8 us -> 17.2 us
  Pallas kernels: 37.4 us -> 35.2 us
    ppermute x21, starting transfers between devices: 27.7 us -> 33.5 us  [exchange(): return lax.ppermute(value, ('gx', 'gy'), pairs)]
    pallas_call x2 -> x1, Pallas kernels: 7 us -> 3.5 us  [fetch_rows(): pl.pallas_call(functools.partial(fetch_rows_kernel, start, pieces), out_s...]
    ppermute x21, waiting for transfers between devices: 12.9 us -> 15.3 us  [exchange(): return lax.ppermute(value, ('gx', 'gy'), pairs)]
    pallas_call x2, Pallas kernels: 5.62 us -> 6.77 us  [attend(): pl.pallas_call(functools.partial(attend_kernel, chunk, offsets, kv_offset...]
  transfers between devices with their start and end apart: 22 -> 22, of which waited for: 10 -> 8; matrix products, arithmetic and copies ran while one was open for 2% -> 2% of each run, Pallas kernels for 35% -> 30%
where the time goes in v8:
time: 89.1 us; the launch traced here: 88.9 us
  Pallas kernels  35.2 us (40%)
  starting transfers between devices  33.6 us (38%)
  waiting for transfers between devices  17.2 us (19%)
  other arithmetic  2.58 us (3%)
    ppermute x21, starting transfers between devices, exchange(): return lax.ppermute(value, ('gx', 'gy'), pairs)  33.5 us
    ppermute x21, waiting for transfers between devices, exchange(): return lax.ppermute(value, ('gx', 'gy'), pairs)  15.3 us
    pallas_call x3, Pallas kernels, project(): pl.pallas_call(functools.partial(project_kernel, n, q_start, kv_start, fi...  13.8 us
    pallas_call x2, Pallas kernels, combine(): pl.pallas_call(functools.partial(combine_kernel, n, block, chunk), out_sh...  7.74 us
    pallas_call x2, Pallas kernels, attend(): pl.pallas_call(functools.partial(attend_kernel, chunk, offsets, kv_offset...  6.77 us
    pallas_call x1, Pallas kernels, fetch_rows(): pl.pallas_call(functools.partial(fetch_rows_kernel, start, pieces), out_s...  3.5 us
    pallas_call x1, Pallas kernels, fetch(): pl.pallas_call(functools.partial(fetch_kernel, len(arrays), pieces), out_...  3.47 us
    ppermute x1, waiting for transfers between devices, shards(): other = lax.ppermute(send, 'gy', [(0, 1), (1, 0)])  1.9 us
  transfers between devices with their start and end apart: 22, of which 8 were waited for; matrix products, arithmetic and copies ran while one was open for 2% of the time, Pallas kernels for 30%

profile of v8, /device:TPU:0, one launch (start us, length us, event | category | flops | bytes accessed | tf_op | source)
XLA Modules:
  0.0 88.9 jit_solution(4312317637136893211)
XLA Ops:
  0.0 4.4 %project.3 = (bf16[128,1152]{1,0:T(8,128)(2,1)S(1)}, f32[128,1152]{1,0:T(8,128)S(1)}, bf16[256,2048]{1,0:T(8,128)(2,1)S(1)}) custom-call(bf16[256,2048]{1,0:T(8,128)(2,1)} %refs_0_.1, f32[1,2048]{1,0:T(1,128)} %bitcast.1, bf16[2048,4096]{1,0:T(8,128)(2,1)} %refs_1_.3, bf16[2048,256]{1,0:T(8,128)(2,1)} %refs_2_.5, bf16[2048,256]{1,0:T(8,128)(2,1)} %refs_3_.5), custom_call_target="tpu_custom_call" | custom-call | tf_op jit(solution)/shard_map/project/pallas_call | solution.py:161
  4.4 3.0 %collective-permute-start = (bf16[128,1152]{1,0:T(8,128)(2,1)S(1)}, bf16[128,1152]{1,0:T(8,128)(2,1)S(1)}, u32[]{:S(2)}, u32[]{:S(2)}) collective-permute-start(bf16[128,1152]{1,0:T(8,128)(2,1)S(1)} %get-tuple-element.33), channel_id=1, source_target_pairs={{0,2},{1,5},{2,0},{3,7},{4,6},{5,1},{6,4},{7,3},{8,10},{9,13},{10,... | collective-permute-start | bytes 884744 | tf_op jit(solution)/shard_map/ppermute | solution.py:57
  7.4 3.9 %project.4 = (bf16[128,1280]{1,0:T(8,128)(2,1)S(1)}, f32[128,1280]{1,0:T(8,128)S(1)}) custom-call(bf16[256,2048]{1,0:T(8,128)(2,1)S(1)} %get-tuple-element.38.refs_0_, bf16[2048,4096]{1,0:T(8,128)(2,1)} %refs_1_.3, bf16[2048,256]{1,0:T(8,128)(2,1)} %refs_2_.5, bf16[2048,256]{1,0:T(8,128)(2,1)} %refs_3_.5), custom_call_target="tpu_custom_call" | custom-call | tf_op jit(solution)/shard_map/project/pallas_call | solution.py:161
  11.3 0.1 collective-permute-start.1
  11.4 0.8 collective-permute-done
  12.1 0.1 convert_add_fusion.2
  12.2 0.0 copy-start
  12.2 5.5 %project.5 = (bf16[128,2304]{1,0:T(8,128)(2,1)S(1)}, f32[128,2304]{1,0:T(8,128)S(1)}) custom-call(bf16[256,2048]{1,0:T(8,128)(2,1)S(1)} %get-tuple-element.38.refs_0_, bf16[2048,4096]{1,0:T(8,128)(2,1)} %refs_1_.3, bf16[2048,256]{1,0:T(8,128)(2,1)} %refs_2_.5, bf16[2048,256]{1,0:T(8,128)(2,1)} %refs_3_.5), custom_call_target="tpu_custom_call" | custom-call | tf_op jit(solution)/shard_map/project/pallas_call | solution.py:161
  17.7 0.7 collective-permute-done.1
  18.4 0.1 convert_add_fusion.1
  18.5 2.7 %collective-permute-start.3 = (bf16[64,2432]{1,0:T(8,128)(2,1)S(1)}, bf16[64,2432]{1,0:T(8,128)(2,1)}, u32[]{:S(2)}, u32[]{:S(2)}) collective-permute-start(bf16[64,2432]{1,0:T(8,128)(2,1)S(1)} %fusion.1), channel_id=1, source_target_pairs={{0,8},{1,3},{2,10},{3,1},{4,12},{5,7},{6,14},{7,5},{8,0},{9,11},{1... | collective-permute-start | bytes 933896 | tf_op jit(solution)/shard_map/ppermute | solution.py:57
  21.2 0.1 add_convert_fusion.1
  21.2 0.1 convert_element_type.49
  21.3 1.4 %collective-permute-start.2 = (bf16[128,2304]{1,0:T(8,128)(2,1)S(1)}, bf16[128,2304]{1,0:T(8,128)(2,1)S(1)}, u32[]{:S(2)}, u32[]{:S(2)}) collective-permute-start(bf16[128,2304]{1,0:T(8,128)(2,1)S(1)} %get-tuple-element.43), channel_id=1, source_target_pairs={{0,2},{1,5},{2,0},{3,7},{4,6},{5,1},{6,4},{7,3},{8,10},{9,13},{10,... | collective-permute-start | bytes 1769480 | tf_op jit(solution)/shard_map/ppermute | solution.py:57
  22.7 3.5 %fetch_rows.1.refs_8_ = bf16[2048,2048]{1,0:T(8,128)(2,1)S(1)} custom-call(bf16[4096,2048]{1,0:T(8,128)(2,1)} %refs_6_.1), custom_call_target="tpu_custom_call" | custom-call | tf_op jit(solution)/shard_map/fetch_rows/pallas_call | solution.py:343
  26.3 2.7 %collective-permute-done.3 = bf16[64,2432]{1,0:T(8,128)(2,1)} collective-permute-done((bf16[64,2432]{1,0:T(8,128)(2,1)S(1)}, bf16[64,2432]{1,0:T(8,128)(2,1)}, u32[]{:S(2)}, u32[]{:S(2)}) %collective-permute-start.3) | collective-permute-done | bytes 311328 | tf_op jit(solution)/shard_map/ppermute | solution.py:57
  29.0 1.0 %fusion.2 = f32[64,2432]{1,0:T(8,128)S(1)} fusion(f32[128,1280]{1,0:T(8,128)S(1)} %convert_add_fusion.1, f32[128,1152]{1,0:T(8,128)S(1)} %convert_add_fusion.2, bf16[64,2432]{1,0:T(8,128)(2,1)} %collective-permute-done.3), kind=kLoop, calls=%fused_computation.8 | loop fusion | flops 466944 | bytes 2179072 | tf_op jit(solution)/shard_map/add | solution.py:471
  30.1 2.4 %collective-permute-start.5 = (bf16[32,2432]{1,0:T(8,128)(2,1)S(1)}, bf16[32,2432]{1,0:T(8,128)(2,1)S(1)}, u32[]{:S(2)}, u32[]{:S(2)}) collective-permute-start(bf16[32,2432]{1,0:T(8,128)(2,1)S(1)} %slice.64), channel_id=1, source_target_pairs={{0,4},{1,9},{2,6},{3,11},{4,0},{5,13},{6,2},{7,15},{8,12},{9,1},{1... | collective-permute-start | bytes 466952 | tf_op jit(solution)/shard_map/ppermute | solution.py:57
  32.5 0.0 collective-permute-done.2
  32.5 0.1 convert_add_fusion
  32.6 3.2 %collective-permute-start.4 = (bf16[64,2304]{1,0:T(8,128)(2,1)S(1)}, bf16[64,2304]{1,0:T(8,128)(2,1)S(1)}, u32[]{:S(2)}, u32[]{:S(2)}) collective-permute-start(bf16[64,2304]{1,0:T(8,128)(2,1)S(1)} %slice.63), channel_id=1, source_target_pairs={{0,8},{1,3},{2,10},{3,1},{4,12},{5,7},{6,14},{7,5},{8,0},{9,11},{1... | collective-permute-start | bytes 884744 | tf_op jit(solution)/shard_map/ppermute | solution.py:57
  35.8 3.5 %fetch.1 = (bf16[8,1024,256]{2,1,0:T(8,128)(2,1)S(1)}, bf16[8,1024,256]{2,1,0:T(8,128)(2,1)S(1)}) custom-call(bf16[8,1024,256]{2,1,0:T(8,128)(2,1)} %refs_0_.2, bf16[8,1024,256]{2,1,0:T(8,128)(2,1)} %refs_1_.4), custom_call_target="tpu_custom_call" | custom-call | tf_op jit(solution)/shard_map/fetch/pallas_call | solution.py:314
  39.3 0.0 collective-permute-done.5
  39.4 7.2 %collective-permute-done.4 = bf16[64,2304]{1,0:T(8,128)(2,1)S(1)} collective-permute-done((bf16[64,2304]{1,0:T(8,128)(2,1)S(1)}, bf16[64,2304]{1,0:T(8,128)(2,1)S(1)}, u32[]{:S(2)}, u32[]{:S(2)}) %collective-permute-start.4) | collective-permute-done | bytes 294944 | tf_op jit(solution)/shard_map/ppermute | solution.py:57
  46.6 0.1 slice_add_fusion
  46.7 0.1 collective-permute-start.6
  46.8 0.1 fusion.3
  46.9 0.1 pad_maximum_fusion.1
  47.0 4.0 %attend.3 = (bf16[32,2048]{1,0:T(8,128)(2,1)S(1)}, bf16[2048,2048]{1,0:T(8,128)(2,1)S(1)}) custom-call(s32[8]{0:T(128)S(1)} %copy-done, f32[32,2432]{1,0:T(8,128)S(1)} %slice_add_fusion.1.refs_0_, f32[32,128]{1,0:T(8,128)S(1)} %slice.48.refs_1_, f32[32,128]{1,0:T(8,128)S(1)} %get-tuple-element.62.refs_2_, f32[32,128]{1,0:T(8,128)S(1)} %get-tuple-element.63.refs_3_, ...), custom_call_target="tpu_custom_call" | custom-call | tf_op jit(solution)/shard_map/attend/pallas_call | solution.py:281
  51.1 2.1 %collective-permute-start.15 = (bf16[32,2048]{1,0:T(8,128)(2,1)S(1)}, bf16[32,2048]{1,0:T(8,128)(2,1)S(1)}, u32[]{:S(2)}, u32[]{:S(2)}) collective-permute-start(bf16[32,2048]{1,0:T(8,128)(2,1)S(1)} %get-tuple-element.55.refs_0_), channel_id=1, source_target_pairs={{0,4},{1,5},{2,6},{3,7},{4,0},{5,1},{6,2},{7,3},{8,12},{9,13},{10,... | collective-permute-start | bytes 393224 | tf_op jit(solution)/shard_map/ppermute | solution.py:57
  53.1 0.2 collective-permute-done.6
  53.3 1.4 %collective-permute-start.14 = (bf16[32,2048]{1,0:T(8,128)(2,1)S(1)}, bf16[32,2048]{1,0:T(8,128)(2,1)S(1)}, u32[]{:S(2)}, u32[]{:S(2)}) collective-permute-start(bf16[32,2048]{1,0:T(8,128)(2,1)S(1)} %get-tuple-element.55.refs_0_), channel_id=1, source_target_pairs={{0,8},{1,9},{2,10},{3,11},{4,12},{5,13},{6,14},{7,15},{8,0},{9,1},... | collective-permute-start | bytes 393224 | tf_op jit(solution)/shard_map/ppermute | solution.py:57
  54.7 2.7 %attend.2.refs_0_ = bf16[32,2048]{1,0:T(8,128)(2,1)S(1)} custom-call(s32[8]{0:T(128)S(1)} %copy-done, f32[32,2304]{1,0:T(8,128)S(1)} %slice_add_fusion.2.refs_0_, f32[32,128]{1,0:T(8,128)S(1)} %slice.48.refs_1_, f32[32,128]{1,0:T(8,128)S(1)} %get-tuple-element.62.refs_2_, f32[32,128]{1,0:T(8,128)S(1)} %get-tuple-element.63.refs_3_, ...), custom_call_target="tpu_custom_call" | custom-call | tf_op jit(solution)/shard_map/attend/pallas_call | solution.py:281
  57.5 1.8 %collective-permute-start.10 = (bf16[32,2048]{1,0:T(8,128)(2,1)S(1)}, bf16[32,2048]{1,0:T(8,128)(2,1)S(1)}, u32[]{:S(2)}, u32[]{:S(2)}) collective-permute-start(bf16[32,2048]{1,0:T(8,128)(2,1)S(1)} %attend.2.refs_0_), channel_id=1, source_target_pairs={{0,2},{1,5},{2,0},{3,7},{4,6},{5,1},{6,4},{7,3},{8,10},{9,13},{10,... | collective-permute-start | bytes 393224 | tf_op jit(solution)/shard_map/ppermute | solution.py:57
  59.3 1.2 %collective-permute-start.7 = (bf16[32,2048]{1,0:T(8,128)(2,1)S(1)}, bf16[32,2048]{1,0:T(8,128)(2,1)S(1)}, u32[]{:S(2)}, u32[]{:S(2)}) collective-permute-start(bf16[32,2048]{1,0:T(8,128)(2,1)S(1)} %attend.2.refs_0_), channel_id=1, source_target_pairs={{0,8},{1,9},{2,10},{3,11},{4,12},{5,13},{6,14},{7,15},{8,0},{9,1},... | collective-permute-start | bytes 393224 | tf_op jit(solution)/shard_map/ppermute | solution.py:57
  60.4 2.8 %collective-permute-start.8 = (bf16[32,2048]{1,0:T(8,128)(2,1)S(1)}, bf16[32,2048]{1,0:T(8,128)(2,1)S(1)}, u32[]{:S(2)}, u32[]{:S(2)}) collective-permute-start(bf16[32,2048]{1,0:T(8,128)(2,1)S(1)} %attend.2.refs_0_), channel_id=1, source_target_pairs={{0,4},{1,3},{2,6},{3,1},{4,0},{5,7},{6,2},{7,5},{8,12},{9,11},{10,... | collective-permute-start | bytes 393224 | tf_op jit(solution)/shard_map/ppermute | solution.py:57
  63.3 0.0 collective-permute-done.15.refs_2_
  63.3 0.1 collective-permute-start.17
  63.4 0.0 collective-permute-done.14.refs_1_
  63.4 0.1 collective-permute-start.16
  63.5 0.0 collective-permute-done.10.refs_4_
  63.5 2.1 %collective-permute-start.19 = (bf16[32,2048]{1,0:T(8,128)(2,1)S(1)}, bf16[32,2048]{1,0:T(8,128)(2,1)S(1)}, u32[]{:S(2)}, u32[]{:S(2)}) collective-permute-start(bf16[32,2048]{1,0:T(8,128)(2,1)S(1)} %collective-permute-done.15.refs_2_), channel_id=1, source_target_pairs={{0,2},{1,3},{2,0},{3,1},{4,6},{5,7},{6,4},{7,5},{8,10},{9,11},{10,... | collective-permute-start | bytes 393224 | tf_op jit(solution)/shard_map/ppermute | solution.py:57
  65.6 0.0 collective-permute-done.7.refs_1_
  65.6 4.8 %collective-permute-start.9 = (bf16[32,2048]{1,0:T(8,128)(2,1)S(1)}, bf16[32,2048]{1,0:T(8,128)(2,1)S(1)}, u32[]{:S(2)}, u32[]{:S(2)}) collective-permute-start(bf16[32,2048]{1,0:T(8,128)(2,1)S(1)} %collective-permute-done.7.refs_1_), channel_id=1, source_target_pairs={{0,4},{1,3},{2,6},{3,1},{4,0},{5,7},{6,2},{7,5},{8,12},{9,11},{10,... | collective-permute-start | bytes 393224 | tf_op jit(solution)/shard_map/ppermute | solution.py:57
  70.5 0.0 collective-permute-done.8.refs_2_
  70.5 0.0 collective-permute-start.12
  70.5 0.0 collective-permute-done.17.refs_4_
  70.5 2.0 %collective-permute-start.18 = (bf16[32,2048]{1,0:T(8,128)(2,1)S(1)}, bf16[32,2048]{1,0:T(8,128)(2,1)S(1)}, u32[]{:S(2)}, u32[]{:S(2)}) collective-permute-start(bf16[32,2048]{1,0:T(8,128)(2,1)S(1)} %collective-permute-done.14.refs_1_), channel_id=1, source_target_pairs={{0,2},{1,3},{2,0},{3,1},{4,6},{5,7},{6,4},{7,5},{8,10},{9,11},{10,... | collective-permute-start | bytes 393224 | tf_op jit(solution)/shard_map/ppermute | solution.py:57
  72.5 0.0 collective-permute-done.16.refs_3_
  72.5 0.1 collective-permute-start.20
  72.6 0.0 collective-permute-done.19.refs_6_
  72.6 2.0 %collective-permute-start.11 = (bf16[32,2048]{1,0:T(8,128)(2,1)S(1)}, bf16[32,2048]{1,0:T(8,128)(2,1)S(1)}, u32[]{:S(2)}, u32[]{:S(2)}) collective-permute-start(bf16[32,2048]{1,0:T(8,128)(2,1)S(1)} %collective-permute-done.7.refs_1_), channel_id=1, source_target_pairs={{0,2},{1,5},{2,0},{3,7},{4,6},{5,1},{6,4},{7,3},{8,10},{9,13},{10,... | collective-permute-start | bytes 393224 | tf_op jit(solution)/shard_map/ppermute | solution.py:57
  74.5 0.0 collective-permute-done.9.refs_3_
  74.5 0.1 collective-permute-start.13
  74.6 2.2 %collective-permute-done.18.refs_5_ = bf16[32,2048]{1,0:T(8,128)(2,1)S(1)} collective-permute-done((bf16[32,2048]{1,0:T(8,128)(2,1)S(1)}, bf16[32,2048]{1,0:T(8,128)(2,1)S(1)}, u32[]{:S(2)}, u32[]{:S(2)}) %collective-permute-start.18) | collective-permute-done | bytes 131104 | tf_op jit(solution)/shard_map/ppermute | solution.py:57
  76.8 1.4 %collective-permute-done.20.refs_7_ = bf16[32,2048]{1,0:T(8,128)(2,1)S(1)} collective-permute-done((bf16[32,2048]{1,0:T(8,128)(2,1)S(1)}, bf16[32,2048]{1,0:T(8,128)(2,1)S(1)}, u32[]{:S(2)}, u32[]{:S(2)}) %collective-permute-start.20) | collective-permute-done | bytes 131104 | tf_op jit(solution)/shard_map/ppermute | solution.py:57
  78.3 3.8 %combine.2.refs_8_ = f32[256,2048]{1,0:T(8,128)S(1)} custom-call(bf16[32,2048]{1,0:T(8,128)(2,1)S(1)} %get-tuple-element.55.refs_0_, bf16[32,2048]{1,0:T(8,128)(2,1)S(1)} %collective-permute-done.14.refs_1_, bf16[32,2048]{1,0:T(8,128)(2,1)S(1)} %collective-permute-done.15.refs_2_, bf16[32,2048]{1,0:T(8,128)(2,1)S(1)} %collective-permute-done.16.refs_3_, ...), custom_call_target="tpu_custom_call" | custom-call | tf_op jit(solution)/shard_map/combine/pallas_call | solution.py:402
  82.1 0.0 collective-permute-done.12.refs_6_
  82.1 0.0 collective-permute-done.11.refs_5_
  82.1 0.0 collective-permute-done.13.refs_7_
  82.1 3.9 %combine.3 = (bf16[128,2048]{1,0:T(8,128)(2,1)S(1)}, f32[128,2048]{1,0:T(8,128)S(1)}) custom-call(bf16[32,2048]{1,0:T(8,128)(2,1)S(1)} %attend.2.refs_0_, bf16[32,2048]{1,0:T(8,128)(2,1)S(1)} %collective-permute-done.7.refs_1_, bf16[32,2048]{1,0:T(8,128)(2,1)S(1)} %collective-permute-done.8.refs_2_, bf16[32,2048]{1,0:T(8,128)(2,1)S(1)} %collective-permute-done.9.refs_3_, ...), custom_call_target="tpu_custom_call" | custom-call | tf_op jit(solution)/shard_map/combine/pallas_call | solution.py:402
  86.0 0.1 collective-permute-start.21
  86.1 1.9 %collective-permute-done.21 = bf16[128,2048]{1,0:T(8,128)(2,1)S(1)} collective-permute-done((bf16[128,2048]{1,0:T(8,128)(2,1)S(1)}, bf16[128,2048]{1,0:T(8,128)(2,1)S(1)}, u32[]{:S(2)}, u32[]{:S(2)}) %collective-permute-start.21) | collective-permute-done | bytes 524320 | tf_op jit(solution)/shard_map/ppermute | solution.py:530
  88.0 0.9 %add_convert_fusion = bf16[128,2048]{1,0:T(8,128)(2,1)} fusion(f32[128,2048]{1,0:T(8,128)S(1)} %get-tuple-element.57, bf16[128,2048]{1,0:T(8,128)(2,1)S(1)} %collective-permute-done.21), kind=kLoop, calls=%fused_computation.3 | loop fusion | flops 786432 | bytes 2097152 | tf_op jit(solution)/shard_map/convert_element_type | solution.py:531
  (9 shorter events, 0.2 us)
Async XLA Ops:
  4.4 7.7 %collective-permute-start = (bf16[128,1152]{1,0:T(8,128)(2,1)S(1)}, bf16[128,1152]{1,0:T(8,128)(2,1)S(1)}, u32[]{:S(2)}, u32[]{:S(2)}) collective-permute-start(bf16[128,1152]{1,0:T(8,128)(2,1)S(1)} %get-tuple-element.33), channel_id=1, source_target_pairs={{0,2},{1,5},{2,0},{3,7},{4,6},{5,1},{6,4},{7,3},{8,10},{9,13},{10,... | collective-permute-start | bytes 884744 | tf_op jit(solution)/shard_map/ppermute | solution.py:57
  11.3 7.1 %collective-permute-start.1 = (bf16[128,1280]{1,0:T(8,128)(2,1)S(1)}, bf16[128,1280]{1,0:T(8,128)(2,1)S(1)}, u32[]{:S(2)}, u32[]{:S(2)}) collective-permute-start(bf16[128,1280]{1,0:T(8,128)(2,1)S(1)} %get-tuple-element.35), channel_id=1, source_target_pairs={{0,2},{1,5},{2,0},{3,7},{4,6},{5,1},{6,4},{7,3},{8,10},{9,13},{10,... | collective-permute-start | bytes 983048 | tf_op jit(solution)/shard_map/ppermute | solution.py:57
  12.2 9.0 %copy-start = (s32[8]{0:T(128)S(1)}, s32[8]{0:T(128)}, u32[]{:S(2)}) copy-start(s32[8]{0:T(128)} %length_ref.3) | copy-start | bytes 100
  18.5 10.5 %collective-permute-start.3 = (bf16[64,2432]{1,0:T(8,128)(2,1)S(1)}, bf16[64,2432]{1,0:T(8,128)(2,1)}, u32[]{:S(2)}, u32[]{:S(2)}) collective-permute-start(bf16[64,2432]{1,0:T(8,128)(2,1)S(1)} %fusion.1), channel_id=1, source_target_pairs={{0,8},{1,3},{2,10},{3,1},{4,12},{5,7},{6,14},{7,5},{8,0},{9,11},{1... | collective-permute-start | bytes 933896 | tf_op jit(solution)/shard_map/ppermute | solution.py:57
  21.3 11.1 %collective-permute-start.2 = (bf16[128,2304]{1,0:T(8,128)(2,1)S(1)}, bf16[128,2304]{1,0:T(8,128)(2,1)S(1)}, u32[]{:S(2)}, u32[]{:S(2)}) collective-permute-start(bf16[128,2304]{1,0:T(8,128)(2,1)S(1)} %get-tuple-element.43), channel_id=1, source_target_pairs={{0,2},{1,5},{2,0},{3,7},{4,6},{5,1},{6,4},{7,3},{8,10},{9,13},{10,... | collective-permute-start | bytes 1769480 | tf_op jit(solution)/shard_map/ppermute | solution.py:57
  30.1 9.3 %collective-permute-start.5 = (bf16[32,2432]{1,0:T(8,128)(2,1)S(1)}, bf16[32,2432]{1,0:T(8,128)(2,1)S(1)}, u32[]{:S(2)}, u32[]{:S(2)}) collective-permute-start(bf16[32,2432]{1,0:T(8,128)(2,1)S(1)} %slice.64), channel_id=1, source_target_pairs={{0,4},{1,9},{2,6},{3,11},{4,0},{5,13},{6,2},{7,15},{8,12},{9,1},{1... | collective-permute-start | bytes 466952 | tf_op jit(solution)/shard_map/ppermute | solution.py:57
  32.6 14.0 %collective-permute-start.4 = (bf16[64,2304]{1,0:T(8,128)(2,1)S(1)}, bf16[64,2304]{1,0:T(8,128)(2,1)S(1)}, u32[]{:S(2)}, u32[]{:S(2)}) collective-permute-start(bf16[64,2304]{1,0:T(8,128)(2,1)S(1)} %slice.63), channel_id=1, source_target_pairs={{0,8},{1,3},{2,10},{3,1},{4,12},{5,7},{6,14},{7,5},{8,0},{9,11},{1... | collective-permute-start | bytes 884744 | tf_op jit(solution)/shard_map/ppermute | solution.py:57
  46.7 6.6 %collective-permute-start.6 = (bf16[32,2304]{1,0:T(8,128)(2,1)S(1)}, bf16[32,2304]{1,0:T(8,128)(2,1)S(1)}, u32[]{:S(2)}, u32[]{:S(2)}) collective-permute-start(bf16[32,2304]{1,0:T(8,128)(2,1)S(1)} %slice.65), channel_id=1, source_target_pairs={{0,4},{1,9},{2,6},{3,11},{4,0},{5,13},{6,2},{7,15},{8,12},{9,1},{1... | collective-permute-start | bytes 442376 | tf_op jit(solution)/shard_map/ppermute | solution.py:57
  51.1 12.2 %collective-permute-start.15 = (bf16[32,2048]{1,0:T(8,128)(2,1)S(1)}, bf16[32,2048]{1,0:T(8,128)(2,1)S(1)}, u32[]{:S(2)}, u32[]{:S(2)}) collective-permute-start(bf16[32,2048]{1,0:T(8,128)(2,1)S(1)} %get-tuple-element.55.refs_0_), channel_id=1, source_target_pairs={{0,4},{1,5},{2,6},{3,7},{4,0},{5,1},{6,2},{7,3},{8,12},{9,13},{10,... | collective-permute-start | bytes 393224 | tf_op jit(solution)/shard_map/ppermute | solution.py:57
  53.3 10.1 %collective-permute-start.14 = (bf16[32,2048]{1,0:T(8,128)(2,1)S(1)}, bf16[32,2048]{1,0:T(8,128)(2,1)S(1)}, u32[]{:S(2)}, u32[]{:S(2)}) collective-permute-start(bf16[32,2048]{1,0:T(8,128)(2,1)S(1)} %get-tuple-element.55.refs_0_), channel_id=1, source_target_pairs={{0,8},{1,9},{2,10},{3,11},{4,12},{5,13},{6,14},{7,15},{8,0},{9,1},... | collective-permute-start | bytes 393224 | tf_op jit(solution)/shard_map/ppermute | solution.py:57
  57.5 6.1 %collective-permute-start.10 = (bf16[32,2048]{1,0:T(8,128)(2,1)S(1)}, bf16[32,2048]{1,0:T(8,128)(2,1)S(1)}, u32[]{:S(2)}, u32[]{:S(2)}) collective-permute-start(bf16[32,2048]{1,0:T(8,128)(2,1)S(1)} %attend.2.refs_0_), channel_id=1, source_target_pairs={{0,2},{1,5},{2,0},{3,7},{4,6},{5,1},{6,4},{7,3},{8,10},{9,13},{10,... | collective-permute-start | bytes 393224 | tf_op jit(solution)/shard_map/ppermute | solution.py:57
  59.3 6.4 %collective-permute-start.7 = (bf16[32,2048]{1,0:T(8,128)(2,1)S(1)}, bf16[32,2048]{1,0:T(8,128)(2,1)S(1)}, u32[]{:S(2)}, u32[]{:S(2)}) collective-permute-start(bf16[32,2048]{1,0:T(8,128)(2,1)S(1)} %attend.2.refs_0_), channel_id=1, source_target_pairs={{0,8},{1,9},{2,10},{3,11},{4,12},{5,13},{6,14},{7,15},{8,0},{9,1},... | collective-permute-start | bytes 393224 | tf_op jit(solution)/shard_map/ppermute | solution.py:57
  60.4 10.0 %collective-permute-start.8 = (bf16[32,2048]{1,0:T(8,128)(2,1)S(1)}, bf16[32,2048]{1,0:T(8,128)(2,1)S(1)}, u32[]{:S(2)}, u32[]{:S(2)}) collective-permute-start(bf16[32,2048]{1,0:T(8,128)(2,1)S(1)} %attend.2.refs_0_), channel_id=1, source_target_pairs={{0,4},{1,3},{2,6},{3,1},{4,0},{5,7},{6,2},{7,5},{8,12},{9,11},{10,... | collective-permute-start | bytes 393224 | tf_op jit(solution)/shard_map/ppermute | solution.py:57
  63.3 7.2 %collective-permute-start.17 = (bf16[32,2048]{1,0:T(8,128)(2,1)S(1)}, bf16[32,2048]{1,0:T(8,128)(2,1)S(1)}, u32[]{:S(2)}, u32[]{:S(2)}) collective-permute-start(bf16[32,2048]{1,0:T(8,128)(2,1)S(1)} %get-tuple-element.55.refs_0_), channel_id=1, source_target_pairs={{0,2},{1,3},{2,0},{3,1},{4,6},{5,7},{6,4},{7,5},{8,10},{9,11},{10,... | collective-permute-start | bytes 393224 | tf_op jit(solution)/shard_map/ppermute | solution.py:57
  63.4 9.1 %collective-permute-start.16 = (bf16[32,2048]{1,0:T(8,128)(2,1)S(1)}, bf16[32,2048]{1,0:T(8,128)(2,1)S(1)}, u32[]{:S(2)}, u32[]{:S(2)}) collective-permute-start(bf16[32,2048]{1,0:T(8,128)(2,1)S(1)} %collective-permute-done.14.refs_1_), channel_id=1, source_target_pairs={{0,4},{1,5},{2,6},{3,7},{4,0},{5,1},{6,2},{7,3},{8,12},{9,13},{10,... | collective-permute-start | bytes 393224 | tf_op jit(solution)/shard_map/ppermute | solution.py:57
  63.5 9.1 %collective-permute-start.19 = (bf16[32,2048]{1,0:T(8,128)(2,1)S(1)}, bf16[32,2048]{1,0:T(8,128)(2,1)S(1)}, u32[]{:S(2)}, u32[]{:S(2)}) collective-permute-start(bf16[32,2048]{1,0:T(8,128)(2,1)S(1)} %collective-permute-done.15.refs_2_), channel_id=1, source_target_pairs={{0,2},{1,3},{2,0},{3,1},{4,6},{5,7},{6,4},{7,5},{8,10},{9,11},{10,... | collective-permute-start | bytes 393224 | tf_op jit(solution)/shard_map/ppermute | solution.py:57
  65.6 8.9 %collective-permute-start.9 = (bf16[32,2048]{1,0:T(8,128)(2,1)S(1)}, bf16[32,2048]{1,0:T(8,128)(2,1)S(1)}, u32[]{:S(2)}, u32[]{:S(2)}) collective-permute-start(bf16[32,2048]{1,0:T(8,128)(2,1)S(1)} %collective-permute-done.7.refs_1_), channel_id=1, source_target_pairs={{0,4},{1,3},{2,6},{3,1},{4,0},{5,7},{6,2},{7,5},{8,12},{9,11},{10,... | collective-permute-start | bytes 393224 | tf_op jit(solution)/shard_map/ppermute | solution.py:57
  70.5 11.6 %collective-permute-start.12 = (bf16[32,2048]{1,0:T(8,128)(2,1)S(1)}, bf16[32,2048]{1,0:T(8,128)(2,1)S(1)}, u32[]{:S(2)}, u32[]{:S(2)}) collective-permute-start(bf16[32,2048]{1,0:T(8,128)(2,1)S(1)} %collective-permute-done.8.refs_2_), channel_id=1, source_target_pairs={{0,2},{1,5},{2,0},{3,7},{4,6},{5,1},{6,4},{7,3},{8,10},{9,13},{10,... | collective-permute-start | bytes 393224 | tf_op jit(solution)/shard_map/ppermute | solution.py:57
  70.5 6.4 %collective-permute-start.18 = (bf16[32,2048]{1,0:T(8,128)(2,1)S(1)}, bf16[32,2048]{1,0:T(8,128)(2,1)S(1)}, u32[]{:S(2)}, u32[]{:S(2)}) collective-permute-start(bf16[32,2048]{1,0:T(8,128)(2,1)S(1)} %collective-permute-done.14.refs_1_), channel_id=1, source_target_pairs={{0,2},{1,3},{2,0},{3,1},{4,6},{5,7},{6,4},{7,5},{8,10},{9,11},{10,... | collective-permute-start | bytes 393224 | tf_op jit(solution)/shard_map/ppermute | solution.py:57
  72.5 5.7 %collective-permute-start.20 = (bf16[32,2048]{1,0:T(8,128)(2,1)S(1)}, bf16[32,2048]{1,0:T(8,128)(2,1)S(1)}, u32[]{:S(2)}, u32[]{:S(2)}) collective-permute-start(bf16[32,2048]{1,0:T(8,128)(2,1)S(1)} %collective-permute-done.16.refs_3_), channel_id=1, source_target_pairs={{0,2},{1,3},{2,0},{3,1},{4,6},{5,7},{6,4},{7,5},{8,10},{9,11},{10,... | collective-permute-start | bytes 393224 | tf_op jit(solution)/shard_map/ppermute | solution.py:57
  72.6 9.5 %collective-permute-start.11 = (bf16[32,2048]{1,0:T(8,128)(2,1)S(1)}, bf16[32,2048]{1,0:T(8,128)(2,1)S(1)}, u32[]{:S(2)}, u32[]{:S(2)}) collective-permute-start(bf16[32,2048]{1,0:T(8,128)(2,1)S(1)} %collective-permute-done.7.refs_1_), channel_id=1, source_target_pairs={{0,2},{1,5},{2,0},{3,7},{4,6},{5,1},{6,4},{7,3},{8,10},{9,13},{10,... | collective-permute-start | bytes 393224 | tf_op jit(solution)/shard_map/ppermute | solution.py:57
  74.5 7.5 %collective-permute-start.13 = (bf16[32,2048]{1,0:T(8,128)(2,1)S(1)}, bf16[32,2048]{1,0:T(8,128)(2,1)S(1)}, u32[]{:S(2)}, u32[]{:S(2)}) collective-permute-start(bf16[32,2048]{1,0:T(8,128)(2,1)S(1)} %collective-permute-done.9.refs_3_), channel_id=1, source_target_pairs={{0,2},{1,5},{2,0},{3,7},{4,6},{5,1},{6,4},{7,3},{8,10},{9,13},{10,... | collective-permute-start | bytes 393224 | tf_op jit(solution)/shard_map/ppermute | solution.py:57
  86.0 2.0 %collective-permute-start.21 = (bf16[128,2048]{1,0:T(8,128)(2,1)S(1)}, bf16[128,2048]{1,0:T(8,128)(2,1)S(1)}, u32[]{:S(2)}, u32[]{:S(2)}) collective-permute-start(bf16[128,2048]{1,0:T(8,128)(2,1)S(1)} %get-tuple-element.58), channel_id=1, source_target_pairs={{0,1},{1,0},{2,3},{3,2},{4,5},{5,4},{6,7},{7,6},{8,9},{9,8},{10,11... | collective-permute-start | bytes 1572872 | tf_op jit(solution)/shard_map/ppermute | solution.py:530

commit v9 on v6

--- a/solution.py
+++ b/solution.py
@@ -419,73 +419,79 @@
 
     share = q_cols // 2
     orders = bit_orders(n)
+
+    def start(stage, send):
+        return exchange(send, n, cores, stage, orders)
+
+    def added(stage, keep, other):
+        value = keep + other.astype(jnp.float32)
+        low = value.shape[0] // 2 if stage < levels - 1 else 0
+        return value[low:].astype(jnp.bfloat16), value[:low] if low else value
+
     send_a, keep_a, x = column_part(0, share, None)
     x = after(x, send_a)
-    other_a = exchange(send_a, n, cores, 0, orders)
+    other_a = start(0, send_a)
     send_b, keep_b = column_part(share, share, 0)
     x = after(x, send_b)
-    other_b = exchange(send_b, n, cores, 0, orders)
+    other_b = start(0, send_b)
     sum_a = keep_a + other_a.astype(jnp.float32)
     x = after(x, sum_a)
-    later = []
-    for chunk in range(1, CHUNKS):
-        later.append(column_part(chunk * q_cols, q_cols, chunk * kv))
-    other_b = after(other_b, *(send_c for send_c, _ in later))
+    send_c, keep_c = column_part(q_cols, share, None)
+    other_b = after(other_b, send_c)
     first = jnp.concatenate([sum_a, keep_b + other_b.astype(jnp.float32)], axis=1)
     half = first.shape[0] // 2
-    send = first[half:].astype(jnp.bfloat16)
-    flows = [[1, first[:half], send]]
-    for send_c, keep_c in later:
-        flows.append([0, keep_c, after(send_c, flows[-1][2])])
-
-    def start(flow):
-        return exchange(flow[2], n, cores, flow[0], orders)
-
-    def finish(flow, other, *earlier):
-        stage, keep, _ = flow
-        if earlier:
-            other = after(other, *earlier)
-        value = keep + other.astype(jnp.float32)
-        low = value.shape[0] // 2 if stage < levels - 1 else 0
-        flow[:] = stage + 1, value[:low] if low else value, value[low:].astype(jnp.bfloat16)
-
-    lead, follow = flows
+    send, keep = first[half:].astype(jnp.bfloat16), first[:half]
+    x = after(x, send, send_c)
+    send_d, keep_d = column_part(q_cols + share, share, kv)
+
+    other = after(start(1, send), send_d)
+    send, keep = added(1, keep, other)
+    send_1 = after(jnp.concatenate([send_c, send_d], axis=1), send)
+    keep_1 = jnp.concatenate([keep_c, keep_d], axis=1)
+    other_1 = start(0, send_1)
     w_rows = w_out.shape[0] // CHUNKS
-    weights = [fetch_rows(after(w_out, lead[2], follow[2]), 0, w_rows)]
-    while follow[0] < levels:
-        pending = [start(flow) for flow in flows if flow[0] < levels]
-        if lead[0] == levels:
-            finish(follow, pending[0])
-        elif lead[0] == levels - 1:
-            cache_keys, cache_values = fetch(*after((cache_keys, cache_values), follow[2]))
-            finish(lead, pending[0], cache_keys, cache_values)
-            finish(follow, pending[1], lead[1])
-        else:
-            finish(lead, pending[0], *weights)
-            finish(follow, pending[1], lead[2])
-    sums = [flow[1] for flow in flows]
-    squares = sums[0][:, share : share + 128]
+    w_first = fetch_rows(after(w_out, send_1), 0, w_rows)
+    cache_keys, cache_values = fetch(*after((cache_keys, cache_values), w_first))
+    for stage in range(2, levels):
+        other = start(stage, send)
+        if stage == 2:
+            other = after(other, cache_keys, cache_values)
+        send, keep = added(stage, keep, other)
+    sum_0 = keep
+    other_1 = after(other_1, sum_0)
+    send_1, keep_1 = added(0, keep_1, other_1)
+    sum_0 = after(sum_0, send_1)
+    squares = sum_0[:, share : share + 128]
     plain = [h * HD for h in range(q_cols // HD)]
     offsets = [[at if at < share else at + 128 for at in plain], plain]
     kv_offsets = [q_cols + 128, q_cols]
 
-    attentions = []
-    for chunk in range(CHUNKS):
-        attentions.append(
-            attend(
-                chunk,
-                offsets[chunk],
-                kv_offsets[chunk],
-                sums[chunk],
-                squares,
-                cosine,
-                sine,
-                cache_keys,
-                cache_values,
-                cache_lengths,
-            )
+    def attended(chunk, total):
+        return attend(
+            chunk,
+            offsets[chunk],
+            kv_offsets[chunk],
+            total,
+            squares,
+            cosine,
+            sine,
+            cache_keys,
+            cache_values,
+            cache_lengths,
         )
-    weights.append(fetch_rows(after(w_out, attentions[1]), w_rows, w_rows))
+
+    attentions = [attended(0, sum_0)]
+    other_1 = after(start(1, send_1), attentions[0])
+    send_1, keep_1 = added(1, keep_1, other_1)
+    w_second = fetch_rows(after(w_out, send_1), w_rows, w_rows)
+    for stage in range(2, levels):
+        other_1 = start(stage, send_1)
+        if stage == 2:
+            other_1 = after(other_1, w_second)
+        send_1, keep_1 = added(stage, keep_1, other_1)
+    sums = [sum_0, keep_1]
+    weights = [w_first, w_second]
+    attentions.append(attended(1, sums[1]))
     gathered = []
     for chunk in range(CHUNKS):
         slots = [attentions[chunk]]
@@ -494,8 +500,6 @@
             source = slots[slot - (1 << top)]
             if slot == 1 and chunk == 0:
                 source = after(source, sums[1])
-            if slot == 3 and chunk == 1:
-                source = after(source, weights[1])
             slots.append(
                 exchange(source, n, cores, levels - 1 - top, gather_orders(n, chunk))
             )

time: 83.1 us -> 89.9 us (1.082)
  waiting for transfers between devices: 14.8 us -> 22 us
  starting transfers between devices: 27.8 us -> 26 us
  Pallas kernels: 37.4 us -> 38.8 us
    ppermute x21, waiting for transfers between devices: 12.9 us -> 20.1 us  [exchange(): return lax.ppermute(value, ('gx', 'gy'), pairs)]
    ppermute x21, starting transfers between devices: 27.7 us -> 25.9 us  [exchange(): return lax.ppermute(value, ('gx', 'gy'), pairs)]
    pallas_call x3 -> x4, Pallas kernels: 13.8 us -> 15.1 us  [project(): pl.pallas_call(functools.partial(project_kernel, n, q_start, kv_start, fi...]
  transfers between devices with their start and end apart: 22 -> 22, of which waited for: 10 -> 14; matrix products, arithmetic and copies ran while one was open for 2% -> 1% of each run, Pallas kernels for 35% -> 34%
where the time goes in v9:
time: 89.9 us; the launch traced here: 89.8 us
  Pallas kernels  38.8 us (43%)
  starting transfers between devices  26 us (29%)
  waiting for transfers between devices  22 us (24%)
  other arithmetic  2.67 us (3%)
    ppermute x21, starting transfers between devices, exchange(): return lax.ppermute(value, ('gx', 'gy'), pairs)  25.9 us
    ppermute x21, waiting for transfers between devices, exchange(): return lax.ppermute(value, ('gx', 'gy'), pairs)  20.1 us
    pallas_call x4, Pallas kernels, project(): pl.pallas_call(functools.partial(project_kernel, n, q_start, kv_start, fi...  15.1 us
    pallas_call x2, Pallas kernels, combine(): pl.pallas_call(functools.partial(combine_kernel, n, block, chunk), out_sh...  7.55 us
    pallas_call x2, Pallas kernels, fetch_rows(): pl.pallas_call(functools.partial(fetch_rows_kernel, start, pieces), out_s...  7 us
    pallas_call x2, Pallas kernels, attend(): pl.pallas_call(functools.partial(attend_kernel, chunk, offsets, kv_offset...  5.62 us
    pallas_call x1, Pallas kernels, fetch(): pl.pallas_call(functools.partial(fetch_kernel, len(arrays), pieces), out_...  3.48 us
    ppermute x1, waiting for transfers between devices, shards(): other = lax.ppermute(send, 'gy', [(0, 1), (1, 0)])  1.9 us
  transfers between devices with their start and end apart: 22, of which 14 were waited for; matrix products, arithmetic and copies ran while one was open for 1% of the time, Pallas kernels for 34%

profile of v9, /device:TPU:0, one launch (start us, length us, event | category | flops | bytes accessed | tf_op | source)
XLA Modules:
  0.0 89.8 jit_solution(2094358162245406535)
XLA Ops:
  0.0 4.4 %project.4 = (bf16[128,1152]{1,0:T(8,128)(2,1)S(1)}, f32[128,1152]{1,0:T(8,128)S(1)}, bf16[256,2048]{1,0:T(8,128)(2,1)S(1)}) custom-call(bf16[256,2048]{1,0:T(8,128)(2,1)} %refs_0_.1, f32[1,2048]{1,0:T(1,128)} %bitcast.1, bf16[2048,4096]{1,0:T(8,128)(2,1)} %refs_1_.5, bf16[2048,256]{1,0:T(8,128)(2,1)} %refs_2_.7, bf16[2048,256]{1,0:T(8,128)(2,1)} %refs_3_.7), custom_call_target="tpu_custom_call" | custom-call | tf_op jit(solution)/shard_map/project/pallas_call | solution.py:159
  4.4 3.0 %collective-permute-start = (bf16[128,1152]{1,0:T(8,128)(2,1)S(1)}, bf16[128,1152]{1,0:T(8,128)(2,1)S(1)}, u32[]{:S(2)}, u32[]{:S(2)}) collective-permute-start(bf16[128,1152]{1,0:T(8,128)(2,1)S(1)} %get-tuple-element.36), channel_id=1, source_target_pairs={{0,2},{1,5},{2,0},{3,7},{4,6},{5,1},{6,4},{7,3},{8,10},{9,13},{10,... | collective-permute-start | bytes 884744 | tf_op jit(solution)/shard_map/ppermute | solution.py:55
  7.4 3.9 %project.5 = (bf16[128,1280]{1,0:T(8,128)(2,1)S(1)}, f32[128,1280]{1,0:T(8,128)S(1)}) custom-call(bf16[256,2048]{1,0:T(8,128)(2,1)S(1)} %get-tuple-element.46.refs_0_, bf16[2048,4096]{1,0:T(8,128)(2,1)} %refs_1_.5, bf16[2048,256]{1,0:T(8,128)(2,1)} %refs_2_.7, bf16[2048,256]{1,0:T(8,128)(2,1)} %refs_3_.7), custom_call_target="tpu_custom_call" | custom-call | tf_op jit(solution)/shard_map/project/pallas_call | solution.py:159
  11.3 0.1 collective-permute-start.1
  11.4 0.8 collective-permute-done
  12.1 0.1 convert_add_fusion.1
  12.2 3.1 %project.6 = (bf16[128,1024]{1,0:T(8,128)(2,1)S(1)}, f32[128,1024]{1,0:T(8,128)S(1)}) custom-call(bf16[256,2048]{1,0:T(8,128)(2,1)S(1)} %get-tuple-element.46.refs_0_, bf16[2048,4096]{1,0:T(8,128)(2,1)} %refs_1_.5, bf16[2048,256]{1,0:T(8,128)(2,1)} %refs_2_.7, bf16[2048,256]{1,0:T(8,128)(2,1)} %refs_3_.7), custom_call_target="tpu_custom_call" | custom-call | tf_op jit(solution)/shard_map/project/pallas_call | solution.py:159
  15.2 3.2 %collective-permute-done.1 = bf16[128,1280]{1,0:T(8,128)(2,1)S(1)} collective-permute-done((bf16[128,1280]{1,0:T(8,128)(2,1)S(1)}, bf16[128,1280]{1,0:T(8,128)(2,1)S(1)}, u32[]{:S(2)}, u32[]{:S(2)}) %collective-permute-start.1) | collective-permute-done | bytes 327712 | tf_op jit(solution)/shard_map/ppermute | solution.py:55
  18.4 0.1 convert_add_fusion
  18.5 0.0 copy-start
  18.5 1.6 %collective-permute-start.2 = (bf16[64,2432]{1,0:T(8,128)(2,1)S(1)}, bf16[64,2432]{1,0:T(8,128)(2,1)}, u32[]{:S(2)}, u32[]{:S(2)}) collective-permute-start(bf16[64,2432]{1,0:T(8,128)(2,1)S(1)} %fusion.1), channel_id=1, source_target_pairs={{0,4},{1,3},{2,6},{3,1},{4,0},{5,7},{6,2},{7,5},{8,12},{9,11},{10,... | collective-permute-start | bytes 933896 | tf_op jit(solution)/shard_map/ppermute | solution.py:55
  20.2 0.1 add_convert_fusion.1
  20.2 0.1 convert_element_type.47
  20.3 3.9 %project.7 = (bf16[128,1280]{1,0:T(8,128)(2,1)S(1)}, f32[128,1280]{1,0:T(8,128)S(1)}) custom-call(bf16[256,2048]{1,0:T(8,128)(2,1)S(1)} %get-tuple-element.46.refs_0_, bf16[2048,4096]{1,0:T(8,128)(2,1)} %refs_1_.5, bf16[2048,256]{1,0:T(8,128)(2,1)} %refs_2_.7, bf16[2048,256]{1,0:T(8,128)(2,1)} %refs_3_.7), custom_call_target="tpu_custom_call" | custom-call | tf_op jit(solution)/shard_map/project/pallas_call | solution.py:159
  24.2 1.4 %collective-permute-done.2 = bf16[64,2432]{1,0:T(8,128)(2,1)} collective-permute-done((bf16[64,2432]{1,0:T(8,128)(2,1)S(1)}, bf16[64,2432]{1,0:T(8,128)(2,1)}, u32[]{:S(2)}, u32[]{:S(2)}) %collective-permute-start.2) | collective-permute-done | bytes 311328 | tf_op jit(solution)/shard_map/ppermute | solution.py:55
  25.6 1.0 %fusion.2 = f32[64,2432]{1,0:T(8,128)S(1)} fusion(f32[128,1280]{1,0:T(8,128)S(1)} %convert_add_fusion, f32[128,1152]{1,0:T(8,128)S(1)} %convert_add_fusion.1, bf16[64,2432]{1,0:T(8,128)(2,1)} %collective-permute-done.2), kind=kLoop, calls=%fused_computation.8 | loop fusion | flops 466944 | bytes 2179072 | tf_op jit(solution)/shard_map/add | solution.py:427
  26.7 2.7 %collective-permute-start.4 = (bf16[32,2432]{1,0:T(8,128)(2,1)S(1)}, bf16[32,2432]{1,0:T(8,128)(2,1)S(1)}, u32[]{:S(2)}, u32[]{:S(2)}) collective-permute-start(bf16[32,2432]{1,0:T(8,128)(2,1)S(1)} %slice.63), channel_id=1, source_target_pairs={{0,8},{1,9},{2,10},{3,11},{4,12},{5,13},{6,14},{7,15},{8,0},{9,1},... | collective-permute-start | bytes 466952 | tf_op jit(solution)/shard_map/ppermute | solution.py:55
  29.4 0.6 collective-permute-start.3
  29.9 3.5 %fetch_rows.2.refs_8_ = bf16[2048,2048]{1,0:T(8,128)(2,1)S(1)} custom-call(bf16[4096,2048]{1,0:T(8,128)(2,1)} %source.1), custom_call_target="tpu_custom_call" | custom-call | tf_op jit(solution)/shard_map/fetch_rows/pallas_call | solution.py:320
  33.4 3.5 %fetch.1 = (bf16[8,1024,256]{2,1,0:T(8,128)(2,1)S(1)}, bf16[8,1024,256]{2,1,0:T(8,128)(2,1)S(1)}) custom-call(bf16[8,1024,256]{2,1,0:T(8,128)(2,1)} %refs_0_.2, bf16[8,1024,256]{2,1,0:T(8,128)(2,1)} %refs_1_.6), custom_call_target="tpu_custom_call" | custom-call | tf_op jit(solution)/shard_map/fetch/pallas_call | solution.py:291
  36.9 0.0 collective-permute-done.4
  37.0 2.3 %collective-permute-done.3 = bf16[128,2304]{1,0:T(8,128)(2,1)S(1)} collective-permute-done((bf16[128,2304]{1,0:T(8,128)(2,1)S(1)}, bf16[128,2304]{1,0:T(8,128)(2,1)S(1)}, u32[]{:S(2)}, u32[]{:S(2)}) %collective-permute-start.3) | collective-permute-done | bytes 589856 | tf_op jit(solution)/shard_map/ppermute | solution.py:55
  39.3 0.1 maximum_add_fusion
  39.5 1.6 %collective-permute-start.5 = (bf16[64,2304]{1,0:T(8,128)(2,1)S(1)}, bf16[64,2304]{1,0:T(8,128)(2,1)S(1)}, u32[]{:S(2)}, u32[]{:S(2)}) collective-permute-start(bf16[64,2304]{1,0:T(8,128)(2,1)S(1)} %slice.62), channel_id=1, source_target_pairs={{0,4},{1,3},{2,6},{3,1},{4,0},{5,7},{6,2},{7,5},{8,12},{9,11},{10,... | collective-permute-start | bytes 884744 | tf_op jit(solution)/shard_map/ppermute | solution.py:55
  41.1 0.1 fusion.3
  41.3 0.1 pad_maximum_fusion.2
  41.3 2.9 %attend.2.refs_0_ = bf16[32,2048]{1,0:T(8,128)(2,1)S(1)} custom-call(s32[8]{0:T(128)S(1)} %copy-done, f32[32,2432]{1,0:T(8,128)S(1)} %slice_add_fusion.1.refs_0_, f32[32,128]{1,0:T(8,128)S(1)} %slice.37.refs_1_, f32[32,128]{1,0:T(8,128)S(1)} %get-tuple-element.68.refs_2_, f32[32,128]{1,0:T(8,128)S(1)} %get-tuple-element.69.refs_3_, ...), custom_call_target="tpu_custom_call" | custom-call | tf_op jit(solution)/shard_map/attend/pallas_call | solution.py:259
  44.2 2.0 %collective-permute-done.5 = bf16[64,2304]{1,0:T(8,128)(2,1)S(1)} collective-permute-done((bf16[64,2304]{1,0:T(8,128)(2,1)S(1)}, bf16[64,2304]{1,0:T(8,128)(2,1)S(1)}, u32[]{:S(2)}, u32[]{:S(2)}) %collective-permute-start.5) | collective-permute-done | bytes 294944 | tf_op jit(solution)/shard_map/ppermute | solution.py:55
  46.3 0.1 slice_add_fusion
  46.3 0.4 collective-permute-start.6
  46.7 1.6 %collective-permute-start.15 = (bf16[32,2048]{1,0:T(8,128)(2,1)S(1)}, bf16[32,2048]{1,0:T(8,128)(2,1)S(1)}, u32[]{:S(2)}, u32[]{:S(2)}) collective-permute-start(bf16[32,2048]{1,0:T(8,128)(2,1)S(1)} %attend.2.refs_0_), channel_id=1, source_target_pairs={{0,4},{1,5},{2,6},{3,7},{4,0},{5,1},{6,2},{7,3},{8,12},{9,13},{10,... | collective-permute-start | bytes 393224 | tf_op jit(solution)/shard_map/ppermute | solution.py:55
  48.3 3.5 %fetch_rows.3.refs_9_ = bf16[2048,2048]{1,0:T(8,128)(2,1)S(1)} custom-call(bf16[4096,2048]{1,0:T(8,128)(2,1)} %source.1), custom_call_target="tpu_custom_call" | custom-call | tf_op jit(solution)/shard_map/fetch_rows/pallas_call | solution.py:320
  51.8 4.7 %collective-permute-done.6 = bf16[32,2304]{1,0:T(8,128)(2,1)S(1)} collective-permute-done((bf16[32,2304]{1,0:T(8,128)(2,1)S(1)}, bf16[32,2304]{1,0:T(8,128)(2,1)S(1)}, u32[]{:S(2)}, u32[]{:S(2)}) %collective-permute-start.6) | collective-permute-done | bytes 147488 | tf_op jit(solution)/shard_map/ppermute | solution.py:55
  56.6 0.1 collective-permute-start.14
  56.7 2.7 %attend.3.refs_0_ = bf16[32,2048]{1,0:T(8,128)(2,1)S(1)} custom-call(s32[8]{0:T(128)S(1)} %copy-done, f32[32,2304]{1,0:T(8,128)S(1)} %slice_add_fusion.2.refs_0_, f32[32,128]{1,0:T(8,128)S(1)} %slice.37.refs_1_, f32[32,128]{1,0:T(8,128)S(1)} %get-tuple-element.68.refs_2_, f32[32,128]{1,0:T(8,128)S(1)} %get-tuple-element.69.refs_3_, ...), custom_call_target="tpu_custom_call" | custom-call | tf_op jit(solution)/shard_map/attend/pallas_call | solution.py:259
  59.4 3.0 %collective-permute-start.7 = (bf16[32,2048]{1,0:T(8,128)(2,1)S(1)}, bf16[32,2048]{1,0:T(8,128)(2,1)S(1)}, u32[]{:S(2)}, u32[]{:S(2)}) collective-permute-start(bf16[32,2048]{1,0:T(8,128)(2,1)S(1)} %attend.3.refs_0_), channel_id=1, source_target_pairs={{0,8},{1,9},{2,10},{3,11},{4,12},{5,13},{6,14},{7,15},{8,0},{9,1},... | collective-permute-start | bytes 393224 | tf_op jit(solution)/shard_map/ppermute | solution.py:55
  62.4 0.0 collective-permute-start.17
  62.4 0.0 collective-permute-done.15.refs_2_
  62.4 2.0 %collective-permute-start.19 = (bf16[32,2048]{1,0:T(8,128)(2,1)S(1)}, bf16[32,2048]{1,0:T(8,128)(2,1)S(1)}, u32[]{:S(2)}, u32[]{:S(2)}) collective-permute-start(bf16[32,2048]{1,0:T(8,128)(2,1)S(1)} %collective-permute-done.15.refs_2_), channel_id=1, source_target_pairs={{0,2},{1,3},{2,0},{3,1},{4,6},{5,7},{6,4},{7,5},{8,10},{9,11},{10,... | collective-permute-start | bytes 393224 | tf_op jit(solution)/shard_map/ppermute | solution.py:55
  64.4 0.9 %collective-permute-done.14.refs_1_ = bf16[32,2048]{1,0:T(8,128)(2,1)S(1)} collective-permute-done((bf16[32,2048]{1,0:T(8,128)(2,1)S(1)}, bf16[32,2048]{1,0:T(8,128)(2,1)S(1)}, u32[]{:S(2)}, u32[]{:S(2)}) %collective-permute-start.14) | collective-permute-done | bytes 131104 | tf_op jit(solution)/shard_map/ppermute | solution.py:55
  65.3 0.0 collective-permute-start.16
  65.3 2.0 %collective-permute-start.8 = (bf16[32,2048]{1,0:T(8,128)(2,1)S(1)}, bf16[32,2048]{1,0:T(8,128)(2,1)S(1)}, u32[]{:S(2)}, u32[]{:S(2)}) collective-permute-start(bf16[32,2048]{1,0:T(8,128)(2,1)S(1)} %attend.3.refs_0_), channel_id=1, source_target_pairs={{0,4},{1,3},{2,6},{3,1},{4,0},{5,7},{6,2},{7,5},{8,12},{9,11},{10,... | collective-permute-start | bytes 393224 | tf_op jit(solution)/shard_map/ppermute | solution.py:55
  67.4 0.6 collective-permute-done.7.refs_1_
  68.0 0.0 collective-permute-start.9
  68.0 0.0 collective-permute-done.17.refs_4_
  68.0 1.5 %collective-permute-start.18 = (bf16[32,2048]{1,0:T(8,128)(2,1)S(1)}, bf16[32,2048]{1,0:T(8,128)(2,1)S(1)}, u32[]{:S(2)}, u32[]{:S(2)}) collective-permute-start(bf16[32,2048]{1,0:T(8,128)(2,1)S(1)} %collective-permute-done.14.refs_1_), channel_id=1, source_target_pairs={{0,2},{1,3},{2,0},{3,1},{4,6},{5,7},{6,4},{7,5},{8,10},{9,11},{10,... | collective-permute-start | bytes 393224 | tf_op jit(solution)/shard_map/ppermute | solution.py:55
  69.5 0.5 collective-permute-done.19.refs_6_
  69.9 0.9 collective-permute-start.10
  70.8 1.4 %collective-permute-start.20 = (bf16[32,2048]{1,0:T(8,128)(2,1)S(1)}, bf16[32,2048]{1,0:T(8,128)(2,1)S(1)}, u32[]{:S(2)}, u32[]{:S(2)}) collective-permute-start(bf16[32,2048]{1,0:T(8,128)(2,1)S(1)} %collective-permute-done.16.refs_3_), channel_id=1, source_target_pairs={{0,2},{1,3},{2,0},{3,1},{4,6},{5,7},{6,4},{7,5},{8,10},{9,11},{10,... | collective-permute-start | bytes 393224 | tf_op jit(solution)/shard_map/ppermute | solution.py:55
  72.2 0.1 collective-permute-done.8.refs_2_
  72.3 1.4 %collective-permute-start.11 = (bf16[32,2048]{1,0:T(8,128)(2,1)S(1)}, bf16[32,2048]{1,0:T(8,128)(2,1)S(1)}, u32[]{:S(2)}, u32[]{:S(2)}) collective-permute-start(bf16[32,2048]{1,0:T(8,128)(2,1)S(1)} %collective-permute-done.7.refs_1_), channel_id=1, source_target_pairs={{0,2},{1,5},{2,0},{3,7},{4,6},{5,1},{6,4},{7,3},{8,10},{9,13},{10,... | collective-permute-start | bytes 393224 | tf_op jit(solution)/shard_map/ppermute | solution.py:55
  73.8 1.4 %collective-permute-done.9.refs_3_ = bf16[32,2048]{1,0:T(8,128)(2,1)S(1)} collective-permute-done((bf16[32,2048]{1,0:T(8,128)(2,1)S(1)}, bf16[32,2048]{1,0:T(8,128)(2,1)S(1)}, u32[]{:S(2)}, u32[]{:S(2)}) %collective-permute-start.9) | collective-permute-done | bytes 131104 | tf_op jit(solution)/shard_map/ppermute | solution.py:55
  75.1 1.4 %collective-permute-start.12 = (bf16[32,2048]{1,0:T(8,128)(2,1)S(1)}, bf16[32,2048]{1,0:T(8,128)(2,1)S(1)}, u32[]{:S(2)}, u32[]{:S(2)}) collective-permute-start(bf16[32,2048]{1,0:T(8,128)(2,1)S(1)} %collective-permute-done.8.refs_2_), channel_id=1, source_target_pairs={{0,2},{1,5},{2,0},{3,7},{4,6},{5,1},{6,4},{7,3},{8,10},{9,13},{10,... | collective-permute-start | bytes 393224 | tf_op jit(solution)/shard_map/ppermute | solution.py:55
  76.6 0.0 collective-permute-done.18.refs_5_
  76.6 0.6 collective-permute-start.13
  77.2 1.7 %collective-permute-done.20.refs_7_ = bf16[32,2048]{1,0:T(8,128)(2,1)S(1)} collective-permute-done((bf16[32,2048]{1,0:T(8,128)(2,1)S(1)}, bf16[32,2048]{1,0:T(8,128)(2,1)S(1)}, u32[]{:S(2)}, u32[]{:S(2)}) %collective-permute-start.20) | collective-permute-done | bytes 131104 | tf_op jit(solution)/shard_map/ppermute | solution.py:55
  78.9 3.7 %combine.2.refs_8_ = f32[256,2048]{1,0:T(8,128)S(1)} custom-call(bf16[32,2048]{1,0:T(8,128)(2,1)S(1)} %attend.2.refs_0_, bf16[32,2048]{1,0:T(8,128)(2,1)S(1)} %collective-permute-done.14.refs_1_, bf16[32,2048]{1,0:T(8,128)(2,1)S(1)} %collective-permute-done.15.refs_2_, bf16[32,2048]{1,0:T(8,128)(2,1)S(1)} %collective-permute-done.16.refs_3_, ...), custom_call_target="tpu_custom_call" | custom-call | tf_op jit(solution)/shard_map/combine/pallas_call | solution.py:379
  82.6 0.0 collective-permute-done.10.refs_4_
  82.7 0.0 collective-permute-done.12.refs_6_
  82.7 0.4 collective-permute-done.13.refs_7_
  83.1 3.8 %combine.3 = (bf16[128,2048]{1,0:T(8,128)(2,1)S(1)}, f32[128,2048]{1,0:T(8,128)S(1)}) custom-call(bf16[32,2048]{1,0:T(8,128)(2,1)S(1)} %attend.3.refs_0_, bf16[32,2048]{1,0:T(8,128)(2,1)S(1)} %collective-permute-done.7.refs_1_, bf16[32,2048]{1,0:T(8,128)(2,1)S(1)} %collective-permute-done.8.refs_2_, bf16[32,2048]{1,0:T(8,128)(2,1)S(1)} %collective-permute-done.9.refs_3_, ...), custom_call_target="tpu_custom_call" | custom-call | tf_op jit(solution)/shard_map/combine/pallas_call | solution.py:379
  86.9 0.1 collective-permute-start.21
  87.0 1.9 %collective-permute-done.21 = bf16[128,2048]{1,0:T(8,128)(2,1)S(1)} collective-permute-done((bf16[128,2048]{1,0:T(8,128)(2,1)S(1)}, bf16[128,2048]{1,0:T(8,128)(2,1)S(1)}, u32[]{:S(2)}, u32[]{:S(2)}) %collective-permute-start.21) | collective-permute-done | bytes 524320 | tf_op jit(solution)/shard_map/ppermute | solution.py:511
  88.9 0.9 %add_convert_fusion = bf16[128,2048]{1,0:T(8,128)(2,1)} fusion(f32[128,2048]{1,0:T(8,128)S(1)} %get-tuple-element.63, bf16[128,2048]{1,0:T(8,128)(2,1)S(1)} %collective-permute-done.21), kind=kLoop, calls=%fused_computation.3 | loop fusion | flops 786432 | bytes 2097152 | tf_op jit(solution)/shard_map/convert_element_type | solution.py:512
  (12 shorter events, 0.2 us)
Async XLA Ops:
  4.4 7.7 %collective-permute-start = (bf16[128,1152]{1,0:T(8,128)(2,1)S(1)}, bf16[128,1152]{1,0:T(8,128)(2,1)S(1)}, u32[]{:S(2)}, u32[]{:S(2)}) collective-permute-start(bf16[128,1152]{1,0:T(8,128)(2,1)S(1)} %get-tuple-element.36), channel_id=1, source_target_pairs={{0,2},{1,5},{2,0},{3,7},{4,6},{5,1},{6,4},{7,3},{8,10},{9,13},{10,... | collective-permute-start | bytes 884744 | tf_op jit(solution)/shard_map/ppermute | solution.py:55
  11.3 7.1 %collective-permute-start.1 = (bf16[128,1280]{1,0:T(8,128)(2,1)S(1)}, bf16[128,1280]{1,0:T(8,128)(2,1)S(1)}, u32[]{:S(2)}, u32[]{:S(2)}) collective-permute-start(bf16[128,1280]{1,0:T(8,128)(2,1)S(1)} %get-tuple-element.38), channel_id=1, source_target_pairs={{0,2},{1,5},{2,0},{3,7},{4,6},{5,1},{6,4},{7,3},{8,10},{9,13},{10,... | collective-permute-start | bytes 983048 | tf_op jit(solution)/shard_map/ppermute | solution.py:55
  18.5 1.7 %copy-start = (s32[8]{0:T(128)S(1)}, s32[8]{0:T(128)}, u32[]{:S(2)}) copy-start(s32[8]{0:T(128)} %length_ref.3) | copy-start | bytes 100
  18.5 7.1 %collective-permute-start.2 = (bf16[64,2432]{1,0:T(8,128)(2,1)S(1)}, bf16[64,2432]{1,0:T(8,128)(2,1)}, u32[]{:S(2)}, u32[]{:S(2)}) collective-permute-start(bf16[64,2432]{1,0:T(8,128)(2,1)S(1)} %fusion.1), channel_id=1, source_target_pairs={{0,4},{1,3},{2,6},{3,1},{4,0},{5,7},{6,2},{7,5},{8,12},{9,11},{10,... | collective-permute-start | bytes 933896 | tf_op jit(solution)/shard_map/ppermute | solution.py:55
  26.7 10.3 %collective-permute-start.4 = (bf16[32,2432]{1,0:T(8,128)(2,1)S(1)}, bf16[32,2432]{1,0:T(8,128)(2,1)S(1)}, u32[]{:S(2)}, u32[]{:S(2)}) collective-permute-start(bf16[32,2432]{1,0:T(8,128)(2,1)S(1)} %slice.63), channel_id=1, source_target_pairs={{0,8},{1,9},{2,10},{3,11},{4,12},{5,13},{6,14},{7,15},{8,0},{9,1},... | collective-permute-start | bytes 466952 | tf_op jit(solution)/shard_map/ppermute | solution.py:55
  29.4 9.9 %collective-permute-start.3 = (bf16[128,2304]{1,0:T(8,128)(2,1)S(1)}, bf16[128,2304]{1,0:T(8,128)(2,1)S(1)}, u32[]{:S(2)}, u32[]{:S(2)}) collective-permute-start(bf16[128,2304]{1,0:T(8,128)(2,1)S(1)} %pad_maximum_fusion.1), channel_id=1, source_target_pairs={{0,2},{1,5},{2,0},{3,7},{4,6},{5,1},{6,4},{7,3},{8,10},{9,13},{10,... | collective-permute-start | bytes 1769480 | tf_op jit(solution)/shard_map/ppermute | solution.py:55
  39.5 6.8 %collective-permute-start.5 = (bf16[64,2304]{1,0:T(8,128)(2,1)S(1)}, bf16[64,2304]{1,0:T(8,128)(2,1)S(1)}, u32[]{:S(2)}, u32[]{:S(2)}) collective-permute-start(bf16[64,2304]{1,0:T(8,128)(2,1)S(1)} %slice.62), channel_id=1, source_target_pairs={{0,4},{1,3},{2,6},{3,1},{4,0},{5,7},{6,2},{7,5},{8,12},{9,11},{10,... | collective-permute-start | bytes 884744 | tf_op jit(solution)/shard_map/ppermute | solution.py:55
  46.3 10.2 %collective-permute-start.6 = (bf16[32,2304]{1,0:T(8,128)(2,1)S(1)}, bf16[32,2304]{1,0:T(8,128)(2,1)S(1)}, u32[]{:S(2)}, u32[]{:S(2)}) collective-permute-start(bf16[32,2304]{1,0:T(8,128)(2,1)S(1)} %slice.64), channel_id=1, source_target_pairs={{0,8},{1,9},{2,10},{3,11},{4,12},{5,13},{6,14},{7,15},{8,0},{9,1},... | collective-permute-start | bytes 442376 | tf_op jit(solution)/shard_map/ppermute | solution.py:55
  46.7 15.7 %collective-permute-start.15 = (bf16[32,2048]{1,0:T(8,128)(2,1)S(1)}, bf16[32,2048]{1,0:T(8,128)(2,1)S(1)}, u32[]{:S(2)}, u32[]{:S(2)}) collective-permute-start(bf16[32,2048]{1,0:T(8,128)(2,1)S(1)} %attend.2.refs_0_), channel_id=1, source_target_pairs={{0,4},{1,5},{2,6},{3,7},{4,0},{5,1},{6,2},{7,3},{8,12},{9,13},{10,... | collective-permute-start | bytes 393224 | tf_op jit(solution)/shard_map/ppermute | solution.py:55
  56.6 8.7 %collective-permute-start.14 = (bf16[32,2048]{1,0:T(8,128)(2,1)S(1)}, bf16[32,2048]{1,0:T(8,128)(2,1)S(1)}, u32[]{:S(2)}, u32[]{:S(2)}) collective-permute-start(bf16[32,2048]{1,0:T(8,128)(2,1)S(1)} %attend.2.refs_0_), channel_id=1, source_target_pairs={{0,8},{1,9},{2,10},{3,11},{4,12},{5,13},{6,14},{7,15},{8,0},{9,1},... | collective-permute-start | bytes 393224 | tf_op jit(solution)/shard_map/ppermute | solution.py:55
  59.4 8.6 %collective-permute-start.7 = (bf16[32,2048]{1,0:T(8,128)(2,1)S(1)}, bf16[32,2048]{1,0:T(8,128)(2,1)S(1)}, u32[]{:S(2)}, u32[]{:S(2)}) collective-permute-start(bf16[32,2048]{1,0:T(8,128)(2,1)S(1)} %attend.3.refs_0_), channel_id=1, source_target_pairs={{0,8},{1,9},{2,10},{3,11},{4,12},{5,13},{6,14},{7,15},{8,0},{9,1},... | collective-permute-start | bytes 393224 | tf_op jit(solution)/shard_map/ppermute | solution.py:55
  62.4 5.6 %collective-permute-start.17 = (bf16[32,2048]{1,0:T(8,128)(2,1)S(1)}, bf16[32,2048]{1,0:T(8,128)(2,1)S(1)}, u32[]{:S(2)}, u32[]{:S(2)}) collective-permute-start(bf16[32,2048]{1,0:T(8,128)(2,1)S(1)} %attend.2.refs_0_), channel_id=1, source_target_pairs={{0,2},{1,3},{2,0},{3,1},{4,6},{5,7},{6,4},{7,5},{8,10},{9,11},{10,... | collective-permute-start | bytes 393224 | tf_op jit(solution)/shard_map/ppermute | solution.py:55
  62.4 7.5 %collective-permute-start.19 = (bf16[32,2048]{1,0:T(8,128)(2,1)S(1)}, bf16[32,2048]{1,0:T(8,128)(2,1)S(1)}, u32[]{:S(2)}, u32[]{:S(2)}) collective-permute-start(bf16[32,2048]{1,0:T(8,128)(2,1)S(1)} %collective-permute-done.15.refs_2_), channel_id=1, source_target_pairs={{0,2},{1,3},{2,0},{3,1},{4,6},{5,7},{6,4},{7,5},{8,10},{9,11},{10,... | collective-permute-start | bytes 393224 | tf_op jit(solution)/shard_map/ppermute | solution.py:55
  65.3 5.5 %collective-permute-start.16 = (bf16[32,2048]{1,0:T(8,128)(2,1)S(1)}, bf16[32,2048]{1,0:T(8,128)(2,1)S(1)}, u32[]{:S(2)}, u32[]{:S(2)}) collective-permute-start(bf16[32,2048]{1,0:T(8,128)(2,1)S(1)} %collective-permute-done.14.refs_1_), channel_id=1, source_target_pairs={{0,4},{1,5},{2,6},{3,7},{4,0},{5,1},{6,2},{7,3},{8,12},{9,13},{10,... | collective-permute-start | bytes 393224 | tf_op jit(solution)/shard_map/ppermute | solution.py:55
  65.3 7.0 %collective-permute-start.8 = (bf16[32,2048]{1,0:T(8,128)(2,1)S(1)}, bf16[32,2048]{1,0:T(8,128)(2,1)S(1)}, u32[]{:S(2)}, u32[]{:S(2)}) collective-permute-start(bf16[32,2048]{1,0:T(8,128)(2,1)S(1)} %attend.3.refs_0_), channel_id=1, source_target_pairs={{0,4},{1,3},{2,6},{3,1},{4,0},{5,7},{6,2},{7,5},{8,12},{9,11},{10,... | collective-permute-start | bytes 393224 | tf_op jit(solution)/shard_map/ppermute | solution.py:55
  68.0 7.2 %collective-permute-start.9 = (bf16[32,2048]{1,0:T(8,128)(2,1)S(1)}, bf16[32,2048]{1,0:T(8,128)(2,1)S(1)}, u32[]{:S(2)}, u32[]{:S(2)}) collective-permute-start(bf16[32,2048]{1,0:T(8,128)(2,1)S(1)} %collective-permute-done.7.refs_1_), channel_id=1, source_target_pairs={{0,4},{1,3},{2,6},{3,1},{4,0},{5,7},{6,2},{7,5},{8,12},{9,11},{10,... | collective-permute-start | bytes 393224 | tf_op jit(solution)/shard_map/ppermute | solution.py:55
  68.0 8.6 %collective-permute-start.18 = (bf16[32,2048]{1,0:T(8,128)(2,1)S(1)}, bf16[32,2048]{1,0:T(8,128)(2,1)S(1)}, u32[]{:S(2)}, u32[]{:S(2)}) collective-permute-start(bf16[32,2048]{1,0:T(8,128)(2,1)S(1)} %collective-permute-done.14.refs_1_), channel_id=1, source_target_pairs={{0,2},{1,3},{2,0},{3,1},{4,6},{5,7},{6,4},{7,5},{8,10},{9,11},{10,... | collective-permute-start | bytes 393224 | tf_op jit(solution)/shard_map/ppermute | solution.py:55
  69.9 12.7 %collective-permute-start.10 = (bf16[32,2048]{1,0:T(8,128)(2,1)S(1)}, bf16[32,2048]{1,0:T(8,128)(2,1)S(1)}, u32[]{:S(2)}, u32[]{:S(2)}) collective-permute-start(bf16[32,2048]{1,0:T(8,128)(2,1)S(1)} %attend.3.refs_0_), channel_id=1, source_target_pairs={{0,2},{1,5},{2,0},{3,7},{4,6},{5,1},{6,4},{7,3},{8,10},{9,13},{10,... | collective-permute-start | bytes 393224 | tf_op jit(solution)/shard_map/ppermute | solution.py:55
  70.8 8.1 %collective-permute-start.20 = (bf16[32,2048]{1,0:T(8,128)(2,1)S(1)}, bf16[32,2048]{1,0:T(8,128)(2,1)S(1)}, u32[]{:S(2)}, u32[]{:S(2)}) collective-permute-start(bf16[32,2048]{1,0:T(8,128)(2,1)S(1)} %collective-permute-done.16.refs_3_), channel_id=1, source_target_pairs={{0,2},{1,3},{2,0},{3,1},{4,6},{5,7},{6,4},{7,5},{8,10},{9,11},{10,... | collective-permute-start | bytes 393224 | tf_op jit(solution)/shard_map/ppermute | solution.py:55
  72.3 10.3 %collective-permute-start.11 = (bf16[32,2048]{1,0:T(8,128)(2,1)S(1)}, bf16[32,2048]{1,0:T(8,128)(2,1)S(1)}, u32[]{:S(2)}, u32[]{:S(2)}) collective-permute-start(bf16[32,2048]{1,0:T(8,128)(2,1)S(1)} %collective-permute-done.7.refs_1_), channel_id=1, source_target_pairs={{0,2},{1,5},{2,0},{3,7},{4,6},{5,1},{6,4},{7,3},{8,10},{9,13},{10,... | collective-permute-start | bytes 393224 | tf_op jit(solution)/shard_map/ppermute | solution.py:55
  75.1 7.5 %collective-permute-start.12 = (bf16[32,2048]{1,0:T(8,128)(2,1)S(1)}, bf16[32,2048]{1,0:T(8,128)(2,1)S(1)}, u32[]{:S(2)}, u32[]{:S(2)}) collective-permute-start(bf16[32,2048]{1,0:T(8,128)(2,1)S(1)} %collective-permute-done.8.refs_2_), channel_id=1, source_target_pairs={{0,2},{1,5},{2,0},{3,7},{4,6},{5,1},{6,4},{7,3},{8,10},{9,13},{10,... | collective-permute-start | bytes 393224 | tf_op jit(solution)/shard_map/ppermute | solution.py:55
  76.6 6.5 %collective-permute-start.13 = (bf16[32,2048]{1,0:T(8,128)(2,1)S(1)}, bf16[32,2048]{1,0:T(8,128)(2,1)S(1)}, u32[]{:S(2)}, u32[]{:S(2)}) collective-permute-start(bf16[32,2048]{1,0:T(8,128)(2,1)S(1)} %collective-permute-done.9.refs_3_), channel_id=1, source_target_pairs={{0,2},{1,5},{2,0},{3,7},{4,6},{5,1},{6,4},{7,3},{8,10},{9,13},{10,... | collective-permute-start | bytes 393224 | tf_op jit(solution)/shard_map/ppermute | solution.py:55
  86.9 2.0 %collective-permute-start.21 = (bf16[128,2048]{1,0:T(8,128)(2,1)S(1)}, bf16[128,2048]{1,0:T(8,128)(2,1)S(1)}, u32[]{:S(2)}, u32[]{:S(2)}) collective-permute-start(bf16[128,2048]{1,0:T(8,128)(2,1)S(1)} %get-tuple-element.64), channel_id=1, source_target_pairs={{0,1},{1,0},{2,3},{3,2},{4,5},{5,4},{6,7},{7,6},{8,9},{9,8},{10,11... | collective-permute-start | bytes 1572872 | tf_op jit(solution)/shard_map/ppermute | solution.py:511

commit v10 on v8

--- a/solution.py
+++ b/solution.py
@@ -20,18 +20,16 @@
 
 
 def bit_orders(n):
-    first = list(range(n.bit_length() - 1))
+    levels = n.bit_length() - 1
+    first = list(range(levels))
     second = list(first)
-    if len(first) > 1:
+    if levels > 1:
         second[0], second[1] = second[1], second[0]
-    if len(first) > 2:
-        first[1], first[2] = first[2], first[1]
     return first, second
 
 
 def gather_orders(n, chunk):
-    second = bit_orders(n)[1]
-    first = sorted(second)
+    first, second = bit_orders(n)
     return (first, second) if chunk else (first, first)
 
 
@@ -515,10 +513,6 @@
         for slot in range(1, n):
             top = slot.bit_length() - 1
             source = slots[slot - (1 << top)]
-            if slot == 1 and chunk == 0:
-                source = after(source, sums[1])
-            if chunk == 1 and slot == 3 << (levels - 2):
-                source = after(source, slots[1 << (levels - 1)])
             slots.append(
                 exchange(source, n, cores, levels - 1 - top, gather_orders(n, chunk))
             )

time: 89.1 us -> 84.3 us (0.946)
  starting transfers between devices: 33.6 us -> 30.7 us
  waiting for transfers between devices: 17.2 us -> 15.3 us
    ppermute x21, starting transfers between devices: 33.5 us -> 30.6 us  [exchange(): return lax.ppermute(value, ('gx', 'gy'), pairs)]
    ppermute x21, waiting for transfers between devices: 15.3 us -> 13.4 us  [exchange(): return lax.ppermute(value, ('gx', 'gy'), pairs)]
  transfers between devices with their start and end apart: 22 -> 22, of which waited for: 8 -> 7; matrix products, arithmetic and copies ran while one was open for 2% -> 2% of each run, Pallas kernels for 30% -> 32%
where the time goes in v10:
time: 84.3 us; the launch traced here: 84.2 us
  Pallas kernels  35.3 us (42%)
  starting transfers between devices  30.7 us (36%)
  waiting for transfers between devices  15.3 us (18%)
  other arithmetic  2.58 us (3%)
    ppermute x21, starting transfers between devices, exchange(): return lax.ppermute(value, ('gx', 'gy'), pairs)  30.6 us
    pallas_call x3, Pallas kernels, project(): pl.pallas_call(functools.partial(project_kernel, n, q_start, kv_start, fi...  13.8 us
    ppermute x21, waiting for transfers between devices, exchange(): return lax.ppermute(value, ('gx', 'gy'), pairs)  13.4 us
    pallas_call x2, Pallas kernels, combine(): pl.pallas_call(functools.partial(combine_kernel, n, block, chunk), out_sh...  7.75 us
    pallas_call x2, Pallas kernels, attend(): pl.pallas_call(functools.partial(attend_kernel, chunk, offsets, kv_offset...  6.77 us
    pallas_call x1, Pallas kernels, fetch_rows(): pl.pallas_call(functools.partial(fetch_rows_kernel, start, pieces), out_s...  3.5 us
    pallas_call x1, Pallas kernels, fetch(): pl.pallas_call(functools.partial(fetch_kernel, len(arrays), pieces), out_...  3.47 us
    ppermute x1, waiting for transfers between devices, shards(): other = lax.ppermute(send, 'gy', [(0, 1), (1, 0)])  1.9 us
  transfers between devices with their start and end apart: 22, of which 7 were waited for; matrix products, arithmetic and copies ran while one was open for 2% of the time, Pallas kernels for 32%

profile of v10, /device:TPU:0, one launch (start us, length us, event | category | flops | bytes accessed | tf_op | source)
XLA Modules:
  0.0 84.2 jit_solution(1640060971774710080)
XLA Ops:
  0.0 4.4 %project.3 = (bf16[128,1152]{1,0:T(8,128)(2,1)S(1)}, f32[128,1152]{1,0:T(8,128)S(1)}, bf16[256,2048]{1,0:T(8,128)(2,1)S(1)}) custom-call(bf16[256,2048]{1,0:T(8,128)(2,1)} %refs_0_.1, f32[1,2048]{1,0:T(1,128)} %bitcast.1, bf16[2048,4096]{1,0:T(8,128)(2,1)} %refs_1_.3, bf16[2048,256]{1,0:T(8,128)(2,1)} %refs_2_.5, bf16[2048,256]{1,0:T(8,128)(2,1)} %refs_3_.5), custom_call_target="tpu_custom_call" | custom-call | tf_op jit(solution)/shard_map/project/pallas_call | solution.py:159
  4.4 3.0 %collective-permute-start = (bf16[128,1152]{1,0:T(8,128)(2,1)S(1)}, bf16[128,1152]{1,0:T(8,128)(2,1)S(1)}, u32[]{:S(2)}, u32[]{:S(2)}) collective-permute-start(bf16[128,1152]{1,0:T(8,128)(2,1)S(1)} %get-tuple-element.31), channel_id=1, source_target_pairs={{0,2},{1,5},{2,0},{3,7},{4,6},{5,1},{6,4},{7,3},{8,10},{9,13},{10,... | collective-permute-start | bytes 884744 | tf_op jit(solution)/shard_map/ppermute | solution.py:55
  7.4 3.9 %project.4 = (bf16[128,1280]{1,0:T(8,128)(2,1)S(1)}, f32[128,1280]{1,0:T(8,128)S(1)}) custom-call(bf16[256,2048]{1,0:T(8,128)(2,1)S(1)} %get-tuple-element.36.refs_0_, bf16[2048,4096]{1,0:T(8,128)(2,1)} %refs_1_.3, bf16[2048,256]{1,0:T(8,128)(2,1)} %refs_2_.5, bf16[2048,256]{1,0:T(8,128)(2,1)} %refs_3_.5), custom_call_target="tpu_custom_call" | custom-call | tf_op jit(solution)/shard_map/project/pallas_call | solution.py:159
  11.3 0.1 collective-permute-start.1
  11.4 0.8 collective-permute-done
  12.1 0.1 convert_add_fusion.2
  12.2 0.0 copy-start
  12.2 5.5 %project.5 = (bf16[128,2304]{1,0:T(8,128)(2,1)S(1)}, f32[128,2304]{1,0:T(8,128)S(1)}) custom-call(bf16[256,2048]{1,0:T(8,128)(2,1)S(1)} %get-tuple-element.36.refs_0_, bf16[2048,4096]{1,0:T(8,128)(2,1)} %refs_1_.3, bf16[2048,256]{1,0:T(8,128)(2,1)} %refs_2_.5, bf16[2048,256]{1,0:T(8,128)(2,1)} %refs_3_.5), custom_call_target="tpu_custom_call" | custom-call | tf_op jit(solution)/shard_map/project/pallas_call | solution.py:159
  17.7 0.7 collective-permute-done.1
  18.4 0.1 convert_add_fusion.1
  18.5 1.6 %collective-permute-start.3 = (bf16[64,2432]{1,0:T(8,128)(2,1)S(1)}, bf16[64,2432]{1,0:T(8,128)(2,1)}, u32[]{:S(2)}, u32[]{:S(2)}) collective-permute-start(bf16[64,2432]{1,0:T(8,128)(2,1)S(1)} %fusion.1), channel_id=1, source_target_pairs={{0,4},{1,3},{2,6},{3,1},{4,0},{5,7},{6,2},{7,5},{8,12},{9,11},{10,... | collective-permute-start | bytes 933896 | tf_op jit(solution)/shard_map/ppermute | solution.py:55
  20.2 0.1 add_convert_fusion.1
  20.2 0.1 convert_element_type.49
  20.3 1.4 %collective-permute-start.2 = (bf16[128,2304]{1,0:T(8,128)(2,1)S(1)}, bf16[128,2304]{1,0:T(8,128)(2,1)S(1)}, u32[]{:S(2)}, u32[]{:S(2)}) collective-permute-start(bf16[128,2304]{1,0:T(8,128)(2,1)S(1)} %get-tuple-element.41), channel_id=1, source_target_pairs={{0,2},{1,5},{2,0},{3,7},{4,6},{5,1},{6,4},{7,3},{8,10},{9,13},{10,... | collective-permute-start | bytes 1769480 | tf_op jit(solution)/shard_map/ppermute | solution.py:55
  21.7 3.5 %fetch_rows.1.refs_8_ = bf16[2048,2048]{1,0:T(8,128)(2,1)S(1)} custom-call(bf16[4096,2048]{1,0:T(8,128)(2,1)} %refs_6_.1), custom_call_target="tpu_custom_call" | custom-call | tf_op jit(solution)/shard_map/fetch_rows/pallas_call | solution.py:341
  25.2 5.3 %collective-permute-done.3 = bf16[64,2432]{1,0:T(8,128)(2,1)} collective-permute-done((bf16[64,2432]{1,0:T(8,128)(2,1)S(1)}, bf16[64,2432]{1,0:T(8,128)(2,1)}, u32[]{:S(2)}, u32[]{:S(2)}) %collective-permute-start.3) | collective-permute-done | bytes 311328 | tf_op jit(solution)/shard_map/ppermute | solution.py:55
  30.5 1.0 %fusion.2 = f32[64,2432]{1,0:T(8,128)S(1)} fusion(f32[128,1280]{1,0:T(8,128)S(1)} %convert_add_fusion.1, f32[128,1152]{1,0:T(8,128)S(1)} %convert_add_fusion.2, bf16[64,2432]{1,0:T(8,128)(2,1)} %collective-permute-done.3), kind=kLoop, calls=%fused_computation.8 | loop fusion | flops 466944 | bytes 2179072 | tf_op jit(solution)/shard_map/add | solution.py:469
  31.6 1.0 %collective-permute-start.5 = (bf16[32,2432]{1,0:T(8,128)(2,1)S(1)}, bf16[32,2432]{1,0:T(8,128)(2,1)S(1)}, u32[]{:S(2)}, u32[]{:S(2)}) collective-permute-start(bf16[32,2432]{1,0:T(8,128)(2,1)S(1)} %slice.64), channel_id=1, source_target_pairs={{0,8},{1,9},{2,10},{3,11},{4,12},{5,13},{6,14},{7,15},{8,0},{9,1},... | collective-permute-start | bytes 466952 | tf_op jit(solution)/shard_map/ppermute | solution.py:55
  32.6 0.0 collective-permute-done.2
  32.6 0.1 convert_add_fusion
  32.7 3.3 %collective-permute-start.4 = (bf16[64,2304]{1,0:T(8,128)(2,1)S(1)}, bf16[64,2304]{1,0:T(8,128)(2,1)S(1)}, u32[]{:S(2)}, u32[]{:S(2)}) collective-permute-start(bf16[64,2304]{1,0:T(8,128)(2,1)S(1)} %slice.63), channel_id=1, source_target_pairs={{0,4},{1,3},{2,6},{3,1},{4,0},{5,7},{6,2},{7,5},{8,12},{9,11},{10,... | collective-permute-start | bytes 884744 | tf_op jit(solution)/shard_map/ppermute | solution.py:55
  36.0 3.5 %fetch.1 = (bf16[8,1024,256]{2,1,0:T(8,128)(2,1)S(1)}, bf16[8,1024,256]{2,1,0:T(8,128)(2,1)S(1)}) custom-call(bf16[8,1024,256]{2,1,0:T(8,128)(2,1)} %refs_0_.2, bf16[8,1024,256]{2,1,0:T(8,128)(2,1)} %refs_1_.4), custom_call_target="tpu_custom_call" | custom-call | tf_op jit(solution)/shard_map/fetch/pallas_call | solution.py:312
  39.5 0.0 collective-permute-done.5
  39.6 2.0 %collective-permute-done.4 = bf16[64,2304]{1,0:T(8,128)(2,1)S(1)} collective-permute-done((bf16[64,2304]{1,0:T(8,128)(2,1)S(1)}, bf16[64,2304]{1,0:T(8,128)(2,1)S(1)}, u32[]{:S(2)}, u32[]{:S(2)}) %collective-permute-start.4) | collective-permute-done | bytes 294944 | tf_op jit(solution)/shard_map/ppermute | solution.py:55
  41.6 0.1 slice_add_fusion
  41.7 0.7 collective-permute-start.6
  42.4 0.1 fusion.3
  42.5 0.1 pad_maximum_fusion.1
  42.6 4.0 %attend.3 = (bf16[32,2048]{1,0:T(8,128)(2,1)S(1)}, bf16[2048,2048]{1,0:T(8,128)(2,1)S(1)}) custom-call(s32[8]{0:T(128)S(1)} %copy-done, f32[32,2432]{1,0:T(8,128)S(1)} %slice_add_fusion.1.refs_0_, f32[32,128]{1,0:T(8,128)S(1)} %slice.48.refs_1_, f32[32,128]{1,0:T(8,128)S(1)} %get-tuple-element.58.refs_2_, f32[32,128]{1,0:T(8,128)S(1)} %get-tuple-element.59.refs_3_, ...), custom_call_target="tpu_custom_call" | custom-call | tf_op jit(solution)/shard_map/attend/pallas_call | solution.py:279
  46.7 0.8 collective-permute-start.17
  47.5 1.7 %collective-permute-start.15 = (bf16[32,2048]{1,0:T(8,128)(2,1)S(1)}, bf16[32,2048]{1,0:T(8,128)(2,1)S(1)}, u32[]{:S(2)}, u32[]{:S(2)}) collective-permute-start(bf16[32,2048]{1,0:T(8,128)(2,1)S(1)} %get-tuple-element.51.refs_0_), channel_id=1, source_target_pairs={{0,4},{1,5},{2,6},{3,7},{4,0},{5,1},{6,2},{7,3},{8,12},{9,13},{10,... | collective-permute-start | bytes 393224 | tf_op jit(solution)/shard_map/ppermute | solution.py:55
  49.2 1.1 %collective-permute-start.14 = (bf16[32,2048]{1,0:T(8,128)(2,1)S(1)}, bf16[32,2048]{1,0:T(8,128)(2,1)S(1)}, u32[]{:S(2)}, u32[]{:S(2)}) collective-permute-start(bf16[32,2048]{1,0:T(8,128)(2,1)S(1)} %get-tuple-element.51.refs_0_), channel_id=1, source_target_pairs={{0,8},{1,9},{2,10},{3,11},{4,12},{5,13},{6,14},{7,15},{8,0},{9,1},... | collective-permute-start | bytes 393224 | tf_op jit(solution)/shard_map/ppermute | solution.py:55
  50.3 0.0 collective-permute-done.6
  50.3 2.7 %attend.2.refs_0_ = bf16[32,2048]{1,0:T(8,128)(2,1)S(1)} custom-call(s32[8]{0:T(128)S(1)} %copy-done, f32[32,2304]{1,0:T(8,128)S(1)} %slice_add_fusion.2.refs_0_, f32[32,128]{1,0:T(8,128)S(1)} %slice.48.refs_1_, f32[32,128]{1,0:T(8,128)S(1)} %get-tuple-element.58.refs_2_, f32[32,128]{1,0:T(8,128)S(1)} %get-tuple-element.59.refs_3_, ...), custom_call_target="tpu_custom_call" | custom-call | tf_op jit(solution)/shard_map/attend/pallas_call | solution.py:279
  53.0 1.9 %collective-permute-start.7 = (bf16[32,2048]{1,0:T(8,128)(2,1)S(1)}, bf16[32,2048]{1,0:T(8,128)(2,1)S(1)}, u32[]{:S(2)}, u32[]{:S(2)}) collective-permute-start(bf16[32,2048]{1,0:T(8,128)(2,1)S(1)} %attend.2.refs_0_), channel_id=1, source_target_pairs={{0,8},{1,9},{2,10},{3,11},{4,12},{5,13},{6,14},{7,15},{8,0},{9,1},... | collective-permute-start | bytes 393224 | tf_op jit(solution)/shard_map/ppermute | solution.py:55
  54.9 3.9 %collective-permute-done.14.refs_1_ = bf16[32,2048]{1,0:T(8,128)(2,1)S(1)} collective-permute-done((bf16[32,2048]{1,0:T(8,128)(2,1)S(1)}, bf16[32,2048]{1,0:T(8,128)(2,1)S(1)}, u32[]{:S(2)}, u32[]{:S(2)}) %collective-permute-start.14) | collective-permute-done | bytes 131104 | tf_op jit(solution)/shard_map/ppermute | solution.py:55
  58.8 1.2 %collective-permute-start.16 = (bf16[32,2048]{1,0:T(8,128)(2,1)S(1)}, bf16[32,2048]{1,0:T(8,128)(2,1)S(1)}, u32[]{:S(2)}, u32[]{:S(2)}) collective-permute-start(bf16[32,2048]{1,0:T(8,128)(2,1)S(1)} %collective-permute-done.14.refs_1_), channel_id=1, source_target_pairs={{0,4},{1,5},{2,6},{3,7},{4,0},{5,1},{6,2},{7,3},{8,12},{9,13},{10,... | collective-permute-start | bytes 393224 | tf_op jit(solution)/shard_map/ppermute | solution.py:55
  60.0 0.0 collective-permute-done.15.refs_2_
  60.1 1.8 %collective-permute-start.19 = (bf16[32,2048]{1,0:T(8,128)(2,1)S(1)}, bf16[32,2048]{1,0:T(8,128)(2,1)S(1)}, u32[]{:S(2)}, u32[]{:S(2)}) collective-permute-start(bf16[32,2048]{1,0:T(8,128)(2,1)S(1)} %collective-permute-done.15.refs_2_), channel_id=1, source_target_pairs={{0,2},{1,3},{2,0},{3,1},{4,6},{5,7},{6,4},{7,5},{8,10},{9,11},{10,... | collective-permute-start | bytes 393224 | tf_op jit(solution)/shard_map/ppermute | solution.py:55
  61.8 0.3 collective-permute-start.18
  62.1 0.0 collective-permute-done.17.refs_4_
  62.1 1.8 %collective-permute-start.8 = (bf16[32,2048]{1,0:T(8,128)(2,1)S(1)}, bf16[32,2048]{1,0:T(8,128)(2,1)S(1)}, u32[]{:S(2)}, u32[]{:S(2)}) collective-permute-start(bf16[32,2048]{1,0:T(8,128)(2,1)S(1)} %attend.2.refs_0_), channel_id=1, source_target_pairs={{0,4},{1,3},{2,6},{3,1},{4,0},{5,7},{6,2},{7,5},{8,12},{9,11},{10,... | collective-permute-start | bytes 393224 | tf_op jit(solution)/shard_map/ppermute | solution.py:55
  63.9 0.0 collective-permute-done.7.refs_1_
  63.9 0.2 collective-permute-start.9
  64.1 0.0 collective-permute-done.16.refs_3_
  64.1 3.8 %collective-permute-start.20 = (bf16[32,2048]{1,0:T(8,128)(2,1)S(1)}, bf16[32,2048]{1,0:T(8,128)(2,1)S(1)}, u32[]{:S(2)}, u32[]{:S(2)}) collective-permute-start(bf16[32,2048]{1,0:T(8,128)(2,1)S(1)} %collective-permute-done.16.refs_3_), channel_id=1, source_target_pairs={{0,2},{1,3},{2,0},{3,1},{4,6},{5,7},{6,4},{7,5},{8,10},{9,11},{10,... | collective-permute-start | bytes 393224 | tf_op jit(solution)/shard_map/ppermute | solution.py:55
  67.9 0.0 collective-permute-done.19.refs_6_
  67.9 0.3 collective-permute-start.10
  68.2 0.0 collective-permute-done.18.refs_5_
  68.2 1.7 %collective-permute-start.11 = (bf16[32,2048]{1,0:T(8,128)(2,1)S(1)}, bf16[32,2048]{1,0:T(8,128)(2,1)S(1)}, u32[]{:S(2)}, u32[]{:S(2)}) collective-permute-start(bf16[32,2048]{1,0:T(8,128)(2,1)S(1)} %collective-permute-done.7.refs_1_), channel_id=1, source_target_pairs={{0,2},{1,5},{2,0},{3,7},{4,6},{5,1},{6,4},{7,3},{8,10},{9,13},{10,... | collective-permute-start | bytes 393224 | tf_op jit(solution)/shard_map/ppermute | solution.py:55
  69.9 0.0 collective-permute-done.8.refs_2_
  69.9 0.8 collective-permute-start.12
  70.7 0.6 collective-permute-done.9.refs_3_
  71.3 2.2 %collective-permute-start.13 = (bf16[32,2048]{1,0:T(8,128)(2,1)S(1)}, bf16[32,2048]{1,0:T(8,128)(2,1)S(1)}, u32[]{:S(2)}, u32[]{:S(2)}) collective-permute-start(bf16[32,2048]{1,0:T(8,128)(2,1)S(1)} %collective-permute-done.9.refs_3_), channel_id=1, source_target_pairs={{0,2},{1,5},{2,0},{3,7},{4,6},{5,1},{6,4},{7,3},{8,10},{9,13},{10,... | collective-permute-start | bytes 393224 | tf_op jit(solution)/shard_map/ppermute | solution.py:55
  73.5 0.0 collective-permute-done.20.refs_7_
  73.5 3.8 %combine.2.refs_8_ = f32[256,2048]{1,0:T(8,128)S(1)} custom-call(bf16[32,2048]{1,0:T(8,128)(2,1)S(1)} %get-tuple-element.51.refs_0_, bf16[32,2048]{1,0:T(8,128)(2,1)S(1)} %collective-permute-done.14.refs_1_, bf16[32,2048]{1,0:T(8,128)(2,1)S(1)} %collective-permute-done.15.refs_2_, bf16[32,2048]{1,0:T(8,128)(2,1)S(1)} %collective-permute-done.16.refs_3_, ...), custom_call_target="tpu_custom_call" | custom-call | tf_op jit(solution)/shard_map/combine/pallas_call | solution.py:400
  77.3 0.0 collective-permute-done.10.refs_4_
  77.3 0.0 collective-permute-done.12.refs_6_
  77.3 0.0 collective-permute-done.11.refs_5_
  77.3 0.0 collective-permute-done.13.refs_7_
  77.4 3.9 %combine.3 = (bf16[128,2048]{1,0:T(8,128)(2,1)S(1)}, f32[128,2048]{1,0:T(8,128)S(1)}) custom-call(bf16[32,2048]{1,0:T(8,128)(2,1)S(1)} %attend.2.refs_0_, bf16[32,2048]{1,0:T(8,128)(2,1)S(1)} %collective-permute-done.7.refs_1_, bf16[32,2048]{1,0:T(8,128)(2,1)S(1)} %collective-permute-done.8.refs_2_, bf16[32,2048]{1,0:T(8,128)(2,1)S(1)} %collective-permute-done.9.refs_3_, ...), custom_call_target="tpu_custom_call" | custom-call | tf_op jit(solution)/shard_map/combine/pallas_call | solution.py:400
  81.3 0.1 collective-permute-start.21
  81.4 1.9 %collective-permute-done.21 = bf16[128,2048]{1,0:T(8,128)(2,1)S(1)} collective-permute-done((bf16[128,2048]{1,0:T(8,128)(2,1)S(1)}, bf16[128,2048]{1,0:T(8,128)(2,1)S(1)}, u32[]{:S(2)}, u32[]{:S(2)}) %collective-permute-start.21) | collective-permute-done | bytes 524320 | tf_op jit(solution)/shard_map/ppermute | solution.py:524
  83.3 0.9 %add_convert_fusion = bf16[128,2048]{1,0:T(8,128)(2,1)} fusion(f32[128,2048]{1,0:T(8,128)S(1)} %get-tuple-element.53, bf16[128,2048]{1,0:T(8,128)(2,1)S(1)} %collective-permute-done.21), kind=kLoop, calls=%fused_computation.3 | loop fusion | flops 786432 | bytes 2097152 | tf_op jit(solution)/shard_map/convert_element_type | solution.py:525
  (9 shorter events, 0.2 us)
Async XLA Ops:
  4.4 7.7 %collective-permute-start = (bf16[128,1152]{1,0:T(8,128)(2,1)S(1)}, bf16[128,1152]{1,0:T(8,128)(2,1)S(1)}, u32[]{:S(2)}, u32[]{:S(2)}) collective-permute-start(bf16[128,1152]{1,0:T(8,128)(2,1)S(1)} %get-tuple-element.31), channel_id=1, source_target_pairs={{0,2},{1,5},{2,0},{3,7},{4,6},{5,1},{6,4},{7,3},{8,10},{9,13},{10,... | collective-permute-start | bytes 884744 | tf_op jit(solution)/shard_map/ppermute | solution.py:55
  11.3 7.1 %collective-permute-start.1 = (bf16[128,1280]{1,0:T(8,128)(2,1)S(1)}, bf16[128,1280]{1,0:T(8,128)(2,1)S(1)}, u32[]{:S(2)}, u32[]{:S(2)}) collective-permute-start(bf16[128,1280]{1,0:T(8,128)(2,1)S(1)} %get-tuple-element.33), channel_id=1, source_target_pairs={{0,2},{1,5},{2,0},{3,7},{4,6},{5,1},{6,4},{7,3},{8,10},{9,13},{10,... | collective-permute-start | bytes 983048 | tf_op jit(solution)/shard_map/ppermute | solution.py:55
  12.2 8.0 %copy-start = (s32[8]{0:T(128)S(1)}, s32[8]{0:T(128)}, u32[]{:S(2)}) copy-start(s32[8]{0:T(128)} %length_ref.3) | copy-start | bytes 100
  18.5 12.0 %collective-permute-start.3 = (bf16[64,2432]{1,0:T(8,128)(2,1)S(1)}, bf16[64,2432]{1,0:T(8,128)(2,1)}, u32[]{:S(2)}, u32[]{:S(2)}) collective-permute-start(bf16[64,2432]{1,0:T(8,128)(2,1)S(1)} %fusion.1), channel_id=1, source_target_pairs={{0,4},{1,3},{2,6},{3,1},{4,0},{5,7},{6,2},{7,5},{8,12},{9,11},{10,... | collective-permute-start | bytes 933896 | tf_op jit(solution)/shard_map/ppermute | solution.py:55
  20.3 12.3 %collective-permute-start.2 = (bf16[128,2304]{1,0:T(8,128)(2,1)S(1)}, bf16[128,2304]{1,0:T(8,128)(2,1)S(1)}, u32[]{:S(2)}, u32[]{:S(2)}) collective-permute-start(bf16[128,2304]{1,0:T(8,128)(2,1)S(1)} %get-tuple-element.41), channel_id=1, source_target_pairs={{0,2},{1,5},{2,0},{3,7},{4,6},{5,1},{6,4},{7,3},{8,10},{9,13},{10,... | collective-permute-start | bytes 1769480 | tf_op jit(solution)/shard_map/ppermute | solution.py:55
  31.6 8.0 %collective-permute-start.5 = (bf16[32,2432]{1,0:T(8,128)(2,1)S(1)}, bf16[32,2432]{1,0:T(8,128)(2,1)S(1)}, u32[]{:S(2)}, u32[]{:S(2)}) collective-permute-start(bf16[32,2432]{1,0:T(8,128)(2,1)S(1)} %slice.64), channel_id=1, source_target_pairs={{0,8},{1,9},{2,10},{3,11},{4,12},{5,13},{6,14},{7,15},{8,0},{9,1},... | collective-permute-start | bytes 466952 | tf_op jit(solution)/shard_map/ppermute | solution.py:55
  32.7 8.9 %collective-permute-start.4 = (bf16[64,2304]{1,0:T(8,128)(2,1)S(1)}, bf16[64,2304]{1,0:T(8,128)(2,1)S(1)}, u32[]{:S(2)}, u32[]{:S(2)}) collective-permute-start(bf16[64,2304]{1,0:T(8,128)(2,1)S(1)} %slice.63), channel_id=1, source_target_pairs={{0,4},{1,3},{2,6},{3,1},{4,0},{5,7},{6,2},{7,5},{8,12},{9,11},{10,... | collective-permute-start | bytes 884744 | tf_op jit(solution)/shard_map/ppermute | solution.py:55
  41.7 8.6 %collective-permute-start.6 = (bf16[32,2304]{1,0:T(8,128)(2,1)S(1)}, bf16[32,2304]{1,0:T(8,128)(2,1)S(1)}, u32[]{:S(2)}, u32[]{:S(2)}) collective-permute-start(bf16[32,2304]{1,0:T(8,128)(2,1)S(1)} %slice.65), channel_id=1, source_target_pairs={{0,8},{1,9},{2,10},{3,11},{4,12},{5,13},{6,14},{7,15},{8,0},{9,1},... | collective-permute-start | bytes 442376 | tf_op jit(solution)/shard_map/ppermute | solution.py:55
  46.7 15.4 %collective-permute-start.17 = (bf16[32,2048]{1,0:T(8,128)(2,1)S(1)}, bf16[32,2048]{1,0:T(8,128)(2,1)S(1)}, u32[]{:S(2)}, u32[]{:S(2)}) collective-permute-start(bf16[32,2048]{1,0:T(8,128)(2,1)S(1)} %get-tuple-element.51.refs_0_), channel_id=1, source_target_pairs={{0,2},{1,3},{2,0},{3,1},{4,6},{5,7},{6,4},{7,5},{8,10},{9,11},{10,... | collective-permute-start | bytes 393224 | tf_op jit(solution)/shard_map/ppermute | solution.py:55
  47.5 12.6 %collective-permute-start.15 = (bf16[32,2048]{1,0:T(8,128)(2,1)S(1)}, bf16[32,2048]{1,0:T(8,128)(2,1)S(1)}, u32[]{:S(2)}, u32[]{:S(2)}) collective-permute-start(bf16[32,2048]{1,0:T(8,128)(2,1)S(1)} %get-tuple-element.51.refs_0_), channel_id=1, source_target_pairs={{0,4},{1,5},{2,6},{3,7},{4,0},{5,1},{6,2},{7,3},{8,12},{9,13},{10,... | collective-permute-start | bytes 393224 | tf_op jit(solution)/shard_map/ppermute | solution.py:55
  49.2 9.7 %collective-permute-start.14 = (bf16[32,2048]{1,0:T(8,128)(2,1)S(1)}, bf16[32,2048]{1,0:T(8,128)(2,1)S(1)}, u32[]{:S(2)}, u32[]{:S(2)}) collective-permute-start(bf16[32,2048]{1,0:T(8,128)(2,1)S(1)} %get-tuple-element.51.refs_0_), channel_id=1, source_target_pairs={{0,8},{1,9},{2,10},{3,11},{4,12},{5,13},{6,14},{7,15},{8,0},{9,1},... | collective-permute-start | bytes 393224 | tf_op jit(solution)/shard_map/ppermute | solution.py:55
  53.0 10.9 %collective-permute-start.7 = (bf16[32,2048]{1,0:T(8,128)(2,1)S(1)}, bf16[32,2048]{1,0:T(8,128)(2,1)S(1)}, u32[]{:S(2)}, u32[]{:S(2)}) collective-permute-start(bf16[32,2048]{1,0:T(8,128)(2,1)S(1)} %attend.2.refs_0_), channel_id=1, source_target_pairs={{0,8},{1,9},{2,10},{3,11},{4,12},{5,13},{6,14},{7,15},{8,0},{9,1},... | collective-permute-start | bytes 393224 | tf_op jit(solution)/shard_map/ppermute | solution.py:55
  58.8 5.3 %collective-permute-start.16 = (bf16[32,2048]{1,0:T(8,128)(2,1)S(1)}, bf16[32,2048]{1,0:T(8,128)(2,1)S(1)}, u32[]{:S(2)}, u32[]{:S(2)}) collective-permute-start(bf16[32,2048]{1,0:T(8,128)(2,1)S(1)} %collective-permute-done.14.refs_1_), channel_id=1, source_target_pairs={{0,4},{1,5},{2,6},{3,7},{4,0},{5,1},{6,2},{7,3},{8,12},{9,13},{10,... | collective-permute-start | bytes 393224 | tf_op jit(solution)/shard_map/ppermute | solution.py:55
  60.1 7.8 %collective-permute-start.19 = (bf16[32,2048]{1,0:T(8,128)(2,1)S(1)}, bf16[32,2048]{1,0:T(8,128)(2,1)S(1)}, u32[]{:S(2)}, u32[]{:S(2)}) collective-permute-start(bf16[32,2048]{1,0:T(8,128)(2,1)S(1)} %collective-permute-done.15.refs_2_), channel_id=1, source_target_pairs={{0,2},{1,3},{2,0},{3,1},{4,6},{5,7},{6,4},{7,5},{8,10},{9,11},{10,... | collective-permute-start | bytes 393224 | tf_op jit(solution)/shard_map/ppermute | solution.py:55
  61.8 6.4 %collective-permute-start.18 = (bf16[32,2048]{1,0:T(8,128)(2,1)S(1)}, bf16[32,2048]{1,0:T(8,128)(2,1)S(1)}, u32[]{:S(2)}, u32[]{:S(2)}) collective-permute-start(bf16[32,2048]{1,0:T(8,128)(2,1)S(1)} %collective-permute-done.14.refs_1_), channel_id=1, source_target_pairs={{0,2},{1,3},{2,0},{3,1},{4,6},{5,7},{6,4},{7,5},{8,10},{9,11},{10,... | collective-permute-start | bytes 393224 | tf_op jit(solution)/shard_map/ppermute | solution.py:55
  62.1 7.8 %collective-permute-start.8 = (bf16[32,2048]{1,0:T(8,128)(2,1)S(1)}, bf16[32,2048]{1,0:T(8,128)(2,1)S(1)}, u32[]{:S(2)}, u32[]{:S(2)}) collective-permute-start(bf16[32,2048]{1,0:T(8,128)(2,1)S(1)} %attend.2.refs_0_), channel_id=1, source_target_pairs={{0,4},{1,3},{2,6},{3,1},{4,0},{5,7},{6,2},{7,5},{8,12},{9,11},{10,... | collective-permute-start | bytes 393224 | tf_op jit(solution)/shard_map/ppermute | solution.py:55
  63.9 7.4 %collective-permute-start.9 = (bf16[32,2048]{1,0:T(8,128)(2,1)S(1)}, bf16[32,2048]{1,0:T(8,128)(2,1)S(1)}, u32[]{:S(2)}, u32[]{:S(2)}) collective-permute-start(bf16[32,2048]{1,0:T(8,128)(2,1)S(1)} %collective-permute-done.7.refs_1_), channel_id=1, source_target_pairs={{0,4},{1,3},{2,6},{3,1},{4,0},{5,7},{6,2},{7,5},{8,12},{9,11},{10,... | collective-permute-start | bytes 393224 | tf_op jit(solution)/shard_map/ppermute | solution.py:55
  64.1 9.4 %collective-permute-start.20 = (bf16[32,2048]{1,0:T(8,128)(2,1)S(1)}, bf16[32,2048]{1,0:T(8,128)(2,1)S(1)}, u32[]{:S(2)}, u32[]{:S(2)}) collective-permute-start(bf16[32,2048]{1,0:T(8,128)(2,1)S(1)} %collective-permute-done.16.refs_3_), channel_id=1, source_target_pairs={{0,2},{1,3},{2,0},{3,1},{4,6},{5,7},{6,4},{7,5},{8,10},{9,11},{10,... | collective-permute-start | bytes 393224 | tf_op jit(solution)/shard_map/ppermute | solution.py:55
  67.9 9.4 %collective-permute-start.10 = (bf16[32,2048]{1,0:T(8,128)(2,1)S(1)}, bf16[32,2048]{1,0:T(8,128)(2,1)S(1)}, u32[]{:S(2)}, u32[]{:S(2)}) collective-permute-start(bf16[32,2048]{1,0:T(8,128)(2,1)S(1)} %attend.2.refs_0_), channel_id=1, source_target_pairs={{0,2},{1,5},{2,0},{3,7},{4,6},{5,1},{6,4},{7,3},{8,10},{9,13},{10,... | collective-permute-start | bytes 393224 | tf_op jit(solution)/shard_map/ppermute | solution.py:55
  68.2 9.1 %collective-permute-start.11 = (bf16[32,2048]{1,0:T(8,128)(2,1)S(1)}, bf16[32,2048]{1,0:T(8,128)(2,1)S(1)}, u32[]{:S(2)}, u32[]{:S(2)}) collective-permute-start(bf16[32,2048]{1,0:T(8,128)(2,1)S(1)} %collective-permute-done.7.refs_1_), channel_id=1, source_target_pairs={{0,2},{1,5},{2,0},{3,7},{4,6},{5,1},{6,4},{7,3},{8,10},{9,13},{10,... | collective-permute-start | bytes 393224 | tf_op jit(solution)/shard_map/ppermute | solution.py:55
  69.9 7.4 %collective-permute-start.12 = (bf16[32,2048]{1,0:T(8,128)(2,1)S(1)}, bf16[32,2048]{1,0:T(8,128)(2,1)S(1)}, u32[]{:S(2)}, u32[]{:S(2)}) collective-permute-start(bf16[32,2048]{1,0:T(8,128)(2,1)S(1)} %collective-permute-done.8.refs_2_), channel_id=1, source_target_pairs={{0,2},{1,5},{2,0},{3,7},{4,6},{5,1},{6,4},{7,3},{8,10},{9,13},{10,... | collective-permute-start | bytes 393224 | tf_op jit(solution)/shard_map/ppermute | solution.py:55
  71.3 6.0 %collective-permute-start.13 = (bf16[32,2048]{1,0:T(8,128)(2,1)S(1)}, bf16[32,2048]{1,0:T(8,128)(2,1)S(1)}, u32[]{:S(2)}, u32[]{:S(2)}) collective-permute-start(bf16[32,2048]{1,0:T(8,128)(2,1)S(1)} %collective-permute-done.9.refs_3_), channel_id=1, source_target_pairs={{0,2},{1,5},{2,0},{3,7},{4,6},{5,1},{6,4},{7,3},{8,10},{9,13},{10,... | collective-permute-start | bytes 393224 | tf_op jit(solution)/shard_map/ppermute | solution.py:55
  81.3 2.0 %collective-permute-start.21 = (bf16[128,2048]{1,0:T(8,128)(2,1)S(1)}, bf16[128,2048]{1,0:T(8,128)(2,1)S(1)}, u32[]{:S(2)}, u32[]{:S(2)}) collective-permute-start(bf16[128,2048]{1,0:T(8,128)(2,1)S(1)} %get-tuple-element.54), channel_id=1, source_target_pairs={{0,1},{1,0},{2,3},{3,2},{4,5},{5,4},{6,7},{7,6},{8,9},{9,8},{10,11... | collective-permute-start | bytes 1572872 | tf_op jit(solution)/shard_map/ppermute | solution.py:524

commit v11 on v9

--- a/solution.py
+++ b/solution.py
@@ -30,7 +30,7 @@
 
 def gather_orders(n, chunk):
     first, second = bit_orders(n)
-    return (first, second) if chunk else (first, first)
+    return (first, first) if chunk else (first, second)
 
 
 def slot_shift(slot, order):
@@ -65,7 +65,7 @@
     half = send_ref.shape[0]
     rows = 2 * half
     with_kv = kv_start is not None
-    kv = wk_ref.shape[1] // CHUNKS if with_kv else 0
+    kv = wk_ref.shape[1] if with_kv else 0
     width = w_buf.shape[1]
     cols = width - 2 * kv
     tile = cols // 2
@@ -134,7 +134,7 @@
 
 def project(n, q_start, q_cols, kv_start, first, x, gain, w_query, w_key, w_value):
     rows, depth = x.shape
-    kv = w_key.shape[1] // CHUNKS if kv_start is not None else 0
+    kv = w_key.shape[1] if kv_start is not None else 0
     width = q_cols + 2 * kv
     full = width + (128 if first else 0)
     hbm = pl.BlockSpec(memory_space=pltpu.HBM)
@@ -167,45 +167,45 @@
     )(*args, in_hbm(w_query), in_hbm(w_key), in_hbm(w_value))
 
 
-def attend_kernel(chunk, offsets, kv_offset, groups, heads, seqs, length_ref, *refs):
-    sum_ref, square_ref = refs[:2]
-    cos_ref, sin_ref, k_ref, v_ref, out_ref, q_scr, o_scr = refs[2:]
+def attend_kernel(layout, kv_offset, square_offset, seqs, length_ref, *refs):
+    sum_ref, shared_ref, cos_ref, sin_ref, k_ref, v_ref, out_ref, q_scr, o_scr = refs
     rows = seqs * NEW
-    cols = groups * heads * HD
-    kv = groups * HD
-    seq_count = k_ref.shape[0]
-
+    kv = k_ref.shape[2]
+    seq_count, slots = k_ref.shape[:2]
     scale = HD**-0.5 * math.log2(math.e)
-    slots = k_ref.shape[1]
-    many = heads * NEW
     slot_ids = lax.broadcasted_iota(jnp.int32, (1, slots), 1)
-    new_cols = lax.broadcasted_iota(jnp.int32, (many, rows), 1)
-    new_rows = lax.broadcasted_iota(jnp.int32, (many, rows), 0) % NEW
 
     @pl.loop(0, seq_count // seqs)
     def _(step):
         mine = pl.ds(pl.multiple_of(step * rows, rows), rows)
-        mean = jnp.sum(square_ref[mine, :], axis=1, keepdims=True) / D
+        squares = shared_ref[mine, square_offset : square_offset + 128]
+        mean = jnp.sum(squares, axis=1, keepdims=True) / D
         row_scale = lax.rsqrt(mean + EPS)
         cosine, sine = cos_ref[mine, :], sin_ref[mine, :]
 
-        def raw(start):
-            return sum_ref[mine, start : start + HD] * row_scale
+        def raw(ref, start):
+            return ref[mine, start : start + HD] * row_scale
 
         def rotary(value):
             return value * cosine + pltpu.roll(value, HD // 2, 1) * sine
 
-        for h in range(heads * groups):
-            turned = rotary(raw(offsets[h]))
-            for s in range(seqs):
-                q_scr[s, h * NEW : (h + 1) * NEW, :] = turned[s * NEW : (s + 1) * NEW]
-        for g in range(groups):
-            new_keys = rotary(raw(kv_offset + g * HD)).astype(jnp.bfloat16)
-            new_values = raw(kv_offset + (groups + g) * HD).astype(jnp.bfloat16)
-            lanes = slice(chunk * kv + g * HD, chunk * kv + (g + 1) * HD)
+        done = 0
+        for g, offsets in layout:
+            heads = len(offsets)
+            many = heads * NEW
+            for h, offset in enumerate(offsets):
+                turned = rotary(raw(sum_ref, offset))
+                at = (done + h) * NEW
+                for s in range(seqs):
+                    q_scr[s, at : at + NEW, :] = turned[s * NEW : (s + 1) * NEW]
+            new_cols = lax.broadcasted_iota(jnp.int32, (many, rows), 1)
+            new_rows = lax.broadcasted_iota(jnp.int32, (many, rows), 0) % NEW
+            new_keys = rotary(raw(shared_ref, kv_offset + g * HD)).astype(jnp.bfloat16)
+            new_values = raw(shared_ref, kv_offset + kv + g * HD).astype(jnp.bfloat16)
+            lanes = slice(g * HD, (g + 1) * HD)
             olds, news, mixes = [], [], []
             for s in range(seqs):
-                query = q_scr[s, g * many : (g + 1) * many, :].astype(jnp.bfloat16)
+                query = q_scr[s, done * NEW : (done + heads) * NEW, :].astype(jnp.bfloat16)
                 keys = k_ref[step * seqs + s, :, lanes]
                 olds.append(
                     lax.dot_general(
@@ -239,35 +239,31 @@
                 )
             for s in range(seqs):
                 for h in range(heads):
-                    at = (g * heads + h) * HD
+                    at = (done + h) * HD
                     o_scr[s * NEW : (s + 1) * NEW, at : at + HD] = mixes[s][
                         h * NEW : (h + 1) * NEW
                     ]
+            done += heads
         out_ref[mine, :] = o_scr[...].astype(jnp.bfloat16)
 
 
-def attend(chunk, offsets, kv_offset, sums, squares, cosine, sine, cache_keys, cache_values, lengths):
-    seq_count, slots, kv_all = cache_keys.shape
-    kv = kv_all // CHUNKS
-    groups = kv // HD
-    heads = len(offsets) // groups
-    cols = len(offsets) * HD
+def attend(layout, kv_offset, square_offset, sums, shared, cosine, sine, keys, values, lengths):
+    seq_count = keys.shape[0]
+    heads = sum(len(offsets) for _, offsets in layout)
     seqs = min(4, seq_count)
-    rows = seq_count * NEW
     vmem = pl.BlockSpec(memory_space=pltpu.VMEM)
-    hbm = pl.BlockSpec(memory_space=pltpu.HBM)
     return pl.pallas_call(
-        functools.partial(attend_kernel, chunk, offsets, kv_offset, groups, heads, seqs),
-        out_shape=pltpu.VMEM((rows, cols), jnp.bfloat16),
+        functools.partial(attend_kernel, layout, kv_offset, square_offset, seqs),
+        out_shape=pltpu.VMEM((seq_count * NEW, heads * HD), jnp.bfloat16),
         in_specs=[pl.BlockSpec(memory_space=pltpu.SMEM)] + [vmem] * 6,
         out_specs=vmem,
         scratch_shapes=[
-            pltpu.VMEM((seqs, groups * heads * NEW, HD), jnp.float32),
-            pltpu.VMEM((seqs * NEW, cols), jnp.float32),
+            pltpu.VMEM((seqs, heads * NEW, HD), jnp.float32),
+            pltpu.VMEM((seqs * NEW, heads * HD), jnp.float32),
         ],
         compiler_params=pltpu.CompilerParams(vmem_limit_bytes=16 * MIB),
         name="attend",
-    )(lengths, sums, squares, cosine, sine, cache_keys, cache_values)
+    )(lengths, sums, shared, cosine, sine, keys, values)
 
 
 def fetch_kernel(count, pieces, *refs):
@@ -406,19 +402,18 @@
     sine = jnp.concatenate([-sine, sine], axis=1)
 
     x, gain = tokens, norm_gain[None, :]
-    kv = w_key.shape[1] // CHUNKS
-    q_cols = w_query.shape[1] // CHUNKS
-
-    def column_part(start, size, kv_start):
+    q_cols = w_query.shape[1]
+    share = q_cols // 4
+    orders = bit_orders(n)
+
+    def column_part(part, with_kv):
+        kv_start = 0 if with_kv else None
         return project(
-            n, start, size, kv_start, start == 0, x, gain, w_query, w_key, w_value
+            n, part * share, share, kv_start, part == 0, x, gain, w_query, w_key, w_value
         )
 
     def after(value, *earlier):
         return lax.optimization_barrier((value, earlier))[0]
-
-    share = q_cols // 2
-    orders = bit_orders(n)
 
     def start(stage, send):
         return exchange(send, n, cores, stage, orders)
@@ -428,78 +423,80 @@
         low = value.shape[0] // 2 if stage < levels - 1 else 0
         return value[low:].astype(jnp.bfloat16), value[:low] if low else value
 
-    send_a, keep_a, x = column_part(0, share, None)
+    send_a, keep_a, x = column_part(0, False)
     x = after(x, send_a)
     other_a = start(0, send_a)
-    send_b, keep_b = column_part(share, share, 0)
+    send_b, keep_b = column_part(1, False)
     x = after(x, send_b)
     other_b = start(0, send_b)
     sum_a = keep_a + other_a.astype(jnp.float32)
     x = after(x, sum_a)
-    send_c, keep_c = column_part(q_cols, share, None)
-    other_b = after(other_b, send_c)
-    first = jnp.concatenate([sum_a, keep_b + other_b.astype(jnp.float32)], axis=1)
+    send_c, keep_c = column_part(2, True)
+    x = after(x, send_c)
+    other_c = start(0, send_c)
+    sum_b = keep_b + other_b.astype(jnp.float32)
+    x = after(x, sum_b)
+    send_1, keep_1 = column_part(3, False)
+    other_c = after(other_c, send_1)
+    first = jnp.concatenate([sum_a, sum_b, keep_c + other_c.astype(jnp.float32)], axis=1)
     half = first.shape[0] // 2
     send, keep = first[half:].astype(jnp.bfloat16), first[:half]
-    x = after(x, send, send_c)
-    send_d, keep_d = column_part(q_cols + share, share, kv)
-
-    other = after(start(1, send), send_d)
+
+    w_rows = 3 * w_out.shape[0] // 4
+    w_first = fetch_rows(after(w_out, send), 0, w_rows)
+    send_1 = after(send_1, send)
+    other = after(start(1, send), w_first)
+    other_1 = start(0, send_1)
     send, keep = added(1, keep, other)
-    send_1 = after(jnp.concatenate([send_c, send_d], axis=1), send)
-    keep_1 = jnp.concatenate([keep_c, keep_d], axis=1)
-    other_1 = start(0, send_1)
-    w_rows = w_out.shape[0] // CHUNKS
-    w_first = fetch_rows(after(w_out, send_1), 0, w_rows)
-    cache_keys, cache_values = fetch(*after((cache_keys, cache_values), w_first))
+    send_1, keep_1 = added(0, keep_1, after(other_1, send))
+    cache_keys, cache_values = fetch(*after((cache_keys, cache_values), send, send_1))
+    w_second = fetch_rows(after(w_out, cache_keys), w_rows, w_out.shape[0] - w_rows)
     for stage in range(2, levels):
         other = start(stage, send)
+        other_1 = start(stage - 1, send_1)
         if stage == 2:
-            other = after(other, cache_keys, cache_values)
+            other = after(other, cache_keys, cache_values, w_second)
         send, keep = added(stage, keep, other)
+        send_1, keep_1 = added(stage - 1, keep_1, after(other_1, keep))
     sum_0 = keep
-    other_1 = after(other_1, sum_0)
-    send_1, keep_1 = added(0, keep_1, other_1)
-    sum_0 = after(sum_0, send_1)
-    squares = sum_0[:, share : share + 128]
+    send_1 = after(send_1, sum_0)
+    _, sum_1 = added(levels - 1, keep_1, start(levels - 1, send_1))
+
     plain = [h * HD for h in range(q_cols // HD)]
-    offsets = [[at if at < share else at + 128 for at in plain], plain]
-    kv_offsets = [q_cols + 128, q_cols]
-
-    def attended(chunk, total):
-        return attend(
-            chunk,
-            offsets[chunk],
-            kv_offsets[chunk],
+    group_heads = q_cols // w_key.shape[1]
+    lead = 3 * share // HD
+    columns = [at if at < share else at + 128 for at in plain[:lead]] + plain[: share // HD]
+    layouts = [{}, {}]
+    for h, column in enumerate(columns):
+        layouts[h >= lead].setdefault(h // group_heads, []).append(column)
+    attentions = [
+        attend(
+            list(layouts[chunk].items()),
+            3 * share + 128,
+            share,
             total,
-            squares,
+            sum_0,
             cosine,
             sine,
             cache_keys,
             cache_values,
             cache_lengths,
         )
-
-    attentions = [attended(0, sum_0)]
-    other_1 = after(start(1, send_1), attentions[0])
-    send_1, keep_1 = added(1, keep_1, other_1)
-    w_second = fetch_rows(after(w_out, send_1), w_rows, w_rows)
-    for stage in range(2, levels):
-        other_1 = start(stage, send_1)
-        if stage == 2:
-            other_1 = after(other_1, w_second)
-        send_1, keep_1 = added(stage, keep_1, other_1)
-    sums = [sum_0, keep_1]
+        for chunk, total in enumerate((sum_0, sum_1))
+    ]
     weights = [w_first, w_second]
-    attentions.append(attended(1, sums[1]))
     gathered = []
     for chunk in range(CHUNKS):
         slots = [attentions[chunk]]
         for slot in range(1, n):
             top = slot.bit_length() - 1
             source = slots[slot - (1 << top)]
-            if slot == 1 and chunk == 0:
-                source = after(source, sums[1])
+            if chunk == 0 and slot == 1:
+                source = after(source, sum_1)
+            if chunk == 0 and slot & (slot - 1):
+                source = after(source, attentions[1])
+            if chunk == 0 and slot == 3 << (levels - 2):
+                source = after(source, slots[1 << (levels - 1)])
             slots.append(
                 exchange(source, n, cores, levels - 1 - top, gather_orders(n, chunk))
             )

time: 89.9 us -> 93.4 us (1.039)
  starting transfers between devices: 26 us -> 33.4 us
  waiting for transfers between devices: 22 us -> 17.7 us
  other arithmetic: 2.67 us -> 1.73 us
    ppermute x21 -> x22, starting transfers between devices: 25.9 us -> 33.3 us  [exchange(): return lax.ppermute(value, ('gx', 'gy'), pairs)]
    ppermute x21 -> x22, waiting for transfers between devices: 20.1 us -> 15.8 us  [exchange(): return lax.ppermute(value, ('gx', 'gy'), pairs)]
    add x5, other arithmetic: 1.28 us -> 0.23 us  [added(): value = keep + other.astype(jnp.float32)]
    pallas_call x2, Pallas kernels: 5.62 us -> 6.65 us  [attend(): pl.pallas_call(functools.partial(attend_kernel, layout, kv_offset, square...]
  transfers between devices with their start and end apart: 22 -> 23, of which waited for: 14 -> 8; matrix products, arithmetic and copies ran while one was open for 1% -> 1% of each run, Pallas kernels for 34% -> 35%
where the time goes in v11:
time: 93.4 us; the launch traced here: 93.3 us
  Pallas kernels  39.2 us (42%)
  starting transfers between devices  33.4 us (36%)
  waiting for transfers between devices  17.7 us (19%)
  other arithmetic  1.73 us (2%)
  local copies, waits for them, and re-layouts  0.96 us (1%)
    ppermute x22, starting transfers between devices, exchange(): return lax.ppermute(value, ('gx', 'gy'), pairs)  33.3 us
    ppermute x22, waiting for transfers between devices, exchange(): return lax.ppermute(value, ('gx', 'gy'), pairs)  15.8 us
    pallas_call x4, Pallas kernels, project(): pl.pallas_call(functools.partial(project_kernel, n, q_start, kv_start, fi...  14.6 us
    pallas_call x2, Pallas kernels, combine(): pl.pallas_call(functools.partial(combine_kernel, n, block, chunk), out_sh...  7.64 us
    pallas_call x2, Pallas kernels, fetch_rows(): pl.pallas_call(functools.partial(fetch_rows_kernel, start, pieces), out_s...  6.9 us
    pallas_call x2, Pallas kernels, attend(): pl.pallas_call(functools.partial(attend_kernel, layout, kv_offset, square...  6.65 us
    pallas_call x1, Pallas kernels, fetch(): pl.pallas_call(functools.partial(fetch_kernel, len(arrays), pieces), out_...  3.47 us
    ppermute x1, waiting for transfers between devices, shards(): other = lax.ppermute(send, 'gy', [(0, 1), (1, 0)])  1.9 us
  transfers between devices with their start and end apart: 23, of which 8 were waited for; matrix products, arithmetic and copies ran while one was open for 1% of the time, Pallas kernels for 35%

profile of v11, /device:TPU:0, one launch (start us, length us, event | category | flops | bytes accessed | tf_op | source)
XLA Modules:
  0.0 93.3 jit_solution(5640435579315010025)
XLA Ops:
  0.0 4.4 %project.4 = (bf16[128,1152]{1,0:T(8,128)(2,1)S(1)}, f32[128,1152]{1,0:T(8,128)S(1)}, bf16[256,2048]{1,0:T(8,128)(2,1)S(1)}) custom-call(bf16[256,2048]{1,0:T(8,128)(2,1)} %refs_0_.1, f32[1,2048]{1,0:T(1,128)} %bitcast.1, bf16[2048,4096]{1,0:T(8,128)(2,1)} %refs_1_.5, bf16[2048,256]{1,0:T(8,128)(2,1)} %refs_2_.7, bf16[2048,256]{1,0:T(8,128)(2,1)} %refs_3_.7), custom_call_target="tpu_custom_call" | custom-call | tf_op jit(solution)/shard_map/project/pallas_call | solution.py:159
  4.4 3.0 %collective-permute-start = (bf16[128,1152]{1,0:T(8,128)(2,1)S(1)}, bf16[128,1152]{1,0:T(8,128)(2,1)S(1)}, u32[]{:S(2)}, u32[]{:S(2)}) collective-permute-start(bf16[128,1152]{1,0:T(8,128)(2,1)S(1)} %get-tuple-element.40), channel_id=1, source_target_pairs={{0,2},{1,5},{2,0},{3,7},{4,6},{5,1},{6,4},{7,3},{8,10},{9,13},{10,... | collective-permute-start | bytes 884744 | tf_op jit(solution)/shard_map/ppermute | solution.py:55
  7.4 3.0 %project.5 = (bf16[128,1024]{1,0:T(8,128)(2,1)S(1)}, f32[128,1024]{1,0:T(8,128)S(1)}) custom-call(bf16[256,2048]{1,0:T(8,128)(2,1)S(1)} %get-tuple-element.49.refs_0_, bf16[2048,4096]{1,0:T(8,128)(2,1)} %refs_1_.5, bf16[2048,256]{1,0:T(8,128)(2,1)} %refs_2_.7, bf16[2048,256]{1,0:T(8,128)(2,1)} %refs_3_.7), custom_call_target="tpu_custom_call" | custom-call | tf_op jit(solution)/shard_map/project/pallas_call | solution.py:159
  10.5 0.1 collective-permute-start.1
  10.5 1.6 %collective-permute-done = bf16[128,1152]{1,0:T(8,128)(2,1)S(1)} collective-permute-done((bf16[128,1152]{1,0:T(8,128)(2,1)S(1)}, bf16[128,1152]{1,0:T(8,128)(2,1)S(1)}, u32[]{:S(2)}, u32[]{:S(2)}) %collective-permute-start) | collective-permute-done | bytes 294944 | tf_op jit(solution)/shard_map/ppermute | solution.py:55
  12.1 0.1 convert_add_fusion.1
  12.2 4.1 %project.6 = (bf16[128,1536]{1,0:T(8,128)(2,1)S(1)}, f32[128,1536]{1,0:T(8,128)S(1)}) custom-call(bf16[256,2048]{1,0:T(8,128)(2,1)S(1)} %get-tuple-element.49.refs_0_, bf16[2048,4096]{1,0:T(8,128)(2,1)} %refs_1_.5, bf16[2048,256]{1,0:T(8,128)(2,1)} %refs_2_.7, bf16[2048,256]{1,0:T(8,128)(2,1)} %refs_3_.7), custom_call_target="tpu_custom_call" | custom-call | tf_op jit(solution)/shard_map/project/pallas_call | solution.py:159
  16.3 2.1 %collective-permute-start.2 = (bf16[128,1536]{1,0:T(8,128)(2,1)S(1)}, bf16[128,1536]{1,0:T(8,128)(2,1)S(1)}, u32[]{:S(2)}, u32[]{:S(2)}) collective-permute-start(bf16[128,1536]{1,0:T(8,128)(2,1)S(1)} %get-tuple-element.46), channel_id=1, source_target_pairs={{0,2},{1,5},{2,0},{3,7},{4,6},{5,1},{6,4},{7,3},{8,10},{9,13},{10,... | collective-permute-start | bytes 1179656 | tf_op jit(solution)/shard_map/ppermute | solution.py:55
  18.4 0.0 collective-permute-done.1
  18.4 0.1 convert_add_fusion.3
  18.4 3.0 %project.7 = (bf16[128,1024]{1,0:T(8,128)(2,1)S(1)}, f32[128,1024]{1,0:T(8,128)S(1)}) custom-call(bf16[256,2048]{1,0:T(8,128)(2,1)S(1)} %get-tuple-element.49.refs_0_, bf16[2048,4096]{1,0:T(8,128)(2,1)} %refs_1_.5, bf16[2048,256]{1,0:T(8,128)(2,1)} %refs_2_.7, bf16[2048,256]{1,0:T(8,128)(2,1)} %refs_3_.7), custom_call_target="tpu_custom_call" | custom-call | tf_op jit(solution)/shard_map/project/pallas_call | solution.py:159
  21.5 0.0 copy-start
  21.5 2.6 %collective-permute-done.2 = bf16[128,1536]{1,0:T(8,128)(2,1)S(1)} collective-permute-done((bf16[128,1536]{1,0:T(8,128)(2,1)S(1)}, bf16[128,1536]{1,0:T(8,128)(2,1)S(1)}, u32[]{:S(2)}, u32[]{:S(2)}) %collective-permute-start.2) | collective-permute-done | bytes 393248 | tf_op jit(solution)/shard_map/ppermute | solution.py:55
  24.1 0.1 convert_add_fusion
  24.2 0.1 pad_maximum_fusion
  24.3 0.8 slice.52
  25.2 2.1 %collective-permute-start.4 = (bf16[64,3712]{1,0:T(8,128)(2,1)}, bf16[64,3712]{1,0:T(8,128)(2,1)S(1)}, u32[]{:S(2)}, u32[]{:S(2)}) collective-permute-start(bf16[64,3712]{1,0:T(8,128)(2,1)} %slice.52), channel_id=1, source_target_pairs={{0,4},{1,3},{2,6},{3,1},{4,0},{5,7},{6,2},{7,5},{8,12},{9,11},{10,... | collective-permute-start | bytes 1425416 | tf_op jit(solution)/shard_map/ppermute | solution.py:55
  27.2 0.1 add_convert_fusion.1
  27.3 0.1 convert_element_type.53
  27.4 0.1 fusion
  27.6 4.7 %fetch_rows.2.refs_8_ = bf16[3072,2048]{1,0:T(8,128)(2,1)S(1)} custom-call(bf16[4096,2048]{1,0:T(8,128)(2,1)} %source.1), custom_call_target="tpu_custom_call" | custom-call | tf_op jit(solution)/shard_map/fetch_rows/pallas_call | solution.py:316
  32.3 1.6 %collective-permute-start.3 = (bf16[128,1024]{1,0:T(8,128)(2,1)S(1)}, bf16[128,1024]{1,0:T(8,128)(2,1)S(1)}, u32[]{:S(2)}, u32[]{:S(2)}) collective-permute-start(bf16[128,1024]{1,0:T(8,128)(2,1)S(1)} %get-tuple-element.54), channel_id=1, source_target_pairs={{0,2},{1,5},{2,0},{3,7},{4,6},{5,1},{6,4},{7,3},{8,10},{9,13},{10,... | collective-permute-start | bytes 786440 | tf_op jit(solution)/shard_map/ppermute | solution.py:55
  33.8 1.6 %collective-permute-done.4 = bf16[64,3712]{1,0:T(8,128)(2,1)S(1)} collective-permute-done((bf16[64,3712]{1,0:T(8,128)(2,1)}, bf16[64,3712]{1,0:T(8,128)(2,1)S(1)}, u32[]{:S(2)}, u32[]{:S(2)}) %collective-permute-start.4) | collective-permute-done | bytes 475168 | tf_op jit(solution)/shard_map/ppermute | solution.py:55
  35.5 0.1 slice_add_fusion
  35.6 4.2 %collective-permute-start.6 = (bf16[32,3712]{1,0:T(8,128)(2,1)S(1)}, bf16[32,3712]{1,0:T(8,128)(2,1)S(1)}, u32[]{:S(2)}, u32[]{:S(2)}) collective-permute-start(bf16[32,3712]{1,0:T(8,128)(2,1)S(1)} %slice.53), channel_id=1, source_target_pairs={{0,8},{1,9},{2,10},{3,11},{4,12},{5,13},{6,14},{7,15},{8,0},{9,1},... | collective-permute-start | bytes 712712 | tf_op jit(solution)/shard_map/ppermute | solution.py:55
  39.8 0.0 collective-permute-done.3
  39.8 0.1 convert_add_fusion.2
  39.9 2.6 %collective-permute-start.5 = (bf16[64,1024]{1,0:T(8,128)(2,1)S(1)}, bf16[64,1024]{1,0:T(8,128)(2,1)S(1)}, u32[]{:S(2)}, u32[]{:S(2)}) collective-permute-start(bf16[64,1024]{1,0:T(8,128)(2,1)S(1)} %slice.54), channel_id=1, source_target_pairs={{0,4},{1,3},{2,6},{3,1},{4,0},{5,7},{6,2},{7,5},{8,12},{9,11},{10,... | collective-permute-start | bytes 393224 | tf_op jit(solution)/shard_map/ppermute | solution.py:55
  42.5 3.5 %fetch.1 = (bf16[8,1024,256]{2,1,0:T(8,128)(2,1)S(1)}, bf16[8,1024,256]{2,1,0:T(8,128)(2,1)S(1)}) custom-call(bf16[8,1024,256]{2,1,0:T(8,128)(2,1)} %refs_0_.2, bf16[8,1024,256]{2,1,0:T(8,128)(2,1)} %refs_1_.6), custom_call_target="tpu_custom_call" | custom-call | tf_op jit(solution)/shard_map/fetch/pallas_call | solution.py:287
  46.0 2.2 %fetch_rows.3.refs_9_ = bf16[1024,2048]{1,0:T(8,128)(2,1)S(1)} custom-call(bf16[4096,2048]{1,0:T(8,128)(2,1)} %source.1), custom_call_target="tpu_custom_call" | custom-call | tf_op jit(solution)/shard_map/fetch_rows/pallas_call | solution.py:316
  48.2 0.0 collective-permute-done.6
  48.2 0.0 collective-permute-done.5
  48.3 0.1 collective-permute-start.7
  48.4 0.1 pad_maximum_fusion.1
  48.5 4.2 %attend.3.refs_0_ = bf16[32,3072]{1,0:T(8,128)(2,1)S(1)} custom-call(s32[8]{0:T(128)S(1)} %copy-done, f32[32,3712]{1,0:T(8,128)S(1)} %slice_add_fusion.1.refs_1_.refs_0_, f32[32,3712]{1,0:T(8,128)S(1)} %slice_add_fusion.1.refs_1_.refs_0_, f32[32,128]{1,0:T(8,128)S(1)} %get-tuple-element.76.refs_2_, f32[32,128]{1,0:T(8,128)S(1)} %get-tuple-element.77.refs_3_, ...), custom_call_target="tpu_custom_call" | custom-call | tf_op jit(solution)/shard_map/attend/pallas_call | solution.py:255
  52.7 1.0 %collective-permute-done.7 = bf16[32,1024]{1,0:T(8,128)(2,1)S(1)} collective-permute-done((bf16[32,1024]{1,0:T(8,128)(2,1)S(1)}, bf16[32,1024]{1,0:T(8,128)(2,1)S(1)}, u32[]{:S(2)}, u32[]{:S(2)}) %collective-permute-start.7) | collective-permute-done | bytes 65568 | tf_op jit(solution)/shard_map/ppermute | solution.py:55
  53.7 2.0 %collective-permute-start.15 = (bf16[32,3072]{1,0:T(8,128)(2,1)S(1)}, bf16[32,3072]{1,0:T(8,128)(2,1)S(1)}, u32[]{:S(2)}, u32[]{:S(2)}) collective-permute-start(bf16[32,3072]{1,0:T(8,128)(2,1)S(1)} %attend.3.refs_0_), channel_id=1, source_target_pairs={{0,8},{1,9},{2,10},{3,11},{4,12},{5,13},{6,14},{7,15},{8,0},{9,1},... | collective-permute-start | bytes 589832 | tf_op jit(solution)/shard_map/ppermute | solution.py:55
  55.7 0.6 collective-permute-start.16
  56.2 2.8 %collective-permute-start.18 = (bf16[32,3072]{1,0:T(8,128)(2,1)S(1)}, bf16[32,3072]{1,0:T(8,128)(2,1)S(1)}, u32[]{:S(2)}, u32[]{:S(2)}) collective-permute-start(bf16[32,3072]{1,0:T(8,128)(2,1)S(1)} %attend.3.refs_0_), channel_id=1, source_target_pairs={{0,2},{1,5},{2,0},{3,7},{4,6},{5,1},{6,4},{7,3},{8,10},{9,13},{10,... | collective-permute-start | bytes 589832 | tf_op jit(solution)/shard_map/ppermute | solution.py:55
  59.1 2.5 %attend.2.refs_0_ = bf16[32,1024]{1,0:T(8,128)(2,1)S(1)} custom-call(s32[8]{0:T(128)S(1)} %copy-done, f32[32,1024]{1,0:T(8,128)S(1)} %slice_add_fusion.3.refs_0_, f32[32,3712]{1,0:T(8,128)S(1)} %slice_add_fusion.1.refs_1_.refs_0_, f32[32,128]{1,0:T(8,128)S(1)} %get-tuple-element.76.refs_2_, f32[32,128]{1,0:T(8,128)S(1)} %get-tuple-element.77.refs_3_, ...), custom_call_target="tpu_custom_call" | custom-call | tf_op jit(solution)/shard_map/attend/pallas_call | solution.py:255
  61.5 2.6 %collective-permute-done.15.refs_1_ = bf16[32,3072]{1,0:T(8,128)(2,1)S(1)} collective-permute-done((bf16[32,3072]{1,0:T(8,128)(2,1)S(1)}, bf16[32,3072]{1,0:T(8,128)(2,1)S(1)}, u32[]{:S(2)}, u32[]{:S(2)}) %collective-permute-start.15) | collective-permute-done | bytes 196640 | tf_op jit(solution)/shard_map/ppermute | solution.py:55
  64.2 0.0 collective-permute-start.17
  64.2 0.0 collective-permute-done.16.refs_2_
  64.2 0.0 collective-permute-done.18.refs_4_
  64.2 1.5 %collective-permute-start.20 = (bf16[32,3072]{1,0:T(8,128)(2,1)S(1)}, bf16[32,3072]{1,0:T(8,128)(2,1)S(1)}, u32[]{:S(2)}, u32[]{:S(2)}) collective-permute-start(bf16[32,3072]{1,0:T(8,128)(2,1)S(1)} %collective-permute-done.16.refs_2_), channel_id=1, source_target_pairs={{0,2},{1,5},{2,0},{3,7},{4,6},{5,1},{6,4},{7,3},{8,10},{9,13},{10,... | collective-permute-start | bytes 589832 | tf_op jit(solution)/shard_map/ppermute | solution.py:55
  65.7 0.5 collective-permute-start.19
  66.3 3.1 %collective-permute-start.8 = (bf16[32,1024]{1,0:T(8,128)(2,1)S(1)}, bf16[32,1024]{1,0:T(8,128)(2,1)S(1)}, u32[]{:S(2)}, u32[]{:S(2)}) collective-permute-start(bf16[32,1024]{1,0:T(8,128)(2,1)S(1)} %attend.2.refs_0_), channel_id=1, source_target_pairs={{0,8},{1,9},{2,10},{3,11},{4,12},{5,13},{6,14},{7,15},{8,0},{9,1},... | collective-permute-start | bytes 196616 | tf_op jit(solution)/shard_map/ppermute | solution.py:55
  69.4 4.0 %collective-permute-done.17.refs_3_ = bf16[32,3072]{1,0:T(8,128)(2,1)S(1)} collective-permute-done((bf16[32,3072]{1,0:T(8,128)(2,1)S(1)}, bf16[32,3072]{1,0:T(8,128)(2,1)S(1)}, u32[]{:S(2)}, u32[]{:S(2)}) %collective-permute-start.17) | collective-permute-done | bytes 196640 | tf_op jit(solution)/shard_map/ppermute | solution.py:55
  73.4 1.0 %collective-permute-start.21 = (bf16[32,3072]{1,0:T(8,128)(2,1)S(1)}, bf16[32,3072]{1,0:T(8,128)(2,1)S(1)}, u32[]{:S(2)}, u32[]{:S(2)}) collective-permute-start(bf16[32,3072]{1,0:T(8,128)(2,1)S(1)} %collective-permute-done.17.refs_3_), channel_id=1, source_target_pairs={{0,2},{1,5},{2,0},{3,7},{4,6},{5,1},{6,4},{7,3},{8,10},{9,13},{10,... | collective-permute-start | bytes 589832 | tf_op jit(solution)/shard_map/ppermute | solution.py:55
  74.4 0.0 collective-permute-start.9
  74.4 2.0 %collective-permute-start.10 = (bf16[32,1024]{1,0:T(8,128)(2,1)S(1)}, bf16[32,1024]{1,0:T(8,128)(2,1)S(1)}, u32[]{:S(2)}, u32[]{:S(2)}) collective-permute-start(bf16[32,1024]{1,0:T(8,128)(2,1)S(1)} %collective-permute-done.8.refs_1_), channel_id=1, source_target_pairs={{0,4},{1,5},{2,6},{3,7},{4,0},{5,1},{6,2},{7,3},{8,12},{9,13},{10,... | collective-permute-start | bytes 196616 | tf_op jit(solution)/shard_map/ppermute | solution.py:55
  76.4 2.2 %collective-permute-done.9.refs_2_ = bf16[32,1024]{1,0:T(8,128)(2,1)S(1)} collective-permute-done((bf16[32,1024]{1,0:T(8,128)(2,1)S(1)}, bf16[32,1024]{1,0:T(8,128)(2,1)S(1)}, u32[]{:S(2)}, u32[]{:S(2)}) %collective-permute-start.9) | collective-permute-done | bytes 65568 | tf_op jit(solution)/shard_map/ppermute | solution.py:55
  78.6 1.1 %collective-permute-start.11 = (bf16[32,1024]{1,0:T(8,128)(2,1)S(1)}, bf16[32,1024]{1,0:T(8,128)(2,1)S(1)}, u32[]{:S(2)}, u32[]{:S(2)}) collective-permute-start(bf16[32,1024]{1,0:T(8,128)(2,1)S(1)} %attend.2.refs_0_), channel_id=1, source_target_pairs={{0,2},{1,3},{2,0},{3,1},{4,6},{5,7},{6,4},{7,5},{8,10},{9,11},{10,... | collective-permute-start | bytes 196616 | tf_op jit(solution)/shard_map/ppermute | solution.py:55
  79.7 1.0 %collective-permute-start.12 = (bf16[32,1024]{1,0:T(8,128)(2,1)S(1)}, bf16[32,1024]{1,0:T(8,128)(2,1)S(1)}, u32[]{:S(2)}, u32[]{:S(2)}) collective-permute-start(bf16[32,1024]{1,0:T(8,128)(2,1)S(1)} %collective-permute-done.8.refs_1_), channel_id=1, source_target_pairs={{0,2},{1,3},{2,0},{3,1},{4,6},{5,7},{6,4},{7,5},{8,10},{9,11},{10,... | collective-permute-start | bytes 196616 | tf_op jit(solution)/shard_map/ppermute | solution.py:55
  80.7 1.1 %collective-permute-start.13 = (bf16[32,1024]{1,0:T(8,128)(2,1)S(1)}, bf16[32,1024]{1,0:T(8,128)(2,1)S(1)}, u32[]{:S(2)}, u32[]{:S(2)}) collective-permute-start(bf16[32,1024]{1,0:T(8,128)(2,1)S(1)} %collective-permute-done.9.refs_2_), channel_id=1, source_target_pairs={{0,2},{1,3},{2,0},{3,1},{4,6},{5,7},{6,4},{7,5},{8,10},{9,11},{10,... | collective-permute-start | bytes 196616 | tf_op jit(solution)/shard_map/ppermute | solution.py:55
  81.8 0.0 collective-permute-done.19.refs_5_
  81.8 1.0 %collective-permute-start.14 = (bf16[32,1024]{1,0:T(8,128)(2,1)S(1)}, bf16[32,1024]{1,0:T(8,128)(2,1)S(1)}, u32[]{:S(2)}, u32[]{:S(2)}) collective-permute-start(bf16[32,1024]{1,0:T(8,128)(2,1)S(1)} %collective-permute-done.10.refs_3_), channel_id=1, source_target_pairs={{0,2},{1,3},{2,0},{3,1},{4,6},{5,7},{6,4},{7,5},{8,10},{9,11},{10,... | collective-permute-start | bytes 196616 | tf_op jit(solution)/shard_map/ppermute | solution.py:55
  82.7 0.0 collective-permute-done.21.refs_7_
  82.7 5.6 %combine.2.refs_8_ = f32[256,2048]{1,0:T(8,128)S(1)} custom-call(bf16[32,3072]{1,0:T(8,128)(2,1)S(1)} %attend.3.refs_0_, bf16[32,3072]{1,0:T(8,128)(2,1)S(1)} %collective-permute-done.15.refs_1_, bf16[32,3072]{1,0:T(8,128)(2,1)S(1)} %collective-permute-done.16.refs_2_, bf16[32,3072]{1,0:T(8,128)(2,1)S(1)} %collective-permute-done.17.refs_3_, ...), custom_call_target="tpu_custom_call" | custom-call | tf_op jit(solution)/shard_map/combine/pallas_call | solution.py:375
  88.3 0.0 collective-permute-done.12.refs_5_
  88.4 2.0 %combine.3 = (bf16[128,2048]{1,0:T(8,128)(2,1)S(1)}, f32[128,2048]{1,0:T(8,128)S(1)}) custom-call(bf16[32,1024]{1,0:T(8,128)(2,1)S(1)} %attend.2.refs_0_, bf16[32,1024]{1,0:T(8,128)(2,1)S(1)} %collective-permute-done.8.refs_1_, bf16[32,1024]{1,0:T(8,128)(2,1)S(1)} %collective-permute-done.9.refs_2_, bf16[32,1024]{1,0:T(8,128)(2,1)S(1)} %collective-permute-done.10.refs_3_, ...), custom_call_target="tpu_custom_call" | custom-call | tf_op jit(solution)/shard_map/combine/pallas_call | solution.py:375
  90.4 0.1 collective-permute-start.22
  90.5 1.9 %collective-permute-done.22 = bf16[128,2048]{1,0:T(8,128)(2,1)S(1)} collective-permute-done((bf16[128,2048]{1,0:T(8,128)(2,1)S(1)}, bf16[128,2048]{1,0:T(8,128)(2,1)S(1)}, u32[]{:S(2)}, u32[]{:S(2)}) %collective-permute-start.22) | collective-permute-done | bytes 524320 | tf_op jit(solution)/shard_map/ppermute | solution.py:508
  92.4 0.9 add_convert_fusion
  (14 shorter events, 0.2 us)
Async XLA Ops:
  4.4 7.7 %collective-permute-start = (bf16[128,1152]{1,0:T(8,128)(2,1)S(1)}, bf16[128,1152]{1,0:T(8,128)(2,1)S(1)}, u32[]{:S(2)}, u32[]{:S(2)}) collective-permute-start(bf16[128,1152]{1,0:T(8,128)(2,1)S(1)} %get-tuple-element.40), channel_id=1, source_target_pairs={{0,2},{1,5},{2,0},{3,7},{4,6},{5,1},{6,4},{7,3},{8,10},{9,13},{10,... | collective-permute-start | bytes 884744 | tf_op jit(solution)/shard_map/ppermute | solution.py:55
  10.5 7.9 %collective-permute-start.1 = (bf16[128,1024]{1,0:T(8,128)(2,1)S(1)}, bf16[128,1024]{1,0:T(8,128)(2,1)S(1)}, u32[]{:S(2)}, u32[]{:S(2)}) collective-permute-start(bf16[128,1024]{1,0:T(8,128)(2,1)S(1)} %get-tuple-element.42), channel_id=1, source_target_pairs={{0,2},{1,5},{2,0},{3,7},{4,6},{5,1},{6,4},{7,3},{8,10},{9,13},{10,... | collective-permute-start | bytes 786440 | tf_op jit(solution)/shard_map/ppermute | solution.py:55
  16.3 7.8 %collective-permute-start.2 = (bf16[128,1536]{1,0:T(8,128)(2,1)S(1)}, bf16[128,1536]{1,0:T(8,128)(2,1)S(1)}, u32[]{:S(2)}, u32[]{:S(2)}) collective-permute-start(bf16[128,1536]{1,0:T(8,128)(2,1)S(1)} %get-tuple-element.46), channel_id=1, source_target_pairs={{0,2},{1,5},{2,0},{3,7},{4,6},{5,1},{6,4},{7,3},{8,10},{9,13},{10,... | collective-permute-start | bytes 1179656 | tf_op jit(solution)/shard_map/ppermute | solution.py:55
  21.5 5.8 %copy-start = (s32[8]{0:T(128)S(1)}, s32[8]{0:T(128)}, u32[]{:S(2)}) copy-start(s32[8]{0:T(128)} %length_ref.3) | copy-start | bytes 100
  25.2 10.3 %collective-permute-start.4 = (bf16[64,3712]{1,0:T(8,128)(2,1)}, bf16[64,3712]{1,0:T(8,128)(2,1)S(1)}, u32[]{:S(2)}, u32[]{:S(2)}) collective-permute-start(bf16[64,3712]{1,0:T(8,128)(2,1)} %slice.52), channel_id=1, source_target_pairs={{0,4},{1,3},{2,6},{3,1},{4,0},{5,7},{6,2},{7,5},{8,12},{9,11},{10,... | collective-permute-start | bytes 1425416 | tf_op jit(solution)/shard_map/ppermute | solution.py:55
  32.3 7.5 %collective-permute-start.3 = (bf16[128,1024]{1,0:T(8,128)(2,1)S(1)}, bf16[128,1024]{1,0:T(8,128)(2,1)S(1)}, u32[]{:S(2)}, u32[]{:S(2)}) collective-permute-start(bf16[128,1024]{1,0:T(8,128)(2,1)S(1)} %get-tuple-element.54), channel_id=1, source_target_pairs={{0,2},{1,5},{2,0},{3,7},{4,6},{5,1},{6,4},{7,3},{8,10},{9,13},{10,... | collective-permute-start | bytes 786440 | tf_op jit(solution)/shard_map/ppermute | solution.py:55
  35.6 12.6 %collective-permute-start.6 = (bf16[32,3712]{1,0:T(8,128)(2,1)S(1)}, bf16[32,3712]{1,0:T(8,128)(2,1)S(1)}, u32[]{:S(2)}, u32[]{:S(2)}) collective-permute-start(bf16[32,3712]{1,0:T(8,128)(2,1)S(1)} %slice.53), channel_id=1, source_target_pairs={{0,8},{1,9},{2,10},{3,11},{4,12},{5,13},{6,14},{7,15},{8,0},{9,1},... | collective-permute-start | bytes 712712 | tf_op jit(solution)/shard_map/ppermute | solution.py:55
  39.9 8.3 %collective-permute-start.5 = (bf16[64,1024]{1,0:T(8,128)(2,1)S(1)}, bf16[64,1024]{1,0:T(8,128)(2,1)S(1)}, u32[]{:S(2)}, u32[]{:S(2)}) collective-permute-start(bf16[64,1024]{1,0:T(8,128)(2,1)S(1)} %slice.54), channel_id=1, source_target_pairs={{0,4},{1,3},{2,6},{3,1},{4,0},{5,7},{6,2},{7,5},{8,12},{9,11},{10,... | collective-permute-start | bytes 393224 | tf_op jit(solution)/shard_map/ppermute | solution.py:55
  48.3 5.4 %collective-permute-start.7 = (bf16[32,1024]{1,0:T(8,128)(2,1)S(1)}, bf16[32,1024]{1,0:T(8,128)(2,1)S(1)}, u32[]{:S(2)}, u32[]{:S(2)}) collective-permute-start(bf16[32,1024]{1,0:T(8,128)(2,1)S(1)} %slice.55), channel_id=1, source_target_pairs={{0,8},{1,9},{2,10},{3,11},{4,12},{5,13},{6,14},{7,15},{8,0},{9,1},... | collective-permute-start | bytes 196616 | tf_op jit(solution)/shard_map/ppermute | solution.py:55
  53.7 10.4 %collective-permute-start.15 = (bf16[32,3072]{1,0:T(8,128)(2,1)S(1)}, bf16[32,3072]{1,0:T(8,128)(2,1)S(1)}, u32[]{:S(2)}, u32[]{:S(2)}) collective-permute-start(bf16[32,3072]{1,0:T(8,128)(2,1)S(1)} %attend.3.refs_0_), channel_id=1, source_target_pairs={{0,8},{1,9},{2,10},{3,11},{4,12},{5,13},{6,14},{7,15},{8,0},{9,1},... | collective-permute-start | bytes 589832 | tf_op jit(solution)/shard_map/ppermute | solution.py:55
  55.7 8.5 %collective-permute-start.16 = (bf16[32,3072]{1,0:T(8,128)(2,1)S(1)}, bf16[32,3072]{1,0:T(8,128)(2,1)S(1)}, u32[]{:S(2)}, u32[]{:S(2)}) collective-permute-start(bf16[32,3072]{1,0:T(8,128)(2,1)S(1)} %attend.3.refs_0_), channel_id=1, source_target_pairs={{0,4},{1,3},{2,6},{3,1},{4,0},{5,7},{6,2},{7,5},{8,12},{9,11},{10,... | collective-permute-start | bytes 589832 | tf_op jit(solution)/shard_map/ppermute | solution.py:55
  56.2 7.9 %collective-permute-start.18 = (bf16[32,3072]{1,0:T(8,128)(2,1)S(1)}, bf16[32,3072]{1,0:T(8,128)(2,1)S(1)}, u32[]{:S(2)}, u32[]{:S(2)}) collective-permute-start(bf16[32,3072]{1,0:T(8,128)(2,1)S(1)} %attend.3.refs_0_), channel_id=1, source_target_pairs={{0,2},{1,5},{2,0},{3,7},{4,6},{5,1},{6,4},{7,3},{8,10},{9,13},{10,... | collective-permute-start | bytes 589832 | tf_op jit(solution)/shard_map/ppermute | solution.py:55
  64.2 9.2 %collective-permute-start.17 = (bf16[32,3072]{1,0:T(8,128)(2,1)S(1)}, bf16[32,3072]{1,0:T(8,128)(2,1)S(1)}, u32[]{:S(2)}, u32[]{:S(2)}) collective-permute-start(bf16[32,3072]{1,0:T(8,128)(2,1)S(1)} %collective-permute-done.15.refs_1_), channel_id=1, source_target_pairs={{0,4},{1,3},{2,6},{3,1},{4,0},{5,7},{6,2},{7,5},{8,12},{9,11},{10,... | collective-permute-start | bytes 589832 | tf_op jit(solution)/shard_map/ppermute | solution.py:55
  64.2 16.5 %collective-permute-start.20 = (bf16[32,3072]{1,0:T(8,128)(2,1)S(1)}, bf16[32,3072]{1,0:T(8,128)(2,1)S(1)}, u32[]{:S(2)}, u32[]{:S(2)}) collective-permute-start(bf16[32,3072]{1,0:T(8,128)(2,1)S(1)} %collective-permute-done.16.refs_2_), channel_id=1, source_target_pairs={{0,2},{1,5},{2,0},{3,7},{4,6},{5,1},{6,4},{7,3},{8,10},{9,13},{10,... | collective-permute-start | bytes 589832 | tf_op jit(solution)/shard_map/ppermute | solution.py:55
  65.7 16.0 %collective-permute-start.19 = (bf16[32,3072]{1,0:T(8,128)(2,1)S(1)}, bf16[32,3072]{1,0:T(8,128)(2,1)S(1)}, u32[]{:S(2)}, u32[]{:S(2)}) collective-permute-start(bf16[32,3072]{1,0:T(8,128)(2,1)S(1)} %collective-permute-done.15.refs_1_), channel_id=1, source_target_pairs={{0,2},{1,5},{2,0},{3,7},{4,6},{5,1},{6,4},{7,3},{8,10},{9,13},{10,... | collective-permute-start | bytes 589832 | tf_op jit(solution)/shard_map/ppermute | solution.py:55
  66.3 8.1 %collective-permute-start.8 = (bf16[32,1024]{1,0:T(8,128)(2,1)S(1)}, bf16[32,1024]{1,0:T(8,128)(2,1)S(1)}, u32[]{:S(2)}, u32[]{:S(2)}) collective-permute-start(bf16[32,1024]{1,0:T(8,128)(2,1)S(1)} %attend.2.refs_0_), channel_id=1, source_target_pairs={{0,8},{1,9},{2,10},{3,11},{4,12},{5,13},{6,14},{7,15},{8,0},{9,1},... | collective-permute-start | bytes 196616 | tf_op jit(solution)/shard_map/ppermute | solution.py:55
  73.4 9.3 %collective-permute-start.21 = (bf16[32,3072]{1,0:T(8,128)(2,1)S(1)}, bf16[32,3072]{1,0:T(8,128)(2,1)S(1)}, u32[]{:S(2)}, u32[]{:S(2)}) collective-permute-start(bf16[32,3072]{1,0:T(8,128)(2,1)S(1)} %collective-permute-done.17.refs_3_), channel_id=1, source_target_pairs={{0,2},{1,5},{2,0},{3,7},{4,6},{5,1},{6,4},{7,3},{8,10},{9,13},{10,... | collective-permute-start | bytes 589832 | tf_op jit(solution)/shard_map/ppermute | solution.py:55
  74.4 4.3 %collective-permute-start.9 = (bf16[32,1024]{1,0:T(8,128)(2,1)S(1)}, bf16[32,1024]{1,0:T(8,128)(2,1)S(1)}, u32[]{:S(2)}, u32[]{:S(2)}) collective-permute-start(bf16[32,1024]{1,0:T(8,128)(2,1)S(1)} %attend.2.refs_0_), channel_id=1, source_target_pairs={{0,4},{1,5},{2,6},{3,7},{4,0},{5,1},{6,2},{7,3},{8,12},{9,13},{10,... | collective-permute-start | bytes 196616 | tf_op jit(solution)/shard_map/ppermute | solution.py:55
  74.4 5.3 %collective-permute-start.10 = (bf16[32,1024]{1,0:T(8,128)(2,1)S(1)}, bf16[32,1024]{1,0:T(8,128)(2,1)S(1)}, u32[]{:S(2)}, u32[]{:S(2)}) collective-permute-start(bf16[32,1024]{1,0:T(8,128)(2,1)S(1)} %collective-permute-done.8.refs_1_), channel_id=1, source_target_pairs={{0,4},{1,5},{2,6},{3,7},{4,0},{5,1},{6,2},{7,3},{8,12},{9,13},{10,... | collective-permute-start | bytes 196616 | tf_op jit(solution)/shard_map/ppermute | solution.py:55
  78.6 9.7 %collective-permute-start.11 = (bf16[32,1024]{1,0:T(8,128)(2,1)S(1)}, bf16[32,1024]{1,0:T(8,128)(2,1)S(1)}, u32[]{:S(2)}, u32[]{:S(2)}) collective-permute-start(bf16[32,1024]{1,0:T(8,128)(2,1)S(1)} %attend.2.refs_0_), channel_id=1, source_target_pairs={{0,2},{1,3},{2,0},{3,1},{4,6},{5,7},{6,4},{7,5},{8,10},{9,11},{10,... | collective-permute-start | bytes 196616 | tf_op jit(solution)/shard_map/ppermute | solution.py:55
  79.7 8.6 %collective-permute-start.12 = (bf16[32,1024]{1,0:T(8,128)(2,1)S(1)}, bf16[32,1024]{1,0:T(8,128)(2,1)S(1)}, u32[]{:S(2)}, u32[]{:S(2)}) collective-permute-start(bf16[32,1024]{1,0:T(8,128)(2,1)S(1)} %collective-permute-done.8.refs_1_), channel_id=1, source_target_pairs={{0,2},{1,3},{2,0},{3,1},{4,6},{5,7},{6,4},{7,5},{8,10},{9,11},{10,... | collective-permute-start | bytes 196616 | tf_op jit(solution)/shard_map/ppermute | solution.py:55
  80.7 7.7 %collective-permute-start.13 = (bf16[32,1024]{1,0:T(8,128)(2,1)S(1)}, bf16[32,1024]{1,0:T(8,128)(2,1)S(1)}, u32[]{:S(2)}, u32[]{:S(2)}) collective-permute-start(bf16[32,1024]{1,0:T(8,128)(2,1)S(1)} %collective-permute-done.9.refs_2_), channel_id=1, source_target_pairs={{0,2},{1,3},{2,0},{3,1},{4,6},{5,7},{6,4},{7,5},{8,10},{9,11},{10,... | collective-permute-start | bytes 196616 | tf_op jit(solution)/shard_map/ppermute | solution.py:55
  81.8 6.6 %collective-permute-start.14 = (bf16[32,1024]{1,0:T(8,128)(2,1)S(1)}, bf16[32,1024]{1,0:T(8,128)(2,1)S(1)}, u32[]{:S(2)}, u32[]{:S(2)}) collective-permute-start(bf16[32,1024]{1,0:T(8,128)(2,1)S(1)} %collective-permute-done.10.refs_3_), channel_id=1, source_target_pairs={{0,2},{1,3},{2,0},{3,1},{4,6},{5,7},{6,4},{7,5},{8,10},{9,11},{10,... | collective-permute-start | bytes 196616 | tf_op jit(solution)/shard_map/ppermute | solution.py:55
  90.4 2.0 %collective-permute-start.22 = (bf16[128,2048]{1,0:T(8,128)(2,1)S(1)}, bf16[128,2048]{1,0:T(8,128)(2,1)S(1)}, u32[]{:S(2)}, u32[]{:S(2)}) collective-permute-start(bf16[128,2048]{1,0:T(8,128)(2,1)S(1)} %get-tuple-element.72), channel_id=1, source_target_pairs={{0,1},{1,0},{2,3},{3,2},{4,5},{5,4},{6,7},{7,6},{8,9},{9,8},{10,11... | collective-permute-start | bytes 1572872 | tf_op jit(solution)/shard_map/ppermute | solution.py:508

commit v12 on v10

--- a/solution.py
+++ b/solution.py
@@ -513,6 +513,10 @@
         for slot in range(1, n):
             top = slot.bit_length() - 1
             source = slots[slot - (1 << top)]
+            if slot == 1 and chunk == 0:
+                source = after(source, sums[1])
+            if slot == 3 << (levels - 2):
+                source = after(source, slots[1 << (levels - 1)])
             slots.append(
                 exchange(source, n, cores, levels - 1 - top, gather_orders(n, chunk))
             )

time: 84.3 us -> 82 us (0.973)
  starting transfers between devices: 30.7 us -> 29.1 us
    ppermute x21, starting transfers between devices: 30.6 us -> 29 us  [exchange(): return lax.ppermute(value, ('gx', 'gy'), pairs)]
  transfers between devices with their start and end apart: 22 -> 22, of which waited for: 7 -> 10; matrix products, arithmetic and copies ran while one was open for 2% -> 2% of each run, Pallas kernels for 32% -> 33%
where the time goes in v12:
time: 82 us; the launch traced here: 81.9 us
  Pallas kernels  35.2 us (43%)
  starting transfers between devices  29.1 us (35%)
  waiting for transfers between devices  14.6 us (18%)
  other arithmetic  2.58 us (3%)
    ppermute x21, starting transfers between devices, exchange(): return lax.ppermute(value, ('gx', 'gy'), pairs)  29 us
    pallas_call x3, Pallas kernels, project(): pl.pallas_call(functools.partial(project_kernel, n, q_start, kv_start, fi...  13.8 us
    ppermute x21, waiting for transfers between devices, exchange(): return lax.ppermute(value, ('gx', 'gy'), pairs)  12.7 us
    pallas_call x2, Pallas kernels, combine(): pl.pallas_call(functools.partial(combine_kernel, n, block, chunk), out_sh...  7.74 us
    pallas_call x2, Pallas kernels, attend(): pl.pallas_call(functools.partial(attend_kernel, chunk, offsets, kv_offset...  6.77 us
    pallas_call x1, Pallas kernels, fetch_rows(): pl.pallas_call(functools.partial(fetch_rows_kernel, start, pieces), out_s...  3.5 us
    pallas_call x1, Pallas kernels, fetch(): pl.pallas_call(functools.partial(fetch_kernel, len(arrays), pieces), out_...  3.47 us
    ppermute x1, waiting for transfers between devices, shards(): other = lax.ppermute(send, 'gy', [(0, 1), (1, 0)])  1.9 us
  transfers between devices with their start and end apart: 22, of which 10 were waited for; matrix products, arithmetic and copies ran while one was open for 2% of the time, Pallas kernels for 33%

profile of v12, /device:TPU:0, one launch (start us, length us, event | category | flops | bytes accessed | tf_op | source)
XLA Modules:
  0.0 81.9 jit_solution(3095950614298040099)
XLA Ops:
  0.0 4.4 %project.3 = (bf16[128,1152]{1,0:T(8,128)(2,1)S(1)}, f32[128,1152]{1,0:T(8,128)S(1)}, bf16[256,2048]{1,0:T(8,128)(2,1)S(1)}) custom-call(bf16[256,2048]{1,0:T(8,128)(2,1)} %refs_0_.1, f32[1,2048]{1,0:T(1,128)} %bitcast.1, bf16[2048,4096]{1,0:T(8,128)(2,1)} %refs_1_.3, bf16[2048,256]{1,0:T(8,128)(2,1)} %refs_2_.5, bf16[2048,256]{1,0:T(8,128)(2,1)} %refs_3_.5), custom_call_target="tpu_custom_call" | custom-call | tf_op jit(solution)/shard_map/project/pallas_call | solution.py:159
  4.4 3.0 %collective-permute-start = (bf16[128,1152]{1,0:T(8,128)(2,1)S(1)}, bf16[128,1152]{1,0:T(8,128)(2,1)S(1)}, u32[]{:S(2)}, u32[]{:S(2)}) collective-permute-start(bf16[128,1152]{1,0:T(8,128)(2,1)S(1)} %get-tuple-element.34), channel_id=1, source_target_pairs={{0,2},{1,5},{2,0},{3,7},{4,6},{5,1},{6,4},{7,3},{8,10},{9,13},{10,... | collective-permute-start | bytes 884744 | tf_op jit(solution)/shard_map/ppermute | solution.py:55
  7.4 3.9 %project.4 = (bf16[128,1280]{1,0:T(8,128)(2,1)S(1)}, f32[128,1280]{1,0:T(8,128)S(1)}) custom-call(bf16[256,2048]{1,0:T(8,128)(2,1)S(1)} %get-tuple-element.39.refs_0_, bf16[2048,4096]{1,0:T(8,128)(2,1)} %refs_1_.3, bf16[2048,256]{1,0:T(8,128)(2,1)} %refs_2_.5, bf16[2048,256]{1,0:T(8,128)(2,1)} %refs_3_.5), custom_call_target="tpu_custom_call" | custom-call | tf_op jit(solution)/shard_map/project/pallas_call | solution.py:159
  11.3 0.1 collective-permute-start.1
  11.4 0.8 collective-permute-done
  12.1 0.1 convert_add_fusion.2
  12.2 0.0 copy-start
  12.2 5.5 %project.5 = (bf16[128,2304]{1,0:T(8,128)(2,1)S(1)}, f32[128,2304]{1,0:T(8,128)S(1)}) custom-call(bf16[256,2048]{1,0:T(8,128)(2,1)S(1)} %get-tuple-element.39.refs_0_, bf16[2048,4096]{1,0:T(8,128)(2,1)} %refs_1_.3, bf16[2048,256]{1,0:T(8,128)(2,1)} %refs_2_.5, bf16[2048,256]{1,0:T(8,128)(2,1)} %refs_3_.5), custom_call_target="tpu_custom_call" | custom-call | tf_op jit(solution)/shard_map/project/pallas_call | solution.py:159
  17.7 0.7 collective-permute-done.1
  18.4 0.1 convert_add_fusion.1
  18.5 1.6 %collective-permute-start.3 = (bf16[64,2432]{1,0:T(8,128)(2,1)S(1)}, bf16[64,2432]{1,0:T(8,128)(2,1)}, u32[]{:S(2)}, u32[]{:S(2)}) collective-permute-start(bf16[64,2432]{1,0:T(8,128)(2,1)S(1)} %fusion.1), channel_id=1, source_target_pairs={{0,4},{1,3},{2,6},{3,1},{4,0},{5,7},{6,2},{7,5},{8,12},{9,11},{10,... | collective-permute-start | bytes 933896 | tf_op jit(solution)/shard_map/ppermute | solution.py:55
  20.2 0.1 add_convert_fusion.1
  20.2 0.1 convert_element_type.49
  20.3 1.4 %collective-permute-start.2 = (bf16[128,2304]{1,0:T(8,128)(2,1)S(1)}, bf16[128,2304]{1,0:T(8,128)(2,1)S(1)}, u32[]{:S(2)}, u32[]{:S(2)}) collective-permute-start(bf16[128,2304]{1,0:T(8,128)(2,1)S(1)} %get-tuple-element.44), channel_id=1, source_target_pairs={{0,2},{1,5},{2,0},{3,7},{4,6},{5,1},{6,4},{7,3},{8,10},{9,13},{10,... | collective-permute-start | bytes 1769480 | tf_op jit(solution)/shard_map/ppermute | solution.py:55
  21.7 3.5 %fetch_rows.1.refs_8_ = bf16[2048,2048]{1,0:T(8,128)(2,1)S(1)} custom-call(bf16[4096,2048]{1,0:T(8,128)(2,1)} %refs_6_.1), custom_call_target="tpu_custom_call" | custom-call | tf_op jit(solution)/shard_map/fetch_rows/pallas_call | solution.py:341
  25.2 5.3 %collective-permute-done.3 = bf16[64,2432]{1,0:T(8,128)(2,1)} collective-permute-done((bf16[64,2432]{1,0:T(8,128)(2,1)S(1)}, bf16[64,2432]{1,0:T(8,128)(2,1)}, u32[]{:S(2)}, u32[]{:S(2)}) %collective-permute-start.3) | collective-permute-done | bytes 311328 | tf_op jit(solution)/shard_map/ppermute | solution.py:55
  30.5 1.0 %fusion.2 = f32[64,2432]{1,0:T(8,128)S(1)} fusion(f32[128,1280]{1,0:T(8,128)S(1)} %convert_add_fusion.1, f32[128,1152]{1,0:T(8,128)S(1)} %convert_add_fusion.2, bf16[64,2432]{1,0:T(8,128)(2,1)} %collective-permute-done.3), kind=kLoop, calls=%fused_computation.8 | loop fusion | flops 466944 | bytes 2179072 | tf_op jit(solution)/shard_map/add | solution.py:469
  31.6 1.0 %collective-permute-start.5 = (bf16[32,2432]{1,0:T(8,128)(2,1)S(1)}, bf16[32,2432]{1,0:T(8,128)(2,1)S(1)}, u32[]{:S(2)}, u32[]{:S(2)}) collective-permute-start(bf16[32,2432]{1,0:T(8,128)(2,1)S(1)} %slice.64), channel_id=1, source_target_pairs={{0,8},{1,9},{2,10},{3,11},{4,12},{5,13},{6,14},{7,15},{8,0},{9,1},... | collective-permute-start | bytes 466952 | tf_op jit(solution)/shard_map/ppermute | solution.py:55
  32.6 0.0 collective-permute-done.2
  32.6 0.1 convert_add_fusion
  32.7 3.3 %collective-permute-start.4 = (bf16[64,2304]{1,0:T(8,128)(2,1)S(1)}, bf16[64,2304]{1,0:T(8,128)(2,1)S(1)}, u32[]{:S(2)}, u32[]{:S(2)}) collective-permute-start(bf16[64,2304]{1,0:T(8,128)(2,1)S(1)} %slice.63), channel_id=1, source_target_pairs={{0,4},{1,3},{2,6},{3,1},{4,0},{5,7},{6,2},{7,5},{8,12},{9,11},{10,... | collective-permute-start | bytes 884744 | tf_op jit(solution)/shard_map/ppermute | solution.py:55
  36.0 3.5 %fetch.1 = (bf16[8,1024,256]{2,1,0:T(8,128)(2,1)S(1)}, bf16[8,1024,256]{2,1,0:T(8,128)(2,1)S(1)}) custom-call(bf16[8,1024,256]{2,1,0:T(8,128)(2,1)} %refs_0_.2, bf16[8,1024,256]{2,1,0:T(8,128)(2,1)} %refs_1_.4), custom_call_target="tpu_custom_call" | custom-call | tf_op jit(solution)/shard_map/fetch/pallas_call | solution.py:312
  39.5 0.0 collective-permute-done.5
  39.6 2.0 %collective-permute-done.4 = bf16[64,2304]{1,0:T(8,128)(2,1)S(1)} collective-permute-done((bf16[64,2304]{1,0:T(8,128)(2,1)S(1)}, bf16[64,2304]{1,0:T(8,128)(2,1)S(1)}, u32[]{:S(2)}, u32[]{:S(2)}) %collective-permute-start.4) | collective-permute-done | bytes 294944 | tf_op jit(solution)/shard_map/ppermute | solution.py:55
  41.6 0.1 slice_add_fusion
  41.7 0.7 collective-permute-start.6
  42.4 0.1 fusion.3
  42.5 0.1 pad_maximum_fusion.1
  42.6 4.0 %attend.3 = (bf16[32,2048]{1,0:T(8,128)(2,1)S(1)}, bf16[2048,2048]{1,0:T(8,128)(2,1)S(1)}) custom-call(s32[8]{0:T(128)S(1)} %copy-done, f32[32,2432]{1,0:T(8,128)S(1)} %slice_add_fusion.1.refs_0_, f32[32,128]{1,0:T(8,128)S(1)} %slice.48.refs_1_, f32[32,128]{1,0:T(8,128)S(1)} %get-tuple-element.64.refs_2_, f32[32,128]{1,0:T(8,128)S(1)} %get-tuple-element.65.refs_3_, ...), custom_call_target="tpu_custom_call" | custom-call | tf_op jit(solution)/shard_map/attend/pallas_call | solution.py:279
  46.7 0.8 collective-permute-start.17
  47.5 1.7 %collective-permute-start.15 = (bf16[32,2048]{1,0:T(8,128)(2,1)S(1)}, bf16[32,2048]{1,0:T(8,128)(2,1)S(1)}, u32[]{:S(2)}, u32[]{:S(2)}) collective-permute-start(bf16[32,2048]{1,0:T(8,128)(2,1)S(1)} %get-tuple-element.56.refs_0_), channel_id=1, source_target_pairs={{0,4},{1,5},{2,6},{3,7},{4,0},{5,1},{6,2},{7,3},{8,12},{9,13},{10,... | collective-permute-start | bytes 393224 | tf_op jit(solution)/shard_map/ppermute | solution.py:55
  49.2 0.3 collective-permute-done.6
  49.5 0.8 %collective-permute-start.14 = (bf16[32,2048]{1,0:T(8,128)(2,1)S(1)}, bf16[32,2048]{1,0:T(8,128)(2,1)S(1)}, u32[]{:S(2)}, u32[]{:S(2)}) collective-permute-start(bf16[32,2048]{1,0:T(8,128)(2,1)S(1)} %get-tuple-element.56.refs_0_), channel_id=1, source_target_pairs={{0,8},{1,9},{2,10},{3,11},{4,12},{5,13},{6,14},{7,15},{8,0},{9,1},... | collective-permute-start | bytes 393224 | tf_op jit(solution)/shard_map/ppermute | solution.py:55
  50.4 2.7 %attend.2.refs_0_ = bf16[32,2048]{1,0:T(8,128)(2,1)S(1)} custom-call(s32[8]{0:T(128)S(1)} %copy-done, f32[32,2304]{1,0:T(8,128)S(1)} %slice_add_fusion.2.refs_0_, f32[32,128]{1,0:T(8,128)S(1)} %slice.48.refs_1_, f32[32,128]{1,0:T(8,128)S(1)} %get-tuple-element.64.refs_2_, f32[32,128]{1,0:T(8,128)S(1)} %get-tuple-element.65.refs_3_, ...), custom_call_target="tpu_custom_call" | custom-call | tf_op jit(solution)/shard_map/attend/pallas_call | solution.py:279
  53.1 2.2 %collective-permute-start.7 = (bf16[32,2048]{1,0:T(8,128)(2,1)S(1)}, bf16[32,2048]{1,0:T(8,128)(2,1)S(1)}, u32[]{:S(2)}, u32[]{:S(2)}) collective-permute-start(bf16[32,2048]{1,0:T(8,128)(2,1)S(1)} %attend.2.refs_0_), channel_id=1, source_target_pairs={{0,8},{1,9},{2,10},{3,11},{4,12},{5,13},{6,14},{7,15},{8,0},{9,1},... | collective-permute-start | bytes 393224 | tf_op jit(solution)/shard_map/ppermute | solution.py:55
  55.3 1.5 %collective-permute-start.10 = (bf16[32,2048]{1,0:T(8,128)(2,1)S(1)}, bf16[32,2048]{1,0:T(8,128)(2,1)S(1)}, u32[]{:S(2)}, u32[]{:S(2)}) collective-permute-start(bf16[32,2048]{1,0:T(8,128)(2,1)S(1)} %attend.2.refs_0_), channel_id=1, source_target_pairs={{0,2},{1,5},{2,0},{3,7},{4,6},{5,1},{6,4},{7,3},{8,10},{9,13},{10,... | collective-permute-start | bytes 393224 | tf_op jit(solution)/shard_map/ppermute | solution.py:55
  56.8 0.0 collective-permute-done.17.refs_4_
  56.8 0.0 collective-permute-start.8
  56.8 0.0 collective-permute-done.15.refs_2_
  56.8 2.2 %collective-permute-done.14.refs_1_ = bf16[32,2048]{1,0:T(8,128)(2,1)S(1)} collective-permute-done((bf16[32,2048]{1,0:T(8,128)(2,1)S(1)}, bf16[32,2048]{1,0:T(8,128)(2,1)S(1)}, u32[]{:S(2)}, u32[]{:S(2)}) %collective-permute-start.14) | collective-permute-done | bytes 131104 | tf_op jit(solution)/shard_map/ppermute | solution.py:55
  59.0 0.0 collective-permute-start.16
  59.0 2.3 %collective-permute-start.19 = (bf16[32,2048]{1,0:T(8,128)(2,1)S(1)}, bf16[32,2048]{1,0:T(8,128)(2,1)S(1)}, u32[]{:S(2)}, u32[]{:S(2)}) collective-permute-start(bf16[32,2048]{1,0:T(8,128)(2,1)S(1)} %collective-permute-done.15.refs_2_), channel_id=1, source_target_pairs={{0,2},{1,3},{2,0},{3,1},{4,6},{5,7},{6,4},{7,5},{8,10},{9,11},{10,... | collective-permute-start | bytes 393224 | tf_op jit(solution)/shard_map/ppermute | solution.py:55
  61.3 0.3 collective-permute-done.7.refs_1_
  61.5 1.8 %collective-permute-start.9 = (bf16[32,2048]{1,0:T(8,128)(2,1)S(1)}, bf16[32,2048]{1,0:T(8,128)(2,1)S(1)}, u32[]{:S(2)}, u32[]{:S(2)}) collective-permute-start(bf16[32,2048]{1,0:T(8,128)(2,1)S(1)} %collective-permute-done.7.refs_1_), channel_id=1, source_target_pairs={{0,4},{1,3},{2,6},{3,1},{4,0},{5,7},{6,2},{7,5},{8,12},{9,11},{10,... | collective-permute-start | bytes 393224 | tf_op jit(solution)/shard_map/ppermute | solution.py:55
  63.3 0.0 collective-permute-done.10.refs_4_
  63.3 0.0 collective-permute-done.8.refs_2_
  63.3 1.5 %collective-permute-start.12 = (bf16[32,2048]{1,0:T(8,128)(2,1)S(1)}, bf16[32,2048]{1,0:T(8,128)(2,1)S(1)}, u32[]{:S(2)}, u32[]{:S(2)}) collective-permute-start(bf16[32,2048]{1,0:T(8,128)(2,1)S(1)} %collective-permute-done.8.refs_2_), channel_id=1, source_target_pairs={{0,2},{1,5},{2,0},{3,7},{4,6},{5,1},{6,4},{7,3},{8,10},{9,13},{10,... | collective-permute-start | bytes 393224 | tf_op jit(solution)/shard_map/ppermute | solution.py:55
  64.8 0.5 collective-permute-start.18
  65.4 0.0 collective-permute-done.16.refs_3_
  65.4 2.3 %collective-permute-start.20 = (bf16[32,2048]{1,0:T(8,128)(2,1)S(1)}, bf16[32,2048]{1,0:T(8,128)(2,1)S(1)}, u32[]{:S(2)}, u32[]{:S(2)}) collective-permute-start(bf16[32,2048]{1,0:T(8,128)(2,1)S(1)} %collective-permute-done.16.refs_3_), channel_id=1, source_target_pairs={{0,2},{1,3},{2,0},{3,1},{4,6},{5,7},{6,4},{7,5},{8,10},{9,11},{10,... | collective-permute-start | bytes 393224 | tf_op jit(solution)/shard_map/ppermute | solution.py:55
  67.7 0.0 collective-permute-done.19.refs_6_
  67.7 0.0 collective-permute-start.11
  67.7 0.4 collective-permute-done.9.refs_3_
  68.1 2.4 %collective-permute-start.13 = (bf16[32,2048]{1,0:T(8,128)(2,1)S(1)}, bf16[32,2048]{1,0:T(8,128)(2,1)S(1)}, u32[]{:S(2)}, u32[]{:S(2)}) collective-permute-start(bf16[32,2048]{1,0:T(8,128)(2,1)S(1)} %collective-permute-done.9.refs_3_), channel_id=1, source_target_pairs={{0,2},{1,5},{2,0},{3,7},{4,6},{5,1},{6,4},{7,3},{8,10},{9,13},{10,... | collective-permute-start | bytes 393224 | tf_op jit(solution)/shard_map/ppermute | solution.py:55
  70.5 0.0 collective-permute-done.18.refs_5_
  70.5 0.7 collective-permute-done.20.refs_7_
  71.2 3.8 %combine.2.refs_8_ = f32[256,2048]{1,0:T(8,128)S(1)} custom-call(bf16[32,2048]{1,0:T(8,128)(2,1)S(1)} %get-tuple-element.56.refs_0_, bf16[32,2048]{1,0:T(8,128)(2,1)S(1)} %collective-permute-done.14.refs_1_, bf16[32,2048]{1,0:T(8,128)(2,1)S(1)} %collective-permute-done.15.refs_2_, bf16[32,2048]{1,0:T(8,128)(2,1)S(1)} %collective-permute-done.16.refs_3_, ...), custom_call_target="tpu_custom_call" | custom-call | tf_op jit(solution)/shard_map/combine/pallas_call | solution.py:400
  75.0 0.0 collective-permute-done.12.refs_6_
  75.0 0.0 collective-permute-done.11.refs_5_
  75.0 0.0 collective-permute-done.13.refs_7_
  75.0 3.9 %combine.3 = (bf16[128,2048]{1,0:T(8,128)(2,1)S(1)}, f32[128,2048]{1,0:T(8,128)S(1)}) custom-call(bf16[32,2048]{1,0:T(8,128)(2,1)S(1)} %attend.2.refs_0_, bf16[32,2048]{1,0:T(8,128)(2,1)S(1)} %collective-permute-done.7.refs_1_, bf16[32,2048]{1,0:T(8,128)(2,1)S(1)} %collective-permute-done.8.refs_2_, bf16[32,2048]{1,0:T(8,128)(2,1)S(1)} %collective-permute-done.9.refs_3_, ...), custom_call_target="tpu_custom_call" | custom-call | tf_op jit(solution)/shard_map/combine/pallas_call | solution.py:400
  79.0 0.1 collective-permute-start.21
  79.1 1.9 %collective-permute-done.21 = bf16[128,2048]{1,0:T(8,128)(2,1)S(1)} collective-permute-done((bf16[128,2048]{1,0:T(8,128)(2,1)S(1)}, bf16[128,2048]{1,0:T(8,128)(2,1)S(1)}, u32[]{:S(2)}, u32[]{:S(2)}) %collective-permute-start.21) | collective-permute-done | bytes 524320 | tf_op jit(solution)/shard_map/ppermute | solution.py:528
  81.0 0.9 %add_convert_fusion = bf16[128,2048]{1,0:T(8,128)(2,1)} fusion(f32[128,2048]{1,0:T(8,128)S(1)} %get-tuple-element.59, bf16[128,2048]{1,0:T(8,128)(2,1)S(1)} %collective-permute-done.21), kind=kLoop, calls=%fused_computation.3 | loop fusion | flops 786432 | bytes 2097152 | tf_op jit(solution)/shard_map/convert_element_type | solution.py:529
  (9 shorter events, 0.2 us)
Async XLA Ops:
  4.4 7.7 %collective-permute-start = (bf16[128,1152]{1,0:T(8,128)(2,1)S(1)}, bf16[128,1152]{1,0:T(8,128)(2,1)S(1)}, u32[]{:S(2)}, u32[]{:S(2)}) collective-permute-start(bf16[128,1152]{1,0:T(8,128)(2,1)S(1)} %get-tuple-element.34), channel_id=1, source_target_pairs={{0,2},{1,5},{2,0},{3,7},{4,6},{5,1},{6,4},{7,3},{8,10},{9,13},{10,... | collective-permute-start | bytes 884744 | tf_op jit(solution)/shard_map/ppermute | solution.py:55
  11.3 7.1 %collective-permute-start.1 = (bf16[128,1280]{1,0:T(8,128)(2,1)S(1)}, bf16[128,1280]{1,0:T(8,128)(2,1)S(1)}, u32[]{:S(2)}, u32[]{:S(2)}) collective-permute-start(bf16[128,1280]{1,0:T(8,128)(2,1)S(1)} %get-tuple-element.36), channel_id=1, source_target_pairs={{0,2},{1,5},{2,0},{3,7},{4,6},{5,1},{6,4},{7,3},{8,10},{9,13},{10,... | collective-permute-start | bytes 983048 | tf_op jit(solution)/shard_map/ppermute | solution.py:55
  12.2 8.0 %copy-start = (s32[8]{0:T(128)S(1)}, s32[8]{0:T(128)}, u32[]{:S(2)}) copy-start(s32[8]{0:T(128)} %length_ref.3) | copy-start | bytes 100
  18.5 12.0 %collective-permute-start.3 = (bf16[64,2432]{1,0:T(8,128)(2,1)S(1)}, bf16[64,2432]{1,0:T(8,128)(2,1)}, u32[]{:S(2)}, u32[]{:S(2)}) collective-permute-start(bf16[64,2432]{1,0:T(8,128)(2,1)S(1)} %fusion.1), channel_id=1, source_target_pairs={{0,4},{1,3},{2,6},{3,1},{4,0},{5,7},{6,2},{7,5},{8,12},{9,11},{10,... | collective-permute-start | bytes 933896 | tf_op jit(solution)/shard_map/ppermute | solution.py:55
  20.3 12.3 %collective-permute-start.2 = (bf16[128,2304]{1,0:T(8,128)(2,1)S(1)}, bf16[128,2304]{1,0:T(8,128)(2,1)S(1)}, u32[]{:S(2)}, u32[]{:S(2)}) collective-permute-start(bf16[128,2304]{1,0:T(8,128)(2,1)S(1)} %get-tuple-element.44), channel_id=1, source_target_pairs={{0,2},{1,5},{2,0},{3,7},{4,6},{5,1},{6,4},{7,3},{8,10},{9,13},{10,... | collective-permute-start | bytes 1769480 | tf_op jit(solution)/shard_map/ppermute | solution.py:55
  31.6 8.0 %collective-permute-start.5 = (bf16[32,2432]{1,0:T(8,128)(2,1)S(1)}, bf16[32,2432]{1,0:T(8,128)(2,1)S(1)}, u32[]{:S(2)}, u32[]{:S(2)}) collective-permute-start(bf16[32,2432]{1,0:T(8,128)(2,1)S(1)} %slice.64), channel_id=1, source_target_pairs={{0,8},{1,9},{2,10},{3,11},{4,12},{5,13},{6,14},{7,15},{8,0},{9,1},... | collective-permute-start | bytes 466952 | tf_op jit(solution)/shard_map/ppermute | solution.py:55
  32.7 8.9 %collective-permute-start.4 = (bf16[64,2304]{1,0:T(8,128)(2,1)S(1)}, bf16[64,2304]{1,0:T(8,128)(2,1)S(1)}, u32[]{:S(2)}, u32[]{:S(2)}) collective-permute-start(bf16[64,2304]{1,0:T(8,128)(2,1)S(1)} %slice.63), channel_id=1, source_target_pairs={{0,4},{1,3},{2,6},{3,1},{4,0},{5,7},{6,2},{7,5},{8,12},{9,11},{10,... | collective-permute-start | bytes 884744 | tf_op jit(solution)/shard_map/ppermute | solution.py:55
  41.7 7.8 %collective-permute-start.6 = (bf16[32,2304]{1,0:T(8,128)(2,1)S(1)}, bf16[32,2304]{1,0:T(8,128)(2,1)S(1)}, u32[]{:S(2)}, u32[]{:S(2)}) collective-permute-start(bf16[32,2304]{1,0:T(8,128)(2,1)S(1)} %slice.65), channel_id=1, source_target_pairs={{0,8},{1,9},{2,10},{3,11},{4,12},{5,13},{6,14},{7,15},{8,0},{9,1},... | collective-permute-start | bytes 442376 | tf_op jit(solution)/shard_map/ppermute | solution.py:55
  46.7 10.1 %collective-permute-start.17 = (bf16[32,2048]{1,0:T(8,128)(2,1)S(1)}, bf16[32,2048]{1,0:T(8,128)(2,1)S(1)}, u32[]{:S(2)}, u32[]{:S(2)}) collective-permute-start(bf16[32,2048]{1,0:T(8,128)(2,1)S(1)} %get-tuple-element.56.refs_0_), channel_id=1, source_target_pairs={{0,2},{1,3},{2,0},{3,1},{4,6},{5,7},{6,4},{7,5},{8,10},{9,11},{10,... | collective-permute-start | bytes 393224 | tf_op jit(solution)/shard_map/ppermute | solution.py:55
  47.5 9.3 %collective-permute-start.15 = (bf16[32,2048]{1,0:T(8,128)(2,1)S(1)}, bf16[32,2048]{1,0:T(8,128)(2,1)S(1)}, u32[]{:S(2)}, u32[]{:S(2)}) collective-permute-start(bf16[32,2048]{1,0:T(8,128)(2,1)S(1)} %get-tuple-element.56.refs_0_), channel_id=1, source_target_pairs={{0,4},{1,5},{2,6},{3,7},{4,0},{5,1},{6,2},{7,3},{8,12},{9,13},{10,... | collective-permute-start | bytes 393224 | tf_op jit(solution)/shard_map/ppermute | solution.py:55
  49.5 9.4 %collective-permute-start.14 = (bf16[32,2048]{1,0:T(8,128)(2,1)S(1)}, bf16[32,2048]{1,0:T(8,128)(2,1)S(1)}, u32[]{:S(2)}, u32[]{:S(2)}) collective-permute-start(bf16[32,2048]{1,0:T(8,128)(2,1)S(1)} %get-tuple-element.56.refs_0_), channel_id=1, source_target_pairs={{0,8},{1,9},{2,10},{3,11},{4,12},{5,13},{6,14},{7,15},{8,0},{9,1},... | collective-permute-start | bytes 393224 | tf_op jit(solution)/shard_map/ppermute | solution.py:55
  53.1 8.5 %collective-permute-start.7 = (bf16[32,2048]{1,0:T(8,128)(2,1)S(1)}, bf16[32,2048]{1,0:T(8,128)(2,1)S(1)}, u32[]{:S(2)}, u32[]{:S(2)}) collective-permute-start(bf16[32,2048]{1,0:T(8,128)(2,1)S(1)} %attend.2.refs_0_), channel_id=1, source_target_pairs={{0,8},{1,9},{2,10},{3,11},{4,12},{5,13},{6,14},{7,15},{8,0},{9,1},... | collective-permute-start | bytes 393224 | tf_op jit(solution)/shard_map/ppermute | solution.py:55
  55.3 8.0 %collective-permute-start.10 = (bf16[32,2048]{1,0:T(8,128)(2,1)S(1)}, bf16[32,2048]{1,0:T(8,128)(2,1)S(1)}, u32[]{:S(2)}, u32[]{:S(2)}) collective-permute-start(bf16[32,2048]{1,0:T(8,128)(2,1)S(1)} %attend.2.refs_0_), channel_id=1, source_target_pairs={{0,2},{1,5},{2,0},{3,7},{4,6},{5,1},{6,4},{7,3},{8,10},{9,13},{10,... | collective-permute-start | bytes 393224 | tf_op jit(solution)/shard_map/ppermute | solution.py:55
  56.8 6.5 %collective-permute-start.8 = (bf16[32,2048]{1,0:T(8,128)(2,1)S(1)}, bf16[32,2048]{1,0:T(8,128)(2,1)S(1)}, u32[]{:S(2)}, u32[]{:S(2)}) collective-permute-start(bf16[32,2048]{1,0:T(8,128)(2,1)S(1)} %attend.2.refs_0_), channel_id=1, source_target_pairs={{0,4},{1,3},{2,6},{3,1},{4,0},{5,7},{6,2},{7,5},{8,12},{9,11},{10,... | collective-permute-start | bytes 393224 | tf_op jit(solution)/shard_map/ppermute | solution.py:55
  59.0 6.4 %collective-permute-start.16 = (bf16[32,2048]{1,0:T(8,128)(2,1)S(1)}, bf16[32,2048]{1,0:T(8,128)(2,1)S(1)}, u32[]{:S(2)}, u32[]{:S(2)}) collective-permute-start(bf16[32,2048]{1,0:T(8,128)(2,1)S(1)} %collective-permute-done.14.refs_1_), channel_id=1, source_target_pairs={{0,4},{1,5},{2,6},{3,7},{4,0},{5,1},{6,2},{7,3},{8,12},{9,13},{10,... | collective-permute-start | bytes 393224 | tf_op jit(solution)/shard_map/ppermute | solution.py:55
  59.0 8.7 %collective-permute-start.19 = (bf16[32,2048]{1,0:T(8,128)(2,1)S(1)}, bf16[32,2048]{1,0:T(8,128)(2,1)S(1)}, u32[]{:S(2)}, u32[]{:S(2)}) collective-permute-start(bf16[32,2048]{1,0:T(8,128)(2,1)S(1)} %collective-permute-done.15.refs_2_), channel_id=1, source_target_pairs={{0,2},{1,3},{2,0},{3,1},{4,6},{5,7},{6,4},{7,5},{8,10},{9,11},{10,... | collective-permute-start | bytes 393224 | tf_op jit(solution)/shard_map/ppermute | solution.py:55
  61.5 6.5 %collective-permute-start.9 = (bf16[32,2048]{1,0:T(8,128)(2,1)S(1)}, bf16[32,2048]{1,0:T(8,128)(2,1)S(1)}, u32[]{:S(2)}, u32[]{:S(2)}) collective-permute-start(bf16[32,2048]{1,0:T(8,128)(2,1)S(1)} %collective-permute-done.7.refs_1_), channel_id=1, source_target_pairs={{0,4},{1,3},{2,6},{3,1},{4,0},{5,7},{6,2},{7,5},{8,12},{9,11},{10,... | collective-permute-start | bytes 393224 | tf_op jit(solution)/shard_map/ppermute | solution.py:55
  63.3 11.7 %collective-permute-start.12 = (bf16[32,2048]{1,0:T(8,128)(2,1)S(1)}, bf16[32,2048]{1,0:T(8,128)(2,1)S(1)}, u32[]{:S(2)}, u32[]{:S(2)}) collective-permute-start(bf16[32,2048]{1,0:T(8,128)(2,1)S(1)} %collective-permute-done.8.refs_2_), channel_id=1, source_target_pairs={{0,2},{1,5},{2,0},{3,7},{4,6},{5,1},{6,4},{7,3},{8,10},{9,13},{10,... | collective-permute-start | bytes 393224 | tf_op jit(solution)/shard_map/ppermute | solution.py:55
  64.8 5.7 %collective-permute-start.18 = (bf16[32,2048]{1,0:T(8,128)(2,1)S(1)}, bf16[32,2048]{1,0:T(8,128)(2,1)S(1)}, u32[]{:S(2)}, u32[]{:S(2)}) collective-permute-start(bf16[32,2048]{1,0:T(8,128)(2,1)S(1)} %collective-permute-done.14.refs_1_), channel_id=1, source_target_pairs={{0,2},{1,3},{2,0},{3,1},{4,6},{5,7},{6,4},{7,5},{8,10},{9,11},{10,... | collective-permute-start | bytes 393224 | tf_op jit(solution)/shard_map/ppermute | solution.py:55
  65.4 5.8 %collective-permute-start.20 = (bf16[32,2048]{1,0:T(8,128)(2,1)S(1)}, bf16[32,2048]{1,0:T(8,128)(2,1)S(1)}, u32[]{:S(2)}, u32[]{:S(2)}) collective-permute-start(bf16[32,2048]{1,0:T(8,128)(2,1)S(1)} %collective-permute-done.16.refs_3_), channel_id=1, source_target_pairs={{0,2},{1,3},{2,0},{3,1},{4,6},{5,7},{6,4},{7,5},{8,10},{9,11},{10,... | collective-permute-start | bytes 393224 | tf_op jit(solution)/shard_map/ppermute | solution.py:55
  67.7 7.3 %collective-permute-start.11 = (bf16[32,2048]{1,0:T(8,128)(2,1)S(1)}, bf16[32,2048]{1,0:T(8,128)(2,1)S(1)}, u32[]{:S(2)}, u32[]{:S(2)}) collective-permute-start(bf16[32,2048]{1,0:T(8,128)(2,1)S(1)} %collective-permute-done.7.refs_1_), channel_id=1, source_target_pairs={{0,2},{1,5},{2,0},{3,7},{4,6},{5,1},{6,4},{7,3},{8,10},{9,13},{10,... | collective-permute-start | bytes 393224 | tf_op jit(solution)/shard_map/ppermute | solution.py:55
  68.1 6.9 %collective-permute-start.13 = (bf16[32,2048]{1,0:T(8,128)(2,1)S(1)}, bf16[32,2048]{1,0:T(8,128)(2,1)S(1)}, u32[]{:S(2)}, u32[]{:S(2)}) collective-permute-start(bf16[32,2048]{1,0:T(8,128)(2,1)S(1)} %collective-permute-done.9.refs_3_), channel_id=1, source_target_pairs={{0,2},{1,5},{2,0},{3,7},{4,6},{5,1},{6,4},{7,3},{8,10},{9,13},{10,... | collective-permute-start | bytes 393224 | tf_op jit(solution)/shard_map/ppermute | solution.py:55
  79.0 2.0 %collective-permute-start.21 = (bf16[128,2048]{1,0:T(8,128)(2,1)S(1)}, bf16[128,2048]{1,0:T(8,128)(2,1)S(1)}, u32[]{:S(2)}, u32[]{:S(2)}) collective-permute-start(bf16[128,2048]{1,0:T(8,128)(2,1)S(1)} %get-tuple-element.60), channel_id=1, source_target_pairs={{0,1},{1,0},{2,3},{3,2},{4,5},{5,4},{6,7},{7,6},{8,9},{9,8},{10,11... | collective-permute-start | bytes 1572872 | tf_op jit(solution)/shard_map/ppermute | solution.py:528

commit v13 on v12

--- a/solution.py
+++ b/solution.py
@@ -15,7 +15,7 @@
 THETA = 500000.0
 
 CHUNKS = 2
-TILES = 4
+TILES = 2
 MIB = 1 << 20
 
 
@@ -355,19 +355,12 @@
     moved = jnp.where(gy == 0, n // 2, 0)
     if chunk:
         before_ref, refs = refs[0], refs[1:]
-    w_ref, outs, (x_buf, x_sems) = refs[0], refs[1:-2], refs[-2:]
+    w_ref, outs, x_buf = refs[0], refs[1:-1], refs[-1]
     depth, cols = x_buf.shape[1], w_ref.shape[1]
     half = x_buf.shape[0] // 2
-    x_copies = []
     for slot, piece in enumerate(pieces):
         start = pl.multiple_of((slot_owner(n, slot, gx, gy, gather_orders(n, chunk)) ^ moved) * block, block)
-        x_copies.append(
-            pltpu.make_async_copy(piece, x_buf.at[pl.ds(start, block), :], x_sems.at[slot])
-        )
-    for copy in x_copies:
-        copy.start()
-    for copy in x_copies:
-        copy.wait()
+        x_buf[pl.ds(start, block), :] = piece[...]
 
     tile = cols // TILES
     for start in range(0, cols, tile):
@@ -400,13 +393,10 @@
     return pl.pallas_call(
         functools.partial(combine_kernel, n, block, chunk),
         out_shape=out_shape,
-        in_specs=[pl.BlockSpec(memory_space=pl.ANY)] * len(pieces)
-        + [vmem] * len(earlier)
-        + [vmem],
+        in_specs=[vmem] * (len(pieces) + len(earlier) + 1),
         out_specs=[vmem] * len(out_shape),
         scratch_shapes=[
             pltpu.VMEM((rows, depth), jnp.bfloat16),
-            pltpu.SemaphoreType.DMA((n,)),
         ],
         compiler_params=pltpu.CompilerParams(vmem_limit_bytes=16 * MIB),
         name="combine",
@@ -490,13 +480,16 @@
     offsets = [[at if at < share else at + 128 for at in plain], plain]
     kv_offsets = [q_cols + 128, q_cols]
 
-    attentions = []
+    attentions, early = [], {}
     for chunk in range(CHUNKS):
+        total = sums[chunk]
+        if chunk == 1:
+            total = after(total, *early.values())
         out = attend(
             chunk,
             offsets[chunk],
             kv_offsets[chunk],
-            sums[chunk],
+            total,
             squares,
             cosine,
             sine,
@@ -507,6 +500,11 @@
         )
         attentions.append(out[0])
         weights += out[1:]
+        if chunk == 0:
+            for stage in [0]:
+                early[1 << (levels - 1 - stage)] = exchange(
+                    out[0], n, cores, stage, gather_orders(n, 0)
+                )
     gathered = []
     for chunk in range(CHUNKS):
         slots = [attentions[chunk]]
@@ -517,6 +515,11 @@
                 source = after(source, sums[1])
             if slot == 3 << (levels - 2):
                 source = after(source, slots[1 << (levels - 1)])
+            if chunk == 1 and slot > n // 2:
+                source = after(source, gathered[0][slot])
+            if chunk == 0 and slot in early:
+                slots.append(early[slot])
+                continue
             slots.append(
                 exchange(source, n, cores, levels - 1 - top, gather_orders(n, chunk))
             )

time: 82 us -> 82.8 us (level)
  waiting for transfers between devices: 14.6 us -> 26.3 us
  starting transfers between devices: 29.1 us -> 21.1 us
  Pallas kernels: 35.2 us -> 32.4 us
    ppermute x21, waiting for transfers between devices: 12.7 us -> 24.4 us  [exchange(): return lax.ppermute(value, ('gx', 'gy'), pairs)]
    ppermute x21, starting transfers between devices: 29 us -> 21 us  [exchange(): return lax.ppermute(value, ('gx', 'gy'), pairs)]
    pallas_call x2, Pallas kernels: 7.74 us -> 4.89 us  [combine(): pl.pallas_call(functools.partial(combine_kernel, n, block, chunk), out_sh...]
  transfers between devices with their start and end apart: 22 -> 22, of which waited for: 10 -> 15; matrix products, arithmetic and copies ran while one was open for 2% -> 2% of each run, Pallas kernels for 33% -> 31%
where the time goes in v13:
time: 82.8 us; the launch traced here: 82.7 us
  Pallas kernels  32.4 us (39%)
  waiting for transfers between devices  26.3 us (32%)
  starting transfers between devices  21.1 us (25%)
  other arithmetic  2.58 us (3%)
    ppermute x21, waiting for transfers between devices, exchange(): return lax.ppermute(value, ('gx', 'gy'), pairs)  24.4 us
    ppermute x21, starting transfers between devices, exchange(): return lax.ppermute(value, ('gx', 'gy'), pairs)  21 us
    pallas_call x3, Pallas kernels, project(): pl.pallas_call(functools.partial(project_kernel, n, q_start, kv_start, fi...  13.8 us
    pallas_call x2, Pallas kernels, attend(): pl.pallas_call(functools.partial(attend_kernel, chunk, offsets, kv_offset...  6.77 us
    pallas_call x2, Pallas kernels, combine(): pl.pallas_call(functools.partial(combine_kernel, n, block, chunk), out_sh...  4.89 us
    pallas_call x1, Pallas kernels, fetch_rows(): pl.pallas_call(functools.partial(fetch_rows_kernel, start, pieces), out_s...  3.5 us
    pallas_call x1, Pallas kernels, fetch(): pl.pallas_call(functools.partial(fetch_kernel, len(arrays), pieces), out_...  3.47 us
    ppermute x1, waiting for transfers between devices, shards(): other = lax.ppermute(send, 'gy', [(0, 1), (1, 0)])  1.9 us
  transfers between devices with their start and end apart: 22, of which 15 were waited for; matrix products, arithmetic and copies ran while one was open for 2% of the time, Pallas kernels for 31%

profile of v13, /device:TPU:0, one launch (start us, length us, event | category | flops | bytes accessed | tf_op | source)
XLA Modules:
  0.0 82.7 jit_solution(1947099682970209716)
XLA Ops:
  0.0 4.4 %project.3 = (bf16[128,1152]{1,0:T(8,128)(2,1)S(1)}, f32[128,1152]{1,0:T(8,128)S(1)}, bf16[256,2048]{1,0:T(8,128)(2,1)S(1)}) custom-call(bf16[256,2048]{1,0:T(8,128)(2,1)} %refs_0_.1, f32[1,2048]{1,0:T(1,128)} %bitcast.1, bf16[2048,4096]{1,0:T(8,128)(2,1)} %refs_1_.3, bf16[2048,256]{1,0:T(8,128)(2,1)} %refs_2_.5, bf16[2048,256]{1,0:T(8,128)(2,1)} %refs_3_.5), custom_call_target="tpu_custom_call" | custom-call | tf_op jit(solution)/shard_map/project/pallas_call | solution.py:159
  4.4 3.0 %collective-permute-start = (bf16[128,1152]{1,0:T(8,128)(2,1)S(1)}, bf16[128,1152]{1,0:T(8,128)(2,1)S(1)}, u32[]{:S(2)}, u32[]{:S(2)}) collective-permute-start(bf16[128,1152]{1,0:T(8,128)(2,1)S(1)} %get-tuple-element.38), channel_id=1, source_target_pairs={{0,2},{1,5},{2,0},{3,7},{4,6},{5,1},{6,4},{7,3},{8,10},{9,13},{10,... | collective-permute-start | bytes 884744 | tf_op jit(solution)/shard_map/ppermute | solution.py:55
  7.4 3.9 %project.4 = (bf16[128,1280]{1,0:T(8,128)(2,1)S(1)}, f32[128,1280]{1,0:T(8,128)S(1)}) custom-call(bf16[256,2048]{1,0:T(8,128)(2,1)S(1)} %get-tuple-element.43.refs_0_, bf16[2048,4096]{1,0:T(8,128)(2,1)} %refs_1_.3, bf16[2048,256]{1,0:T(8,128)(2,1)} %refs_2_.5, bf16[2048,256]{1,0:T(8,128)(2,1)} %refs_3_.5), custom_call_target="tpu_custom_call" | custom-call | tf_op jit(solution)/shard_map/project/pallas_call | solution.py:159
  11.3 0.1 collective-permute-start.1
  11.4 0.8 collective-permute-done
  12.1 0.1 convert_add_fusion.2
  12.2 0.0 copy-start
  12.2 5.5 %project.5 = (bf16[128,2304]{1,0:T(8,128)(2,1)S(1)}, f32[128,2304]{1,0:T(8,128)S(1)}) custom-call(bf16[256,2048]{1,0:T(8,128)(2,1)S(1)} %get-tuple-element.43.refs_0_, bf16[2048,4096]{1,0:T(8,128)(2,1)} %refs_1_.3, bf16[2048,256]{1,0:T(8,128)(2,1)} %refs_2_.5, bf16[2048,256]{1,0:T(8,128)(2,1)} %refs_3_.5), custom_call_target="tpu_custom_call" | custom-call | tf_op jit(solution)/shard_map/project/pallas_call | solution.py:159
  17.7 0.7 collective-permute-done.1
  18.4 0.1 convert_add_fusion.1
  18.5 1.6 %collective-permute-start.3 = (bf16[64,2432]{1,0:T(8,128)(2,1)S(1)}, bf16[64,2432]{1,0:T(8,128)(2,1)}, u32[]{:S(2)}, u32[]{:S(2)}) collective-permute-start(bf16[64,2432]{1,0:T(8,128)(2,1)S(1)} %fusion.1), channel_id=1, source_target_pairs={{0,4},{1,3},{2,6},{3,1},{4,0},{5,7},{6,2},{7,5},{8,12},{9,11},{10,... | collective-permute-start | bytes 933896 | tf_op jit(solution)/shard_map/ppermute | solution.py:55
  20.2 0.1 add_convert_fusion.1
  20.2 0.1 convert_element_type.49
  20.3 1.4 %collective-permute-start.2 = (bf16[128,2304]{1,0:T(8,128)(2,1)S(1)}, bf16[128,2304]{1,0:T(8,128)(2,1)S(1)}, u32[]{:S(2)}, u32[]{:S(2)}) collective-permute-start(bf16[128,2304]{1,0:T(8,128)(2,1)S(1)} %get-tuple-element.48), channel_id=1, source_target_pairs={{0,2},{1,5},{2,0},{3,7},{4,6},{5,1},{6,4},{7,3},{8,10},{9,13},{10,... | collective-permute-start | bytes 1769480 | tf_op jit(solution)/shard_map/ppermute | solution.py:55
  21.7 3.5 %fetch_rows.1.refs_8_ = bf16[2048,2048]{1,0:T(8,128)(2,1)S(1)} custom-call(bf16[4096,2048]{1,0:T(8,128)(2,1)} %refs_6_.1), custom_call_target="tpu_custom_call" | custom-call | tf_op jit(solution)/shard_map/fetch_rows/pallas_call | solution.py:341
  25.2 5.3 %collective-permute-done.3 = bf16[64,2432]{1,0:T(8,128)(2,1)} collective-permute-done((bf16[64,2432]{1,0:T(8,128)(2,1)S(1)}, bf16[64,2432]{1,0:T(8,128)(2,1)}, u32[]{:S(2)}, u32[]{:S(2)}) %collective-permute-start.3) | collective-permute-done | bytes 311328 | tf_op jit(solution)/shard_map/ppermute | solution.py:55
  30.5 1.0 %fusion.2 = f32[64,2432]{1,0:T(8,128)S(1)} fusion(f32[128,1280]{1,0:T(8,128)S(1)} %convert_add_fusion.1, f32[128,1152]{1,0:T(8,128)S(1)} %convert_add_fusion.2, bf16[64,2432]{1,0:T(8,128)(2,1)} %collective-permute-done.3), kind=kLoop, calls=%fused_computation.8 | loop fusion | flops 466944 | bytes 2179072 | tf_op jit(solution)/shard_map/add | solution.py:459
  31.6 1.0 %collective-permute-start.5 = (bf16[32,2432]{1,0:T(8,128)(2,1)S(1)}, bf16[32,2432]{1,0:T(8,128)(2,1)S(1)}, u32[]{:S(2)}, u32[]{:S(2)}) collective-permute-start(bf16[32,2432]{1,0:T(8,128)(2,1)S(1)} %slice.64), channel_id=1, source_target_pairs={{0,8},{1,9},{2,10},{3,11},{4,12},{5,13},{6,14},{7,15},{8,0},{9,1},... | collective-permute-start | bytes 466952 | tf_op jit(solution)/shard_map/ppermute | solution.py:55
  32.6 0.0 collective-permute-done.2
  32.6 0.1 convert_add_fusion
  32.7 3.3 %collective-permute-start.4 = (bf16[64,2304]{1,0:T(8,128)(2,1)S(1)}, bf16[64,2304]{1,0:T(8,128)(2,1)S(1)}, u32[]{:S(2)}, u32[]{:S(2)}) collective-permute-start(bf16[64,2304]{1,0:T(8,128)(2,1)S(1)} %slice.63), channel_id=1, source_target_pairs={{0,4},{1,3},{2,6},{3,1},{4,0},{5,7},{6,2},{7,5},{8,12},{9,11},{10,... | collective-permute-start | bytes 884744 | tf_op jit(solution)/shard_map/ppermute | solution.py:55
  36.0 3.5 %fetch.1 = (bf16[8,1024,256]{2,1,0:T(8,128)(2,1)S(1)}, bf16[8,1024,256]{2,1,0:T(8,128)(2,1)S(1)}) custom-call(bf16[8,1024,256]{2,1,0:T(8,128)(2,1)} %refs_0_.2, bf16[8,1024,256]{2,1,0:T(8,128)(2,1)} %refs_1_.4), custom_call_target="tpu_custom_call" | custom-call | tf_op jit(solution)/shard_map/fetch/pallas_call | solution.py:312
  39.5 0.0 collective-permute-done.5
  39.6 2.0 %collective-permute-done.4 = bf16[64,2304]{1,0:T(8,128)(2,1)S(1)} collective-permute-done((bf16[64,2304]{1,0:T(8,128)(2,1)S(1)}, bf16[64,2304]{1,0:T(8,128)(2,1)S(1)}, u32[]{:S(2)}, u32[]{:S(2)}) %collective-permute-start.4) | collective-permute-done | bytes 294944 | tf_op jit(solution)/shard_map/ppermute | solution.py:55
  41.6 0.1 slice_add_fusion
  41.7 0.7 collective-permute-start.6
  42.4 0.1 fusion.3
  42.5 0.1 pad_maximum_fusion.1
  42.6 4.0 %attend.2 = (bf16[32,2048]{1,0:T(8,128)(2,1)S(1)}, bf16[2048,2048]{1,0:T(8,128)(2,1)S(1)}) custom-call(s32[8]{0:T(128)S(1)} %copy-done, f32[32,2432]{1,0:T(8,128)S(1)} %slice_add_fusion.1.refs_0_, f32[32,128]{1,0:T(8,128)S(1)} %slice.48.refs_1_, f32[32,128]{1,0:T(8,128)S(1)} %get-tuple-element.72.refs_2_, f32[32,128]{1,0:T(8,128)S(1)} %get-tuple-element.73.refs_3_, ...), custom_call_target="tpu_custom_call" | custom-call | tf_op jit(solution)/shard_map/attend/pallas_call | solution.py:279
  46.7 0.8 collective-permute-start.7
  47.5 2.4 %collective-permute-done.6 = bf16[32,2304]{1,0:T(8,128)(2,1)S(1)} collective-permute-done((bf16[32,2304]{1,0:T(8,128)(2,1)S(1)}, bf16[32,2304]{1,0:T(8,128)(2,1)S(1)}, u32[]{:S(2)}, u32[]{:S(2)}) %collective-permute-start.6) | collective-permute-done | bytes 147488 | tf_op jit(solution)/shard_map/ppermute | solution.py:55
  49.9 0.3 collective-permute-start.12
  50.1 3.4 %collective-permute-start.15 = (bf16[32,2048]{1,0:T(8,128)(2,1)S(1)}, bf16[32,2048]{1,0:T(8,128)(2,1)S(1)}, u32[]{:S(2)}, u32[]{:S(2)}) collective-permute-start(bf16[32,2048]{1,0:T(8,128)(2,1)S(1)} %get-tuple-element.60.refs_0_), channel_id=1, source_target_pairs={{0,4},{1,5},{2,6},{3,7},{4,0},{5,1},{6,2},{7,3},{8,12},{9,13},{10,... | collective-permute-start | bytes 393224 | tf_op jit(solution)/shard_map/ppermute | solution.py:55
  53.6 0.0 collective-permute-done.7.refs_4_
  53.6 2.7 %attend.3.refs_0_ = bf16[32,2048]{1,0:T(8,128)(2,1)S(1)} custom-call(s32[8]{0:T(128)S(1)} %copy-done, f32[32,2304]{1,0:T(8,128)S(1)} %slice_add_fusion.2.refs_0_, f32[32,128]{1,0:T(8,128)S(1)} %slice.48.refs_1_, f32[32,128]{1,0:T(8,128)S(1)} %get-tuple-element.72.refs_2_, f32[32,128]{1,0:T(8,128)S(1)} %get-tuple-element.73.refs_3_, ...), custom_call_target="tpu_custom_call" | custom-call | tf_op jit(solution)/shard_map/attend/pallas_call | solution.py:279
  56.3 0.5 collective-permute-start.8
  56.8 1.1 %collective-permute-start.9 = (bf16[32,2048]{1,0:T(8,128)(2,1)S(1)}, bf16[32,2048]{1,0:T(8,128)(2,1)S(1)}, u32[]{:S(2)}, u32[]{:S(2)}) collective-permute-start(bf16[32,2048]{1,0:T(8,128)(2,1)S(1)} %attend.3.refs_0_), channel_id=1, source_target_pairs={{0,4},{1,3},{2,6},{3,1},{4,0},{5,7},{6,2},{7,5},{8,12},{9,11},{10,... | collective-permute-start | bytes 393224 | tf_op jit(solution)/shard_map/ppermute | solution.py:55
  57.9 1.2 %collective-permute-done.12.refs_1_ = bf16[32,2048]{1,0:T(8,128)(2,1)S(1)} collective-permute-done((bf16[32,2048]{1,0:T(8,128)(2,1)S(1)}, bf16[32,2048]{1,0:T(8,128)(2,1)S(1)}, u32[]{:S(2)}, u32[]{:S(2)}) %collective-permute-start.12) | collective-permute-done | bytes 131104 | tf_op jit(solution)/shard_map/ppermute | solution.py:55
  59.1 0.1 collective-permute-start.18
  59.2 0.0 collective-permute-done.15.refs_2_
  59.2 0.7 collective-permute-start.11
  59.9 1.4 %collective-permute-start.16 = (bf16[32,2048]{1,0:T(8,128)(2,1)S(1)}, bf16[32,2048]{1,0:T(8,128)(2,1)S(1)}, u32[]{:S(2)}, u32[]{:S(2)}) collective-permute-start(bf16[32,2048]{1,0:T(8,128)(2,1)S(1)} %collective-permute-done.15.refs_2_), channel_id=1, source_target_pairs={{0,2},{1,3},{2,0},{3,1},{4,6},{5,7},{6,4},{7,5},{8,10},{9,11},{10,... | collective-permute-start | bytes 393224 | tf_op jit(solution)/shard_map/ppermute | solution.py:55
  61.2 2.4 %collective-permute-done.8.refs_1_ = bf16[32,2048]{1,0:T(8,128)(2,1)S(1)} collective-permute-done((bf16[32,2048]{1,0:T(8,128)(2,1)S(1)}, bf16[32,2048]{1,0:T(8,128)(2,1)S(1)}, u32[]{:S(2)}, u32[]{:S(2)}) %collective-permute-start.8) | collective-permute-done | bytes 131104 | tf_op jit(solution)/shard_map/ppermute | solution.py:55
  63.6 0.0 collective-permute-start.13
  63.6 1.0 %collective-permute-done.9.refs_2_ = bf16[32,2048]{1,0:T(8,128)(2,1)S(1)} collective-permute-done((bf16[32,2048]{1,0:T(8,128)(2,1)S(1)}, bf16[32,2048]{1,0:T(8,128)(2,1)S(1)}, u32[]{:S(2)}, u32[]{:S(2)}) %collective-permute-start.9) | collective-permute-done | bytes 131104 | tf_op jit(solution)/shard_map/ppermute | solution.py:55
  64.7 0.1 collective-permute-start.10
  64.7 1.4 %collective-permute-done.18.refs_3_ = bf16[32,2048]{1,0:T(8,128)(2,1)S(1)} collective-permute-done((bf16[32,2048]{1,0:T(8,128)(2,1)S(1)}, bf16[32,2048]{1,0:T(8,128)(2,1)S(1)}, u32[]{:S(2)}, u32[]{:S(2)}) %collective-permute-start.18) | collective-permute-done | bytes 131104 | tf_op jit(solution)/shard_map/ppermute | solution.py:55
  66.1 0.0 collective-permute-start.19
  66.1 0.0 collective-permute-done.11.refs_4_
  66.1 2.3 %collective-permute-done.16.refs_6_ = bf16[32,2048]{1,0:T(8,128)(2,1)S(1)} collective-permute-done((bf16[32,2048]{1,0:T(8,128)(2,1)S(1)}, bf16[32,2048]{1,0:T(8,128)(2,1)S(1)}, u32[]{:S(2)}, u32[]{:S(2)}) %collective-permute-start.16) | collective-permute-done | bytes 131104 | tf_op jit(solution)/shard_map/ppermute | solution.py:55
  68.4 0.6 collective-permute-start.17
  69.0 2.0 %collective-permute-done.13.refs_5_ = bf16[32,2048]{1,0:T(8,128)(2,1)S(1)} collective-permute-done((bf16[32,2048]{1,0:T(8,128)(2,1)S(1)}, bf16[32,2048]{1,0:T(8,128)(2,1)S(1)}, u32[]{:S(2)}, u32[]{:S(2)}) %collective-permute-start.13) | collective-permute-done | bytes 131104 | tf_op jit(solution)/shard_map/ppermute | solution.py:55
  71.0 0.3 collective-permute-start.14
  71.3 0.0 collective-permute-done.10.refs_3_
  71.3 1.1 %collective-permute-done.19.refs_7_ = bf16[32,2048]{1,0:T(8,128)(2,1)S(1)} collective-permute-done((bf16[32,2048]{1,0:T(8,128)(2,1)S(1)}, bf16[32,2048]{1,0:T(8,128)(2,1)S(1)}, u32[]{:S(2)}, u32[]{:S(2)}) %collective-permute-start.19) | collective-permute-done | bytes 131104 | tf_op jit(solution)/shard_map/ppermute | solution.py:55
  72.4 0.6 collective-permute-start.20
  73.0 2.4 %combine.2.refs_8_ = f32[256,2048]{1,0:T(8,128)S(1)} custom-call(bf16[32,2048]{1,0:T(8,128)(2,1)S(1)} %get-tuple-element.60.refs_0_, bf16[32,2048]{1,0:T(8,128)(2,1)S(1)} %collective-permute-done.12.refs_1_, bf16[32,2048]{1,0:T(8,128)(2,1)S(1)} %collective-permute-done.15.refs_2_, bf16[32,2048]{1,0:T(8,128)(2,1)S(1)} %collective-permute-done.18.refs_3_, ...), custom_call_target="tpu_custom_call" | custom-call | tf_op jit(solution)/shard_map/combine/pallas_call | solution.py:393
  75.4 0.0 collective-permute-done.17.refs_6_
  75.4 0.5 collective-permute-done.14.refs_5_
  75.9 1.4 %collective-permute-done.20.refs_7_ = bf16[32,2048]{1,0:T(8,128)(2,1)S(1)} collective-permute-done((bf16[32,2048]{1,0:T(8,128)(2,1)S(1)}, bf16[32,2048]{1,0:T(8,128)(2,1)S(1)}, u32[]{:S(2)}, u32[]{:S(2)}) %collective-permute-start.20) | collective-permute-done | bytes 131104 | tf_op jit(solution)/shard_map/ppermute | solution.py:55
  77.3 2.5 %combine.3 = (bf16[128,2048]{1,0:T(8,128)(2,1)S(1)}, f32[128,2048]{1,0:T(8,128)S(1)}) custom-call(bf16[32,2048]{1,0:T(8,128)(2,1)S(1)} %attend.3.refs_0_, bf16[32,2048]{1,0:T(8,128)(2,1)S(1)} %collective-permute-done.8.refs_1_, bf16[32,2048]{1,0:T(8,128)(2,1)S(1)} %collective-permute-done.9.refs_2_, bf16[32,2048]{1,0:T(8,128)(2,1)S(1)} %collective-permute-done.10.refs_3_, ...), custom_call_target="tpu_custom_call" | custom-call | tf_op jit(solution)/shard_map/combine/pallas_call | solution.py:393
  79.8 0.1 collective-permute-start.21
  79.9 1.9 %collective-permute-done.21 = bf16[128,2048]{1,0:T(8,128)(2,1)S(1)} collective-permute-done((bf16[128,2048]{1,0:T(8,128)(2,1)S(1)}, bf16[128,2048]{1,0:T(8,128)(2,1)S(1)}, u32[]{:S(2)}, u32[]{:S(2)}) %collective-permute-start.21) | collective-permute-done | bytes 524320 | tf_op jit(solution)/shard_map/ppermute | solution.py:531
  81.8 0.9 %add_convert_fusion = bf16[128,2048]{1,0:T(8,128)(2,1)} fusion(f32[128,2048]{1,0:T(8,128)S(1)} %get-tuple-element.67, bf16[128,2048]{1,0:T(8,128)(2,1)S(1)} %collective-permute-done.21), kind=kLoop, calls=%fused_computation.3 | loop fusion | flops 786432 | bytes 2097152 | tf_op jit(solution)/shard_map/convert_element_type | solution.py:532
  (9 shorter events, 0.2 us)
Async XLA Ops:
  4.4 7.7 %collective-permute-start = (bf16[128,1152]{1,0:T(8,128)(2,1)S(1)}, bf16[128,1152]{1,0:T(8,128)(2,1)S(1)}, u32[]{:S(2)}, u32[]{:S(2)}) collective-permute-start(bf16[128,1152]{1,0:T(8,128)(2,1)S(1)} %get-tuple-element.38), channel_id=1, source_target_pairs={{0,2},{1,5},{2,0},{3,7},{4,6},{5,1},{6,4},{7,3},{8,10},{9,13},{10,... | collective-permute-start | bytes 884744 | tf_op jit(solution)/shard_map/ppermute | solution.py:55
  11.3 7.1 %collective-permute-start.1 = (bf16[128,1280]{1,0:T(8,128)(2,1)S(1)}, bf16[128,1280]{1,0:T(8,128)(2,1)S(1)}, u32[]{:S(2)}, u32[]{:S(2)}) collective-permute-start(bf16[128,1280]{1,0:T(8,128)(2,1)S(1)} %get-tuple-element.40), channel_id=1, source_target_pairs={{0,2},{1,5},{2,0},{3,7},{4,6},{5,1},{6,4},{7,3},{8,10},{9,13},{10,... | collective-permute-start | bytes 983048 | tf_op jit(solution)/shard_map/ppermute | solution.py:55
  12.2 8.0 %copy-start = (s32[8]{0:T(128)S(1)}, s32[8]{0:T(128)}, u32[]{:S(2)}) copy-start(s32[8]{0:T(128)} %length_ref.3) | copy-start | bytes 100
  18.5 12.0 %collective-permute-start.3 = (bf16[64,2432]{1,0:T(8,128)(2,1)S(1)}, bf16[64,2432]{1,0:T(8,128)(2,1)}, u32[]{:S(2)}, u32[]{:S(2)}) collective-permute-start(bf16[64,2432]{1,0:T(8,128)(2,1)S(1)} %fusion.1), channel_id=1, source_target_pairs={{0,4},{1,3},{2,6},{3,1},{4,0},{5,7},{6,2},{7,5},{8,12},{9,11},{10,... | collective-permute-start | bytes 933896 | tf_op jit(solution)/shard_map/ppermute | solution.py:55
  20.3 12.3 %collective-permute-start.2 = (bf16[128,2304]{1,0:T(8,128)(2,1)S(1)}, bf16[128,2304]{1,0:T(8,128)(2,1)S(1)}, u32[]{:S(2)}, u32[]{:S(2)}) collective-permute-start(bf16[128,2304]{1,0:T(8,128)(2,1)S(1)} %get-tuple-element.48), channel_id=1, source_target_pairs={{0,2},{1,5},{2,0},{3,7},{4,6},{5,1},{6,4},{7,3},{8,10},{9,13},{10,... | collective-permute-start | bytes 1769480 | tf_op jit(solution)/shard_map/ppermute | solution.py:55
  31.6 8.0 %collective-permute-start.5 = (bf16[32,2432]{1,0:T(8,128)(2,1)S(1)}, bf16[32,2432]{1,0:T(8,128)(2,1)S(1)}, u32[]{:S(2)}, u32[]{:S(2)}) collective-permute-start(bf16[32,2432]{1,0:T(8,128)(2,1)S(1)} %slice.64), channel_id=1, source_target_pairs={{0,8},{1,9},{2,10},{3,11},{4,12},{5,13},{6,14},{7,15},{8,0},{9,1},... | collective-permute-start | bytes 466952 | tf_op jit(solution)/shard_map/ppermute | solution.py:55
  32.7 8.9 %collective-permute-start.4 = (bf16[64,2304]{1,0:T(8,128)(2,1)S(1)}, bf16[64,2304]{1,0:T(8,128)(2,1)S(1)}, u32[]{:S(2)}, u32[]{:S(2)}) collective-permute-start(bf16[64,2304]{1,0:T(8,128)(2,1)S(1)} %slice.63), channel_id=1, source_target_pairs={{0,4},{1,3},{2,6},{3,1},{4,0},{5,7},{6,2},{7,5},{8,12},{9,11},{10,... | collective-permute-start | bytes 884744 | tf_op jit(solution)/shard_map/ppermute | solution.py:55
  41.7 8.1 %collective-permute-start.6 = (bf16[32,2304]{1,0:T(8,128)(2,1)S(1)}, bf16[32,2304]{1,0:T(8,128)(2,1)S(1)}, u32[]{:S(2)}, u32[]{:S(2)}) collective-permute-start(bf16[32,2304]{1,0:T(8,128)(2,1)S(1)} %slice.65), channel_id=1, source_target_pairs={{0,8},{1,9},{2,10},{3,11},{4,12},{5,13},{6,14},{7,15},{8,0},{9,1},... | collective-permute-start | bytes 442376 | tf_op jit(solution)/shard_map/ppermute | solution.py:55
  46.7 6.9 %collective-permute-start.7 = (bf16[32,2048]{1,0:T(8,128)(2,1)S(1)}, bf16[32,2048]{1,0:T(8,128)(2,1)S(1)}, u32[]{:S(2)}, u32[]{:S(2)}) collective-permute-start(bf16[32,2048]{1,0:T(8,128)(2,1)S(1)} %get-tuple-element.60.refs_0_), channel_id=1, source_target_pairs={{0,2},{1,3},{2,0},{3,1},{4,6},{5,7},{6,4},{7,5},{8,10},{9,11},{10,... | collective-permute-start | bytes 393224 | tf_op jit(solution)/shard_map/ppermute | solution.py:55
  49.9 9.2 %collective-permute-start.12 = (bf16[32,2048]{1,0:T(8,128)(2,1)S(1)}, bf16[32,2048]{1,0:T(8,128)(2,1)S(1)}, u32[]{:S(2)}, u32[]{:S(2)}) collective-permute-start(bf16[32,2048]{1,0:T(8,128)(2,1)S(1)} %get-tuple-element.60.refs_0_), channel_id=1, source_target_pairs={{0,8},{1,9},{2,10},{3,11},{4,12},{5,13},{6,14},{7,15},{8,0},{9,1},... | collective-permute-start | bytes 393224 | tf_op jit(solution)/shard_map/ppermute | solution.py:55
  50.1 9.1 %collective-permute-start.15 = (bf16[32,2048]{1,0:T(8,128)(2,1)S(1)}, bf16[32,2048]{1,0:T(8,128)(2,1)S(1)}, u32[]{:S(2)}, u32[]{:S(2)}) collective-permute-start(bf16[32,2048]{1,0:T(8,128)(2,1)S(1)} %get-tuple-element.60.refs_0_), channel_id=1, source_target_pairs={{0,4},{1,5},{2,6},{3,7},{4,0},{5,1},{6,2},{7,3},{8,12},{9,13},{10,... | collective-permute-start | bytes 393224 | tf_op jit(solution)/shard_map/ppermute | solution.py:55
  56.3 7.3 %collective-permute-start.8 = (bf16[32,2048]{1,0:T(8,128)(2,1)S(1)}, bf16[32,2048]{1,0:T(8,128)(2,1)S(1)}, u32[]{:S(2)}, u32[]{:S(2)}) collective-permute-start(bf16[32,2048]{1,0:T(8,128)(2,1)S(1)} %attend.3.refs_0_), channel_id=1, source_target_pairs={{0,8},{1,9},{2,10},{3,11},{4,12},{5,13},{6,14},{7,15},{8,0},{9,1},... | collective-permute-start | bytes 393224 | tf_op jit(solution)/shard_map/ppermute | solution.py:55
  56.8 7.8 %collective-permute-start.9 = (bf16[32,2048]{1,0:T(8,128)(2,1)S(1)}, bf16[32,2048]{1,0:T(8,128)(2,1)S(1)}, u32[]{:S(2)}, u32[]{:S(2)}) collective-permute-start(bf16[32,2048]{1,0:T(8,128)(2,1)S(1)} %attend.3.refs_0_), channel_id=1, source_target_pairs={{0,4},{1,3},{2,6},{3,1},{4,0},{5,7},{6,2},{7,5},{8,12},{9,11},{10,... | collective-permute-start | bytes 393224 | tf_op jit(solution)/shard_map/ppermute | solution.py:55
  59.1 7.0 %collective-permute-start.18 = (bf16[32,2048]{1,0:T(8,128)(2,1)S(1)}, bf16[32,2048]{1,0:T(8,128)(2,1)S(1)}, u32[]{:S(2)}, u32[]{:S(2)}) collective-permute-start(bf16[32,2048]{1,0:T(8,128)(2,1)S(1)} %collective-permute-done.12.refs_1_), channel_id=1, source_target_pairs={{0,4},{1,5},{2,6},{3,7},{4,0},{5,1},{6,2},{7,3},{8,12},{9,13},{10,... | collective-permute-start | bytes 393224 | tf_op jit(solution)/shard_map/ppermute | solution.py:55
  59.2 6.9 %collective-permute-start.11 = (bf16[32,2048]{1,0:T(8,128)(2,1)S(1)}, bf16[32,2048]{1,0:T(8,128)(2,1)S(1)}, u32[]{:S(2)}, u32[]{:S(2)}) collective-permute-start(bf16[32,2048]{1,0:T(8,128)(2,1)S(1)} %attend.3.refs_0_), channel_id=1, source_target_pairs={{0,2},{1,5},{2,0},{3,7},{4,6},{5,1},{6,4},{7,3},{8,10},{9,13},{10,... | collective-permute-start | bytes 393224 | tf_op jit(solution)/shard_map/ppermute | solution.py:55
  59.9 8.5 %collective-permute-start.16 = (bf16[32,2048]{1,0:T(8,128)(2,1)S(1)}, bf16[32,2048]{1,0:T(8,128)(2,1)S(1)}, u32[]{:S(2)}, u32[]{:S(2)}) collective-permute-start(bf16[32,2048]{1,0:T(8,128)(2,1)S(1)} %collective-permute-done.15.refs_2_), channel_id=1, source_target_pairs={{0,2},{1,3},{2,0},{3,1},{4,6},{5,7},{6,4},{7,5},{8,10},{9,11},{10,... | collective-permute-start | bytes 393224 | tf_op jit(solution)/shard_map/ppermute | solution.py:55
  63.6 7.4 %collective-permute-start.13 = (bf16[32,2048]{1,0:T(8,128)(2,1)S(1)}, bf16[32,2048]{1,0:T(8,128)(2,1)S(1)}, u32[]{:S(2)}, u32[]{:S(2)}) collective-permute-start(bf16[32,2048]{1,0:T(8,128)(2,1)S(1)} %collective-permute-done.12.refs_1_), channel_id=1, source_target_pairs={{0,2},{1,3},{2,0},{3,1},{4,6},{5,7},{6,4},{7,5},{8,10},{9,11},{10,... | collective-permute-start | bytes 393224 | tf_op jit(solution)/shard_map/ppermute | solution.py:55
  64.7 6.6 %collective-permute-start.10 = (bf16[32,2048]{1,0:T(8,128)(2,1)S(1)}, bf16[32,2048]{1,0:T(8,128)(2,1)S(1)}, u32[]{:S(2)}, u32[]{:S(2)}) collective-permute-start(bf16[32,2048]{1,0:T(8,128)(2,1)S(1)} %collective-permute-done.8.refs_1_), channel_id=1, source_target_pairs={{0,4},{1,3},{2,6},{3,1},{4,0},{5,7},{6,2},{7,5},{8,12},{9,11},{10,... | collective-permute-start | bytes 393224 | tf_op jit(solution)/shard_map/ppermute | solution.py:55
  66.1 6.3 %collective-permute-start.19 = (bf16[32,2048]{1,0:T(8,128)(2,1)S(1)}, bf16[32,2048]{1,0:T(8,128)(2,1)S(1)}, u32[]{:S(2)}, u32[]{:S(2)}) collective-permute-start(bf16[32,2048]{1,0:T(8,128)(2,1)S(1)} %collective-permute-done.18.refs_3_), channel_id=1, source_target_pairs={{0,2},{1,3},{2,0},{3,1},{4,6},{5,7},{6,4},{7,5},{8,10},{9,11},{10,... | collective-permute-start | bytes 393224 | tf_op jit(solution)/shard_map/ppermute | solution.py:55
  68.4 7.1 %collective-permute-start.17 = (bf16[32,2048]{1,0:T(8,128)(2,1)S(1)}, bf16[32,2048]{1,0:T(8,128)(2,1)S(1)}, u32[]{:S(2)}, u32[]{:S(2)}) collective-permute-start(bf16[32,2048]{1,0:T(8,128)(2,1)S(1)} %collective-permute-done.9.refs_2_), channel_id=1, source_target_pairs={{0,2},{1,5},{2,0},{3,7},{4,6},{5,1},{6,4},{7,3},{8,10},{9,13},{10,... | collective-permute-start | bytes 393224 | tf_op jit(solution)/shard_map/ppermute | solution.py:55
  71.0 5.0 %collective-permute-start.14 = (bf16[32,2048]{1,0:T(8,128)(2,1)S(1)}, bf16[32,2048]{1,0:T(8,128)(2,1)S(1)}, u32[]{:S(2)}, u32[]{:S(2)}) collective-permute-start(bf16[32,2048]{1,0:T(8,128)(2,1)S(1)} %collective-permute-done.8.refs_1_), channel_id=1, source_target_pairs={{0,2},{1,5},{2,0},{3,7},{4,6},{5,1},{6,4},{7,3},{8,10},{9,13},{10,... | collective-permute-start | bytes 393224 | tf_op jit(solution)/shard_map/ppermute | solution.py:55
  72.4 5.0 %collective-permute-start.20 = (bf16[32,2048]{1,0:T(8,128)(2,1)S(1)}, bf16[32,2048]{1,0:T(8,128)(2,1)S(1)}, u32[]{:S(2)}, u32[]{:S(2)}) collective-permute-start(bf16[32,2048]{1,0:T(8,128)(2,1)S(1)} %collective-permute-done.10.refs_3_), channel_id=1, source_target_pairs={{0,2},{1,5},{2,0},{3,7},{4,6},{5,1},{6,4},{7,3},{8,10},{9,13},{10,... | collective-permute-start | bytes 393224 | tf_op jit(solution)/shard_map/ppermute | solution.py:55
  79.8 2.0 %collective-permute-start.21 = (bf16[128,2048]{1,0:T(8,128)(2,1)S(1)}, bf16[128,2048]{1,0:T(8,128)(2,1)S(1)}, u32[]{:S(2)}, u32[]{:S(2)}) collective-permute-start(bf16[128,2048]{1,0:T(8,128)(2,1)S(1)} %get-tuple-element.68), channel_id=1, source_target_pairs={{0,1},{1,0},{2,3},{3,2},{4,5},{5,4},{6,7},{7,6},{8,9},{9,8},{10,11... | collective-permute-start | bytes 1572872 | tf_op jit(solution)/shard_map/ppermute | solution.py:531

commit v14 on v13

--- a/solution.py
+++ b/solution.py
@@ -68,17 +68,18 @@
     kv = wk_ref.shape[1] // CHUNKS if with_kv else 0
     width = w_buf.shape[1]
     cols = width - 2 * kv
-    tile = cols // 2
+    pieces = 4 if cols > 1024 else 2
+    tile = cols // pieces
 
     def w_copy(ref, start, size, at, sem):
         return pltpu.make_async_copy(
             ref.at[:, start : start + size], w_buf.at[:, at : at + size], sems.at[sem]
         )
 
-    copies = [[w_copy(wq_ref, q_start + at, tile, at, at // tile)] for at in (0, tile)]
+    copies = [[w_copy(wq_ref, q_start + p * tile, tile, p * tile, p)] for p in range(pieces)]
     if with_kv:
-        copies[1].append(w_copy(wk_ref, kv_start, kv, cols, 2))
-        copies[1].append(w_copy(wv_ref, kv_start, kv, cols + kv, 3))
+        copies[-1].append(w_copy(wk_ref, kv_start, kv, cols, pieces))
+        copies[-1].append(w_copy(wv_ref, kv_start, kv, cols + kv, pieces + 1))
 
     if first:
         block = rows // n
@@ -120,7 +121,8 @@
                 at = (slot - n // 2) * block
                 send_ref[at : at + block, width : width + 128] = packed.astype(jnp.bfloat16)
 
-    for p, (start, end) in enumerate(((0, tile), (tile, width))):
+    for p in range(pieces):
+        start, end = p * tile, (p + 1) * tile if p < pieces - 1 else width
         for copy in copies[p]:
             copy.wait()
         product = jnp.dot(x_ref[...], w_buf[:, start:end], preferred_element_type=jnp.float32)
@@ -143,7 +145,7 @@
         pltpu.VMEM((rows // 2, full), jnp.bfloat16),
         pltpu.VMEM((rows // 2, full), jnp.float32),
     ]
-    scratch = [pltpu.VMEM((depth, width), jnp.bfloat16), pltpu.SemaphoreType.DMA((4,))]
+    scratch = [pltpu.VMEM((depth, width), jnp.bfloat16), pltpu.SemaphoreType.DMA((6,))]
     if first:
         out_shape.append(pltpu.VMEM((rows, depth), jnp.bfloat16))
         args = [in_hbm(x), in_hbm(gain)]
@@ -480,16 +482,13 @@
     offsets = [[at if at < share else at + 128 for at in plain], plain]
     kv_offsets = [q_cols + 128, q_cols]
 
-    attentions, early = [], {}
+    attentions = []
     for chunk in range(CHUNKS):
-        total = sums[chunk]
-        if chunk == 1:
-            total = after(total, *early.values())
         out = attend(
             chunk,
             offsets[chunk],
             kv_offsets[chunk],
-            total,
+            sums[chunk],
             squares,
             cosine,
             sine,
@@ -500,11 +499,6 @@
         )
         attentions.append(out[0])
         weights += out[1:]
-        if chunk == 0:
-            for stage in [0]:
-                early[1 << (levels - 1 - stage)] = exchange(
-                    out[0], n, cores, stage, gather_orders(n, 0)
-                )
     gathered = []
     for chunk in range(CHUNKS):
         slots = [attentions[chunk]]
@@ -515,11 +509,6 @@
                 source = after(source, sums[1])
             if slot == 3 << (levels - 2):
                 source = after(source, slots[1 << (levels - 1)])
-            if chunk == 1 and slot > n // 2:
-                source = after(source, gathered[0][slot])
-            if chunk == 0 and slot in early:
-                slots.append(early[slot])
-                continue
             slots.append(
                 exchange(source, n, cores, levels - 1 - top, gather_orders(n, chunk))
             )

time: 82.8 us -> 79.3 us (0.958)
  waiting for transfers between devices: 26.3 us -> 16.9 us
  starting transfers between devices: 21.1 us -> 27.1 us
    ppermute x21, waiting for transfers between devices: 24.4 us -> 15 us  [exchange(): return lax.ppermute(value, ('gx', 'gy'), pairs)]
    ppermute x21, starting transfers between devices: 21 us -> 27.1 us  [exchange(): return lax.ppermute(value, ('gx', 'gy'), pairs)]
  transfers between devices with their start and end apart: 22 -> 22, of which waited for: 15 -> 12; matrix products, arithmetic and copies ran while one was open for 2% -> 2% of each run, Pallas kernels for 31% -> 32%
where the time goes in v14:
time: 79.3 us; the launch traced here: 79.2 us
  Pallas kernels  32.2 us (41%)
  starting transfers between devices  27.1 us (34%)
  waiting for transfers between devices  16.9 us (21%)
  other arithmetic  2.58 us (3%)
    ppermute x21, starting transfers between devices, exchange(): return lax.ppermute(value, ('gx', 'gy'), pairs)  27.1 us
    ppermute x21, waiting for transfers between devices, exchange(): return lax.ppermute(value, ('gx', 'gy'), pairs)  15 us
    pallas_call x3, Pallas kernels, project(): pl.pallas_call(functools.partial(project_kernel, n, q_start, kv_start, fi...  13.6 us
    pallas_call x2, Pallas kernels, attend(): pl.pallas_call(functools.partial(attend_kernel, chunk, offsets, kv_offset...  6.77 us
    pallas_call x2, Pallas kernels, combine(): pl.pallas_call(functools.partial(combine_kernel, n, block, chunk), out_sh...  4.89 us
    pallas_call x1, Pallas kernels, fetch_rows(): pl.pallas_call(functools.partial(fetch_rows_kernel, start, pieces), out_s...  3.5 us
    pallas_call x1, Pallas kernels, fetch(): pl.pallas_call(functools.partial(fetch_kernel, len(arrays), pieces), out_...  3.47 us
    ppermute x1, waiting for transfers between devices, shards(): other = lax.ppermute(send, 'gy', [(0, 1), (1, 0)])  1.9 us
  transfers between devices with their start and end apart: 22, of which 12 were waited for; matrix products, arithmetic and copies ran while one was open for 2% of the time, Pallas kernels for 32%

profile of v14, /device:TPU:0, one launch (start us, length us, event | category | flops | bytes accessed | tf_op | source)
XLA Modules:
  0.0 79.2 jit_solution(2325851065059156543)
XLA Ops:
  0.0 4.4 %project.3 = (bf16[128,1152]{1,0:T(8,128)(2,1)S(1)}, f32[128,1152]{1,0:T(8,128)S(1)}, bf16[256,2048]{1,0:T(8,128)(2,1)S(1)}) custom-call(bf16[256,2048]{1,0:T(8,128)(2,1)} %refs_0_.1, f32[1,2048]{1,0:T(1,128)} %bitcast.1, bf16[2048,4096]{1,0:T(8,128)(2,1)} %refs_1_.3, bf16[2048,256]{1,0:T(8,128)(2,1)} %refs_2_.5, bf16[2048,256]{1,0:T(8,128)(2,1)} %refs_3_.5), custom_call_target="tpu_custom_call" | custom-call | tf_op jit(solution)/shard_map/project/pallas_call | solution.py:161
  4.4 3.0 %collective-permute-start = (bf16[128,1152]{1,0:T(8,128)(2,1)S(1)}, bf16[128,1152]{1,0:T(8,128)(2,1)S(1)}, u32[]{:S(2)}, u32[]{:S(2)}) collective-permute-start(bf16[128,1152]{1,0:T(8,128)(2,1)S(1)} %get-tuple-element.34), channel_id=1, source_target_pairs={{0,2},{1,5},{2,0},{3,7},{4,6},{5,1},{6,4},{7,3},{8,10},{9,13},{10,... | collective-permute-start | bytes 884744 | tf_op jit(solution)/shard_map/ppermute | solution.py:55
  7.4 3.9 %project.4 = (bf16[128,1280]{1,0:T(8,128)(2,1)S(1)}, f32[128,1280]{1,0:T(8,128)S(1)}) custom-call(bf16[256,2048]{1,0:T(8,128)(2,1)S(1)} %get-tuple-element.39.refs_0_, bf16[2048,4096]{1,0:T(8,128)(2,1)} %refs_1_.3, bf16[2048,256]{1,0:T(8,128)(2,1)} %refs_2_.5, bf16[2048,256]{1,0:T(8,128)(2,1)} %refs_3_.5), custom_call_target="tpu_custom_call" | custom-call | tf_op jit(solution)/shard_map/project/pallas_call | solution.py:161
  11.3 0.1 collective-permute-start.1
  11.4 0.7 collective-permute-done
  12.1 0.1 convert_add_fusion.2
  12.2 0.0 copy-start
  12.2 5.3 %project.5 = (bf16[128,2304]{1,0:T(8,128)(2,1)S(1)}, f32[128,2304]{1,0:T(8,128)S(1)}) custom-call(bf16[256,2048]{1,0:T(8,128)(2,1)S(1)} %get-tuple-element.39.refs_0_, bf16[2048,4096]{1,0:T(8,128)(2,1)} %refs_1_.3, bf16[2048,256]{1,0:T(8,128)(2,1)} %refs_2_.5, bf16[2048,256]{1,0:T(8,128)(2,1)} %refs_3_.5), custom_call_target="tpu_custom_call" | custom-call | tf_op jit(solution)/shard_map/project/pallas_call | solution.py:161
  17.5 0.9 %collective-permute-done.1 = bf16[128,1280]{1,0:T(8,128)(2,1)S(1)} collective-permute-done((bf16[128,1280]{1,0:T(8,128)(2,1)S(1)}, bf16[128,1280]{1,0:T(8,128)(2,1)S(1)}, u32[]{:S(2)}, u32[]{:S(2)}) %collective-permute-start.1) | collective-permute-done | bytes 327712 | tf_op jit(solution)/shard_map/ppermute | solution.py:55
  18.4 0.1 convert_add_fusion.1
  18.5 1.6 %collective-permute-start.3 = (bf16[64,2432]{1,0:T(8,128)(2,1)S(1)}, bf16[64,2432]{1,0:T(8,128)(2,1)}, u32[]{:S(2)}, u32[]{:S(2)}) collective-permute-start(bf16[64,2432]{1,0:T(8,128)(2,1)S(1)} %fusion.1), channel_id=1, source_target_pairs={{0,4},{1,3},{2,6},{3,1},{4,0},{5,7},{6,2},{7,5},{8,12},{9,11},{10,... | collective-permute-start | bytes 933896 | tf_op jit(solution)/shard_map/ppermute | solution.py:55
  20.2 0.1 add_convert_fusion.1
  20.3 0.1 convert_element_type.49
  20.4 1.2 %collective-permute-start.2 = (bf16[128,2304]{1,0:T(8,128)(2,1)S(1)}, bf16[128,2304]{1,0:T(8,128)(2,1)S(1)}, u32[]{:S(2)}, u32[]{:S(2)}) collective-permute-start(bf16[128,2304]{1,0:T(8,128)(2,1)S(1)} %get-tuple-element.44), channel_id=1, source_target_pairs={{0,2},{1,5},{2,0},{3,7},{4,6},{5,1},{6,4},{7,3},{8,10},{9,13},{10,... | collective-permute-start | bytes 1769480 | tf_op jit(solution)/shard_map/ppermute | solution.py:55
  21.5 3.5 %fetch_rows.1.refs_8_ = bf16[2048,2048]{1,0:T(8,128)(2,1)S(1)} custom-call(bf16[4096,2048]{1,0:T(8,128)(2,1)} %refs_6_.1), custom_call_target="tpu_custom_call" | custom-call | tf_op jit(solution)/shard_map/fetch_rows/pallas_call | solution.py:343
  25.0 5.6 %collective-permute-done.3 = bf16[64,2432]{1,0:T(8,128)(2,1)} collective-permute-done((bf16[64,2432]{1,0:T(8,128)(2,1)S(1)}, bf16[64,2432]{1,0:T(8,128)(2,1)}, u32[]{:S(2)}, u32[]{:S(2)}) %collective-permute-start.3) | collective-permute-done | bytes 311328 | tf_op jit(solution)/shard_map/ppermute | solution.py:55
  30.6 1.0 %fusion.2 = f32[64,2432]{1,0:T(8,128)S(1)} fusion(f32[128,1280]{1,0:T(8,128)S(1)} %convert_add_fusion.1, f32[128,1152]{1,0:T(8,128)S(1)} %convert_add_fusion.2, bf16[64,2432]{1,0:T(8,128)(2,1)} %collective-permute-done.3), kind=kLoop, calls=%fused_computation.8 | loop fusion | flops 466944 | bytes 2179072 | tf_op jit(solution)/shard_map/add | solution.py:461
  31.7 1.5 %collective-permute-start.5 = (bf16[32,2432]{1,0:T(8,128)(2,1)S(1)}, bf16[32,2432]{1,0:T(8,128)(2,1)S(1)}, u32[]{:S(2)}, u32[]{:S(2)}) collective-permute-start(bf16[32,2432]{1,0:T(8,128)(2,1)S(1)} %slice.64), channel_id=1, source_target_pairs={{0,8},{1,9},{2,10},{3,11},{4,12},{5,13},{6,14},{7,15},{8,0},{9,1},... | collective-permute-start | bytes 466952 | tf_op jit(solution)/shard_map/ppermute | solution.py:55
  33.2 0.0 collective-permute-done.2
  33.2 0.1 convert_add_fusion
  33.3 2.8 %collective-permute-start.4 = (bf16[64,2304]{1,0:T(8,128)(2,1)S(1)}, bf16[64,2304]{1,0:T(8,128)(2,1)S(1)}, u32[]{:S(2)}, u32[]{:S(2)}) collective-permute-start(bf16[64,2304]{1,0:T(8,128)(2,1)S(1)} %slice.63), channel_id=1, source_target_pairs={{0,4},{1,3},{2,6},{3,1},{4,0},{5,7},{6,2},{7,5},{8,12},{9,11},{10,... | collective-permute-start | bytes 884744 | tf_op jit(solution)/shard_map/ppermute | solution.py:55
  36.1 3.5 %fetch.1 = (bf16[8,1024,256]{2,1,0:T(8,128)(2,1)S(1)}, bf16[8,1024,256]{2,1,0:T(8,128)(2,1)S(1)}) custom-call(bf16[8,1024,256]{2,1,0:T(8,128)(2,1)} %refs_0_.2, bf16[8,1024,256]{2,1,0:T(8,128)(2,1)} %refs_1_.4), custom_call_target="tpu_custom_call" | custom-call | tf_op jit(solution)/shard_map/fetch/pallas_call | solution.py:314
  39.6 0.0 collective-permute-done.5
  39.7 2.0 %collective-permute-done.4 = bf16[64,2304]{1,0:T(8,128)(2,1)S(1)} collective-permute-done((bf16[64,2304]{1,0:T(8,128)(2,1)S(1)}, bf16[64,2304]{1,0:T(8,128)(2,1)S(1)}, u32[]{:S(2)}, u32[]{:S(2)}) %collective-permute-start.4) | collective-permute-done | bytes 294944 | tf_op jit(solution)/shard_map/ppermute | solution.py:55
  41.7 0.1 slice_add_fusion
  41.8 0.7 collective-permute-start.6
  42.5 0.1 fusion.3
  42.6 0.1 pad_maximum_fusion.1
  42.7 4.0 %attend.3 = (bf16[32,2048]{1,0:T(8,128)(2,1)S(1)}, bf16[2048,2048]{1,0:T(8,128)(2,1)S(1)}) custom-call(s32[8]{0:T(128)S(1)} %copy-done, f32[32,2432]{1,0:T(8,128)S(1)} %slice_add_fusion.1.refs_0_, f32[32,128]{1,0:T(8,128)S(1)} %slice.48.refs_1_, f32[32,128]{1,0:T(8,128)S(1)} %get-tuple-element.64.refs_2_, f32[32,128]{1,0:T(8,128)S(1)} %get-tuple-element.65.refs_3_, ...), custom_call_target="tpu_custom_call" | custom-call | tf_op jit(solution)/shard_map/attend/pallas_call | solution.py:281
  46.7 0.5 collective-permute-start.17
  47.2 1.9 %collective-permute-start.15 = (bf16[32,2048]{1,0:T(8,128)(2,1)S(1)}, bf16[32,2048]{1,0:T(8,128)(2,1)S(1)}, u32[]{:S(2)}, u32[]{:S(2)}) collective-permute-start(bf16[32,2048]{1,0:T(8,128)(2,1)S(1)} %get-tuple-element.56.refs_0_), channel_id=1, source_target_pairs={{0,4},{1,5},{2,6},{3,7},{4,0},{5,1},{6,2},{7,3},{8,12},{9,13},{10,... | collective-permute-start | bytes 393224 | tf_op jit(solution)/shard_map/ppermute | solution.py:55
  49.1 0.5 collective-permute-done.6
  49.6 0.8 %collective-permute-start.14 = (bf16[32,2048]{1,0:T(8,128)(2,1)S(1)}, bf16[32,2048]{1,0:T(8,128)(2,1)S(1)}, u32[]{:S(2)}, u32[]{:S(2)}) collective-permute-start(bf16[32,2048]{1,0:T(8,128)(2,1)S(1)} %get-tuple-element.56.refs_0_), channel_id=1, source_target_pairs={{0,8},{1,9},{2,10},{3,11},{4,12},{5,13},{6,14},{7,15},{8,0},{9,1},... | collective-permute-start | bytes 393224 | tf_op jit(solution)/shard_map/ppermute | solution.py:55
  50.4 2.7 %attend.2.refs_0_ = bf16[32,2048]{1,0:T(8,128)(2,1)S(1)} custom-call(s32[8]{0:T(128)S(1)} %copy-done, f32[32,2304]{1,0:T(8,128)S(1)} %slice_add_fusion.2.refs_0_, f32[32,128]{1,0:T(8,128)S(1)} %slice.48.refs_1_, f32[32,128]{1,0:T(8,128)S(1)} %get-tuple-element.64.refs_2_, f32[32,128]{1,0:T(8,128)S(1)} %get-tuple-element.65.refs_3_, ...), custom_call_target="tpu_custom_call" | custom-call | tf_op jit(solution)/shard_map/attend/pallas_call | solution.py:281
  53.2 2.2 %collective-permute-start.7 = (bf16[32,2048]{1,0:T(8,128)(2,1)S(1)}, bf16[32,2048]{1,0:T(8,128)(2,1)S(1)}, u32[]{:S(2)}, u32[]{:S(2)}) collective-permute-start(bf16[32,2048]{1,0:T(8,128)(2,1)S(1)} %attend.2.refs_0_), channel_id=1, source_target_pairs={{0,8},{1,9},{2,10},{3,11},{4,12},{5,13},{6,14},{7,15},{8,0},{9,1},... | collective-permute-start | bytes 393224 | tf_op jit(solution)/shard_map/ppermute | solution.py:55
  55.4 1.5 %collective-permute-start.10 = (bf16[32,2048]{1,0:T(8,128)(2,1)S(1)}, bf16[32,2048]{1,0:T(8,128)(2,1)S(1)}, u32[]{:S(2)}, u32[]{:S(2)}) collective-permute-start(bf16[32,2048]{1,0:T(8,128)(2,1)S(1)} %attend.2.refs_0_), channel_id=1, source_target_pairs={{0,2},{1,5},{2,0},{3,7},{4,6},{5,1},{6,4},{7,3},{8,10},{9,13},{10,... | collective-permute-start | bytes 393224 | tf_op jit(solution)/shard_map/ppermute | solution.py:55
  56.9 0.0 collective-permute-done.17.refs_4_
  56.9 0.0 collective-permute-start.8
  56.9 0.0 collective-permute-done.15.refs_2_
  56.9 1.9 %collective-permute-done.14.refs_1_ = bf16[32,2048]{1,0:T(8,128)(2,1)S(1)} collective-permute-done((bf16[32,2048]{1,0:T(8,128)(2,1)S(1)}, bf16[32,2048]{1,0:T(8,128)(2,1)S(1)}, u32[]{:S(2)}, u32[]{:S(2)}) %collective-permute-start.14) | collective-permute-done | bytes 131104 | tf_op jit(solution)/shard_map/ppermute | solution.py:55
  58.7 0.2 collective-permute-start.16
  58.9 1.8 %collective-permute-start.19 = (bf16[32,2048]{1,0:T(8,128)(2,1)S(1)}, bf16[32,2048]{1,0:T(8,128)(2,1)S(1)}, u32[]{:S(2)}, u32[]{:S(2)}) collective-permute-start(bf16[32,2048]{1,0:T(8,128)(2,1)S(1)} %collective-permute-done.15.refs_2_), channel_id=1, source_target_pairs={{0,2},{1,3},{2,0},{3,1},{4,6},{5,7},{6,4},{7,5},{8,10},{9,11},{10,... | collective-permute-start | bytes 393224 | tf_op jit(solution)/shard_map/ppermute | solution.py:55
  60.7 0.7 collective-permute-done.7.refs_1_
  61.4 1.3 %collective-permute-start.9 = (bf16[32,2048]{1,0:T(8,128)(2,1)S(1)}, bf16[32,2048]{1,0:T(8,128)(2,1)S(1)}, u32[]{:S(2)}, u32[]{:S(2)}) collective-permute-start(bf16[32,2048]{1,0:T(8,128)(2,1)S(1)} %collective-permute-done.7.refs_1_), channel_id=1, source_target_pairs={{0,4},{1,3},{2,6},{3,1},{4,0},{5,7},{6,2},{7,5},{8,12},{9,11},{10,... | collective-permute-start | bytes 393224 | tf_op jit(solution)/shard_map/ppermute | solution.py:55
  62.7 0.0 collective-permute-done.10.refs_4_
  62.7 0.0 collective-permute-done.8.refs_2_
  62.7 1.9 %collective-permute-start.12 = (bf16[32,2048]{1,0:T(8,128)(2,1)S(1)}, bf16[32,2048]{1,0:T(8,128)(2,1)S(1)}, u32[]{:S(2)}, u32[]{:S(2)}) collective-permute-start(bf16[32,2048]{1,0:T(8,128)(2,1)S(1)} %collective-permute-done.8.refs_2_), channel_id=1, source_target_pairs={{0,2},{1,5},{2,0},{3,7},{4,6},{5,1},{6,4},{7,3},{8,10},{9,13},{10,... | collective-permute-start | bytes 393224 | tf_op jit(solution)/shard_map/ppermute | solution.py:55
  64.6 0.1 collective-permute-start.18
  64.7 0.8 collective-permute-done.16.refs_3_
  65.5 1.9 %collective-permute-start.20 = (bf16[32,2048]{1,0:T(8,128)(2,1)S(1)}, bf16[32,2048]{1,0:T(8,128)(2,1)S(1)}, u32[]{:S(2)}, u32[]{:S(2)}) collective-permute-start(bf16[32,2048]{1,0:T(8,128)(2,1)S(1)} %collective-permute-done.16.refs_3_), channel_id=1, source_target_pairs={{0,2},{1,3},{2,0},{3,1},{4,6},{5,7},{6,4},{7,5},{8,10},{9,11},{10,... | collective-permute-start | bytes 393224 | tf_op jit(solution)/shard_map/ppermute | solution.py:55
  67.5 0.0 collective-permute-done.19.refs_6_
  67.5 0.1 collective-permute-start.11
  67.6 0.8 collective-permute-done.9.refs_3_
  68.3 1.9 %collective-permute-start.13 = (bf16[32,2048]{1,0:T(8,128)(2,1)S(1)}, bf16[32,2048]{1,0:T(8,128)(2,1)S(1)}, u32[]{:S(2)}, u32[]{:S(2)}) collective-permute-start(bf16[32,2048]{1,0:T(8,128)(2,1)S(1)} %collective-permute-done.9.refs_3_), channel_id=1, source_target_pairs={{0,2},{1,5},{2,0},{3,7},{4,6},{5,1},{6,4},{7,3},{8,10},{9,13},{10,... | collective-permute-start | bytes 393224 | tf_op jit(solution)/shard_map/ppermute | solution.py:55
  70.3 0.0 collective-permute-done.18.refs_5_
  70.3 0.8 collective-permute-done.20.refs_7_
  71.0 2.4 %combine.2.refs_8_ = f32[256,2048]{1,0:T(8,128)S(1)} custom-call(bf16[32,2048]{1,0:T(8,128)(2,1)S(1)} %get-tuple-element.56.refs_0_, bf16[32,2048]{1,0:T(8,128)(2,1)S(1)} %collective-permute-done.14.refs_1_, bf16[32,2048]{1,0:T(8,128)(2,1)S(1)} %collective-permute-done.15.refs_2_, bf16[32,2048]{1,0:T(8,128)(2,1)S(1)} %collective-permute-done.16.refs_3_, ...), custom_call_target="tpu_custom_call" | custom-call | tf_op jit(solution)/shard_map/combine/pallas_call | solution.py:395
  73.4 0.0 collective-permute-done.12.refs_6_
  73.5 0.0 collective-permute-done.11.refs_5_
  73.5 0.4 collective-permute-done.13.refs_7_
  73.8 2.5 %combine.3 = (bf16[128,2048]{1,0:T(8,128)(2,1)S(1)}, f32[128,2048]{1,0:T(8,128)S(1)}) custom-call(bf16[32,2048]{1,0:T(8,128)(2,1)S(1)} %attend.2.refs_0_, bf16[32,2048]{1,0:T(8,128)(2,1)S(1)} %collective-permute-done.7.refs_1_, bf16[32,2048]{1,0:T(8,128)(2,1)S(1)} %collective-permute-done.8.refs_2_, bf16[32,2048]{1,0:T(8,128)(2,1)S(1)} %collective-permute-done.9.refs_3_, ...), custom_call_target="tpu_custom_call" | custom-call | tf_op jit(solution)/shard_map/combine/pallas_call | solution.py:395
  76.3 0.1 collective-permute-start.21
  76.4 1.9 %collective-permute-done.21 = bf16[128,2048]{1,0:T(8,128)(2,1)S(1)} collective-permute-done((bf16[128,2048]{1,0:T(8,128)(2,1)S(1)}, bf16[128,2048]{1,0:T(8,128)(2,1)S(1)}, u32[]{:S(2)}, u32[]{:S(2)}) %collective-permute-start.21) | collective-permute-done | bytes 524320 | tf_op jit(solution)/shard_map/ppermute | solution.py:520
  78.3 0.9 %add_convert_fusion = bf16[128,2048]{1,0:T(8,128)(2,1)} fusion(f32[128,2048]{1,0:T(8,128)S(1)} %get-tuple-element.59, bf16[128,2048]{1,0:T(8,128)(2,1)S(1)} %collective-permute-done.21), kind=kLoop, calls=%fused_computation.3 | loop fusion | flops 786432 | bytes 2097152 | tf_op jit(solution)/shard_map/convert_element_type | solution.py:521
  (9 shorter events, 0.2 us)
Async XLA Ops:
  4.4 7.7 %collective-permute-start = (bf16[128,1152]{1,0:T(8,128)(2,1)S(1)}, bf16[128,1152]{1,0:T(8,128)(2,1)S(1)}, u32[]{:S(2)}, u32[]{:S(2)}) collective-permute-start(bf16[128,1152]{1,0:T(8,128)(2,1)S(1)} %get-tuple-element.34), channel_id=1, source_target_pairs={{0,2},{1,5},{2,0},{3,7},{4,6},{5,1},{6,4},{7,3},{8,10},{9,13},{10,... | collective-permute-start | bytes 884744 | tf_op jit(solution)/shard_map/ppermute | solution.py:55
  11.3 7.1 %collective-permute-start.1 = (bf16[128,1280]{1,0:T(8,128)(2,1)S(1)}, bf16[128,1280]{1,0:T(8,128)(2,1)S(1)}, u32[]{:S(2)}, u32[]{:S(2)}) collective-permute-start(bf16[128,1280]{1,0:T(8,128)(2,1)S(1)} %get-tuple-element.36), channel_id=1, source_target_pairs={{0,2},{1,5},{2,0},{3,7},{4,6},{5,1},{6,4},{7,3},{8,10},{9,13},{10,... | collective-permute-start | bytes 983048 | tf_op jit(solution)/shard_map/ppermute | solution.py:55
  12.2 8.0 %copy-start = (s32[8]{0:T(128)S(1)}, s32[8]{0:T(128)}, u32[]{:S(2)}) copy-start(s32[8]{0:T(128)} %length_ref.3) | copy-start | bytes 100
  18.5 12.1 %collective-permute-start.3 = (bf16[64,2432]{1,0:T(8,128)(2,1)S(1)}, bf16[64,2432]{1,0:T(8,128)(2,1)}, u32[]{:S(2)}, u32[]{:S(2)}) collective-permute-start(bf16[64,2432]{1,0:T(8,128)(2,1)S(1)} %fusion.1), channel_id=1, source_target_pairs={{0,4},{1,3},{2,6},{3,1},{4,0},{5,7},{6,2},{7,5},{8,12},{9,11},{10,... | collective-permute-start | bytes 933896 | tf_op jit(solution)/shard_map/ppermute | solution.py:55
  20.4 12.8 %collective-permute-start.2 = (bf16[128,2304]{1,0:T(8,128)(2,1)S(1)}, bf16[128,2304]{1,0:T(8,128)(2,1)S(1)}, u32[]{:S(2)}, u32[]{:S(2)}) collective-permute-start(bf16[128,2304]{1,0:T(8,128)(2,1)S(1)} %get-tuple-element.44), channel_id=1, source_target_pairs={{0,2},{1,5},{2,0},{3,7},{4,6},{5,1},{6,4},{7,3},{8,10},{9,13},{10,... | collective-permute-start | bytes 1769480 | tf_op jit(solution)/shard_map/ppermute | solution.py:55
  31.7 8.0 %collective-permute-start.5 = (bf16[32,2432]{1,0:T(8,128)(2,1)S(1)}, bf16[32,2432]{1,0:T(8,128)(2,1)S(1)}, u32[]{:S(2)}, u32[]{:S(2)}) collective-permute-start(bf16[32,2432]{1,0:T(8,128)(2,1)S(1)} %slice.64), channel_id=1, source_target_pairs={{0,8},{1,9},{2,10},{3,11},{4,12},{5,13},{6,14},{7,15},{8,0},{9,1},... | collective-permute-start | bytes 466952 | tf_op jit(solution)/shard_map/ppermute | solution.py:55
  33.3 8.4 %collective-permute-start.4 = (bf16[64,2304]{1,0:T(8,128)(2,1)S(1)}, bf16[64,2304]{1,0:T(8,128)(2,1)S(1)}, u32[]{:S(2)}, u32[]{:S(2)}) collective-permute-start(bf16[64,2304]{1,0:T(8,128)(2,1)S(1)} %slice.63), channel_id=1, source_target_pairs={{0,4},{1,3},{2,6},{3,1},{4,0},{5,7},{6,2},{7,5},{8,12},{9,11},{10,... | collective-permute-start | bytes 884744 | tf_op jit(solution)/shard_map/ppermute | solution.py:55
  41.8 7.8 %collective-permute-start.6 = (bf16[32,2304]{1,0:T(8,128)(2,1)S(1)}, bf16[32,2304]{1,0:T(8,128)(2,1)S(1)}, u32[]{:S(2)}, u32[]{:S(2)}) collective-permute-start(bf16[32,2304]{1,0:T(8,128)(2,1)S(1)} %slice.65), channel_id=1, source_target_pairs={{0,8},{1,9},{2,10},{3,11},{4,12},{5,13},{6,14},{7,15},{8,0},{9,1},... | collective-permute-start | bytes 442376 | tf_op jit(solution)/shard_map/ppermute | solution.py:55
  46.7 10.1 %collective-permute-start.17 = (bf16[32,2048]{1,0:T(8,128)(2,1)S(1)}, bf16[32,2048]{1,0:T(8,128)(2,1)S(1)}, u32[]{:S(2)}, u32[]{:S(2)}) collective-permute-start(bf16[32,2048]{1,0:T(8,128)(2,1)S(1)} %get-tuple-element.56.refs_0_), channel_id=1, source_target_pairs={{0,2},{1,3},{2,0},{3,1},{4,6},{5,7},{6,4},{7,5},{8,10},{9,11},{10,... | collective-permute-start | bytes 393224 | tf_op jit(solution)/shard_map/ppermute | solution.py:55
  47.2 9.6 %collective-permute-start.15 = (bf16[32,2048]{1,0:T(8,128)(2,1)S(1)}, bf16[32,2048]{1,0:T(8,128)(2,1)S(1)}, u32[]{:S(2)}, u32[]{:S(2)}) collective-permute-start(bf16[32,2048]{1,0:T(8,128)(2,1)S(1)} %get-tuple-element.56.refs_0_), channel_id=1, source_target_pairs={{0,4},{1,5},{2,6},{3,7},{4,0},{5,1},{6,2},{7,3},{8,12},{9,13},{10,... | collective-permute-start | bytes 393224 | tf_op jit(solution)/shard_map/ppermute | solution.py:55
  49.6 9.1 %collective-permute-start.14 = (bf16[32,2048]{1,0:T(8,128)(2,1)S(1)}, bf16[32,2048]{1,0:T(8,128)(2,1)S(1)}, u32[]{:S(2)}, u32[]{:S(2)}) collective-permute-start(bf16[32,2048]{1,0:T(8,128)(2,1)S(1)} %get-tuple-element.56.refs_0_), channel_id=1, source_target_pairs={{0,8},{1,9},{2,10},{3,11},{4,12},{5,13},{6,14},{7,15},{8,0},{9,1},... | collective-permute-start | bytes 393224 | tf_op jit(solution)/shard_map/ppermute | solution.py:55
  53.2 8.2 %collective-permute-start.7 = (bf16[32,2048]{1,0:T(8,128)(2,1)S(1)}, bf16[32,2048]{1,0:T(8,128)(2,1)S(1)}, u32[]{:S(2)}, u32[]{:S(2)}) collective-permute-start(bf16[32,2048]{1,0:T(8,128)(2,1)S(1)} %attend.2.refs_0_), channel_id=1, source_target_pairs={{0,8},{1,9},{2,10},{3,11},{4,12},{5,13},{6,14},{7,15},{8,0},{9,1},... | collective-permute-start | bytes 393224 | tf_op jit(solution)/shard_map/ppermute | solution.py:55
  55.4 7.3 %collective-permute-start.10 = (bf16[32,2048]{1,0:T(8,128)(2,1)S(1)}, bf16[32,2048]{1,0:T(8,128)(2,1)S(1)}, u32[]{:S(2)}, u32[]{:S(2)}) collective-permute-start(bf16[32,2048]{1,0:T(8,128)(2,1)S(1)} %attend.2.refs_0_), channel_id=1, source_target_pairs={{0,2},{1,5},{2,0},{3,7},{4,6},{5,1},{6,4},{7,3},{8,10},{9,13},{10,... | collective-permute-start | bytes 393224 | tf_op jit(solution)/shard_map/ppermute | solution.py:55
  56.9 5.8 %collective-permute-start.8 = (bf16[32,2048]{1,0:T(8,128)(2,1)S(1)}, bf16[32,2048]{1,0:T(8,128)(2,1)S(1)}, u32[]{:S(2)}, u32[]{:S(2)}) collective-permute-start(bf16[32,2048]{1,0:T(8,128)(2,1)S(1)} %attend.2.refs_0_), channel_id=1, source_target_pairs={{0,4},{1,3},{2,6},{3,1},{4,0},{5,7},{6,2},{7,5},{8,12},{9,11},{10,... | collective-permute-start | bytes 393224 | tf_op jit(solution)/shard_map/ppermute | solution.py:55
  58.7 6.8 %collective-permute-start.16 = (bf16[32,2048]{1,0:T(8,128)(2,1)S(1)}, bf16[32,2048]{1,0:T(8,128)(2,1)S(1)}, u32[]{:S(2)}, u32[]{:S(2)}) collective-permute-start(bf16[32,2048]{1,0:T(8,128)(2,1)S(1)} %collective-permute-done.14.refs_1_), channel_id=1, source_target_pairs={{0,4},{1,5},{2,6},{3,7},{4,0},{5,1},{6,2},{7,3},{8,12},{9,13},{10,... | collective-permute-start | bytes 393224 | tf_op jit(solution)/shard_map/ppermute | solution.py:55
  58.9 8.5 %collective-permute-start.19 = (bf16[32,2048]{1,0:T(8,128)(2,1)S(1)}, bf16[32,2048]{1,0:T(8,128)(2,1)S(1)}, u32[]{:S(2)}, u32[]{:S(2)}) collective-permute-start(bf16[32,2048]{1,0:T(8,128)(2,1)S(1)} %collective-permute-done.15.refs_2_), channel_id=1, source_target_pairs={{0,2},{1,3},{2,0},{3,1},{4,6},{5,7},{6,4},{7,5},{8,10},{9,11},{10,... | collective-permute-start | bytes 393224 | tf_op jit(solution)/shard_map/ppermute | solution.py:55
  61.4 7.0 %collective-permute-start.9 = (bf16[32,2048]{1,0:T(8,128)(2,1)S(1)}, bf16[32,2048]{1,0:T(8,128)(2,1)S(1)}, u32[]{:S(2)}, u32[]{:S(2)}) collective-permute-start(bf16[32,2048]{1,0:T(8,128)(2,1)S(1)} %collective-permute-done.7.refs_1_), channel_id=1, source_target_pairs={{0,4},{1,3},{2,6},{3,1},{4,0},{5,7},{6,2},{7,5},{8,12},{9,11},{10,... | collective-permute-start | bytes 393224 | tf_op jit(solution)/shard_map/ppermute | solution.py:55
  62.7 10.7 %collective-permute-start.12 = (bf16[32,2048]{1,0:T(8,128)(2,1)S(1)}, bf16[32,2048]{1,0:T(8,128)(2,1)S(1)}, u32[]{:S(2)}, u32[]{:S(2)}) collective-permute-start(bf16[32,2048]{1,0:T(8,128)(2,1)S(1)} %collective-permute-done.8.refs_2_), channel_id=1, source_target_pairs={{0,2},{1,5},{2,0},{3,7},{4,6},{5,1},{6,4},{7,3},{8,10},{9,13},{10,... | collective-permute-start | bytes 393224 | tf_op jit(solution)/shard_map/ppermute | solution.py:55
  64.6 5.6 %collective-permute-start.18 = (bf16[32,2048]{1,0:T(8,128)(2,1)S(1)}, bf16[32,2048]{1,0:T(8,128)(2,1)S(1)}, u32[]{:S(2)}, u32[]{:S(2)}) collective-permute-start(bf16[32,2048]{1,0:T(8,128)(2,1)S(1)} %collective-permute-done.14.refs_1_), channel_id=1, source_target_pairs={{0,2},{1,3},{2,0},{3,1},{4,6},{5,7},{6,4},{7,5},{8,10},{9,11},{10,... | collective-permute-start | bytes 393224 | tf_op jit(solution)/shard_map/ppermute | solution.py:55
  65.5 5.5 %collective-permute-start.20 = (bf16[32,2048]{1,0:T(8,128)(2,1)S(1)}, bf16[32,2048]{1,0:T(8,128)(2,1)S(1)}, u32[]{:S(2)}, u32[]{:S(2)}) collective-permute-start(bf16[32,2048]{1,0:T(8,128)(2,1)S(1)} %collective-permute-done.16.refs_3_), channel_id=1, source_target_pairs={{0,2},{1,3},{2,0},{3,1},{4,6},{5,7},{6,4},{7,5},{8,10},{9,11},{10,... | collective-permute-start | bytes 393224 | tf_op jit(solution)/shard_map/ppermute | solution.py:55
  67.5 6.0 %collective-permute-start.11 = (bf16[32,2048]{1,0:T(8,128)(2,1)S(1)}, bf16[32,2048]{1,0:T(8,128)(2,1)S(1)}, u32[]{:S(2)}, u32[]{:S(2)}) collective-permute-start(bf16[32,2048]{1,0:T(8,128)(2,1)S(1)} %collective-permute-done.7.refs_1_), channel_id=1, source_target_pairs={{0,2},{1,5},{2,0},{3,7},{4,6},{5,1},{6,4},{7,3},{8,10},{9,13},{10,... | collective-permute-start | bytes 393224 | tf_op jit(solution)/shard_map/ppermute | solution.py:55
  68.3 5.5 %collective-permute-start.13 = (bf16[32,2048]{1,0:T(8,128)(2,1)S(1)}, bf16[32,2048]{1,0:T(8,128)(2,1)S(1)}, u32[]{:S(2)}, u32[]{:S(2)}) collective-permute-start(bf16[32,2048]{1,0:T(8,128)(2,1)S(1)} %collective-permute-done.9.refs_3_), channel_id=1, source_target_pairs={{0,2},{1,5},{2,0},{3,7},{4,6},{5,1},{6,4},{7,3},{8,10},{9,13},{10,... | collective-permute-start | bytes 393224 | tf_op jit(solution)/shard_map/ppermute | solution.py:55
  76.3 2.0 %collective-permute-start.21 = (bf16[128,2048]{1,0:T(8,128)(2,1)S(1)}, bf16[128,2048]{1,0:T(8,128)(2,1)S(1)}, u32[]{:S(2)}, u32[]{:S(2)}) collective-permute-start(bf16[128,2048]{1,0:T(8,128)(2,1)S(1)} %get-tuple-element.60), channel_id=1, source_target_pairs={{0,1},{1,0},{2,3},{3,2},{4,5},{5,4},{6,7},{7,6},{8,9},{9,8},{10,11... | collective-permute-start | bytes 1572872 | tf_op jit(solution)/shard_map/ppermute | solution.py:520

commit v15 on v14

--- a/solution.py
+++ b/solution.py
@@ -465,6 +465,7 @@
     lead, follow = flows
     w_rows = w_out.shape[0] // CHUNKS
     weights = [fetch_rows(after(w_out, lead[2], follow[2]), 0, w_rows)]
+    follow[2] = after(follow[2], weights[0])
     while follow[0] < levels:
         pending = [start(flow) for flow in flows if flow[0] < levels]
         if lead[0] == levels:

time: 79.3 us -> 84.1 us (1.061)
  waiting for transfers between devices: 16.9 us -> 25.8 us
  starting transfers between devices: 27.1 us -> 23 us
    ppermute x21, waiting for transfers between devices: 15 us -> 23.9 us  [exchange(): return lax.ppermute(value, ('gx', 'gy'), pairs)]
    ppermute x21, starting transfers between devices: 27.1 us -> 22.9 us  [exchange(): return lax.ppermute(value, ('gx', 'gy'), pairs)]
  transfers between devices with their start and end apart: 22 -> 22, of which waited for: 12 -> 15; matrix products, arithmetic and copies ran while one was open for 2% -> 2% of each run, Pallas kernels for 32% -> 30%
where the time goes in v15:
time: 84.1 us; the launch traced here: 83.9 us
  Pallas kernels  32.2 us (38%)
  waiting for transfers between devices  25.8 us (31%)
  starting transfers between devices  23 us (27%)
  other arithmetic  2.58 us (3%)
    ppermute x21, waiting for transfers between devices, exchange(): return lax.ppermute(value, ('gx', 'gy'), pairs)  23.9 us
    ppermute x21, starting transfers between devices, exchange(): return lax.ppermute(value, ('gx', 'gy'), pairs)  22.9 us
    pallas_call x3, Pallas kernels, project(): pl.pallas_call(functools.partial(project_kernel, n, q_start, kv_start, fi...  13.6 us
    pallas_call x2, Pallas kernels, attend(): pl.pallas_call(functools.partial(attend_kernel, chunk, offsets, kv_offset...  6.78 us
    pallas_call x2, Pallas kernels, combine(): pl.pallas_call(functools.partial(combine_kernel, n, block, chunk), out_sh...  4.89 us
    pallas_call x1, Pallas kernels, fetch_rows(): pl.pallas_call(functools.partial(fetch_rows_kernel, start, pieces), out_s...  3.51 us
    pallas_call x1, Pallas kernels, fetch(): pl.pallas_call(functools.partial(fetch_kernel, len(arrays), pieces), out_...  3.47 us
    ppermute x1, waiting for transfers between devices, shards(): other = lax.ppermute(send, 'gy', [(0, 1), (1, 0)])  1.9 us
  transfers between devices with their start and end apart: 22, of which 15 were waited for; matrix products, arithmetic and copies ran while one was open for 2% of the time, Pallas kernels for 30%

profile of v15, /device:TPU:0, one launch (start us, length us, event | category | flops | bytes accessed | tf_op | source)
XLA Modules:
  0.0 83.9 jit_solution(12941713782176198873)
XLA Ops:
  0.0 4.4 %project.3 = (bf16[128,1152]{1,0:T(8,128)(2,1)S(1)}, f32[128,1152]{1,0:T(8,128)S(1)}, bf16[256,2048]{1,0:T(8,128)(2,1)S(1)}) custom-call(bf16[256,2048]{1,0:T(8,128)(2,1)} %refs_0_.1, f32[1,2048]{1,0:T(1,128)} %bitcast.1, bf16[2048,4096]{1,0:T(8,128)(2,1)} %refs_1_.3, bf16[2048,256]{1,0:T(8,128)(2,1)} %refs_2_.5, bf16[2048,256]{1,0:T(8,128)(2,1)} %refs_3_.5), custom_call_target="tpu_custom_call" | custom-call | tf_op jit(solution)/shard_map/project/pallas_call | solution.py:161
  4.4 3.0 %collective-permute-start = (bf16[128,1152]{1,0:T(8,128)(2,1)S(1)}, bf16[128,1152]{1,0:T(8,128)(2,1)S(1)}, u32[]{:S(2)}, u32[]{:S(2)}) collective-permute-start(bf16[128,1152]{1,0:T(8,128)(2,1)S(1)} %get-tuple-element.35), channel_id=1, source_target_pairs={{0,2},{1,5},{2,0},{3,7},{4,6},{5,1},{6,4},{7,3},{8,10},{9,13},{10,... | collective-permute-start | bytes 884744 | tf_op jit(solution)/shard_map/ppermute | solution.py:55
  7.4 3.9 %project.4 = (bf16[128,1280]{1,0:T(8,128)(2,1)S(1)}, f32[128,1280]{1,0:T(8,128)S(1)}) custom-call(bf16[256,2048]{1,0:T(8,128)(2,1)S(1)} %get-tuple-element.40.refs_0_, bf16[2048,4096]{1,0:T(8,128)(2,1)} %refs_1_.3, bf16[2048,256]{1,0:T(8,128)(2,1)} %refs_2_.5, bf16[2048,256]{1,0:T(8,128)(2,1)} %refs_3_.5), custom_call_target="tpu_custom_call" | custom-call | tf_op jit(solution)/shard_map/project/pallas_call | solution.py:161
  11.3 0.1 collective-permute-start.1
  11.4 0.7 collective-permute-done
  12.1 0.1 convert_add_fusion.2
  12.2 0.0 copy-start
  12.2 5.3 %project.5 = (bf16[128,2304]{1,0:T(8,128)(2,1)S(1)}, f32[128,2304]{1,0:T(8,128)S(1)}) custom-call(bf16[256,2048]{1,0:T(8,128)(2,1)S(1)} %get-tuple-element.40.refs_0_, bf16[2048,4096]{1,0:T(8,128)(2,1)} %refs_1_.3, bf16[2048,256]{1,0:T(8,128)(2,1)} %refs_2_.5, bf16[2048,256]{1,0:T(8,128)(2,1)} %refs_3_.5), custom_call_target="tpu_custom_call" | custom-call | tf_op jit(solution)/shard_map/project/pallas_call | solution.py:161
  17.5 0.9 %collective-permute-done.1 = bf16[128,1280]{1,0:T(8,128)(2,1)S(1)} collective-permute-done((bf16[128,1280]{1,0:T(8,128)(2,1)S(1)}, bf16[128,1280]{1,0:T(8,128)(2,1)S(1)}, u32[]{:S(2)}, u32[]{:S(2)}) %collective-permute-start.1) | collective-permute-done | bytes 327712 | tf_op jit(solution)/shard_map/ppermute | solution.py:55
  18.4 0.1 convert_add_fusion.1
  18.5 1.6 %collective-permute-start.3 = (bf16[64,2432]{1,0:T(8,128)(2,1)S(1)}, bf16[64,2432]{1,0:T(8,128)(2,1)}, u32[]{:S(2)}, u32[]{:S(2)}) collective-permute-start(bf16[64,2432]{1,0:T(8,128)(2,1)S(1)} %fusion.1), channel_id=1, source_target_pairs={{0,4},{1,3},{2,6},{3,1},{4,0},{5,7},{6,2},{7,5},{8,12},{9,11},{10,... | collective-permute-start | bytes 933896 | tf_op jit(solution)/shard_map/ppermute | solution.py:55
  20.2 0.1 add_convert_fusion.1
  20.3 0.1 convert_element_type.49
  20.4 3.5 %fetch_rows.1.refs_8_ = bf16[2048,2048]{1,0:T(8,128)(2,1)S(1)} custom-call(bf16[4096,2048]{1,0:T(8,128)(2,1)} %refs_6_.1), custom_call_target="tpu_custom_call" | custom-call | tf_op jit(solution)/shard_map/fetch_rows/pallas_call | solution.py:343
  23.9 1.2 %collective-permute-start.2 = (bf16[128,2304]{1,0:T(8,128)(2,1)S(1)}, bf16[128,2304]{1,0:T(8,128)(2,1)S(1)}, u32[]{:S(2)}, u32[]{:S(2)}) collective-permute-start(bf16[128,2304]{1,0:T(8,128)(2,1)S(1)} %get-tuple-element.47), channel_id=1, source_target_pairs={{0,2},{1,5},{2,0},{3,7},{4,6},{5,1},{6,4},{7,3},{8,10},{9,13},{10,... | collective-permute-start | bytes 1769480 | tf_op jit(solution)/shard_map/ppermute | solution.py:55
  25.0 1.2 %collective-permute-done.3 = bf16[64,2432]{1,0:T(8,128)(2,1)} collective-permute-done((bf16[64,2432]{1,0:T(8,128)(2,1)S(1)}, bf16[64,2432]{1,0:T(8,128)(2,1)}, u32[]{:S(2)}, u32[]{:S(2)}) %collective-permute-start.3) | collective-permute-done | bytes 311328 | tf_op jit(solution)/shard_map/ppermute | solution.py:55
  26.2 1.0 %fusion.2 = f32[64,2432]{1,0:T(8,128)S(1)} fusion(f32[128,1280]{1,0:T(8,128)S(1)} %convert_add_fusion.1, f32[128,1152]{1,0:T(8,128)S(1)} %convert_add_fusion.2, bf16[64,2432]{1,0:T(8,128)(2,1)} %collective-permute-done.3), kind=kLoop, calls=%fused_computation.8 | loop fusion | flops 466944 | bytes 2179072 | tf_op jit(solution)/shard_map/add | solution.py:461
  27.3 2.5 %collective-permute-start.5 = (bf16[32,2432]{1,0:T(8,128)(2,1)S(1)}, bf16[32,2432]{1,0:T(8,128)(2,1)S(1)}, u32[]{:S(2)}, u32[]{:S(2)}) collective-permute-start(bf16[32,2432]{1,0:T(8,128)(2,1)S(1)} %slice.64), channel_id=1, source_target_pairs={{0,8},{1,9},{2,10},{3,11},{4,12},{5,13},{6,14},{7,15},{8,0},{9,1},... | collective-permute-start | bytes 466952 | tf_op jit(solution)/shard_map/ppermute | solution.py:55
  29.8 4.0 %collective-permute-done.2 = bf16[128,2304]{1,0:T(8,128)(2,1)S(1)} collective-permute-done((bf16[128,2304]{1,0:T(8,128)(2,1)S(1)}, bf16[128,2304]{1,0:T(8,128)(2,1)S(1)}, u32[]{:S(2)}, u32[]{:S(2)}) %collective-permute-start.2) | collective-permute-done | bytes 589856 | tf_op jit(solution)/shard_map/ppermute | solution.py:55
  33.8 0.1 convert_add_fusion
  34.0 0.5 collective-permute-start.4
  34.5 3.5 %fetch.1 = (bf16[8,1024,256]{2,1,0:T(8,128)(2,1)S(1)}, bf16[8,1024,256]{2,1,0:T(8,128)(2,1)S(1)}) custom-call(bf16[8,1024,256]{2,1,0:T(8,128)(2,1)} %refs_0_.2, bf16[8,1024,256]{2,1,0:T(8,128)(2,1)} %refs_1_.4), custom_call_target="tpu_custom_call" | custom-call | tf_op jit(solution)/shard_map/fetch/pallas_call | solution.py:314
  38.0 0.0 collective-permute-done.5
  38.0 2.7 %collective-permute-done.4 = bf16[64,2304]{1,0:T(8,128)(2,1)S(1)} collective-permute-done((bf16[64,2304]{1,0:T(8,128)(2,1)S(1)}, bf16[64,2304]{1,0:T(8,128)(2,1)S(1)}, u32[]{:S(2)}, u32[]{:S(2)}) %collective-permute-start.4) | collective-permute-done | bytes 294944 | tf_op jit(solution)/shard_map/ppermute | solution.py:55
  40.8 0.1 slice_add_fusion
  40.8 2.7 %collective-permute-start.6 = (bf16[32,2304]{1,0:T(8,128)(2,1)S(1)}, bf16[32,2304]{1,0:T(8,128)(2,1)S(1)}, u32[]{:S(2)}, u32[]{:S(2)}) collective-permute-start(bf16[32,2304]{1,0:T(8,128)(2,1)S(1)} %slice.65), channel_id=1, source_target_pairs={{0,8},{1,9},{2,10},{3,11},{4,12},{5,13},{6,14},{7,15},{8,0},{9,1},... | collective-permute-start | bytes 442376 | tf_op jit(solution)/shard_map/ppermute | solution.py:55
  43.5 0.1 fusion.3
  43.6 0.1 pad_maximum_fusion.1
  43.7 4.0 %attend.3 = (bf16[32,2048]{1,0:T(8,128)(2,1)S(1)}, bf16[2048,2048]{1,0:T(8,128)(2,1)S(1)}) custom-call(s32[8]{0:T(128)S(1)} %copy-done, f32[32,2432]{1,0:T(8,128)S(1)} %slice_add_fusion.1.refs_0_, f32[32,128]{1,0:T(8,128)S(1)} %slice.48.refs_1_, f32[32,128]{1,0:T(8,128)S(1)} %get-tuple-element.66.refs_2_, f32[32,128]{1,0:T(8,128)S(1)} %get-tuple-element.67.refs_3_, ...), custom_call_target="tpu_custom_call" | custom-call | tf_op jit(solution)/shard_map/attend/pallas_call | solution.py:281
  47.8 1.2 %collective-permute-start.17 = (bf16[32,2048]{1,0:T(8,128)(2,1)S(1)}, bf16[32,2048]{1,0:T(8,128)(2,1)S(1)}, u32[]{:S(2)}, u32[]{:S(2)}) collective-permute-start(bf16[32,2048]{1,0:T(8,128)(2,1)S(1)} %get-tuple-element.58.refs_0_), channel_id=1, source_target_pairs={{0,2},{1,3},{2,0},{3,1},{4,6},{5,7},{6,4},{7,5},{8,10},{9,11},{10,... | collective-permute-start | bytes 393224 | tf_op jit(solution)/shard_map/ppermute | solution.py:55
  48.9 0.6 collective-permute-start.15
  49.5 1.3 %collective-permute-done.6 = bf16[32,2304]{1,0:T(8,128)(2,1)S(1)} collective-permute-done((bf16[32,2304]{1,0:T(8,128)(2,1)S(1)}, bf16[32,2304]{1,0:T(8,128)(2,1)S(1)}, u32[]{:S(2)}, u32[]{:S(2)}) %collective-permute-start.6) | collective-permute-done | bytes 147488 | tf_op jit(solution)/shard_map/ppermute | solution.py:55
  50.8 0.1 collective-permute-start.14
  50.9 2.7 %attend.2.refs_0_ = bf16[32,2048]{1,0:T(8,128)(2,1)S(1)} custom-call(s32[8]{0:T(128)S(1)} %copy-done, f32[32,2304]{1,0:T(8,128)S(1)} %slice_add_fusion.2.refs_0_, f32[32,128]{1,0:T(8,128)S(1)} %slice.48.refs_1_, f32[32,128]{1,0:T(8,128)S(1)} %get-tuple-element.66.refs_2_, f32[32,128]{1,0:T(8,128)S(1)} %get-tuple-element.67.refs_3_, ...), custom_call_target="tpu_custom_call" | custom-call | tf_op jit(solution)/shard_map/attend/pallas_call | solution.py:281
  53.6 3.0 %collective-permute-start.7 = (bf16[32,2048]{1,0:T(8,128)(2,1)S(1)}, bf16[32,2048]{1,0:T(8,128)(2,1)S(1)}, u32[]{:S(2)}, u32[]{:S(2)}) collective-permute-start(bf16[32,2048]{1,0:T(8,128)(2,1)S(1)} %attend.2.refs_0_), channel_id=1, source_target_pairs={{0,8},{1,9},{2,10},{3,11},{4,12},{5,13},{6,14},{7,15},{8,0},{9,1},... | collective-permute-start | bytes 393224 | tf_op jit(solution)/shard_map/ppermute | solution.py:55
  56.6 1.1 %collective-permute-start.10 = (bf16[32,2048]{1,0:T(8,128)(2,1)S(1)}, bf16[32,2048]{1,0:T(8,128)(2,1)S(1)}, u32[]{:S(2)}, u32[]{:S(2)}) collective-permute-start(bf16[32,2048]{1,0:T(8,128)(2,1)S(1)} %attend.2.refs_0_), channel_id=1, source_target_pairs={{0,2},{1,5},{2,0},{3,7},{4,6},{5,1},{6,4},{7,3},{8,10},{9,13},{10,... | collective-permute-start | bytes 393224 | tf_op jit(solution)/shard_map/ppermute | solution.py:55
  57.7 0.0 collective-permute-done.17.refs_4_
  57.7 0.0 collective-permute-start.8
  57.7 0.0 collective-permute-done.15.refs_2_
  57.7 4.3 %collective-permute-done.14.refs_1_ = bf16[32,2048]{1,0:T(8,128)(2,1)S(1)} collective-permute-done((bf16[32,2048]{1,0:T(8,128)(2,1)S(1)}, bf16[32,2048]{1,0:T(8,128)(2,1)S(1)}, u32[]{:S(2)}, u32[]{:S(2)}) %collective-permute-start.14) | collective-permute-done | bytes 131104 | tf_op jit(solution)/shard_map/ppermute | solution.py:55
  62.0 0.0 collective-permute-start.16
  62.0 0.5 collective-permute-start.19
  62.5 2.5 %collective-permute-done.7.refs_1_ = bf16[32,2048]{1,0:T(8,128)(2,1)S(1)} collective-permute-done((bf16[32,2048]{1,0:T(8,128)(2,1)S(1)}, bf16[32,2048]{1,0:T(8,128)(2,1)S(1)}, u32[]{:S(2)}, u32[]{:S(2)}) %collective-permute-start.7) | collective-permute-done | bytes 131104 | tf_op jit(solution)/shard_map/ppermute | solution.py:55
  65.0 0.0 collective-permute-start.9
  65.0 0.0 collective-permute-done.10.refs_4_
  65.0 1.2 %collective-permute-done.8.refs_2_ = bf16[32,2048]{1,0:T(8,128)(2,1)S(1)} collective-permute-done((bf16[32,2048]{1,0:T(8,128)(2,1)S(1)}, bf16[32,2048]{1,0:T(8,128)(2,1)S(1)}, u32[]{:S(2)}, u32[]{:S(2)}) %collective-permute-start.8) | collective-permute-done | bytes 131104 | tf_op jit(solution)/shard_map/ppermute | solution.py:55
  66.2 0.8 collective-permute-start.12
  67.0 1.2 %collective-permute-start.18 = (bf16[32,2048]{1,0:T(8,128)(2,1)S(1)}, bf16[32,2048]{1,0:T(8,128)(2,1)S(1)}, u32[]{:S(2)}, u32[]{:S(2)}) collective-permute-start(bf16[32,2048]{1,0:T(8,128)(2,1)S(1)} %collective-permute-done.14.refs_1_), channel_id=1, source_target_pairs={{0,2},{1,3},{2,0},{3,1},{4,6},{5,7},{6,4},{7,5},{8,10},{9,11},{10,... | collective-permute-start | bytes 393224 | tf_op jit(solution)/shard_map/ppermute | solution.py:55
  68.2 0.4 collective-permute-done.16.refs_3_
  68.6 0.8 collective-permute-start.20
  69.4 0.0 collective-permute-done.19.refs_6_
  69.4 1.2 %collective-permute-start.11 = (bf16[32,2048]{1,0:T(8,128)(2,1)S(1)}, bf16[32,2048]{1,0:T(8,128)(2,1)S(1)}, u32[]{:S(2)}, u32[]{:S(2)}) collective-permute-start(bf16[32,2048]{1,0:T(8,128)(2,1)S(1)} %collective-permute-done.7.refs_1_), channel_id=1, source_target_pairs={{0,2},{1,5},{2,0},{3,7},{4,6},{5,1},{6,4},{7,3},{8,10},{9,13},{10,... | collective-permute-start | bytes 393224 | tf_op jit(solution)/shard_map/ppermute | solution.py:55
  70.6 0.6 collective-permute-done.9.refs_3_
  71.2 0.9 %collective-permute-start.13 = (bf16[32,2048]{1,0:T(8,128)(2,1)S(1)}, bf16[32,2048]{1,0:T(8,128)(2,1)S(1)}, u32[]{:S(2)}, u32[]{:S(2)}) collective-permute-start(bf16[32,2048]{1,0:T(8,128)(2,1)S(1)} %collective-permute-done.9.refs_3_), channel_id=1, source_target_pairs={{0,2},{1,5},{2,0},{3,7},{4,6},{5,1},{6,4},{7,3},{8,10},{9,13},{10,... | collective-permute-start | bytes 393224 | tf_op jit(solution)/shard_map/ppermute | solution.py:55
  72.1 2.3 %collective-permute-done.18.refs_5_ = bf16[32,2048]{1,0:T(8,128)(2,1)S(1)} collective-permute-done((bf16[32,2048]{1,0:T(8,128)(2,1)S(1)}, bf16[32,2048]{1,0:T(8,128)(2,1)S(1)}, u32[]{:S(2)}, u32[]{:S(2)}) %collective-permute-start.18) | collective-permute-done | bytes 131104 | tf_op jit(solution)/shard_map/ppermute | solution.py:55
  74.4 1.4 %collective-permute-done.20.refs_7_ = bf16[32,2048]{1,0:T(8,128)(2,1)S(1)} collective-permute-done((bf16[32,2048]{1,0:T(8,128)(2,1)S(1)}, bf16[32,2048]{1,0:T(8,128)(2,1)S(1)}, u32[]{:S(2)}, u32[]{:S(2)}) %collective-permute-start.20) | collective-permute-done | bytes 131104 | tf_op jit(solution)/shard_map/ppermute | solution.py:55
  75.8 2.4 %combine.2.refs_8_ = f32[256,2048]{1,0:T(8,128)S(1)} custom-call(bf16[32,2048]{1,0:T(8,128)(2,1)S(1)} %get-tuple-element.58.refs_0_, bf16[32,2048]{1,0:T(8,128)(2,1)S(1)} %collective-permute-done.14.refs_1_, bf16[32,2048]{1,0:T(8,128)(2,1)S(1)} %collective-permute-done.15.refs_2_, bf16[32,2048]{1,0:T(8,128)(2,1)S(1)} %collective-permute-done.16.refs_3_, ...), custom_call_target="tpu_custom_call" | custom-call | tf_op jit(solution)/shard_map/combine/pallas_call | solution.py:395
  78.2 0.0 collective-permute-done.12.refs_6_
  78.2 0.0 collective-permute-done.11.refs_5_
  78.2 0.4 collective-permute-done.13.refs_7_
  78.6 2.5 %combine.3 = (bf16[128,2048]{1,0:T(8,128)(2,1)S(1)}, f32[128,2048]{1,0:T(8,128)S(1)}) custom-call(bf16[32,2048]{1,0:T(8,128)(2,1)S(1)} %attend.2.refs_0_, bf16[32,2048]{1,0:T(8,128)(2,1)S(1)} %collective-permute-done.7.refs_1_, bf16[32,2048]{1,0:T(8,128)(2,1)S(1)} %collective-permute-done.8.refs_2_, bf16[32,2048]{1,0:T(8,128)(2,1)S(1)} %collective-permute-done.9.refs_3_, ...), custom_call_target="tpu_custom_call" | custom-call | tf_op jit(solution)/shard_map/combine/pallas_call | solution.py:395
  81.1 0.1 collective-permute-start.21
  81.2 1.9 %collective-permute-done.21 = bf16[128,2048]{1,0:T(8,128)(2,1)S(1)} collective-permute-done((bf16[128,2048]{1,0:T(8,128)(2,1)S(1)}, bf16[128,2048]{1,0:T(8,128)(2,1)S(1)}, u32[]{:S(2)}, u32[]{:S(2)}) %collective-permute-start.21) | collective-permute-done | bytes 524320 | tf_op jit(solution)/shard_map/ppermute | solution.py:521
  83.0 0.9 %add_convert_fusion = bf16[128,2048]{1,0:T(8,128)(2,1)} fusion(f32[128,2048]{1,0:T(8,128)S(1)} %get-tuple-element.61, bf16[128,2048]{1,0:T(8,128)(2,1)S(1)} %collective-permute-done.21), kind=kLoop, calls=%fused_computation.3 | loop fusion | flops 786432 | bytes 2097152 | tf_op jit(solution)/shard_map/convert_element_type | solution.py:522
  (9 shorter events, 0.2 us)
Async XLA Ops:
  4.4 7.7 %collective-permute-start = (bf16[128,1152]{1,0:T(8,128)(2,1)S(1)}, bf16[128,1152]{1,0:T(8,128)(2,1)S(1)}, u32[]{:S(2)}, u32[]{:S(2)}) collective-permute-start(bf16[128,1152]{1,0:T(8,128)(2,1)S(1)} %get-tuple-element.35), channel_id=1, source_target_pairs={{0,2},{1,5},{2,0},{3,7},{4,6},{5,1},{6,4},{7,3},{8,10},{9,13},{10,... | collective-permute-start | bytes 884744 | tf_op jit(solution)/shard_map/ppermute | solution.py:55
  11.3 7.1 %collective-permute-start.1 = (bf16[128,1280]{1,0:T(8,128)(2,1)S(1)}, bf16[128,1280]{1,0:T(8,128)(2,1)S(1)}, u32[]{:S(2)}, u32[]{:S(2)}) collective-permute-start(bf16[128,1280]{1,0:T(8,128)(2,1)S(1)} %get-tuple-element.37), channel_id=1, source_target_pairs={{0,2},{1,5},{2,0},{3,7},{4,6},{5,1},{6,4},{7,3},{8,10},{9,13},{10,... | collective-permute-start | bytes 983048 | tf_op jit(solution)/shard_map/ppermute | solution.py:55
  12.2 8.0 %copy-start = (s32[8]{0:T(128)S(1)}, s32[8]{0:T(128)}, u32[]{:S(2)}) copy-start(s32[8]{0:T(128)} %length_ref.3) | copy-start | bytes 100
  18.5 7.7 %collective-permute-start.3 = (bf16[64,2432]{1,0:T(8,128)(2,1)S(1)}, bf16[64,2432]{1,0:T(8,128)(2,1)}, u32[]{:S(2)}, u32[]{:S(2)}) collective-permute-start(bf16[64,2432]{1,0:T(8,128)(2,1)S(1)} %fusion.1), channel_id=1, source_target_pairs={{0,4},{1,3},{2,6},{3,1},{4,0},{5,7},{6,2},{7,5},{8,12},{9,11},{10,... | collective-permute-start | bytes 933896 | tf_op jit(solution)/shard_map/ppermute | solution.py:55
  23.9 9.9 %collective-permute-start.2 = (bf16[128,2304]{1,0:T(8,128)(2,1)S(1)}, bf16[128,2304]{1,0:T(8,128)(2,1)S(1)}, u32[]{:S(2)}, u32[]{:S(2)}) collective-permute-start(bf16[128,2304]{1,0:T(8,128)(2,1)S(1)} %get-tuple-element.47), channel_id=1, source_target_pairs={{0,2},{1,5},{2,0},{3,7},{4,6},{5,1},{6,4},{7,3},{8,10},{9,13},{10,... | collective-permute-start | bytes 1769480 | tf_op jit(solution)/shard_map/ppermute | solution.py:55
  27.3 10.7 %collective-permute-start.5 = (bf16[32,2432]{1,0:T(8,128)(2,1)S(1)}, bf16[32,2432]{1,0:T(8,128)(2,1)S(1)}, u32[]{:S(2)}, u32[]{:S(2)}) collective-permute-start(bf16[32,2432]{1,0:T(8,128)(2,1)S(1)} %slice.64), channel_id=1, source_target_pairs={{0,8},{1,9},{2,10},{3,11},{4,12},{5,13},{6,14},{7,15},{8,0},{9,1},... | collective-permute-start | bytes 466952 | tf_op jit(solution)/shard_map/ppermute | solution.py:55
  34.0 6.8 %collective-permute-start.4 = (bf16[64,2304]{1,0:T(8,128)(2,1)S(1)}, bf16[64,2304]{1,0:T(8,128)(2,1)S(1)}, u32[]{:S(2)}, u32[]{:S(2)}) collective-permute-start(bf16[64,2304]{1,0:T(8,128)(2,1)S(1)} %slice.63), channel_id=1, source_target_pairs={{0,4},{1,3},{2,6},{3,1},{4,0},{5,7},{6,2},{7,5},{8,12},{9,11},{10,... | collective-permute-start | bytes 884744 | tf_op jit(solution)/shard_map/ppermute | solution.py:55
  40.8 10.0 %collective-permute-start.6 = (bf16[32,2304]{1,0:T(8,128)(2,1)S(1)}, bf16[32,2304]{1,0:T(8,128)(2,1)S(1)}, u32[]{:S(2)}, u32[]{:S(2)}) collective-permute-start(bf16[32,2304]{1,0:T(8,128)(2,1)S(1)} %slice.65), channel_id=1, source_target_pairs={{0,8},{1,9},{2,10},{3,11},{4,12},{5,13},{6,14},{7,15},{8,0},{9,1},... | collective-permute-start | bytes 442376 | tf_op jit(solution)/shard_map/ppermute | solution.py:55
  47.8 10.0 %collective-permute-start.17 = (bf16[32,2048]{1,0:T(8,128)(2,1)S(1)}, bf16[32,2048]{1,0:T(8,128)(2,1)S(1)}, u32[]{:S(2)}, u32[]{:S(2)}) collective-permute-start(bf16[32,2048]{1,0:T(8,128)(2,1)S(1)} %get-tuple-element.58.refs_0_), channel_id=1, source_target_pairs={{0,2},{1,3},{2,0},{3,1},{4,6},{5,7},{6,4},{7,5},{8,10},{9,11},{10,... | collective-permute-start | bytes 393224 | tf_op jit(solution)/shard_map/ppermute | solution.py:55
  48.9 8.8 %collective-permute-start.15 = (bf16[32,2048]{1,0:T(8,128)(2,1)S(1)}, bf16[32,2048]{1,0:T(8,128)(2,1)S(1)}, u32[]{:S(2)}, u32[]{:S(2)}) collective-permute-start(bf16[32,2048]{1,0:T(8,128)(2,1)S(1)} %get-tuple-element.58.refs_0_), channel_id=1, source_target_pairs={{0,4},{1,5},{2,6},{3,7},{4,0},{5,1},{6,2},{7,3},{8,12},{9,13},{10,... | collective-permute-start | bytes 393224 | tf_op jit(solution)/shard_map/ppermute | solution.py:55
  50.8 11.2 %collective-permute-start.14 = (bf16[32,2048]{1,0:T(8,128)(2,1)S(1)}, bf16[32,2048]{1,0:T(8,128)(2,1)S(1)}, u32[]{:S(2)}, u32[]{:S(2)}) collective-permute-start(bf16[32,2048]{1,0:T(8,128)(2,1)S(1)} %get-tuple-element.58.refs_0_), channel_id=1, source_target_pairs={{0,8},{1,9},{2,10},{3,11},{4,12},{5,13},{6,14},{7,15},{8,0},{9,1},... | collective-permute-start | bytes 393224 | tf_op jit(solution)/shard_map/ppermute | solution.py:55
  53.6 11.3 %collective-permute-start.7 = (bf16[32,2048]{1,0:T(8,128)(2,1)S(1)}, bf16[32,2048]{1,0:T(8,128)(2,1)S(1)}, u32[]{:S(2)}, u32[]{:S(2)}) collective-permute-start(bf16[32,2048]{1,0:T(8,128)(2,1)S(1)} %attend.2.refs_0_), channel_id=1, source_target_pairs={{0,8},{1,9},{2,10},{3,11},{4,12},{5,13},{6,14},{7,15},{8,0},{9,1},... | collective-permute-start | bytes 393224 | tf_op jit(solution)/shard_map/ppermute | solution.py:55
  56.6 8.4 %collective-permute-start.10 = (bf16[32,2048]{1,0:T(8,128)(2,1)S(1)}, bf16[32,2048]{1,0:T(8,128)(2,1)S(1)}, u32[]{:S(2)}, u32[]{:S(2)}) collective-permute-start(bf16[32,2048]{1,0:T(8,128)(2,1)S(1)} %attend.2.refs_0_), channel_id=1, source_target_pairs={{0,2},{1,5},{2,0},{3,7},{4,6},{5,1},{6,4},{7,3},{8,10},{9,13},{10,... | collective-permute-start | bytes 393224 | tf_op jit(solution)/shard_map/ppermute | solution.py:55
  57.7 8.5 %collective-permute-start.8 = (bf16[32,2048]{1,0:T(8,128)(2,1)S(1)}, bf16[32,2048]{1,0:T(8,128)(2,1)S(1)}, u32[]{:S(2)}, u32[]{:S(2)}) collective-permute-start(bf16[32,2048]{1,0:T(8,128)(2,1)S(1)} %attend.2.refs_0_), channel_id=1, source_target_pairs={{0,4},{1,3},{2,6},{3,1},{4,0},{5,7},{6,2},{7,5},{8,12},{9,11},{10,... | collective-permute-start | bytes 393224 | tf_op jit(solution)/shard_map/ppermute | solution.py:55
  62.0 6.6 %collective-permute-start.16 = (bf16[32,2048]{1,0:T(8,128)(2,1)S(1)}, bf16[32,2048]{1,0:T(8,128)(2,1)S(1)}, u32[]{:S(2)}, u32[]{:S(2)}) collective-permute-start(bf16[32,2048]{1,0:T(8,128)(2,1)S(1)} %collective-permute-done.14.refs_1_), channel_id=1, source_target_pairs={{0,4},{1,5},{2,6},{3,7},{4,0},{5,1},{6,2},{7,3},{8,12},{9,13},{10,... | collective-permute-start | bytes 393224 | tf_op jit(solution)/shard_map/ppermute | solution.py:55
  62.0 7.4 %collective-permute-start.19 = (bf16[32,2048]{1,0:T(8,128)(2,1)S(1)}, bf16[32,2048]{1,0:T(8,128)(2,1)S(1)}, u32[]{:S(2)}, u32[]{:S(2)}) collective-permute-start(bf16[32,2048]{1,0:T(8,128)(2,1)S(1)} %collective-permute-done.15.refs_2_), channel_id=1, source_target_pairs={{0,2},{1,3},{2,0},{3,1},{4,6},{5,7},{6,4},{7,5},{8,10},{9,11},{10,... | collective-permute-start | bytes 393224 | tf_op jit(solution)/shard_map/ppermute | solution.py:55
  65.0 6.3 %collective-permute-start.9 = (bf16[32,2048]{1,0:T(8,128)(2,1)S(1)}, bf16[32,2048]{1,0:T(8,128)(2,1)S(1)}, u32[]{:S(2)}, u32[]{:S(2)}) collective-permute-start(bf16[32,2048]{1,0:T(8,128)(2,1)S(1)} %collective-permute-done.7.refs_1_), channel_id=1, source_target_pairs={{0,4},{1,3},{2,6},{3,1},{4,0},{5,7},{6,2},{7,5},{8,12},{9,11},{10,... | collective-permute-start | bytes 393224 | tf_op jit(solution)/shard_map/ppermute | solution.py:55
  66.2 12.0 %collective-permute-start.12 = (bf16[32,2048]{1,0:T(8,128)(2,1)S(1)}, bf16[32,2048]{1,0:T(8,128)(2,1)S(1)}, u32[]{:S(2)}, u32[]{:S(2)}) collective-permute-start(bf16[32,2048]{1,0:T(8,128)(2,1)S(1)} %collective-permute-done.8.refs_2_), channel_id=1, source_target_pairs={{0,2},{1,5},{2,0},{3,7},{4,6},{5,1},{6,4},{7,3},{8,10},{9,13},{10,... | collective-permute-start | bytes 393224 | tf_op jit(solution)/shard_map/ppermute | solution.py:55
  67.0 7.4 %collective-permute-start.18 = (bf16[32,2048]{1,0:T(8,128)(2,1)S(1)}, bf16[32,2048]{1,0:T(8,128)(2,1)S(1)}, u32[]{:S(2)}, u32[]{:S(2)}) collective-permute-start(bf16[32,2048]{1,0:T(8,128)(2,1)S(1)} %collective-permute-done.14.refs_1_), channel_id=1, source_target_pairs={{0,2},{1,3},{2,0},{3,1},{4,6},{5,7},{6,4},{7,5},{8,10},{9,11},{10,... | collective-permute-start | bytes 393224 | tf_op jit(solution)/shard_map/ppermute | solution.py:55
  68.6 7.2 %collective-permute-start.20 = (bf16[32,2048]{1,0:T(8,128)(2,1)S(1)}, bf16[32,2048]{1,0:T(8,128)(2,1)S(1)}, u32[]{:S(2)}, u32[]{:S(2)}) collective-permute-start(bf16[32,2048]{1,0:T(8,128)(2,1)S(1)} %collective-permute-done.16.refs_3_), channel_id=1, source_target_pairs={{0,2},{1,3},{2,0},{3,1},{4,6},{5,7},{6,4},{7,5},{8,10},{9,11},{10,... | collective-permute-start | bytes 393224 | tf_op jit(solution)/shard_map/ppermute | solution.py:55
  69.4 8.8 %collective-permute-start.11 = (bf16[32,2048]{1,0:T(8,128)(2,1)S(1)}, bf16[32,2048]{1,0:T(8,128)(2,1)S(1)}, u32[]{:S(2)}, u32[]{:S(2)}) collective-permute-start(bf16[32,2048]{1,0:T(8,128)(2,1)S(1)} %collective-permute-done.7.refs_1_), channel_id=1, source_target_pairs={{0,2},{1,5},{2,0},{3,7},{4,6},{5,1},{6,4},{7,3},{8,10},{9,13},{10,... | collective-permute-start | bytes 393224 | tf_op jit(solution)/shard_map/ppermute | solution.py:55
  71.2 7.4 %collective-permute-start.13 = (bf16[32,2048]{1,0:T(8,128)(2,1)S(1)}, bf16[32,2048]{1,0:T(8,128)(2,1)S(1)}, u32[]{:S(2)}, u32[]{:S(2)}) collective-permute-start(bf16[32,2048]{1,0:T(8,128)(2,1)S(1)} %collective-permute-done.9.refs_3_), channel_id=1, source_target_pairs={{0,2},{1,5},{2,0},{3,7},{4,6},{5,1},{6,4},{7,3},{8,10},{9,13},{10,... | collective-permute-start | bytes 393224 | tf_op jit(solution)/shard_map/ppermute | solution.py:55
  81.1 2.0 %collective-permute-start.21 = (bf16[128,2048]{1,0:T(8,128)(2,1)S(1)}, bf16[128,2048]{1,0:T(8,128)(2,1)S(1)}, u32[]{:S(2)}, u32[]{:S(2)}) collective-permute-start(bf16[128,2048]{1,0:T(8,128)(2,1)S(1)} %get-tuple-element.62), channel_id=1, source_target_pairs={{0,1},{1,0},{2,3},{3,2},{4,5},{5,4},{6,7},{7,6},{8,9},{9,8},{10,11... | collective-permute-start | bytes 1572872 | tf_op jit(solution)/shard_map/ppermute | solution.py:521

commit v16 on v14

--- a/solution.py
+++ b/solution.py
@@ -30,7 +30,7 @@
 
 def gather_orders(n, chunk):
     first, second = bit_orders(n)
-    return (first, second) if chunk else (first, first)
+    return (second, first) if chunk else (first, first)
 
 
 def slot_shift(slot, order):

time: 79.3 us -> 81.8 us (1.032)
  waiting for transfers between devices: 16.9 us -> 18.7 us
    ppermute x21, waiting for transfers between devices: 15 us -> 16.8 us  [exchange(): return lax.ppermute(value, ('gx', 'gy'), pairs)]
  transfers between devices with their start and end apart: 22 -> 22, of which waited for: 12 -> 11; matrix products, arithmetic and copies ran while one was open for 2% -> 2% of each run, Pallas kernels for 32% -> 31%
where the time goes in v16:
time: 81.8 us; the launch traced here: 81.5 us
  Pallas kernels  32.2 us (39%)
  starting transfers between devices  27.7 us (34%)
  waiting for transfers between devices  18.7 us (23%)
  other arithmetic  2.58 us (3%)
    ppermute x21, starting transfers between devices, exchange(): return lax.ppermute(value, ('gx', 'gy'), pairs)  27.6 us
    ppermute x21, waiting for transfers between devices, exchange(): return lax.ppermute(value, ('gx', 'gy'), pairs)  16.8 us
    pallas_call x3, Pallas kernels, project(): pl.pallas_call(functools.partial(project_kernel, n, q_start, kv_start, fi...  13.6 us
    pallas_call x2, Pallas kernels, attend(): pl.pallas_call(functools.partial(attend_kernel, chunk, offsets, kv_offset...  6.77 us
    pallas_call x2, Pallas kernels, combine(): pl.pallas_call(functools.partial(combine_kernel, n, block, chunk), out_sh...  4.9 us
    pallas_call x1, Pallas kernels, fetch_rows(): pl.pallas_call(functools.partial(fetch_rows_kernel, start, pieces), out_s...  3.5 us
    pallas_call x1, Pallas kernels, fetch(): pl.pallas_call(functools.partial(fetch_kernel, len(arrays), pieces), out_...  3.47 us
    ppermute x1, waiting for transfers between devices, shards(): other = lax.ppermute(send, 'gy', [(0, 1), (1, 0)])  1.9 us
  transfers between devices with their start and end apart: 22, of which 11 were waited for; matrix products, arithmetic and copies ran while one was open for 2% of the time, Pallas kernels for 31%

profile of v16, /device:TPU:0, one launch (start us, length us, event | category | flops | bytes accessed | tf_op | source)
XLA Modules:
  0.0 81.5 jit_solution(9233571118514060416)
XLA Ops:
  0.0 4.4 %project.3 = (bf16[128,1152]{1,0:T(8,128)(2,1)S(1)}, f32[128,1152]{1,0:T(8,128)S(1)}, bf16[256,2048]{1,0:T(8,128)(2,1)S(1)}) custom-call(bf16[256,2048]{1,0:T(8,128)(2,1)} %refs_0_.1, f32[1,2048]{1,0:T(1,128)} %bitcast.1, bf16[2048,4096]{1,0:T(8,128)(2,1)} %refs_1_.3, bf16[2048,256]{1,0:T(8,128)(2,1)} %refs_2_.5, bf16[2048,256]{1,0:T(8,128)(2,1)} %refs_3_.5), custom_call_target="tpu_custom_call" | custom-call | tf_op jit(solution)/shard_map/project/pallas_call | solution.py:161
  4.4 3.0 %collective-permute-start = (bf16[128,1152]{1,0:T(8,128)(2,1)S(1)}, bf16[128,1152]{1,0:T(8,128)(2,1)S(1)}, u32[]{:S(2)}, u32[]{:S(2)}) collective-permute-start(bf16[128,1152]{1,0:T(8,128)(2,1)S(1)} %get-tuple-element.34), channel_id=1, source_target_pairs={{0,2},{1,5},{2,0},{3,7},{4,6},{5,1},{6,4},{7,3},{8,10},{9,13},{10,... | collective-permute-start | bytes 884744 | tf_op jit(solution)/shard_map/ppermute | solution.py:55
  7.4 3.9 %project.4 = (bf16[128,1280]{1,0:T(8,128)(2,1)S(1)}, f32[128,1280]{1,0:T(8,128)S(1)}) custom-call(bf16[256,2048]{1,0:T(8,128)(2,1)S(1)} %get-tuple-element.39.refs_0_, bf16[2048,4096]{1,0:T(8,128)(2,1)} %refs_1_.3, bf16[2048,256]{1,0:T(8,128)(2,1)} %refs_2_.5, bf16[2048,256]{1,0:T(8,128)(2,1)} %refs_3_.5), custom_call_target="tpu_custom_call" | custom-call | tf_op jit(solution)/shard_map/project/pallas_call | solution.py:161
  11.3 0.1 collective-permute-start.1
  11.4 0.7 collective-permute-done
  12.1 0.1 convert_add_fusion.2
  12.2 0.0 copy-start
  12.2 5.3 %project.5 = (bf16[128,2304]{1,0:T(8,128)(2,1)S(1)}, f32[128,2304]{1,0:T(8,128)S(1)}) custom-call(bf16[256,2048]{1,0:T(8,128)(2,1)S(1)} %get-tuple-element.39.refs_0_, bf16[2048,4096]{1,0:T(8,128)(2,1)} %refs_1_.3, bf16[2048,256]{1,0:T(8,128)(2,1)} %refs_2_.5, bf16[2048,256]{1,0:T(8,128)(2,1)} %refs_3_.5), custom_call_target="tpu_custom_call" | custom-call | tf_op jit(solution)/shard_map/project/pallas_call | solution.py:161
  17.5 0.9 %collective-permute-done.1 = bf16[128,1280]{1,0:T(8,128)(2,1)S(1)} collective-permute-done((bf16[128,1280]{1,0:T(8,128)(2,1)S(1)}, bf16[128,1280]{1,0:T(8,128)(2,1)S(1)}, u32[]{:S(2)}, u32[]{:S(2)}) %collective-permute-start.1) | collective-permute-done | bytes 327712 | tf_op jit(solution)/shard_map/ppermute | solution.py:55
  18.4 0.1 convert_add_fusion.1
  18.5 1.6 %collective-permute-start.3 = (bf16[64,2432]{1,0:T(8,128)(2,1)S(1)}, bf16[64,2432]{1,0:T(8,128)(2,1)}, u32[]{:S(2)}, u32[]{:S(2)}) collective-permute-start(bf16[64,2432]{1,0:T(8,128)(2,1)S(1)} %fusion.1), channel_id=1, source_target_pairs={{0,4},{1,3},{2,6},{3,1},{4,0},{5,7},{6,2},{7,5},{8,12},{9,11},{10,... | collective-permute-start | bytes 933896 | tf_op jit(solution)/shard_map/ppermute | solution.py:55
  20.2 0.1 add_convert_fusion.1
  20.3 0.1 convert_element_type.49
  20.4 1.2 %collective-permute-start.2 = (bf16[128,2304]{1,0:T(8,128)(2,1)S(1)}, bf16[128,2304]{1,0:T(8,128)(2,1)S(1)}, u32[]{:S(2)}, u32[]{:S(2)}) collective-permute-start(bf16[128,2304]{1,0:T(8,128)(2,1)S(1)} %get-tuple-element.44), channel_id=1, source_target_pairs={{0,2},{1,5},{2,0},{3,7},{4,6},{5,1},{6,4},{7,3},{8,10},{9,13},{10,... | collective-permute-start | bytes 1769480 | tf_op jit(solution)/shard_map/ppermute | solution.py:55
  21.5 3.5 %fetch_rows.1.refs_8_ = bf16[2048,2048]{1,0:T(8,128)(2,1)S(1)} custom-call(bf16[4096,2048]{1,0:T(8,128)(2,1)} %refs_6_.1), custom_call_target="tpu_custom_call" | custom-call | tf_op jit(solution)/shard_map/fetch_rows/pallas_call | solution.py:343
  25.0 5.6 %collective-permute-done.3 = bf16[64,2432]{1,0:T(8,128)(2,1)} collective-permute-done((bf16[64,2432]{1,0:T(8,128)(2,1)S(1)}, bf16[64,2432]{1,0:T(8,128)(2,1)}, u32[]{:S(2)}, u32[]{:S(2)}) %collective-permute-start.3) | collective-permute-done | bytes 311328 | tf_op jit(solution)/shard_map/ppermute | solution.py:55
  30.6 1.0 %fusion.2 = f32[64,2432]{1,0:T(8,128)S(1)} fusion(f32[128,1280]{1,0:T(8,128)S(1)} %convert_add_fusion.1, f32[128,1152]{1,0:T(8,128)S(1)} %convert_add_fusion.2, bf16[64,2432]{1,0:T(8,128)(2,1)} %collective-permute-done.3), kind=kLoop, calls=%fused_computation.8 | loop fusion | flops 466944 | bytes 2179072 | tf_op jit(solution)/shard_map/add | solution.py:461
  31.7 1.5 %collective-permute-start.5 = (bf16[32,2432]{1,0:T(8,128)(2,1)S(1)}, bf16[32,2432]{1,0:T(8,128)(2,1)S(1)}, u32[]{:S(2)}, u32[]{:S(2)}) collective-permute-start(bf16[32,2432]{1,0:T(8,128)(2,1)S(1)} %slice.64), channel_id=1, source_target_pairs={{0,8},{1,9},{2,10},{3,11},{4,12},{5,13},{6,14},{7,15},{8,0},{9,1},... | collective-permute-start | bytes 466952 | tf_op jit(solution)/shard_map/ppermute | solution.py:55
  33.2 0.0 collective-permute-done.2
  33.2 0.1 convert_add_fusion
  33.3 2.8 %collective-permute-start.4 = (bf16[64,2304]{1,0:T(8,128)(2,1)S(1)}, bf16[64,2304]{1,0:T(8,128)(2,1)S(1)}, u32[]{:S(2)}, u32[]{:S(2)}) collective-permute-start(bf16[64,2304]{1,0:T(8,128)(2,1)S(1)} %slice.63), channel_id=1, source_target_pairs={{0,4},{1,3},{2,6},{3,1},{4,0},{5,7},{6,2},{7,5},{8,12},{9,11},{10,... | collective-permute-start | bytes 884744 | tf_op jit(solution)/shard_map/ppermute | solution.py:55
  36.1 3.5 %fetch.1 = (bf16[8,1024,256]{2,1,0:T(8,128)(2,1)S(1)}, bf16[8,1024,256]{2,1,0:T(8,128)(2,1)S(1)}) custom-call(bf16[8,1024,256]{2,1,0:T(8,128)(2,1)} %refs_0_.2, bf16[8,1024,256]{2,1,0:T(8,128)(2,1)} %refs_1_.4), custom_call_target="tpu_custom_call" | custom-call | tf_op jit(solution)/shard_map/fetch/pallas_call | solution.py:314
  39.6 0.0 collective-permute-done.5
  39.7 2.0 %collective-permute-done.4 = bf16[64,2304]{1,0:T(8,128)(2,1)S(1)} collective-permute-done((bf16[64,2304]{1,0:T(8,128)(2,1)S(1)}, bf16[64,2304]{1,0:T(8,128)(2,1)S(1)}, u32[]{:S(2)}, u32[]{:S(2)}) %collective-permute-start.4) | collective-permute-done | bytes 294944 | tf_op jit(solution)/shard_map/ppermute | solution.py:55
  41.7 0.1 slice_add_fusion
  41.8 0.7 collective-permute-start.6
  42.5 0.1 fusion.3
  42.6 0.1 pad_maximum_fusion.1
  42.7 4.0 %attend.3 = (bf16[32,2048]{1,0:T(8,128)(2,1)S(1)}, bf16[2048,2048]{1,0:T(8,128)(2,1)S(1)}) custom-call(s32[8]{0:T(128)S(1)} %copy-done, f32[32,2432]{1,0:T(8,128)S(1)} %slice_add_fusion.1.refs_0_, f32[32,128]{1,0:T(8,128)S(1)} %slice.48.refs_1_, f32[32,128]{1,0:T(8,128)S(1)} %get-tuple-element.64.refs_2_, f32[32,128]{1,0:T(8,128)S(1)} %get-tuple-element.65.refs_3_, ...), custom_call_target="tpu_custom_call" | custom-call | tf_op jit(solution)/shard_map/attend/pallas_call | solution.py:281
  46.7 0.5 collective-permute-start.17
  47.2 1.9 %collective-permute-start.15 = (bf16[32,2048]{1,0:T(8,128)(2,1)S(1)}, bf16[32,2048]{1,0:T(8,128)(2,1)S(1)}, u32[]{:S(2)}, u32[]{:S(2)}) collective-permute-start(bf16[32,2048]{1,0:T(8,128)(2,1)S(1)} %get-tuple-element.56.refs_0_), channel_id=1, source_target_pairs={{0,4},{1,5},{2,6},{3,7},{4,0},{5,1},{6,2},{7,3},{8,12},{9,13},{10,... | collective-permute-start | bytes 393224 | tf_op jit(solution)/shard_map/ppermute | solution.py:55
  49.1 0.5 collective-permute-done.6
  49.6 0.8 %collective-permute-start.14 = (bf16[32,2048]{1,0:T(8,128)(2,1)S(1)}, bf16[32,2048]{1,0:T(8,128)(2,1)S(1)}, u32[]{:S(2)}, u32[]{:S(2)}) collective-permute-start(bf16[32,2048]{1,0:T(8,128)(2,1)S(1)} %get-tuple-element.56.refs_0_), channel_id=1, source_target_pairs={{0,8},{1,9},{2,10},{3,11},{4,12},{5,13},{6,14},{7,15},{8,0},{9,1},... | collective-permute-start | bytes 393224 | tf_op jit(solution)/shard_map/ppermute | solution.py:55
  50.4 2.7 %attend.2.refs_0_ = bf16[32,2048]{1,0:T(8,128)(2,1)S(1)} custom-call(s32[8]{0:T(128)S(1)} %copy-done, f32[32,2304]{1,0:T(8,128)S(1)} %slice_add_fusion.2.refs_0_, f32[32,128]{1,0:T(8,128)S(1)} %slice.48.refs_1_, f32[32,128]{1,0:T(8,128)S(1)} %get-tuple-element.64.refs_2_, f32[32,128]{1,0:T(8,128)S(1)} %get-tuple-element.65.refs_3_, ...), custom_call_target="tpu_custom_call" | custom-call | tf_op jit(solution)/shard_map/attend/pallas_call | solution.py:281
  53.2 2.2 %collective-permute-start.7 = (bf16[32,2048]{1,0:T(8,128)(2,1)S(1)}, bf16[32,2048]{1,0:T(8,128)(2,1)S(1)}, u32[]{:S(2)}, u32[]{:S(2)}) collective-permute-start(bf16[32,2048]{1,0:T(8,128)(2,1)S(1)} %attend.2.refs_0_), channel_id=1, source_target_pairs={{0,8},{1,9},{2,10},{3,11},{4,12},{5,13},{6,14},{7,15},{8,0},{9,1},... | collective-permute-start | bytes 393224 | tf_op jit(solution)/shard_map/ppermute | solution.py:55
  55.4 0.0 collective-permute-start.10
  55.4 0.0 collective-permute-done.17.refs_4_
  55.4 1.5 %collective-permute-start.8 = (bf16[32,2048]{1,0:T(8,128)(2,1)S(1)}, bf16[32,2048]{1,0:T(8,128)(2,1)S(1)}, u32[]{:S(2)}, u32[]{:S(2)}) collective-permute-start(bf16[32,2048]{1,0:T(8,128)(2,1)S(1)} %attend.2.refs_0_), channel_id=1, source_target_pairs={{0,2},{1,5},{2,0},{3,7},{4,6},{5,1},{6,4},{7,3},{8,10},{9,13},{10,... | collective-permute-start | bytes 393224 | tf_op jit(solution)/shard_map/ppermute | solution.py:55
  56.9 0.0 collective-permute-done.15.refs_2_
  56.9 1.9 %collective-permute-done.14.refs_1_ = bf16[32,2048]{1,0:T(8,128)(2,1)S(1)} collective-permute-done((bf16[32,2048]{1,0:T(8,128)(2,1)S(1)}, bf16[32,2048]{1,0:T(8,128)(2,1)S(1)}, u32[]{:S(2)}, u32[]{:S(2)}) %collective-permute-start.14) | collective-permute-done | bytes 131104 | tf_op jit(solution)/shard_map/ppermute | solution.py:55
  58.7 0.2 collective-permute-start.16
  58.9 1.8 %collective-permute-start.19 = (bf16[32,2048]{1,0:T(8,128)(2,1)S(1)}, bf16[32,2048]{1,0:T(8,128)(2,1)S(1)}, u32[]{:S(2)}, u32[]{:S(2)}) collective-permute-start(bf16[32,2048]{1,0:T(8,128)(2,1)S(1)} %collective-permute-done.15.refs_2_), channel_id=1, source_target_pairs={{0,2},{1,3},{2,0},{3,1},{4,6},{5,7},{6,4},{7,5},{8,10},{9,11},{10,... | collective-permute-start | bytes 393224 | tf_op jit(solution)/shard_map/ppermute | solution.py:55
  60.7 0.7 collective-permute-done.7.refs_1_
  61.4 1.8 %collective-permute-start.9 = (bf16[32,2048]{1,0:T(8,128)(2,1)S(1)}, bf16[32,2048]{1,0:T(8,128)(2,1)S(1)}, u32[]{:S(2)}, u32[]{:S(2)}) collective-permute-start(bf16[32,2048]{1,0:T(8,128)(2,1)S(1)} %collective-permute-done.7.refs_1_), channel_id=1, source_target_pairs={{0,2},{1,5},{2,0},{3,7},{4,6},{5,1},{6,4},{7,3},{8,10},{9,13},{10,... | collective-permute-start | bytes 393224 | tf_op jit(solution)/shard_map/ppermute | solution.py:55
  63.2 0.0 collective-permute-done.10.refs_4_
  63.2 0.0 collective-permute-done.8.refs_2_
  63.2 0.1 collective-permute-start.12
  63.3 2.6 %collective-permute-start.18 = (bf16[32,2048]{1,0:T(8,128)(2,1)S(1)}, bf16[32,2048]{1,0:T(8,128)(2,1)S(1)}, u32[]{:S(2)}, u32[]{:S(2)}) collective-permute-start(bf16[32,2048]{1,0:T(8,128)(2,1)S(1)} %collective-permute-done.14.refs_1_), channel_id=1, source_target_pairs={{0,2},{1,3},{2,0},{3,1},{4,6},{5,7},{6,4},{7,5},{8,10},{9,11},{10,... | collective-permute-start | bytes 393224 | tf_op jit(solution)/shard_map/ppermute | solution.py:55
  65.9 0.0 collective-permute-done.16.refs_3_
  65.9 0.7 collective-permute-start.20
  66.6 0.0 collective-permute-done.19.refs_6_
  66.6 0.7 collective-permute-start.11
  67.3 0.7 collective-permute-done.9.refs_3_
  68.0 2.0 %collective-permute-start.13 = (bf16[32,2048]{1,0:T(8,128)(2,1)S(1)}, bf16[32,2048]{1,0:T(8,128)(2,1)S(1)}, u32[]{:S(2)}, u32[]{:S(2)}) collective-permute-start(bf16[32,2048]{1,0:T(8,128)(2,1)S(1)} %collective-permute-done.9.refs_3_), channel_id=1, source_target_pairs={{0,4},{1,3},{2,6},{3,1},{4,0},{5,7},{6,2},{7,5},{8,12},{9,11},{10,... | collective-permute-start | bytes 393224 | tf_op jit(solution)/shard_map/ppermute | solution.py:55
  70.0 0.8 %collective-permute-done.18.refs_5_ = bf16[32,2048]{1,0:T(8,128)(2,1)S(1)} collective-permute-done((bf16[32,2048]{1,0:T(8,128)(2,1)S(1)}, bf16[32,2048]{1,0:T(8,128)(2,1)S(1)}, u32[]{:S(2)}, u32[]{:S(2)}) %collective-permute-start.18) | collective-permute-done | bytes 131104 | tf_op jit(solution)/shard_map/ppermute | solution.py:55
  70.9 2.8 %collective-permute-done.20.refs_7_ = bf16[32,2048]{1,0:T(8,128)(2,1)S(1)} collective-permute-done((bf16[32,2048]{1,0:T(8,128)(2,1)S(1)}, bf16[32,2048]{1,0:T(8,128)(2,1)S(1)}, u32[]{:S(2)}, u32[]{:S(2)}) %collective-permute-start.20) | collective-permute-done | bytes 131104 | tf_op jit(solution)/shard_map/ppermute | solution.py:55
  73.7 2.4 %combine.2.refs_8_ = f32[256,2048]{1,0:T(8,128)S(1)} custom-call(bf16[32,2048]{1,0:T(8,128)(2,1)S(1)} %get-tuple-element.56.refs_0_, bf16[32,2048]{1,0:T(8,128)(2,1)S(1)} %collective-permute-done.14.refs_1_, bf16[32,2048]{1,0:T(8,128)(2,1)S(1)} %collective-permute-done.15.refs_2_, bf16[32,2048]{1,0:T(8,128)(2,1)S(1)} %collective-permute-done.16.refs_3_, ...), custom_call_target="tpu_custom_call" | custom-call | tf_op jit(solution)/shard_map/combine/pallas_call | solution.py:395
  76.1 0.0 collective-permute-done.12.refs_6_
  76.1 0.0 collective-permute-done.11.refs_5_
  76.1 0.0 collective-permute-done.13.refs_7_
  76.1 2.5 %combine.3 = (bf16[128,2048]{1,0:T(8,128)(2,1)S(1)}, f32[128,2048]{1,0:T(8,128)S(1)}) custom-call(bf16[32,2048]{1,0:T(8,128)(2,1)S(1)} %attend.2.refs_0_, bf16[32,2048]{1,0:T(8,128)(2,1)S(1)} %collective-permute-done.7.refs_1_, bf16[32,2048]{1,0:T(8,128)(2,1)S(1)} %collective-permute-done.8.refs_2_, bf16[32,2048]{1,0:T(8,128)(2,1)S(1)} %collective-permute-done.9.refs_3_, ...), custom_call_target="tpu_custom_call" | custom-call | tf_op jit(solution)/shard_map/combine/pallas_call | solution.py:395
  78.6 0.1 collective-permute-start.21
  78.7 1.9 %collective-permute-done.21 = bf16[128,2048]{1,0:T(8,128)(2,1)S(1)} collective-permute-done((bf16[128,2048]{1,0:T(8,128)(2,1)S(1)}, bf16[128,2048]{1,0:T(8,128)(2,1)S(1)}, u32[]{:S(2)}, u32[]{:S(2)}) %collective-permute-start.21) | collective-permute-done | bytes 524320 | tf_op jit(solution)/shard_map/ppermute | solution.py:520
  80.6 0.9 %add_convert_fusion = bf16[128,2048]{1,0:T(8,128)(2,1)} fusion(f32[128,2048]{1,0:T(8,128)S(1)} %get-tuple-element.59, bf16[128,2048]{1,0:T(8,128)(2,1)S(1)} %collective-permute-done.21), kind=kLoop, calls=%fused_computation.3 | loop fusion | flops 786432 | bytes 2097152 | tf_op jit(solution)/shard_map/convert_element_type | solution.py:521
  (9 shorter events, 0.2 us)
Async XLA Ops:
  4.4 7.7 %collective-permute-start = (bf16[128,1152]{1,0:T(8,128)(2,1)S(1)}, bf16[128,1152]{1,0:T(8,128)(2,1)S(1)}, u32[]{:S(2)}, u32[]{:S(2)}) collective-permute-start(bf16[128,1152]{1,0:T(8,128)(2,1)S(1)} %get-tuple-element.34), channel_id=1, source_target_pairs={{0,2},{1,5},{2,0},{3,7},{4,6},{5,1},{6,4},{7,3},{8,10},{9,13},{10,... | collective-permute-start | bytes 884744 | tf_op jit(solution)/shard_map/ppermute | solution.py:55
  11.3 7.1 %collective-permute-start.1 = (bf16[128,1280]{1,0:T(8,128)(2,1)S(1)}, bf16[128,1280]{1,0:T(8,128)(2,1)S(1)}, u32[]{:S(2)}, u32[]{:S(2)}) collective-permute-start(bf16[128,1280]{1,0:T(8,128)(2,1)S(1)} %get-tuple-element.36), channel_id=1, source_target_pairs={{0,2},{1,5},{2,0},{3,7},{4,6},{5,1},{6,4},{7,3},{8,10},{9,13},{10,... | collective-permute-start | bytes 983048 | tf_op jit(solution)/shard_map/ppermute | solution.py:55
  12.2 8.0 %copy-start = (s32[8]{0:T(128)S(1)}, s32[8]{0:T(128)}, u32[]{:S(2)}) copy-start(s32[8]{0:T(128)} %length_ref.3) | copy-start | bytes 100
  18.5 12.1 %collective-permute-start.3 = (bf16[64,2432]{1,0:T(8,128)(2,1)S(1)}, bf16[64,2432]{1,0:T(8,128)(2,1)}, u32[]{:S(2)}, u32[]{:S(2)}) collective-permute-start(bf16[64,2432]{1,0:T(8,128)(2,1)S(1)} %fusion.1), channel_id=1, source_target_pairs={{0,4},{1,3},{2,6},{3,1},{4,0},{5,7},{6,2},{7,5},{8,12},{9,11},{10,... | collective-permute-start | bytes 933896 | tf_op jit(solution)/shard_map/ppermute | solution.py:55
  20.4 12.8 %collective-permute-start.2 = (bf16[128,2304]{1,0:T(8,128)(2,1)S(1)}, bf16[128,2304]{1,0:T(8,128)(2,1)S(1)}, u32[]{:S(2)}, u32[]{:S(2)}) collective-permute-start(bf16[128,2304]{1,0:T(8,128)(2,1)S(1)} %get-tuple-element.44), channel_id=1, source_target_pairs={{0,2},{1,5},{2,0},{3,7},{4,6},{5,1},{6,4},{7,3},{8,10},{9,13},{10,... | collective-permute-start | bytes 1769480 | tf_op jit(solution)/shard_map/ppermute | solution.py:55
  31.7 8.0 %collective-permute-start.5 = (bf16[32,2432]{1,0:T(8,128)(2,1)S(1)}, bf16[32,2432]{1,0:T(8,128)(2,1)S(1)}, u32[]{:S(2)}, u32[]{:S(2)}) collective-permute-start(bf16[32,2432]{1,0:T(8,128)(2,1)S(1)} %slice.64), channel_id=1, source_target_pairs={{0,8},{1,9},{2,10},{3,11},{4,12},{5,13},{6,14},{7,15},{8,0},{9,1},... | collective-permute-start | bytes 466952 | tf_op jit(solution)/shard_map/ppermute | solution.py:55
  33.3 8.4 %collective-permute-start.4 = (bf16[64,2304]{1,0:T(8,128)(2,1)S(1)}, bf16[64,2304]{1,0:T(8,128)(2,1)S(1)}, u32[]{:S(2)}, u32[]{:S(2)}) collective-permute-start(bf16[64,2304]{1,0:T(8,128)(2,1)S(1)} %slice.63), channel_id=1, source_target_pairs={{0,4},{1,3},{2,6},{3,1},{4,0},{5,7},{6,2},{7,5},{8,12},{9,11},{10,... | collective-permute-start | bytes 884744 | tf_op jit(solution)/shard_map/ppermute | solution.py:55
  41.8 7.8 %collective-permute-start.6 = (bf16[32,2304]{1,0:T(8,128)(2,1)S(1)}, bf16[32,2304]{1,0:T(8,128)(2,1)S(1)}, u32[]{:S(2)}, u32[]{:S(2)}) collective-permute-start(bf16[32,2304]{1,0:T(8,128)(2,1)S(1)} %slice.65), channel_id=1, source_target_pairs={{0,8},{1,9},{2,10},{3,11},{4,12},{5,13},{6,14},{7,15},{8,0},{9,1},... | collective-permute-start | bytes 442376 | tf_op jit(solution)/shard_map/ppermute | solution.py:55
  46.7 8.6 %collective-permute-start.17 = (bf16[32,2048]{1,0:T(8,128)(2,1)S(1)}, bf16[32,2048]{1,0:T(8,128)(2,1)S(1)}, u32[]{:S(2)}, u32[]{:S(2)}) collective-permute-start(bf16[32,2048]{1,0:T(8,128)(2,1)S(1)} %get-tuple-element.56.refs_0_), channel_id=1, source_target_pairs={{0,2},{1,3},{2,0},{3,1},{4,6},{5,7},{6,4},{7,5},{8,10},{9,11},{10,... | collective-permute-start | bytes 393224 | tf_op jit(solution)/shard_map/ppermute | solution.py:55
  47.2 9.6 %collective-permute-start.15 = (bf16[32,2048]{1,0:T(8,128)(2,1)S(1)}, bf16[32,2048]{1,0:T(8,128)(2,1)S(1)}, u32[]{:S(2)}, u32[]{:S(2)}) collective-permute-start(bf16[32,2048]{1,0:T(8,128)(2,1)S(1)} %get-tuple-element.56.refs_0_), channel_id=1, source_target_pairs={{0,4},{1,5},{2,6},{3,7},{4,0},{5,1},{6,2},{7,3},{8,12},{9,13},{10,... | collective-permute-start | bytes 393224 | tf_op jit(solution)/shard_map/ppermute | solution.py:55
  49.6 9.1 %collective-permute-start.14 = (bf16[32,2048]{1,0:T(8,128)(2,1)S(1)}, bf16[32,2048]{1,0:T(8,128)(2,1)S(1)}, u32[]{:S(2)}, u32[]{:S(2)}) collective-permute-start(bf16[32,2048]{1,0:T(8,128)(2,1)S(1)} %get-tuple-element.56.refs_0_), channel_id=1, source_target_pairs={{0,8},{1,9},{2,10},{3,11},{4,12},{5,13},{6,14},{7,15},{8,0},{9,1},... | collective-permute-start | bytes 393224 | tf_op jit(solution)/shard_map/ppermute | solution.py:55
  53.2 8.2 %collective-permute-start.7 = (bf16[32,2048]{1,0:T(8,128)(2,1)S(1)}, bf16[32,2048]{1,0:T(8,128)(2,1)S(1)}, u32[]{:S(2)}, u32[]{:S(2)}) collective-permute-start(bf16[32,2048]{1,0:T(8,128)(2,1)S(1)} %attend.2.refs_0_), channel_id=1, source_target_pairs={{0,8},{1,9},{2,10},{3,11},{4,12},{5,13},{6,14},{7,15},{8,0},{9,1},... | collective-permute-start | bytes 393224 | tf_op jit(solution)/shard_map/ppermute | solution.py:55
  55.4 7.8 %collective-permute-start.10 = (bf16[32,2048]{1,0:T(8,128)(2,1)S(1)}, bf16[32,2048]{1,0:T(8,128)(2,1)S(1)}, u32[]{:S(2)}, u32[]{:S(2)}) collective-permute-start(bf16[32,2048]{1,0:T(8,128)(2,1)S(1)} %attend.2.refs_0_), channel_id=1, source_target_pairs={{0,4},{1,3},{2,6},{3,1},{4,0},{5,7},{6,2},{7,5},{8,12},{9,11},{10,... | collective-permute-start | bytes 393224 | tf_op jit(solution)/shard_map/ppermute | solution.py:55
  55.4 7.8 %collective-permute-start.8 = (bf16[32,2048]{1,0:T(8,128)(2,1)S(1)}, bf16[32,2048]{1,0:T(8,128)(2,1)S(1)}, u32[]{:S(2)}, u32[]{:S(2)}) collective-permute-start(bf16[32,2048]{1,0:T(8,128)(2,1)S(1)} %attend.2.refs_0_), channel_id=1, source_target_pairs={{0,2},{1,5},{2,0},{3,7},{4,6},{5,1},{6,4},{7,3},{8,10},{9,13},{10,... | collective-permute-start | bytes 393224 | tf_op jit(solution)/shard_map/ppermute | solution.py:55
  58.7 7.2 %collective-permute-start.16 = (bf16[32,2048]{1,0:T(8,128)(2,1)S(1)}, bf16[32,2048]{1,0:T(8,128)(2,1)S(1)}, u32[]{:S(2)}, u32[]{:S(2)}) collective-permute-start(bf16[32,2048]{1,0:T(8,128)(2,1)S(1)} %collective-permute-done.14.refs_1_), channel_id=1, source_target_pairs={{0,4},{1,5},{2,6},{3,7},{4,0},{5,1},{6,2},{7,3},{8,12},{9,13},{10,... | collective-permute-start | bytes 393224 | tf_op jit(solution)/shard_map/ppermute | solution.py:55
  58.9 7.7 %collective-permute-start.19 = (bf16[32,2048]{1,0:T(8,128)(2,1)S(1)}, bf16[32,2048]{1,0:T(8,128)(2,1)S(1)}, u32[]{:S(2)}, u32[]{:S(2)}) collective-permute-start(bf16[32,2048]{1,0:T(8,128)(2,1)S(1)} %collective-permute-done.15.refs_2_), channel_id=1, source_target_pairs={{0,2},{1,3},{2,0},{3,1},{4,6},{5,7},{6,4},{7,5},{8,10},{9,11},{10,... | collective-permute-start | bytes 393224 | tf_op jit(solution)/shard_map/ppermute | solution.py:55
  61.4 6.7 %collective-permute-start.9 = (bf16[32,2048]{1,0:T(8,128)(2,1)S(1)}, bf16[32,2048]{1,0:T(8,128)(2,1)S(1)}, u32[]{:S(2)}, u32[]{:S(2)}) collective-permute-start(bf16[32,2048]{1,0:T(8,128)(2,1)S(1)} %collective-permute-done.7.refs_1_), channel_id=1, source_target_pairs={{0,2},{1,5},{2,0},{3,7},{4,6},{5,1},{6,4},{7,3},{8,10},{9,13},{10,... | collective-permute-start | bytes 393224 | tf_op jit(solution)/shard_map/ppermute | solution.py:55
  63.2 12.9 %collective-permute-start.12 = (bf16[32,2048]{1,0:T(8,128)(2,1)S(1)}, bf16[32,2048]{1,0:T(8,128)(2,1)S(1)}, u32[]{:S(2)}, u32[]{:S(2)}) collective-permute-start(bf16[32,2048]{1,0:T(8,128)(2,1)S(1)} %collective-permute-done.8.refs_2_), channel_id=1, source_target_pairs={{0,4},{1,3},{2,6},{3,1},{4,0},{5,7},{6,2},{7,5},{8,12},{9,11},{10,... | collective-permute-start | bytes 393224 | tf_op jit(solution)/shard_map/ppermute | solution.py:55
  63.3 7.6 %collective-permute-start.18 = (bf16[32,2048]{1,0:T(8,128)(2,1)S(1)}, bf16[32,2048]{1,0:T(8,128)(2,1)S(1)}, u32[]{:S(2)}, u32[]{:S(2)}) collective-permute-start(bf16[32,2048]{1,0:T(8,128)(2,1)S(1)} %collective-permute-done.14.refs_1_), channel_id=1, source_target_pairs={{0,2},{1,3},{2,0},{3,1},{4,6},{5,7},{6,4},{7,5},{8,10},{9,11},{10,... | collective-permute-start | bytes 393224 | tf_op jit(solution)/shard_map/ppermute | solution.py:55
  65.9 7.8 %collective-permute-start.20 = (bf16[32,2048]{1,0:T(8,128)(2,1)S(1)}, bf16[32,2048]{1,0:T(8,128)(2,1)S(1)}, u32[]{:S(2)}, u32[]{:S(2)}) collective-permute-start(bf16[32,2048]{1,0:T(8,128)(2,1)S(1)} %collective-permute-done.16.refs_3_), channel_id=1, source_target_pairs={{0,2},{1,3},{2,0},{3,1},{4,6},{5,7},{6,4},{7,5},{8,10},{9,11},{10,... | collective-permute-start | bytes 393224 | tf_op jit(solution)/shard_map/ppermute | solution.py:55
  66.6 9.5 %collective-permute-start.11 = (bf16[32,2048]{1,0:T(8,128)(2,1)S(1)}, bf16[32,2048]{1,0:T(8,128)(2,1)S(1)}, u32[]{:S(2)}, u32[]{:S(2)}) collective-permute-start(bf16[32,2048]{1,0:T(8,128)(2,1)S(1)} %collective-permute-done.7.refs_1_), channel_id=1, source_target_pairs={{0,4},{1,3},{2,6},{3,1},{4,0},{5,7},{6,2},{7,5},{8,12},{9,11},{10,... | collective-permute-start | bytes 393224 | tf_op jit(solution)/shard_map/ppermute | solution.py:55
  68.0 8.1 %collective-permute-start.13 = (bf16[32,2048]{1,0:T(8,128)(2,1)S(1)}, bf16[32,2048]{1,0:T(8,128)(2,1)S(1)}, u32[]{:S(2)}, u32[]{:S(2)}) collective-permute-start(bf16[32,2048]{1,0:T(8,128)(2,1)S(1)} %collective-permute-done.9.refs_3_), channel_id=1, source_target_pairs={{0,4},{1,3},{2,6},{3,1},{4,0},{5,7},{6,2},{7,5},{8,12},{9,11},{10,... | collective-permute-start | bytes 393224 | tf_op jit(solution)/shard_map/ppermute | solution.py:55
  78.6 2.0 %collective-permute-start.21 = (bf16[128,2048]{1,0:T(8,128)(2,1)S(1)}, bf16[128,2048]{1,0:T(8,128)(2,1)S(1)}, u32[]{:S(2)}, u32[]{:S(2)}) collective-permute-start(bf16[128,2048]{1,0:T(8,128)(2,1)S(1)} %get-tuple-element.60), channel_id=1, source_target_pairs={{0,1},{1,0},{2,3},{3,2},{4,5},{5,4},{6,7},{7,6},{8,9},{9,8},{10,11... | collective-permute-start | bytes 1572872 | tf_op jit(solution)/shard_map/ppermute | solution.py:520

commit v17 on v16

--- a/solution.py
+++ b/solution.py
@@ -30,7 +30,7 @@
 
 def gather_orders(n, chunk):
     first, second = bit_orders(n)
-    return (second, first) if chunk else (first, first)
+    return (first, first) if chunk else (first, second)
 
 
 def slot_shift(slot, order):
@@ -68,7 +68,7 @@
     kv = wk_ref.shape[1] // CHUNKS if with_kv else 0
     width = w_buf.shape[1]
     cols = width - 2 * kv
-    pieces = 4 if cols > 1024 else 2
+    pieces = 1 if first else 4 if cols > 1024 else 2
     tile = cols // pieces
 
     def w_copy(ref, start, size, at, sem):
@@ -197,7 +197,7 @@
     new_cols = lax.broadcasted_iota(jnp.int32, (many, rows), 1)
     new_rows = lax.broadcasted_iota(jnp.int32, (many, rows), 0) % NEW
 
-    @pl.loop(0, seq_count // seqs)
+    @pl.loop(0, seq_count // seqs, unroll=True)
     def _(step):
         mine = pl.ds(pl.multiple_of(step * rows, rows), rows)
         mean = jnp.sum(square_ref[mine, :], axis=1, keepdims=True) / D

time: 81.8 us -> 81.5 us (level)
  starting transfers between devices: 27.7 us -> 26.2 us
  waiting for transfers between devices: 18.7 us -> 19.8 us
    ppermute x21, starting transfers between devices: 27.6 us -> 26.1 us  [exchange(): return lax.ppermute(value, ('gx', 'gy'), pairs)]
    ppermute x21, waiting for transfers between devices: 16.8 us -> 17.9 us  [exchange(): return lax.ppermute(value, ('gx', 'gy'), pairs)]
  transfers between devices with their start and end apart: 22 -> 22, of which waited for: 11 -> 13; matrix products, arithmetic and copies ran while one was open for 2% -> 2% of each run, Pallas kernels for 31% -> 32%
where the time goes in v17:
time: 81.5 us; the launch traced here: 81.3 us
  Pallas kernels  32.4 us (40%)
  starting transfers between devices  26.2 us (32%)
  waiting for transfers between devices  19.8 us (24%)
  other arithmetic  2.58 us (3%)
    ppermute x21, starting transfers between devices, exchange(): return lax.ppermute(value, ('gx', 'gy'), pairs)  26.1 us
    ppermute x21, waiting for transfers between devices, exchange(): return lax.ppermute(value, ('gx', 'gy'), pairs)  17.9 us
    pallas_call x3, Pallas kernels, project(): pl.pallas_call(functools.partial(project_kernel, n, q_start, kv_start, fi...  13.2 us
    pallas_call x2, Pallas kernels, attend(): pl.pallas_call(functools.partial(attend_kernel, chunk, offsets, kv_offset...  7.32 us
    pallas_call x2, Pallas kernels, combine(): pl.pallas_call(functools.partial(combine_kernel, n, block, chunk), out_sh...  4.89 us
    pallas_call x1, Pallas kernels, fetch_rows(): pl.pallas_call(functools.partial(fetch_rows_kernel, start, pieces), out_s...  3.5 us
    pallas_call x1, Pallas kernels, fetch(): pl.pallas_call(functools.partial(fetch_kernel, len(arrays), pieces), out_...  3.47 us
    ppermute x1, waiting for transfers between devices, shards(): other = lax.ppermute(send, 'gy', [(0, 1), (1, 0)])  1.9 us
  transfers between devices with their start and end apart: 22, of which 13 were waited for; matrix products, arithmetic and copies ran while one was open for 2% of the time, Pallas kernels for 32%

profile of v17, /device:TPU:0, one launch (start us, length us, event | category | flops | bytes accessed | tf_op | source)
XLA Modules:
  0.0 81.3 jit_solution(16448088310507194053)
XLA Ops:
  0.0 4.0 %project.3 = (bf16[128,1152]{1,0:T(8,128)(2,1)S(1)}, f32[128,1152]{1,0:T(8,128)S(1)}, bf16[256,2048]{1,0:T(8,128)(2,1)S(1)}) custom-call(bf16[256,2048]{1,0:T(8,128)(2,1)} %refs_0_.1, f32[1,2048]{1,0:T(1,128)} %bitcast.1, bf16[2048,4096]{1,0:T(8,128)(2,1)} %refs_1_.3, bf16[2048,256]{1,0:T(8,128)(2,1)} %refs_2_.5, bf16[2048,256]{1,0:T(8,128)(2,1)} %refs_3_.5), custom_call_target="tpu_custom_call" | custom-call | tf_op jit(solution)/shard_map/project/pallas_call | solution.py:161
  4.0 3.0 %collective-permute-start = (bf16[128,1152]{1,0:T(8,128)(2,1)S(1)}, bf16[128,1152]{1,0:T(8,128)(2,1)S(1)}, u32[]{:S(2)}, u32[]{:S(2)}) collective-permute-start(bf16[128,1152]{1,0:T(8,128)(2,1)S(1)} %get-tuple-element.34), channel_id=1, source_target_pairs={{0,2},{1,5},{2,0},{3,7},{4,6},{5,1},{6,4},{7,3},{8,10},{9,13},{10,... | collective-permute-start | bytes 884744 | tf_op jit(solution)/shard_map/ppermute | solution.py:55
  7.0 3.9 %project.4 = (bf16[128,1280]{1,0:T(8,128)(2,1)S(1)}, f32[128,1280]{1,0:T(8,128)S(1)}) custom-call(bf16[256,2048]{1,0:T(8,128)(2,1)S(1)} %get-tuple-element.39.refs_0_, bf16[2048,4096]{1,0:T(8,128)(2,1)} %refs_1_.3, bf16[2048,256]{1,0:T(8,128)(2,1)} %refs_2_.5, bf16[2048,256]{1,0:T(8,128)(2,1)} %refs_3_.5), custom_call_target="tpu_custom_call" | custom-call | tf_op jit(solution)/shard_map/project/pallas_call | solution.py:161
  10.9 0.1 collective-permute-start.1
  11.0 0.7 collective-permute-done
  11.7 0.1 convert_add_fusion.2
  11.8 0.0 copy-start
  11.8 5.3 %project.5 = (bf16[128,2304]{1,0:T(8,128)(2,1)S(1)}, f32[128,2304]{1,0:T(8,128)S(1)}) custom-call(bf16[256,2048]{1,0:T(8,128)(2,1)S(1)} %get-tuple-element.39.refs_0_, bf16[2048,4096]{1,0:T(8,128)(2,1)} %refs_1_.3, bf16[2048,256]{1,0:T(8,128)(2,1)} %refs_2_.5, bf16[2048,256]{1,0:T(8,128)(2,1)} %refs_3_.5), custom_call_target="tpu_custom_call" | custom-call | tf_op jit(solution)/shard_map/project/pallas_call | solution.py:161
  17.1 0.9 %collective-permute-done.1 = bf16[128,1280]{1,0:T(8,128)(2,1)S(1)} collective-permute-done((bf16[128,1280]{1,0:T(8,128)(2,1)S(1)}, bf16[128,1280]{1,0:T(8,128)(2,1)S(1)}, u32[]{:S(2)}, u32[]{:S(2)}) %collective-permute-start.1) | collective-permute-done | bytes 327712 | tf_op jit(solution)/shard_map/ppermute | solution.py:55
  18.1 0.1 convert_add_fusion.1
  18.2 1.6 %collective-permute-start.3 = (bf16[64,2432]{1,0:T(8,128)(2,1)S(1)}, bf16[64,2432]{1,0:T(8,128)(2,1)}, u32[]{:S(2)}, u32[]{:S(2)}) collective-permute-start(bf16[64,2432]{1,0:T(8,128)(2,1)S(1)} %fusion.1), channel_id=1, source_target_pairs={{0,4},{1,3},{2,6},{3,1},{4,0},{5,7},{6,2},{7,5},{8,12},{9,11},{10,... | collective-permute-start | bytes 933896 | tf_op jit(solution)/shard_map/ppermute | solution.py:55
  19.8 0.1 add_convert_fusion.1
  19.9 0.1 convert_element_type.49
  20.0 1.2 %collective-permute-start.2 = (bf16[128,2304]{1,0:T(8,128)(2,1)S(1)}, bf16[128,2304]{1,0:T(8,128)(2,1)S(1)}, u32[]{:S(2)}, u32[]{:S(2)}) collective-permute-start(bf16[128,2304]{1,0:T(8,128)(2,1)S(1)} %get-tuple-element.44), channel_id=1, source_target_pairs={{0,2},{1,5},{2,0},{3,7},{4,6},{5,1},{6,4},{7,3},{8,10},{9,13},{10,... | collective-permute-start | bytes 1769480 | tf_op jit(solution)/shard_map/ppermute | solution.py:55
  21.1 3.5 %fetch_rows.1.refs_8_ = bf16[2048,2048]{1,0:T(8,128)(2,1)S(1)} custom-call(bf16[4096,2048]{1,0:T(8,128)(2,1)} %refs_6_.1), custom_call_target="tpu_custom_call" | custom-call | tf_op jit(solution)/shard_map/fetch_rows/pallas_call | solution.py:343
  24.6 5.6 %collective-permute-done.3 = bf16[64,2432]{1,0:T(8,128)(2,1)} collective-permute-done((bf16[64,2432]{1,0:T(8,128)(2,1)S(1)}, bf16[64,2432]{1,0:T(8,128)(2,1)}, u32[]{:S(2)}, u32[]{:S(2)}) %collective-permute-start.3) | collective-permute-done | bytes 311328 | tf_op jit(solution)/shard_map/ppermute | solution.py:55
  30.2 1.0 %fusion.2 = f32[64,2432]{1,0:T(8,128)S(1)} fusion(f32[128,1280]{1,0:T(8,128)S(1)} %convert_add_fusion.1, f32[128,1152]{1,0:T(8,128)S(1)} %convert_add_fusion.2, bf16[64,2432]{1,0:T(8,128)(2,1)} %collective-permute-done.3), kind=kLoop, calls=%fused_computation.8 | loop fusion | flops 466944 | bytes 2179072 | tf_op jit(solution)/shard_map/add | solution.py:461
  31.3 1.5 %collective-permute-start.5 = (bf16[32,2432]{1,0:T(8,128)(2,1)S(1)}, bf16[32,2432]{1,0:T(8,128)(2,1)S(1)}, u32[]{:S(2)}, u32[]{:S(2)}) collective-permute-start(bf16[32,2432]{1,0:T(8,128)(2,1)S(1)} %slice.64), channel_id=1, source_target_pairs={{0,8},{1,9},{2,10},{3,11},{4,12},{5,13},{6,14},{7,15},{8,0},{9,1},... | collective-permute-start | bytes 466952 | tf_op jit(solution)/shard_map/ppermute | solution.py:55
  32.8 0.0 collective-permute-done.2
  32.8 0.1 convert_add_fusion
  32.9 2.8 %collective-permute-start.4 = (bf16[64,2304]{1,0:T(8,128)(2,1)S(1)}, bf16[64,2304]{1,0:T(8,128)(2,1)S(1)}, u32[]{:S(2)}, u32[]{:S(2)}) collective-permute-start(bf16[64,2304]{1,0:T(8,128)(2,1)S(1)} %slice.63), channel_id=1, source_target_pairs={{0,4},{1,3},{2,6},{3,1},{4,0},{5,7},{6,2},{7,5},{8,12},{9,11},{10,... | collective-permute-start | bytes 884744 | tf_op jit(solution)/shard_map/ppermute | solution.py:55
  35.7 3.5 %fetch.1 = (bf16[8,1024,256]{2,1,0:T(8,128)(2,1)S(1)}, bf16[8,1024,256]{2,1,0:T(8,128)(2,1)S(1)}) custom-call(bf16[8,1024,256]{2,1,0:T(8,128)(2,1)} %refs_0_.2, bf16[8,1024,256]{2,1,0:T(8,128)(2,1)} %refs_1_.4), custom_call_target="tpu_custom_call" | custom-call | tf_op jit(solution)/shard_map/fetch/pallas_call | solution.py:314
  39.2 0.0 collective-permute-done.5
  39.3 2.0 %collective-permute-done.4 = bf16[64,2304]{1,0:T(8,128)(2,1)S(1)} collective-permute-done((bf16[64,2304]{1,0:T(8,128)(2,1)S(1)}, bf16[64,2304]{1,0:T(8,128)(2,1)S(1)}, u32[]{:S(2)}, u32[]{:S(2)}) %collective-permute-start.4) | collective-permute-done | bytes 294944 | tf_op jit(solution)/shard_map/ppermute | solution.py:55
  41.3 0.1 slice_add_fusion
  41.4 0.7 collective-permute-start.6
  42.1 0.1 fusion.3
  42.2 0.1 pad_maximum_fusion.1
  42.3 4.9 %attend.3 = (bf16[32,2048]{1,0:T(8,128)(2,1)S(1)}, bf16[2048,2048]{1,0:T(8,128)(2,1)S(1)}) custom-call(s32[8]{0:T(128)S(1)} %copy-done, f32[32,2432]{1,0:T(8,128)S(1)} %slice_add_fusion.1.refs_0_, f32[32,128]{1,0:T(8,128)S(1)} %slice.48.refs_1_, f32[32,128]{1,0:T(8,128)S(1)} %get-tuple-element.64.refs_2_, f32[32,128]{1,0:T(8,128)S(1)} %get-tuple-element.65.refs_3_, ...), custom_call_target="tpu_custom_call" | custom-call | tf_op jit(solution)/shard_map/attend/pallas_call | solution.py:281
  47.2 0.5 collective-permute-start.17
  47.7 1.9 %collective-permute-start.15 = (bf16[32,2048]{1,0:T(8,128)(2,1)S(1)}, bf16[32,2048]{1,0:T(8,128)(2,1)S(1)}, u32[]{:S(2)}, u32[]{:S(2)}) collective-permute-start(bf16[32,2048]{1,0:T(8,128)(2,1)S(1)} %get-tuple-element.56.refs_0_), channel_id=1, source_target_pairs={{0,4},{1,3},{2,6},{3,1},{4,0},{5,7},{6,2},{7,5},{8,12},{9,11},{10,... | collective-permute-start | bytes 393224 | tf_op jit(solution)/shard_map/ppermute | solution.py:55
  49.5 0.0 collective-permute-done.6
  49.6 1.3 %collective-permute-start.14 = (bf16[32,2048]{1,0:T(8,128)(2,1)S(1)}, bf16[32,2048]{1,0:T(8,128)(2,1)S(1)}, u32[]{:S(2)}, u32[]{:S(2)}) collective-permute-start(bf16[32,2048]{1,0:T(8,128)(2,1)S(1)} %get-tuple-element.56.refs_0_), channel_id=1, source_target_pairs={{0,8},{1,9},{2,10},{3,11},{4,12},{5,13},{6,14},{7,15},{8,0},{9,1},... | collective-permute-start | bytes 393224 | tf_op jit(solution)/shard_map/ppermute | solution.py:55
  50.9 2.5 %attend.2.refs_0_ = bf16[32,2048]{1,0:T(8,128)(2,1)S(1)} custom-call(s32[8]{0:T(128)S(1)} %copy-done, f32[32,2304]{1,0:T(8,128)S(1)} %slice_add_fusion.2.refs_0_, f32[32,128]{1,0:T(8,128)S(1)} %slice.48.refs_1_, f32[32,128]{1,0:T(8,128)S(1)} %get-tuple-element.64.refs_2_, f32[32,128]{1,0:T(8,128)S(1)} %get-tuple-element.65.refs_3_, ...), custom_call_target="tpu_custom_call" | custom-call | tf_op jit(solution)/shard_map/attend/pallas_call | solution.py:281
  53.3 1.8 %collective-permute-start.7 = (bf16[32,2048]{1,0:T(8,128)(2,1)S(1)}, bf16[32,2048]{1,0:T(8,128)(2,1)S(1)}, u32[]{:S(2)}, u32[]{:S(2)}) collective-permute-start(bf16[32,2048]{1,0:T(8,128)(2,1)S(1)} %attend.2.refs_0_), channel_id=1, source_target_pairs={{0,8},{1,9},{2,10},{3,11},{4,12},{5,13},{6,14},{7,15},{8,0},{9,1},... | collective-permute-start | bytes 393224 | tf_op jit(solution)/shard_map/ppermute | solution.py:55
  55.1 1.9 %collective-permute-start.10 = (bf16[32,2048]{1,0:T(8,128)(2,1)S(1)}, bf16[32,2048]{1,0:T(8,128)(2,1)S(1)}, u32[]{:S(2)}, u32[]{:S(2)}) collective-permute-start(bf16[32,2048]{1,0:T(8,128)(2,1)S(1)} %attend.2.refs_0_), channel_id=1, source_target_pairs={{0,2},{1,3},{2,0},{3,1},{4,6},{5,7},{6,4},{7,5},{8,10},{9,11},{10,... | collective-permute-start | bytes 393224 | tf_op jit(solution)/shard_map/ppermute | solution.py:55
  57.0 0.0 collective-permute-done.17.refs_4_
  57.1 0.0 collective-permute-start.8
  57.1 0.0 collective-permute-done.15.refs_2_
  57.1 2.2 %collective-permute-done.14.refs_1_ = bf16[32,2048]{1,0:T(8,128)(2,1)S(1)} collective-permute-done((bf16[32,2048]{1,0:T(8,128)(2,1)S(1)}, bf16[32,2048]{1,0:T(8,128)(2,1)S(1)}, u32[]{:S(2)}, u32[]{:S(2)}) %collective-permute-start.14) | collective-permute-done | bytes 131104 | tf_op jit(solution)/shard_map/ppermute | solution.py:55
  59.2 0.4 collective-permute-start.16
  59.7 1.3 %collective-permute-start.19 = (bf16[32,2048]{1,0:T(8,128)(2,1)S(1)}, bf16[32,2048]{1,0:T(8,128)(2,1)S(1)}, u32[]{:S(2)}, u32[]{:S(2)}) collective-permute-start(bf16[32,2048]{1,0:T(8,128)(2,1)S(1)} %collective-permute-done.15.refs_2_), channel_id=1, source_target_pairs={{0,2},{1,5},{2,0},{3,7},{4,6},{5,1},{6,4},{7,3},{8,10},{9,13},{10,... | collective-permute-start | bytes 393224 | tf_op jit(solution)/shard_map/ppermute | solution.py:55
  61.0 0.9 %collective-permute-done.7.refs_1_ = bf16[32,2048]{1,0:T(8,128)(2,1)S(1)} collective-permute-done((bf16[32,2048]{1,0:T(8,128)(2,1)S(1)}, bf16[32,2048]{1,0:T(8,128)(2,1)S(1)}, u32[]{:S(2)}, u32[]{:S(2)}) %collective-permute-start.7) | collective-permute-done | bytes 131104 | tf_op jit(solution)/shard_map/ppermute | solution.py:55
  61.9 1.1 %collective-permute-start.9 = (bf16[32,2048]{1,0:T(8,128)(2,1)S(1)}, bf16[32,2048]{1,0:T(8,128)(2,1)S(1)}, u32[]{:S(2)}, u32[]{:S(2)}) collective-permute-start(bf16[32,2048]{1,0:T(8,128)(2,1)S(1)} %collective-permute-done.7.refs_1_), channel_id=1, source_target_pairs={{0,4},{1,5},{2,6},{3,7},{4,0},{5,1},{6,2},{7,3},{8,12},{9,13},{10,... | collective-permute-start | bytes 393224 | tf_op jit(solution)/shard_map/ppermute | solution.py:55
  63.0 0.0 collective-permute-done.10.refs_4_
  63.0 1.2 %collective-permute-done.8.refs_2_ = bf16[32,2048]{1,0:T(8,128)(2,1)S(1)} collective-permute-done((bf16[32,2048]{1,0:T(8,128)(2,1)S(1)}, bf16[32,2048]{1,0:T(8,128)(2,1)S(1)}, u32[]{:S(2)}, u32[]{:S(2)}) %collective-permute-start.8) | collective-permute-done | bytes 131104 | tf_op jit(solution)/shard_map/ppermute | solution.py:55
  64.2 0.9 %collective-permute-start.12 = (bf16[32,2048]{1,0:T(8,128)(2,1)S(1)}, bf16[32,2048]{1,0:T(8,128)(2,1)S(1)}, u32[]{:S(2)}, u32[]{:S(2)}) collective-permute-start(bf16[32,2048]{1,0:T(8,128)(2,1)S(1)} %collective-permute-done.8.refs_2_), channel_id=1, source_target_pairs={{0,2},{1,3},{2,0},{3,1},{4,6},{5,7},{6,4},{7,5},{8,10},{9,11},{10,... | collective-permute-start | bytes 393224 | tf_op jit(solution)/shard_map/ppermute | solution.py:55
  65.1 1.1 %collective-permute-start.18 = (bf16[32,2048]{1,0:T(8,128)(2,1)S(1)}, bf16[32,2048]{1,0:T(8,128)(2,1)S(1)}, u32[]{:S(2)}, u32[]{:S(2)}) collective-permute-start(bf16[32,2048]{1,0:T(8,128)(2,1)S(1)} %collective-permute-done.14.refs_1_), channel_id=1, source_target_pairs={{0,2},{1,5},{2,0},{3,7},{4,6},{5,1},{6,4},{7,3},{8,10},{9,13},{10,... | collective-permute-start | bytes 393224 | tf_op jit(solution)/shard_map/ppermute | solution.py:55
  66.2 0.8 collective-permute-done.16.refs_3_
  67.0 0.9 %collective-permute-start.20 = (bf16[32,2048]{1,0:T(8,128)(2,1)S(1)}, bf16[32,2048]{1,0:T(8,128)(2,1)S(1)}, u32[]{:S(2)}, u32[]{:S(2)}) collective-permute-start(bf16[32,2048]{1,0:T(8,128)(2,1)S(1)} %collective-permute-done.16.refs_3_), channel_id=1, source_target_pairs={{0,2},{1,5},{2,0},{3,7},{4,6},{5,1},{6,4},{7,3},{8,10},{9,13},{10,... | collective-permute-start | bytes 393224 | tf_op jit(solution)/shard_map/ppermute | solution.py:55
  67.9 0.0 collective-permute-done.19.refs_6_
  67.9 1.1 %collective-permute-start.11 = (bf16[32,2048]{1,0:T(8,128)(2,1)S(1)}, bf16[32,2048]{1,0:T(8,128)(2,1)S(1)}, u32[]{:S(2)}, u32[]{:S(2)}) collective-permute-start(bf16[32,2048]{1,0:T(8,128)(2,1)S(1)} %collective-permute-done.7.refs_1_), channel_id=1, source_target_pairs={{0,2},{1,3},{2,0},{3,1},{4,6},{5,7},{6,4},{7,5},{8,10},{9,11},{10,... | collective-permute-start | bytes 393224 | tf_op jit(solution)/shard_map/ppermute | solution.py:55
  69.0 0.8 collective-permute-done.9.refs_3_
  69.8 0.9 %collective-permute-start.13 = (bf16[32,2048]{1,0:T(8,128)(2,1)S(1)}, bf16[32,2048]{1,0:T(8,128)(2,1)S(1)}, u32[]{:S(2)}, u32[]{:S(2)}) collective-permute-start(bf16[32,2048]{1,0:T(8,128)(2,1)S(1)} %collective-permute-done.9.refs_3_), channel_id=1, source_target_pairs={{0,2},{1,3},{2,0},{3,1},{4,6},{5,7},{6,4},{7,5},{8,10},{9,11},{10,... | collective-permute-start | bytes 393224 | tf_op jit(solution)/shard_map/ppermute | solution.py:55
  70.7 1.0 %collective-permute-done.18.refs_5_ = bf16[32,2048]{1,0:T(8,128)(2,1)S(1)} collective-permute-done((bf16[32,2048]{1,0:T(8,128)(2,1)S(1)}, bf16[32,2048]{1,0:T(8,128)(2,1)S(1)}, u32[]{:S(2)}, u32[]{:S(2)}) %collective-permute-start.18) | collective-permute-done | bytes 131104 | tf_op jit(solution)/shard_map/ppermute | solution.py:55
  71.7 1.4 %collective-permute-done.20.refs_7_ = bf16[32,2048]{1,0:T(8,128)(2,1)S(1)} collective-permute-done((bf16[32,2048]{1,0:T(8,128)(2,1)S(1)}, bf16[32,2048]{1,0:T(8,128)(2,1)S(1)}, u32[]{:S(2)}, u32[]{:S(2)}) %collective-permute-start.20) | collective-permute-done | bytes 131104 | tf_op jit(solution)/shard_map/ppermute | solution.py:55
  73.1 2.4 %combine.2.refs_8_ = f32[256,2048]{1,0:T(8,128)S(1)} custom-call(bf16[32,2048]{1,0:T(8,128)(2,1)S(1)} %get-tuple-element.56.refs_0_, bf16[32,2048]{1,0:T(8,128)(2,1)S(1)} %collective-permute-done.14.refs_1_, bf16[32,2048]{1,0:T(8,128)(2,1)S(1)} %collective-permute-done.15.refs_2_, bf16[32,2048]{1,0:T(8,128)(2,1)S(1)} %collective-permute-done.16.refs_3_, ...), custom_call_target="tpu_custom_call" | custom-call | tf_op jit(solution)/shard_map/combine/pallas_call | solution.py:395
  75.6 0.0 collective-permute-done.12.refs_6_
  75.6 0.0 collective-permute-done.11.refs_5_
  75.6 0.4 collective-permute-done.13.refs_7_
  76.0 2.5 %combine.3 = (bf16[128,2048]{1,0:T(8,128)(2,1)S(1)}, f32[128,2048]{1,0:T(8,128)S(1)}) custom-call(bf16[32,2048]{1,0:T(8,128)(2,1)S(1)} %attend.2.refs_0_, bf16[32,2048]{1,0:T(8,128)(2,1)S(1)} %collective-permute-done.7.refs_1_, bf16[32,2048]{1,0:T(8,128)(2,1)S(1)} %collective-permute-done.8.refs_2_, bf16[32,2048]{1,0:T(8,128)(2,1)S(1)} %collective-permute-done.9.refs_3_, ...), custom_call_target="tpu_custom_call" | custom-call | tf_op jit(solution)/shard_map/combine/pallas_call | solution.py:395
  78.4 0.1 collective-permute-start.21
  78.5 1.9 %collective-permute-done.21 = bf16[128,2048]{1,0:T(8,128)(2,1)S(1)} collective-permute-done((bf16[128,2048]{1,0:T(8,128)(2,1)S(1)}, bf16[128,2048]{1,0:T(8,128)(2,1)S(1)}, u32[]{:S(2)}, u32[]{:S(2)}) %collective-permute-start.21) | collective-permute-done | bytes 524320 | tf_op jit(solution)/shard_map/ppermute | solution.py:520
  80.4 0.9 %add_convert_fusion = bf16[128,2048]{1,0:T(8,128)(2,1)} fusion(f32[128,2048]{1,0:T(8,128)S(1)} %get-tuple-element.59, bf16[128,2048]{1,0:T(8,128)(2,1)S(1)} %collective-permute-done.21), kind=kLoop, calls=%fused_computation.3 | loop fusion | flops 786432 | bytes 2097152 | tf_op jit(solution)/shard_map/convert_element_type | solution.py:521
  (9 shorter events, 0.2 us)
Async XLA Ops:
  4.0 7.7 %collective-permute-start = (bf16[128,1152]{1,0:T(8,128)(2,1)S(1)}, bf16[128,1152]{1,0:T(8,128)(2,1)S(1)}, u32[]{:S(2)}, u32[]{:S(2)}) collective-permute-start(bf16[128,1152]{1,0:T(8,128)(2,1)S(1)} %get-tuple-element.34), channel_id=1, source_target_pairs={{0,2},{1,5},{2,0},{3,7},{4,6},{5,1},{6,4},{7,3},{8,10},{9,13},{10,... | collective-permute-start | bytes 884744 | tf_op jit(solution)/shard_map/ppermute | solution.py:55
  10.9 7.1 %collective-permute-start.1 = (bf16[128,1280]{1,0:T(8,128)(2,1)S(1)}, bf16[128,1280]{1,0:T(8,128)(2,1)S(1)}, u32[]{:S(2)}, u32[]{:S(2)}) collective-permute-start(bf16[128,1280]{1,0:T(8,128)(2,1)S(1)} %get-tuple-element.36), channel_id=1, source_target_pairs={{0,2},{1,5},{2,0},{3,7},{4,6},{5,1},{6,4},{7,3},{8,10},{9,13},{10,... | collective-permute-start | bytes 983048 | tf_op jit(solution)/shard_map/ppermute | solution.py:55
  11.8 8.0 %copy-start = (s32[8]{0:T(128)S(1)}, s32[8]{0:T(128)}, u32[]{:S(2)}) copy-start(s32[8]{0:T(128)} %length_ref.3) | copy-start | bytes 100
  18.2 12.1 %collective-permute-start.3 = (bf16[64,2432]{1,0:T(8,128)(2,1)S(1)}, bf16[64,2432]{1,0:T(8,128)(2,1)}, u32[]{:S(2)}, u32[]{:S(2)}) collective-permute-start(bf16[64,2432]{1,0:T(8,128)(2,1)S(1)} %fusion.1), channel_id=1, source_target_pairs={{0,4},{1,3},{2,6},{3,1},{4,0},{5,7},{6,2},{7,5},{8,12},{9,11},{10,... | collective-permute-start | bytes 933896 | tf_op jit(solution)/shard_map/ppermute | solution.py:55
  20.0 12.8 %collective-permute-start.2 = (bf16[128,2304]{1,0:T(8,128)(2,1)S(1)}, bf16[128,2304]{1,0:T(8,128)(2,1)S(1)}, u32[]{:S(2)}, u32[]{:S(2)}) collective-permute-start(bf16[128,2304]{1,0:T(8,128)(2,1)S(1)} %get-tuple-element.44), channel_id=1, source_target_pairs={{0,2},{1,5},{2,0},{3,7},{4,6},{5,1},{6,4},{7,3},{8,10},{9,13},{10,... | collective-permute-start | bytes 1769480 | tf_op jit(solution)/shard_map/ppermute | solution.py:55
  31.3 8.0 %collective-permute-start.5 = (bf16[32,2432]{1,0:T(8,128)(2,1)S(1)}, bf16[32,2432]{1,0:T(8,128)(2,1)S(1)}, u32[]{:S(2)}, u32[]{:S(2)}) collective-permute-start(bf16[32,2432]{1,0:T(8,128)(2,1)S(1)} %slice.64), channel_id=1, source_target_pairs={{0,8},{1,9},{2,10},{3,11},{4,12},{5,13},{6,14},{7,15},{8,0},{9,1},... | collective-permute-start | bytes 466952 | tf_op jit(solution)/shard_map/ppermute | solution.py:55
  32.9 8.4 %collective-permute-start.4 = (bf16[64,2304]{1,0:T(8,128)(2,1)S(1)}, bf16[64,2304]{1,0:T(8,128)(2,1)S(1)}, u32[]{:S(2)}, u32[]{:S(2)}) collective-permute-start(bf16[64,2304]{1,0:T(8,128)(2,1)S(1)} %slice.63), channel_id=1, source_target_pairs={{0,4},{1,3},{2,6},{3,1},{4,0},{5,7},{6,2},{7,5},{8,12},{9,11},{10,... | collective-permute-start | bytes 884744 | tf_op jit(solution)/shard_map/ppermute | solution.py:55
  41.4 8.1 %collective-permute-start.6 = (bf16[32,2304]{1,0:T(8,128)(2,1)S(1)}, bf16[32,2304]{1,0:T(8,128)(2,1)S(1)}, u32[]{:S(2)}, u32[]{:S(2)}) collective-permute-start(bf16[32,2304]{1,0:T(8,128)(2,1)S(1)} %slice.65), channel_id=1, source_target_pairs={{0,8},{1,9},{2,10},{3,11},{4,12},{5,13},{6,14},{7,15},{8,0},{9,1},... | collective-permute-start | bytes 442376 | tf_op jit(solution)/shard_map/ppermute | solution.py:55
  47.2 9.9 %collective-permute-start.17 = (bf16[32,2048]{1,0:T(8,128)(2,1)S(1)}, bf16[32,2048]{1,0:T(8,128)(2,1)S(1)}, u32[]{:S(2)}, u32[]{:S(2)}) collective-permute-start(bf16[32,2048]{1,0:T(8,128)(2,1)S(1)} %get-tuple-element.56.refs_0_), channel_id=1, source_target_pairs={{0,2},{1,5},{2,0},{3,7},{4,6},{5,1},{6,4},{7,3},{8,10},{9,13},{10,... | collective-permute-start | bytes 393224 | tf_op jit(solution)/shard_map/ppermute | solution.py:55
  47.7 9.4 %collective-permute-start.15 = (bf16[32,2048]{1,0:T(8,128)(2,1)S(1)}, bf16[32,2048]{1,0:T(8,128)(2,1)S(1)}, u32[]{:S(2)}, u32[]{:S(2)}) collective-permute-start(bf16[32,2048]{1,0:T(8,128)(2,1)S(1)} %get-tuple-element.56.refs_0_), channel_id=1, source_target_pairs={{0,4},{1,3},{2,6},{3,1},{4,0},{5,7},{6,2},{7,5},{8,12},{9,11},{10,... | collective-permute-start | bytes 393224 | tf_op jit(solution)/shard_map/ppermute | solution.py:55
  49.6 9.6 %collective-permute-start.14 = (bf16[32,2048]{1,0:T(8,128)(2,1)S(1)}, bf16[32,2048]{1,0:T(8,128)(2,1)S(1)}, u32[]{:S(2)}, u32[]{:S(2)}) collective-permute-start(bf16[32,2048]{1,0:T(8,128)(2,1)S(1)} %get-tuple-element.56.refs_0_), channel_id=1, source_target_pairs={{0,8},{1,9},{2,10},{3,11},{4,12},{5,13},{6,14},{7,15},{8,0},{9,1},... | collective-permute-start | bytes 393224 | tf_op jit(solution)/shard_map/ppermute | solution.py:55
  53.3 8.5 %collective-permute-start.7 = (bf16[32,2048]{1,0:T(8,128)(2,1)S(1)}, bf16[32,2048]{1,0:T(8,128)(2,1)S(1)}, u32[]{:S(2)}, u32[]{:S(2)}) collective-permute-start(bf16[32,2048]{1,0:T(8,128)(2,1)S(1)} %attend.2.refs_0_), channel_id=1, source_target_pairs={{0,8},{1,9},{2,10},{3,11},{4,12},{5,13},{6,14},{7,15},{8,0},{9,1},... | collective-permute-start | bytes 393224 | tf_op jit(solution)/shard_map/ppermute | solution.py:55
  55.1 7.9 %collective-permute-start.10 = (bf16[32,2048]{1,0:T(8,128)(2,1)S(1)}, bf16[32,2048]{1,0:T(8,128)(2,1)S(1)}, u32[]{:S(2)}, u32[]{:S(2)}) collective-permute-start(bf16[32,2048]{1,0:T(8,128)(2,1)S(1)} %attend.2.refs_0_), channel_id=1, source_target_pairs={{0,2},{1,3},{2,0},{3,1},{4,6},{5,7},{6,4},{7,5},{8,10},{9,11},{10,... | collective-permute-start | bytes 393224 | tf_op jit(solution)/shard_map/ppermute | solution.py:55
  57.1 7.1 %collective-permute-start.8 = (bf16[32,2048]{1,0:T(8,128)(2,1)S(1)}, bf16[32,2048]{1,0:T(8,128)(2,1)S(1)}, u32[]{:S(2)}, u32[]{:S(2)}) collective-permute-start(bf16[32,2048]{1,0:T(8,128)(2,1)S(1)} %attend.2.refs_0_), channel_id=1, source_target_pairs={{0,4},{1,5},{2,6},{3,7},{4,0},{5,1},{6,2},{7,3},{8,12},{9,13},{10,... | collective-permute-start | bytes 393224 | tf_op jit(solution)/shard_map/ppermute | solution.py:55
  59.2 7.8 %collective-permute-start.16 = (bf16[32,2048]{1,0:T(8,128)(2,1)S(1)}, bf16[32,2048]{1,0:T(8,128)(2,1)S(1)}, u32[]{:S(2)}, u32[]{:S(2)}) collective-permute-start(bf16[32,2048]{1,0:T(8,128)(2,1)S(1)} %collective-permute-done.14.refs_1_), channel_id=1, source_target_pairs={{0,4},{1,3},{2,6},{3,1},{4,0},{5,7},{6,2},{7,5},{8,12},{9,11},{10,... | collective-permute-start | bytes 393224 | tf_op jit(solution)/shard_map/ppermute | solution.py:55
  59.7 8.3 %collective-permute-start.19 = (bf16[32,2048]{1,0:T(8,128)(2,1)S(1)}, bf16[32,2048]{1,0:T(8,128)(2,1)S(1)}, u32[]{:S(2)}, u32[]{:S(2)}) collective-permute-start(bf16[32,2048]{1,0:T(8,128)(2,1)S(1)} %collective-permute-done.15.refs_2_), channel_id=1, source_target_pairs={{0,2},{1,5},{2,0},{3,7},{4,6},{5,1},{6,4},{7,3},{8,10},{9,13},{10,... | collective-permute-start | bytes 393224 | tf_op jit(solution)/shard_map/ppermute | solution.py:55
  61.9 7.9 %collective-permute-start.9 = (bf16[32,2048]{1,0:T(8,128)(2,1)S(1)}, bf16[32,2048]{1,0:T(8,128)(2,1)S(1)}, u32[]{:S(2)}, u32[]{:S(2)}) collective-permute-start(bf16[32,2048]{1,0:T(8,128)(2,1)S(1)} %collective-permute-done.7.refs_1_), channel_id=1, source_target_pairs={{0,4},{1,5},{2,6},{3,7},{4,0},{5,1},{6,2},{7,3},{8,12},{9,13},{10,... | collective-permute-start | bytes 393224 | tf_op jit(solution)/shard_map/ppermute | solution.py:55
  64.2 11.4 %collective-permute-start.12 = (bf16[32,2048]{1,0:T(8,128)(2,1)S(1)}, bf16[32,2048]{1,0:T(8,128)(2,1)S(1)}, u32[]{:S(2)}, u32[]{:S(2)}) collective-permute-start(bf16[32,2048]{1,0:T(8,128)(2,1)S(1)} %collective-permute-done.8.refs_2_), channel_id=1, source_target_pairs={{0,2},{1,3},{2,0},{3,1},{4,6},{5,7},{6,4},{7,5},{8,10},{9,11},{10,... | collective-permute-start | bytes 393224 | tf_op jit(solution)/shard_map/ppermute | solution.py:55
  65.1 6.6 %collective-permute-start.18 = (bf16[32,2048]{1,0:T(8,128)(2,1)S(1)}, bf16[32,2048]{1,0:T(8,128)(2,1)S(1)}, u32[]{:S(2)}, u32[]{:S(2)}) collective-permute-start(bf16[32,2048]{1,0:T(8,128)(2,1)S(1)} %collective-permute-done.14.refs_1_), channel_id=1, source_target_pairs={{0,2},{1,5},{2,0},{3,7},{4,6},{5,1},{6,4},{7,3},{8,10},{9,13},{10,... | collective-permute-start | bytes 393224 | tf_op jit(solution)/shard_map/ppermute | solution.py:55
  67.0 6.1 %collective-permute-start.20 = (bf16[32,2048]{1,0:T(8,128)(2,1)S(1)}, bf16[32,2048]{1,0:T(8,128)(2,1)S(1)}, u32[]{:S(2)}, u32[]{:S(2)}) collective-permute-start(bf16[32,2048]{1,0:T(8,128)(2,1)S(1)} %collective-permute-done.16.refs_3_), channel_id=1, source_target_pairs={{0,2},{1,5},{2,0},{3,7},{4,6},{5,1},{6,4},{7,3},{8,10},{9,13},{10,... | collective-permute-start | bytes 393224 | tf_op jit(solution)/shard_map/ppermute | solution.py:55
  67.9 7.7 %collective-permute-start.11 = (bf16[32,2048]{1,0:T(8,128)(2,1)S(1)}, bf16[32,2048]{1,0:T(8,128)(2,1)S(1)}, u32[]{:S(2)}, u32[]{:S(2)}) collective-permute-start(bf16[32,2048]{1,0:T(8,128)(2,1)S(1)} %collective-permute-done.7.refs_1_), channel_id=1, source_target_pairs={{0,2},{1,3},{2,0},{3,1},{4,6},{5,7},{6,4},{7,5},{8,10},{9,11},{10,... | collective-permute-start | bytes 393224 | tf_op jit(solution)/shard_map/ppermute | solution.py:55
  69.8 6.1 %collective-permute-start.13 = (bf16[32,2048]{1,0:T(8,128)(2,1)S(1)}, bf16[32,2048]{1,0:T(8,128)(2,1)S(1)}, u32[]{:S(2)}, u32[]{:S(2)}) collective-permute-start(bf16[32,2048]{1,0:T(8,128)(2,1)S(1)} %collective-permute-done.9.refs_3_), channel_id=1, source_target_pairs={{0,2},{1,3},{2,0},{3,1},{4,6},{5,7},{6,4},{7,5},{8,10},{9,11},{10,... | collective-permute-start | bytes 393224 | tf_op jit(solution)/shard_map/ppermute | solution.py:55
  78.4 2.0 %collective-permute-start.21 = (bf16[128,2048]{1,0:T(8,128)(2,1)S(1)}, bf16[128,2048]{1,0:T(8,128)(2,1)S(1)}, u32[]{:S(2)}, u32[]{:S(2)}) collective-permute-start(bf16[128,2048]{1,0:T(8,128)(2,1)S(1)} %get-tuple-element.60), channel_id=1, source_target_pairs={{0,1},{1,0},{2,3},{3,2},{4,5},{5,4},{6,7},{7,6},{8,9},{9,8},{10,11... | collective-permute-start | bytes 1572872 | tf_op jit(solution)/shard_map/ppermute | solution.py:520

commit v18 on v17

--- a/solution.py
+++ b/solution.py
@@ -30,7 +30,7 @@
 
 def gather_orders(n, chunk):
     first, second = bit_orders(n)
-    return (first, first) if chunk else (first, second)
+    return (first, second) if chunk else (first, first)
 
 
 def slot_shift(slot, order):
@@ -197,7 +197,7 @@
     new_cols = lax.broadcasted_iota(jnp.int32, (many, rows), 1)
     new_rows = lax.broadcasted_iota(jnp.int32, (many, rows), 0) % NEW
 
-    @pl.loop(0, seq_count // seqs, unroll=True)
+    @pl.loop(0, seq_count // seqs, unroll=chunk > 0)
     def _(step):
         mine = pl.ds(pl.multiple_of(step * rows, rows), rows)
         mean = jnp.sum(square_ref[mine, :], axis=1, keepdims=True) / D
@@ -361,7 +361,8 @@
     depth, cols = x_buf.shape[1], w_ref.shape[1]
     half = x_buf.shape[0] // 2
     for slot, piece in enumerate(pieces):
-        start = pl.multiple_of((slot_owner(n, slot, gx, gy, gather_orders(n, chunk)) ^ moved) * block, block)
+        owner = slot_owner(n, slot, gx, gy, gather_orders(n, chunk))
+        start = pl.multiple_of((owner ^ moved) * block, block)
         x_buf[pl.ds(start, block), :] = piece[...]
 
     tile = cols // TILES

time: 81.5 us -> 79 us (0.969)
  waiting for transfers between devices: 19.8 us -> 17.9 us
    ppermute x21, waiting for transfers between devices: 17.9 us -> 16 us  [exchange(): return lax.ppermute(value, ('gx', 'gy'), pairs)]
where the time goes in v18:
time: 79 us; the launch traced here: 78.8 us
  Pallas kernels  31.6 us (40%)
  starting transfers between devices  26.4 us (33%)
  waiting for transfers between devices  17.9 us (23%)
  other arithmetic  2.58 us (3%)
    ppermute x21, starting transfers between devices, exchange(): return lax.ppermute(value, ('gx', 'gy'), pairs)  26.3 us
    ppermute x21, waiting for transfers between devices, exchange(): return lax.ppermute(value, ('gx', 'gy'), pairs)  16 us
    pallas_call x3, Pallas kernels, project(): pl.pallas_call(functools.partial(project_kernel, n, q_start, kv_start, fi...  13.2 us
    pallas_call x2, Pallas kernels, attend(): pl.pallas_call(functools.partial(attend_kernel, chunk, offsets, kv_offset...  6.52 us
    pallas_call x2, Pallas kernels, combine(): pl.pallas_call(functools.partial(combine_kernel, n, block, chunk), out_sh...  4.89 us
    pallas_call x1, Pallas kernels, fetch_rows(): pl.pallas_call(functools.partial(fetch_rows_kernel, start, pieces), out_s...  3.5 us
    pallas_call x1, Pallas kernels, fetch(): pl.pallas_call(functools.partial(fetch_kernel, len(arrays), pieces), out_...  3.47 us
    ppermute x1, waiting for transfers between devices, shards(): other = lax.ppermute(send, 'gy', [(0, 1), (1, 0)])  1.9 us
  transfers between devices with their start and end apart: 22, of which 13 were waited for; matrix products, arithmetic and copies ran while one was open for 2% of the time, Pallas kernels for 32%

profile of v18, /device:TPU:0, one launch (start us, length us, event | category | flops | bytes accessed | tf_op | source)
XLA Modules:
  0.0 78.8 jit_solution(4351339721271382278)
XLA Ops:
  0.0 4.0 %project.3 = (bf16[128,1152]{1,0:T(8,128)(2,1)S(1)}, f32[128,1152]{1,0:T(8,128)S(1)}, bf16[256,2048]{1,0:T(8,128)(2,1)S(1)}) custom-call(bf16[256,2048]{1,0:T(8,128)(2,1)} %refs_0_.1, f32[1,2048]{1,0:T(1,128)} %bitcast.1, bf16[2048,4096]{1,0:T(8,128)(2,1)} %refs_1_.3, bf16[2048,256]{1,0:T(8,128)(2,1)} %refs_2_.5, bf16[2048,256]{1,0:T(8,128)(2,1)} %refs_3_.5), custom_call_target="tpu_custom_call" | custom-call | tf_op jit(solution)/shard_map/project/pallas_call | solution.py:161
  4.0 3.0 %collective-permute-start = (bf16[128,1152]{1,0:T(8,128)(2,1)S(1)}, bf16[128,1152]{1,0:T(8,128)(2,1)S(1)}, u32[]{:S(2)}, u32[]{:S(2)}) collective-permute-start(bf16[128,1152]{1,0:T(8,128)(2,1)S(1)} %get-tuple-element.34), channel_id=1, source_target_pairs={{0,2},{1,5},{2,0},{3,7},{4,6},{5,1},{6,4},{7,3},{8,10},{9,13},{10,... | collective-permute-start | bytes 884744 | tf_op jit(solution)/shard_map/ppermute | solution.py:55
  7.0 3.9 %project.4 = (bf16[128,1280]{1,0:T(8,128)(2,1)S(1)}, f32[128,1280]{1,0:T(8,128)S(1)}) custom-call(bf16[256,2048]{1,0:T(8,128)(2,1)S(1)} %get-tuple-element.39.refs_0_, bf16[2048,4096]{1,0:T(8,128)(2,1)} %refs_1_.3, bf16[2048,256]{1,0:T(8,128)(2,1)} %refs_2_.5, bf16[2048,256]{1,0:T(8,128)(2,1)} %refs_3_.5), custom_call_target="tpu_custom_call" | custom-call | tf_op jit(solution)/shard_map/project/pallas_call | solution.py:161
  10.9 0.1 collective-permute-start.1
  11.0 0.7 collective-permute-done
  11.7 0.1 convert_add_fusion.2
  11.8 0.0 copy-start
  11.8 5.3 %project.5 = (bf16[128,2304]{1,0:T(8,128)(2,1)S(1)}, f32[128,2304]{1,0:T(8,128)S(1)}) custom-call(bf16[256,2048]{1,0:T(8,128)(2,1)S(1)} %get-tuple-element.39.refs_0_, bf16[2048,4096]{1,0:T(8,128)(2,1)} %refs_1_.3, bf16[2048,256]{1,0:T(8,128)(2,1)} %refs_2_.5, bf16[2048,256]{1,0:T(8,128)(2,1)} %refs_3_.5), custom_call_target="tpu_custom_call" | custom-call | tf_op jit(solution)/shard_map/project/pallas_call | solution.py:161
  17.1 0.9 %collective-permute-done.1 = bf16[128,1280]{1,0:T(8,128)(2,1)S(1)} collective-permute-done((bf16[128,1280]{1,0:T(8,128)(2,1)S(1)}, bf16[128,1280]{1,0:T(8,128)(2,1)S(1)}, u32[]{:S(2)}, u32[]{:S(2)}) %collective-permute-start.1) | collective-permute-done | bytes 327712 | tf_op jit(solution)/shard_map/ppermute | solution.py:55
  18.1 0.1 convert_add_fusion.1
  18.2 1.6 %collective-permute-start.3 = (bf16[64,2432]{1,0:T(8,128)(2,1)S(1)}, bf16[64,2432]{1,0:T(8,128)(2,1)}, u32[]{:S(2)}, u32[]{:S(2)}) collective-permute-start(bf16[64,2432]{1,0:T(8,128)(2,1)S(1)} %fusion.1), channel_id=1, source_target_pairs={{0,4},{1,3},{2,6},{3,1},{4,0},{5,7},{6,2},{7,5},{8,12},{9,11},{10,... | collective-permute-start | bytes 933896 | tf_op jit(solution)/shard_map/ppermute | solution.py:55
  19.8 0.1 add_convert_fusion.1
  19.9 0.1 convert_element_type.49
  20.0 1.2 %collective-permute-start.2 = (bf16[128,2304]{1,0:T(8,128)(2,1)S(1)}, bf16[128,2304]{1,0:T(8,128)(2,1)S(1)}, u32[]{:S(2)}, u32[]{:S(2)}) collective-permute-start(bf16[128,2304]{1,0:T(8,128)(2,1)S(1)} %get-tuple-element.44), channel_id=1, source_target_pairs={{0,2},{1,5},{2,0},{3,7},{4,6},{5,1},{6,4},{7,3},{8,10},{9,13},{10,... | collective-permute-start | bytes 1769480 | tf_op jit(solution)/shard_map/ppermute | solution.py:55
  21.1 3.5 %fetch_rows.1.refs_8_ = bf16[2048,2048]{1,0:T(8,128)(2,1)S(1)} custom-call(bf16[4096,2048]{1,0:T(8,128)(2,1)} %refs_6_.1), custom_call_target="tpu_custom_call" | custom-call | tf_op jit(solution)/shard_map/fetch_rows/pallas_call | solution.py:343
  24.6 5.6 %collective-permute-done.3 = bf16[64,2432]{1,0:T(8,128)(2,1)} collective-permute-done((bf16[64,2432]{1,0:T(8,128)(2,1)S(1)}, bf16[64,2432]{1,0:T(8,128)(2,1)}, u32[]{:S(2)}, u32[]{:S(2)}) %collective-permute-start.3) | collective-permute-done | bytes 311328 | tf_op jit(solution)/shard_map/ppermute | solution.py:55
  30.2 1.0 %fusion.2 = f32[64,2432]{1,0:T(8,128)S(1)} fusion(f32[128,1280]{1,0:T(8,128)S(1)} %convert_add_fusion.1, f32[128,1152]{1,0:T(8,128)S(1)} %convert_add_fusion.2, bf16[64,2432]{1,0:T(8,128)(2,1)} %collective-permute-done.3), kind=kLoop, calls=%fused_computation.8 | loop fusion | flops 466944 | bytes 2179072 | tf_op jit(solution)/shard_map/add | solution.py:462
  31.3 1.5 %collective-permute-start.5 = (bf16[32,2432]{1,0:T(8,128)(2,1)S(1)}, bf16[32,2432]{1,0:T(8,128)(2,1)S(1)}, u32[]{:S(2)}, u32[]{:S(2)}) collective-permute-start(bf16[32,2432]{1,0:T(8,128)(2,1)S(1)} %slice.64), channel_id=1, source_target_pairs={{0,8},{1,9},{2,10},{3,11},{4,12},{5,13},{6,14},{7,15},{8,0},{9,1},... | collective-permute-start | bytes 466952 | tf_op jit(solution)/shard_map/ppermute | solution.py:55
  32.8 0.0 collective-permute-done.2
  32.8 0.1 convert_add_fusion
  32.9 2.8 %collective-permute-start.4 = (bf16[64,2304]{1,0:T(8,128)(2,1)S(1)}, bf16[64,2304]{1,0:T(8,128)(2,1)S(1)}, u32[]{:S(2)}, u32[]{:S(2)}) collective-permute-start(bf16[64,2304]{1,0:T(8,128)(2,1)S(1)} %slice.63), channel_id=1, source_target_pairs={{0,4},{1,3},{2,6},{3,1},{4,0},{5,7},{6,2},{7,5},{8,12},{9,11},{10,... | collective-permute-start | bytes 884744 | tf_op jit(solution)/shard_map/ppermute | solution.py:55
  35.7 3.5 %fetch.1 = (bf16[8,1024,256]{2,1,0:T(8,128)(2,1)S(1)}, bf16[8,1024,256]{2,1,0:T(8,128)(2,1)S(1)}) custom-call(bf16[8,1024,256]{2,1,0:T(8,128)(2,1)} %refs_0_.2, bf16[8,1024,256]{2,1,0:T(8,128)(2,1)} %refs_1_.4), custom_call_target="tpu_custom_call" | custom-call | tf_op jit(solution)/shard_map/fetch/pallas_call | solution.py:314
  39.2 0.0 collective-permute-done.5
  39.3 2.0 %collective-permute-done.4 = bf16[64,2304]{1,0:T(8,128)(2,1)S(1)} collective-permute-done((bf16[64,2304]{1,0:T(8,128)(2,1)S(1)}, bf16[64,2304]{1,0:T(8,128)(2,1)S(1)}, u32[]{:S(2)}, u32[]{:S(2)}) %collective-permute-start.4) | collective-permute-done | bytes 294944 | tf_op jit(solution)/shard_map/ppermute | solution.py:55
  41.3 0.1 slice_add_fusion
  41.4 0.7 collective-permute-start.6
  42.1 0.1 fusion.3
  42.2 0.1 pad_maximum_fusion.1
  42.3 4.0 %attend.3 = (bf16[32,2048]{1,0:T(8,128)(2,1)S(1)}, bf16[2048,2048]{1,0:T(8,128)(2,1)S(1)}) custom-call(s32[8]{0:T(128)S(1)} %copy-done, f32[32,2432]{1,0:T(8,128)S(1)} %slice_add_fusion.1.refs_0_, f32[32,128]{1,0:T(8,128)S(1)} %slice.48.refs_1_, f32[32,128]{1,0:T(8,128)S(1)} %get-tuple-element.64.refs_2_, f32[32,128]{1,0:T(8,128)S(1)} %get-tuple-element.65.refs_3_, ...), custom_call_target="tpu_custom_call" | custom-call | tf_op jit(solution)/shard_map/attend/pallas_call | solution.py:281
  46.4 0.5 collective-permute-start.17
  46.9 1.9 %collective-permute-start.15 = (bf16[32,2048]{1,0:T(8,128)(2,1)S(1)}, bf16[32,2048]{1,0:T(8,128)(2,1)S(1)}, u32[]{:S(2)}, u32[]{:S(2)}) collective-permute-start(bf16[32,2048]{1,0:T(8,128)(2,1)S(1)} %get-tuple-element.56.refs_0_), channel_id=1, source_target_pairs={{0,4},{1,5},{2,6},{3,7},{4,0},{5,1},{6,2},{7,3},{8,12},{9,13},{10,... | collective-permute-start | bytes 393224 | tf_op jit(solution)/shard_map/ppermute | solution.py:55
  48.7 0.5 collective-permute-done.6
  49.2 0.8 %collective-permute-start.14 = (bf16[32,2048]{1,0:T(8,128)(2,1)S(1)}, bf16[32,2048]{1,0:T(8,128)(2,1)S(1)}, u32[]{:S(2)}, u32[]{:S(2)}) collective-permute-start(bf16[32,2048]{1,0:T(8,128)(2,1)S(1)} %get-tuple-element.56.refs_0_), channel_id=1, source_target_pairs={{0,8},{1,9},{2,10},{3,11},{4,12},{5,13},{6,14},{7,15},{8,0},{9,1},... | collective-permute-start | bytes 393224 | tf_op jit(solution)/shard_map/ppermute | solution.py:55
  50.1 2.5 %attend.2.refs_0_ = bf16[32,2048]{1,0:T(8,128)(2,1)S(1)} custom-call(s32[8]{0:T(128)S(1)} %copy-done, f32[32,2304]{1,0:T(8,128)S(1)} %slice_add_fusion.2.refs_0_, f32[32,128]{1,0:T(8,128)S(1)} %slice.48.refs_1_, f32[32,128]{1,0:T(8,128)S(1)} %get-tuple-element.64.refs_2_, f32[32,128]{1,0:T(8,128)S(1)} %get-tuple-element.65.refs_3_, ...), custom_call_target="tpu_custom_call" | custom-call | tf_op jit(solution)/shard_map/attend/pallas_call | solution.py:281
  52.5 2.2 %collective-permute-start.7 = (bf16[32,2048]{1,0:T(8,128)(2,1)S(1)}, bf16[32,2048]{1,0:T(8,128)(2,1)S(1)}, u32[]{:S(2)}, u32[]{:S(2)}) collective-permute-start(bf16[32,2048]{1,0:T(8,128)(2,1)S(1)} %attend.2.refs_0_), channel_id=1, source_target_pairs={{0,8},{1,9},{2,10},{3,11},{4,12},{5,13},{6,14},{7,15},{8,0},{9,1},... | collective-permute-start | bytes 393224 | tf_op jit(solution)/shard_map/ppermute | solution.py:55
  54.7 1.5 %collective-permute-start.10 = (bf16[32,2048]{1,0:T(8,128)(2,1)S(1)}, bf16[32,2048]{1,0:T(8,128)(2,1)S(1)}, u32[]{:S(2)}, u32[]{:S(2)}) collective-permute-start(bf16[32,2048]{1,0:T(8,128)(2,1)S(1)} %attend.2.refs_0_), channel_id=1, source_target_pairs={{0,2},{1,5},{2,0},{3,7},{4,6},{5,1},{6,4},{7,3},{8,10},{9,13},{10,... | collective-permute-start | bytes 393224 | tf_op jit(solution)/shard_map/ppermute | solution.py:55
  56.2 0.0 collective-permute-done.17.refs_4_
  56.2 0.0 collective-permute-start.8
  56.2 0.0 collective-permute-done.15.refs_2_
  56.2 2.1 %collective-permute-done.14.refs_1_ = bf16[32,2048]{1,0:T(8,128)(2,1)S(1)} collective-permute-done((bf16[32,2048]{1,0:T(8,128)(2,1)S(1)}, bf16[32,2048]{1,0:T(8,128)(2,1)S(1)}, u32[]{:S(2)}, u32[]{:S(2)}) %collective-permute-start.14) | collective-permute-done | bytes 131104 | tf_op jit(solution)/shard_map/ppermute | solution.py:55
  58.4 0.4 collective-permute-start.16
  58.8 1.3 %collective-permute-start.19 = (bf16[32,2048]{1,0:T(8,128)(2,1)S(1)}, bf16[32,2048]{1,0:T(8,128)(2,1)S(1)}, u32[]{:S(2)}, u32[]{:S(2)}) collective-permute-start(bf16[32,2048]{1,0:T(8,128)(2,1)S(1)} %collective-permute-done.15.refs_2_), channel_id=1, source_target_pairs={{0,2},{1,3},{2,0},{3,1},{4,6},{5,7},{6,4},{7,5},{8,10},{9,11},{10,... | collective-permute-start | bytes 393224 | tf_op jit(solution)/shard_map/ppermute | solution.py:55
  60.1 1.1 %collective-permute-done.7.refs_1_ = bf16[32,2048]{1,0:T(8,128)(2,1)S(1)} collective-permute-done((bf16[32,2048]{1,0:T(8,128)(2,1)S(1)}, bf16[32,2048]{1,0:T(8,128)(2,1)S(1)}, u32[]{:S(2)}, u32[]{:S(2)}) %collective-permute-start.7) | collective-permute-done | bytes 131104 | tf_op jit(solution)/shard_map/ppermute | solution.py:55
  61.2 0.9 %collective-permute-start.9 = (bf16[32,2048]{1,0:T(8,128)(2,1)S(1)}, bf16[32,2048]{1,0:T(8,128)(2,1)S(1)}, u32[]{:S(2)}, u32[]{:S(2)}) collective-permute-start(bf16[32,2048]{1,0:T(8,128)(2,1)S(1)} %collective-permute-done.7.refs_1_), channel_id=1, source_target_pairs={{0,4},{1,3},{2,6},{3,1},{4,0},{5,7},{6,2},{7,5},{8,12},{9,11},{10,... | collective-permute-start | bytes 393224 | tf_op jit(solution)/shard_map/ppermute | solution.py:55
  62.1 0.0 collective-permute-done.10.refs_4_
  62.1 0.6 collective-permute-done.8.refs_2_
  62.7 1.6 %collective-permute-start.12 = (bf16[32,2048]{1,0:T(8,128)(2,1)S(1)}, bf16[32,2048]{1,0:T(8,128)(2,1)S(1)}, u32[]{:S(2)}, u32[]{:S(2)}) collective-permute-start(bf16[32,2048]{1,0:T(8,128)(2,1)S(1)} %collective-permute-done.8.refs_2_), channel_id=1, source_target_pairs={{0,2},{1,5},{2,0},{3,7},{4,6},{5,1},{6,4},{7,3},{8,10},{9,13},{10,... | collective-permute-start | bytes 393224 | tf_op jit(solution)/shard_map/ppermute | solution.py:55
  64.3 0.4 collective-permute-start.18
  64.7 0.5 collective-permute-done.16.refs_3_
  65.3 1.8 %collective-permute-start.20 = (bf16[32,2048]{1,0:T(8,128)(2,1)S(1)}, bf16[32,2048]{1,0:T(8,128)(2,1)S(1)}, u32[]{:S(2)}, u32[]{:S(2)}) collective-permute-start(bf16[32,2048]{1,0:T(8,128)(2,1)S(1)} %collective-permute-done.16.refs_3_), channel_id=1, source_target_pairs={{0,2},{1,3},{2,0},{3,1},{4,6},{5,7},{6,4},{7,5},{8,10},{9,11},{10,... | collective-permute-start | bytes 393224 | tf_op jit(solution)/shard_map/ppermute | solution.py:55
  67.1 0.0 collective-permute-done.19.refs_6_
  67.1 0.2 collective-permute-start.11
  67.3 0.8 collective-permute-done.9.refs_3_
  68.1 1.8 %collective-permute-start.13 = (bf16[32,2048]{1,0:T(8,128)(2,1)S(1)}, bf16[32,2048]{1,0:T(8,128)(2,1)S(1)}, u32[]{:S(2)}, u32[]{:S(2)}) collective-permute-start(bf16[32,2048]{1,0:T(8,128)(2,1)S(1)} %collective-permute-done.9.refs_3_), channel_id=1, source_target_pairs={{0,2},{1,5},{2,0},{3,7},{4,6},{5,1},{6,4},{7,3},{8,10},{9,13},{10,... | collective-permute-start | bytes 393224 | tf_op jit(solution)/shard_map/ppermute | solution.py:55
  69.9 0.0 collective-permute-done.18.refs_5_
  69.9 0.8 collective-permute-done.20.refs_7_
  70.7 2.4 %combine.2.refs_8_ = f32[256,2048]{1,0:T(8,128)S(1)} custom-call(bf16[32,2048]{1,0:T(8,128)(2,1)S(1)} %get-tuple-element.56.refs_0_, bf16[32,2048]{1,0:T(8,128)(2,1)S(1)} %collective-permute-done.14.refs_1_, bf16[32,2048]{1,0:T(8,128)(2,1)S(1)} %collective-permute-done.15.refs_2_, bf16[32,2048]{1,0:T(8,128)(2,1)S(1)} %collective-permute-done.16.refs_3_, ...), custom_call_target="tpu_custom_call" | custom-call | tf_op jit(solution)/shard_map/combine/pallas_call | solution.py:396
  73.1 0.0 collective-permute-done.12.refs_6_
  73.1 0.0 collective-permute-done.11.refs_5_
  73.1 0.4 collective-permute-done.13.refs_7_
  73.5 2.5 %combine.3 = (bf16[128,2048]{1,0:T(8,128)(2,1)S(1)}, f32[128,2048]{1,0:T(8,128)S(1)}) custom-call(bf16[32,2048]{1,0:T(8,128)(2,1)S(1)} %attend.2.refs_0_, bf16[32,2048]{1,0:T(8,128)(2,1)S(1)} %collective-permute-done.7.refs_1_, bf16[32,2048]{1,0:T(8,128)(2,1)S(1)} %collective-permute-done.8.refs_2_, bf16[32,2048]{1,0:T(8,128)(2,1)S(1)} %collective-permute-done.9.refs_3_, ...), custom_call_target="tpu_custom_call" | custom-call | tf_op jit(solution)/shard_map/combine/pallas_call | solution.py:396
  76.0 0.1 collective-permute-start.21
  76.0 1.9 %collective-permute-done.21 = bf16[128,2048]{1,0:T(8,128)(2,1)S(1)} collective-permute-done((bf16[128,2048]{1,0:T(8,128)(2,1)S(1)}, bf16[128,2048]{1,0:T(8,128)(2,1)S(1)}, u32[]{:S(2)}, u32[]{:S(2)}) %collective-permute-start.21) | collective-permute-done | bytes 524320 | tf_op jit(solution)/shard_map/ppermute | solution.py:521
  77.9 0.9 %add_convert_fusion = bf16[128,2048]{1,0:T(8,128)(2,1)} fusion(f32[128,2048]{1,0:T(8,128)S(1)} %get-tuple-element.59, bf16[128,2048]{1,0:T(8,128)(2,1)S(1)} %collective-permute-done.21), kind=kLoop, calls=%fused_computation.3 | loop fusion | flops 786432 | bytes 2097152 | tf_op jit(solution)/shard_map/convert_element_type | solution.py:522
  (9 shorter events, 0.2 us)
Async XLA Ops:
  4.0 7.7 %collective-permute-start = (bf16[128,1152]{1,0:T(8,128)(2,1)S(1)}, bf16[128,1152]{1,0:T(8,128)(2,1)S(1)}, u32[]{:S(2)}, u32[]{:S(2)}) collective-permute-start(bf16[128,1152]{1,0:T(8,128)(2,1)S(1)} %get-tuple-element.34), channel_id=1, source_target_pairs={{0,2},{1,5},{2,0},{3,7},{4,6},{5,1},{6,4},{7,3},{8,10},{9,13},{10,... | collective-permute-start | bytes 884744 | tf_op jit(solution)/shard_map/ppermute | solution.py:55
  10.9 7.1 %collective-permute-start.1 = (bf16[128,1280]{1,0:T(8,128)(2,1)S(1)}, bf16[128,1280]{1,0:T(8,128)(2,1)S(1)}, u32[]{:S(2)}, u32[]{:S(2)}) collective-permute-start(bf16[128,1280]{1,0:T(8,128)(2,1)S(1)} %get-tuple-element.36), channel_id=1, source_target_pairs={{0,2},{1,5},{2,0},{3,7},{4,6},{5,1},{6,4},{7,3},{8,10},{9,13},{10,... | collective-permute-start | bytes 983048 | tf_op jit(solution)/shard_map/ppermute | solution.py:55
  11.8 8.0 %copy-start = (s32[8]{0:T(128)S(1)}, s32[8]{0:T(128)}, u32[]{:S(2)}) copy-start(s32[8]{0:T(128)} %length_ref.3) | copy-start | bytes 100
  18.2 12.1 %collective-permute-start.3 = (bf16[64,2432]{1,0:T(8,128)(2,1)S(1)}, bf16[64,2432]{1,0:T(8,128)(2,1)}, u32[]{:S(2)}, u32[]{:S(2)}) collective-permute-start(bf16[64,2432]{1,0:T(8,128)(2,1)S(1)} %fusion.1), channel_id=1, source_target_pairs={{0,4},{1,3},{2,6},{3,1},{4,0},{5,7},{6,2},{7,5},{8,12},{9,11},{10,... | collective-permute-start | bytes 933896 | tf_op jit(solution)/shard_map/ppermute | solution.py:55
  20.0 12.8 %collective-permute-start.2 = (bf16[128,2304]{1,0:T(8,128)(2,1)S(1)}, bf16[128,2304]{1,0:T(8,128)(2,1)S(1)}, u32[]{:S(2)}, u32[]{:S(2)}) collective-permute-start(bf16[128,2304]{1,0:T(8,128)(2,1)S(1)} %get-tuple-element.44), channel_id=1, source_target_pairs={{0,2},{1,5},{2,0},{3,7},{4,6},{5,1},{6,4},{7,3},{8,10},{9,13},{10,... | collective-permute-start | bytes 1769480 | tf_op jit(solution)/shard_map/ppermute | solution.py:55
  31.3 8.0 %collective-permute-start.5 = (bf16[32,2432]{1,0:T(8,128)(2,1)S(1)}, bf16[32,2432]{1,0:T(8,128)(2,1)S(1)}, u32[]{:S(2)}, u32[]{:S(2)}) collective-permute-start(bf16[32,2432]{1,0:T(8,128)(2,1)S(1)} %slice.64), channel_id=1, source_target_pairs={{0,8},{1,9},{2,10},{3,11},{4,12},{5,13},{6,14},{7,15},{8,0},{9,1},... | collective-permute-start | bytes 466952 | tf_op jit(solution)/shard_map/ppermute | solution.py:55
  32.9 8.4 %collective-permute-start.4 = (bf16[64,2304]{1,0:T(8,128)(2,1)S(1)}, bf16[64,2304]{1,0:T(8,128)(2,1)S(1)}, u32[]{:S(2)}, u32[]{:S(2)}) collective-permute-start(bf16[64,2304]{1,0:T(8,128)(2,1)S(1)} %slice.63), channel_id=1, source_target_pairs={{0,4},{1,3},{2,6},{3,1},{4,0},{5,7},{6,2},{7,5},{8,12},{9,11},{10,... | collective-permute-start | bytes 884744 | tf_op jit(solution)/shard_map/ppermute | solution.py:55
  41.4 7.8 %collective-permute-start.6 = (bf16[32,2304]{1,0:T(8,128)(2,1)S(1)}, bf16[32,2304]{1,0:T(8,128)(2,1)S(1)}, u32[]{:S(2)}, u32[]{:S(2)}) collective-permute-start(bf16[32,2304]{1,0:T(8,128)(2,1)S(1)} %slice.65), channel_id=1, source_target_pairs={{0,8},{1,9},{2,10},{3,11},{4,12},{5,13},{6,14},{7,15},{8,0},{9,1},... | collective-permute-start | bytes 442376 | tf_op jit(solution)/shard_map/ppermute | solution.py:55
  46.4 9.9 %collective-permute-start.17 = (bf16[32,2048]{1,0:T(8,128)(2,1)S(1)}, bf16[32,2048]{1,0:T(8,128)(2,1)S(1)}, u32[]{:S(2)}, u32[]{:S(2)}) collective-permute-start(bf16[32,2048]{1,0:T(8,128)(2,1)S(1)} %get-tuple-element.56.refs_0_), channel_id=1, source_target_pairs={{0,2},{1,3},{2,0},{3,1},{4,6},{5,7},{6,4},{7,5},{8,10},{9,11},{10,... | collective-permute-start | bytes 393224 | tf_op jit(solution)/shard_map/ppermute | solution.py:55
  46.9 9.4 %collective-permute-start.15 = (bf16[32,2048]{1,0:T(8,128)(2,1)S(1)}, bf16[32,2048]{1,0:T(8,128)(2,1)S(1)}, u32[]{:S(2)}, u32[]{:S(2)}) collective-permute-start(bf16[32,2048]{1,0:T(8,128)(2,1)S(1)} %get-tuple-element.56.refs_0_), channel_id=1, source_target_pairs={{0,4},{1,5},{2,6},{3,7},{4,0},{5,1},{6,2},{7,3},{8,12},{9,13},{10,... | collective-permute-start | bytes 393224 | tf_op jit(solution)/shard_map/ppermute | solution.py:55
  49.2 9.1 %collective-permute-start.14 = (bf16[32,2048]{1,0:T(8,128)(2,1)S(1)}, bf16[32,2048]{1,0:T(8,128)(2,1)S(1)}, u32[]{:S(2)}, u32[]{:S(2)}) collective-permute-start(bf16[32,2048]{1,0:T(8,128)(2,1)S(1)} %get-tuple-element.56.refs_0_), channel_id=1, source_target_pairs={{0,8},{1,9},{2,10},{3,11},{4,12},{5,13},{6,14},{7,15},{8,0},{9,1},... | collective-permute-start | bytes 393224 | tf_op jit(solution)/shard_map/ppermute | solution.py:55
  52.5 8.7 %collective-permute-start.7 = (bf16[32,2048]{1,0:T(8,128)(2,1)S(1)}, bf16[32,2048]{1,0:T(8,128)(2,1)S(1)}, u32[]{:S(2)}, u32[]{:S(2)}) collective-permute-start(bf16[32,2048]{1,0:T(8,128)(2,1)S(1)} %attend.2.refs_0_), channel_id=1, source_target_pairs={{0,8},{1,9},{2,10},{3,11},{4,12},{5,13},{6,14},{7,15},{8,0},{9,1},... | collective-permute-start | bytes 393224 | tf_op jit(solution)/shard_map/ppermute | solution.py:55
  54.7 7.4 %collective-permute-start.10 = (bf16[32,2048]{1,0:T(8,128)(2,1)S(1)}, bf16[32,2048]{1,0:T(8,128)(2,1)S(1)}, u32[]{:S(2)}, u32[]{:S(2)}) collective-permute-start(bf16[32,2048]{1,0:T(8,128)(2,1)S(1)} %attend.2.refs_0_), channel_id=1, source_target_pairs={{0,2},{1,5},{2,0},{3,7},{4,6},{5,1},{6,4},{7,3},{8,10},{9,13},{10,... | collective-permute-start | bytes 393224 | tf_op jit(solution)/shard_map/ppermute | solution.py:55
  56.2 6.5 %collective-permute-start.8 = (bf16[32,2048]{1,0:T(8,128)(2,1)S(1)}, bf16[32,2048]{1,0:T(8,128)(2,1)S(1)}, u32[]{:S(2)}, u32[]{:S(2)}) collective-permute-start(bf16[32,2048]{1,0:T(8,128)(2,1)S(1)} %attend.2.refs_0_), channel_id=1, source_target_pairs={{0,4},{1,3},{2,6},{3,1},{4,0},{5,7},{6,2},{7,5},{8,12},{9,11},{10,... | collective-permute-start | bytes 393224 | tf_op jit(solution)/shard_map/ppermute | solution.py:55
  58.4 6.9 %collective-permute-start.16 = (bf16[32,2048]{1,0:T(8,128)(2,1)S(1)}, bf16[32,2048]{1,0:T(8,128)(2,1)S(1)}, u32[]{:S(2)}, u32[]{:S(2)}) collective-permute-start(bf16[32,2048]{1,0:T(8,128)(2,1)S(1)} %collective-permute-done.14.refs_1_), channel_id=1, source_target_pairs={{0,4},{1,5},{2,6},{3,7},{4,0},{5,1},{6,2},{7,3},{8,12},{9,13},{10,... | collective-permute-start | bytes 393224 | tf_op jit(solution)/shard_map/ppermute | solution.py:55
  58.8 8.3 %collective-permute-start.19 = (bf16[32,2048]{1,0:T(8,128)(2,1)S(1)}, bf16[32,2048]{1,0:T(8,128)(2,1)S(1)}, u32[]{:S(2)}, u32[]{:S(2)}) collective-permute-start(bf16[32,2048]{1,0:T(8,128)(2,1)S(1)} %collective-permute-done.15.refs_2_), channel_id=1, source_target_pairs={{0,2},{1,3},{2,0},{3,1},{4,6},{5,7},{6,4},{7,5},{8,10},{9,11},{10,... | collective-permute-start | bytes 393224 | tf_op jit(solution)/shard_map/ppermute | solution.py:55
  61.2 6.9 %collective-permute-start.9 = (bf16[32,2048]{1,0:T(8,128)(2,1)S(1)}, bf16[32,2048]{1,0:T(8,128)(2,1)S(1)}, u32[]{:S(2)}, u32[]{:S(2)}) collective-permute-start(bf16[32,2048]{1,0:T(8,128)(2,1)S(1)} %collective-permute-done.7.refs_1_), channel_id=1, source_target_pairs={{0,4},{1,3},{2,6},{3,1},{4,0},{5,7},{6,2},{7,5},{8,12},{9,11},{10,... | collective-permute-start | bytes 393224 | tf_op jit(solution)/shard_map/ppermute | solution.py:55
  62.7 10.4 %collective-permute-start.12 = (bf16[32,2048]{1,0:T(8,128)(2,1)S(1)}, bf16[32,2048]{1,0:T(8,128)(2,1)S(1)}, u32[]{:S(2)}, u32[]{:S(2)}) collective-permute-start(bf16[32,2048]{1,0:T(8,128)(2,1)S(1)} %collective-permute-done.8.refs_2_), channel_id=1, source_target_pairs={{0,2},{1,5},{2,0},{3,7},{4,6},{5,1},{6,4},{7,3},{8,10},{9,13},{10,... | collective-permute-start | bytes 393224 | tf_op jit(solution)/shard_map/ppermute | solution.py:55
  64.3 5.6 %collective-permute-start.18 = (bf16[32,2048]{1,0:T(8,128)(2,1)S(1)}, bf16[32,2048]{1,0:T(8,128)(2,1)S(1)}, u32[]{:S(2)}, u32[]{:S(2)}) collective-permute-start(bf16[32,2048]{1,0:T(8,128)(2,1)S(1)} %collective-permute-done.14.refs_1_), channel_id=1, source_target_pairs={{0,2},{1,3},{2,0},{3,1},{4,6},{5,7},{6,4},{7,5},{8,10},{9,11},{10,... | collective-permute-start | bytes 393224 | tf_op jit(solution)/shard_map/ppermute | solution.py:55
  65.3 5.4 %collective-permute-start.20 = (bf16[32,2048]{1,0:T(8,128)(2,1)S(1)}, bf16[32,2048]{1,0:T(8,128)(2,1)S(1)}, u32[]{:S(2)}, u32[]{:S(2)}) collective-permute-start(bf16[32,2048]{1,0:T(8,128)(2,1)S(1)} %collective-permute-done.16.refs_3_), channel_id=1, source_target_pairs={{0,2},{1,3},{2,0},{3,1},{4,6},{5,7},{6,4},{7,5},{8,10},{9,11},{10,... | collective-permute-start | bytes 393224 | tf_op jit(solution)/shard_map/ppermute | solution.py:55
  67.1 6.0 %collective-permute-start.11 = (bf16[32,2048]{1,0:T(8,128)(2,1)S(1)}, bf16[32,2048]{1,0:T(8,128)(2,1)S(1)}, u32[]{:S(2)}, u32[]{:S(2)}) collective-permute-start(bf16[32,2048]{1,0:T(8,128)(2,1)S(1)} %collective-permute-done.7.refs_1_), channel_id=1, source_target_pairs={{0,2},{1,5},{2,0},{3,7},{4,6},{5,1},{6,4},{7,3},{8,10},{9,13},{10,... | collective-permute-start | bytes 393224 | tf_op jit(solution)/shard_map/ppermute | solution.py:55
  68.1 5.4 %collective-permute-start.13 = (bf16[32,2048]{1,0:T(8,128)(2,1)S(1)}, bf16[32,2048]{1,0:T(8,128)(2,1)S(1)}, u32[]{:S(2)}, u32[]{:S(2)}) collective-permute-start(bf16[32,2048]{1,0:T(8,128)(2,1)S(1)} %collective-permute-done.9.refs_3_), channel_id=1, source_target_pairs={{0,2},{1,5},{2,0},{3,7},{4,6},{5,1},{6,4},{7,3},{8,10},{9,13},{10,... | collective-permute-start | bytes 393224 | tf_op jit(solution)/shard_map/ppermute | solution.py:55
  76.0 2.0 %collective-permute-start.21 = (bf16[128,2048]{1,0:T(8,128)(2,1)S(1)}, bf16[128,2048]{1,0:T(8,128)(2,1)S(1)}, u32[]{:S(2)}, u32[]{:S(2)}) collective-permute-start(bf16[128,2048]{1,0:T(8,128)(2,1)S(1)} %get-tuple-element.60), channel_id=1, source_target_pairs={{0,1},{1,0},{2,3},{3,2},{4,5},{5,4},{6,7},{7,6},{8,9},{9,8},{10,11... | collective-permute-start | bytes 1572872 | tf_op jit(solution)/shard_map/ppermute | solution.py:521

commit v19 on v18

--- a/solution.py
+++ b/solution.py
@@ -500,16 +500,25 @@
         )
         attentions.append(out[0])
         weights += out[1:]
+    early = {
+        1 << (levels - 1 - stage): exchange(
+            attentions[1], n, cores, stage, gather_orders(n, 1)
+        )
+        for stage in range(min(2, levels - 1))
+    }
     gathered = []
     for chunk in range(CHUNKS):
         slots = [attentions[chunk]]
         for slot in range(1, n):
+            if chunk == 1 and slot in early:
+                slots.append(early[slot])
+                continue
             top = slot.bit_length() - 1
             source = slots[slot - (1 << top)]
-            if slot == 1 and chunk == 0:
-                source = after(source, sums[1])
             if slot == 3 << (levels - 2):
                 source = after(source, slots[1 << (levels - 1)])
+            if chunk == 0 and slot == 3:
+                source = after(source, *early.values())
             slots.append(
                 exchange(source, n, cores, levels - 1 - top, gather_orders(n, chunk))
             )

time: 79 us -> 82.2 us (1.041)
  waiting for transfers between devices: 17.9 us -> 23.1 us
  starting transfers between devices: 26.4 us -> 24.4 us
    ppermute x21, waiting for transfers between devices: 16 us -> 21.2 us  [exchange(): return lax.ppermute(value, ('gx', 'gy'), pairs)]
    ppermute x21, starting transfers between devices: 26.3 us -> 24.3 us  [exchange(): return lax.ppermute(value, ('gx', 'gy'), pairs)]
  transfers between devices with their start and end apart: 22 -> 22, of which waited for: 13 -> 12; matrix products, arithmetic and copies ran while one was open for 2% -> 2% of each run, Pallas kernels for 32% -> 31%
where the time goes in v19:
time: 82.2 us; the launch traced here: 82 us
  Pallas kernels  31.6 us (38%)
  starting transfers between devices  24.4 us (30%)
  waiting for transfers between devices  23.1 us (28%)
  other arithmetic  2.58 us (3%)
    ppermute x21, starting transfers between devices, exchange(): return lax.ppermute(value, ('gx', 'gy'), pairs)  24.3 us
    ppermute x21, waiting for transfers between devices, exchange(): return lax.ppermute(value, ('gx', 'gy'), pairs)  21.2 us
    pallas_call x3, Pallas kernels, project(): pl.pallas_call(functools.partial(project_kernel, n, q_start, kv_start, fi...  13.2 us
    pallas_call x2, Pallas kernels, attend(): pl.pallas_call(functools.partial(attend_kernel, chunk, offsets, kv_offset...  6.51 us
    pallas_call x2, Pallas kernels, combine(): pl.pallas_call(functools.partial(combine_kernel, n, block, chunk), out_sh...  4.89 us
    pallas_call x1, Pallas kernels, fetch_rows(): pl.pallas_call(functools.partial(fetch_rows_kernel, start, pieces), out_s...  3.5 us
    pallas_call x1, Pallas kernels, fetch(): pl.pallas_call(functools.partial(fetch_kernel, len(arrays), pieces), out_...  3.47 us
    ppermute x1, waiting for transfers between devices, shards(): other = lax.ppermute(send, 'gy', [(0, 1), (1, 0)])  1.9 us
  transfers between devices with their start and end apart: 22, of which 12 were waited for; matrix products, arithmetic and copies ran while one was open for 2% of the time, Pallas kernels for 31%

profile of v19, /device:TPU:0, one launch (start us, length us, event | category | flops | bytes accessed | tf_op | source)
XLA Modules:
  0.0 82.0 jit_solution(14059329423575331649)
XLA Ops:
  0.0 4.0 %project.3 = (bf16[128,1152]{1,0:T(8,128)(2,1)S(1)}, f32[128,1152]{1,0:T(8,128)S(1)}, bf16[256,2048]{1,0:T(8,128)(2,1)S(1)}) custom-call(bf16[256,2048]{1,0:T(8,128)(2,1)} %refs_0_.1, f32[1,2048]{1,0:T(1,128)} %bitcast.1, bf16[2048,4096]{1,0:T(8,128)(2,1)} %refs_1_.3, bf16[2048,256]{1,0:T(8,128)(2,1)} %refs_2_.5, bf16[2048,256]{1,0:T(8,128)(2,1)} %refs_3_.5), custom_call_target="tpu_custom_call" | custom-call | tf_op jit(solution)/shard_map/project/pallas_call | solution.py:161
  4.0 3.0 %collective-permute-start = (bf16[128,1152]{1,0:T(8,128)(2,1)S(1)}, bf16[128,1152]{1,0:T(8,128)(2,1)S(1)}, u32[]{:S(2)}, u32[]{:S(2)}) collective-permute-start(bf16[128,1152]{1,0:T(8,128)(2,1)S(1)} %get-tuple-element.34), channel_id=1, source_target_pairs={{0,2},{1,5},{2,0},{3,7},{4,6},{5,1},{6,4},{7,3},{8,10},{9,13},{10,... | collective-permute-start | bytes 884744 | tf_op jit(solution)/shard_map/ppermute | solution.py:55
  7.0 3.9 %project.4 = (bf16[128,1280]{1,0:T(8,128)(2,1)S(1)}, f32[128,1280]{1,0:T(8,128)S(1)}) custom-call(bf16[256,2048]{1,0:T(8,128)(2,1)S(1)} %get-tuple-element.39.refs_0_, bf16[2048,4096]{1,0:T(8,128)(2,1)} %refs_1_.3, bf16[2048,256]{1,0:T(8,128)(2,1)} %refs_2_.5, bf16[2048,256]{1,0:T(8,128)(2,1)} %refs_3_.5), custom_call_target="tpu_custom_call" | custom-call | tf_op jit(solution)/shard_map/project/pallas_call | solution.py:161
  10.9 0.1 collective-permute-start.1
  11.0 0.7 collective-permute-done
  11.7 0.1 convert_add_fusion.2
  11.8 0.0 copy-start
  11.8 5.3 %project.5 = (bf16[128,2304]{1,0:T(8,128)(2,1)S(1)}, f32[128,2304]{1,0:T(8,128)S(1)}) custom-call(bf16[256,2048]{1,0:T(8,128)(2,1)S(1)} %get-tuple-element.39.refs_0_, bf16[2048,4096]{1,0:T(8,128)(2,1)} %refs_1_.3, bf16[2048,256]{1,0:T(8,128)(2,1)} %refs_2_.5, bf16[2048,256]{1,0:T(8,128)(2,1)} %refs_3_.5), custom_call_target="tpu_custom_call" | custom-call | tf_op jit(solution)/shard_map/project/pallas_call | solution.py:161
  17.1 0.9 %collective-permute-done.1 = bf16[128,1280]{1,0:T(8,128)(2,1)S(1)} collective-permute-done((bf16[128,1280]{1,0:T(8,128)(2,1)S(1)}, bf16[128,1280]{1,0:T(8,128)(2,1)S(1)}, u32[]{:S(2)}, u32[]{:S(2)}) %collective-permute-start.1) | collective-permute-done | bytes 327712 | tf_op jit(solution)/shard_map/ppermute | solution.py:55
  18.1 0.1 convert_add_fusion.1
  18.2 1.6 %collective-permute-start.3 = (bf16[64,2432]{1,0:T(8,128)(2,1)S(1)}, bf16[64,2432]{1,0:T(8,128)(2,1)}, u32[]{:S(2)}, u32[]{:S(2)}) collective-permute-start(bf16[64,2432]{1,0:T(8,128)(2,1)S(1)} %fusion.1), channel_id=1, source_target_pairs={{0,4},{1,3},{2,6},{3,1},{4,0},{5,7},{6,2},{7,5},{8,12},{9,11},{10,... | collective-permute-start | bytes 933896 | tf_op jit(solution)/shard_map/ppermute | solution.py:55
  19.8 0.1 add_convert_fusion.1
  19.9 0.1 convert_element_type.49
  20.0 1.2 %collective-permute-start.2 = (bf16[128,2304]{1,0:T(8,128)(2,1)S(1)}, bf16[128,2304]{1,0:T(8,128)(2,1)S(1)}, u32[]{:S(2)}, u32[]{:S(2)}) collective-permute-start(bf16[128,2304]{1,0:T(8,128)(2,1)S(1)} %get-tuple-element.44), channel_id=1, source_target_pairs={{0,2},{1,5},{2,0},{3,7},{4,6},{5,1},{6,4},{7,3},{8,10},{9,13},{10,... | collective-permute-start | bytes 1769480 | tf_op jit(solution)/shard_map/ppermute | solution.py:55
  21.1 3.5 %fetch_rows.1.refs_8_ = bf16[2048,2048]{1,0:T(8,128)(2,1)S(1)} custom-call(bf16[4096,2048]{1,0:T(8,128)(2,1)} %refs_6_.1), custom_call_target="tpu_custom_call" | custom-call | tf_op jit(solution)/shard_map/fetch_rows/pallas_call | solution.py:343
  24.6 5.6 %collective-permute-done.3 = bf16[64,2432]{1,0:T(8,128)(2,1)} collective-permute-done((bf16[64,2432]{1,0:T(8,128)(2,1)S(1)}, bf16[64,2432]{1,0:T(8,128)(2,1)}, u32[]{:S(2)}, u32[]{:S(2)}) %collective-permute-start.3) | collective-permute-done | bytes 311328 | tf_op jit(solution)/shard_map/ppermute | solution.py:55
  30.2 1.0 %fusion.2 = f32[64,2432]{1,0:T(8,128)S(1)} fusion(f32[128,1280]{1,0:T(8,128)S(1)} %convert_add_fusion.1, f32[128,1152]{1,0:T(8,128)S(1)} %convert_add_fusion.2, bf16[64,2432]{1,0:T(8,128)(2,1)} %collective-permute-done.3), kind=kLoop, calls=%fused_computation.8 | loop fusion | flops 466944 | bytes 2179072 | tf_op jit(solution)/shard_map/add | solution.py:462
  31.3 1.5 %collective-permute-start.5 = (bf16[32,2432]{1,0:T(8,128)(2,1)S(1)}, bf16[32,2432]{1,0:T(8,128)(2,1)S(1)}, u32[]{:S(2)}, u32[]{:S(2)}) collective-permute-start(bf16[32,2432]{1,0:T(8,128)(2,1)S(1)} %slice.64), channel_id=1, source_target_pairs={{0,8},{1,9},{2,10},{3,11},{4,12},{5,13},{6,14},{7,15},{8,0},{9,1},... | collective-permute-start | bytes 466952 | tf_op jit(solution)/shard_map/ppermute | solution.py:55
  32.8 0.0 collective-permute-done.2
  32.8 0.1 convert_add_fusion
  32.9 2.8 %collective-permute-start.4 = (bf16[64,2304]{1,0:T(8,128)(2,1)S(1)}, bf16[64,2304]{1,0:T(8,128)(2,1)S(1)}, u32[]{:S(2)}, u32[]{:S(2)}) collective-permute-start(bf16[64,2304]{1,0:T(8,128)(2,1)S(1)} %slice.63), channel_id=1, source_target_pairs={{0,4},{1,3},{2,6},{3,1},{4,0},{5,7},{6,2},{7,5},{8,12},{9,11},{10,... | collective-permute-start | bytes 884744 | tf_op jit(solution)/shard_map/ppermute | solution.py:55
  35.7 3.5 %fetch.1 = (bf16[8,1024,256]{2,1,0:T(8,128)(2,1)S(1)}, bf16[8,1024,256]{2,1,0:T(8,128)(2,1)S(1)}) custom-call(bf16[8,1024,256]{2,1,0:T(8,128)(2,1)} %refs_0_.2, bf16[8,1024,256]{2,1,0:T(8,128)(2,1)} %refs_1_.4), custom_call_target="tpu_custom_call" | custom-call | tf_op jit(solution)/shard_map/fetch/pallas_call | solution.py:314
  39.2 0.0 collective-permute-done.5
  39.3 2.0 %collective-permute-done.4 = bf16[64,2304]{1,0:T(8,128)(2,1)S(1)} collective-permute-done((bf16[64,2304]{1,0:T(8,128)(2,1)S(1)}, bf16[64,2304]{1,0:T(8,128)(2,1)S(1)}, u32[]{:S(2)}, u32[]{:S(2)}) %collective-permute-start.4) | collective-permute-done | bytes 294944 | tf_op jit(solution)/shard_map/ppermute | solution.py:55
  41.3 0.1 slice_add_fusion
  41.4 0.7 collective-permute-start.6
  42.1 0.1 fusion.3
  42.2 0.1 pad_maximum_fusion.1
  42.3 4.0 %attend.3 = (bf16[32,2048]{1,0:T(8,128)(2,1)S(1)}, bf16[2048,2048]{1,0:T(8,128)(2,1)S(1)}) custom-call(s32[8]{0:T(128)S(1)} %copy-done, f32[32,2432]{1,0:T(8,128)S(1)} %slice_add_fusion.1.refs_0_, f32[32,128]{1,0:T(8,128)S(1)} %slice.48.refs_1_, f32[32,128]{1,0:T(8,128)S(1)} %get-tuple-element.64.refs_2_, f32[32,128]{1,0:T(8,128)S(1)} %get-tuple-element.65.refs_3_, ...), custom_call_target="tpu_custom_call" | custom-call | tf_op jit(solution)/shard_map/attend/pallas_call | solution.py:281
  46.4 0.5 collective-permute-start.17
  46.9 1.9 %collective-permute-start.15 = (bf16[32,2048]{1,0:T(8,128)(2,1)S(1)}, bf16[32,2048]{1,0:T(8,128)(2,1)S(1)}, u32[]{:S(2)}, u32[]{:S(2)}) collective-permute-start(bf16[32,2048]{1,0:T(8,128)(2,1)S(1)} %get-tuple-element.55.refs_0_), channel_id=1, source_target_pairs={{0,4},{1,5},{2,6},{3,7},{4,0},{5,1},{6,2},{7,3},{8,12},{9,13},{10,... | collective-permute-start | bytes 393224 | tf_op jit(solution)/shard_map/ppermute | solution.py:55
  48.7 1.2 %collective-permute-start.14 = (bf16[32,2048]{1,0:T(8,128)(2,1)S(1)}, bf16[32,2048]{1,0:T(8,128)(2,1)S(1)}, u32[]{:S(2)}, u32[]{:S(2)}) collective-permute-start(bf16[32,2048]{1,0:T(8,128)(2,1)S(1)} %get-tuple-element.55.refs_0_), channel_id=1, source_target_pairs={{0,8},{1,9},{2,10},{3,11},{4,12},{5,13},{6,14},{7,15},{8,0},{9,1},... | collective-permute-start | bytes 393224 | tf_op jit(solution)/shard_map/ppermute | solution.py:55
  50.0 0.0 collective-permute-done.6
  50.0 2.5 %attend.2.refs_0_ = bf16[32,2048]{1,0:T(8,128)(2,1)S(1)} custom-call(s32[8]{0:T(128)S(1)} %copy-done, f32[32,2304]{1,0:T(8,128)S(1)} %slice_add_fusion.2.refs_0_, f32[32,128]{1,0:T(8,128)S(1)} %slice.48.refs_1_, f32[32,128]{1,0:T(8,128)S(1)} %get-tuple-element.64.refs_2_, f32[32,128]{1,0:T(8,128)S(1)} %get-tuple-element.65.refs_3_, ...), custom_call_target="tpu_custom_call" | custom-call | tf_op jit(solution)/shard_map/attend/pallas_call | solution.py:281
  52.5 2.0 %collective-permute-start.10 = (bf16[32,2048]{1,0:T(8,128)(2,1)S(1)}, bf16[32,2048]{1,0:T(8,128)(2,1)S(1)}, u32[]{:S(2)}, u32[]{:S(2)}) collective-permute-start(bf16[32,2048]{1,0:T(8,128)(2,1)S(1)} %attend.2.refs_0_), channel_id=1, source_target_pairs={{0,2},{1,5},{2,0},{3,7},{4,6},{5,1},{6,4},{7,3},{8,10},{9,13},{10,... | collective-permute-start | bytes 393224 | tf_op jit(solution)/shard_map/ppermute | solution.py:55
  54.5 0.9 %collective-permute-start.8 = (bf16[32,2048]{1,0:T(8,128)(2,1)S(1)}, bf16[32,2048]{1,0:T(8,128)(2,1)S(1)}, u32[]{:S(2)}, u32[]{:S(2)}) collective-permute-start(bf16[32,2048]{1,0:T(8,128)(2,1)S(1)} %attend.2.refs_0_), channel_id=1, source_target_pairs={{0,4},{1,3},{2,6},{3,1},{4,0},{5,7},{6,2},{7,5},{8,12},{9,11},{10,... | collective-permute-start | bytes 393224 | tf_op jit(solution)/shard_map/ppermute | solution.py:55
  55.4 0.0 collective-permute-done.17.refs_4_
  55.4 0.8 %collective-permute-start.7 = (bf16[32,2048]{1,0:T(8,128)(2,1)S(1)}, bf16[32,2048]{1,0:T(8,128)(2,1)S(1)}, u32[]{:S(2)}, u32[]{:S(2)}) collective-permute-start(bf16[32,2048]{1,0:T(8,128)(2,1)S(1)} %attend.2.refs_0_), channel_id=1, source_target_pairs={{0,8},{1,9},{2,10},{3,11},{4,12},{5,13},{6,14},{7,15},{8,0},{9,1},... | collective-permute-start | bytes 393224 | tf_op jit(solution)/shard_map/ppermute | solution.py:55
  56.2 0.0 collective-permute-done.15.refs_2_
  56.2 0.1 collective-permute-done.14.refs_1_
  56.3 1.2 %collective-permute-done.10.refs_4_ = bf16[32,2048]{1,0:T(8,128)(2,1)S(1)} collective-permute-done((bf16[32,2048]{1,0:T(8,128)(2,1)S(1)}, bf16[32,2048]{1,0:T(8,128)(2,1)S(1)}, u32[]{:S(2)}, u32[]{:S(2)}) %collective-permute-start.10) | collective-permute-done | bytes 131104 | tf_op jit(solution)/shard_map/ppermute | solution.py:55
  57.5 5.0 %collective-permute-done.8.refs_2_ = bf16[32,2048]{1,0:T(8,128)(2,1)S(1)} collective-permute-done((bf16[32,2048]{1,0:T(8,128)(2,1)S(1)}, bf16[32,2048]{1,0:T(8,128)(2,1)S(1)}, u32[]{:S(2)}, u32[]{:S(2)}) %collective-permute-start.8) | collective-permute-done | bytes 131104 | tf_op jit(solution)/shard_map/ppermute | solution.py:55
  62.5 0.0 collective-permute-start.16
  62.5 0.0 collective-permute-start.19
  62.5 0.0 collective-permute-done.7.refs_1_
  62.5 2.0 %collective-permute-start.9 = (bf16[32,2048]{1,0:T(8,128)(2,1)S(1)}, bf16[32,2048]{1,0:T(8,128)(2,1)S(1)}, u32[]{:S(2)}, u32[]{:S(2)}) collective-permute-start(bf16[32,2048]{1,0:T(8,128)(2,1)S(1)} %collective-permute-done.7.refs_1_), channel_id=1, source_target_pairs={{0,4},{1,3},{2,6},{3,1},{4,0},{5,7},{6,2},{7,5},{8,12},{9,11},{10,... | collective-permute-start | bytes 393224 | tf_op jit(solution)/shard_map/ppermute | solution.py:55
  64.5 2.0 %collective-permute-start.18 = (bf16[32,2048]{1,0:T(8,128)(2,1)S(1)}, bf16[32,2048]{1,0:T(8,128)(2,1)S(1)}, u32[]{:S(2)}, u32[]{:S(2)}) collective-permute-start(bf16[32,2048]{1,0:T(8,128)(2,1)S(1)} %collective-permute-done.14.refs_1_), channel_id=1, source_target_pairs={{0,2},{1,3},{2,0},{3,1},{4,6},{5,7},{6,4},{7,5},{8,10},{9,11},{10,... | collective-permute-start | bytes 393224 | tf_op jit(solution)/shard_map/ppermute | solution.py:55
  66.6 0.0 collective-permute-start.12
  66.6 2.3 %collective-permute-done.16.refs_3_ = bf16[32,2048]{1,0:T(8,128)(2,1)S(1)} collective-permute-done((bf16[32,2048]{1,0:T(8,128)(2,1)S(1)}, bf16[32,2048]{1,0:T(8,128)(2,1)S(1)}, u32[]{:S(2)}, u32[]{:S(2)}) %collective-permute-start.16) | collective-permute-done | bytes 131104 | tf_op jit(solution)/shard_map/ppermute | solution.py:55
  68.9 0.0 collective-permute-start.20
  68.9 0.0 collective-permute-done.19.refs_6_
  68.9 2.0 %collective-permute-start.11 = (bf16[32,2048]{1,0:T(8,128)(2,1)S(1)}, bf16[32,2048]{1,0:T(8,128)(2,1)S(1)}, u32[]{:S(2)}, u32[]{:S(2)}) collective-permute-start(bf16[32,2048]{1,0:T(8,128)(2,1)S(1)} %collective-permute-done.7.refs_1_), channel_id=1, source_target_pairs={{0,2},{1,5},{2,0},{3,7},{4,6},{5,1},{6,4},{7,3},{8,10},{9,13},{10,... | collective-permute-start | bytes 393224 | tf_op jit(solution)/shard_map/ppermute | solution.py:55
  70.9 0.5 collective-permute-done.9.refs_3_
  71.4 0.0 collective-permute-start.13
  71.4 0.0 collective-permute-done.18.refs_5_
  71.4 2.4 %collective-permute-done.20.refs_7_ = bf16[32,2048]{1,0:T(8,128)(2,1)S(1)} collective-permute-done((bf16[32,2048]{1,0:T(8,128)(2,1)S(1)}, bf16[32,2048]{1,0:T(8,128)(2,1)S(1)}, u32[]{:S(2)}, u32[]{:S(2)}) %collective-permute-start.20) | collective-permute-done | bytes 131104 | tf_op jit(solution)/shard_map/ppermute | solution.py:55
  73.8 2.4 %combine.2.refs_8_ = f32[256,2048]{1,0:T(8,128)S(1)} custom-call(bf16[32,2048]{1,0:T(8,128)(2,1)S(1)} %get-tuple-element.55.refs_0_, bf16[32,2048]{1,0:T(8,128)(2,1)S(1)} %collective-permute-done.14.refs_1_, bf16[32,2048]{1,0:T(8,128)(2,1)S(1)} %collective-permute-done.15.refs_2_, bf16[32,2048]{1,0:T(8,128)(2,1)S(1)} %collective-permute-done.16.refs_3_, ...), custom_call_target="tpu_custom_call" | custom-call | tf_op jit(solution)/shard_map/combine/pallas_call | solution.py:396
  76.3 0.0 collective-permute-done.12.refs_6_
  76.3 0.0 collective-permute-done.11.refs_5_
  76.3 0.4 collective-permute-done.13.refs_7_
  76.7 2.5 %combine.3 = (bf16[128,2048]{1,0:T(8,128)(2,1)S(1)}, f32[128,2048]{1,0:T(8,128)S(1)}) custom-call(bf16[32,2048]{1,0:T(8,128)(2,1)S(1)} %attend.2.refs_0_, bf16[32,2048]{1,0:T(8,128)(2,1)S(1)} %collective-permute-done.7.refs_1_, bf16[32,2048]{1,0:T(8,128)(2,1)S(1)} %collective-permute-done.8.refs_2_, bf16[32,2048]{1,0:T(8,128)(2,1)S(1)} %collective-permute-done.9.refs_3_, ...), custom_call_target="tpu_custom_call" | custom-call | tf_op jit(solution)/shard_map/combine/pallas_call | solution.py:396
  79.1 0.1 collective-permute-start.21
  79.2 1.9 %collective-permute-done.21 = bf16[128,2048]{1,0:T(8,128)(2,1)S(1)} collective-permute-done((bf16[128,2048]{1,0:T(8,128)(2,1)S(1)}, bf16[128,2048]{1,0:T(8,128)(2,1)S(1)}, u32[]{:S(2)}, u32[]{:S(2)}) %collective-permute-start.21) | collective-permute-done | bytes 524320 | tf_op jit(solution)/shard_map/ppermute | solution.py:530
  81.1 0.9 %add_convert_fusion = bf16[128,2048]{1,0:T(8,128)(2,1)} fusion(f32[128,2048]{1,0:T(8,128)S(1)} %get-tuple-element.59, bf16[128,2048]{1,0:T(8,128)(2,1)S(1)} %collective-permute-done.21), kind=kLoop, calls=%fused_computation.3 | loop fusion | flops 786432 | bytes 2097152 | tf_op jit(solution)/shard_map/convert_element_type | solution.py:531
  (9 shorter events, 0.2 us)
Async XLA Ops:
  4.0 7.7 %collective-permute-start = (bf16[128,1152]{1,0:T(8,128)(2,1)S(1)}, bf16[128,1152]{1,0:T(8,128)(2,1)S(1)}, u32[]{:S(2)}, u32[]{:S(2)}) collective-permute-start(bf16[128,1152]{1,0:T(8,128)(2,1)S(1)} %get-tuple-element.34), channel_id=1, source_target_pairs={{0,2},{1,5},{2,0},{3,7},{4,6},{5,1},{6,4},{7,3},{8,10},{9,13},{10,... | collective-permute-start | bytes 884744 | tf_op jit(solution)/shard_map/ppermute | solution.py:55
  10.9 7.1 %collective-permute-start.1 = (bf16[128,1280]{1,0:T(8,128)(2,1)S(1)}, bf16[128,1280]{1,0:T(8,128)(2,1)S(1)}, u32[]{:S(2)}, u32[]{:S(2)}) collective-permute-start(bf16[128,1280]{1,0:T(8,128)(2,1)S(1)} %get-tuple-element.36), channel_id=1, source_target_pairs={{0,2},{1,5},{2,0},{3,7},{4,6},{5,1},{6,4},{7,3},{8,10},{9,13},{10,... | collective-permute-start | bytes 983048 | tf_op jit(solution)/shard_map/ppermute | solution.py:55
  11.8 8.0 %copy-start = (s32[8]{0:T(128)S(1)}, s32[8]{0:T(128)}, u32[]{:S(2)}) copy-start(s32[8]{0:T(128)} %length_ref.3) | copy-start | bytes 100
  18.2 12.1 %collective-permute-start.3 = (bf16[64,2432]{1,0:T(8,128)(2,1)S(1)}, bf16[64,2432]{1,0:T(8,128)(2,1)}, u32[]{:S(2)}, u32[]{:S(2)}) collective-permute-start(bf16[64,2432]{1,0:T(8,128)(2,1)S(1)} %fusion.1), channel_id=1, source_target_pairs={{0,4},{1,3},{2,6},{3,1},{4,0},{5,7},{6,2},{7,5},{8,12},{9,11},{10,... | collective-permute-start | bytes 933896 | tf_op jit(solution)/shard_map/ppermute | solution.py:55
  20.0 12.8 %collective-permute-start.2 = (bf16[128,2304]{1,0:T(8,128)(2,1)S(1)}, bf16[128,2304]{1,0:T(8,128)(2,1)S(1)}, u32[]{:S(2)}, u32[]{:S(2)}) collective-permute-start(bf16[128,2304]{1,0:T(8,128)(2,1)S(1)} %get-tuple-element.44), channel_id=1, source_target_pairs={{0,2},{1,5},{2,0},{3,7},{4,6},{5,1},{6,4},{7,3},{8,10},{9,13},{10,... | collective-permute-start | bytes 1769480 | tf_op jit(solution)/shard_map/ppermute | solution.py:55
  31.3 8.0 %collective-permute-start.5 = (bf16[32,2432]{1,0:T(8,128)(2,1)S(1)}, bf16[32,2432]{1,0:T(8,128)(2,1)S(1)}, u32[]{:S(2)}, u32[]{:S(2)}) collective-permute-start(bf16[32,2432]{1,0:T(8,128)(2,1)S(1)} %slice.64), channel_id=1, source_target_pairs={{0,8},{1,9},{2,10},{3,11},{4,12},{5,13},{6,14},{7,15},{8,0},{9,1},... | collective-permute-start | bytes 466952 | tf_op jit(solution)/shard_map/ppermute | solution.py:55
  32.9 8.4 %collective-permute-start.4 = (bf16[64,2304]{1,0:T(8,128)(2,1)S(1)}, bf16[64,2304]{1,0:T(8,128)(2,1)S(1)}, u32[]{:S(2)}, u32[]{:S(2)}) collective-permute-start(bf16[64,2304]{1,0:T(8,128)(2,1)S(1)} %slice.63), channel_id=1, source_target_pairs={{0,4},{1,3},{2,6},{3,1},{4,0},{5,7},{6,2},{7,5},{8,12},{9,11},{10,... | collective-permute-start | bytes 884744 | tf_op jit(solution)/shard_map/ppermute | solution.py:55
  41.4 8.6 %collective-permute-start.6 = (bf16[32,2304]{1,0:T(8,128)(2,1)S(1)}, bf16[32,2304]{1,0:T(8,128)(2,1)S(1)}, u32[]{:S(2)}, u32[]{:S(2)}) collective-permute-start(bf16[32,2304]{1,0:T(8,128)(2,1)S(1)} %slice.65), channel_id=1, source_target_pairs={{0,8},{1,9},{2,10},{3,11},{4,12},{5,13},{6,14},{7,15},{8,0},{9,1},... | collective-permute-start | bytes 442376 | tf_op jit(solution)/shard_map/ppermute | solution.py:55
  46.4 9.0 %collective-permute-start.17 = (bf16[32,2048]{1,0:T(8,128)(2,1)S(1)}, bf16[32,2048]{1,0:T(8,128)(2,1)S(1)}, u32[]{:S(2)}, u32[]{:S(2)}) collective-permute-start(bf16[32,2048]{1,0:T(8,128)(2,1)S(1)} %get-tuple-element.55.refs_0_), channel_id=1, source_target_pairs={{0,2},{1,3},{2,0},{3,1},{4,6},{5,7},{6,4},{7,5},{8,10},{9,11},{10,... | collective-permute-start | bytes 393224 | tf_op jit(solution)/shard_map/ppermute | solution.py:55
  46.9 9.3 %collective-permute-start.15 = (bf16[32,2048]{1,0:T(8,128)(2,1)S(1)}, bf16[32,2048]{1,0:T(8,128)(2,1)S(1)}, u32[]{:S(2)}, u32[]{:S(2)}) collective-permute-start(bf16[32,2048]{1,0:T(8,128)(2,1)S(1)} %get-tuple-element.55.refs_0_), channel_id=1, source_target_pairs={{0,4},{1,5},{2,6},{3,7},{4,0},{5,1},{6,2},{7,3},{8,12},{9,13},{10,... | collective-permute-start | bytes 393224 | tf_op jit(solution)/shard_map/ppermute | solution.py:55
  48.7 7.6 %collective-permute-start.14 = (bf16[32,2048]{1,0:T(8,128)(2,1)S(1)}, bf16[32,2048]{1,0:T(8,128)(2,1)S(1)}, u32[]{:S(2)}, u32[]{:S(2)}) collective-permute-start(bf16[32,2048]{1,0:T(8,128)(2,1)S(1)} %get-tuple-element.55.refs_0_), channel_id=1, source_target_pairs={{0,8},{1,9},{2,10},{3,11},{4,12},{5,13},{6,14},{7,15},{8,0},{9,1},... | collective-permute-start | bytes 393224 | tf_op jit(solution)/shard_map/ppermute | solution.py:55
  52.5 5.0 %collective-permute-start.10 = (bf16[32,2048]{1,0:T(8,128)(2,1)S(1)}, bf16[32,2048]{1,0:T(8,128)(2,1)S(1)}, u32[]{:S(2)}, u32[]{:S(2)}) collective-permute-start(bf16[32,2048]{1,0:T(8,128)(2,1)S(1)} %attend.2.refs_0_), channel_id=1, source_target_pairs={{0,2},{1,5},{2,0},{3,7},{4,6},{5,1},{6,4},{7,3},{8,10},{9,13},{10,... | collective-permute-start | bytes 393224 | tf_op jit(solution)/shard_map/ppermute | solution.py:55
  54.5 8.0 %collective-permute-start.8 = (bf16[32,2048]{1,0:T(8,128)(2,1)S(1)}, bf16[32,2048]{1,0:T(8,128)(2,1)S(1)}, u32[]{:S(2)}, u32[]{:S(2)}) collective-permute-start(bf16[32,2048]{1,0:T(8,128)(2,1)S(1)} %attend.2.refs_0_), channel_id=1, source_target_pairs={{0,4},{1,3},{2,6},{3,1},{4,0},{5,7},{6,2},{7,5},{8,12},{9,11},{10,... | collective-permute-start | bytes 393224 | tf_op jit(solution)/shard_map/ppermute | solution.py:55
  55.4 7.2 %collective-permute-start.7 = (bf16[32,2048]{1,0:T(8,128)(2,1)S(1)}, bf16[32,2048]{1,0:T(8,128)(2,1)S(1)}, u32[]{:S(2)}, u32[]{:S(2)}) collective-permute-start(bf16[32,2048]{1,0:T(8,128)(2,1)S(1)} %attend.2.refs_0_), channel_id=1, source_target_pairs={{0,8},{1,9},{2,10},{3,11},{4,12},{5,13},{6,14},{7,15},{8,0},{9,1},... | collective-permute-start | bytes 393224 | tf_op jit(solution)/shard_map/ppermute | solution.py:55
  62.5 6.4 %collective-permute-start.16 = (bf16[32,2048]{1,0:T(8,128)(2,1)S(1)}, bf16[32,2048]{1,0:T(8,128)(2,1)S(1)}, u32[]{:S(2)}, u32[]{:S(2)}) collective-permute-start(bf16[32,2048]{1,0:T(8,128)(2,1)S(1)} %collective-permute-done.14.refs_1_), channel_id=1, source_target_pairs={{0,4},{1,5},{2,6},{3,7},{4,0},{5,1},{6,2},{7,3},{8,12},{9,13},{10,... | collective-permute-start | bytes 393224 | tf_op jit(solution)/shard_map/ppermute | solution.py:55
  62.5 6.4 %collective-permute-start.19 = (bf16[32,2048]{1,0:T(8,128)(2,1)S(1)}, bf16[32,2048]{1,0:T(8,128)(2,1)S(1)}, u32[]{:S(2)}, u32[]{:S(2)}) collective-permute-start(bf16[32,2048]{1,0:T(8,128)(2,1)S(1)} %collective-permute-done.15.refs_2_), channel_id=1, source_target_pairs={{0,2},{1,3},{2,0},{3,1},{4,6},{5,7},{6,4},{7,5},{8,10},{9,11},{10,... | collective-permute-start | bytes 393224 | tf_op jit(solution)/shard_map/ppermute | solution.py:55
  62.5 8.9 %collective-permute-start.9 = (bf16[32,2048]{1,0:T(8,128)(2,1)S(1)}, bf16[32,2048]{1,0:T(8,128)(2,1)S(1)}, u32[]{:S(2)}, u32[]{:S(2)}) collective-permute-start(bf16[32,2048]{1,0:T(8,128)(2,1)S(1)} %collective-permute-done.7.refs_1_), channel_id=1, source_target_pairs={{0,4},{1,3},{2,6},{3,1},{4,0},{5,7},{6,2},{7,5},{8,12},{9,11},{10,... | collective-permute-start | bytes 393224 | tf_op jit(solution)/shard_map/ppermute | solution.py:55
  64.5 6.9 %collective-permute-start.18 = (bf16[32,2048]{1,0:T(8,128)(2,1)S(1)}, bf16[32,2048]{1,0:T(8,128)(2,1)S(1)}, u32[]{:S(2)}, u32[]{:S(2)}) collective-permute-start(bf16[32,2048]{1,0:T(8,128)(2,1)S(1)} %collective-permute-done.14.refs_1_), channel_id=1, source_target_pairs={{0,2},{1,3},{2,0},{3,1},{4,6},{5,7},{6,4},{7,5},{8,10},{9,11},{10,... | collective-permute-start | bytes 393224 | tf_op jit(solution)/shard_map/ppermute | solution.py:55
  66.6 9.7 %collective-permute-start.12 = (bf16[32,2048]{1,0:T(8,128)(2,1)S(1)}, bf16[32,2048]{1,0:T(8,128)(2,1)S(1)}, u32[]{:S(2)}, u32[]{:S(2)}) collective-permute-start(bf16[32,2048]{1,0:T(8,128)(2,1)S(1)} %collective-permute-done.8.refs_2_), channel_id=1, source_target_pairs={{0,2},{1,5},{2,0},{3,7},{4,6},{5,1},{6,4},{7,3},{8,10},{9,13},{10,... | collective-permute-start | bytes 393224 | tf_op jit(solution)/shard_map/ppermute | solution.py:55
  68.9 5.0 %collective-permute-start.20 = (bf16[32,2048]{1,0:T(8,128)(2,1)S(1)}, bf16[32,2048]{1,0:T(8,128)(2,1)S(1)}, u32[]{:S(2)}, u32[]{:S(2)}) collective-permute-start(bf16[32,2048]{1,0:T(8,128)(2,1)S(1)} %collective-permute-done.16.refs_3_), channel_id=1, source_target_pairs={{0,2},{1,3},{2,0},{3,1},{4,6},{5,7},{6,4},{7,5},{8,10},{9,11},{10,... | collective-permute-start | bytes 393224 | tf_op jit(solution)/shard_map/ppermute | solution.py:55
  68.9 7.4 %collective-permute-start.11 = (bf16[32,2048]{1,0:T(8,128)(2,1)S(1)}, bf16[32,2048]{1,0:T(8,128)(2,1)S(1)}, u32[]{:S(2)}, u32[]{:S(2)}) collective-permute-start(bf16[32,2048]{1,0:T(8,128)(2,1)S(1)} %collective-permute-done.7.refs_1_), channel_id=1, source_target_pairs={{0,2},{1,5},{2,0},{3,7},{4,6},{5,1},{6,4},{7,3},{8,10},{9,13},{10,... | collective-permute-start | bytes 393224 | tf_op jit(solution)/shard_map/ppermute | solution.py:55
  71.4 5.2 %collective-permute-start.13 = (bf16[32,2048]{1,0:T(8,128)(2,1)S(1)}, bf16[32,2048]{1,0:T(8,128)(2,1)S(1)}, u32[]{:S(2)}, u32[]{:S(2)}) collective-permute-start(bf16[32,2048]{1,0:T(8,128)(2,1)S(1)} %collective-permute-done.9.refs_3_), channel_id=1, source_target_pairs={{0,2},{1,5},{2,0},{3,7},{4,6},{5,1},{6,4},{7,3},{8,10},{9,13},{10,... | collective-permute-start | bytes 393224 | tf_op jit(solution)/shard_map/ppermute | solution.py:55
  79.1 2.0 %collective-permute-start.21 = (bf16[128,2048]{1,0:T(8,128)(2,1)S(1)}, bf16[128,2048]{1,0:T(8,128)(2,1)S(1)}, u32[]{:S(2)}, u32[]{:S(2)}) collective-permute-start(bf16[128,2048]{1,0:T(8,128)(2,1)S(1)} %get-tuple-element.60), channel_id=1, source_target_pairs={{0,1},{1,0},{2,3},{3,2},{4,5},{5,4},{6,7},{7,6},{8,9},{9,8},{10,11... | collective-permute-start | bytes 1572872 | tf_op jit(solution)/shard_map/ppermute | solution.py:530

commit v20 on v18

--- a/solution.py
+++ b/solution.py
@@ -15,7 +15,7 @@
 THETA = 500000.0
 
 CHUNKS = 2
-TILES = 2
+TILES = 1
 MIB = 1 << 20
 
 

time: 79 us -> 79 us (level)
  no operation moved by 1% of the time
where the time goes in v20:
time: 79 us; the launch traced here: 78.8 us
  Pallas kernels  31.5 us (40%)
  starting transfers between devices  26.4 us (33%)
  waiting for transfers between devices  17.9 us (23%)
  other arithmetic  2.58 us (3%)
    ppermute x21, starting transfers between devices, exchange(): return lax.ppermute(value, ('gx', 'gy'), pairs)  26.3 us
    ppermute x21, waiting for transfers between devices, exchange(): return lax.ppermute(value, ('gx', 'gy'), pairs)  16 us
    pallas_call x3, Pallas kernels, project(): pl.pallas_call(functools.partial(project_kernel, n, q_start, kv_start, fi...  13.2 us
    pallas_call x2, Pallas kernels, attend(): pl.pallas_call(functools.partial(attend_kernel, chunk, offsets, kv_offset...  6.52 us
    pallas_call x2, Pallas kernels, combine(): pl.pallas_call(functools.partial(combine_kernel, n, block, chunk), out_sh...  4.87 us
    pallas_call x1, Pallas kernels, fetch_rows(): pl.pallas_call(functools.partial(fetch_rows_kernel, start, pieces), out_s...  3.5 us
    pallas_call x1, Pallas kernels, fetch(): pl.pallas_call(functools.partial(fetch_kernel, len(arrays), pieces), out_...  3.47 us
    ppermute x1, waiting for transfers between devices, shards(): other = lax.ppermute(send, 'gy', [(0, 1), (1, 0)])  1.9 us
  transfers between devices with their start and end apart: 22, of which 13 were waited for; matrix products, arithmetic and copies ran while one was open for 2% of the time, Pallas kernels for 32%

profile of v20, /device:TPU:0, one launch (start us, length us, event | category | flops | bytes accessed | tf_op | source)
XLA Modules:
  0.0 78.8 jit_solution(17713559565401129970)
XLA Ops:
  0.0 4.0 %project.3 = (bf16[128,1152]{1,0:T(8,128)(2,1)S(1)}, f32[128,1152]{1,0:T(8,128)S(1)}, bf16[256,2048]{1,0:T(8,128)(2,1)S(1)}) custom-call(bf16[256,2048]{1,0:T(8,128)(2,1)} %refs_0_.1, f32[1,2048]{1,0:T(1,128)} %bitcast.1, bf16[2048,4096]{1,0:T(8,128)(2,1)} %refs_1_.3, bf16[2048,256]{1,0:T(8,128)(2,1)} %refs_2_.5, bf16[2048,256]{1,0:T(8,128)(2,1)} %refs_3_.5), custom_call_target="tpu_custom_call" | custom-call | tf_op jit(solution)/shard_map/project/pallas_call | solution.py:161
  4.0 3.0 %collective-permute-start = (bf16[128,1152]{1,0:T(8,128)(2,1)S(1)}, bf16[128,1152]{1,0:T(8,128)(2,1)S(1)}, u32[]{:S(2)}, u32[]{:S(2)}) collective-permute-start(bf16[128,1152]{1,0:T(8,128)(2,1)S(1)} %get-tuple-element.34), channel_id=1, source_target_pairs={{0,2},{1,5},{2,0},{3,7},{4,6},{5,1},{6,4},{7,3},{8,10},{9,13},{10,... | collective-permute-start | bytes 884744 | tf_op jit(solution)/shard_map/ppermute | solution.py:55
  7.0 3.9 %project.4 = (bf16[128,1280]{1,0:T(8,128)(2,1)S(1)}, f32[128,1280]{1,0:T(8,128)S(1)}) custom-call(bf16[256,2048]{1,0:T(8,128)(2,1)S(1)} %get-tuple-element.39.refs_0_, bf16[2048,4096]{1,0:T(8,128)(2,1)} %refs_1_.3, bf16[2048,256]{1,0:T(8,128)(2,1)} %refs_2_.5, bf16[2048,256]{1,0:T(8,128)(2,1)} %refs_3_.5), custom_call_target="tpu_custom_call" | custom-call | tf_op jit(solution)/shard_map/project/pallas_call | solution.py:161
  10.9 0.1 collective-permute-start.1
  11.0 0.7 collective-permute-done
  11.7 0.1 convert_add_fusion.2
  11.8 0.0 copy-start
  11.8 5.3 %project.5 = (bf16[128,2304]{1,0:T(8,128)(2,1)S(1)}, f32[128,2304]{1,0:T(8,128)S(1)}) custom-call(bf16[256,2048]{1,0:T(8,128)(2,1)S(1)} %get-tuple-element.39.refs_0_, bf16[2048,4096]{1,0:T(8,128)(2,1)} %refs_1_.3, bf16[2048,256]{1,0:T(8,128)(2,1)} %refs_2_.5, bf16[2048,256]{1,0:T(8,128)(2,1)} %refs_3_.5), custom_call_target="tpu_custom_call" | custom-call | tf_op jit(solution)/shard_map/project/pallas_call | solution.py:161
  17.1 0.9 %collective-permute-done.1 = bf16[128,1280]{1,0:T(8,128)(2,1)S(1)} collective-permute-done((bf16[128,1280]{1,0:T(8,128)(2,1)S(1)}, bf16[128,1280]{1,0:T(8,128)(2,1)S(1)}, u32[]{:S(2)}, u32[]{:S(2)}) %collective-permute-start.1) | collective-permute-done | bytes 327712 | tf_op jit(solution)/shard_map/ppermute | solution.py:55
  18.1 0.1 convert_add_fusion.1
  18.2 1.6 %collective-permute-start.3 = (bf16[64,2432]{1,0:T(8,128)(2,1)S(1)}, bf16[64,2432]{1,0:T(8,128)(2,1)}, u32[]{:S(2)}, u32[]{:S(2)}) collective-permute-start(bf16[64,2432]{1,0:T(8,128)(2,1)S(1)} %fusion.1), channel_id=1, source_target_pairs={{0,4},{1,3},{2,6},{3,1},{4,0},{5,7},{6,2},{7,5},{8,12},{9,11},{10,... | collective-permute-start | bytes 933896 | tf_op jit(solution)/shard_map/ppermute | solution.py:55
  19.8 0.1 add_convert_fusion.1
  19.9 0.1 convert_element_type.49
  20.0 1.2 %collective-permute-start.2 = (bf16[128,2304]{1,0:T(8,128)(2,1)S(1)}, bf16[128,2304]{1,0:T(8,128)(2,1)S(1)}, u32[]{:S(2)}, u32[]{:S(2)}) collective-permute-start(bf16[128,2304]{1,0:T(8,128)(2,1)S(1)} %get-tuple-element.44), channel_id=1, source_target_pairs={{0,2},{1,5},{2,0},{3,7},{4,6},{5,1},{6,4},{7,3},{8,10},{9,13},{10,... | collective-permute-start | bytes 1769480 | tf_op jit(solution)/shard_map/ppermute | solution.py:55
  21.1 3.5 %fetch_rows.1.refs_8_ = bf16[2048,2048]{1,0:T(8,128)(2,1)S(1)} custom-call(bf16[4096,2048]{1,0:T(8,128)(2,1)} %refs_6_.1), custom_call_target="tpu_custom_call" | custom-call | tf_op jit(solution)/shard_map/fetch_rows/pallas_call | solution.py:343
  24.6 5.6 %collective-permute-done.3 = bf16[64,2432]{1,0:T(8,128)(2,1)} collective-permute-done((bf16[64,2432]{1,0:T(8,128)(2,1)S(1)}, bf16[64,2432]{1,0:T(8,128)(2,1)}, u32[]{:S(2)}, u32[]{:S(2)}) %collective-permute-start.3) | collective-permute-done | bytes 311328 | tf_op jit(solution)/shard_map/ppermute | solution.py:55
  30.2 1.0 %fusion.2 = f32[64,2432]{1,0:T(8,128)S(1)} fusion(f32[128,1280]{1,0:T(8,128)S(1)} %convert_add_fusion.1, f32[128,1152]{1,0:T(8,128)S(1)} %convert_add_fusion.2, bf16[64,2432]{1,0:T(8,128)(2,1)} %collective-permute-done.3), kind=kLoop, calls=%fused_computation.8 | loop fusion | flops 466944 | bytes 2179072 | tf_op jit(solution)/shard_map/add | solution.py:462
  31.3 1.5 %collective-permute-start.5 = (bf16[32,2432]{1,0:T(8,128)(2,1)S(1)}, bf16[32,2432]{1,0:T(8,128)(2,1)S(1)}, u32[]{:S(2)}, u32[]{:S(2)}) collective-permute-start(bf16[32,2432]{1,0:T(8,128)(2,1)S(1)} %slice.64), channel_id=1, source_target_pairs={{0,8},{1,9},{2,10},{3,11},{4,12},{5,13},{6,14},{7,15},{8,0},{9,1},... | collective-permute-start | bytes 466952 | tf_op jit(solution)/shard_map/ppermute | solution.py:55
  32.8 0.0 collective-permute-done.2
  32.8 0.1 convert_add_fusion
  32.9 2.8 %collective-permute-start.4 = (bf16[64,2304]{1,0:T(8,128)(2,1)S(1)}, bf16[64,2304]{1,0:T(8,128)(2,1)S(1)}, u32[]{:S(2)}, u32[]{:S(2)}) collective-permute-start(bf16[64,2304]{1,0:T(8,128)(2,1)S(1)} %slice.63), channel_id=1, source_target_pairs={{0,4},{1,3},{2,6},{3,1},{4,0},{5,7},{6,2},{7,5},{8,12},{9,11},{10,... | collective-permute-start | bytes 884744 | tf_op jit(solution)/shard_map/ppermute | solution.py:55
  35.7 3.5 %fetch.1 = (bf16[8,1024,256]{2,1,0:T(8,128)(2,1)S(1)}, bf16[8,1024,256]{2,1,0:T(8,128)(2,1)S(1)}) custom-call(bf16[8,1024,256]{2,1,0:T(8,128)(2,1)} %refs_0_.2, bf16[8,1024,256]{2,1,0:T(8,128)(2,1)} %refs_1_.4), custom_call_target="tpu_custom_call" | custom-call | tf_op jit(solution)/shard_map/fetch/pallas_call | solution.py:314
  39.2 0.0 collective-permute-done.5
  39.3 2.0 %collective-permute-done.4 = bf16[64,2304]{1,0:T(8,128)(2,1)S(1)} collective-permute-done((bf16[64,2304]{1,0:T(8,128)(2,1)S(1)}, bf16[64,2304]{1,0:T(8,128)(2,1)S(1)}, u32[]{:S(2)}, u32[]{:S(2)}) %collective-permute-start.4) | collective-permute-done | bytes 294944 | tf_op jit(solution)/shard_map/ppermute | solution.py:55
  41.3 0.1 slice_add_fusion
  41.4 0.7 collective-permute-start.6
  42.1 0.1 fusion.3
  42.2 0.1 pad_maximum_fusion.1
  42.3 4.0 %attend.3 = (bf16[32,2048]{1,0:T(8,128)(2,1)S(1)}, bf16[2048,2048]{1,0:T(8,128)(2,1)S(1)}) custom-call(s32[8]{0:T(128)S(1)} %copy-done, f32[32,2432]{1,0:T(8,128)S(1)} %slice_add_fusion.1.refs_0_, f32[32,128]{1,0:T(8,128)S(1)} %slice.48.refs_1_, f32[32,128]{1,0:T(8,128)S(1)} %get-tuple-element.64.refs_2_, f32[32,128]{1,0:T(8,128)S(1)} %get-tuple-element.65.refs_3_, ...), custom_call_target="tpu_custom_call" | custom-call | tf_op jit(solution)/shard_map/attend/pallas_call | solution.py:281
  46.4 0.5 collective-permute-start.17
  46.9 1.9 %collective-permute-start.15 = (bf16[32,2048]{1,0:T(8,128)(2,1)S(1)}, bf16[32,2048]{1,0:T(8,128)(2,1)S(1)}, u32[]{:S(2)}, u32[]{:S(2)}) collective-permute-start(bf16[32,2048]{1,0:T(8,128)(2,1)S(1)} %get-tuple-element.56.refs_0_), channel_id=1, source_target_pairs={{0,4},{1,5},{2,6},{3,7},{4,0},{5,1},{6,2},{7,3},{8,12},{9,13},{10,... | collective-permute-start | bytes 393224 | tf_op jit(solution)/shard_map/ppermute | solution.py:55
  48.7 0.5 collective-permute-done.6
  49.2 0.8 %collective-permute-start.14 = (bf16[32,2048]{1,0:T(8,128)(2,1)S(1)}, bf16[32,2048]{1,0:T(8,128)(2,1)S(1)}, u32[]{:S(2)}, u32[]{:S(2)}) collective-permute-start(bf16[32,2048]{1,0:T(8,128)(2,1)S(1)} %get-tuple-element.56.refs_0_), channel_id=1, source_target_pairs={{0,8},{1,9},{2,10},{3,11},{4,12},{5,13},{6,14},{7,15},{8,0},{9,1},... | collective-permute-start | bytes 393224 | tf_op jit(solution)/shard_map/ppermute | solution.py:55
  50.1 2.5 %attend.2.refs_0_ = bf16[32,2048]{1,0:T(8,128)(2,1)S(1)} custom-call(s32[8]{0:T(128)S(1)} %copy-done, f32[32,2304]{1,0:T(8,128)S(1)} %slice_add_fusion.2.refs_0_, f32[32,128]{1,0:T(8,128)S(1)} %slice.48.refs_1_, f32[32,128]{1,0:T(8,128)S(1)} %get-tuple-element.64.refs_2_, f32[32,128]{1,0:T(8,128)S(1)} %get-tuple-element.65.refs_3_, ...), custom_call_target="tpu_custom_call" | custom-call | tf_op jit(solution)/shard_map/attend/pallas_call | solution.py:281
  52.5 2.2 %collective-permute-start.7 = (bf16[32,2048]{1,0:T(8,128)(2,1)S(1)}, bf16[32,2048]{1,0:T(8,128)(2,1)S(1)}, u32[]{:S(2)}, u32[]{:S(2)}) collective-permute-start(bf16[32,2048]{1,0:T(8,128)(2,1)S(1)} %attend.2.refs_0_), channel_id=1, source_target_pairs={{0,8},{1,9},{2,10},{3,11},{4,12},{5,13},{6,14},{7,15},{8,0},{9,1},... | collective-permute-start | bytes 393224 | tf_op jit(solution)/shard_map/ppermute | solution.py:55
  54.7 1.5 %collective-permute-start.10 = (bf16[32,2048]{1,0:T(8,128)(2,1)S(1)}, bf16[32,2048]{1,0:T(8,128)(2,1)S(1)}, u32[]{:S(2)}, u32[]{:S(2)}) collective-permute-start(bf16[32,2048]{1,0:T(8,128)(2,1)S(1)} %attend.2.refs_0_), channel_id=1, source_target_pairs={{0,2},{1,5},{2,0},{3,7},{4,6},{5,1},{6,4},{7,3},{8,10},{9,13},{10,... | collective-permute-start | bytes 393224 | tf_op jit(solution)/shard_map/ppermute | solution.py:55
  56.2 0.0 collective-permute-done.17.refs_4_
  56.2 0.0 collective-permute-start.8
  56.2 0.0 collective-permute-done.15.refs_2_
  56.2 2.1 %collective-permute-done.14.refs_1_ = bf16[32,2048]{1,0:T(8,128)(2,1)S(1)} collective-permute-done((bf16[32,2048]{1,0:T(8,128)(2,1)S(1)}, bf16[32,2048]{1,0:T(8,128)(2,1)S(1)}, u32[]{:S(2)}, u32[]{:S(2)}) %collective-permute-start.14) | collective-permute-done | bytes 131104 | tf_op jit(solution)/shard_map/ppermute | solution.py:55
  58.4 0.4 collective-permute-start.16
  58.8 1.3 %collective-permute-start.19 = (bf16[32,2048]{1,0:T(8,128)(2,1)S(1)}, bf16[32,2048]{1,0:T(8,128)(2,1)S(1)}, u32[]{:S(2)}, u32[]{:S(2)}) collective-permute-start(bf16[32,2048]{1,0:T(8,128)(2,1)S(1)} %collective-permute-done.15.refs_2_), channel_id=1, source_target_pairs={{0,2},{1,3},{2,0},{3,1},{4,6},{5,7},{6,4},{7,5},{8,10},{9,11},{10,... | collective-permute-start | bytes 393224 | tf_op jit(solution)/shard_map/ppermute | solution.py:55
  60.1 1.1 %collective-permute-done.7.refs_1_ = bf16[32,2048]{1,0:T(8,128)(2,1)S(1)} collective-permute-done((bf16[32,2048]{1,0:T(8,128)(2,1)S(1)}, bf16[32,2048]{1,0:T(8,128)(2,1)S(1)}, u32[]{:S(2)}, u32[]{:S(2)}) %collective-permute-start.7) | collective-permute-done | bytes 131104 | tf_op jit(solution)/shard_map/ppermute | solution.py:55
  61.2 0.9 %collective-permute-start.9 = (bf16[32,2048]{1,0:T(8,128)(2,1)S(1)}, bf16[32,2048]{1,0:T(8,128)(2,1)S(1)}, u32[]{:S(2)}, u32[]{:S(2)}) collective-permute-start(bf16[32,2048]{1,0:T(8,128)(2,1)S(1)} %collective-permute-done.7.refs_1_), channel_id=1, source_target_pairs={{0,4},{1,3},{2,6},{3,1},{4,0},{5,7},{6,2},{7,5},{8,12},{9,11},{10,... | collective-permute-start | bytes 393224 | tf_op jit(solution)/shard_map/ppermute | solution.py:55
  62.1 0.0 collective-permute-done.10.refs_4_
  62.1 0.6 collective-permute-done.8.refs_2_
  62.7 1.6 %collective-permute-start.12 = (bf16[32,2048]{1,0:T(8,128)(2,1)S(1)}, bf16[32,2048]{1,0:T(8,128)(2,1)S(1)}, u32[]{:S(2)}, u32[]{:S(2)}) collective-permute-start(bf16[32,2048]{1,0:T(8,128)(2,1)S(1)} %collective-permute-done.8.refs_2_), channel_id=1, source_target_pairs={{0,2},{1,5},{2,0},{3,7},{4,6},{5,1},{6,4},{7,3},{8,10},{9,13},{10,... | collective-permute-start | bytes 393224 | tf_op jit(solution)/shard_map/ppermute | solution.py:55
  64.3 0.4 collective-permute-start.18
  64.7 0.5 collective-permute-done.16.refs_3_
  65.3 1.8 %collective-permute-start.20 = (bf16[32,2048]{1,0:T(8,128)(2,1)S(1)}, bf16[32,2048]{1,0:T(8,128)(2,1)S(1)}, u32[]{:S(2)}, u32[]{:S(2)}) collective-permute-start(bf16[32,2048]{1,0:T(8,128)(2,1)S(1)} %collective-permute-done.16.refs_3_), channel_id=1, source_target_pairs={{0,2},{1,3},{2,0},{3,1},{4,6},{5,7},{6,4},{7,5},{8,10},{9,11},{10,... | collective-permute-start | bytes 393224 | tf_op jit(solution)/shard_map/ppermute | solution.py:55
  67.1 0.0 collective-permute-done.19.refs_6_
  67.1 0.2 collective-permute-start.11
  67.3 0.8 collective-permute-done.9.refs_3_
  68.1 1.8 %collective-permute-start.13 = (bf16[32,2048]{1,0:T(8,128)(2,1)S(1)}, bf16[32,2048]{1,0:T(8,128)(2,1)S(1)}, u32[]{:S(2)}, u32[]{:S(2)}) collective-permute-start(bf16[32,2048]{1,0:T(8,128)(2,1)S(1)} %collective-permute-done.9.refs_3_), channel_id=1, source_target_pairs={{0,2},{1,5},{2,0},{3,7},{4,6},{5,1},{6,4},{7,3},{8,10},{9,13},{10,... | collective-permute-start | bytes 393224 | tf_op jit(solution)/shard_map/ppermute | solution.py:55
  69.9 0.0 collective-permute-done.18.refs_5_
  69.9 0.8 collective-permute-done.20.refs_7_
  70.7 2.4 %combine.2.refs_8_ = f32[256,2048]{1,0:T(8,128)S(1)} custom-call(bf16[32,2048]{1,0:T(8,128)(2,1)S(1)} %get-tuple-element.56.refs_0_, bf16[32,2048]{1,0:T(8,128)(2,1)S(1)} %collective-permute-done.14.refs_1_, bf16[32,2048]{1,0:T(8,128)(2,1)S(1)} %collective-permute-done.15.refs_2_, bf16[32,2048]{1,0:T(8,128)(2,1)S(1)} %collective-permute-done.16.refs_3_, ...), custom_call_target="tpu_custom_call" | custom-call | tf_op jit(solution)/shard_map/combine/pallas_call | solution.py:396
  73.1 0.0 collective-permute-done.12.refs_6_
  73.1 0.0 collective-permute-done.11.refs_5_
  73.1 0.4 collective-permute-done.13.refs_7_
  73.5 2.5 %combine.3 = (bf16[128,2048]{1,0:T(8,128)(2,1)S(1)}, f32[128,2048]{1,0:T(8,128)S(1)}) custom-call(bf16[32,2048]{1,0:T(8,128)(2,1)S(1)} %attend.2.refs_0_, bf16[32,2048]{1,0:T(8,128)(2,1)S(1)} %collective-permute-done.7.refs_1_, bf16[32,2048]{1,0:T(8,128)(2,1)S(1)} %collective-permute-done.8.refs_2_, bf16[32,2048]{1,0:T(8,128)(2,1)S(1)} %collective-permute-done.9.refs_3_, ...), custom_call_target="tpu_custom_call" | custom-call | tf_op jit(solution)/shard_map/combine/pallas_call | solution.py:396
  75.9 0.1 collective-permute-start.21
  76.0 1.9 %collective-permute-done.21 = bf16[128,2048]{1,0:T(8,128)(2,1)S(1)} collective-permute-done((bf16[128,2048]{1,0:T(8,128)(2,1)S(1)}, bf16[128,2048]{1,0:T(8,128)(2,1)S(1)}, u32[]{:S(2)}, u32[]{:S(2)}) %collective-permute-start.21) | collective-permute-done | bytes 524320 | tf_op jit(solution)/shard_map/ppermute | solution.py:521
  77.9 0.9 %add_convert_fusion = bf16[128,2048]{1,0:T(8,128)(2,1)} fusion(f32[128,2048]{1,0:T(8,128)S(1)} %get-tuple-element.59, bf16[128,2048]{1,0:T(8,128)(2,1)S(1)} %collective-permute-done.21), kind=kLoop, calls=%fused_computation.3 | loop fusion | flops 786432 | bytes 2097152 | tf_op jit(solution)/shard_map/convert_element_type | solution.py:522
  (9 shorter events, 0.2 us)
Async XLA Ops:
  4.0 7.7 %collective-permute-start = (bf16[128,1152]{1,0:T(8,128)(2,1)S(1)}, bf16[128,1152]{1,0:T(8,128)(2,1)S(1)}, u32[]{:S(2)}, u32[]{:S(2)}) collective-permute-start(bf16[128,1152]{1,0:T(8,128)(2,1)S(1)} %get-tuple-element.34), channel_id=1, source_target_pairs={{0,2},{1,5},{2,0},{3,7},{4,6},{5,1},{6,4},{7,3},{8,10},{9,13},{10,... | collective-permute-start | bytes 884744 | tf_op jit(solution)/shard_map/ppermute | solution.py:55
  10.9 7.1 %collective-permute-start.1 = (bf16[128,1280]{1,0:T(8,128)(2,1)S(1)}, bf16[128,1280]{1,0:T(8,128)(2,1)S(1)}, u32[]{:S(2)}, u32[]{:S(2)}) collective-permute-start(bf16[128,1280]{1,0:T(8,128)(2,1)S(1)} %get-tuple-element.36), channel_id=1, source_target_pairs={{0,2},{1,5},{2,0},{3,7},{4,6},{5,1},{6,4},{7,3},{8,10},{9,13},{10,... | collective-permute-start | bytes 983048 | tf_op jit(solution)/shard_map/ppermute | solution.py:55
  11.8 8.0 %copy-start = (s32[8]{0:T(128)S(1)}, s32[8]{0:T(128)}, u32[]{:S(2)}) copy-start(s32[8]{0:T(128)} %length_ref.3) | copy-start | bytes 100
  18.2 12.1 %collective-permute-start.3 = (bf16[64,2432]{1,0:T(8,128)(2,1)S(1)}, bf16[64,2432]{1,0:T(8,128)(2,1)}, u32[]{:S(2)}, u32[]{:S(2)}) collective-permute-start(bf16[64,2432]{1,0:T(8,128)(2,1)S(1)} %fusion.1), channel_id=1, source_target_pairs={{0,4},{1,3},{2,6},{3,1},{4,0},{5,7},{6,2},{7,5},{8,12},{9,11},{10,... | collective-permute-start | bytes 933896 | tf_op jit(solution)/shard_map/ppermute | solution.py:55
  20.0 12.8 %collective-permute-start.2 = (bf16[128,2304]{1,0:T(8,128)(2,1)S(1)}, bf16[128,2304]{1,0:T(8,128)(2,1)S(1)}, u32[]{:S(2)}, u32[]{:S(2)}) collective-permute-start(bf16[128,2304]{1,0:T(8,128)(2,1)S(1)} %get-tuple-element.44), channel_id=1, source_target_pairs={{0,2},{1,5},{2,0},{3,7},{4,6},{5,1},{6,4},{7,3},{8,10},{9,13},{10,... | collective-permute-start | bytes 1769480 | tf_op jit(solution)/shard_map/ppermute | solution.py:55
  31.3 8.0 %collective-permute-start.5 = (bf16[32,2432]{1,0:T(8,128)(2,1)S(1)}, bf16[32,2432]{1,0:T(8,128)(2,1)S(1)}, u32[]{:S(2)}, u32[]{:S(2)}) collective-permute-start(bf16[32,2432]{1,0:T(8,128)(2,1)S(1)} %slice.64), channel_id=1, source_target_pairs={{0,8},{1,9},{2,10},{3,11},{4,12},{5,13},{6,14},{7,15},{8,0},{9,1},... | collective-permute-start | bytes 466952 | tf_op jit(solution)/shard_map/ppermute | solution.py:55
  32.9 8.4 %collective-permute-start.4 = (bf16[64,2304]{1,0:T(8,128)(2,1)S(1)}, bf16[64,2304]{1,0:T(8,128)(2,1)S(1)}, u32[]{:S(2)}, u32[]{:S(2)}) collective-permute-start(bf16[64,2304]{1,0:T(8,128)(2,1)S(1)} %slice.63), channel_id=1, source_target_pairs={{0,4},{1,3},{2,6},{3,1},{4,0},{5,7},{6,2},{7,5},{8,12},{9,11},{10,... | collective-permute-start | bytes 884744 | tf_op jit(solution)/shard_map/ppermute | solution.py:55
  41.4 7.8 %collective-permute-start.6 = (bf16[32,2304]{1,0:T(8,128)(2,1)S(1)}, bf16[32,2304]{1,0:T(8,128)(2,1)S(1)}, u32[]{:S(2)}, u32[]{:S(2)}) collective-permute-start(bf16[32,2304]{1,0:T(8,128)(2,1)S(1)} %slice.65), channel_id=1, source_target_pairs={{0,8},{1,9},{2,10},{3,11},{4,12},{5,13},{6,14},{7,15},{8,0},{9,1},... | collective-permute-start | bytes 442376 | tf_op jit(solution)/shard_map/ppermute | solution.py:55
  46.4 9.9 %collective-permute-start.17 = (bf16[32,2048]{1,0:T(8,128)(2,1)S(1)}, bf16[32,2048]{1,0:T(8,128)(2,1)S(1)}, u32[]{:S(2)}, u32[]{:S(2)}) collective-permute-start(bf16[32,2048]{1,0:T(8,128)(2,1)S(1)} %get-tuple-element.56.refs_0_), channel_id=1, source_target_pairs={{0,2},{1,3},{2,0},{3,1},{4,6},{5,7},{6,4},{7,5},{8,10},{9,11},{10,... | collective-permute-start | bytes 393224 | tf_op jit(solution)/shard_map/ppermute | solution.py:55
  46.9 9.4 %collective-permute-start.15 = (bf16[32,2048]{1,0:T(8,128)(2,1)S(1)}, bf16[32,2048]{1,0:T(8,128)(2,1)S(1)}, u32[]{:S(2)}, u32[]{:S(2)}) collective-permute-start(bf16[32,2048]{1,0:T(8,128)(2,1)S(1)} %get-tuple-element.56.refs_0_), channel_id=1, source_target_pairs={{0,4},{1,5},{2,6},{3,7},{4,0},{5,1},{6,2},{7,3},{8,12},{9,13},{10,... | collective-permute-start | bytes 393224 | tf_op jit(solution)/shard_map/ppermute | solution.py:55
  49.2 9.1 %collective-permute-start.14 = (bf16[32,2048]{1,0:T(8,128)(2,1)S(1)}, bf16[32,2048]{1,0:T(8,128)(2,1)S(1)}, u32[]{:S(2)}, u32[]{:S(2)}) collective-permute-start(bf16[32,2048]{1,0:T(8,128)(2,1)S(1)} %get-tuple-element.56.refs_0_), channel_id=1, source_target_pairs={{0,8},{1,9},{2,10},{3,11},{4,12},{5,13},{6,14},{7,15},{8,0},{9,1},... | collective-permute-start | bytes 393224 | tf_op jit(solution)/shard_map/ppermute | solution.py:55
  52.5 8.7 %collective-permute-start.7 = (bf16[32,2048]{1,0:T(8,128)(2,1)S(1)}, bf16[32,2048]{1,0:T(8,128)(2,1)S(1)}, u32[]{:S(2)}, u32[]{:S(2)}) collective-permute-start(bf16[32,2048]{1,0:T(8,128)(2,1)S(1)} %attend.2.refs_0_), channel_id=1, source_target_pairs={{0,8},{1,9},{2,10},{3,11},{4,12},{5,13},{6,14},{7,15},{8,0},{9,1},... | collective-permute-start | bytes 393224 | tf_op jit(solution)/shard_map/ppermute | solution.py:55
  54.7 7.4 %collective-permute-start.10 = (bf16[32,2048]{1,0:T(8,128)(2,1)S(1)}, bf16[32,2048]{1,0:T(8,128)(2,1)S(1)}, u32[]{:S(2)}, u32[]{:S(2)}) collective-permute-start(bf16[32,2048]{1,0:T(8,128)(2,1)S(1)} %attend.2.refs_0_), channel_id=1, source_target_pairs={{0,2},{1,5},{2,0},{3,7},{4,6},{5,1},{6,4},{7,3},{8,10},{9,13},{10,... | collective-permute-start | bytes 393224 | tf_op jit(solution)/shard_map/ppermute | solution.py:55
  56.2 6.5 %collective-permute-start.8 = (bf16[32,2048]{1,0:T(8,128)(2,1)S(1)}, bf16[32,2048]{1,0:T(8,128)(2,1)S(1)}, u32[]{:S(2)}, u32[]{:S(2)}) collective-permute-start(bf16[32,2048]{1,0:T(8,128)(2,1)S(1)} %attend.2.refs_0_), channel_id=1, source_target_pairs={{0,4},{1,3},{2,6},{3,1},{4,0},{5,7},{6,2},{7,5},{8,12},{9,11},{10,... | collective-permute-start | bytes 393224 | tf_op jit(solution)/shard_map/ppermute | solution.py:55
  58.4 6.9 %collective-permute-start.16 = (bf16[32,2048]{1,0:T(8,128)(2,1)S(1)}, bf16[32,2048]{1,0:T(8,128)(2,1)S(1)}, u32[]{:S(2)}, u32[]{:S(2)}) collective-permute-start(bf16[32,2048]{1,0:T(8,128)(2,1)S(1)} %collective-permute-done.14.refs_1_), channel_id=1, source_target_pairs={{0,4},{1,5},{2,6},{3,7},{4,0},{5,1},{6,2},{7,3},{8,12},{9,13},{10,... | collective-permute-start | bytes 393224 | tf_op jit(solution)/shard_map/ppermute | solution.py:55
  58.8 8.3 %collective-permute-start.19 = (bf16[32,2048]{1,0:T(8,128)(2,1)S(1)}, bf16[32,2048]{1,0:T(8,128)(2,1)S(1)}, u32[]{:S(2)}, u32[]{:S(2)}) collective-permute-start(bf16[32,2048]{1,0:T(8,128)(2,1)S(1)} %collective-permute-done.15.refs_2_), channel_id=1, source_target_pairs={{0,2},{1,3},{2,0},{3,1},{4,6},{5,7},{6,4},{7,5},{8,10},{9,11},{10,... | collective-permute-start | bytes 393224 | tf_op jit(solution)/shard_map/ppermute | solution.py:55
  61.2 6.9 %collective-permute-start.9 = (bf16[32,2048]{1,0:T(8,128)(2,1)S(1)}, bf16[32,2048]{1,0:T(8,128)(2,1)S(1)}, u32[]{:S(2)}, u32[]{:S(2)}) collective-permute-start(bf16[32,2048]{1,0:T(8,128)(2,1)S(1)} %collective-permute-done.7.refs_1_), channel_id=1, source_target_pairs={{0,4},{1,3},{2,6},{3,1},{4,0},{5,7},{6,2},{7,5},{8,12},{9,11},{10,... | collective-permute-start | bytes 393224 | tf_op jit(solution)/shard_map/ppermute | solution.py:55
  62.7 10.4 %collective-permute-start.12 = (bf16[32,2048]{1,0:T(8,128)(2,1)S(1)}, bf16[32,2048]{1,0:T(8,128)(2,1)S(1)}, u32[]{:S(2)}, u32[]{:S(2)}) collective-permute-start(bf16[32,2048]{1,0:T(8,128)(2,1)S(1)} %collective-permute-done.8.refs_2_), channel_id=1, source_target_pairs={{0,2},{1,5},{2,0},{3,7},{4,6},{5,1},{6,4},{7,3},{8,10},{9,13},{10,... | collective-permute-start | bytes 393224 | tf_op jit(solution)/shard_map/ppermute | solution.py:55
  64.3 5.6 %collective-permute-start.18 = (bf16[32,2048]{1,0:T(8,128)(2,1)S(1)}, bf16[32,2048]{1,0:T(8,128)(2,1)S(1)}, u32[]{:S(2)}, u32[]{:S(2)}) collective-permute-start(bf16[32,2048]{1,0:T(8,128)(2,1)S(1)} %collective-permute-done.14.refs_1_), channel_id=1, source_target_pairs={{0,2},{1,3},{2,0},{3,1},{4,6},{5,7},{6,4},{7,5},{8,10},{9,11},{10,... | collective-permute-start | bytes 393224 | tf_op jit(solution)/shard_map/ppermute | solution.py:55
  65.3 5.4 %collective-permute-start.20 = (bf16[32,2048]{1,0:T(8,128)(2,1)S(1)}, bf16[32,2048]{1,0:T(8,128)(2,1)S(1)}, u32[]{:S(2)}, u32[]{:S(2)}) collective-permute-start(bf16[32,2048]{1,0:T(8,128)(2,1)S(1)} %collective-permute-done.16.refs_3_), channel_id=1, source_target_pairs={{0,2},{1,3},{2,0},{3,1},{4,6},{5,7},{6,4},{7,5},{8,10},{9,11},{10,... | collective-permute-start | bytes 393224 | tf_op jit(solution)/shard_map/ppermute | solution.py:55
  67.1 6.0 %collective-permute-start.11 = (bf16[32,2048]{1,0:T(8,128)(2,1)S(1)}, bf16[32,2048]{1,0:T(8,128)(2,1)S(1)}, u32[]{:S(2)}, u32[]{:S(2)}) collective-permute-start(bf16[32,2048]{1,0:T(8,128)(2,1)S(1)} %collective-permute-done.7.refs_1_), channel_id=1, source_target_pairs={{0,2},{1,5},{2,0},{3,7},{4,6},{5,1},{6,4},{7,3},{8,10},{9,13},{10,... | collective-permute-start | bytes 393224 | tf_op jit(solution)/shard_map/ppermute | solution.py:55
  68.1 5.4 %collective-permute-start.13 = (bf16[32,2048]{1,0:T(8,128)(2,1)S(1)}, bf16[32,2048]{1,0:T(8,128)(2,1)S(1)}, u32[]{:S(2)}, u32[]{:S(2)}) collective-permute-start(bf16[32,2048]{1,0:T(8,128)(2,1)S(1)} %collective-permute-done.9.refs_3_), channel_id=1, source_target_pairs={{0,2},{1,5},{2,0},{3,7},{4,6},{5,1},{6,4},{7,3},{8,10},{9,13},{10,... | collective-permute-start | bytes 393224 | tf_op jit(solution)/shard_map/ppermute | solution.py:55
  75.9 2.0 %collective-permute-start.21 = (bf16[128,2048]{1,0:T(8,128)(2,1)S(1)}, bf16[128,2048]{1,0:T(8,128)(2,1)S(1)}, u32[]{:S(2)}, u32[]{:S(2)}) collective-permute-start(bf16[128,2048]{1,0:T(8,128)(2,1)S(1)} %get-tuple-element.60), channel_id=1, source_target_pairs={{0,1},{1,0},{2,3},{3,2},{4,5},{5,4},{6,7},{7,6},{8,9},{9,8},{10,11... | collective-permute-start | bytes 1572872 | tf_op jit(solution)/shard_map/ppermute | solution.py:521

commit v21 on v18

--- a/solution.py
+++ b/solution.py
@@ -68,7 +68,7 @@
     kv = wk_ref.shape[1] // CHUNKS if with_kv else 0
     width = w_buf.shape[1]
     cols = width - 2 * kv
-    pieces = 1 if first else 4 if cols > 1024 else 2
+    pieces = 4 if cols > 1024 else 1
     tile = cols // pieces
 
     def w_copy(ref, start, size, at, sem):

time: 79 us -> 79.2 us (level)
  starting transfers between devices: 26.4 us -> 27.2 us
  transfers between devices with their start and end apart: 22 -> 22, of which waited for: 13 -> 11; matrix products, arithmetic and copies ran while one was open for 2% -> 2% of each run, Pallas kernels for 32% -> 32%
where the time goes in v21:
time: 79.2 us; the launch traced here: 79.1 us
  Pallas kernels  31.7 us (40%)
  starting transfers between devices  27.2 us (34%)
  waiting for transfers between devices  17.2 us (22%)
  other arithmetic  2.58 us (3%)
    ppermute x21, starting transfers between devices, exchange(): return lax.ppermute(value, ('gx', 'gy'), pairs)  27.1 us
    ppermute x21, waiting for transfers between devices, exchange(): return lax.ppermute(value, ('gx', 'gy'), pairs)  15.3 us
    pallas_call x3, Pallas kernels, project(): pl.pallas_call(functools.partial(project_kernel, n, q_start, kv_start, fi...  13.4 us
    pallas_call x2, Pallas kernels, attend(): pl.pallas_call(functools.partial(attend_kernel, chunk, offsets, kv_offset...  6.51 us
    pallas_call x2, Pallas kernels, combine(): pl.pallas_call(functools.partial(combine_kernel, n, block, chunk), out_sh...  4.89 us
    pallas_call x1, Pallas kernels, fetch_rows(): pl.pallas_call(functools.partial(fetch_rows_kernel, start, pieces), out_s...  3.5 us
    pallas_call x1, Pallas kernels, fetch(): pl.pallas_call(functools.partial(fetch_kernel, len(arrays), pieces), out_...  3.47 us
    ppermute x1, waiting for transfers between devices, shards(): other = lax.ppermute(send, 'gy', [(0, 1), (1, 0)])  1.9 us
  transfers between devices with their start and end apart: 22, of which 11 were waited for; matrix products, arithmetic and copies ran while one was open for 2% of the time, Pallas kernels for 32%

profile of v21, /device:TPU:0, one launch (start us, length us, event | category | flops | bytes accessed | tf_op | source)
XLA Modules:
  0.0 79.1 jit_solution(10510357825444583179)
XLA Ops:
  0.0 4.0 %project.3 = (bf16[128,1152]{1,0:T(8,128)(2,1)S(1)}, f32[128,1152]{1,0:T(8,128)S(1)}, bf16[256,2048]{1,0:T(8,128)(2,1)S(1)}) custom-call(bf16[256,2048]{1,0:T(8,128)(2,1)} %refs_0_.1, f32[1,2048]{1,0:T(1,128)} %bitcast.1, bf16[2048,4096]{1,0:T(8,128)(2,1)} %refs_1_.3, bf16[2048,256]{1,0:T(8,128)(2,1)} %refs_2_.5, bf16[2048,256]{1,0:T(8,128)(2,1)} %refs_3_.5), custom_call_target="tpu_custom_call" | custom-call | tf_op jit(solution)/shard_map/project/pallas_call | solution.py:161
  4.0 3.0 %collective-permute-start = (bf16[128,1152]{1,0:T(8,128)(2,1)S(1)}, bf16[128,1152]{1,0:T(8,128)(2,1)S(1)}, u32[]{:S(2)}, u32[]{:S(2)}) collective-permute-start(bf16[128,1152]{1,0:T(8,128)(2,1)S(1)} %get-tuple-element.34), channel_id=1, source_target_pairs={{0,2},{1,5},{2,0},{3,7},{4,6},{5,1},{6,4},{7,3},{8,10},{9,13},{10,... | collective-permute-start | bytes 884744 | tf_op jit(solution)/shard_map/ppermute | solution.py:55
  7.0 4.0 %project.4 = (bf16[128,1280]{1,0:T(8,128)(2,1)S(1)}, f32[128,1280]{1,0:T(8,128)S(1)}) custom-call(bf16[256,2048]{1,0:T(8,128)(2,1)S(1)} %get-tuple-element.39.refs_0_, bf16[2048,4096]{1,0:T(8,128)(2,1)} %refs_1_.3, bf16[2048,256]{1,0:T(8,128)(2,1)} %refs_2_.5, bf16[2048,256]{1,0:T(8,128)(2,1)} %refs_3_.5), custom_call_target="tpu_custom_call" | custom-call | tf_op jit(solution)/shard_map/project/pallas_call | solution.py:161
  11.1 0.1 collective-permute-start.1
  11.2 0.6 collective-permute-done
  11.7 0.1 convert_add_fusion.2
  11.8 0.0 copy-start
  11.8 5.3 %project.5 = (bf16[128,2304]{1,0:T(8,128)(2,1)S(1)}, f32[128,2304]{1,0:T(8,128)S(1)}) custom-call(bf16[256,2048]{1,0:T(8,128)(2,1)S(1)} %get-tuple-element.39.refs_0_, bf16[2048,4096]{1,0:T(8,128)(2,1)} %refs_1_.3, bf16[2048,256]{1,0:T(8,128)(2,1)} %refs_2_.5, bf16[2048,256]{1,0:T(8,128)(2,1)} %refs_3_.5), custom_call_target="tpu_custom_call" | custom-call | tf_op jit(solution)/shard_map/project/pallas_call | solution.py:161
  17.1 1.1 %collective-permute-done.1 = bf16[128,1280]{1,0:T(8,128)(2,1)S(1)} collective-permute-done((bf16[128,1280]{1,0:T(8,128)(2,1)S(1)}, bf16[128,1280]{1,0:T(8,128)(2,1)S(1)}, u32[]{:S(2)}, u32[]{:S(2)}) %collective-permute-start.1) | collective-permute-done | bytes 327712 | tf_op jit(solution)/shard_map/ppermute | solution.py:55
  18.2 0.1 convert_add_fusion.1
  18.3 1.6 %collective-permute-start.3 = (bf16[64,2432]{1,0:T(8,128)(2,1)S(1)}, bf16[64,2432]{1,0:T(8,128)(2,1)}, u32[]{:S(2)}, u32[]{:S(2)}) collective-permute-start(bf16[64,2432]{1,0:T(8,128)(2,1)S(1)} %fusion.1), channel_id=1, source_target_pairs={{0,4},{1,3},{2,6},{3,1},{4,0},{5,7},{6,2},{7,5},{8,12},{9,11},{10,... | collective-permute-start | bytes 933896 | tf_op jit(solution)/shard_map/ppermute | solution.py:55
  20.0 0.1 add_convert_fusion.1
  20.1 0.1 convert_element_type.49
  20.2 1.0 %collective-permute-start.2 = (bf16[128,2304]{1,0:T(8,128)(2,1)S(1)}, bf16[128,2304]{1,0:T(8,128)(2,1)S(1)}, u32[]{:S(2)}, u32[]{:S(2)}) collective-permute-start(bf16[128,2304]{1,0:T(8,128)(2,1)S(1)} %get-tuple-element.44), channel_id=1, source_target_pairs={{0,2},{1,5},{2,0},{3,7},{4,6},{5,1},{6,4},{7,3},{8,10},{9,13},{10,... | collective-permute-start | bytes 1769480 | tf_op jit(solution)/shard_map/ppermute | solution.py:55
  21.1 3.5 %fetch_rows.1.refs_8_ = bf16[2048,2048]{1,0:T(8,128)(2,1)S(1)} custom-call(bf16[4096,2048]{1,0:T(8,128)(2,1)} %refs_6_.1), custom_call_target="tpu_custom_call" | custom-call | tf_op jit(solution)/shard_map/fetch_rows/pallas_call | solution.py:343
  24.6 5.8 %collective-permute-done.3 = bf16[64,2432]{1,0:T(8,128)(2,1)} collective-permute-done((bf16[64,2432]{1,0:T(8,128)(2,1)S(1)}, bf16[64,2432]{1,0:T(8,128)(2,1)}, u32[]{:S(2)}, u32[]{:S(2)}) %collective-permute-start.3) | collective-permute-done | bytes 311328 | tf_op jit(solution)/shard_map/ppermute | solution.py:55
  30.4 1.0 %fusion.2 = f32[64,2432]{1,0:T(8,128)S(1)} fusion(f32[128,1280]{1,0:T(8,128)S(1)} %convert_add_fusion.1, f32[128,1152]{1,0:T(8,128)S(1)} %convert_add_fusion.2, bf16[64,2432]{1,0:T(8,128)(2,1)} %collective-permute-done.3), kind=kLoop, calls=%fused_computation.8 | loop fusion | flops 466944 | bytes 2179072 | tf_op jit(solution)/shard_map/add | solution.py:462
  31.5 1.7 %collective-permute-start.5 = (bf16[32,2432]{1,0:T(8,128)(2,1)S(1)}, bf16[32,2432]{1,0:T(8,128)(2,1)S(1)}, u32[]{:S(2)}, u32[]{:S(2)}) collective-permute-start(bf16[32,2432]{1,0:T(8,128)(2,1)S(1)} %slice.64), channel_id=1, source_target_pairs={{0,8},{1,9},{2,10},{3,11},{4,12},{5,13},{6,14},{7,15},{8,0},{9,1},... | collective-permute-start | bytes 466952 | tf_op jit(solution)/shard_map/ppermute | solution.py:55
  33.1 0.0 collective-permute-done.2
  33.1 0.1 convert_add_fusion
  33.3 2.7 %collective-permute-start.4 = (bf16[64,2304]{1,0:T(8,128)(2,1)S(1)}, bf16[64,2304]{1,0:T(8,128)(2,1)S(1)}, u32[]{:S(2)}, u32[]{:S(2)}) collective-permute-start(bf16[64,2304]{1,0:T(8,128)(2,1)S(1)} %slice.63), channel_id=1, source_target_pairs={{0,4},{1,3},{2,6},{3,1},{4,0},{5,7},{6,2},{7,5},{8,12},{9,11},{10,... | collective-permute-start | bytes 884744 | tf_op jit(solution)/shard_map/ppermute | solution.py:55
  35.9 3.5 %fetch.1 = (bf16[8,1024,256]{2,1,0:T(8,128)(2,1)S(1)}, bf16[8,1024,256]{2,1,0:T(8,128)(2,1)S(1)}) custom-call(bf16[8,1024,256]{2,1,0:T(8,128)(2,1)} %refs_0_.2, bf16[8,1024,256]{2,1,0:T(8,128)(2,1)} %refs_1_.4), custom_call_target="tpu_custom_call" | custom-call | tf_op jit(solution)/shard_map/fetch/pallas_call | solution.py:314
  39.4 0.0 collective-permute-done.5
  39.5 2.0 %collective-permute-done.4 = bf16[64,2304]{1,0:T(8,128)(2,1)S(1)} collective-permute-done((bf16[64,2304]{1,0:T(8,128)(2,1)S(1)}, bf16[64,2304]{1,0:T(8,128)(2,1)S(1)}, u32[]{:S(2)}, u32[]{:S(2)}) %collective-permute-start.4) | collective-permute-done | bytes 294944 | tf_op jit(solution)/shard_map/ppermute | solution.py:55
  41.5 0.1 slice_add_fusion
  41.6 0.7 collective-permute-start.6
  42.3 0.1 fusion.3
  42.4 0.1 pad_maximum_fusion.1
  42.5 4.0 %attend.3 = (bf16[32,2048]{1,0:T(8,128)(2,1)S(1)}, bf16[2048,2048]{1,0:T(8,128)(2,1)S(1)}) custom-call(s32[8]{0:T(128)S(1)} %copy-done, f32[32,2432]{1,0:T(8,128)S(1)} %slice_add_fusion.1.refs_0_, f32[32,128]{1,0:T(8,128)S(1)} %slice.48.refs_1_, f32[32,128]{1,0:T(8,128)S(1)} %get-tuple-element.64.refs_2_, f32[32,128]{1,0:T(8,128)S(1)} %get-tuple-element.65.refs_3_, ...), custom_call_target="tpu_custom_call" | custom-call | tf_op jit(solution)/shard_map/attend/pallas_call | solution.py:281
  46.6 0.3 collective-permute-start.17
  46.8 2.1 %collective-permute-start.15 = (bf16[32,2048]{1,0:T(8,128)(2,1)S(1)}, bf16[32,2048]{1,0:T(8,128)(2,1)S(1)}, u32[]{:S(2)}, u32[]{:S(2)}) collective-permute-start(bf16[32,2048]{1,0:T(8,128)(2,1)S(1)} %get-tuple-element.56.refs_0_), channel_id=1, source_target_pairs={{0,4},{1,5},{2,6},{3,7},{4,0},{5,1},{6,2},{7,3},{8,12},{9,13},{10,... | collective-permute-start | bytes 393224 | tf_op jit(solution)/shard_map/ppermute | solution.py:55
  48.9 0.4 collective-permute-done.6
  49.4 0.9 %collective-permute-start.14 = (bf16[32,2048]{1,0:T(8,128)(2,1)S(1)}, bf16[32,2048]{1,0:T(8,128)(2,1)S(1)}, u32[]{:S(2)}, u32[]{:S(2)}) collective-permute-start(bf16[32,2048]{1,0:T(8,128)(2,1)S(1)} %get-tuple-element.56.refs_0_), channel_id=1, source_target_pairs={{0,8},{1,9},{2,10},{3,11},{4,12},{5,13},{6,14},{7,15},{8,0},{9,1},... | collective-permute-start | bytes 393224 | tf_op jit(solution)/shard_map/ppermute | solution.py:55
  50.3 2.5 %attend.2.refs_0_ = bf16[32,2048]{1,0:T(8,128)(2,1)S(1)} custom-call(s32[8]{0:T(128)S(1)} %copy-done, f32[32,2304]{1,0:T(8,128)S(1)} %slice_add_fusion.2.refs_0_, f32[32,128]{1,0:T(8,128)S(1)} %slice.48.refs_1_, f32[32,128]{1,0:T(8,128)S(1)} %get-tuple-element.64.refs_2_, f32[32,128]{1,0:T(8,128)S(1)} %get-tuple-element.65.refs_3_, ...), custom_call_target="tpu_custom_call" | custom-call | tf_op jit(solution)/shard_map/attend/pallas_call | solution.py:281
  52.7 2.2 %collective-permute-start.7 = (bf16[32,2048]{1,0:T(8,128)(2,1)S(1)}, bf16[32,2048]{1,0:T(8,128)(2,1)S(1)}, u32[]{:S(2)}, u32[]{:S(2)}) collective-permute-start(bf16[32,2048]{1,0:T(8,128)(2,1)S(1)} %attend.2.refs_0_), channel_id=1, source_target_pairs={{0,8},{1,9},{2,10},{3,11},{4,12},{5,13},{6,14},{7,15},{8,0},{9,1},... | collective-permute-start | bytes 393224 | tf_op jit(solution)/shard_map/ppermute | solution.py:55
  54.9 1.5 %collective-permute-start.10 = (bf16[32,2048]{1,0:T(8,128)(2,1)S(1)}, bf16[32,2048]{1,0:T(8,128)(2,1)S(1)}, u32[]{:S(2)}, u32[]{:S(2)}) collective-permute-start(bf16[32,2048]{1,0:T(8,128)(2,1)S(1)} %attend.2.refs_0_), channel_id=1, source_target_pairs={{0,2},{1,5},{2,0},{3,7},{4,6},{5,1},{6,4},{7,3},{8,10},{9,13},{10,... | collective-permute-start | bytes 393224 | tf_op jit(solution)/shard_map/ppermute | solution.py:55
  56.4 0.0 collective-permute-done.17.refs_4_
  56.4 0.0 collective-permute-start.8
  56.4 0.0 collective-permute-done.15.refs_2_
  56.5 1.9 %collective-permute-done.14.refs_1_ = bf16[32,2048]{1,0:T(8,128)(2,1)S(1)} collective-permute-done((bf16[32,2048]{1,0:T(8,128)(2,1)S(1)}, bf16[32,2048]{1,0:T(8,128)(2,1)S(1)}, u32[]{:S(2)}, u32[]{:S(2)}) %collective-permute-start.14) | collective-permute-done | bytes 131104 | tf_op jit(solution)/shard_map/ppermute | solution.py:55
  58.3 0.1 collective-permute-start.16
  58.5 1.4 %collective-permute-start.19 = (bf16[32,2048]{1,0:T(8,128)(2,1)S(1)}, bf16[32,2048]{1,0:T(8,128)(2,1)S(1)}, u32[]{:S(2)}, u32[]{:S(2)}) collective-permute-start(bf16[32,2048]{1,0:T(8,128)(2,1)S(1)} %collective-permute-done.15.refs_2_), channel_id=1, source_target_pairs={{0,2},{1,3},{2,0},{3,1},{4,6},{5,7},{6,4},{7,5},{8,10},{9,11},{10,... | collective-permute-start | bytes 393224 | tf_op jit(solution)/shard_map/ppermute | solution.py:55
  59.9 1.2 %collective-permute-done.7.refs_1_ = bf16[32,2048]{1,0:T(8,128)(2,1)S(1)} collective-permute-done((bf16[32,2048]{1,0:T(8,128)(2,1)S(1)}, bf16[32,2048]{1,0:T(8,128)(2,1)S(1)}, u32[]{:S(2)}, u32[]{:S(2)}) %collective-permute-start.7) | collective-permute-done | bytes 131104 | tf_op jit(solution)/shard_map/ppermute | solution.py:55
  61.1 0.9 %collective-permute-start.9 = (bf16[32,2048]{1,0:T(8,128)(2,1)S(1)}, bf16[32,2048]{1,0:T(8,128)(2,1)S(1)}, u32[]{:S(2)}, u32[]{:S(2)}) collective-permute-start(bf16[32,2048]{1,0:T(8,128)(2,1)S(1)} %collective-permute-done.7.refs_1_), channel_id=1, source_target_pairs={{0,4},{1,3},{2,6},{3,1},{4,0},{5,7},{6,2},{7,5},{8,12},{9,11},{10,... | collective-permute-start | bytes 393224 | tf_op jit(solution)/shard_map/ppermute | solution.py:55
  61.9 0.0 collective-permute-done.10.refs_4_
  61.9 1.2 %collective-permute-done.8.refs_2_ = bf16[32,2048]{1,0:T(8,128)(2,1)S(1)} collective-permute-done((bf16[32,2048]{1,0:T(8,128)(2,1)S(1)}, bf16[32,2048]{1,0:T(8,128)(2,1)S(1)}, u32[]{:S(2)}, u32[]{:S(2)}) %collective-permute-start.8) | collective-permute-done | bytes 131104 | tf_op jit(solution)/shard_map/ppermute | solution.py:55
  63.1 1.4 %collective-permute-start.12 = (bf16[32,2048]{1,0:T(8,128)(2,1)S(1)}, bf16[32,2048]{1,0:T(8,128)(2,1)S(1)}, u32[]{:S(2)}, u32[]{:S(2)}) collective-permute-start(bf16[32,2048]{1,0:T(8,128)(2,1)S(1)} %collective-permute-done.8.refs_2_), channel_id=1, source_target_pairs={{0,2},{1,5},{2,0},{3,7},{4,6},{5,1},{6,4},{7,3},{8,10},{9,13},{10,... | collective-permute-start | bytes 393224 | tf_op jit(solution)/shard_map/ppermute | solution.py:55
  64.5 0.7 collective-permute-start.18
  65.1 0.0 collective-permute-done.16.refs_3_
  65.1 2.1 %collective-permute-start.20 = (bf16[32,2048]{1,0:T(8,128)(2,1)S(1)}, bf16[32,2048]{1,0:T(8,128)(2,1)S(1)}, u32[]{:S(2)}, u32[]{:S(2)}) collective-permute-start(bf16[32,2048]{1,0:T(8,128)(2,1)S(1)} %collective-permute-done.16.refs_3_), channel_id=1, source_target_pairs={{0,2},{1,3},{2,0},{3,1},{4,6},{5,7},{6,4},{7,5},{8,10},{9,11},{10,... | collective-permute-start | bytes 393224 | tf_op jit(solution)/shard_map/ppermute | solution.py:55
  67.3 0.0 collective-permute-done.19.refs_6_
  67.3 0.0 collective-permute-start.11
  67.3 0.0 collective-permute-done.9.refs_3_
  67.3 2.8 %collective-permute-start.13 = (bf16[32,2048]{1,0:T(8,128)(2,1)S(1)}, bf16[32,2048]{1,0:T(8,128)(2,1)S(1)}, u32[]{:S(2)}, u32[]{:S(2)}) collective-permute-start(bf16[32,2048]{1,0:T(8,128)(2,1)S(1)} %collective-permute-done.9.refs_3_), channel_id=1, source_target_pairs={{0,2},{1,5},{2,0},{3,7},{4,6},{5,1},{6,4},{7,3},{8,10},{9,13},{10,... | collective-permute-start | bytes 393224 | tf_op jit(solution)/shard_map/ppermute | solution.py:55
  70.1 0.0 collective-permute-done.18.refs_5_
  70.1 0.8 collective-permute-done.20.refs_7_
  70.9 2.4 %combine.2.refs_8_ = f32[256,2048]{1,0:T(8,128)S(1)} custom-call(bf16[32,2048]{1,0:T(8,128)(2,1)S(1)} %get-tuple-element.56.refs_0_, bf16[32,2048]{1,0:T(8,128)(2,1)S(1)} %collective-permute-done.14.refs_1_, bf16[32,2048]{1,0:T(8,128)(2,1)S(1)} %collective-permute-done.15.refs_2_, bf16[32,2048]{1,0:T(8,128)(2,1)S(1)} %collective-permute-done.16.refs_3_, ...), custom_call_target="tpu_custom_call" | custom-call | tf_op jit(solution)/shard_map/combine/pallas_call | solution.py:396
  73.3 0.0 collective-permute-done.12.refs_6_
  73.3 0.0 collective-permute-done.11.refs_5_
  73.3 0.4 collective-permute-done.13.refs_7_
  73.7 2.5 %combine.3 = (bf16[128,2048]{1,0:T(8,128)(2,1)S(1)}, f32[128,2048]{1,0:T(8,128)S(1)}) custom-call(bf16[32,2048]{1,0:T(8,128)(2,1)S(1)} %attend.2.refs_0_, bf16[32,2048]{1,0:T(8,128)(2,1)S(1)} %collective-permute-done.7.refs_1_, bf16[32,2048]{1,0:T(8,128)(2,1)S(1)} %collective-permute-done.8.refs_2_, bf16[32,2048]{1,0:T(8,128)(2,1)S(1)} %collective-permute-done.9.refs_3_, ...), custom_call_target="tpu_custom_call" | custom-call | tf_op jit(solution)/shard_map/combine/pallas_call | solution.py:396
  76.2 0.1 collective-permute-start.21
  76.3 1.9 %collective-permute-done.21 = bf16[128,2048]{1,0:T(8,128)(2,1)S(1)} collective-permute-done((bf16[128,2048]{1,0:T(8,128)(2,1)S(1)}, bf16[128,2048]{1,0:T(8,128)(2,1)S(1)}, u32[]{:S(2)}, u32[]{:S(2)}) %collective-permute-start.21) | collective-permute-done | bytes 524320 | tf_op jit(solution)/shard_map/ppermute | solution.py:521
  78.2 0.9 %add_convert_fusion = bf16[128,2048]{1,0:T(8,128)(2,1)} fusion(f32[128,2048]{1,0:T(8,128)S(1)} %get-tuple-element.59, bf16[128,2048]{1,0:T(8,128)(2,1)S(1)} %collective-permute-done.21), kind=kLoop, calls=%fused_computation.3 | loop fusion | flops 786432 | bytes 2097152 | tf_op jit(solution)/shard_map/convert_element_type | solution.py:522
  (9 shorter events, 0.2 us)
Async XLA Ops:
  4.0 7.7 %collective-permute-start = (bf16[128,1152]{1,0:T(8,128)(2,1)S(1)}, bf16[128,1152]{1,0:T(8,128)(2,1)S(1)}, u32[]{:S(2)}, u32[]{:S(2)}) collective-permute-start(bf16[128,1152]{1,0:T(8,128)(2,1)S(1)} %get-tuple-element.34), channel_id=1, source_target_pairs={{0,2},{1,5},{2,0},{3,7},{4,6},{5,1},{6,4},{7,3},{8,10},{9,13},{10,... | collective-permute-start | bytes 884744 | tf_op jit(solution)/shard_map/ppermute | solution.py:55
  11.1 7.1 %collective-permute-start.1 = (bf16[128,1280]{1,0:T(8,128)(2,1)S(1)}, bf16[128,1280]{1,0:T(8,128)(2,1)S(1)}, u32[]{:S(2)}, u32[]{:S(2)}) collective-permute-start(bf16[128,1280]{1,0:T(8,128)(2,1)S(1)} %get-tuple-element.36), channel_id=1, source_target_pairs={{0,2},{1,5},{2,0},{3,7},{4,6},{5,1},{6,4},{7,3},{8,10},{9,13},{10,... | collective-permute-start | bytes 983048 | tf_op jit(solution)/shard_map/ppermute | solution.py:55
  11.8 8.2 %copy-start = (s32[8]{0:T(128)S(1)}, s32[8]{0:T(128)}, u32[]{:S(2)}) copy-start(s32[8]{0:T(128)} %length_ref.3) | copy-start | bytes 100
  18.3 12.1 %collective-permute-start.3 = (bf16[64,2432]{1,0:T(8,128)(2,1)S(1)}, bf16[64,2432]{1,0:T(8,128)(2,1)}, u32[]{:S(2)}, u32[]{:S(2)}) collective-permute-start(bf16[64,2432]{1,0:T(8,128)(2,1)S(1)} %fusion.1), channel_id=1, source_target_pairs={{0,4},{1,3},{2,6},{3,1},{4,0},{5,7},{6,2},{7,5},{8,12},{9,11},{10,... | collective-permute-start | bytes 933896 | tf_op jit(solution)/shard_map/ppermute | solution.py:55
  20.2 13.0 %collective-permute-start.2 = (bf16[128,2304]{1,0:T(8,128)(2,1)S(1)}, bf16[128,2304]{1,0:T(8,128)(2,1)S(1)}, u32[]{:S(2)}, u32[]{:S(2)}) collective-permute-start(bf16[128,2304]{1,0:T(8,128)(2,1)S(1)} %get-tuple-element.44), channel_id=1, source_target_pairs={{0,2},{1,5},{2,0},{3,7},{4,6},{5,1},{6,4},{7,3},{8,10},{9,13},{10,... | collective-permute-start | bytes 1769480 | tf_op jit(solution)/shard_map/ppermute | solution.py:55
  31.5 8.0 %collective-permute-start.5 = (bf16[32,2432]{1,0:T(8,128)(2,1)S(1)}, bf16[32,2432]{1,0:T(8,128)(2,1)S(1)}, u32[]{:S(2)}, u32[]{:S(2)}) collective-permute-start(bf16[32,2432]{1,0:T(8,128)(2,1)S(1)} %slice.64), channel_id=1, source_target_pairs={{0,8},{1,9},{2,10},{3,11},{4,12},{5,13},{6,14},{7,15},{8,0},{9,1},... | collective-permute-start | bytes 466952 | tf_op jit(solution)/shard_map/ppermute | solution.py:55
  33.3 8.2 %collective-permute-start.4 = (bf16[64,2304]{1,0:T(8,128)(2,1)S(1)}, bf16[64,2304]{1,0:T(8,128)(2,1)S(1)}, u32[]{:S(2)}, u32[]{:S(2)}) collective-permute-start(bf16[64,2304]{1,0:T(8,128)(2,1)S(1)} %slice.63), channel_id=1, source_target_pairs={{0,4},{1,3},{2,6},{3,1},{4,0},{5,7},{6,2},{7,5},{8,12},{9,11},{10,... | collective-permute-start | bytes 884744 | tf_op jit(solution)/shard_map/ppermute | solution.py:55
  41.6 7.8 %collective-permute-start.6 = (bf16[32,2304]{1,0:T(8,128)(2,1)S(1)}, bf16[32,2304]{1,0:T(8,128)(2,1)S(1)}, u32[]{:S(2)}, u32[]{:S(2)}) collective-permute-start(bf16[32,2304]{1,0:T(8,128)(2,1)S(1)} %slice.65), channel_id=1, source_target_pairs={{0,8},{1,9},{2,10},{3,11},{4,12},{5,13},{6,14},{7,15},{8,0},{9,1},... | collective-permute-start | bytes 442376 | tf_op jit(solution)/shard_map/ppermute | solution.py:55
  46.6 9.9 %collective-permute-start.17 = (bf16[32,2048]{1,0:T(8,128)(2,1)S(1)}, bf16[32,2048]{1,0:T(8,128)(2,1)S(1)}, u32[]{:S(2)}, u32[]{:S(2)}) collective-permute-start(bf16[32,2048]{1,0:T(8,128)(2,1)S(1)} %get-tuple-element.56.refs_0_), channel_id=1, source_target_pairs={{0,2},{1,3},{2,0},{3,1},{4,6},{5,7},{6,4},{7,5},{8,10},{9,11},{10,... | collective-permute-start | bytes 393224 | tf_op jit(solution)/shard_map/ppermute | solution.py:55
  46.8 9.6 %collective-permute-start.15 = (bf16[32,2048]{1,0:T(8,128)(2,1)S(1)}, bf16[32,2048]{1,0:T(8,128)(2,1)S(1)}, u32[]{:S(2)}, u32[]{:S(2)}) collective-permute-start(bf16[32,2048]{1,0:T(8,128)(2,1)S(1)} %get-tuple-element.56.refs_0_), channel_id=1, source_target_pairs={{0,4},{1,5},{2,6},{3,7},{4,0},{5,1},{6,2},{7,3},{8,12},{9,13},{10,... | collective-permute-start | bytes 393224 | tf_op jit(solution)/shard_map/ppermute | solution.py:55
  49.4 8.9 %collective-permute-start.14 = (bf16[32,2048]{1,0:T(8,128)(2,1)S(1)}, bf16[32,2048]{1,0:T(8,128)(2,1)S(1)}, u32[]{:S(2)}, u32[]{:S(2)}) collective-permute-start(bf16[32,2048]{1,0:T(8,128)(2,1)S(1)} %get-tuple-element.56.refs_0_), channel_id=1, source_target_pairs={{0,8},{1,9},{2,10},{3,11},{4,12},{5,13},{6,14},{7,15},{8,0},{9,1},... | collective-permute-start | bytes 393224 | tf_op jit(solution)/shard_map/ppermute | solution.py:55
  52.7 8.3 %collective-permute-start.7 = (bf16[32,2048]{1,0:T(8,128)(2,1)S(1)}, bf16[32,2048]{1,0:T(8,128)(2,1)S(1)}, u32[]{:S(2)}, u32[]{:S(2)}) collective-permute-start(bf16[32,2048]{1,0:T(8,128)(2,1)S(1)} %attend.2.refs_0_), channel_id=1, source_target_pairs={{0,8},{1,9},{2,10},{3,11},{4,12},{5,13},{6,14},{7,15},{8,0},{9,1},... | collective-permute-start | bytes 393224 | tf_op jit(solution)/shard_map/ppermute | solution.py:55
  54.9 7.0 %collective-permute-start.10 = (bf16[32,2048]{1,0:T(8,128)(2,1)S(1)}, bf16[32,2048]{1,0:T(8,128)(2,1)S(1)}, u32[]{:S(2)}, u32[]{:S(2)}) collective-permute-start(bf16[32,2048]{1,0:T(8,128)(2,1)S(1)} %attend.2.refs_0_), channel_id=1, source_target_pairs={{0,2},{1,5},{2,0},{3,7},{4,6},{5,1},{6,4},{7,3},{8,10},{9,13},{10,... | collective-permute-start | bytes 393224 | tf_op jit(solution)/shard_map/ppermute | solution.py:55
  56.4 6.7 %collective-permute-start.8 = (bf16[32,2048]{1,0:T(8,128)(2,1)S(1)}, bf16[32,2048]{1,0:T(8,128)(2,1)S(1)}, u32[]{:S(2)}, u32[]{:S(2)}) collective-permute-start(bf16[32,2048]{1,0:T(8,128)(2,1)S(1)} %attend.2.refs_0_), channel_id=1, source_target_pairs={{0,4},{1,3},{2,6},{3,1},{4,0},{5,7},{6,2},{7,5},{8,12},{9,11},{10,... | collective-permute-start | bytes 393224 | tf_op jit(solution)/shard_map/ppermute | solution.py:55
  58.3 6.8 %collective-permute-start.16 = (bf16[32,2048]{1,0:T(8,128)(2,1)S(1)}, bf16[32,2048]{1,0:T(8,128)(2,1)S(1)}, u32[]{:S(2)}, u32[]{:S(2)}) collective-permute-start(bf16[32,2048]{1,0:T(8,128)(2,1)S(1)} %collective-permute-done.14.refs_1_), channel_id=1, source_target_pairs={{0,4},{1,5},{2,6},{3,7},{4,0},{5,1},{6,2},{7,3},{8,12},{9,13},{10,... | collective-permute-start | bytes 393224 | tf_op jit(solution)/shard_map/ppermute | solution.py:55
  58.5 8.8 %collective-permute-start.19 = (bf16[32,2048]{1,0:T(8,128)(2,1)S(1)}, bf16[32,2048]{1,0:T(8,128)(2,1)S(1)}, u32[]{:S(2)}, u32[]{:S(2)}) collective-permute-start(bf16[32,2048]{1,0:T(8,128)(2,1)S(1)} %collective-permute-done.15.refs_2_), channel_id=1, source_target_pairs={{0,2},{1,3},{2,0},{3,1},{4,6},{5,7},{6,4},{7,5},{8,10},{9,11},{10,... | collective-permute-start | bytes 393224 | tf_op jit(solution)/shard_map/ppermute | solution.py:55
  61.1 6.3 %collective-permute-start.9 = (bf16[32,2048]{1,0:T(8,128)(2,1)S(1)}, bf16[32,2048]{1,0:T(8,128)(2,1)S(1)}, u32[]{:S(2)}, u32[]{:S(2)}) collective-permute-start(bf16[32,2048]{1,0:T(8,128)(2,1)S(1)} %collective-permute-done.7.refs_1_), channel_id=1, source_target_pairs={{0,4},{1,3},{2,6},{3,1},{4,0},{5,7},{6,2},{7,5},{8,12},{9,11},{10,... | collective-permute-start | bytes 393224 | tf_op jit(solution)/shard_map/ppermute | solution.py:55
  63.1 10.2 %collective-permute-start.12 = (bf16[32,2048]{1,0:T(8,128)(2,1)S(1)}, bf16[32,2048]{1,0:T(8,128)(2,1)S(1)}, u32[]{:S(2)}, u32[]{:S(2)}) collective-permute-start(bf16[32,2048]{1,0:T(8,128)(2,1)S(1)} %collective-permute-done.8.refs_2_), channel_id=1, source_target_pairs={{0,2},{1,5},{2,0},{3,7},{4,6},{5,1},{6,4},{7,3},{8,10},{9,13},{10,... | collective-permute-start | bytes 393224 | tf_op jit(solution)/shard_map/ppermute | solution.py:55
  64.5 5.6 %collective-permute-start.18 = (bf16[32,2048]{1,0:T(8,128)(2,1)S(1)}, bf16[32,2048]{1,0:T(8,128)(2,1)S(1)}, u32[]{:S(2)}, u32[]{:S(2)}) collective-permute-start(bf16[32,2048]{1,0:T(8,128)(2,1)S(1)} %collective-permute-done.14.refs_1_), channel_id=1, source_target_pairs={{0,2},{1,3},{2,0},{3,1},{4,6},{5,7},{6,4},{7,5},{8,10},{9,11},{10,... | collective-permute-start | bytes 393224 | tf_op jit(solution)/shard_map/ppermute | solution.py:55
  65.1 5.7 %collective-permute-start.20 = (bf16[32,2048]{1,0:T(8,128)(2,1)S(1)}, bf16[32,2048]{1,0:T(8,128)(2,1)S(1)}, u32[]{:S(2)}, u32[]{:S(2)}) collective-permute-start(bf16[32,2048]{1,0:T(8,128)(2,1)S(1)} %collective-permute-done.16.refs_3_), channel_id=1, source_target_pairs={{0,2},{1,3},{2,0},{3,1},{4,6},{5,7},{6,4},{7,5},{8,10},{9,11},{10,... | collective-permute-start | bytes 393224 | tf_op jit(solution)/shard_map/ppermute | solution.py:55
  67.3 6.0 %collective-permute-start.11 = (bf16[32,2048]{1,0:T(8,128)(2,1)S(1)}, bf16[32,2048]{1,0:T(8,128)(2,1)S(1)}, u32[]{:S(2)}, u32[]{:S(2)}) collective-permute-start(bf16[32,2048]{1,0:T(8,128)(2,1)S(1)} %collective-permute-done.7.refs_1_), channel_id=1, source_target_pairs={{0,2},{1,5},{2,0},{3,7},{4,6},{5,1},{6,4},{7,3},{8,10},{9,13},{10,... | collective-permute-start | bytes 393224 | tf_op jit(solution)/shard_map/ppermute | solution.py:55
  67.3 6.4 %collective-permute-start.13 = (bf16[32,2048]{1,0:T(8,128)(2,1)S(1)}, bf16[32,2048]{1,0:T(8,128)(2,1)S(1)}, u32[]{:S(2)}, u32[]{:S(2)}) collective-permute-start(bf16[32,2048]{1,0:T(8,128)(2,1)S(1)} %collective-permute-done.9.refs_3_), channel_id=1, source_target_pairs={{0,2},{1,5},{2,0},{3,7},{4,6},{5,1},{6,4},{7,3},{8,10},{9,13},{10,... | collective-permute-start | bytes 393224 | tf_op jit(solution)/shard_map/ppermute | solution.py:55
  76.2 2.0 %collective-permute-start.21 = (bf16[128,2048]{1,0:T(8,128)(2,1)S(1)}, bf16[128,2048]{1,0:T(8,128)(2,1)S(1)}, u32[]{:S(2)}, u32[]{:S(2)}) collective-permute-start(bf16[128,2048]{1,0:T(8,128)(2,1)S(1)} %get-tuple-element.60), channel_id=1, source_target_pairs={{0,1},{1,0},{2,3},{3,2},{4,5},{5,4},{6,7},{7,6},{8,9},{9,8},{10,11... | collective-permute-start | bytes 1572872 | tf_op jit(solution)/shard_map/ppermute | solution.py:521
